TPU v7x, 32 devices: a whole 2x2x4 slice. The times are simulated.
32 devices in a mesh: seq: 8 (over z, y), roll: 4 (over x, core).
Axes of the slice: x: 2, y: 2, z: 4, core: 2. Of those that a mesh axis runs over, the one named last changes fastest.
Arguments:
- tokens: int32 [4, 3968], P('roll', 'seq'), may hold values from 0 to 29
- breaks: int32 [4, 3968], P('roll', 'seq'), may hold values 0 or 1
- lengths: int32 [4], P('roll'), may hold values from 1984 to 3968, as said below
- embed_table: float32 [30, 1280], replicated, may hold values from -6 to 6
- break_vec: float32 [1280], replicated, may hold values from -6 to 6
- gain_in: float32 [2, 1280], replicated, may hold values from 0.25 to 1.75
- gain_mid: float32 [2, 640], replicated, may hold values from 0.25 to 1.75
- gain_out: float32 [2, 640], replicated, may hold values from 0.25 to 1.75
- w_in: bfloat16 [2, 1280, 640], P(None, 'roll'), may hold values from -0.15625 to 0.15625
- convolution_weight: bfloat16 [2, 640, 3200], P(None, 'roll'), may hold values from -0.109375 to 0.109375
- w_out: bfloat16 [2, 640, 1280], P(None, 'roll'), may hold values from -0.25 to 0.25
Outputs:
- encoded: bfloat16 [4, 3968, 1280], P('roll', 'seq')
Inputs may be any that keep to these rules, and one draw needn't show every extreme that they name: `lengths`: some complex has all 3968 residues valid in every draw.
All inputs are finite; a program needn't handle non-finite values. No bound on the sum of `breaks` on one device may be relied on, other than what follows from the above.
Results may differ from a plain program's by a relative error of at most 0.014.
Values may be sent and summed in bfloat16 or wider, within the bound.
No kernel may reach another device: no remote copies, remote signals or barrier semaphores. Data moves between devices by JAX's collectives and lax.ppermute only.
A program may use at most 64 MiB of HBM per device.

v0:
```python
import functools

import jax
import jax.numpy as jnp
from jax import lax
from jax.experimental import pallas as pl
from jax.experimental.pallas import tpu as pltpu
from jax.sharding import PartitionSpec as P

H = 640
KERNEL = 5
VOCAB = 30
SLOT = 32
CODES = 2 * SLOT
BASE_DILATION = 64
DIL0 = BASE_DILATION
DIL1 = 2 * BASE_DILATION
HALF = KERNEL // 2
EDGE = HALF * DIL1
REACH = EDGE + HALF * DIL0
VMEM_LIMIT = 48 * 1024 * 1024
BF = jnp.bfloat16
F32 = jnp.float32
VMEM = pl.BlockSpec(memory_space=pltpu.VMEM)
SMEM = pl.BlockSpec(memory_space=pltpu.SMEM)
ANY = pl.BlockSpec(memory_space=pl.ANY)


def params():
    return pltpu.CompilerParams(vmem_limit_bytes=VMEM_LIMIT)


def gelu(x):
    u = jnp.abs(x)
    t = 1.0 / (1.0 + (0.3275911 * 0.5**0.5) * u)
    q = 0.5 * 1.061405429
    for a in (-1.453152027, 1.421413741, -0.284496736, 0.254829592):
        q = q * t + 0.5 * a
    q = q * t * jnp.exp(-0.5 * u * u)
    return jnp.maximum(x, 0.0) - u * q


def norm(x, gain):
    center = jnp.mean(x, axis=-1, keepdims=True)
    d = x - center
    spread = jnp.mean(d * d, axis=-1, keepdims=True)
    return d * lax.rsqrt(spread + 1e-5) * gain


def dot(a, b):
    return jnp.dot(a, b, preferred_element_type=F32)


def pick(rows, columns, start):
    i = lax.broadcasted_iota(jnp.int32, (rows, columns), 0)
    j = lax.broadcasted_iota(jnp.int32, (rows, columns), 1)
    return jnp.where(i == j + start, 1.0, 0.0).astype(BF)


def embed_kernel(at, embed, brk, gain, w, table, part, scratch):
    scratch[...] = jnp.zeros_like(scratch)
    scratch[0:VOCAB] = embed[...]
    scratch[SLOT : SLOT + VOCAB] = embed[...] + brk[...]
    hidden = scratch[...].astype(BF)
    table[...] = hidden
    normed = gelu(norm(hidden.astype(F32), gain[0:1])).astype(BF)
    rows = w.shape[0]
    mine = dot(normed, pick(normed.shape[1], rows, at[0] * rows)).astype(BF)
    part[...] = dot(mine, w[...])


def table_kernel(at, own, other, gain, w, out):
    wide = own[...] + other[...].astype(F32)
    t = gelu(norm(wide, gain[0:1])).astype(BF)
    rows = w.shape[0]
    mine = dot(t, pick(t.shape[1], rows, at[0] * rows)).astype(BF)
    out[...] = dot(mine, w[...]).astype(out.dtype)


def rows_kernel(at, hot5, hot1, table, taps, gain_out, gain_in, gain_mid, w_out, w_in, ci, hid, tw):
    @pl.when(pl.program_id(0) == 0)
    def _():
        for k in range(KERNEL):
            tw[k * CODES : (k + 1) * CODES] = taps[:, k * H : (k + 1) * H]

    mixed = dot(hot5[...], tw[...])
    act = gelu(norm(mixed, gain_out[0:1])).astype(BF)
    hidden = (dot(hot1[...], table[...]) + dot(act, w_out[...])).astype(BF)
    hid[...] = hidden
    normed = gelu(norm(hidden.astype(F32), gain_in[1:2])).astype(BF)
    wide = dot(normed, w_in[...])
    rows = wide.shape[0]
    pos = at[0] + pl.program_id(0) * rows + lax.broadcasted_iota(jnp.int32, (rows, 1), 0)
    valid = jnp.where((pos >= 0) & (pos < at[1]), 1.0, 0.0)
    ci[...] = (gelu(norm(wide, gain_mid[1:2])) * valid).astype(BF)


def last_kernel(ci, hid, gain_out, w_conv, w_out, out):
    rows = out.shape[0]
    mixed = dot(ci[0:rows], w_conv[:, 0:H])
    for k in range(1, KERNEL):
        mixed += dot(ci[k * DIL1 : k * DIL1 + rows], w_conv[:, k * H : (k + 1) * H])
    act = gelu(norm(mixed, gain_out[1:2])).astype(BF)
    out[...] = (hid[EDGE : EDGE + rows].astype(F32) + dot(act, w_out[...])).astype(BF)


def per_device(tokens, breaks, lengths, embed_table, break_vec, gain_in, gain_mid, gain_out, w_in, conv_w, w_out):
    rows = tokens.shape[1]
    width = embed_table.shape[1]
    roll_at = lax.axis_index("roll")
    seq_at = lax.axis_index("seq")
    rolls = lax.axis_size("roll")
    seqs = lax.axis_size("seq")
    at = roll_at.astype(jnp.int32).reshape(1)

    codes = tokens + SLOT * breaks
    all_codes = lax.all_gather(codes[0], "seq").reshape(-1)
    out0 = lax.all_gather(w_out[0], "roll", axis=0, tiled=True)
    in1 = lax.all_gather(w_in[1], "roll", axis=0, tiled=True)
    conv1 = lax.all_gather(conv_w[1], "roll", axis=0, tiled=True)
    out1 = lax.all_gather(w_out[1], "roll", axis=0, tiled=True)

    table, part = pl.pallas_call(
        embed_kernel,
        out_shape=(
            jax.ShapeDtypeStruct((CODES, width), BF),
            jax.ShapeDtypeStruct((CODES, H), F32),
        ),
        in_specs=[SMEM, VMEM, VMEM, VMEM, VMEM],
        out_specs=(VMEM, VMEM),
        scratch_shapes=[pltpu.VMEM((CODES, width), F32)],
        compiler_params=params(),
    )(at, embed_table, break_vec[None], gain_in, w_in[0])

    def swap(x, step):
        return lax.ppermute(x, "roll", [(i, i ^ step) for i in range(rolls)])

    special = rolls == 4
    if special:
        own = part + swap(part, 1)
        other = swap(own.astype(BF), 2)
    else:
        own = lax.psum(part, "roll")
        other = jnp.zeros((CODES, H), BF)
    taps = pl.pallas_call(
        table_kernel,
        out_shape=jax.ShapeDtypeStruct((CODES, KERNEL * H), BF),
        in_specs=[SMEM, VMEM, VMEM, VMEM, VMEM],
        out_specs=VMEM,
        compiler_params=params(),
    )(at, own, other, gain_mid, conv_w[0])
    if special:
        core = roll_at % 2
        mine = lax.dynamic_slice_in_dim(taps, core * SLOT, SLOT, axis=0)
        theirs = lax.dynamic_slice_in_dim(taps, (1 - core) * SLOT, SLOT, axis=0)
        mine = mine.astype(F32) + swap(theirs, 1).astype(F32)
        mine = (mine + swap(mine.astype(BF), 2).astype(F32)).astype(BF)
        theirs = swap(mine, 1)
        first = core == 0
        taps = jnp.concatenate([jnp.where(first, mine, theirs), jnp.where(first, theirs, mine)], axis=0)
    else:
        taps = lax.psum(taps.astype(F32), "roll").astype(BF)

    start = seq_at * rows
    padded = jnp.pad(all_codes, (REACH, REACH))
    near = lax.dynamic_slice_in_dim(padded, start, rows + 2 * REACH)
    pos = start - REACH + jnp.arange(rows + 2 * REACH, dtype=jnp.int32)
    near_valid = jnp.where((pos >= 0) & (pos < lengths[0]), near, -1)
    wide_rows = rows + 2 * EDGE
    lanes = jnp.arange(CODES, dtype=jnp.int32)
    tap_codes = jnp.stack([near_valid[k * DIL0 : k * DIL0 + wide_rows] for k in range(KERNEL)], axis=1)
    hot5 = (tap_codes[:, :, None] == lanes).astype(BF).reshape(wide_rows, KERNEL * CODES)
    center = near[HALF * DIL0 : HALF * DIL0 + wide_rows]
    hot1 = (center[:, None] == lanes).astype(BF)

    span = jnp.stack([start.astype(jnp.int32) - EDGE, lengths[0]])
    steps = 3
    block = wide_rows // steps
    row_block = lambda n: pl.BlockSpec((block, n), lambda i: (i, 0))
    whole = lambda x: pl.BlockSpec(x.shape, lambda i: (0,) * x.ndim, pipeline_mode=pl.Buffered(1))
    ci, hid = pl.pallas_call(
        rows_kernel,
        grid=(steps,),
        out_shape=(
            jax.ShapeDtypeStruct((wide_rows, H), BF),
            jax.ShapeDtypeStruct((wide_rows, width), BF),
        ),
        in_specs=[SMEM, row_block(KERNEL * CODES), row_block(CODES)]
        + [whole(x) for x in (table, taps, gain_out, gain_in, gain_mid, out0, in1)],
        out_specs=(row_block(H), row_block(width)),
        scratch_shapes=[pltpu.VMEM((KERNEL * CODES, H), BF)],
        compiler_params=params(),
    )(span, hot5, hot1, table, taps, gain_out, gain_in, gain_mid, out0, in1)

    out = pl.pallas_call(
        last_kernel,
        out_shape=jax.ShapeDtypeStruct((rows, width), BF),
        in_specs=[VMEM] * 5,
        out_specs=VMEM,
        compiler_params=params(),
    )(ci, hid, gain_out, conv1, out1)
    return out[None]


def solution(mesh):
    placed = (
        P("roll", "seq"),
        P("roll", "seq"),
        P("roll"),
        P(),
        P(),
        P(),
        P(),
        P(),
        P(None, "roll", None),
        P(None, "roll", None),
        P(None, "roll", None),
    )
    return jax.shard_map(
        per_device, mesh=mesh, in_specs=placed, out_specs=P("roll", "seq", None), check_vma=False
    )
```

profile of v0, /device:TPU:0, one launch (start us, length us, event | category | flops | bytes accessed | tf_op | source)
XLA Modules:
  0.0 131.9 jit_solution(14967819929949286879)
XLA Ops:
  6.5 2.2 %fusion.8 = (bf16[1,160,1280]{2,1,0:T(8,128)(2,1)}, bf16[1,160,1280]{2,1,0:T(8,128)(2,1)}) fusion(bf16[2,160,1280]{2,1,0:T(8,128)(2,1)} %param.21), kind=kLoop, calls=%fused_computation.23 | loop fusion | bytes 1638400 | tf_op jit(solution)/shard_map/slice | solution.py:121
  8.8 0.9 fusion.9
  9.7 0.7 all-gather.16.cloned.1.call-update
  10.5 2.7 %fusion.7 = (bf16[1,160,3200]{2,1,0:T(8,128)(2,1)}, bf16[160,3200]{1,0:T(8,128)(2,1)S(1)}) fusion(bf16[2,160,3200]{2,1,0:T(8,128)(2,1)} %param.20), kind=kLoop, calls=%fused_computation.22 | loop fusion | bytes 4096000 | tf_op jit(solution)/shard_map/slice | solution.py:120
  13.3 0.9 shard_map.109
  14.2 0.5 collective-permute-start
  14.8 27.4 %all-gather.4 = s32[8,1,496]{2,1,0:T(1,128)S(1)} all-gather(s32[1,1,496]{2,1,0:T(1,128)S(1)} %add_bitcast_fusion), channel_id=1, replica_groups=mesh['seq'=8,'roll'=4] {'seq'}, dimensions={0}, use_global_device_ids=true | all-gather | bytes 17856 | tf_op jit(solution)/shard_map/all_gather | solution.py:117
  42.2 0.1 reshape.11
  42.9 0.1 fusion.2
  43.0 1.6 %collective-permute-start.1 = (bf16[64,640]{1,0:T(8,128)(2,1)S(1)}, bf16[64,640]{1,0:T(8,128)(2,1)S(1)}, u32[]{:S(2)}, u32[]{:S(2)}) collective-permute-start(bf16[64,640]{1,0:T(8,128)(2,1)S(1)} %get-tuple-element.13), channel_id=1, source_target_pairs={{0,2},{1,3},{2,0},{3,1},{4,6},{5,7},{6,4},{7,5},{8,10},{9,11},{10,... | collective-permute-start | bytes 245768 | tf_op jit(solution)/shard_map/ppermute | solution.py:136
  44.6 0.1 fusion.10
  44.7 0.1 eq.38
  44.9 1.6 %copy.14 = s32[1008,320]{1,0:T(8,128)} copy(s32[1008,320]{0,1:T(8,128)S(1)} %bitcast.24) | data formatting | bytes 2580480 | tf_op jit(solution)/shard_map/eq | solution.py:172
  46.5 0.1 eq.41
  46.5 2.7 %collective-permute-done.1.other = bf16[64,640]{1,0:T(8,128)(2,1)S(1)} collective-permute-done((bf16[64,640]{1,0:T(8,128)(2,1)S(1)}, bf16[64,640]{1,0:T(8,128)(2,1)S(1)}, u32[]{:S(2)}, u32[]{:S(2)}) %collective-permute-start.1) | collective-permute-done | bytes 81952 | tf_op jit(solution)/shard_map/ppermute | solution.py:136
  49.3 0.7 shard_map.110
  50.1 0.1 pad_add_fusion.at
  50.2 0.1 pad_dynamic-slice_fusion
  50.3 1.3 collective-permute-done.2
  51.6 1.6 %collective-permute-start.3 = (bf16[32,3200]{1,0:T(8,128)(2,1)S(1)}, bf16[32,3200]{1,0:T(8,128)(2,1)S(1)}, u32[]{:S(2)}, u32[]{:S(2)}) collective-permute-start(bf16[32,3200]{1,0:T(8,128)(2,1)S(1)} %fusion.1), channel_id=1, source_target_pairs={{0,2},{1,3},{2,0},{3,1},{4,6},{5,7},{6,4},{7,5},{8,10},{9,11},{10,... | collective-permute-start | bytes 614408 | tf_op jit(solution)/shard_map/ppermute | solution.py:136
  53.2 0.2 compare_convert_fusion.hot5
  53.3 5.5 %collective-permute-done.3 = bf16[32,3200]{1,0:T(8,128)(2,1)S(1)} collective-permute-done((bf16[32,3200]{1,0:T(8,128)(2,1)S(1)}, bf16[32,3200]{1,0:T(8,128)(2,1)S(1)}, u32[]{:S(2)}, u32[]{:S(2)}) %collective-permute-start.3) | collective-permute-done | bytes 204832 | tf_op jit(solution)/shard_map/ppermute | solution.py:136
  58.8 0.1 add_convert_fusion
  59.0 0.2 fusion.hot1
  59.2 1.2 collective-permute-done.4
  60.6 1.4 %copy-done.1 = bf16[1,640,1280]{2,1,0:T(8,128)(2,1)S(1)} copy-done((bf16[1,640,1280]{2,1,0:T(8,128)(2,1)S(1)}, bf16[1,640,1280]{2,1,0:T(8,128)(2,1)}, u32[]{:S(2)}) %copy-start.1) | copy-done | bytes 1638424
  62.0 1.5 %copy-done.2 = bf16[1,1280,640]{2,1,0:T(8,128)(2,1)S(1)} copy-done((bf16[1,1280,640]{2,1,0:T(8,128)(2,1)S(1)}, bf16[1,1280,640]{2,1,0:T(8,128)(2,1)}, u32[]{:S(2)}) %copy-start.2) | copy-done | bytes 1638424
  63.5 16.6 %shard_map.111 = (bf16[1008,640]{1,0:T(8,128)(2,1)S(1)}, bf16[1008,1280]{1,0:T(8,128)(2,1)}) custom-call(s32[2]{0:T(128)S(1)} %pad_add_fusion.at, bf16[1008,320]{1,0:T(8,128)(2,1)S(1)} %compare_convert_fusion.hot5, bf16[1008,64]{1,0:T(8,128)(2,1)S(1)} %fusion.hot1, bf16[64,1280]{1,0:T(8,128)(2,1)S(1)} %get-tuple-element.9.table, ...), custom_call_target="tpu_custom_call" | custom-call | tf_op jit(solution)/shard_map/pallas_call | solution.py:181
  80.1 31.9 %all-gather.14.cloned.1.call-done = bf16[1,640,3200]{2,1,0:T(8,128)(2,1)} async-done(((bf16[1,160,3200]{2,1,0:T(8,128)(2,1)}), bf16[1,640,3200]{2,1,0:T(8,128)(2,1)}) %all-gather.14.cloned.1.call-update) | async-done | bytes 4096016 | tf_op jit(solution)/shard_map/all_gather | solution.py:120
  112.0 1.7 %copy-done = bf16[1008,1280]{1,0:T(8,128)(2,1)S(1)} copy-done((bf16[1008,1280]{1,0:T(8,128)(2,1)S(1)}, bf16[1008,1280]{1,0:T(8,128)(2,1)}, u32[]{:S(2)}) %copy-start) | copy-done | bytes 2580504
  113.7 1.4 %copy-done.3 = bf16[1,640,1280]{2,1,0:T(8,128)(2,1)S(1)} copy-done((bf16[1,640,1280]{2,1,0:T(8,128)(2,1)S(1)}, bf16[1,640,1280]{2,1,0:T(8,128)(2,1)}, u32[]{:S(2)}) %copy-start.3) | copy-done | bytes 1638424
  115.2 10.2 %shard_map.112 = bf16[496,1280]{1,0:T(8,128)(2,1)} custom-call(bf16[1008,640]{1,0:T(8,128)(2,1)S(1)} %get-tuple-element.11.ci, bf16[1008,1280]{1,0:T(8,128)(2,1)S(1)} %copy-done, f32[2,640]{1,0:T(2,128)S(1)} %copy-done.6, bf16[640,3200]{1,0:T(8,128)(2,1)} %bitcast.25, bf16[640,1280]{1,0:T(8,128)(2,1)S(1)} %bitcast.23), custom_call_target="tpu_custom_call" | custom-call | tf_op jit(solution)/shard_map/pallas_call | solution.py:195
  (45 shorter events, 0.7 us)
Async XLA Ops:
  6.5 2.3 %copy-start.9 = (bf16[2,320,640]{2,1,0:T(8,128)(2,1)S(1)}, bf16[2,320,640]{2,1,0:T(8,128)(2,1)}, u32[]{:S(2)}) copy-start(bf16[2,320,640]{2,1,0:T(8,128)(2,1)} %param.19) | copy-start | bytes 2457604
  6.5 54.0 %all-gather.10.cloned.1.call-start = ((), (), s32[]{:S(2)}) async-start(), calls=%async_computation | async-start | bytes 2048000 | tf_op jit(solution)/shard_map/all_gather | solution.py:118
  8.8 51.8 %all-gather.12.cloned.1.call-start = ((), (), s32[]{:S(2)}) async-start(), calls=%async_computation.1 | async-start | bytes 2048000 | tf_op jit(solution)/shard_map/all_gather | solution.py:119
  9.7 70.4 %all-gather.16.cloned.1.call-start = ((), (), s32[]{:S(2)}) async-start(), calls=%async_computation.3 | async-start | bytes 2048000 | tf_op jit(solution)/shard_map/all_gather | solution.py:121
  10.4 2.8 %copy-start.10 = (f32[1280]{0:T(1024)S(1)}, f32[1280]{0:T(1024)}, u32[]{:S(2)}) copy-start(f32[1280]{0:T(1024)} %param.15) | copy-start | bytes 15364
  10.4 2.8 %copy-start.4 = (f32[30,1280]{1,0:T(8,128)S(1)}, f32[30,1280]{1,0:T(8,128)}, u32[]{:S(2)}) copy-start(f32[30,1280]{1,0:T(8,128)} %embed.1) | copy-start | bytes 460804
  10.5 2.8 %copy-start.5 = (f32[2,1280]{1,0:T(2,128)S(1)}, f32[2,1280]{1,0:T(2,128)}, u32[]{:S(2)}) copy-start(f32[2,1280]{1,0:T(2,128)} %gain_in.1) | copy-start | bytes 30724
  10.5 101.5 %all-gather.14.cloned.1.call-start = ((), (), s32[]{:S(2)}) async-start(), calls=%async_computation.2 | async-start | bytes 5120000 | tf_op jit(solution)/shard_map/all_gather | solution.py:120
  13.2 1.5 %copy-start.11 = (s32[1,496]{1,0:T(1,128)S(1)}, s32[1,496]{1,0:T(1,128)}, u32[]{:S(2)}) copy-start(s32[1,496]{1,0:T(1,128)} %param.11) | copy-start | bytes 5956
  13.2 1.5 %copy-start.12 = (s32[1,496]{1,0:T(1,128)S(1)}, s32[1,496]{1,0:T(1,128)}, u32[]{:S(2)}) copy-start(s32[1,496]{1,0:T(1,128)} %param.12) | copy-start | bytes 5956
  14.2 28.8 %collective-permute-start = (f32[64,640]{1,0:T(8,128)S(1)}, f32[64,640]{1,0:T(8,128)S(1)}, u32[]{:S(2)}, u32[]{:S(2)}) collective-permute-start(f32[64,640]{1,0:T(8,128)S(1)} %get-tuple-element.10), channel_id=1, source_target_pairs={{0,1},{1,0},{2,3},{3,2},{4,5},{5,4},{6,7},{7,6},{8,9},{9,8},{10,11... | collective-permute-start | bytes 491528 | tf_op jit(solution)/shard_map/ppermute | solution.py:136
  43.0 6.2 %collective-permute-start.1 = (bf16[64,640]{1,0:T(8,128)(2,1)S(1)}, bf16[64,640]{1,0:T(8,128)(2,1)S(1)}, u32[]{:S(2)}, u32[]{:S(2)}) collective-permute-start(bf16[64,640]{1,0:T(8,128)(2,1)S(1)} %get-tuple-element.13), channel_id=1, source_target_pairs={{0,2},{1,3},{2,0},{3,1},{4,6},{5,7},{6,4},{7,5},{8,10},{9,11},{10,... | collective-permute-start | bytes 245768 | tf_op jit(solution)/shard_map/ppermute | solution.py:136
  44.8 4.4 %copy-start.7 = (f32[2,640]{1,0:T(2,128)S(1)}, f32[2,640]{1,0:T(2,128)}, u32[]{:S(2)}) copy-start(f32[2,640]{1,0:T(2,128)} %gain_mid.1) | copy-start | bytes 15364
  46.5 6.6 %copy-start.8 = (s32[1008,320]{1,0:T(8,128)S(1)}, s32[1008,320]{1,0:T(8,128)}, u32[]{:S(2)}) copy-start(s32[1008,320]{1,0:T(8,128)} %copy.14) | copy-start | bytes 3870724
  50.0 1.5 %collective-permute-start.2 = (bf16[32,3200]{1,0:T(8,128)(2,1)S(1)}, bf16[32,3200]{1,0:T(8,128)(2,1)S(1)}, u32[]{:S(2)}, u32[]{:S(2)}) collective-permute-start(bf16[32,3200]{1,0:T(8,128)(2,1)S(1)} %constant_dynamic-slice_fusion), channel_id=1, source_target_pairs={{0,1},{1,0},{2,3},{3,2},{4,5},{5,4},{6,7},{7,6},{8,9},{9,8},{10,11... | collective-permute-start | bytes 614408 | tf_op jit(solution)/shard_map/ppermute | solution.py:136
  51.6 7.2 %collective-permute-start.3 = (bf16[32,3200]{1,0:T(8,128)(2,1)S(1)}, bf16[32,3200]{1,0:T(8,128)(2,1)S(1)}, u32[]{:S(2)}, u32[]{:S(2)}) collective-permute-start(bf16[32,3200]{1,0:T(8,128)(2,1)S(1)} %fusion.1), channel_id=1, source_target_pairs={{0,2},{1,3},{2,0},{3,1},{4,6},{5,7},{6,4},{7,5},{8,10},{9,11},{10,... | collective-permute-start | bytes 614408 | tf_op jit(solution)/shard_map/ppermute | solution.py:136
  53.3 7.2 %copy-start.6 = (f32[2,640]{1,0:T(2,128)S(1)}, f32[2,640]{1,0:T(2,128)}, u32[]{:S(2)}) copy-start(f32[2,640]{1,0:T(2,128)} %gain_out.3) | copy-start | bytes 15364
  58.9 1.5 %collective-permute-start.4 = (bf16[32,3200]{1,0:T(8,128)(2,1)S(1)}, bf16[32,3200]{1,0:T(8,128)(2,1)S(1)}, u32[]{:S(2)}, u32[]{:S(2)}) collective-permute-start(bf16[32,3200]{1,0:T(8,128)(2,1)S(1)} %add_convert_fusion), channel_id=1, source_target_pairs={{0,1},{1,0},{2,3},{3,2},{4,5},{5,4},{6,7},{7,6},{8,9},{9,8},{10,11... | collective-permute-start | bytes 614408 | tf_op jit(solution)/shard_map/ppermute | solution.py:136
  60.5 1.4 %copy-start.1 = (bf16[1,640,1280]{2,1,0:T(8,128)(2,1)S(1)}, bf16[1,640,1280]{2,1,0:T(8,128)(2,1)}, u32[]{:S(2)}) copy-start(bf16[1,640,1280]{2,1,0:T(8,128)(2,1)} %all-gather.10.cloned.1.call-done) | copy-start | bytes 4915204
  62.0 1.5 %copy-start.2 = (bf16[1,1280,640]{2,1,0:T(8,128)(2,1)S(1)}, bf16[1,1280,640]{2,1,0:T(8,128)(2,1)}, u32[]{:S(2)}) copy-start(bf16[1,1280,640]{2,1,0:T(8,128)(2,1)} %all-gather.12.cloned.1.call-done) | copy-start | bytes 4915204
  112.0 1.7 %copy-start = (bf16[1008,1280]{1,0:T(8,128)(2,1)S(1)}, bf16[1008,1280]{1,0:T(8,128)(2,1)}, u32[]{:S(2)}) copy-start(bf16[1008,1280]{1,0:T(8,128)(2,1)} %get-tuple-element.12.hid) | copy-start | bytes 7741444
  113.7 1.4 %copy-start.3 = (bf16[1,640,1280]{2,1,0:T(8,128)(2,1)S(1)}, bf16[1,640,1280]{2,1,0:T(8,128)(2,1)}, u32[]{:S(2)}) copy-start(bf16[1,640,1280]{2,1,0:T(8,128)(2,1)} %all-gather.16.cloned.1.call-done) | copy-start | bytes 4915204
Sparse Core Ops, SparseCore 0:
  8.9 22.7 all-gather.9
  33.2 20.8 all-gather.11
  55.7 20.8 all-gather.15
  78.1 33.9 all-gather.13
where the time goes:
time: 132 us
  waiting for transfers between devices  43.3 us (33%)
  Pallas kernels  28.5 us (22%)
  blocking collectives  27.4 us (21%)
  local copies, waits for them, and re-layouts  14 us (11%)
  between operations  14 us (11%)
  starting transfers between devices  3.9 us (3%)
    all_gather x1, waiting for transfers between devices, per_device(): conv1 = lax.all_gather(conv_w[1], 'roll', axis=0, tiled=True)  31.9 us
    all_gather x1, blocking collectives, per_device(): all_codes = lax.all_gather(codes[0], 'seq').reshape(-1)  27.4 us
    pallas_call x1, Pallas kernels, per_device(): pl.pallas_call(rows_kernel, grid=(steps,), out_shape=(jax.ShapeDtypeStruc...  16.6 us
    ppermute x5, waiting for transfers between devices, swap(): return lax.ppermute(x, 'roll', [(i, i ^ step) for i in range(rolls)])  10.7 us
    pallas_call x1, Pallas kernels, per_device(): pl.pallas_call(last_kernel, out_shape=jax.ShapeDtypeStruct((rows, width),...  10.2 us
    unnamed x26, local copies, waits for them, and re-layouts  6.14 us
    ppermute x5, starting transfers between devices, swap(): return lax.ppermute(x, 'roll', [(i, i ^ step) for i in range(rolls)])  3.77 us
    slice x1, local copies, waits for them, and re-layouts, per_device(): conv1 = lax.all_gather(conv_w[1], 'roll', axis=0, tiled=True)  2.67 us
  transfers between devices with their start and end apart: 9, of which 5 were waited for; matrix products, arithmetic and copies ran while one was open for 5% of the time, Pallas kernels for 14%

commit v1 on v0

v1 whole, which is shorter than its diff:
```python
import functools

import jax
import jax.numpy as jnp
from jax import lax
from jax.experimental import pallas as pl
from jax.experimental.pallas import tpu as pltpu
from jax.sharding import PartitionSpec as P

H = 640
KERNEL = 5
VOCAB = 30
SLOT = 32
CODES = 2 * SLOT
BASE_DILATION = 64
DIL0 = BASE_DILATION
DIL1 = 2 * BASE_DILATION
HALF = KERNEL // 2
EDGE = HALF * DIL1
REACH = EDGE + HALF * DIL0
VMEM_LIMIT = 44 * 1024 * 1024
BF = jnp.bfloat16
F32 = jnp.float32
VMEM = pl.BlockSpec(memory_space=pltpu.VMEM)
SMEM = pl.BlockSpec(memory_space=pltpu.SMEM)
ANY = pl.BlockSpec(memory_space=pl.ANY)
CUT_A = 18 * 128
CUT_B = 17 * 128


def params():
    return pltpu.CompilerParams(vmem_limit_bytes=VMEM_LIMIT)


def gelu(x):
    return (0.5 * x) * (1.0 + lax.erf(x * 0.5**0.5))


def norm(x, gain):
    center = jnp.mean(x, axis=-1, keepdims=True)
    d = x - center
    spread = jnp.mean(d * d, axis=-1, keepdims=True)
    return d * lax.rsqrt(spread + 1e-5) * gain


def dot(a, b):
    return jnp.dot(a, b, preferred_element_type=F32)


def place():
    roll, seq = lax.axis_index("roll"), lax.axis_index("seq")
    return lax.div(roll, 2), lax.rem(roll, 2), lax.rem(seq, 2), lax.rem(lax.div(seq, 2), 2)


def start(copies):
    for c in copies:
        c.start()


def wait(copies):
    for c in copies:
        c.wait()


def pick(rows, columns, first):
    i = lax.broadcasted_iota(jnp.int32, (rows, columns), 0)
    j = lax.broadcasted_iota(jnp.int32, (rows, columns), 1)
    return jnp.where(i == j + first, 1.0, 0.0).astype(BF)


def part_kernel(w_in, conv_w, w_out, a, b, sem):
    _, _, y, z = place()
    n = a.shape[0]
    r = pl.multiple_of(z * n, 16)
    r2 = pl.multiple_of(z * 2 * n, 16)
    rest = conv_w.shape[2] - CUT_B

    def go(pairs):
        copies = [pltpu.make_async_copy(s, d, sem) for s, d in pairs]
        start(copies)
        wait(copies)

    @pl.when(y == 0)
    def _():
        go([
            (w_out.at[0, pl.ds(r, n)], a),
            (conv_w.at[1, pl.ds(r, n), 0:CUT_A], b),
        ])

    @pl.when(y == 1)
    def _():
        go([
            (w_in.at[1, pl.ds(r2, n)], a.at[:, 0:H]),
            (w_in.at[1, pl.ds(r2 + n, n)], a.at[:, H : 2 * H]),
            (conv_w.at[1, pl.ds(r, n), CUT_B:], b.at[:, 0:rest]),
            (w_out.at[1, pl.ds(r, n)], b.at[:, rest:]),
        ])


def embed_kernel(embed, brk, gain, w_all, table, part, scratch, w, sem):
    copy = pltpu.make_async_copy(w_all.at[0], w, sem)
    copy.start()
    scratch[...] = jnp.zeros_like(scratch)
    scratch[0:VOCAB] = embed[...]
    scratch[SLOT : SLOT + VOCAB] = embed[...] + brk[...]
    hidden = scratch[...].astype(BF)
    table[...] = hidden
    normed = gelu(norm(hidden.astype(F32), gain[0:1])).astype(BF)
    rows = w.shape[0]
    mine = dot(normed, pick(normed.shape[1], rows, lax.axis_index("roll") * rows)).astype(BF)
    copy.wait()
    part[...] = dot(mine, w[...])


def table_kernel(own, other, gain, w_all, out, w, sem):
    copy = pltpu.make_async_copy(w_all.at[0], w, sem)
    copy.start()
    wide = own[...] + other[...].astype(F32)
    t = gelu(norm(wide, gain[0:1])).astype(BF)
    rows = w.shape[0]
    mine = dot(t, pick(t.shape[1], rows, lax.axis_index("roll") * rows)).astype(BF)
    copy.wait()
    out[...] = dot(mine, w[...]).astype(out.dtype)


def rows_kernel(split, span, hot5, hot1, table, taps, gain_out, gain_in, gain_mid, *rest):
    *w, ci, hid, tw, wo, wi, sem = rest
    depth = wo.shape[0] - CODES
    first = [
        pltpu.make_async_copy(taps.at[:, k * H : (k + 1) * H], tw.at[k * CODES : (k + 1) * CODES], sem.at[0])
        for k in range(KERNEL)
    ]
    first.append(pltpu.make_async_copy(table, wo.at[depth:], sem.at[0]))
    start(first)
    if not split:
        out_copies = [pltpu.make_async_copy(w[0], wo.at[0:depth], sem.at[1])]
        in_copies = [pltpu.make_async_copy(w[1], wi, sem.at[2])]
        start(out_copies + in_copies)
    else:
        w_out, w_in, near_out, near_in = w[:4]
        parts, near_parts = w[4:8], w[8:12]
        x, core, y, z = place()
        n = w_out.shape[1]
        m = w_in.shape[1]
        half = n // 2
        out_copies, in_copies = [], []
        for c, o, i in ((core, w_out, w_in), (1 - core, near_out, near_in)):
            at = 2 * x + c
            out_copies.append(pltpu.make_async_copy(o.at[0], wo.at[pl.ds(pl.multiple_of(at * n, 16), n)], sem.at[1]))
            in_copies.append(pltpu.make_async_copy(i.at[1], wi.at[pl.ds(pl.multiple_of(at * m, 16), m)], sem.at[2]))

        def far(outs, ins):
            out, into = [], []
            for c, of in ((core, parts), (1 - core, near_parts)):
                at = 2 * (1 - x) + c
                for p, zz in zip(outs, (z, 1 - z)):
                    row = pl.multiple_of(at * n + zz * half, 16)
                    out.append(pltpu.make_async_copy(of[p], wo.at[pl.ds(row, half)], sem.at[1]))
                for p, zz in zip(ins, (z, 1 - z)):
                    for j in range(2):
                        row = pl.multiple_of(at * m + zz * n + j * half, 16)
                        into.append(
                            pltpu.make_async_copy(of[p].at[:, j * H : (j + 1) * H], wi.at[pl.ds(row, half)], sem.at[2])
                        )
            return out, into

        start(out_copies + in_copies)
        far0, far1 = far((0, 2), (1, 3)), far((1, 3), (0, 2))

        @pl.when(y == 0)
        def _():
            start(far0[0] + far0[1])

        @pl.when(y == 1)
        def _():
            start(far1[0] + far1[1])

        out_copies += far0[0]
        in_copies += far0[1]

    wait(first)
    mixed = dot(hot5[...], tw[...])
    act = gelu(norm(mixed, gain_out[0:1])).astype(BF)
    wait(out_copies)
    hidden = dot(jnp.concatenate([act, hot1[...]], axis=1), wo[...]).astype(BF)
    rows = hidden.shape[0]
    hid[...] = hidden[EDGE : rows - EDGE]
    normed = gelu(norm(hidden.astype(F32), gain_in[1:2])).astype(BF)
    wait(in_copies)
    wide = dot(normed, wi[...])
    pos = span[0] + lax.broadcasted_iota(jnp.int32, (rows, 1), 0)
    valid = jnp.where((pos >= 0) & (pos < span[1]), 1.0, 0.0)
    ci[...] = (gelu(norm(wide, gain_mid[1:2])) * valid).astype(BF)


def last_kernel(split, ci, hid, gain_out, *rest):
    *w, out, wt, wo, sem = rest

    def conv(src, col, width, row, n):
        copies = []
        done = 0
        while done < width:
            tap, inner = divmod(col + done, H)
            step = min(H - inner, width - done)
            copies.append(
                pltpu.make_async_copy(
                    src.at[:, done : done + step],
                    wt.at[pl.ds(tap * H + row, n), inner : inner + step],
                    sem.at[0],
                )
            )
            done += step
        return copies

    if not split:
        conv_copies = conv(w[0], 0, KERNEL * H, 0, H)
        out_copies = [pltpu.make_async_copy(w[1], wo, sem.at[1])]
        start(conv_copies + out_copies)
    else:
        w_conv, w_out, near_conv, near_out = w[:4]
        parts, near_parts = w[4:8], w[8:12]
        x, core, y, z = place()
        n = w_out.shape[1]
        half = n // 2
        rest_cols = KERNEL * H - CUT_B
        conv_copies, out_copies = [], []
        for c, v, o in ((core, w_conv, w_out), (1 - core, near_conv, near_out)):
            row = pl.multiple_of((2 * x + c) * n, 16)
            conv_copies += conv(v.at[1], 0, KERNEL * H, row, n)
            out_copies.append(pltpu.make_async_copy(o.at[1], wo.at[pl.ds(row, n)], sem.at[1]))

        def far(head, tail):
            cv, out = [], []
            for c, of in ((core, parts), (1 - core, near_parts)):
                for p, zz in zip(head, (z, 1 - z)):
                    row = pl.multiple_of((2 * (1 - x) + c) * n + zz * half, 16)
                    cv += conv(of[p], 0, CUT_A, row, half)
                for p, zz in zip(tail, (z, 1 - z)):
                    row = pl.multiple_of((2 * (1 - x) + c) * n + zz * half, 16)
                    skip = CUT_A - CUT_B
                    cv += conv(of[p].at[:, skip:rest_cols], CUT_A, rest_cols - skip, row, half)
                    out.append(pltpu.make_async_copy(of[p].at[:, rest_cols:], wo.at[pl.ds(row, half)], sem.at[1]))
            return cv, out

        start(conv_copies + out_copies)
        far0, far1 = far((0, 2), (1, 3)), far((1, 3), (0, 2))

        @pl.when(y == 0)
        def _():
            start(far0[0] + far0[1])

        @pl.when(y == 1)
        def _():
            start(far1[0] + far1[1])

        conv_copies += far0[0]
        out_copies += far0[1]

    rows = out.shape[0]
    blocks = [0, 16 * (rows // 32), rows]
    for b in range(2):
        lo, hi = blocks[b], blocks[b + 1]
        lhs = jnp.concatenate([ci[lo + k * DIL1 : hi + k * DIL1] for k in range(KERNEL)], axis=1)
        if b == 0:
            wait(conv_copies)
        mixed = dot(lhs, wt[...])
        act = gelu(norm(mixed, gain_out[1:2])).astype(BF)
        if b == 0:
            wait(out_copies)
        out[lo:hi] = (hid[lo:hi].astype(F32) + dot(act, wo[...])).astype(BF)


def after(x, *deps):
    return lax.optimization_barrier((x, *deps))[0]


def per_device(tokens, breaks, lengths, embed_table, break_vec, gain_in, gain_mid, gain_out, w_in, conv_w, w_out):
    rows = tokens.shape[1]
    width = embed_table.shape[1]
    roll_at = lax.axis_index("roll")
    seq_at = lax.axis_index("seq")
    rolls = lax.axis_size("roll")
    seqs = lax.axis_size("seq")
    split = rolls == 4 and seqs % 4 == 0

    def core_swap(x):
        return lax.ppermute(x, "roll", [(i, i ^ 1) for i in range(rolls)])

    def x_swap(x):
        return lax.ppermute(x, "roll", [(i, i ^ 2) for i in range(rolls)])

    def seq_swap(x, bits):
        return lax.ppermute(x, "seq", [(i, i ^ bits) for i in range(seqs)])

    if split:
        shard = w_out.shape[1] // 2
        part_a, part_b = pl.pallas_call(
            part_kernel,
            out_shape=(jax.ShapeDtypeStruct((shard, width), BF), jax.ShapeDtypeStruct((shard, CUT_A), BF)),
            in_specs=[ANY] * 3,
            out_specs=(ANY, ANY),
            scratch_shapes=[pltpu.SemaphoreType.DMA],
            compiler_params=params(),
        )(w_in, conv_w, w_out)
        far_a = x_swap(part_a)
        near_in, near_conv, near_out = core_swap(w_in), core_swap(conv_w), core_swap(w_out)
    else:
        out0 = lax.all_gather(w_out[0], "roll", axis=0, tiled=True)
        in1 = lax.all_gather(w_in[1], "roll", axis=0, tiled=True)
        conv1 = lax.all_gather(conv_w[1], "roll", axis=0, tiled=True)
        out1 = lax.all_gather(w_out[1], "roll", axis=0, tiled=True)

    table, part = pl.pallas_call(
        embed_kernel,
        out_shape=(
            jax.ShapeDtypeStruct((CODES, width), BF),
            jax.ShapeDtypeStruct((CODES, H), F32),
        ),
        in_specs=[VMEM, VMEM, VMEM, ANY],
        out_specs=(VMEM, VMEM),
        scratch_shapes=[
            pltpu.VMEM((CODES, width), F32),
            pltpu.VMEM(w_in.shape[1:], BF),
            pltpu.SemaphoreType.DMA,
        ],
        compiler_params=params(),
    )(embed_table, break_vec[None], gain_in, w_in)

    if split:
        own = part + core_swap(part)
        other = x_swap(own.astype(BF))
    else:
        own = lax.psum(part, "roll")
        other = jnp.zeros((CODES, H), BF)

    codes = tokens[0] + SLOT * breaks[0]
    if split:
        codes = after(codes, own)
    up = [(i, i + 1) for i in range(seqs - 1)]
    down = [(i + 1, i) for i in range(seqs - 1)]
    near = jnp.concatenate(
        [lax.ppermute(codes[rows - REACH :], "seq", up), codes, lax.ppermute(codes[:REACH], "seq", down)]
    )
    if split:
        far_b = x_swap(after(part_b, own))

    taps = pl.pallas_call(
        table_kernel,
        out_shape=jax.ShapeDtypeStruct((CODES, KERNEL * H), BF),
        in_specs=[VMEM, VMEM, VMEM, ANY],
        out_specs=VMEM,
        scratch_shapes=[pltpu.VMEM(conv_w.shape[1:], BF), pltpu.SemaphoreType.DMA],
        compiler_params=params(),
    )(own, other, gain_mid, conv_w)
    if split:
        core = roll_at % 2
        mine = lax.dynamic_slice_in_dim(taps, core * SLOT, SLOT, axis=0)
        theirs = lax.dynamic_slice_in_dim(taps, (1 - core) * SLOT, SLOT, axis=0)
        mine = mine.astype(F32) + core_swap(theirs).astype(F32)
        sent = mine.astype(BF)
        relay = after(far_a, sent)
        parts_a = [far_a] + [seq_swap(relay, b) for b in (1, 2, 3)]
        mine = (mine + x_swap(sent).astype(F32)).astype(BF)
        theirs = core_swap(mine)
        first = core == 0
        taps = jnp.concatenate([jnp.where(first, mine, theirs), jnp.where(first, theirs, mine)], axis=0)
        relay = after(far_b, mine)
        parts_b = [far_b] + [seq_swap(relay, b) for b in (1, 2, 3)]
        near_a = [core_swap(p) for p in parts_a]
        near_b = [core_swap(p) for p in parts_b]
        weights_a = [w_out, w_in, near_out, near_in] + parts_a + near_a
        weights_b = [conv_w, w_out, near_conv, near_out] + parts_b + near_b
    else:
        taps = lax.psum(taps.astype(F32), "roll").astype(BF)
        weights_a, weights_b = [out0, in1], [conv1, out1]

    begin = seq_at * rows
    pos = begin - REACH + jnp.arange(rows + 2 * REACH, dtype=jnp.int32)
    near_valid = jnp.where((pos >= 0) & (pos < lengths[0]), near, -1)
    wide_rows = rows + 2 * EDGE
    lanes = jnp.arange(CODES, dtype=jnp.int32)
    tap_codes = jnp.stack([near_valid[k * DIL0 : k * DIL0 + wide_rows] for k in range(KERNEL)], axis=1)
    hot5 = (tap_codes[:, :, None] == lanes).astype(BF).reshape(wide_rows, KERNEL * CODES)
    center = near[HALF * DIL0 : HALF * DIL0 + wide_rows]
    hot1 = (center[:, None] == lanes).astype(BF)

    span = jnp.stack([begin.astype(jnp.int32) - EDGE, lengths[0]])
    ci, hid = pl.pallas_call(
        functools.partial(rows_kernel, split),
        out_shape=(
            jax.ShapeDtypeStruct((wide_rows, H), BF),
            jax.ShapeDtypeStruct((rows, width), BF),
        ),
        in_specs=[SMEM, VMEM, VMEM, ANY, ANY, VMEM, VMEM, VMEM] + [ANY] * len(weights_a),
        out_specs=(VMEM, VMEM),
        scratch_shapes=[
            pltpu.VMEM((KERNEL * CODES, H), BF),
            pltpu.VMEM((H + CODES, width), BF),
            pltpu.VMEM((width, H), BF),
            pltpu.SemaphoreType.DMA((3,)),
        ],
        compiler_params=params(),
    )(span, hot5, hot1, table, taps, gain_out, gain_in, gain_mid, *weights_a)

    out = pl.pallas_call(
        functools.partial(last_kernel, split),
        out_shape=jax.ShapeDtypeStruct((rows, width), BF),
        in_specs=[VMEM] * 3 + [ANY] * len(weights_b),
        out_specs=VMEM,
        scratch_shapes=[
            pltpu.VMEM((KERNEL * H, H), BF),
            pltpu.VMEM((H, width), BF),
            pltpu.SemaphoreType.DMA((2,)),
        ],
        compiler_params=params(),
    )(ci, hid, gain_out, *weights_b)
    return out[None]


def solution(mesh):
    placed = (
        P("roll", "seq"),
        P("roll", "seq"),
        P("roll"),
        P(),
        P(),
        P(),
        P(),
        P(),
        P(None, "roll", None),
        P(None, "roll", None),
        P(None, "roll", None),
    )
    return jax.shard_map(
        per_device, mesh=mesh, in_specs=placed, out_specs=P("roll", "seq", None), check_vma=False
    )
```

time: 132 us -> 95.1 us (0.72)
  blocking collectives: 27.4 us -> 0 us
  starting transfers between devices: 3.9 us -> 22.7 us
  waiting for transfers between devices: 43.3 us -> 29 us
  between operations: 14 us -> 1.14 us
  Pallas kernels: 28.5 us -> 23.5 us
  other arithmetic: 0.8 us -> 3.94 us
    all_gather x4 -> x0, waiting for transfers between devices: 31.9 us -> none  [the longest x1 31.9 us: per_device(): conv1 = lax.all_gather(conv_w[1], 'roll', axis=0, tiled=True)]
    all_gather x1 -> x0, blocking collectives: 27.4 us -> none  [per_device(): all_codes = lax.all_gather(codes[0], 'seq').reshape(-1)]
    ppermute x5 -> x26, starting transfers between devices: 3.77 us -> 22.7 us  [the longest x6 10.2 us: seq_swap(): return lax.ppermute(x, 'seq', [(i, i ^ bits) for i in range(seqs)])]
    ppermute x5 -> x26, waiting for transfers between devices: 10.7 us -> 29 us  [the longest x6 22.5 us: seq_swap(): return lax.ppermute(x, 'seq', [(i, i ^ bits) for i in range(seqs)])]
    slice x3 -> x1, local copies, waits for them, and re-layouts: 5.72 us -> 0.07 us  [per_device(): codes[:REACH]]
    pallas_call x2 -> x3, Pallas kernels: 26.8 us -> 21.4 us  [the longest x1 13.1 us: per_device(): pl.pallas_call(functools.partial(rows_kernel, split), out_shape=(jax.Shap...]
    eq x4, local copies, waits for them, and re-layouts: 1.82 us -> 4.25 us  [per_device(): tap_codes[:, :, None] == lanes]
    unnamed x26 -> x34, local copies, waits for them, and re-layouts: 6.14 us -> 8.24 us
  transfers between devices with their start and end apart: 9 -> 26, of which waited for: 5 -> 9; matrix products, arithmetic and copies ran while one was open for 5% -> 10% of each run, Pallas kernels for 14% -> 16%
where the time goes in v1:
time: 95.1 us; the launch traced here: 94.5 us
  waiting for transfers between devices  29 us (30%)
  Pallas kernels  23.5 us (25%)
  starting transfers between devices  22.7 us (24%)
  local copies, waits for them, and re-layouts  14.2 us (15%)
  other arithmetic  3.94 us (4%)
  between operations  1.14 us (1%)
    ppermute x6, waiting for transfers between devices, seq_swap(): return lax.ppermute(x, 'seq', [(i, i ^ bits) for i in range(seqs)])  22.5 us
    pallas_call x1, Pallas kernels, per_device(): pl.pallas_call(functools.partial(rows_kernel, split), out_shape=(jax.Shap...  13.1 us
    ppermute x6, starting transfers between devices, seq_swap(): return lax.ppermute(x, 'seq', [(i, i ^ bits) for i in range(seqs)])  10.2 us
    unnamed x34, local copies, waits for them, and re-layouts  8.24 us
    pallas_call x1, Pallas kernels, per_device(): pl.pallas_call(functools.partial(last_kernel, split), out_shape=jax.Shape...  7.51 us
    ppermute x4, starting transfers between devices, x_swap(): return lax.ppermute(x, 'roll', [(i, i ^ 2) for i in range(rolls)])  5.51 us
    eq x4, local copies, waits for them, and re-layouts, per_device(): tap_codes[:, :, None] == lanes  4.25 us
    ppermute x1, starting transfers between devices, per_device(): lax.ppermute(codes[rows - REACH:], 'seq', up)  3.42 us
  transfers between devices with their start and end apart: 26, of which 9 were waited for; matrix products, arithmetic and copies ran while one was open for 10% of the time, Pallas kernels for 16%

profile of v1, /device:TPU:0, one launch (start us, length us, event | category | flops | bytes accessed | tf_op | source)
XLA Modules:
  0.0 94.5 jit_solution(16662540541337607518)
XLA Ops:
  0.0 0.8 broadcast_in_dim.14.brk
  0.8 1.1 %copy-done.3 = bf16[2,320,640]{2,1,0:T(8,128)(2,1)S(1)} copy-done((bf16[2,320,640]{2,1,0:T(8,128)(2,1)S(1)}, bf16[2,320,640]{2,1,0:T(8,128)(2,1)}, u32[]{:S(2)}) %copy-start.3) | copy-done | bytes 819224
  1.9 0.9 copy-done.8
  3.5 1.1 %shard_map.109 = (bf16[64,1280]{1,0:T(8,128)(2,1)S(1)}, f32[64,640]{1,0:T(8,128)S(1)}) custom-call(f32[30,1280]{1,0:T(8,128)S(1)} %copy-done.8, f32[1,1280]{1,0:T(1,128)S(1)} %broadcast_in_dim.14.brk, f32[2,1280]{1,0:T(2,128)S(1)} %copy-done.9, bf16[2,320,640]{2,1,0:T(8,128)(2,1)S(1)} %copy-done.3), custom_call_target="tpu_custom_call" | custom-call | tf_op jit(solution)/shard_map/pallas_call | solution.py:313
  5.8 1.6 %copy-done = bf16[2,160,3200]{2,1,0:T(8,128)(2,1)S(1)} copy-done((bf16[2,160,3200]{2,1,0:T(8,128)(2,1)S(1)}, bf16[2,160,3200]{2,1,0:T(8,128)(2,1)}, u32[]{:S(2)}) %copy-start) | copy-done | bytes 2048024
  7.4 1.1 %copy-done.4 = bf16[2,320,640]{2,1,0:T(8,128)(2,1)S(1)} copy-done((bf16[2,320,640]{2,1,0:T(8,128)(2,1)S(1)}, bf16[2,320,640]{2,1,0:T(8,128)(2,1)}, u32[]{:S(2)}) %copy-start.4) | copy-done | bytes 819224
  10.0 2.9 %collective-permute-start.9 = (bf16[80,1280]{1,0:T(8,128)(2,1)}, bf16[80,1280]{1,0:T(8,128)(2,1)}, u32[]{:S(2)}, u32[]{:S(2)}) collective-permute-start(bf16[80,1280]{1,0:T(8,128)(2,1)} %get-tuple-element.18), channel_id=1, source_target_pairs={{0,2},{1,3},{2,0},{3,1},{4,6},{5,7},{6,4},{7,5},{8,10},{9,11},{10,... | collective-permute-start | bytes 614408 | tf_op jit(solution)/shard_map/ppermute | solution.py:290
  13.8 3.4 %collective-permute-start.1 = (s32[384]{0:T(512)S(1)}, s32[384]{0:T(512)S(1)}, u32[]{:S(2)}, u32[]{:S(2)}) collective-permute-start(s32[384]{0:T(512)S(1)} %get-tuple-element.35), channel_id=1, source_target_pairs={{0,4},{4,8},{8,12},{12,16},{16,20},{20,24},{24,28},{1,5},{5,9},{9,... | collective-permute-start | bytes 4616 | tf_op jit(solution)/shard_map/ppermute | solution.py:342
  17.2 1.3 %collective-permute-start.2 = (s32[384]{0:T(512)S(1)}, s32[384]{0:T(512)S(1)}, u32[]{:S(2)}, u32[]{:S(2)}) collective-permute-start(s32[384]{0:T(512)S(1)} %get-tuple-element.34), channel_id=1, source_target_pairs={{4,0},{8,4},{12,8},{16,12},{20,16},{24,20},{28,24},{5,1},{9,5},{13... | collective-permute-start | bytes 4616 | tf_op jit(solution)/shard_map/ppermute | solution.py:342
  19.2 1.5 %collective-permute-start.18 = (bf16[80,2304]{1,0:T(8,128)(2,1)}, bf16[80,2304]{1,0:T(8,128)(2,1)}, u32[]{:S(2)}, u32[]{:S(2)}) collective-permute-start(bf16[80,2304]{1,0:T(8,128)(2,1)} %copy-done.13), channel_id=1, source_target_pairs={{0,2},{1,3},{2,0},{3,1},{4,6},{5,7},{6,4},{7,5},{8,10},{9,11},{10,... | collective-permute-start | bytes 1105928 | tf_op jit(solution)/shard_map/ppermute | solution.py:290
  20.7 2.0 %collective-permute-done.2 = s32[384]{0:T(512)S(1)} collective-permute-done((s32[384]{0:T(512)S(1)}, s32[384]{0:T(512)S(1)}, u32[]{:S(2)}, u32[]{:S(2)}) %collective-permute-start.2) | collective-permute-done | bytes 1568 | tf_op jit(solution)/shard_map/ppermute | solution.py:342
  22.8 1.2 %collective-permute-done.3.other = bf16[64,640]{1,0:T(8,128)(2,1)S(1)} collective-permute-done((bf16[64,640]{1,0:T(8,128)(2,1)S(1)}, bf16[64,640]{1,0:T(8,128)(2,1)S(1)}, u32[]{:S(2)}, u32[]{:S(2)}) %collective-permute-start.3) | collective-permute-done | bytes 81952 | tf_op jit(solution)/shard_map/ppermute | solution.py:290
  24.0 1.1 %shard_map.110 = bf16[64,3200]{1,0:T(8,128)(2,1)S(1)} custom-call(f32[64,640]{1,0:T(8,128)S(1)} %get-tuple-element.26.own, bf16[64,640]{1,0:T(8,128)(2,1)S(1)} %collective-permute-done.3.other, f32[2,640]{1,0:T(2,128)S(1)} %copy-done.11, bf16[2,160,3200]{2,1,0:T(8,128)(2,1)S(1)} %copy-done.1), custom_call_target="tpu_custom_call" | custom-call | tf_op jit(solution)/shard_map/pallas_call | solution.py:347
  26.0 1.2 %eq.38 = s32[1008,5,64]{0,2,1:T(8,128)} broadcast(s32[1008,5]{0,1:T(8,128)S(1)} %stack.31), dimensions={0,1} | broadcast | bytes 1310400 | tf_op jit(solution)/shard_map/eq | solution.py:383
  27.2 3.0 %copy.13 = s32[1008,320]{1,0:T(8,128)} copy(s32[1008,320]{0,1:T(8,128)} %bitcast.11) | data formatting | bytes 2580480 | tf_op jit(solution)/shard_map/eq | solution.py:383
  30.6 1.0 %fusion.1 = bf16[32,3200]{1,0:T(8,128)(2,1)S(1)} fusion(bf16[32,3200]{1,0:T(8,128)(2,1)} %collective-permute-done.4, bf16[64,3200]{1,0:T(8,128)(2,1)S(1)} %shard_map.110, s32[]{:T(128)S(6)} %select_n.32), kind=kLoop, calls=%fused_computation.6 | loop fusion | flops 409600 | bytes 614404 | tf_op jit(solution)/shard_map/convert_element_type | solution.py:360
  32.2 2.6 %collective-permute-start.10 = (bf16[80,1280]{1,0:T(8,128)(2,1)}, bf16[80,1280]{1,0:T(8,128)(2,1)S(1)}, u32[]{:S(2)}, u32[]{:S(2)}) collective-permute-start(bf16[80,1280]{1,0:T(8,128)(2,1)} %collective-permute-done.9.rest_4_), channel_id=1, source_target_pairs={{0,4},{4,0},{8,12},{12,8},{16,20},{20,16},{24,28},{28,24},{1,5},{5... | collective-permute-start | bytes 614408 | tf_op jit(solution)/shard_map/ppermute | solution.py:293
  34.7 1.5 %compare_convert_fusion.hot5 = bf16[1008,320]{1,0:T(8,128)(2,1)S(1)} fusion(s32[1008,320]{1,0:T(8,128)} %copy.13, s32[320]{0:T(512)S(1)} %eq.41), kind=kLoop, calls=%fused_computation | loop fusion | flops 645120 | bytes 1936640 | tf_op jit(solution)/shard_map/convert_element_type | solution.py:383
  36.9 1.8 %collective-permute-done.5 = bf16[32,3200]{1,0:T(8,128)(2,1)S(1)} collective-permute-done((bf16[32,3200]{1,0:T(8,128)(2,1)S(1)}, bf16[32,3200]{1,0:T(8,128)(2,1)S(1)}, u32[]{:S(2)}, u32[]{:S(2)}) %collective-permute-start.5) | collective-permute-done | bytes 204832 | tf_op jit(solution)/shard_map/ppermute | solution.py:290
  38.8 3.6 %collective-permute-start.11 = (bf16[80,1280]{1,0:T(8,128)(2,1)}, bf16[80,1280]{1,0:T(8,128)(2,1)S(1)}, u32[]{:S(2)}, u32[]{:S(2)}) collective-permute-start(bf16[80,1280]{1,0:T(8,128)(2,1)} %collective-permute-done.9.rest_4_), channel_id=1, source_target_pairs={{0,8},{4,12},{8,0},{12,4},{16,24},{20,28},{24,16},{28,20},{1,9},{5... | collective-permute-start | bytes 614408 | tf_op jit(solution)/shard_map/ppermute | solution.py:293
  42.9 1.0 %add_convert_fusion = bf16[32,3200]{1,0:T(8,128)(2,1)S(1)} fusion(bf16[32,3200]{1,0:T(8,128)(2,1)S(1)} %collective-permute-done.5, bf16[32,3200]{1,0:T(8,128)(2,1)} %collective-permute-done.4, bf16[64,3200]{1,0:T(8,128)(2,1)S(1)} %shard_map.110, s32[]{:T(128)S(6)} %select_n.32), kind=kLoop, calls=%fused_computation.4 | loop fusion | flops 614400 | bytes 819204 | tf_op jit(solution)/shard_map/convert_element_type | solution.py:363
  43.9 4.7 %collective-permute-done.11.rest_6_ = bf16[80,1280]{1,0:T(8,128)(2,1)S(1)} collective-permute-done((bf16[80,1280]{1,0:T(8,128)(2,1)}, bf16[80,1280]{1,0:T(8,128)(2,1)S(1)}, u32[]{:S(2)}, u32[]{:S(2)}) %collective-permute-start.11) | collective-permute-done | bytes 204832 | tf_op jit(solution)/shard_map/ppermute | solution.py:293
  48.6 3.1 %collective-permute-done.12.rest_7_ = bf16[80,1280]{1,0:T(8,128)(2,1)S(1)} collective-permute-done((bf16[80,1280]{1,0:T(8,128)(2,1)}, bf16[80,1280]{1,0:T(8,128)(2,1)S(1)}, u32[]{:S(2)}, u32[]{:S(2)}) %collective-permute-start.12) | collective-permute-done | bytes 204832 | tf_op jit(solution)/shard_map/ppermute | solution.py:293
  52.4 1.3 %collective-permute-start.19 = (bf16[80,2304]{1,0:T(8,128)(2,1)}, bf16[80,2304]{1,0:T(8,128)(2,1)S(1)}, u32[]{:S(2)}, u32[]{:S(2)}) collective-permute-start(bf16[80,2304]{1,0:T(8,128)(2,1)} %collective-permute-done.18.rest_4_), channel_id=1, source_target_pairs={{0,4},{4,0},{8,12},{12,8},{16,20},{20,16},{24,28},{28,24},{1,5},{5... | collective-permute-start | bytes 1105928 | tf_op jit(solution)/shard_map/ppermute | solution.py:293
  53.7 1.7 %collective-permute-start.20 = (bf16[80,2304]{1,0:T(8,128)(2,1)}, bf16[80,2304]{1,0:T(8,128)(2,1)S(1)}, u32[]{:S(2)}, u32[]{:S(2)}) collective-permute-start(bf16[80,2304]{1,0:T(8,128)(2,1)} %collective-permute-done.18.rest_4_), channel_id=1, source_target_pairs={{0,8},{4,12},{8,0},{12,4},{16,24},{20,28},{24,16},{28,20},{1,9},{5... | collective-permute-start | bytes 1105928 | tf_op jit(solution)/shard_map/ppermute | solution.py:293
  56.0 1.4 %collective-permute-done.16.rest_11_ = bf16[80,1280]{1,0:T(8,128)(2,1)S(1)} collective-permute-done((bf16[80,1280]{1,0:T(8,128)(2,1)S(1)}, bf16[80,1280]{1,0:T(8,128)(2,1)S(1)}, u32[]{:S(2)}, u32[]{:S(2)}) %collective-permute-start.16) | collective-permute-done | bytes 204832 | tf_op jit(solution)/shard_map/ppermute | solution.py:287
  57.6 5.7 %collective-permute-done.19.rest_5_ = bf16[80,2304]{1,0:T(8,128)(2,1)S(1)} collective-permute-done((bf16[80,2304]{1,0:T(8,128)(2,1)}, bf16[80,2304]{1,0:T(8,128)(2,1)S(1)}, u32[]{:S(2)}, u32[]{:S(2)}) %collective-permute-start.19) | collective-permute-done | bytes 368672 | tf_op jit(solution)/shard_map/ppermute | solution.py:293
  63.3 2.1 %collective-permute-done.20.rest_6_ = bf16[80,2304]{1,0:T(8,128)(2,1)S(1)} collective-permute-done((bf16[80,2304]{1,0:T(8,128)(2,1)}, bf16[80,2304]{1,0:T(8,128)(2,1)S(1)}, u32[]{:S(2)}, u32[]{:S(2)}) %collective-permute-start.20) | collective-permute-done | bytes 368672 | tf_op jit(solution)/shard_map/ppermute | solution.py:293
  65.4 6.9 %collective-permute-done.21.rest_7_ = bf16[80,2304]{1,0:T(8,128)(2,1)S(1)} collective-permute-done((bf16[80,2304]{1,0:T(8,128)(2,1)}, bf16[80,2304]{1,0:T(8,128)(2,1)S(1)}, u32[]{:S(2)}, u32[]{:S(2)}) %collective-permute-start.21) | collective-permute-done | bytes 368672 | tf_op jit(solution)/shard_map/ppermute | solution.py:293
  72.3 13.1 %shard_map.112 = (bf16[1008,640]{1,0:T(8,128)(2,1)S(1)}, bf16[496,1280]{1,0:T(8,128)(2,1)S(1)}) custom-call(s32[2]{0:T(128)S(1)} %pad_add_fusion.span, bf16[1008,320]{1,0:T(8,128)(2,1)S(1)} %compare_convert_fusion.hot5, bf16[1008,64]{1,0:T(8,128)(2,1)S(1)} %fusion.hot1, bf16[64,1280]{1,0:T(8,128)(2,1)S(1)} %copy-done.7, ...), custom_call_target="tpu_custom_call" | custom-call | tf_op jit(solution)/shard_map/pallas_call | solution.py:388
  85.5 1.3 %copy-done.14 = bf16[2,160,3200]{2,1,0:T(8,128)(2,1)} copy-done((bf16[2,160,3200]{2,1,0:T(8,128)(2,1)}, bf16[2,160,3200]{2,1,0:T(8,128)(2,1)S(1)}, u32[]{:S(2)}) %copy-start.14) | copy-done | bytes 2048024
  86.9 7.5 %shard_map.113 = bf16[496,1280]{1,0:T(8,128)(2,1)} custom-call(bf16[1008,640]{1,0:T(8,128)(2,1)S(1)} %get-tuple-element.20.ci, bf16[496,1280]{1,0:T(8,128)(2,1)S(1)} %get-tuple-element.21.hid, f32[2,640]{1,0:T(2,128)S(1)} %copy-done.12, bf16[2,160,3200]{2,1,0:T(8,128)(2,1)S(1)} %copy-done.1, bf16[2,160,1280]{2,1,0:T(8,128)(2,1)S(1)} %copy-done.2, ...), custom_call_target="tpu_custom_call" | custom-call | tf_op jit(solution)/shard_map/pallas_call | solution.py:405
  (80 shorter events, 8.7 us)
Async XLA Ops:
  5.3 8.4 %collective-permute-start = (f32[64,640]{1,0:T(8,128)S(1)}, f32[64,640]{1,0:T(8,128)S(1)}, u32[]{:S(2)}, u32[]{:S(2)}) collective-permute-start(f32[64,640]{1,0:T(8,128)S(1)} %get-tuple-element.15), channel_id=1, source_target_pairs={{0,1},{1,0},{2,3},{3,2},{4,5},{5,4},{6,7},{7,6},{8,9},{9,8},{10,11... | collective-permute-start | bytes 491528 | tf_op jit(solution)/shard_map/ppermute | solution.py:287
  5.7 45.9 %collective-permute-start.7 = (bf16[2,160,1280]{2,1,0:T(8,128)(2,1)}, bf16[2,160,1280]{2,1,0:T(8,128)(2,1)}, u32[]{:S(2)}, u32[]{:S(2)}) collective-permute-start(bf16[2,160,1280]{2,1,0:T(8,128)(2,1)} %rest_1_.3), channel_id=1, source_target_pairs={{0,1},{1,0},{2,3},{3,2},{4,5},{5,4},{6,7},{7,6},{8,9},{9,8},{10,11... | collective-permute-start | bytes 2457608 | tf_op jit(solution)/shard_map/ppermute | solution.py:287
  8.5 15.5 %copy-start.1 = (bf16[2,160,3200]{2,1,0:T(8,128)(2,1)S(1)}, bf16[2,160,3200]{2,1,0:T(8,128)(2,1)}, u32[]{:S(2)}) copy-start(bf16[2,160,3200]{2,1,0:T(8,128)(2,1)} %rest_0_.3) | copy-start | bytes 6144004
  8.5 15.5 %copy-start.11 = (f32[2,640]{1,0:T(2,128)S(1)}, f32[2,640]{1,0:T(2,128)}, u32[]{:S(2)}) copy-start(f32[2,640]{1,0:T(2,128)} %gain_mid.1) | copy-start | bytes 15364
  10.0 20.1 %collective-permute-start.9 = (bf16[80,1280]{1,0:T(8,128)(2,1)}, bf16[80,1280]{1,0:T(8,128)(2,1)}, u32[]{:S(2)}, u32[]{:S(2)}) collective-permute-start(bf16[80,1280]{1,0:T(8,128)(2,1)} %get-tuple-element.18), channel_id=1, source_target_pairs={{0,2},{1,3},{2,0},{3,1},{4,6},{5,7},{6,4},{7,5},{8,10},{9,11},{10,... | collective-permute-start | bytes 614408 | tf_op jit(solution)/shard_map/ppermute | solution.py:290
  13.8 5.4 %collective-permute-start.1 = (s32[384]{0:T(512)S(1)}, s32[384]{0:T(512)S(1)}, u32[]{:S(2)}, u32[]{:S(2)}) collective-permute-start(s32[384]{0:T(512)S(1)} %get-tuple-element.35), channel_id=1, source_target_pairs={{0,4},{4,8},{8,12},{12,16},{16,20},{20,24},{24,28},{1,5},{5,9},{9,... | collective-permute-start | bytes 4616 | tf_op jit(solution)/shard_map/ppermute | solution.py:342
  17.2 5.5 %collective-permute-start.2 = (s32[384]{0:T(512)S(1)}, s32[384]{0:T(512)S(1)}, u32[]{:S(2)}, u32[]{:S(2)}) collective-permute-start(s32[384]{0:T(512)S(1)} %get-tuple-element.34), channel_id=1, source_target_pairs={{4,0},{8,4},{12,8},{16,12},{20,16},{24,20},{28,24},{5,1},{9,5},{13... | collective-permute-start | bytes 4616 | tf_op jit(solution)/shard_map/ppermute | solution.py:342
  18.6 5.4 %collective-permute-start.3 = (bf16[64,640]{1,0:T(8,128)(2,1)S(1)}, bf16[64,640]{1,0:T(8,128)(2,1)S(1)}, u32[]{:S(2)}, u32[]{:S(2)}) collective-permute-start(bf16[64,640]{1,0:T(8,128)(2,1)S(1)} %get-tuple-element.25), channel_id=1, source_target_pairs={{0,2},{1,3},{2,0},{3,1},{4,6},{5,7},{6,4},{7,5},{8,10},{9,11},{10,... | collective-permute-start | bytes 245768 | tf_op jit(solution)/shard_map/ppermute | solution.py:290
  19.2 17.3 %collective-permute-start.18 = (bf16[80,2304]{1,0:T(8,128)(2,1)}, bf16[80,2304]{1,0:T(8,128)(2,1)}, u32[]{:S(2)}, u32[]{:S(2)}) collective-permute-start(bf16[80,2304]{1,0:T(8,128)(2,1)} %copy-done.13), channel_id=1, source_target_pairs={{0,2},{1,3},{2,0},{3,1},{4,6},{5,7},{6,4},{7,5},{8,10},{9,11},{10,... | collective-permute-start | bytes 1105928 | tf_op jit(solution)/shard_map/ppermute | solution.py:290
  25.8 4.8 %collective-permute-start.4 = (bf16[32,3200]{1,0:T(8,128)(2,1)}, bf16[32,3200]{1,0:T(8,128)(2,1)}, u32[]{:S(2)}, u32[]{:S(2)}) collective-permute-start(bf16[32,3200]{1,0:T(8,128)(2,1)} %constant_dynamic-slice_fusion), channel_id=1, source_target_pairs={{0,1},{1,0},{2,3},{3,2},{4,5},{5,4},{6,7},{7,6},{8,9},{9,8},{10,11... | collective-permute-start | bytes 614408 | tf_op jit(solution)/shard_map/ppermute | solution.py:287
  30.1 6.2 %copy-start.5 = (bf16[2,320,640]{2,1,0:T(8,128)(2,1)S(1)}, bf16[2,320,640]{2,1,0:T(8,128)(2,1)}, u32[]{:S(2)}) copy-start(bf16[2,320,640]{2,1,0:T(8,128)(2,1)} %rest_1_.2) | copy-start | bytes 2457604
  30.1 6.2 %collective-permute-start.13 = (bf16[80,1280]{1,0:T(8,128)(2,1)}, bf16[80,1280]{1,0:T(8,128)(2,1)S(1)}, u32[]{:S(2)}, u32[]{:S(2)}) collective-permute-start(bf16[80,1280]{1,0:T(8,128)(2,1)} %collective-permute-done.9.rest_4_), channel_id=1, source_target_pairs={{0,1},{1,0},{2,3},{3,2},{4,5},{5,4},{6,7},{7,6},{8,9},{9,8},{10,11... | collective-permute-start | bytes 614408 | tf_op jit(solution)/shard_map/ppermute | solution.py:287
  31.6 7.1 %collective-permute-start.5 = (bf16[32,3200]{1,0:T(8,128)(2,1)S(1)}, bf16[32,3200]{1,0:T(8,128)(2,1)S(1)}, u32[]{:S(2)}, u32[]{:S(2)}) collective-permute-start(bf16[32,3200]{1,0:T(8,128)(2,1)S(1)} %fusion.1), channel_id=1, source_target_pairs={{0,2},{1,3},{2,0},{3,1},{4,6},{5,7},{6,4},{7,5},{8,10},{9,11},{10,... | collective-permute-start | bytes 614408 | tf_op jit(solution)/shard_map/ppermute | solution.py:290
  32.2 10.2 %collective-permute-start.10 = (bf16[80,1280]{1,0:T(8,128)(2,1)}, bf16[80,1280]{1,0:T(8,128)(2,1)S(1)}, u32[]{:S(2)}, u32[]{:S(2)}) collective-permute-start(bf16[80,1280]{1,0:T(8,128)(2,1)} %collective-permute-done.9.rest_4_), channel_id=1, source_target_pairs={{0,4},{4,0},{8,12},{12,8},{16,20},{20,16},{24,28},{28,24},{1,5},{5... | collective-permute-start | bytes 614408 | tf_op jit(solution)/shard_map/ppermute | solution.py:293
  36.3 36.0 %copy-start.7 = (bf16[64,1280]{1,0:T(8,128)(2,1)S(1)}, bf16[64,1280]{1,0:T(8,128)(2,1)}, u32[]{:S(2)}) copy-start(bf16[64,1280]{1,0:T(8,128)(2,1)} %copy-done.6) | copy-start | bytes 491524
  36.3 36.0 %copy-start.10 = (f32[2,1280]{1,0:T(2,128)S(1)}, f32[2,1280]{1,0:T(2,128)}, u32[]{:S(2)}) copy-start(f32[2,1280]{1,0:T(2,128)} %gain_in.1) | copy-start | bytes 30724
  36.3 36.0 %copy-start.12 = (f32[2,640]{1,0:T(2,128)S(1)}, f32[2,640]{1,0:T(2,128)}, u32[]{:S(2)}) copy-start(f32[2,640]{1,0:T(2,128)} %gain_out.3) | copy-start | bytes 15364
  36.3 16.0 %collective-permute-start.8 = (bf16[2,320,640]{2,1,0:T(8,128)(2,1)S(1)}, bf16[2,320,640]{2,1,0:T(8,128)(2,1)S(1)}, u32[]{:S(2)}, u32[]{:S(2)}) collective-permute-start(bf16[2,320,640]{2,1,0:T(8,128)(2,1)S(1)} %copy-done.5), channel_id=1, source_target_pairs={{0,1},{1,0},{2,3},{3,2},{4,5},{5,4},{6,7},{7,6},{8,9},{9,8},{10,11... | collective-permute-start | bytes 2457608 | tf_op jit(solution)/shard_map/ppermute | solution.py:287
  36.4 49.1 %collective-permute-start.17 = (bf16[2,160,3200]{2,1,0:T(8,128)(2,1)S(1)}, bf16[2,160,3200]{2,1,0:T(8,128)(2,1)S(1)}, u32[]{:S(2)}, u32[]{:S(2)}) collective-permute-start(bf16[2,160,3200]{2,1,0:T(8,128)(2,1)S(1)} %copy-done.1), channel_id=1, source_target_pairs={{0,1},{1,0},{2,3},{3,2},{4,5},{5,4},{6,7},{7,6},{8,9},{9,8},{10,11... | collective-permute-start | bytes 6144008 | tf_op jit(solution)/shard_map/ppermute | solution.py:287
  38.8 9.8 %collective-permute-start.11 = (bf16[80,1280]{1,0:T(8,128)(2,1)}, bf16[80,1280]{1,0:T(8,128)(2,1)S(1)}, u32[]{:S(2)}, u32[]{:S(2)}) collective-permute-start(bf16[80,1280]{1,0:T(8,128)(2,1)} %collective-permute-done.9.rest_4_), channel_id=1, source_target_pairs={{0,8},{4,12},{8,0},{12,4},{16,24},{20,28},{24,16},{28,20},{1,9},{5... | collective-permute-start | bytes 614408 | tf_op jit(solution)/shard_map/ppermute | solution.py:293
  42.4 9.3 %collective-permute-start.12 = (bf16[80,1280]{1,0:T(8,128)(2,1)}, bf16[80,1280]{1,0:T(8,128)(2,1)S(1)}, u32[]{:S(2)}, u32[]{:S(2)}) collective-permute-start(bf16[80,1280]{1,0:T(8,128)(2,1)} %collective-permute-done.9.rest_4_), channel_id=1, source_target_pairs={{0,12},{4,8},{8,4},{12,0},{16,28},{20,24},{24,20},{28,16},{1,13},{... | collective-permute-start | bytes 614408 | tf_op jit(solution)/shard_map/ppermute | solution.py:293
  48.6 5.1 %collective-permute-start.6 = (bf16[32,3200]{1,0:T(8,128)(2,1)S(1)}, bf16[32,3200]{1,0:T(8,128)(2,1)S(1)}, u32[]{:S(2)}, u32[]{:S(2)}) collective-permute-start(bf16[32,3200]{1,0:T(8,128)(2,1)S(1)} %add_convert_fusion), channel_id=1, source_target_pairs={{0,1},{1,0},{2,3},{3,2},{4,5},{5,4},{6,7},{7,6},{8,9},{9,8},{10,11... | collective-permute-start | bytes 614408 | tf_op jit(solution)/shard_map/ppermute | solution.py:287
  51.7 3.8 %collective-permute-start.14 = (bf16[80,1280]{1,0:T(8,128)(2,1)S(1)}, bf16[80,1280]{1,0:T(8,128)(2,1)S(1)}, u32[]{:S(2)}, u32[]{:S(2)}) collective-permute-start(bf16[80,1280]{1,0:T(8,128)(2,1)S(1)} %collective-permute-done.10.rest_5_), channel_id=1, source_target_pairs={{0,1},{1,0},{2,3},{3,2},{4,5},{5,4},{6,7},{7,6},{8,9},{9,8},{10,11... | collective-permute-start | bytes 614408 | tf_op jit(solution)/shard_map/ppermute | solution.py:287
  51.7 4.3 %collective-permute-start.15 = (bf16[80,1280]{1,0:T(8,128)(2,1)S(1)}, bf16[80,1280]{1,0:T(8,128)(2,1)S(1)}, u32[]{:S(2)}, u32[]{:S(2)}) collective-permute-start(bf16[80,1280]{1,0:T(8,128)(2,1)S(1)} %collective-permute-done.11.rest_6_), channel_id=1, source_target_pairs={{0,1},{1,0},{2,3},{3,2},{4,5},{5,4},{6,7},{7,6},{8,9},{9,8},{10,11... | collective-permute-start | bytes 614408 | tf_op jit(solution)/shard_map/ppermute | solution.py:287
  52.4 10.9 %collective-permute-start.19 = (bf16[80,2304]{1,0:T(8,128)(2,1)}, bf16[80,2304]{1,0:T(8,128)(2,1)S(1)}, u32[]{:S(2)}, u32[]{:S(2)}) collective-permute-start(bf16[80,2304]{1,0:T(8,128)(2,1)} %collective-permute-done.18.rest_4_), channel_id=1, source_target_pairs={{0,4},{4,0},{8,12},{12,8},{16,20},{20,16},{24,28},{28,24},{1,5},{5... | collective-permute-start | bytes 1105928 | tf_op jit(solution)/shard_map/ppermute | solution.py:293
  53.7 11.7 %collective-permute-start.20 = (bf16[80,2304]{1,0:T(8,128)(2,1)}, bf16[80,2304]{1,0:T(8,128)(2,1)S(1)}, u32[]{:S(2)}, u32[]{:S(2)}) collective-permute-start(bf16[80,2304]{1,0:T(8,128)(2,1)} %collective-permute-done.18.rest_4_), channel_id=1, source_target_pairs={{0,8},{4,12},{8,0},{12,4},{16,24},{20,28},{24,16},{28,20},{1,9},{5... | collective-permute-start | bytes 1105928 | tf_op jit(solution)/shard_map/ppermute | solution.py:293
  55.4 16.8 %collective-permute-start.21 = (bf16[80,2304]{1,0:T(8,128)(2,1)}, bf16[80,2304]{1,0:T(8,128)(2,1)S(1)}, u32[]{:S(2)}, u32[]{:S(2)}) collective-permute-start(bf16[80,2304]{1,0:T(8,128)(2,1)} %collective-permute-done.18.rest_4_), channel_id=1, source_target_pairs={{0,12},{4,8},{8,4},{12,0},{16,28},{20,24},{24,20},{28,16},{1,13},{... | collective-permute-start | bytes 1105928 | tf_op jit(solution)/shard_map/ppermute | solution.py:293
  56.0 1.5 %collective-permute-start.16 = (bf16[80,1280]{1,0:T(8,128)(2,1)S(1)}, bf16[80,1280]{1,0:T(8,128)(2,1)S(1)}, u32[]{:S(2)}, u32[]{:S(2)}) collective-permute-start(bf16[80,1280]{1,0:T(8,128)(2,1)S(1)} %collective-permute-done.12.rest_7_), channel_id=1, source_target_pairs={{0,1},{1,0},{2,3},{3,2},{4,5},{5,4},{6,7},{7,6},{8,9},{9,8},{10,11... | collective-permute-start | bytes 614408 | tf_op jit(solution)/shard_map/ppermute | solution.py:287
  57.4 28.1 %collective-permute-start.22 = (bf16[80,2304]{1,0:T(8,128)(2,1)}, bf16[80,2304]{1,0:T(8,128)(2,1)S(1)}, u32[]{:S(2)}, u32[]{:S(2)}) collective-permute-start(bf16[80,2304]{1,0:T(8,128)(2,1)} %collective-permute-done.18.rest_4_), channel_id=1, source_target_pairs={{0,1},{1,0},{2,3},{3,2},{4,5},{5,4},{6,7},{7,6},{8,9},{9,8},{10,11... | collective-permute-start | bytes 1105928 | tf_op jit(solution)/shard_map/ppermute | solution.py:287
  63.3 22.2 %collective-permute-start.23 = (bf16[80,2304]{1,0:T(8,128)(2,1)S(1)}, bf16[80,2304]{1,0:T(8,128)(2,1)S(1)}, u32[]{:S(2)}, u32[]{:S(2)}) collective-permute-start(bf16[80,2304]{1,0:T(8,128)(2,1)S(1)} %collective-permute-done.19.rest_5_), channel_id=1, source_target_pairs={{0,1},{1,0},{2,3},{3,2},{4,5},{5,4},{6,7},{7,6},{8,9},{9,8},{10,11... | collective-permute-start | bytes 1105928 | tf_op jit(solution)/shard_map/ppermute | solution.py:287
  65.4 20.1 %collective-permute-start.24 = (bf16[80,2304]{1,0:T(8,128)(2,1)S(1)}, bf16[80,2304]{1,0:T(8,128)(2,1)S(1)}, u32[]{:S(2)}, u32[]{:S(2)}) collective-permute-start(bf16[80,2304]{1,0:T(8,128)(2,1)S(1)} %collective-permute-done.20.rest_6_), channel_id=1, source_target_pairs={{0,1},{1,0},{2,3},{3,2},{4,5},{5,4},{6,7},{7,6},{8,9},{9,8},{10,11... | collective-permute-start | bytes 1105928 | tf_op jit(solution)/shard_map/ppermute | solution.py:287
  72.3 13.3 %collective-permute-start.25 = (bf16[80,2304]{1,0:T(8,128)(2,1)S(1)}, bf16[80,2304]{1,0:T(8,128)(2,1)S(1)}, u32[]{:S(2)}, u32[]{:S(2)}) collective-permute-start(bf16[80,2304]{1,0:T(8,128)(2,1)S(1)} %collective-permute-done.21.rest_7_), channel_id=1, source_target_pairs={{0,1},{1,0},{2,3},{3,2},{4,5},{5,4},{6,7},{7,6},{8,9},{9,8},{10,11... | collective-permute-start | bytes 1105928 | tf_op jit(solution)/shard_map/ppermute | solution.py:287
  (11 other events, 22.9 us)

commit v2 on v1

--- a/solution.py
+++ b/solution.py
@@ -18,18 +18,18 @@
 HALF = KERNEL // 2
 EDGE = HALF * DIL1
 REACH = EDGE + HALF * DIL0
-VMEM_LIMIT = 44 * 1024 * 1024
 BF = jnp.bfloat16
 F32 = jnp.float32
 VMEM = pl.BlockSpec(memory_space=pltpu.VMEM)
 SMEM = pl.BlockSpec(memory_space=pltpu.SMEM)
 ANY = pl.BlockSpec(memory_space=pl.ANY)
+HBM = pl.BlockSpec(memory_space=pltpu.HBM)
 CUT_A = 18 * 128
 CUT_B = 17 * 128
 
 
-def params():
-    return pltpu.CompilerParams(vmem_limit_bytes=VMEM_LIMIT)
+def params(mib):
+    return pltpu.CompilerParams(vmem_limit_bytes=mib * 1024 * 1024)
 
 
 def gelu(x):
@@ -112,7 +112,8 @@
     part[...] = dot(mine, w[...])
 
 
-def table_kernel(own, other, gain, w_all, out, w, sem):
+def table_kernel(split, own, other, gain, w_all, *rest):
+    *outs, w, full, sem = rest
     copy = pltpu.make_async_copy(w_all.at[0], w, sem)
     copy.start()
     wide = own[...] + other[...].astype(F32)
@@ -120,14 +121,44 @@
     rows = w.shape[0]
     mine = dot(t, pick(t.shape[1], rows, lax.axis_index("roll") * rows)).astype(BF)
     copy.wait()
-    out[...] = dot(mine, w[...]).astype(out.dtype)
-
-
-def rows_kernel(split, span, hot5, hot1, table, taps, gain_out, gain_in, gain_mid, *rest):
+    full[...] = dot(mine, w[...])
+    if split:
+        core = lax.rem(lax.axis_index("roll"), 2)
+        outs[0][...] = full[pl.ds(pl.multiple_of(core * SLOT, SLOT), SLOT)]
+        outs[1][...] = full[pl.ds(pl.multiple_of((1 - core) * SLOT, SLOT), SLOT)].astype(BF)
+    else:
+        outs[0][...] = full[...]
+
+
+def hot_kernel(span, near, hot5, hot1):
+    codes = near[...]
+    count = codes.shape[1]
+    rows = hot5.shape[0]
+    pos = span[0] - HALF * DIL0 + lax.broadcasted_iota(jnp.int32, codes.shape, 1)
+    masked = jnp.where((pos >= 0) & (pos < span[1]), codes, -1)
+    lanes = lax.broadcasted_iota(jnp.int32, (CODES, count), 0)
+    taps = jnp.where(lanes == masked, 1.0, 0.0).T.astype(BF)
+    for k in range(KERNEL):
+        hot5[:, k * CODES : (k + 1) * CODES] = taps[k * DIL0 : k * DIL0 + rows]
+    center = jnp.where(lanes == codes, 1.0, 0.0).T.astype(BF)
+    hot1[...] = center[HALF * DIL0 : HALF * DIL0 + rows]
+
+
+def rows_kernel(split, span, hot5, hot1, table, gain_out, gain_in, gain_mid, *rest):
     *w, ci, hid, tw, wo, wi, sem = rest
     depth = wo.shape[0] - CODES
+    if split:
+        core = lax.rem(lax.axis_index("roll"), 2)
+        taps = ((w[0], core * SLOT, SLOT), (w[1], (1 - core) * SLOT, SLOT))
+        w = w[2:]
+    else:
+        taps = ((w[0], 0, CODES),)
+        w = w[1:]
     first = [
-        pltpu.make_async_copy(taps.at[:, k * H : (k + 1) * H], tw.at[k * CODES : (k + 1) * CODES], sem.at[0])
+        pltpu.make_async_copy(
+            t.at[:, k * H : (k + 1) * H], tw.at[pl.ds(pl.multiple_of(k * CODES + at, 16), n)], sem.at[0]
+        )
+        for t, at, n in taps
         for k in range(KERNEL)
     ]
     first.append(pltpu.make_async_copy(table, wo.at[depth:], sem.at[0]))
@@ -292,23 +323,22 @@
     def seq_swap(x, bits):
         return lax.ppermute(x, "seq", [(i, i ^ bits) for i in range(seqs)])
 
+    span = jnp.stack([(seq_at * rows).astype(jnp.int32) - EDGE, lengths[0]])
+    wide_rows = rows + 2 * EDGE
+    codes = tokens[0] + SLOT * breaks[0]
+
     if split:
         shard = w_out.shape[1] // 2
         part_a, part_b = pl.pallas_call(
             part_kernel,
             out_shape=(jax.ShapeDtypeStruct((shard, width), BF), jax.ShapeDtypeStruct((shard, CUT_A), BF)),
-            in_specs=[ANY] * 3,
-            out_specs=(ANY, ANY),
+            in_specs=[HBM] * 3,
+            out_specs=(HBM, HBM),
             scratch_shapes=[pltpu.SemaphoreType.DMA],
-            compiler_params=params(),
+            compiler_params=params(4),
         )(w_in, conv_w, w_out)
         far_a = x_swap(part_a)
         near_in, near_conv, near_out = core_swap(w_in), core_swap(conv_w), core_swap(w_out)
-    else:
-        out0 = lax.all_gather(w_out[0], "roll", axis=0, tiled=True)
-        in1 = lax.all_gather(w_in[1], "roll", axis=0, tiled=True)
-        conv1 = lax.all_gather(conv_w[1], "roll", axis=0, tiled=True)
-        out1 = lax.all_gather(w_out[1], "roll", axis=0, tiled=True)
 
     table, part = pl.pallas_call(
         embed_kernel,
@@ -316,82 +346,90 @@
             jax.ShapeDtypeStruct((CODES, width), BF),
             jax.ShapeDtypeStruct((CODES, H), F32),
         ),
-        in_specs=[VMEM, VMEM, VMEM, ANY],
+        in_specs=[VMEM, VMEM, VMEM, HBM],
         out_specs=(VMEM, VMEM),
         scratch_shapes=[
             pltpu.VMEM((CODES, width), F32),
             pltpu.VMEM(w_in.shape[1:], BF),
             pltpu.SemaphoreType.DMA,
         ],
-        compiler_params=params(),
+        compiler_params=params(12),
     )(embed_table, break_vec[None], gain_in, w_in)
 
     if split:
         own = part + core_swap(part)
         other = x_swap(own.astype(BF))
+        codes = after(codes, own)
+        low = seq_at % 2 == 0
+        ends = codes[rows - REACH :], codes[:REACH]
+        even = seq_swap(jnp.where(low, *ends), 1)
+        pairs = [(i, i + 1) for i in range(1, seqs - 1, 2)]
+        odd = lax.ppermute(jnp.where(low, *ends[::-1]), "seq", pairs + [(j, i) for i, j in pairs])
+        before, behind = jnp.where(low, odd, even), jnp.where(low, even, odd)
+        far_b = x_swap(after(part_b, own))
+        other = after(other, near_in, near_conv, near_out)
     else:
         own = lax.psum(part, "roll")
         other = jnp.zeros((CODES, H), BF)
-
-    codes = tokens[0] + SLOT * breaks[0]
-    if split:
-        codes = after(codes, own)
-    up = [(i, i + 1) for i in range(seqs - 1)]
-    down = [(i + 1, i) for i in range(seqs - 1)]
-    near = jnp.concatenate(
-        [lax.ppermute(codes[rows - REACH :], "seq", up), codes, lax.ppermute(codes[:REACH], "seq", down)]
-    )
-    if split:
-        far_b = x_swap(after(part_b, own))
-
+        pairs = [(i, i + 1) for i in range(seqs - 1)]
+        before = lax.ppermute(codes[rows - REACH :], "seq", pairs)
+        behind = lax.ppermute(codes[:REACH], "seq", [(j, i) for i, j in pairs])
+    count = rows + 2 * REACH
+    spare = jnp.zeros((-count % 128,), jnp.int32)
+    near = jnp.concatenate([before, codes, behind, spare])[None]
+
+    wide = KERNEL * H
+    shapes = [(SLOT, F32), (SLOT, BF)] if split else [(CODES, F32)]
     taps = pl.pallas_call(
-        table_kernel,
-        out_shape=jax.ShapeDtypeStruct((CODES, KERNEL * H), BF),
-        in_specs=[VMEM, VMEM, VMEM, ANY],
-        out_specs=VMEM,
-        scratch_shapes=[pltpu.VMEM(conv_w.shape[1:], BF), pltpu.SemaphoreType.DMA],
-        compiler_params=params(),
+        functools.partial(table_kernel, split),
+        out_shape=[jax.ShapeDtypeStruct((n, wide), t) for n, t in shapes],
+        in_specs=[VMEM, VMEM, VMEM, HBM],
+        out_specs=[VMEM] * len(shapes),
+        scratch_shapes=[
+            pltpu.VMEM(conv_w.shape[1:], BF),
+            pltpu.VMEM((CODES, wide), F32),
+            pltpu.SemaphoreType.DMA,
+        ],
+        compiler_params=params(12),
     )(own, other, gain_mid, conv_w)
     if split:
-        core = roll_at % 2
-        mine = lax.dynamic_slice_in_dim(taps, core * SLOT, SLOT, axis=0)
-        theirs = lax.dynamic_slice_in_dim(taps, (1 - core) * SLOT, SLOT, axis=0)
-        mine = mine.astype(F32) + core_swap(theirs).astype(F32)
+        mine = taps[0] + core_swap(taps[1]).astype(F32)
         sent = mine.astype(BF)
         relay = after(far_a, sent)
         parts_a = [far_a] + [seq_swap(relay, b) for b in (1, 2, 3)]
-        mine = (mine + x_swap(sent).astype(F32)).astype(BF)
+        near = after(near, sent)
+        other = x_swap(sent)
+
+    hot5, hot1 = pl.pallas_call(
+        hot_kernel,
+        out_shape=(
+            jax.ShapeDtypeStruct((wide_rows, KERNEL * CODES), BF),
+            jax.ShapeDtypeStruct((wide_rows, CODES), BF),
+        ),
+        in_specs=[SMEM, VMEM],
+        out_specs=(VMEM, VMEM),
+        compiler_params=params(12),
+    )(span, near)
+
+    if split:
+        mine = (mine + after(other, hot1).astype(F32)).astype(BF)
         theirs = core_swap(mine)
-        first = core == 0
-        taps = jnp.concatenate([jnp.where(first, mine, theirs), jnp.where(first, theirs, mine)], axis=0)
+        near_a = [core_swap(relay)] + [core_swap(after(p, theirs)) for p in parts_a[1:]]
         relay = after(far_b, mine)
         parts_b = [far_b] + [seq_swap(relay, b) for b in (1, 2, 3)]
-        near_a = [core_swap(p) for p in parts_a]
-        near_b = [core_swap(p) for p in parts_b]
-        weights_a = [w_out, w_in, near_out, near_in] + parts_a + near_a
-        weights_b = [conv_w, w_out, near_conv, near_out] + parts_b + near_b
-    else:
-        taps = lax.psum(taps.astype(F32), "roll").astype(BF)
-        weights_a, weights_b = [out0, in1], [conv1, out1]
-
-    begin = seq_at * rows
-    pos = begin - REACH + jnp.arange(rows + 2 * REACH, dtype=jnp.int32)
-    near_valid = jnp.where((pos >= 0) & (pos < lengths[0]), near, -1)
-    wide_rows = rows + 2 * EDGE
-    lanes = jnp.arange(CODES, dtype=jnp.int32)
-    tap_codes = jnp.stack([near_valid[k * DIL0 : k * DIL0 + wide_rows] for k in range(KERNEL)], axis=1)
-    hot5 = (tap_codes[:, :, None] == lanes).astype(BF).reshape(wide_rows, KERNEL * CODES)
-    center = near[HALF * DIL0 : HALF * DIL0 + wide_rows]
-    hot1 = (center[:, None] == lanes).astype(BF)
-
-    span = jnp.stack([begin.astype(jnp.int32) - EDGE, lengths[0]])
+        weights_a = [mine, theirs, w_out, w_in, near_out, near_in] + parts_a + near_a
+    else:
+        taps = lax.psum(taps[0], "roll").astype(BF)
+        gather = lambda w: lax.all_gather(w, "roll", axis=0, tiled=True)
+        weights_a, weights_b = [taps, gather(w_out[0]), gather(w_in[1])], [gather(conv_w[1]), gather(w_out[1])]
+
     ci, hid = pl.pallas_call(
         functools.partial(rows_kernel, split),
         out_shape=(
             jax.ShapeDtypeStruct((wide_rows, H), BF),
             jax.ShapeDtypeStruct((rows, width), BF),
         ),
-        in_specs=[SMEM, VMEM, VMEM, ANY, ANY, VMEM, VMEM, VMEM] + [ANY] * len(weights_a),
+        in_specs=[SMEM, VMEM, VMEM, ANY, VMEM, VMEM, VMEM] + [HBM if w is w_out or w is w_in else ANY for w in weights_a],
         out_specs=(VMEM, VMEM),
         scratch_shapes=[
             pltpu.VMEM((KERNEL * CODES, H), BF),
@@ -399,20 +437,23 @@
             pltpu.VMEM((width, H), BF),
             pltpu.SemaphoreType.DMA((3,)),
         ],
-        compiler_params=params(),
-    )(span, hot5, hot1, table, taps, gain_out, gain_in, gain_mid, *weights_a)
-
+        compiler_params=params(36),
+    )(span, hot5, hot1, table, gain_out, gain_in, gain_mid, *weights_a)
+
+    if split:
+        near_b = [core_swap(after(p, ci)) for p in parts_b]
+        weights_b = [conv_w, w_out, near_conv, near_out] + parts_b + near_b
     out = pl.pallas_call(
         functools.partial(last_kernel, split),
         out_shape=jax.ShapeDtypeStruct((rows, width), BF),
-        in_specs=[VMEM] * 3 + [ANY] * len(weights_b),
+        in_specs=[VMEM] * 3 + [HBM if w is w_out or w is conv_w else ANY for w in weights_b],
         out_specs=VMEM,
         scratch_shapes=[
             pltpu.VMEM((KERNEL * H, H), BF),
             pltpu.VMEM((H, width), BF),
             pltpu.SemaphoreType.DMA((2,)),
         ],
-        compiler_params=params(),
+        compiler_params=params(24),
     )(ci, hid, gain_out, *weights_b)
     return out[None]
 

time: 95.1 us -> 82.3 us (0.87)
  local copies, waits for them, and re-layouts: 14.2 us -> 6.74 us
  waiting for transfers between devices: 29 us -> 24.9 us
  other arithmetic: 3.94 us -> 2.01 us
  Pallas kernels: 23.5 us -> 24.9 us
    ppermute x6 -> x7, waiting for transfers between devices: 22.5 us -> 8.51 us  [seq_swap(): return lax.ppermute(x, 'seq', [(i, i ^ bits) for i in range(seqs)])]
    ppermute x4, waiting for transfers between devices: 3.07 us -> 12.9 us  [x_swap(): return lax.ppermute(x, 'roll', [(i, i ^ 2) for i in range(rolls)])]
    eq x4 -> x0, local copies, waits for them, and re-layouts: 4.25 us -> none  [per_device(): tap_codes[:, :, None] == lanes]
    ppermute x2 -> x1, starting transfers between devices: 4.71 us -> 0.65 us  [per_device(): lax.ppermute(jnp.where(low, *ends[::-1]), 'seq', pairs + [(j, i) for i, j...]
    ppermute x6 -> x7, starting transfers between devices: 10.2 us -> 13.1 us  [seq_swap(): return lax.ppermute(x, 'seq', [(i, i ^ bits) for i in range(seqs)])]
    unnamed x34 -> x30, local copies, waits for them, and re-layouts: 8.24 us -> 5.95 us
    ppermute x14, waiting for transfers between devices: 1.44 us -> 3.49 us  [core_swap(): return lax.ppermute(x, 'roll', [(i, i ^ 1) for i in range(rolls)])]
    ppermute x2 -> x1, waiting for transfers between devices: 2.03 us -> 0.01 us  [per_device(): lax.ppermute(jnp.where(low, *ends[::-1]), 'seq', pairs + [(j, i) for i, j...]
  transfers between devices with their start and end apart: 26 -> 26, of which waited for: 9 -> 10; matrix products, arithmetic and copies ran while one was open for 10% -> 3% of each run, Pallas kernels for 16% -> 21%
where the time goes in v2:
time: 82.3 us; the launch traced here: 81.9 us
  Pallas kernels  24.9 us (30%)
  waiting for transfers between devices  24.9 us (30%)
  starting transfers between devices  22.2 us (27%)
  local copies, waits for them, and re-layouts  6.74 us (8%)
  other arithmetic  2.01 us (2%)
  between operations  1.06 us (1%)
    pallas_call x1, Pallas kernels, per_device(): pl.pallas_call(functools.partial(rows_kernel, split), out_shape=(jax.Shap...  13.3 us
    ppermute x7, starting transfers between devices, seq_swap(): return lax.ppermute(x, 'seq', [(i, i ^ bits) for i in range(seqs)])  13.1 us
    ppermute x4, waiting for transfers between devices, x_swap(): return lax.ppermute(x, 'roll', [(i, i ^ 2) for i in range(rolls)])  12.9 us
    ppermute x7, waiting for transfers between devices, seq_swap(): return lax.ppermute(x, 'seq', [(i, i ^ bits) for i in range(seqs)])  8.51 us
    pallas_call x1, Pallas kernels, per_device(): pl.pallas_call(functools.partial(last_kernel, split), out_shape=jax.Shape...  7.56 us
    unnamed x30, local copies, waits for them, and re-layouts  5.95 us
    ppermute x4, starting transfers between devices, x_swap(): return lax.ppermute(x, 'roll', [(i, i ^ 2) for i in range(rolls)])  5.18 us
    ppermute x14, waiting for transfers between devices, core_swap(): return lax.ppermute(x, 'roll', [(i, i ^ 1) for i in range(rolls)])  3.49 us
  transfers between devices with their start and end apart: 26, of which 10 were waited for; matrix products, arithmetic and copies ran while one was open for 3% of the time, Pallas kernels for 21%

profile of v2, /device:TPU:0, one launch (start us, length us, event | category | flops | bytes accessed | tf_op | source)
XLA Modules:
  0.0 81.9 jit_solution(15551481968495638933)
XLA Ops:
  1.0 0.7 broadcast_in_dim.9.brk
  1.7 1.1 %copy-done.3 = bf16[2,320,640]{2,1,0:T(8,128)(2,1)S(1)} copy-done((bf16[2,320,640]{2,1,0:T(8,128)(2,1)S(1)}, bf16[2,320,640]{2,1,0:T(8,128)(2,1)}, u32[]{:S(2)}) %copy-start.3) | copy-done | bytes 819224
  2.8 0.9 %copy-done.7 = f32[30,1280]{1,0:T(8,128)S(1)} copy-done((f32[30,1280]{1,0:T(8,128)S(1)}, f32[30,1280]{1,0:T(8,128)}, u32[]{:S(2)}) %copy-start.7) | copy-done | bytes 153624
  3.7 0.7 copy-done.8
  4.4 1.1 %shard_map.109 = (bf16[64,1280]{1,0:T(8,128)(2,1)S(1)}, f32[64,640]{1,0:T(8,128)S(1)}) custom-call(f32[30,1280]{1,0:T(8,128)S(1)} %copy-done.7, f32[1,1280]{1,0:T(1,128)S(1)} %broadcast_in_dim.9.brk, f32[2,1280]{1,0:T(2,128)S(1)} %copy-done.8, bf16[2,320,640]{2,1,0:T(8,128)(2,1)S(1)} %copy-done.3), custom_call_target="tpu_custom_call" | custom-call | tf_op jit(solution)/shard_map/pallas_call | solution.py:343
  5.7 1.6 %copy-done = bf16[2,160,3200]{2,1,0:T(8,128)(2,1)S(1)} copy-done((bf16[2,160,3200]{2,1,0:T(8,128)(2,1)S(1)}, bf16[2,160,3200]{2,1,0:T(8,128)(2,1)}, u32[]{:S(2)}) %copy-start) | copy-done | bytes 2048024
  7.2 0.8 %shard_map.112 = (bf16[80,1280]{1,0:T(8,128)(2,1)}, bf16[80,2304]{1,0:T(8,128)(2,1)}) custom-call(bf16[2,320,640]{2,1,0:T(8,128)(2,1)S(1)} %copy-done.3, bf16[2,160,3200]{2,1,0:T(8,128)(2,1)S(1)} %copy-done, bf16[2,160,1280]{2,1,0:T(8,128)(2,1)S(1)} %copy-done.2), custom_call_target="tpu_custom_call" | custom-call | tf_op jit(solution)/shard_map/pallas_call | solution.py:332
  8.1 3.0 %collective-permute-start.10 = (bf16[80,1280]{1,0:T(8,128)(2,1)}, bf16[80,1280]{1,0:T(8,128)(2,1)S(1)}, u32[]{:S(2)}, u32[]{:S(2)}) collective-permute-start(bf16[80,1280]{1,0:T(8,128)(2,1)} %get-tuple-element.39), channel_id=1, source_target_pairs={{0,2},{1,3},{2,0},{3,1},{4,6},{5,7},{6,4},{7,5},{8,10},{9,11},{10,... | collective-permute-start | bytes 614408 | tf_op jit(solution)/shard_map/ppermute | solution.py:321
  12.0 6.4 %collective-permute-done.3.other = bf16[64,640]{1,0:T(8,128)(2,1)S(1)} collective-permute-done((bf16[64,640]{1,0:T(8,128)(2,1)S(1)}, bf16[64,640]{1,0:T(8,128)(2,1)S(1)}, u32[]{:S(2)}, u32[]{:S(2)}) %collective-permute-start.3) | collective-permute-done | bytes 81952 | tf_op jit(solution)/shard_map/ppermute | solution.py:321
  18.4 1.2 %shard_map.110 = (f32[32,3200]{1,0:T(8,128)S(1)}, bf16[32,3200]{1,0:T(8,128)(2,1)S(1)}) custom-call(f32[64,640]{1,0:T(8,128)S(1)} %get-tuple-element.54.own, bf16[64,640]{1,0:T(8,128)(2,1)S(1)} %collective-permute-done.3.other, f32[2,640]{1,0:T(2,128)S(1)} %copy-done.10, bf16[2,160,3200]{2,1,0:T(8,128)(2,1)S(1)} %copy-done.1), custom_call_target="tpu_custom_call" | custom-call | tf_op jit(solution)/shard_map/pallas_call | solution.py:383
  19.8 1.8 %collective-permute-start.2 = (s32[384]{0:T(512)S(1)}, s32[384]{0:T(512)S(1)}, u32[]{:S(2)}, u32[]{:S(2)}) collective-permute-start(s32[384]{0:T(512)S(1)} %get-tuple-element.57), channel_id=1, source_target_pairs={{0,4},{4,0},{8,12},{12,8},{16,20},{20,16},{24,28},{28,24},{1,5},{5... | collective-permute-start | bytes 4616 | tf_op jit(solution)/shard_map/ppermute | solution.py:324
  21.5 0.6 collective-permute-start.1
  22.2 1.6 %collective-permute-start.18 = (bf16[80,2304]{1,0:T(8,128)(2,1)}, bf16[80,2304]{1,0:T(8,128)(2,1)}, u32[]{:S(2)}, u32[]{:S(2)}) collective-permute-start(bf16[80,2304]{1,0:T(8,128)(2,1)} %get-tuple-element.47), channel_id=1, source_target_pairs={{0,2},{1,3},{2,0},{3,1},{4,6},{5,7},{6,4},{7,5},{8,10},{9,11},{10,... | collective-permute-start | bytes 1105928 | tf_op jit(solution)/shard_map/ppermute | solution.py:321
  23.7 0.7 copy-done.12
  24.4 0.7 fusion
  25.1 0.5 collective-permute-start.8
  25.8 4.3 %collective-permute-start.11 = (bf16[80,1280]{1,0:T(8,128)(2,1)S(1)}, bf16[80,1280]{1,0:T(8,128)(2,1)S(1)}, u32[]{:S(2)}, u32[]{:S(2)}) collective-permute-start(bf16[80,1280]{1,0:T(8,128)(2,1)S(1)} %collective-permute-done.10.rest_6_), channel_id=1, source_target_pairs={{0,4},{4,0},{8,12},{12,8},{16,20},{20,16},{24,28},{28,24},{1,5},{5... | collective-permute-start | bytes 614408 | tf_op jit(solution)/shard_map/ppermute | solution.py:324
  30.1 1.0 %shard_map.111 = (bf16[1008,320]{1,0:T(8,128)(2,1)S(1)}, bf16[1008,64]{1,0:T(8,128)(2,1)S(1)}) custom-call(s32[2]{0:T(128)S(1)} %pad_add_fusion.span, s32[1,1280]{1,0:T(1,128)S(1)} %broadcast_in_dim.10.near), custom_call_target="tpu_custom_call" | custom-call | tf_op jit(solution)/shard_map/pallas_call | solution.py:403
  31.1 6.5 %collective-permute-done.8 = bf16[32,3200]{1,0:T(8,128)(2,1)} collective-permute-done((bf16[32,3200]{1,0:T(8,128)(2,1)}, bf16[32,3200]{1,0:T(8,128)(2,1)}, u32[]{:S(2)}, u32[]{:S(2)}) %collective-permute-start.8) | collective-permute-done | bytes 204832 | tf_op jit(solution)/shard_map/ppermute | solution.py:321
  37.7 1.1 %add_convert_fusion.rest_0_ = bf16[32,3200]{1,0:T(8,128)(2,1)S(1)} fusion(bf16[32,3200]{1,0:T(8,128)(2,1)} %collective-permute-done.8, f32[32,3200]{1,0:T(8,128)S(1)} %get-tuple-element.32, bf16[32,3200]{1,0:T(8,128)(2,1)} %copy-done.12), kind=kLoop, calls=%fused_computation | loop fusion | flops 512000 | bytes 1024000 | tf_op jit(solution)/shard_map/convert_element_type | solution.py:415
  38.8 5.1 %collective-permute-start.13 = (bf16[80,1280]{1,0:T(8,128)(2,1)S(1)}, bf16[80,1280]{1,0:T(8,128)(2,1)S(1)}, u32[]{:S(2)}, u32[]{:S(2)}) collective-permute-start(bf16[80,1280]{1,0:T(8,128)(2,1)S(1)} %collective-permute-done.10.rest_6_), channel_id=1, source_target_pairs={{0,12},{4,8},{8,4},{12,0},{16,28},{20,24},{24,20},{28,16},{1,13},{... | collective-permute-start | bytes 614408 | tf_op jit(solution)/shard_map/ppermute | solution.py:324
  44.9 0.6 collective-permute-start.21
  45.5 4.4 %collective-permute-done.13.rest_9_ = bf16[80,1280]{1,0:T(8,128)(2,1)S(1)} collective-permute-done((bf16[80,1280]{1,0:T(8,128)(2,1)S(1)}, bf16[80,1280]{1,0:T(8,128)(2,1)S(1)}, u32[]{:S(2)}, u32[]{:S(2)}) %collective-permute-start.13) | collective-permute-done | bytes 204832 | tf_op jit(solution)/shard_map/ppermute | solution.py:324
  49.9 0.7 collective-permute-start.20
  50.5 4.1 %collective-permute-done.12.rest_8_ = bf16[80,1280]{1,0:T(8,128)(2,1)S(1)} collective-permute-done((bf16[80,1280]{1,0:T(8,128)(2,1)S(1)}, bf16[80,1280]{1,0:T(8,128)(2,1)S(1)}, u32[]{:S(2)}, u32[]{:S(2)}) %collective-permute-start.12) | collective-permute-done | bytes 204832 | tf_op jit(solution)/shard_map/ppermute | solution.py:324
  55.3 0.9 %collective-permute-done.16.rest_12_ = bf16[80,1280]{1,0:T(8,128)(2,1)S(1)} collective-permute-done((bf16[80,1280]{1,0:T(8,128)(2,1)S(1)}, bf16[80,1280]{1,0:T(8,128)(2,1)S(1)}, u32[]{:S(2)}, u32[]{:S(2)}) %collective-permute-start.16) | collective-permute-done | bytes 204832 | tf_op jit(solution)/shard_map/ppermute | solution.py:318
  56.6 0.9 %copy-done.6 = bf16[64,1280]{1,0:T(8,128)(2,1)S(1)} copy-done((bf16[64,1280]{1,0:T(8,128)(2,1)S(1)}, bf16[64,1280]{1,0:T(8,128)(2,1)}, u32[]{:S(2)}) %copy-start.6) | copy-done | bytes 163864
  57.5 13.3 %shard_map.113 = (bf16[1008,640]{1,0:T(8,128)(2,1)S(1)}, bf16[496,1280]{1,0:T(8,128)(2,1)S(1)}) custom-call(s32[2]{0:T(128)S(1)} %pad_add_fusion.span, bf16[1008,320]{1,0:T(8,128)(2,1)S(1)} %get-tuple-element.35.hot5, bf16[1008,64]{1,0:T(8,128)(2,1)S(1)} %get-tuple-element.36.hot1, bf16[64,1280]{1,0:T(8,128)(2,1)S(1)} %copy-done.6, f32[2,640]{1,0:T(2,128)S(1)} %copy-done.11, ...), custom_call_target="tpu_custom_call" | custom-call | tf_op jit(solution)/shard_map/pallas_call | solution.py:426
  71.9 0.9 %collective-permute-done.22.rest_8_ = bf16[80,2304]{1,0:T(8,128)(2,1)S(1)} collective-permute-done((bf16[80,2304]{1,0:T(8,128)(2,1)}, bf16[80,2304]{1,0:T(8,128)(2,1)S(1)}, u32[]{:S(2)}, u32[]{:S(2)}) %collective-permute-start.22) | collective-permute-done | bytes 368672 | tf_op jit(solution)/shard_map/ppermute | solution.py:318
  73.1 0.5 collective-permute-done.24.rest_10_
  73.6 0.5 collective-permute-done.23.rest_9_
  74.1 7.6 %shard_map.114 = bf16[496,1280]{1,0:T(8,128)(2,1)} custom-call(bf16[1008,640]{1,0:T(8,128)(2,1)S(1)} %get-tuple-element.44.ci, bf16[496,1280]{1,0:T(8,128)(2,1)S(1)} %get-tuple-element.45.hid, f32[2,640]{1,0:T(2,128)S(1)} %copy-done.11, bf16[2,160,3200]{2,1,0:T(8,128)(2,1)S(1)} %copy-done.1, bf16[2,160,1280]{2,1,0:T(8,128)(2,1)S(1)} %copy-done.2, ...), custom_call_target="tpu_custom_call" | custom-call | tf_op jit(solution)/shard_map/pallas_call | solution.py:446
  (67 shorter events, 5.0 us)
Async XLA Ops:
  0.0 5.7 %copy-start.2 = (bf16[2,160,1280]{2,1,0:T(8,128)(2,1)S(1)}, bf16[2,160,1280]{2,1,0:T(8,128)(2,1)}, u32[]{:S(2)}) copy-start(bf16[2,160,1280]{2,1,0:T(8,128)(2,1)} %rest_1_.1) | copy-start | bytes 2457604
  0.0 18.4 %collective-permute-start.5 = (bf16[2,160,3200]{2,1,0:T(8,128)(2,1)}, bf16[2,160,3200]{2,1,0:T(8,128)(2,1)}, u32[]{:S(2)}, u32[]{:S(2)}) collective-permute-start(bf16[2,160,3200]{2,1,0:T(8,128)(2,1)} %rest_0_.1), channel_id=1, source_target_pairs={{0,1},{1,0},{2,3},{3,2},{4,5},{5,4},{6,7},{7,6},{8,9},{9,8},{10,11... | collective-permute-start | bytes 6144008 | tf_op jit(solution)/shard_map/ppermute | solution.py:318
  0.5 17.9 %collective-permute-start.4 = (bf16[2,320,640]{2,1,0:T(8,128)(2,1)}, bf16[2,320,640]{2,1,0:T(8,128)(2,1)}, u32[]{:S(2)}, u32[]{:S(2)}) collective-permute-start(bf16[2,320,640]{2,1,0:T(8,128)(2,1)} %rest_3_.1), channel_id=1, source_target_pairs={{0,1},{1,0},{2,3},{3,2},{4,5},{5,4},{6,7},{7,6},{8,9},{9,8},{10,11... | collective-permute-start | bytes 2457608 | tf_op jit(solution)/shard_map/ppermute | solution.py:318
  0.5 17.8 %collective-permute-start.6 = (bf16[2,160,1280]{2,1,0:T(8,128)(2,1)}, bf16[2,160,1280]{2,1,0:T(8,128)(2,1)}, u32[]{:S(2)}, u32[]{:S(2)}) collective-permute-start(bf16[2,160,1280]{2,1,0:T(8,128)(2,1)} %rest_1_.1), channel_id=1, source_target_pairs={{0,1},{1,0},{2,3},{3,2},{4,5},{5,4},{6,7},{7,6},{8,9},{9,8},{10,11... | collective-permute-start | bytes 2457608 | tf_op jit(solution)/shard_map/ppermute | solution.py:318
  5.5 6.3 %collective-permute-start = (f32[64,640]{1,0:T(8,128)S(1)}, f32[64,640]{1,0:T(8,128)S(1)}, u32[]{:S(2)}, u32[]{:S(2)}) collective-permute-start(f32[64,640]{1,0:T(8,128)S(1)} %get-tuple-element.29), channel_id=1, source_target_pairs={{0,1},{1,0},{2,3},{3,2},{4,5},{5,4},{6,7},{7,6},{8,9},{9,8},{10,11... | collective-permute-start | bytes 491528 | tf_op jit(solution)/shard_map/ppermute | solution.py:318
  7.2 11.1 %copy-start.1 = (bf16[2,160,3200]{2,1,0:T(8,128)(2,1)S(1)}, bf16[2,160,3200]{2,1,0:T(8,128)(2,1)}, u32[]{:S(2)}) copy-start(bf16[2,160,3200]{2,1,0:T(8,128)(2,1)} %rest_0_.1) | copy-start | bytes 6144004
  7.2 11.2 %copy-start.10 = (f32[2,640]{1,0:T(2,128)S(1)}, f32[2,640]{1,0:T(2,128)}, u32[]{:S(2)}) copy-start(f32[2,640]{1,0:T(2,128)} %gain_mid.1) | copy-start | bytes 15364
  8.1 17.7 %collective-permute-start.10 = (bf16[80,1280]{1,0:T(8,128)(2,1)}, bf16[80,1280]{1,0:T(8,128)(2,1)S(1)}, u32[]{:S(2)}, u32[]{:S(2)}) collective-permute-start(bf16[80,1280]{1,0:T(8,128)(2,1)} %get-tuple-element.39), channel_id=1, source_target_pairs={{0,2},{1,3},{2,0},{3,1},{4,6},{5,7},{6,4},{7,5},{8,10},{9,11},{10,... | collective-permute-start | bytes 614408 | tf_op jit(solution)/shard_map/ppermute | solution.py:321
  11.8 6.5 %collective-permute-start.3 = (bf16[64,640]{1,0:T(8,128)(2,1)S(1)}, bf16[64,640]{1,0:T(8,128)(2,1)S(1)}, u32[]{:S(2)}, u32[]{:S(2)}) collective-permute-start(bf16[64,640]{1,0:T(8,128)(2,1)S(1)} %get-tuple-element.53), channel_id=1, source_target_pairs={{0,2},{1,3},{2,0},{3,1},{4,6},{5,7},{6,4},{7,5},{8,10},{9,11},{10,... | collective-permute-start | bytes 245768 | tf_op jit(solution)/shard_map/ppermute | solution.py:321
  19.6 37.0 %copy-start.9 = (f32[2,1280]{1,0:T(2,128)S(1)}, f32[2,1280]{1,0:T(2,128)}, u32[]{:S(2)}) copy-start(f32[2,1280]{1,0:T(2,128)} %gain_in.1) | copy-start | bytes 30724
  19.6 37.0 %copy-start.11 = (f32[2,640]{1,0:T(2,128)S(1)}, f32[2,640]{1,0:T(2,128)}, u32[]{:S(2)}) copy-start(f32[2,640]{1,0:T(2,128)} %gain_out.3) | copy-start | bytes 15364
  19.6 4.1 %collective-permute-start.7 = (bf16[32,3200]{1,0:T(8,128)(2,1)S(1)}, bf16[32,3200]{1,0:T(8,128)(2,1)S(1)}, u32[]{:S(2)}, u32[]{:S(2)}) collective-permute-start(bf16[32,3200]{1,0:T(8,128)(2,1)S(1)} %get-tuple-element.33), channel_id=1, source_target_pairs={{0,1},{1,0},{2,3},{3,2},{4,5},{5,4},{6,7},{7,6},{8,9},{9,8},{10,11... | collective-permute-start | bytes 614408 | tf_op jit(solution)/shard_map/ppermute | solution.py:318
  19.8 5.9 %collective-permute-start.2 = (s32[384]{0:T(512)S(1)}, s32[384]{0:T(512)S(1)}, u32[]{:S(2)}, u32[]{:S(2)}) collective-permute-start(s32[384]{0:T(512)S(1)} %get-tuple-element.57), channel_id=1, source_target_pairs={{0,4},{4,0},{8,12},{12,8},{16,20},{20,16},{24,28},{28,24},{1,5},{5... | collective-permute-start | bytes 4616 | tf_op jit(solution)/shard_map/ppermute | solution.py:324
  21.5 4.2 %collective-permute-start.1 = (s32[384]{0:T(512)S(1)}, s32[384]{0:T(512)S(1)}, u32[]{:S(2)}, u32[]{:S(2)}) collective-permute-start(s32[384]{0:T(512)S(1)} %get-tuple-element.58), channel_id=1, source_target_pairs={{4,8},{12,16},{20,24},{8,4},{16,12},{24,20},{5,9},{13,17},{21,25},... | collective-permute-start | bytes 4616 | tf_op jit(solution)/shard_map/ppermute | solution.py:367
  22.2 22.7 %collective-permute-start.18 = (bf16[80,2304]{1,0:T(8,128)(2,1)}, bf16[80,2304]{1,0:T(8,128)(2,1)}, u32[]{:S(2)}, u32[]{:S(2)}) collective-permute-start(bf16[80,2304]{1,0:T(8,128)(2,1)} %get-tuple-element.47), channel_id=1, source_target_pairs={{0,2},{1,3},{2,0},{3,1},{4,6},{5,7},{6,4},{7,5},{8,10},{9,11},{10,... | collective-permute-start | bytes 1105928 | tf_op jit(solution)/shard_map/ppermute | solution.py:321
  25.1 12.5 %collective-permute-start.8 = (bf16[32,3200]{1,0:T(8,128)(2,1)}, bf16[32,3200]{1,0:T(8,128)(2,1)}, u32[]{:S(2)}, u32[]{:S(2)}) collective-permute-start(bf16[32,3200]{1,0:T(8,128)(2,1)} %fusion), channel_id=1, source_target_pairs={{0,2},{1,3},{2,0},{3,1},{4,6},{5,7},{6,4},{7,5},{8,10},{9,11},{10,... | collective-permute-start | bytes 614408 | tf_op jit(solution)/shard_map/ppermute | solution.py:321
  25.8 30.8 %copy-start.4 = (bf16[2,320,640]{2,1,0:T(8,128)(2,1)S(1)}, bf16[2,320,640]{2,1,0:T(8,128)(2,1)}, u32[]{:S(2)}) copy-start(bf16[2,320,640]{2,1,0:T(8,128)(2,1)} %rest_3_.1) | copy-start | bytes 2457604
  25.8 18.6 %collective-permute-start.11 = (bf16[80,1280]{1,0:T(8,128)(2,1)S(1)}, bf16[80,1280]{1,0:T(8,128)(2,1)S(1)}, u32[]{:S(2)}, u32[]{:S(2)}) collective-permute-start(bf16[80,1280]{1,0:T(8,128)(2,1)S(1)} %collective-permute-done.10.rest_6_), channel_id=1, source_target_pairs={{0,4},{4,0},{8,12},{12,8},{16,20},{20,16},{24,28},{28,24},{1,5},{5... | collective-permute-start | bytes 614408 | tf_op jit(solution)/shard_map/ppermute | solution.py:324
  38.8 5.6 %collective-permute-start.9 = (bf16[32,3200]{1,0:T(8,128)(2,1)S(1)}, bf16[32,3200]{1,0:T(8,128)(2,1)S(1)}, u32[]{:S(2)}, u32[]{:S(2)}) collective-permute-start(bf16[32,3200]{1,0:T(8,128)(2,1)S(1)} %add_convert_fusion.rest_0_), channel_id=1, source_target_pairs={{0,1},{1,0},{2,3},{3,2},{4,5},{5,4},{6,7},{7,6},{8,9},{9,8},{10,11... | collective-permute-start | bytes 614408 | tf_op jit(solution)/shard_map/ppermute | solution.py:318
  38.8 11.0 %collective-permute-start.13 = (bf16[80,1280]{1,0:T(8,128)(2,1)S(1)}, bf16[80,1280]{1,0:T(8,128)(2,1)S(1)}, u32[]{:S(2)}, u32[]{:S(2)}) collective-permute-start(bf16[80,1280]{1,0:T(8,128)(2,1)S(1)} %collective-permute-done.10.rest_6_), channel_id=1, source_target_pairs={{0,12},{4,8},{8,4},{12,0},{16,28},{20,24},{24,20},{28,16},{1,13},{... | collective-permute-start | bytes 614408 | tf_op jit(solution)/shard_map/ppermute | solution.py:324
  43.9 10.7 %collective-permute-start.12 = (bf16[80,1280]{1,0:T(8,128)(2,1)S(1)}, bf16[80,1280]{1,0:T(8,128)(2,1)S(1)}, u32[]{:S(2)}, u32[]{:S(2)}) collective-permute-start(bf16[80,1280]{1,0:T(8,128)(2,1)S(1)} %collective-permute-done.10.rest_6_), channel_id=1, source_target_pairs={{0,8},{4,12},{8,0},{12,4},{16,24},{20,28},{24,16},{28,20},{1,9},{5... | collective-permute-start | bytes 614408 | tf_op jit(solution)/shard_map/ppermute | solution.py:324
  44.4 10.4 %collective-permute-start.14 = (bf16[80,1280]{1,0:T(8,128)(2,1)S(1)}, bf16[80,1280]{1,0:T(8,128)(2,1)S(1)}, u32[]{:S(2)}, u32[]{:S(2)}) collective-permute-start(bf16[80,1280]{1,0:T(8,128)(2,1)S(1)} %collective-permute-done.10.rest_6_), channel_id=1, source_target_pairs={{0,1},{1,0},{2,3},{3,2},{4,5},{5,4},{6,7},{7,6},{8,9},{9,8},{10,11... | collective-permute-start | bytes 614408 | tf_op jit(solution)/shard_map/ppermute | solution.py:318
  44.4 10.4 %collective-permute-start.15 = (bf16[80,1280]{1,0:T(8,128)(2,1)S(1)}, bf16[80,1280]{1,0:T(8,128)(2,1)S(1)}, u32[]{:S(2)}, u32[]{:S(2)}) collective-permute-start(bf16[80,1280]{1,0:T(8,128)(2,1)S(1)} %collective-permute-done.11.rest_7_), channel_id=1, source_target_pairs={{0,1},{1,0},{2,3},{3,2},{4,5},{5,4},{6,7},{7,6},{8,9},{9,8},{10,11... | collective-permute-start | bytes 614408 | tf_op jit(solution)/shard_map/ppermute | solution.py:318
  44.9 26.2 %collective-permute-start.21 = (bf16[80,2304]{1,0:T(8,128)(2,1)}, bf16[80,2304]{1,0:T(8,128)(2,1)S(1)}, u32[]{:S(2)}, u32[]{:S(2)}) collective-permute-start(bf16[80,2304]{1,0:T(8,128)(2,1)} %collective-permute-done.18.rest_4_), channel_id=1, source_target_pairs={{0,12},{4,8},{8,4},{12,0},{16,28},{20,24},{24,20},{28,16},{1,13},{... | collective-permute-start | bytes 1105928 | tf_op jit(solution)/shard_map/ppermute | solution.py:324
  49.9 21.5 %collective-permute-start.20 = (bf16[80,2304]{1,0:T(8,128)(2,1)}, bf16[80,2304]{1,0:T(8,128)(2,1)S(1)}, u32[]{:S(2)}, u32[]{:S(2)}) collective-permute-start(bf16[80,2304]{1,0:T(8,128)(2,1)} %collective-permute-done.18.rest_4_), channel_id=1, source_target_pairs={{0,8},{4,12},{8,0},{12,4},{16,24},{20,28},{24,16},{28,20},{1,9},{5... | collective-permute-start | bytes 1105928 | tf_op jit(solution)/shard_map/ppermute | solution.py:324
  54.6 17.0 %collective-permute-start.19 = (bf16[80,2304]{1,0:T(8,128)(2,1)}, bf16[80,2304]{1,0:T(8,128)(2,1)S(1)}, u32[]{:S(2)}, u32[]{:S(2)}) collective-permute-start(bf16[80,2304]{1,0:T(8,128)(2,1)} %collective-permute-done.18.rest_4_), channel_id=1, source_target_pairs={{0,4},{4,0},{8,12},{12,8},{16,20},{20,16},{24,28},{28,24},{1,5},{5... | collective-permute-start | bytes 1105928 | tf_op jit(solution)/shard_map/ppermute | solution.py:324
  54.8 1.5 %collective-permute-start.16 = (bf16[80,1280]{1,0:T(8,128)(2,1)S(1)}, bf16[80,1280]{1,0:T(8,128)(2,1)S(1)}, u32[]{:S(2)}, u32[]{:S(2)}) collective-permute-start(bf16[80,1280]{1,0:T(8,128)(2,1)S(1)} %collective-permute-done.12.rest_8_), channel_id=1, source_target_pairs={{0,1},{1,0},{2,3},{3,2},{4,5},{5,4},{6,7},{7,6},{8,9},{9,8},{10,11... | collective-permute-start | bytes 614408 | tf_op jit(solution)/shard_map/ppermute | solution.py:318
  54.8 1.7 %collective-permute-start.17 = (bf16[80,1280]{1,0:T(8,128)(2,1)S(1)}, bf16[80,1280]{1,0:T(8,128)(2,1)S(1)}, u32[]{:S(2)}, u32[]{:S(2)}) collective-permute-start(bf16[80,1280]{1,0:T(8,128)(2,1)S(1)} %collective-permute-done.13.rest_9_), channel_id=1, source_target_pairs={{0,1},{1,0},{2,3},{3,2},{4,5},{5,4},{6,7},{7,6},{8,9},{9,8},{10,11... | collective-permute-start | bytes 614408 | tf_op jit(solution)/shard_map/ppermute | solution.py:318
  70.8 2.0 %collective-permute-start.22 = (bf16[80,2304]{1,0:T(8,128)(2,1)}, bf16[80,2304]{1,0:T(8,128)(2,1)S(1)}, u32[]{:S(2)}, u32[]{:S(2)}) collective-permute-start(bf16[80,2304]{1,0:T(8,128)(2,1)} %collective-permute-done.18.rest_4_), channel_id=1, source_target_pairs={{0,1},{1,0},{2,3},{3,2},{4,5},{5,4},{6,7},{7,6},{8,9},{9,8},{10,11... | collective-permute-start | bytes 1105928 | tf_op jit(solution)/shard_map/ppermute | solution.py:318
  71.1 2.0 %collective-permute-start.25 = (bf16[80,2304]{1,0:T(8,128)(2,1)S(1)}, bf16[80,2304]{1,0:T(8,128)(2,1)S(1)}, u32[]{:S(2)}, u32[]{:S(2)}) collective-permute-start(bf16[80,2304]{1,0:T(8,128)(2,1)S(1)} %collective-permute-done.21.rest_7_), channel_id=1, source_target_pairs={{0,1},{1,0},{2,3},{3,2},{4,5},{5,4},{6,7},{7,6},{8,9},{9,8},{10,11... | collective-permute-start | bytes 1105928 | tf_op jit(solution)/shard_map/ppermute | solution.py:318
  71.4 2.2 %collective-permute-start.24 = (bf16[80,2304]{1,0:T(8,128)(2,1)S(1)}, bf16[80,2304]{1,0:T(8,128)(2,1)S(1)}, u32[]{:S(2)}, u32[]{:S(2)}) collective-permute-start(bf16[80,2304]{1,0:T(8,128)(2,1)S(1)} %collective-permute-done.20.rest_6_), channel_id=1, source_target_pairs={{0,1},{1,0},{2,3},{3,2},{4,5},{5,4},{6,7},{7,6},{8,9},{9,8},{10,11... | collective-permute-start | bytes 1105928 | tf_op jit(solution)/shard_map/ppermute | solution.py:318
  71.6 2.5 %collective-permute-start.23 = (bf16[80,2304]{1,0:T(8,128)(2,1)S(1)}, bf16[80,2304]{1,0:T(8,128)(2,1)S(1)}, u32[]{:S(2)}, u32[]{:S(2)}) collective-permute-start(bf16[80,2304]{1,0:T(8,128)(2,1)S(1)} %collective-permute-done.19.rest_5_), channel_id=1, source_target_pairs={{0,1},{1,0},{2,3},{3,2},{4,5},{5,4},{6,7},{7,6},{8,9},{9,8},{10,11... | collective-permute-start | bytes 1105928 | tf_op jit(solution)/shard_map/ppermute | solution.py:318
  (9 other events, 17.5 us)

commit v3 on v2

--- a/solution.py
+++ b/solution.py
@@ -68,48 +68,64 @@
     return jnp.where(i == j + first, 1.0, 0.0).astype(BF)
 
 
-def part_kernel(w_in, conv_w, w_out, a, b, sem):
-    _, _, y, z = place()
-    n = a.shape[0]
-    r = pl.multiple_of(z * n, 16)
-    r2 = pl.multiple_of(z * 2 * n, 16)
+def part_copies(y_is_one, row_bit, w_in, conv_w, w_out, a, b, sem):
+    n = b.shape[0]
+    r = pl.multiple_of(row_bit * n, 16)
+    r2 = pl.multiple_of(row_bit * 2 * n, 16)
     rest = conv_w.shape[2] - CUT_B
-
-    def go(pairs):
-        copies = [pltpu.make_async_copy(s, d, sem) for s, d in pairs]
-        start(copies)
-        wait(copies)
-
-    @pl.when(y == 0)
-    def _():
-        go([
-            (w_out.at[0, pl.ds(r, n)], a),
-            (conv_w.at[1, pl.ds(r, n), 0:CUT_A], b),
-        ])
-
-    @pl.when(y == 1)
-    def _():
-        go([
-            (w_in.at[1, pl.ds(r2, n)], a.at[:, 0:H]),
-            (w_in.at[1, pl.ds(r2 + n, n)], a.at[:, H : 2 * H]),
+    if y_is_one:
+        pairs = [
             (conv_w.at[1, pl.ds(r, n), CUT_B:], b.at[:, 0:rest]),
             (w_out.at[1, pl.ds(r, n)], b.at[:, rest:]),
-        ])
-
-
-def embed_kernel(embed, brk, gain, w_all, table, part, scratch, w, sem):
-    copy = pltpu.make_async_copy(w_all.at[0], w, sem)
-    copy.start()
-    scratch[...] = jnp.zeros_like(scratch)
-    scratch[0:VOCAB] = embed[...]
-    scratch[SLOT : SLOT + VOCAB] = embed[...] + brk[...]
-    hidden = scratch[...].astype(BF)
+        ]
+        if a is not None:
+            pairs += [
+                (w_in.at[1, pl.ds(r2, n)], a.at[:, 0:H]),
+                (w_in.at[1, pl.ds(r2 + n, n)], a.at[:, H : 2 * H]),
+            ]
+    else:
+        pairs = [(conv_w.at[1, pl.ds(r, n), 0:CUT_A], b)]
+        if a is not None:
+            pairs.append((w_out.at[0, pl.ds(r, n)], a))
+    return [pltpu.make_async_copy(s, d, sem) for s, d in pairs]
+
+
+def first_kernel(split, embed, brk, gain, w_in, conv_w, w_out, table, part, *rest):
+    *parts, emb, bv, g, w, full, sem = rest
+    copies = [
+        pltpu.make_async_copy(s, d, sem.at[0])
+        for s, d in ((embed, emb), (brk, bv), (gain, g), (w_in.at[0], w))
+    ]
+    start(copies)
+    if split:
+        _, _, y, z = place()
+        kinds = []
+        for kind in range(2):
+            kinds.append(
+                part_copies(kind == 1, z, w_in, conv_w, w_out, parts[0], parts[1], sem.at[1])
+                + part_copies(kind == 0, 1 - z, w_in, conv_w, w_out, None, parts[2], sem.at[1])
+            )
+
+            @pl.when(y == kind)
+            def _():
+                start(kinds[kind])
+
+    wait(copies)
+    full[...] = jnp.zeros_like(full)
+    full[0:VOCAB] = emb[...]
+    full[SLOT : SLOT + VOCAB] = emb[...] + bv[...]
+    hidden = full[...].astype(BF)
     table[...] = hidden
-    normed = gelu(norm(hidden.astype(F32), gain[0:1])).astype(BF)
+    normed = gelu(norm(hidden.astype(F32), g[0:1])).astype(BF)
     rows = w.shape[0]
     mine = dot(normed, pick(normed.shape[1], rows, lax.axis_index("roll") * rows)).astype(BF)
-    copy.wait()
     part[...] = dot(mine, w[...])
+    if split:
+        for kind in range(2):
+
+            @pl.when(y == kind)
+            def _():
+                wait(kinds[kind])
 
 
 def table_kernel(split, own, other, gain, w_all, *rest):
@@ -327,37 +343,30 @@
     wide_rows = rows + 2 * EDGE
     codes = tokens[0] + SLOT * breaks[0]
 
-    if split:
-        shard = w_out.shape[1] // 2
-        part_a, part_b = pl.pallas_call(
-            part_kernel,
-            out_shape=(jax.ShapeDtypeStruct((shard, width), BF), jax.ShapeDtypeStruct((shard, CUT_A), BF)),
-            in_specs=[HBM] * 3,
-            out_specs=(HBM, HBM),
-            scratch_shapes=[pltpu.SemaphoreType.DMA],
-            compiler_params=params(4),
-        )(w_in, conv_w, w_out)
-        far_a = x_swap(part_a)
+    shard = w_out.shape[1] // 2
+    shapes = [((CODES, width), BF), ((CODES, H), F32)]
+    if split:
         near_in, near_conv, near_out = core_swap(w_in), core_swap(conv_w), core_swap(w_out)
-
-    table, part = pl.pallas_call(
-        embed_kernel,
-        out_shape=(
-            jax.ShapeDtypeStruct((CODES, width), BF),
-            jax.ShapeDtypeStruct((CODES, H), F32),
-        ),
-        in_specs=[VMEM, VMEM, VMEM, HBM],
-        out_specs=(VMEM, VMEM),
+        shapes += [((shard, width), BF), ((shard, CUT_A), BF), ((shard, CUT_A), BF)]
+    table, part, *parts = pl.pallas_call(
+        functools.partial(first_kernel, split),
+        out_shape=[jax.ShapeDtypeStruct(n, t) for n, t in shapes],
+        in_specs=[HBM] * 6,
+        out_specs=[VMEM] * 2 + [HBM] * (len(shapes) - 2),
         scratch_shapes=[
+            pltpu.VMEM(embed_table.shape, F32),
+            pltpu.VMEM((1, width), F32),
+            pltpu.VMEM(gain_in.shape, F32),
+            pltpu.VMEM(w_in.shape[1:], BF),
             pltpu.VMEM((CODES, width), F32),
-            pltpu.VMEM(w_in.shape[1:], BF),
-            pltpu.SemaphoreType.DMA,
+            pltpu.SemaphoreType.DMA((2,)),
         ],
-        compiler_params=params(12),
-    )(embed_table, break_vec[None], gain_in, w_in)
+        compiler_params=params(56),
+    )(embed_table, break_vec[None], gain_in, w_in, conv_w, w_out)
 
     if split:
         own = part + core_swap(part)
+        far_a = x_swap(parts[0])
         other = x_swap(own.astype(BF))
         codes = after(codes, own)
         low = seq_at % 2 == 0
@@ -366,7 +375,7 @@
         pairs = [(i, i + 1) for i in range(1, seqs - 1, 2)]
         odd = lax.ppermute(jnp.where(low, *ends[::-1]), "seq", pairs + [(j, i) for i, j in pairs])
         before, behind = jnp.where(low, odd, even), jnp.where(low, even, odd)
-        far_b = x_swap(after(part_b, own))
+        far_b = x_swap(after(parts[1], own))
         other = after(other, near_in, near_conv, near_out)
     else:
         own = lax.psum(part, "roll")
@@ -395,7 +404,7 @@
     if split:
         mine = taps[0] + core_swap(taps[1]).astype(F32)
         sent = mine.astype(BF)
-        relay = after(far_a, sent)
+        relay = after(far_a, taps[1])
         parts_a = [far_a] + [seq_swap(relay, b) for b in (1, 2, 3)]
         near = after(near, sent)
         other = x_swap(sent)
@@ -412,11 +421,11 @@
     )(span, near)
 
     if split:
-        mine = (mine + after(other, hot1).astype(F32)).astype(BF)
+        mine = (mine + after(other, hot1, *parts_a).astype(F32)).astype(BF)
         theirs = core_swap(mine)
-        near_a = [core_swap(relay)] + [core_swap(after(p, theirs)) for p in parts_a[1:]]
+        near_a = [core_swap(relay)] + [core_swap(after(p, mine)) for p in parts_a[1:]]
         relay = after(far_b, mine)
-        parts_b = [far_b] + [seq_swap(relay, b) for b in (1, 2, 3)]
+        parts_b = [far_b, seq_swap(relay, 1), seq_swap(relay, 2), x_swap(after(parts[2], mine))]
         weights_a = [mine, theirs, w_out, w_in, near_out, near_in] + parts_a + near_a
     else:
         taps = lax.psum(taps[0], "roll").astype(BF)
@@ -437,7 +446,7 @@
             pltpu.VMEM((width, H), BF),
             pltpu.SemaphoreType.DMA((3,)),
         ],
-        compiler_params=params(36),
+        compiler_params=params(30),
     )(span, hot5, hot1, table, gain_out, gain_in, gain_mid, *weights_a)
 
     if split:

time: 82.3 us -> 100 us (1.22)
  Pallas kernels: 24.9 us -> 53.2 us
  waiting for transfers between devices: 24.9 us -> 15 us
  local copies, waits for them, and re-layouts: 6.74 us -> 4.36 us
  starting transfers between devices: 22.2 us -> 23.4 us
    pallas_call x2 -> x1, Pallas kernels: 1.91 us -> 30.4 us  [per_device(): pl.pallas_call(functools.partial(first_kernel, split), out_shape=[jax.Sha...]
    ppermute x4 -> x5, waiting for transfers between devices: 12.9 us -> 4.96 us  [x_swap(): return lax.ppermute(x, 'roll', [(i, i ^ 2) for i in range(rolls)])]
    unnamed x30 -> x24, local copies, waits for them, and re-layouts: 5.95 us -> 2.99 us
    ppermute x4 -> x5, starting transfers between devices: 5.18 us -> 7.14 us  [x_swap(): return lax.ppermute(x, 'roll', [(i, i ^ 2) for i in range(rolls)])]
    ppermute x7 -> x6, waiting for transfers between devices: 8.51 us -> 6.58 us  [seq_swap(): return lax.ppermute(x, 'seq', [(i, i ^ bits) for i in range(seqs)])]
    ppermute x7 -> x6, starting transfers between devices: 13.1 us -> 12.3 us  [seq_swap(): return lax.ppermute(x, 'seq', [(i, i ^ bits) for i in range(seqs)])]
  transfers between devices with their start and end apart: 26 -> 26, of which waited for: 10 -> 9; matrix products, arithmetic and copies ran while one was open for 3% -> 4% of each run, Pallas kernels for 21% -> 46%
where the time goes in v3:
time: 100 us
  Pallas kernels  53.2 us (53%)
  starting transfers between devices  23.4 us (23%)
  waiting for transfers between devices  15 us (15%)
  local copies, waits for them, and re-layouts  4.36 us (4%)
  other arithmetic  2.95 us (3%)
  between operations  1.01 us (1%)
    pallas_call x1, Pallas kernels, per_device(): pl.pallas_call(functools.partial(first_kernel, split), out_shape=[jax.Sha...  30.4 us
    pallas_call x1, Pallas kernels, per_device(): pl.pallas_call(functools.partial(rows_kernel, split), out_shape=(jax.Shap...  13.2 us
    ppermute x6, starting transfers between devices, seq_swap(): return lax.ppermute(x, 'seq', [(i, i ^ bits) for i in range(seqs)])  12.3 us
    pallas_call x1, Pallas kernels, per_device(): pl.pallas_call(functools.partial(last_kernel, split), out_shape=jax.Shape...  7.42 us
    ppermute x5, starting transfers between devices, x_swap(): return lax.ppermute(x, 'roll', [(i, i ^ 2) for i in range(rolls)])  7.14 us
    ppermute x6, waiting for transfers between devices, seq_swap(): return lax.ppermute(x, 'seq', [(i, i ^ bits) for i in range(seqs)])  6.58 us
    ppermute x5, waiting for transfers between devices, x_swap(): return lax.ppermute(x, 'roll', [(i, i ^ 2) for i in range(rolls)])  4.96 us
    ppermute x14, waiting for transfers between devices, core_swap(): return lax.ppermute(x, 'roll', [(i, i ^ 1) for i in range(rolls)])  3.49 us
  transfers between devices with their start and end apart: 26, of which 9 were waited for; matrix products, arithmetic and copies ran while one was open for 4% of the time, Pallas kernels for 46%

profile of v3, /device:TPU:0, one launch (start us, length us, event | category | flops | bytes accessed | tf_op | source)
XLA Modules:
  0.0 100.0 jit_solution(9872281358192360517)
XLA Ops:
  0.5 0.5 collective-permute-start.6
  1.0 1.3 %broadcast_in_dim.9.brk = f32[1,1280]{1,0:T(1,128)} reshape(f32[1280]{0:T(1024)} %param.15) | data formatting | bytes 10240 | tf_op jit(solution)/shard_map/broadcast_in_dim | solution.py:365
  2.3 30.4 %shard_map.109 = (bf16[64,1280]{1,0:T(8,128)(2,1)}, f32[64,640]{1,0:T(8,128)}, bf16[80,1280]{1,0:T(8,128)(2,1)}, bf16[80,2304]{1,0:T(8,128)(2,1)}, bf16[80,2304]{1,0:T(8,128)(2,1)}) custom-call(f32[30,1280]{1,0:T(8,128)} %embed.1, f32[1,1280]{1,0:T(1,128)} %broadcast_in_dim.9.brk, f32[2,1280]{1,0:T(2,128)} %gain_in.1, bf16[2,320,640]{2,1,0:T(8,128)(2,1)} %rest_3_.1, ...), custom_call_target="tpu_custom_call" | custom-call | tf_op jit(solution)/shard_map/pallas_call | solution.py:351
  32.8 2.9 %collective-permute-start.9 = (bf16[80,1280]{1,0:T(8,128)(2,1)}, bf16[80,1280]{1,0:T(8,128)(2,1)S(1)}, u32[]{:S(2)}, u32[]{:S(2)}) collective-permute-start(bf16[80,1280]{1,0:T(8,128)(2,1)} %get-tuple-element.40), channel_id=1, source_target_pairs={{0,2},{1,3},{2,0},{3,1},{4,6},{5,7},{6,4},{7,5},{8,10},{9,11},{10,... | collective-permute-start | bytes 614408 | tf_op jit(solution)/shard_map/ppermute | solution.py:337
  36.4 0.9 fusion.1
  37.4 0.6 collective-permute-start.3
  38.1 4.9 %collective-permute-done.3.other = bf16[64,640]{1,0:T(8,128)(2,1)S(1)} collective-permute-done((bf16[64,640]{1,0:T(8,128)(2,1)S(1)}, bf16[64,640]{1,0:T(8,128)(2,1)S(1)}, u32[]{:S(2)}, u32[]{:S(2)}) %collective-permute-start.3) | collective-permute-done | bytes 81952 | tf_op jit(solution)/shard_map/ppermute | solution.py:337
  43.0 0.9 copy-done.2
  43.9 1.2 %shard_map.110 = (f32[32,3200]{1,0:T(8,128)S(1)}, bf16[32,3200]{1,0:T(8,128)(2,1)S(1)}) custom-call(f32[64,640]{1,0:T(8,128)S(1)} %get-tuple-element.58.own, bf16[64,640]{1,0:T(8,128)(2,1)S(1)} %collective-permute-done.3.other, f32[2,640]{1,0:T(2,128)S(1)} %copy-done.7, bf16[2,160,3200]{2,1,0:T(8,128)(2,1)S(1)} %copy-done), custom_call_target="tpu_custom_call" | custom-call | tf_op jit(solution)/shard_map/pallas_call | solution.py:392
  45.3 1.8 %collective-permute-start.2 = (s32[384]{0:T(512)S(1)}, s32[384]{0:T(512)S(1)}, u32[]{:S(2)}, u32[]{:S(2)}) collective-permute-start(s32[384]{0:T(512)S(1)} %get-tuple-element.61), channel_id=1, source_target_pairs={{0,4},{4,0},{8,12},{12,8},{16,20},{20,16},{24,28},{28,24},{1,5},{5... | collective-permute-start | bytes 4616 | tf_op jit(solution)/shard_map/ppermute | solution.py:340
  47.1 0.6 collective-permute-start.1
  47.7 1.6 %collective-permute-start.18 = (bf16[80,2304]{1,0:T(8,128)(2,1)}, bf16[80,2304]{1,0:T(8,128)(2,1)}, u32[]{:S(2)}, u32[]{:S(2)}) collective-permute-start(bf16[80,2304]{1,0:T(8,128)(2,1)} %get-tuple-element.49), channel_id=1, source_target_pairs={{0,2},{1,3},{2,0},{3,1},{4,6},{5,7},{6,4},{7,5},{8,10},{9,11},{10,... | collective-permute-start | bytes 1105928 | tf_op jit(solution)/shard_map/ppermute | solution.py:337
  49.3 5.3 %collective-permute-start.12 = (bf16[80,1280]{1,0:T(8,128)(2,1)S(1)}, bf16[80,1280]{1,0:T(8,128)(2,1)}, u32[]{:S(2)}, u32[]{:S(2)}) collective-permute-start(bf16[80,1280]{1,0:T(8,128)(2,1)S(1)} %collective-permute-done.9.rest_6_), channel_id=1, source_target_pairs={{0,12},{4,8},{8,4},{12,0},{16,28},{20,24},{24,20},{28,16},{1,13},{... | collective-permute-start | bytes 614408 | tf_op jit(solution)/shard_map/ppermute | solution.py:340
  55.1 0.7 fusion
  56.0 0.5 collective-permute-start.8
  56.6 1.0 shard_map.111
  57.6 3.0 %collective-permute-done.12.rest_9_ = bf16[80,1280]{1,0:T(8,128)(2,1)} collective-permute-done((bf16[80,1280]{1,0:T(8,128)(2,1)S(1)}, bf16[80,1280]{1,0:T(8,128)(2,1)}, u32[]{:S(2)}, u32[]{:S(2)}) %collective-permute-start.12) | collective-permute-done | bytes 204832 | tf_op jit(solution)/shard_map/ppermute | solution.py:340
  60.6 3.5 %collective-permute-done.11.rest_8_ = bf16[80,1280]{1,0:T(8,128)(2,1)} collective-permute-done((bf16[80,1280]{1,0:T(8,128)(2,1)S(1)}, bf16[80,1280]{1,0:T(8,128)(2,1)}, u32[]{:S(2)}, u32[]{:S(2)}) %collective-permute-start.11) | collective-permute-done | bytes 204832 | tf_op jit(solution)/shard_map/ppermute | solution.py:340
  64.2 1.1 %add_convert_fusion.rest_0_ = bf16[32,3200]{1,0:T(8,128)(2,1)S(1)} fusion(bf16[32,3200]{1,0:T(8,128)(2,1)} %collective-permute-done.8, f32[32,3200]{1,0:T(8,128)S(1)} %get-tuple-element.34, bf16[32,3200]{1,0:T(8,128)(2,1)} %copy-done.9), kind=kLoop, calls=%fused_computation | loop fusion | flops 512000 | bytes 1024000 | tf_op jit(solution)/shard_map/convert_element_type | solution.py:424
  65.4 0.5 collective-permute-start.16
  65.9 1.9 %collective-permute-start.20 = (bf16[80,2304]{1,0:T(8,128)(2,1)}, bf16[80,2304]{1,0:T(8,128)(2,1)S(1)}, u32[]{:S(2)}, u32[]{:S(2)}) collective-permute-start(bf16[80,2304]{1,0:T(8,128)(2,1)} %collective-permute-done.18.rest_4_), channel_id=1, source_target_pairs={{0,8},{4,12},{8,0},{12,4},{16,24},{20,28},{24,16},{28,20},{1,9},{5... | collective-permute-start | bytes 1105928 | tf_op jit(solution)/shard_map/ppermute | solution.py:340
  67.7 2.7 %collective-permute-start.19 = (bf16[80,2304]{1,0:T(8,128)(2,1)}, bf16[80,2304]{1,0:T(8,128)(2,1)S(1)}, u32[]{:S(2)}, u32[]{:S(2)}) collective-permute-start(bf16[80,2304]{1,0:T(8,128)(2,1)} %collective-permute-done.18.rest_4_), channel_id=1, source_target_pairs={{0,4},{4,0},{8,12},{12,8},{16,20},{20,16},{24,28},{28,24},{1,5},{5... | collective-permute-start | bytes 1105928 | tf_op jit(solution)/shard_map/ppermute | solution.py:340
  70.5 1.5 %collective-permute-start.21 = (bf16[80,2304]{1,0:T(8,128)(2,1)}, bf16[80,2304]{1,0:T(8,128)(2,1)S(1)}, u32[]{:S(2)}, u32[]{:S(2)}) collective-permute-start(bf16[80,2304]{1,0:T(8,128)(2,1)} %get-tuple-element.52), channel_id=1, source_target_pairs={{0,2},{1,3},{2,0},{3,1},{4,6},{5,7},{6,4},{7,5},{8,10},{9,11},{10,... | collective-permute-start | bytes 1105928 | tf_op jit(solution)/shard_map/ppermute | solution.py:337
  72.0 0.5 collective-permute-start.13
  72.5 1.1 %collective-permute-done.17.rest_13_ = bf16[80,1280]{1,0:T(8,128)(2,1)S(1)} collective-permute-done((bf16[80,1280]{1,0:T(8,128)(2,1)}, bf16[80,1280]{1,0:T(8,128)(2,1)S(1)}, u32[]{:S(2)}, u32[]{:S(2)}) %collective-permute-start.17) | collective-permute-done | bytes 204832 | tf_op jit(solution)/shard_map/ppermute | solution.py:334
  73.8 1.1 %copy-done.4 = bf16[2,320,640]{2,1,0:T(8,128)(2,1)S(1)} copy-done((bf16[2,320,640]{2,1,0:T(8,128)(2,1)S(1)}, bf16[2,320,640]{2,1,0:T(8,128)(2,1)}, u32[]{:S(2)}) %copy-start.4) | copy-done | bytes 819224
  74.9 0.9 copy-done.5
  75.8 13.2 %shard_map.112 = (bf16[1008,640]{1,0:T(8,128)(2,1)S(1)}, bf16[496,1280]{1,0:T(8,128)(2,1)S(1)}) custom-call(s32[2]{0:T(128)S(1)} %pad_add_fusion.span, bf16[1008,320]{1,0:T(8,128)(2,1)S(1)} %get-tuple-element.37.hot5, bf16[1008,64]{1,0:T(8,128)(2,1)S(1)} %get-tuple-element.38.hot1, bf16[64,1280]{1,0:T(8,128)(2,1)S(1)} %copy-done.5, f32[2,640]{1,0:T(2,128)S(1)} %copy-done.8, ...), custom_call_target="tpu_custom_call" | custom-call | tf_op jit(solution)/shard_map/pallas_call | solution.py:435
  90.1 0.9 collective-permute-done.22.rest_8_
  91.3 0.5 collective-permute-done.23.rest_9_
  91.8 0.5 collective-permute-done.25.rest_11_
  92.4 7.4 %shard_map.113 = bf16[496,1280]{1,0:T(8,128)(2,1)} custom-call(bf16[1008,640]{1,0:T(8,128)(2,1)S(1)} %get-tuple-element.46.ci, bf16[496,1280]{1,0:T(8,128)(2,1)S(1)} %get-tuple-element.47.hid, f32[2,640]{1,0:T(2,128)S(1)} %copy-done.8, bf16[2,160,3200]{2,1,0:T(8,128)(2,1)S(1)} %copy-done, bf16[2,160,1280]{2,1,0:T(8,128)(2,1)S(1)} %copy-done.1, ...), custom_call_target="tpu_custom_call" | custom-call | tf_op jit(solution)/shard_map/pallas_call | solution.py:455
  (60 shorter events, 3.2 us)
Async XLA Ops:
  0.0 43.9 %collective-permute-start.5 = (bf16[2,160,3200]{2,1,0:T(8,128)(2,1)}, bf16[2,160,3200]{2,1,0:T(8,128)(2,1)}, u32[]{:S(2)}, u32[]{:S(2)}) collective-permute-start(bf16[2,160,3200]{2,1,0:T(8,128)(2,1)} %rest_0_.1), channel_id=1, source_target_pairs={{0,1},{1,0},{2,3},{3,2},{4,5},{5,4},{6,7},{7,6},{8,9},{9,8},{10,11... | collective-permute-start | bytes 6144008 | tf_op jit(solution)/shard_map/ppermute | solution.py:334
  0.5 42.6 %collective-permute-start.4 = (bf16[2,320,640]{2,1,0:T(8,128)(2,1)}, bf16[2,320,640]{2,1,0:T(8,128)(2,1)}, u32[]{:S(2)}, u32[]{:S(2)}) collective-permute-start(bf16[2,320,640]{2,1,0:T(8,128)(2,1)} %rest_3_.1), channel_id=1, source_target_pairs={{0,1},{1,0},{2,3},{3,2},{4,5},{5,4},{6,7},{7,6},{8,9},{9,8},{10,11... | collective-permute-start | bytes 2457608 | tf_op jit(solution)/shard_map/ppermute | solution.py:334
  0.5 42.5 %collective-permute-start.6 = (bf16[2,160,1280]{2,1,0:T(8,128)(2,1)}, bf16[2,160,1280]{2,1,0:T(8,128)(2,1)S(1)}, u32[]{:S(2)}, u32[]{:S(2)}) collective-permute-start(bf16[2,160,1280]{2,1,0:T(8,128)(2,1)} %rest_1_.1), channel_id=1, source_target_pairs={{0,1},{1,0},{2,3},{3,2},{4,5},{5,4},{6,7},{7,6},{8,9},{9,8},{10,11... | collective-permute-start | bytes 2457608 | tf_op jit(solution)/shard_map/ppermute | solution.py:334
  2.3 34.1 %copy-start.10 = (s32[1,496]{1,0:T(1,128)S(1)}, s32[1,496]{1,0:T(1,128)}, u32[]{:S(2)}) copy-start(s32[1,496]{1,0:T(1,128)} %param.11) | copy-start | bytes 5956
  2.3 34.1 %copy-start.11 = (s32[1,496]{1,0:T(1,128)S(1)}, s32[1,496]{1,0:T(1,128)}, u32[]{:S(2)}) copy-start(s32[1,496]{1,0:T(1,128)} %param.12) | copy-start | bytes 5956
  2.3 41.7 %copy-start = (bf16[2,160,3200]{2,1,0:T(8,128)(2,1)S(1)}, bf16[2,160,3200]{2,1,0:T(8,128)(2,1)}, u32[]{:S(2)}) copy-start(bf16[2,160,3200]{2,1,0:T(8,128)(2,1)} %rest_0_.1) | copy-start | bytes 6144004
  2.3 41.7 %copy-start.7 = (f32[2,640]{1,0:T(2,128)S(1)}, f32[2,640]{1,0:T(2,128)}, u32[]{:S(2)}) copy-start(f32[2,640]{1,0:T(2,128)} %gain_mid.1) | copy-start | bytes 15364
  32.7 3.8 %collective-permute-start = (f32[64,640]{1,0:T(8,128)}, f32[64,640]{1,0:T(8,128)S(1)}, u32[]{:S(2)}, u32[]{:S(2)}) collective-permute-start(f32[64,640]{1,0:T(8,128)} %get-tuple-element.31), channel_id=1, source_target_pairs={{0,1},{1,0},{2,3},{3,2},{4,5},{5,4},{6,7},{7,6},{8,9},{9,8},{10,11... | collective-permute-start | bytes 491528 | tf_op jit(solution)/shard_map/ppermute | solution.py:334
  32.8 16.5 %collective-permute-start.9 = (bf16[80,1280]{1,0:T(8,128)(2,1)}, bf16[80,1280]{1,0:T(8,128)(2,1)S(1)}, u32[]{:S(2)}, u32[]{:S(2)}) collective-permute-start(bf16[80,1280]{1,0:T(8,128)(2,1)} %get-tuple-element.40), channel_id=1, source_target_pairs={{0,2},{1,3},{2,0},{3,1},{4,6},{5,7},{6,4},{7,5},{8,10},{9,11},{10,... | collective-permute-start | bytes 614408 | tf_op jit(solution)/shard_map/ppermute | solution.py:337
  37.4 5.6 %collective-permute-start.3 = (bf16[64,640]{1,0:T(8,128)(2,1)S(1)}, bf16[64,640]{1,0:T(8,128)(2,1)S(1)}, u32[]{:S(2)}, u32[]{:S(2)}) collective-permute-start(bf16[64,640]{1,0:T(8,128)(2,1)S(1)} %get-tuple-element.57), channel_id=1, source_target_pairs={{0,2},{1,3},{2,0},{3,1},{4,6},{5,7},{6,4},{7,5},{8,10},{9,11},{10,... | collective-permute-start | bytes 245768 | tf_op jit(solution)/shard_map/ppermute | solution.py:337
  45.1 28.6 %copy-start.1 = (bf16[2,160,1280]{2,1,0:T(8,128)(2,1)S(1)}, bf16[2,160,1280]{2,1,0:T(8,128)(2,1)}, u32[]{:S(2)}) copy-start(bf16[2,160,1280]{2,1,0:T(8,128)(2,1)} %rest_1_.1) | copy-start | bytes 2457604
  45.1 28.6 %copy-start.6 = (f32[2,1280]{1,0:T(2,128)S(1)}, f32[2,1280]{1,0:T(2,128)}, u32[]{:S(2)}) copy-start(f32[2,1280]{1,0:T(2,128)} %gain_in.1) | copy-start | bytes 30724
  45.2 9.5 %collective-permute-start.7 = (bf16[32,3200]{1,0:T(8,128)(2,1)S(1)}, bf16[32,3200]{1,0:T(8,128)(2,1)S(1)}, u32[]{:S(2)}, u32[]{:S(2)}) collective-permute-start(bf16[32,3200]{1,0:T(8,128)(2,1)S(1)} %get-tuple-element.35), channel_id=1, source_target_pairs={{0,1},{1,0},{2,3},{3,2},{4,5},{5,4},{6,7},{7,6},{8,9},{9,8},{10,11... | collective-permute-start | bytes 614408 | tf_op jit(solution)/shard_map/ppermute | solution.py:334
  45.3 10.5 %collective-permute-start.2 = (s32[384]{0:T(512)S(1)}, s32[384]{0:T(512)S(1)}, u32[]{:S(2)}, u32[]{:S(2)}) collective-permute-start(s32[384]{0:T(512)S(1)} %get-tuple-element.61), channel_id=1, source_target_pairs={{0,4},{4,0},{8,12},{12,8},{16,20},{20,16},{24,28},{28,24},{1,5},{5... | collective-permute-start | bytes 4616 | tf_op jit(solution)/shard_map/ppermute | solution.py:340
  47.1 8.9 %collective-permute-start.1 = (s32[384]{0:T(512)S(1)}, s32[384]{0:T(512)S(1)}, u32[]{:S(2)}, u32[]{:S(2)}) collective-permute-start(s32[384]{0:T(512)S(1)} %get-tuple-element.62), channel_id=1, source_target_pairs={{4,8},{12,16},{20,24},{8,4},{16,12},{24,20},{5,9},{13,17},{21,25},... | collective-permute-start | bytes 4616 | tf_op jit(solution)/shard_map/ppermute | solution.py:376
  47.7 18.1 %collective-permute-start.18 = (bf16[80,2304]{1,0:T(8,128)(2,1)}, bf16[80,2304]{1,0:T(8,128)(2,1)}, u32[]{:S(2)}, u32[]{:S(2)}) collective-permute-start(bf16[80,2304]{1,0:T(8,128)(2,1)} %get-tuple-element.49), channel_id=1, source_target_pairs={{0,2},{1,3},{2,0},{3,1},{4,6},{5,7},{6,4},{7,5},{8,10},{9,11},{10,... | collective-permute-start | bytes 1105928 | tf_op jit(solution)/shard_map/ppermute | solution.py:337
  49.3 11.3 %collective-permute-start.12 = (bf16[80,1280]{1,0:T(8,128)(2,1)S(1)}, bf16[80,1280]{1,0:T(8,128)(2,1)}, u32[]{:S(2)}, u32[]{:S(2)}) collective-permute-start(bf16[80,1280]{1,0:T(8,128)(2,1)S(1)} %collective-permute-done.9.rest_6_), channel_id=1, source_target_pairs={{0,12},{4,8},{8,4},{12,0},{16,28},{20,24},{24,20},{28,16},{1,13},{... | collective-permute-start | bytes 614408 | tf_op jit(solution)/shard_map/ppermute | solution.py:340
  54.6 9.6 %collective-permute-start.11 = (bf16[80,1280]{1,0:T(8,128)(2,1)S(1)}, bf16[80,1280]{1,0:T(8,128)(2,1)}, u32[]{:S(2)}, u32[]{:S(2)}) collective-permute-start(bf16[80,1280]{1,0:T(8,128)(2,1)S(1)} %collective-permute-done.9.rest_6_), channel_id=1, source_target_pairs={{0,8},{4,12},{8,0},{12,4},{16,24},{20,28},{24,16},{28,20},{1,9},{5... | collective-permute-start | bytes 614408 | tf_op jit(solution)/shard_map/ppermute | solution.py:340
  55.8 8.4 %collective-permute-start.10 = (bf16[80,1280]{1,0:T(8,128)(2,1)S(1)}, bf16[80,1280]{1,0:T(8,128)(2,1)}, u32[]{:S(2)}, u32[]{:S(2)}) collective-permute-start(bf16[80,1280]{1,0:T(8,128)(2,1)S(1)} %collective-permute-done.9.rest_6_), channel_id=1, source_target_pairs={{0,4},{4,0},{8,12},{12,8},{16,20},{20,16},{24,28},{28,24},{1,5},{5... | collective-permute-start | bytes 614408 | tf_op jit(solution)/shard_map/ppermute | solution.py:340
  56.0 8.2 %collective-permute-start.8 = (bf16[32,3200]{1,0:T(8,128)(2,1)}, bf16[32,3200]{1,0:T(8,128)(2,1)}, u32[]{:S(2)}, u32[]{:S(2)}) collective-permute-start(bf16[32,3200]{1,0:T(8,128)(2,1)} %fusion), channel_id=1, source_target_pairs={{0,2},{1,3},{2,0},{3,1},{4,6},{5,7},{6,4},{7,5},{8,10},{9,11},{10,... | collective-permute-start | bytes 614408 | tf_op jit(solution)/shard_map/ppermute | solution.py:337
  60.6 9.8 %collective-permute-start.14 = (bf16[80,1280]{1,0:T(8,128)(2,1)S(1)}, bf16[80,1280]{1,0:T(8,128)(2,1)S(1)}, u32[]{:S(2)}, u32[]{:S(2)}) collective-permute-start(bf16[80,1280]{1,0:T(8,128)(2,1)S(1)} %collective-permute-done.9.rest_6_), channel_id=1, source_target_pairs={{0,1},{1,0},{2,3},{3,2},{4,5},{5,4},{6,7},{7,6},{8,9},{9,8},{10,11... | collective-permute-start | bytes 614408 | tf_op jit(solution)/shard_map/ppermute | solution.py:334
  65.3 6.7 %collective-permute-start.15 = (bf16[80,1280]{1,0:T(8,128)(2,1)}, bf16[80,1280]{1,0:T(8,128)(2,1)S(1)}, u32[]{:S(2)}, u32[]{:S(2)}) collective-permute-start(bf16[80,1280]{1,0:T(8,128)(2,1)} %collective-permute-done.10.rest_7_), channel_id=1, source_target_pairs={{0,1},{1,0},{2,3},{3,2},{4,5},{5,4},{6,7},{7,6},{8,9},{9,8},{10,11... | collective-permute-start | bytes 614408 | tf_op jit(solution)/shard_map/ppermute | solution.py:334
  65.4 6.6 %collective-permute-start.16 = (bf16[80,1280]{1,0:T(8,128)(2,1)}, bf16[80,1280]{1,0:T(8,128)(2,1)S(1)}, u32[]{:S(2)}, u32[]{:S(2)}) collective-permute-start(bf16[80,1280]{1,0:T(8,128)(2,1)} %collective-permute-done.11.rest_8_), channel_id=1, source_target_pairs={{0,1},{1,0},{2,3},{3,2},{4,5},{5,4},{6,7},{7,6},{8,9},{9,8},{10,11... | collective-permute-start | bytes 614408 | tf_op jit(solution)/shard_map/ppermute | solution.py:334
  65.9 23.4 %collective-permute-start.20 = (bf16[80,2304]{1,0:T(8,128)(2,1)}, bf16[80,2304]{1,0:T(8,128)(2,1)S(1)}, u32[]{:S(2)}, u32[]{:S(2)}) collective-permute-start(bf16[80,2304]{1,0:T(8,128)(2,1)} %collective-permute-done.18.rest_4_), channel_id=1, source_target_pairs={{0,8},{4,12},{8,0},{12,4},{16,24},{20,28},{24,16},{28,20},{1,9},{5... | collective-permute-start | bytes 1105928 | tf_op jit(solution)/shard_map/ppermute | solution.py:340
  67.7 21.9 %collective-permute-start.19 = (bf16[80,2304]{1,0:T(8,128)(2,1)}, bf16[80,2304]{1,0:T(8,128)(2,1)S(1)}, u32[]{:S(2)}, u32[]{:S(2)}) collective-permute-start(bf16[80,2304]{1,0:T(8,128)(2,1)} %collective-permute-done.18.rest_4_), channel_id=1, source_target_pairs={{0,4},{4,0},{8,12},{12,8},{16,20},{20,16},{24,28},{28,24},{1,5},{5... | collective-permute-start | bytes 1105928 | tf_op jit(solution)/shard_map/ppermute | solution.py:340
  70.5 19.3 %collective-permute-start.21 = (bf16[80,2304]{1,0:T(8,128)(2,1)}, bf16[80,2304]{1,0:T(8,128)(2,1)S(1)}, u32[]{:S(2)}, u32[]{:S(2)}) collective-permute-start(bf16[80,2304]{1,0:T(8,128)(2,1)} %get-tuple-element.52), channel_id=1, source_target_pairs={{0,2},{1,3},{2,0},{3,1},{4,6},{5,7},{6,4},{7,5},{8,10},{9,11},{10,... | collective-permute-start | bytes 1105928 | tf_op jit(solution)/shard_map/ppermute | solution.py:337
  72.0 1.7 %collective-permute-start.17 = (bf16[80,1280]{1,0:T(8,128)(2,1)}, bf16[80,1280]{1,0:T(8,128)(2,1)S(1)}, u32[]{:S(2)}, u32[]{:S(2)}) collective-permute-start(bf16[80,1280]{1,0:T(8,128)(2,1)} %collective-permute-done.12.rest_9_), channel_id=1, source_target_pairs={{0,1},{1,0},{2,3},{3,2},{4,5},{5,4},{6,7},{7,6},{8,9},{9,8},{10,11... | collective-permute-start | bytes 614408 | tf_op jit(solution)/shard_map/ppermute | solution.py:334
  72.0 1.7 %collective-permute-start.13 = (bf16[32,3200]{1,0:T(8,128)(2,1)S(1)}, bf16[32,3200]{1,0:T(8,128)(2,1)S(1)}, u32[]{:S(2)}, u32[]{:S(2)}) collective-permute-start(bf16[32,3200]{1,0:T(8,128)(2,1)S(1)} %add_convert_fusion.rest_0_), channel_id=1, source_target_pairs={{0,1},{1,0},{2,3},{3,2},{4,5},{5,4},{6,7},{7,6},{8,9},{9,8},{10,11... | collective-permute-start | bytes 614408 | tf_op jit(solution)/shard_map/ppermute | solution.py:334
  89.0 2.0 %collective-permute-start.22 = (bf16[80,2304]{1,0:T(8,128)(2,1)}, bf16[80,2304]{1,0:T(8,128)(2,1)S(1)}, u32[]{:S(2)}, u32[]{:S(2)}) collective-permute-start(bf16[80,2304]{1,0:T(8,128)(2,1)} %collective-permute-done.18.rest_4_), channel_id=1, source_target_pairs={{0,1},{1,0},{2,3},{3,2},{4,5},{5,4},{6,7},{7,6},{8,9},{9,8},{10,11... | collective-permute-start | bytes 1105928 | tf_op jit(solution)/shard_map/ppermute | solution.py:334
  89.3 2.0 %collective-permute-start.24 = (bf16[80,2304]{1,0:T(8,128)(2,1)S(1)}, bf16[80,2304]{1,0:T(8,128)(2,1)S(1)}, u32[]{:S(2)}, u32[]{:S(2)}) collective-permute-start(bf16[80,2304]{1,0:T(8,128)(2,1)S(1)} %collective-permute-done.20.rest_6_), channel_id=1, source_target_pairs={{0,1},{1,0},{2,3},{3,2},{4,5},{5,4},{6,7},{7,6},{8,9},{9,8},{10,11... | collective-permute-start | bytes 1105928 | tf_op jit(solution)/shard_map/ppermute | solution.py:334
  89.6 2.2 %collective-permute-start.23 = (bf16[80,2304]{1,0:T(8,128)(2,1)S(1)}, bf16[80,2304]{1,0:T(8,128)(2,1)S(1)}, u32[]{:S(2)}, u32[]{:S(2)}) collective-permute-start(bf16[80,2304]{1,0:T(8,128)(2,1)S(1)} %collective-permute-done.19.rest_5_), channel_id=1, source_target_pairs={{0,1},{1,0},{2,3},{3,2},{4,5},{5,4},{6,7},{7,6},{8,9},{9,8},{10,11... | collective-permute-start | bytes 1105928 | tf_op jit(solution)/shard_map/ppermute | solution.py:334
  89.8 2.5 %collective-permute-start.25 = (bf16[80,2304]{1,0:T(8,128)(2,1)S(1)}, bf16[80,2304]{1,0:T(8,128)(2,1)S(1)}, u32[]{:S(2)}, u32[]{:S(2)}) collective-permute-start(bf16[80,2304]{1,0:T(8,128)(2,1)S(1)} %collective-permute-done.21.rest_7_), channel_id=1, source_target_pairs={{0,1},{1,0},{2,3},{3,2},{4,5},{5,4},{6,7},{7,6},{8,9},{9,8},{10,11... | collective-permute-start | bytes 1105928 | tf_op jit(solution)/shard_map/ppermute | solution.py:334
  (6 other events, 49.9 us)

commit v4 on v3

--- a/solution.py
+++ b/solution.py
@@ -62,6 +62,13 @@
         c.wait()
 
 
+def stagger(stages):
+    for t in range(len(stages) + 1):
+        for b in range(2):
+            if 0 <= t - b < len(stages):
+                stages[t - b](b)
+
+
 def pick(rows, columns, first):
     i = lax.broadcasted_iota(jnp.int32, (rows, columns), 0)
     j = lax.broadcasted_iota(jnp.int32, (rows, columns), 1)
@@ -113,7 +120,7 @@
     wait(copies)
     full[...] = jnp.zeros_like(full)
     full[0:VOCAB] = emb[...]
-    full[SLOT : SLOT + VOCAB] = emb[...] + bv[...]
+    full[SLOT : SLOT + VOCAB] = emb[...] + bv[...][None, :]
     hidden = full[...].astype(BF)
     table[...] = hidden
     normed = gelu(norm(hidden.astype(F32), g[0:1])).astype(BF)
@@ -225,19 +232,43 @@
         out_copies += far0[0]
         in_copies += far0[1]
 
-    wait(first)
-    mixed = dot(hot5[...], tw[...])
-    act = gelu(norm(mixed, gain_out[0:1])).astype(BF)
-    wait(out_copies)
-    hidden = dot(jnp.concatenate([act, hot1[...]], axis=1), wo[...]).astype(BF)
-    rows = hidden.shape[0]
-    hid[...] = hidden[EDGE : rows - EDGE]
-    normed = gelu(norm(hidden.astype(F32), gain_in[1:2])).astype(BF)
-    wait(in_copies)
-    wide = dot(normed, wi[...])
-    pos = span[0] + lax.broadcasted_iota(jnp.int32, (rows, 1), 0)
-    valid = jnp.where((pos >= 0) & (pos < span[1]), 1.0, 0.0)
-    ci[...] = (gelu(norm(wide, gain_mid[1:2])) * valid).astype(BF)
+    rows = hid.shape[0] + 2 * EDGE
+    cuts = [0, 512, rows]
+    state = [None, None]
+
+    def once(b, copies):
+        if b == 0:
+            wait(copies)
+
+    def mix(b):
+        once(b, first)
+        state[b] = dot(hot5[cuts[b] : cuts[b + 1]], tw[...])
+
+    def act(b):
+        state[b] = gelu(norm(state[b], gain_out[0:1])).astype(BF)
+
+    def update(b):
+        once(b, out_copies)
+        lhs = jnp.concatenate([state[b], hot1[cuts[b] : cuts[b + 1]]], axis=1)
+        state[b] = dot(lhs, wo[...]).astype(BF)
+
+    def enter(b):
+        hidden = state[b]
+        lo, hi = max(cuts[b], EDGE), min(cuts[b + 1], rows - EDGE)
+        hid[lo - EDGE : hi - EDGE] = hidden[lo - cuts[b] : hi - cuts[b]]
+        state[b] = gelu(norm(hidden.astype(F32), gain_in[1:2])).astype(BF)
+
+    def widen(b):
+        once(b, in_copies)
+        state[b] = dot(state[b], wi[...])
+
+    def leave(b):
+        n = cuts[b + 1] - cuts[b]
+        pos = span[0] + cuts[b] + lax.broadcasted_iota(jnp.int32, (n, 1), 0)
+        valid = jnp.where((pos >= 0) & (pos < span[1]), 1.0, 0.0)
+        ci[cuts[b] : cuts[b + 1]] = (gelu(norm(state[b], gain_mid[1:2])) * valid).astype(BF)
+
+    stagger((mix, act, update, enter, widen, leave))
 
 
 def last_kernel(split, ci, hid, gain_out, *rest):
@@ -304,17 +335,25 @@
         out_copies += far0[1]
 
     rows = out.shape[0]
-    blocks = [0, 16 * (rows // 32), rows]
-    for b in range(2):
-        lo, hi = blocks[b], blocks[b + 1]
-        lhs = jnp.concatenate([ci[lo + k * DIL1 : hi + k * DIL1] for k in range(KERNEL)], axis=1)
+    cuts = [0, 16 * ((rows + 31) // 32), rows]
+    state = [None, None]
+
+    def mix(b):
+        lhs = jnp.concatenate([ci[cuts[b] + k * DIL1 : cuts[b + 1] + k * DIL1] for k in range(KERNEL)], axis=1)
         if b == 0:
             wait(conv_copies)
-        mixed = dot(lhs, wt[...])
-        act = gelu(norm(mixed, gain_out[1:2])).astype(BF)
+        state[b] = dot(lhs, wt[...])
+
+    def act(b):
+        state[b] = gelu(norm(state[b], gain_out[1:2])).astype(BF)
+
+    def update(b):
         if b == 0:
             wait(out_copies)
-        out[lo:hi] = (hid[lo:hi].astype(F32) + dot(act, wo[...])).astype(BF)
+        hidden = hid[cuts[b] : cuts[b + 1]].astype(F32)
+        out[cuts[b] : cuts[b + 1]] = (hidden + dot(state[b], wo[...])).astype(BF)
+
+    stagger((mix, act, update))
 
 
 def after(x, *deps):
@@ -346,26 +385,26 @@
     shard = w_out.shape[1] // 2
     shapes = [((CODES, width), BF), ((CODES, H), F32)]
     if split:
-        near_in, near_conv, near_out = core_swap(w_in), core_swap(conv_w), core_swap(w_out)
         shapes += [((shard, width), BF), ((shard, CUT_A), BF), ((shard, CUT_A), BF)]
     table, part, *parts = pl.pallas_call(
         functools.partial(first_kernel, split),
         out_shape=[jax.ShapeDtypeStruct(n, t) for n, t in shapes],
         in_specs=[HBM] * 6,
-        out_specs=[VMEM] * 2 + [HBM] * (len(shapes) - 2),
+        out_specs=[VMEM] * len(shapes),
         scratch_shapes=[
             pltpu.VMEM(embed_table.shape, F32),
-            pltpu.VMEM((1, width), F32),
+            pltpu.VMEM((width,), F32),
             pltpu.VMEM(gain_in.shape, F32),
             pltpu.VMEM(w_in.shape[1:], BF),
             pltpu.VMEM((CODES, width), F32),
             pltpu.SemaphoreType.DMA((2,)),
         ],
-        compiler_params=params(56),
-    )(embed_table, break_vec[None], gain_in, w_in, conv_w, w_out)
+        compiler_params=params(48),
+    )(embed_table, break_vec, gain_in, w_in, conv_w, w_out)
 
     if split:
         own = part + core_swap(part)
+        near_in, near_conv, near_out = [core_swap(after(w, own)) for w in (w_in, conv_w, w_out)]
         far_a = x_swap(parts[0])
         other = x_swap(own.astype(BF))
         codes = after(codes, own)
@@ -373,10 +412,11 @@
         ends = codes[rows - REACH :], codes[:REACH]
         even = seq_swap(jnp.where(low, *ends), 1)
         pairs = [(i, i + 1) for i in range(1, seqs - 1, 2)]
+        pairs.append((seqs - 1, 0))
         odd = lax.ppermute(jnp.where(low, *ends[::-1]), "seq", pairs + [(j, i) for i, j in pairs])
         before, behind = jnp.where(low, odd, even), jnp.where(low, even, odd)
         far_b = x_swap(after(parts[1], own))
-        other = after(other, near_in, near_conv, near_out)
+        other = after(other, before, behind)
     else:
         own = lax.psum(part, "roll")
         other = jnp.zeros((CODES, H), BF)
@@ -404,7 +444,7 @@
     if split:
         mine = taps[0] + core_swap(taps[1]).astype(F32)
         sent = mine.astype(BF)
-        relay = after(far_a, taps[1])
+        relay = after(far_a, sent)
         parts_a = [far_a] + [seq_swap(relay, b) for b in (1, 2, 3)]
         near = after(near, sent)
         other = x_swap(sent)

time: 100 us -> 76.5 us (0.77)
  Pallas kernels: 53.2 us -> 21 us
  waiting for transfers between devices: 15 us -> 22.4 us
  local copies, waits for them, and re-layouts: 4.36 us -> 9.36 us
  starting transfers between devices: 23.4 us -> 20.3 us
    pallas_call x1, Pallas kernels: 30.4 us -> 1.64 us  [per_device(): pl.pallas_call(functools.partial(first_kernel, split), out_shape=[jax.Sha...]
    unnamed x24 -> x42, local copies, waits for them, and re-layouts: 2.99 us -> 9.28 us
    ppermute x5, waiting for transfers between devices: 4.96 us -> 10.9 us  [x_swap(): return lax.ppermute(x, 'roll', [(i, i ^ 2) for i in range(rolls)])]
    ppermute x6, starting transfers between devices: 12.3 us -> 6.99 us  [seq_swap(): return lax.ppermute(x, 'seq', [(i, i ^ bits) for i in range(seqs)])]
    ppermute x1, starting transfers between devices: 0.65 us -> 3.78 us  [per_device(): lax.ppermute(jnp.where(low, *ends[::-1]), 'seq', pairs + [(j, i) for i, j...]
    pallas_call x1, Pallas kernels: 13.2 us -> 10.3 us  [per_device(): pl.pallas_call(functools.partial(rows_kernel, split), out_shape=(jax.Shap...]
    ppermute x14, waiting for transfers between devices: 3.49 us -> 5.72 us  [core_swap(): return lax.ppermute(x, 'roll', [(i, i ^ 1) for i in range(rolls)])]
    ppermute x6, waiting for transfers between devices: 6.58 us -> 4.69 us  [seq_swap(): return lax.ppermute(x, 'seq', [(i, i ^ bits) for i in range(seqs)])]
  transfers between devices with their start and end apart: 26 -> 26, of which waited for: 9 -> 15; matrix products, arithmetic and copies ran while one was open for 4% -> 3% of each run, Pallas kernels for 46% -> 15%
where the time goes in v4:
time: 76.5 us; the launch traced here: 76.1 us
  waiting for transfers between devices  22.4 us (29%)
  Pallas kernels  21 us (27%)
  starting transfers between devices  20.3 us (27%)
  local copies, waits for them, and re-layouts  9.36 us (12%)
  other arithmetic  2.05 us (3%)
  between operations  0.99 us (1%)
    ppermute x5, waiting for transfers between devices, x_swap(): return lax.ppermute(x, 'roll', [(i, i ^ 2) for i in range(rolls)])  10.9 us
    pallas_call x1, Pallas kernels, per_device(): pl.pallas_call(functools.partial(rows_kernel, split), out_shape=(jax.Shap...  10.3 us
    unnamed x42, local copies, waits for them, and re-layouts  9.28 us
    ppermute x6, starting transfers between devices, seq_swap(): return lax.ppermute(x, 'seq', [(i, i ^ bits) for i in range(seqs)])  6.99 us
    pallas_call x1, Pallas kernels, per_device(): pl.pallas_call(functools.partial(last_kernel, split), out_shape=jax.Shape...  6.93 us
    ppermute x5, starting transfers between devices, x_swap(): return lax.ppermute(x, 'roll', [(i, i ^ 2) for i in range(rolls)])  6.57 us
    ppermute x14, waiting for transfers between devices, core_swap(): return lax.ppermute(x, 'roll', [(i, i ^ 1) for i in range(rolls)])  5.72 us
    ppermute x6, waiting for transfers between devices, seq_swap(): return lax.ppermute(x, 'seq', [(i, i ^ bits) for i in range(seqs)])  4.69 us
  transfers between devices with their start and end apart: 26, of which 15 were waited for; matrix products, arithmetic and copies ran while one was open for 3% of the time, Pallas kernels for 15%

profile of v4, /device:TPU:0, one launch (start us, length us, event | category | flops | bytes accessed | tf_op | source)
XLA Modules:
  0.0 76.1 jit_solution(1845488597550640814)
XLA Ops:
  0.0 1.6 %copy-done = bf16[2,160,3200]{2,1,0:T(8,128)(2,1)S(1)} copy-done((bf16[2,160,3200]{2,1,0:T(8,128)(2,1)S(1)}, bf16[2,160,3200]{2,1,0:T(8,128)(2,1)}, u32[]{:S(2)}) %copy-start) | copy-done | bytes 2048024
  1.6 1.1 %copy-done.2 = bf16[2,160,1280]{2,1,0:T(8,128)(2,1)S(1)} copy-done((bf16[2,160,1280]{2,1,0:T(8,128)(2,1)S(1)}, bf16[2,160,1280]{2,1,0:T(8,128)(2,1)}, u32[]{:S(2)}) %copy-start.2) | copy-done | bytes 819224
  2.7 1.1 %copy-done.4 = bf16[2,320,640]{2,1,0:T(8,128)(2,1)S(1)} copy-done((bf16[2,320,640]{2,1,0:T(8,128)(2,1)S(1)}, bf16[2,320,640]{2,1,0:T(8,128)(2,1)}, u32[]{:S(2)}) %copy-start.4) | copy-done | bytes 819224
  3.9 0.9 %copy-done.6 = f32[30,1280]{1,0:T(8,128)S(1)} copy-done((f32[30,1280]{1,0:T(8,128)S(1)}, f32[30,1280]{1,0:T(8,128)}, u32[]{:S(2)}) %copy-start.6) | copy-done | bytes 153624
  6.2 1.6 %shard_map.109 = (bf16[64,1280]{1,0:T(8,128)(2,1)S(1)}, f32[64,640]{1,0:T(8,128)S(1)}, bf16[80,1280]{1,0:T(8,128)(2,1)S(1)}, bf16[80,2304]{1,0:T(8,128)(2,1)S(1)}, bf16[80,2304]{1,0:T(8,128)(2,1)S(1)}) custom-call(f32[30,1280]{1,0:T(8,128)S(1)} %copy-done.6, f32[1280]{0:T(1024)S(1)} %copy-done.13, f32[2,1280]{1,0:T(2,128)S(1)} %copy-done.9, ...), custom_call_target="tpu_custom_call" | custom-call | tf_op jit(solution)/shard_map/pallas_call | solution.py:389
  8.5 0.7 copy-done.14
  9.3 0.7 copy-done.15
  10.5 1.0 %collective-permute-done = f32[64,640]{1,0:T(8,128)S(1)} collective-permute-done((f32[64,640]{1,0:T(8,128)S(1)}, f32[64,640]{1,0:T(8,128)S(1)}, u32[]{:S(2)}, u32[]{:S(2)}) %collective-permute-start) | collective-permute-done | bytes 163872 | tf_op jit(solution)/shard_map/ppermute | solution.py:373
  11.6 2.6 %collective-permute-start.2 = (s32[384]{0:T(512)S(1)}, s32[384]{0:T(512)S(1)}, u32[]{:S(2)}, u32[]{:S(2)}) collective-permute-start(s32[384]{0:T(512)S(1)} %get-tuple-element.67), channel_id=1, source_target_pairs={{0,4},{4,0},{8,12},{12,8},{16,20},{20,16},{24,28},{28,24},{1,5},{5... | collective-permute-start | bytes 4616 | tf_op jit(solution)/shard_map/ppermute | solution.py:379
  14.2 3.8 %collective-permute-start.1 = (s32[384]{0:T(512)S(1)}, s32[384]{0:T(512)S(1)}, u32[]{:S(2)}, u32[]{:S(2)}) collective-permute-start(s32[384]{0:T(512)S(1)} %get-tuple-element.68), channel_id=1, source_target_pairs={{4,8},{12,16},{20,24},{28,0},{8,4},{16,12},{24,20},{0,28},{5,9},{1... | collective-permute-start | bytes 4616 | tf_op jit(solution)/shard_map/ppermute | solution.py:416
  18.0 1.5 %collective-permute-start.3 = (bf16[64,640]{1,0:T(8,128)(2,1)S(1)}, bf16[64,640]{1,0:T(8,128)(2,1)S(1)}, u32[]{:S(2)}, u32[]{:S(2)}) collective-permute-start(bf16[64,640]{1,0:T(8,128)(2,1)S(1)} %get-tuple-element.63), channel_id=1, source_target_pairs={{0,2},{1,3},{2,0},{3,1},{4,6},{5,7},{6,4},{7,5},{8,10},{9,11},{10,... | collective-permute-start | bytes 245768 | tf_op jit(solution)/shard_map/ppermute | solution.py:376
  19.5 1.0 %collective-permute-done.1 = s32[384]{0:T(512)S(1)} collective-permute-done((s32[384]{0:T(512)S(1)}, s32[384]{0:T(512)S(1)}, u32[]{:S(2)}, u32[]{:S(2)}) %collective-permute-start.1) | collective-permute-done | bytes 1568 | tf_op jit(solution)/shard_map/ppermute | solution.py:416
  20.5 1.9 %collective-permute-done.3.other = bf16[64,640]{1,0:T(8,128)(2,1)S(1)} collective-permute-done((bf16[64,640]{1,0:T(8,128)(2,1)S(1)}, bf16[64,640]{1,0:T(8,128)(2,1)S(1)}, u32[]{:S(2)}, u32[]{:S(2)}) %collective-permute-start.3) | collective-permute-done | bytes 81952 | tf_op jit(solution)/shard_map/ppermute | solution.py:376
  22.5 1.2 %shard_map.110 = (f32[32,3200]{1,0:T(8,128)S(1)}, bf16[32,3200]{1,0:T(8,128)(2,1)S(1)}) custom-call(f32[64,640]{1,0:T(8,128)S(1)} %get-tuple-element.64.own, bf16[64,640]{1,0:T(8,128)(2,1)S(1)} %collective-permute-done.3.other, f32[2,640]{1,0:T(2,128)S(1)} %copy-done.11, bf16[2,160,3200]{2,1,0:T(8,128)(2,1)S(1)} %copy-done.1), custom_call_target="tpu_custom_call" | custom-call | tf_op jit(solution)/shard_map/pallas_call | solution.py:432
  23.8 1.6 %collective-permute-start.6 = (bf16[80,1280]{1,0:T(8,128)(2,1)S(1)}, bf16[80,1280]{1,0:T(8,128)(2,1)S(1)}, u32[]{:S(2)}, u32[]{:S(2)}) collective-permute-start(bf16[80,1280]{1,0:T(8,128)(2,1)S(1)} %copy-done.17), channel_id=1, source_target_pairs={{0,2},{1,3},{2,0},{3,1},{4,6},{5,7},{6,4},{7,5},{8,10},{9,11},{10,... | collective-permute-start | bytes 614408 | tf_op jit(solution)/shard_map/ppermute | solution.py:376
  25.3 0.8 %fusion = bf16[32,3200]{1,0:T(8,128)(2,1)} fusion(f32[32,3200]{1,0:T(8,128)S(1)} %get-tuple-element.37, bf16[32,3200]{1,0:T(8,128)(2,1)S(1)} %collective-permute-done.4), kind=kLoop, calls=%fused_computation.2 | loop fusion | flops 307200 | bytes 819200 | tf_op jit(solution)/shard_map/convert_element_type | solution.py:446
  26.1 5.2 %collective-permute-done.6.rest_6_ = bf16[80,1280]{1,0:T(8,128)(2,1)S(1)} collective-permute-done((bf16[80,1280]{1,0:T(8,128)(2,1)S(1)}, bf16[80,1280]{1,0:T(8,128)(2,1)S(1)}, u32[]{:S(2)}, u32[]{:S(2)}) %collective-permute-start.6) | collective-permute-done | bytes 204832 | tf_op jit(solution)/shard_map/ppermute | solution.py:376
  32.0 2.8 %collective-permute-start.7 = (bf16[80,1280]{1,0:T(8,128)(2,1)S(1)}, bf16[80,1280]{1,0:T(8,128)(2,1)}, u32[]{:S(2)}, u32[]{:S(2)}) collective-permute-start(bf16[80,1280]{1,0:T(8,128)(2,1)S(1)} %collective-permute-done.6.rest_6_), channel_id=1, source_target_pairs={{0,4},{4,0},{8,12},{12,8},{16,20},{20,16},{24,28},{28,24},{1,5},{5... | collective-permute-start | bytes 614408 | tf_op jit(solution)/shard_map/ppermute | solution.py:379
  34.8 1.5 %collective-permute-start.5 = (bf16[32,3200]{1,0:T(8,128)(2,1)}, bf16[32,3200]{1,0:T(8,128)(2,1)}, u32[]{:S(2)}, u32[]{:S(2)}) collective-permute-start(bf16[32,3200]{1,0:T(8,128)(2,1)} %fusion), channel_id=1, source_target_pairs={{0,2},{1,3},{2,0},{3,1},{4,6},{5,7},{6,4},{7,5},{8,10},{9,11},{10,... | collective-permute-start | bytes 614408 | tf_op jit(solution)/shard_map/ppermute | solution.py:376
  37.6 1.0 %shard_map.111 = (bf16[1008,320]{1,0:T(8,128)(2,1)S(1)}, bf16[1008,64]{1,0:T(8,128)(2,1)S(1)}) custom-call(s32[2]{0:T(128)S(1)} %pad_add_fusion.span, s32[1,1280]{1,0:T(1,128)S(1)} %broadcast_in_dim.6.near), custom_call_target="tpu_custom_call" | custom-call | tf_op jit(solution)/shard_map/pallas_call | solution.py:452
  38.6 1.7 %collective-permute-done.9.rest_9_ = bf16[80,1280]{1,0:T(8,128)(2,1)} collective-permute-done((bf16[80,1280]{1,0:T(8,128)(2,1)S(1)}, bf16[80,1280]{1,0:T(8,128)(2,1)}, u32[]{:S(2)}, u32[]{:S(2)}) %collective-permute-start.9) | collective-permute-done | bytes 204832 | tf_op jit(solution)/shard_map/ppermute | solution.py:379
  40.3 0.8 %collective-permute-done.8.rest_8_ = bf16[80,1280]{1,0:T(8,128)(2,1)} collective-permute-done((bf16[80,1280]{1,0:T(8,128)(2,1)S(1)}, bf16[80,1280]{1,0:T(8,128)(2,1)}, u32[]{:S(2)}, u32[]{:S(2)}) %collective-permute-start.8) | collective-permute-done | bytes 204832 | tf_op jit(solution)/shard_map/ppermute | solution.py:379
  41.1 2.2 %collective-permute-done.7.rest_7_ = bf16[80,1280]{1,0:T(8,128)(2,1)} collective-permute-done((bf16[80,1280]{1,0:T(8,128)(2,1)S(1)}, bf16[80,1280]{1,0:T(8,128)(2,1)}, u32[]{:S(2)}, u32[]{:S(2)}) %collective-permute-start.7) | collective-permute-done | bytes 204832 | tf_op jit(solution)/shard_map/ppermute | solution.py:379
  43.8 1.1 %add_convert_fusion.rest_0_ = bf16[32,3200]{1,0:T(8,128)(2,1)S(1)} fusion(bf16[32,3200]{1,0:T(8,128)(2,1)} %collective-permute-done.5, f32[32,3200]{1,0:T(8,128)S(1)} %get-tuple-element.37, bf16[32,3200]{1,0:T(8,128)(2,1)} %copy-done.18), kind=kLoop, calls=%fused_computation | loop fusion | flops 512000 | bytes 1024000 | tf_op jit(solution)/shard_map/convert_element_type | solution.py:464
  44.9 3.8 %collective-permute-done.18.rest_4_ = bf16[80,2304]{1,0:T(8,128)(2,1)} collective-permute-done((bf16[80,2304]{1,0:T(8,128)(2,1)}, bf16[80,2304]{1,0:T(8,128)(2,1)}, u32[]{:S(2)}, u32[]{:S(2)}) %collective-permute-start.18) | collective-permute-done | bytes 368672 | tf_op jit(solution)/shard_map/ppermute | solution.py:376
  49.3 1.1 %collective-permute-done.14.rest_11_ = bf16[80,1280]{1,0:T(8,128)(2,1)S(1)} collective-permute-done((bf16[80,1280]{1,0:T(8,128)(2,1)}, bf16[80,1280]{1,0:T(8,128)(2,1)S(1)}, u32[]{:S(2)}, u32[]{:S(2)}) %collective-permute-start.14) | collective-permute-done | bytes 204832 | tf_op jit(solution)/shard_map/ppermute | solution.py:373
  51.0 1.1 %collective-permute-done.16.rest_13_ = bf16[80,1280]{1,0:T(8,128)(2,1)S(1)} collective-permute-done((bf16[80,1280]{1,0:T(8,128)(2,1)}, bf16[80,1280]{1,0:T(8,128)(2,1)S(1)}, u32[]{:S(2)}, u32[]{:S(2)}) %collective-permute-start.16) | collective-permute-done | bytes 204832 | tf_op jit(solution)/shard_map/ppermute | solution.py:373
  53.0 1.5 %collective-permute-start.21 = (bf16[80,2304]{1,0:T(8,128)(2,1)}, bf16[80,2304]{1,0:T(8,128)(2,1)S(1)}, u32[]{:S(2)}, u32[]{:S(2)}) collective-permute-start(bf16[80,2304]{1,0:T(8,128)(2,1)} %copy-done.14), channel_id=1, source_target_pairs={{0,2},{1,3},{2,0},{3,1},{4,6},{5,7},{6,4},{7,5},{8,10},{9,11},{10,... | collective-permute-start | bytes 1105928 | tf_op jit(solution)/shard_map/ppermute | solution.py:376
  54.5 0.9 %copy-done.8 = bf16[64,1280]{1,0:T(8,128)(2,1)S(1)} copy-done((bf16[64,1280]{1,0:T(8,128)(2,1)S(1)}, bf16[64,1280]{1,0:T(8,128)(2,1)}, u32[]{:S(2)}) %copy-start.8) | copy-done | bytes 163864
  55.4 10.3 %shard_map.112 = (bf16[1008,640]{1,0:T(8,128)(2,1)S(1)}, bf16[496,1280]{1,0:T(8,128)(2,1)S(1)}) custom-call(s32[2]{0:T(128)S(1)} %pad_add_fusion.span, bf16[1008,320]{1,0:T(8,128)(2,1)S(1)} %get-tuple-element.40.hot5, bf16[1008,64]{1,0:T(8,128)(2,1)S(1)} %get-tuple-element.41.hot1, bf16[64,1280]{1,0:T(8,128)(2,1)S(1)} %copy-done.8, f32[2,640]{1,0:T(2,128)S(1)} %copy-done.12, ...), custom_call_target="tpu_custom_call" | custom-call | tf_op jit(solution)/shard_map/pallas_call | solution.py:475
  66.7 0.9 %collective-permute-done.22.rest_8_ = bf16[80,2304]{1,0:T(8,128)(2,1)S(1)} collective-permute-done((bf16[80,2304]{1,0:T(8,128)(2,1)}, bf16[80,2304]{1,0:T(8,128)(2,1)S(1)}, u32[]{:S(2)}, u32[]{:S(2)}) %collective-permute-start.22) | collective-permute-done | bytes 368672 | tf_op jit(solution)/shard_map/ppermute | solution.py:373
  69.0 6.9 %shard_map.113 = bf16[496,1280]{1,0:T(8,128)(2,1)} custom-call(bf16[1008,640]{1,0:T(8,128)(2,1)S(1)} %get-tuple-element.51.ci, bf16[496,1280]{1,0:T(8,128)(2,1)S(1)} %get-tuple-element.52.hid, f32[2,640]{1,0:T(2,128)S(1)} %copy-done.12, bf16[2,160,3200]{2,1,0:T(8,128)(2,1)S(1)} %copy-done.1, bf16[2,160,1280]{2,1,0:T(8,128)(2,1)S(1)} %copy-done.3, ...), custom_call_target="tpu_custom_call" | custom-call | tf_op jit(solution)/shard_map/pallas_call | solution.py:495
  (77 shorter events, 9.0 us)
Async XLA Ops:
  6.2 16.3 %copy-start.1 = (bf16[2,160,3200]{2,1,0:T(8,128)(2,1)S(1)}, bf16[2,160,3200]{2,1,0:T(8,128)(2,1)}, u32[]{:S(2)}) copy-start(bf16[2,160,3200]{2,1,0:T(8,128)(2,1)} %rest_0_.1) | copy-start | bytes 6144004
  6.2 16.3 %copy-start.11 = (f32[2,640]{1,0:T(2,128)S(1)}, f32[2,640]{1,0:T(2,128)}, u32[]{:S(2)}) copy-start(f32[2,640]{1,0:T(2,128)} %gain_mid.1) | copy-start | bytes 15364
  10.0 1.5 %collective-permute-start = (f32[64,640]{1,0:T(8,128)S(1)}, f32[64,640]{1,0:T(8,128)S(1)}, u32[]{:S(2)}, u32[]{:S(2)}) collective-permute-start(f32[64,640]{1,0:T(8,128)S(1)} %get-tuple-element.34), channel_id=1, source_target_pairs={{0,1},{1,0},{2,3},{3,2},{4,5},{5,4},{6,7},{7,6},{8,9},{9,8},{10,11... | collective-permute-start | bytes 491528 | tf_op jit(solution)/shard_map/ppermute | solution.py:373
  11.6 7.9 %collective-permute-start.2 = (s32[384]{0:T(512)S(1)}, s32[384]{0:T(512)S(1)}, u32[]{:S(2)}, u32[]{:S(2)}) collective-permute-start(s32[384]{0:T(512)S(1)} %get-tuple-element.67), channel_id=1, source_target_pairs={{0,4},{4,0},{8,12},{12,8},{16,20},{20,16},{24,28},{28,24},{1,5},{5... | collective-permute-start | bytes 4616 | tf_op jit(solution)/shard_map/ppermute | solution.py:379
  14.2 6.3 %collective-permute-start.1 = (s32[384]{0:T(512)S(1)}, s32[384]{0:T(512)S(1)}, u32[]{:S(2)}, u32[]{:S(2)}) collective-permute-start(s32[384]{0:T(512)S(1)} %get-tuple-element.68), channel_id=1, source_target_pairs={{4,8},{12,16},{20,24},{28,0},{8,4},{16,12},{24,20},{0,28},{5,9},{1... | collective-permute-start | bytes 4616 | tf_op jit(solution)/shard_map/ppermute | solution.py:416
  18.0 4.4 %collective-permute-start.3 = (bf16[64,640]{1,0:T(8,128)(2,1)S(1)}, bf16[64,640]{1,0:T(8,128)(2,1)S(1)}, u32[]{:S(2)}, u32[]{:S(2)}) collective-permute-start(bf16[64,640]{1,0:T(8,128)(2,1)S(1)} %get-tuple-element.63), channel_id=1, source_target_pairs={{0,2},{1,3},{2,0},{3,1},{4,6},{5,7},{6,4},{7,5},{8,10},{9,11},{10,... | collective-permute-start | bytes 245768 | tf_op jit(solution)/shard_map/ppermute | solution.py:376
  22.5 17.8 %copy-start.3 = (bf16[2,160,1280]{2,1,0:T(8,128)(2,1)S(1)}, bf16[2,160,1280]{2,1,0:T(8,128)(2,1)}, u32[]{:S(2)}) copy-start(bf16[2,160,1280]{2,1,0:T(8,128)(2,1)} %rest_1_.1) | copy-start | bytes 2457604
  23.7 30.8 %copy-start.10 = (f32[2,1280]{1,0:T(2,128)S(1)}, f32[2,1280]{1,0:T(2,128)}, u32[]{:S(2)}) copy-start(f32[2,1280]{1,0:T(2,128)} %gain_in.1) | copy-start | bytes 30724
  23.7 30.8 %copy-start.12 = (f32[2,640]{1,0:T(2,128)S(1)}, f32[2,640]{1,0:T(2,128)}, u32[]{:S(2)}) copy-start(f32[2,640]{1,0:T(2,128)} %gain_out.3) | copy-start | bytes 15364
  23.7 1.7 %collective-permute-start.4 = (bf16[32,3200]{1,0:T(8,128)(2,1)S(1)}, bf16[32,3200]{1,0:T(8,128)(2,1)S(1)}, u32[]{:S(2)}, u32[]{:S(2)}) collective-permute-start(bf16[32,3200]{1,0:T(8,128)(2,1)S(1)} %get-tuple-element.38), channel_id=1, source_target_pairs={{0,1},{1,0},{2,3},{3,2},{4,5},{5,4},{6,7},{7,6},{8,9},{9,8},{10,11... | collective-permute-start | bytes 614408 | tf_op jit(solution)/shard_map/ppermute | solution.py:373
  23.8 7.5 %collective-permute-start.6 = (bf16[80,1280]{1,0:T(8,128)(2,1)S(1)}, bf16[80,1280]{1,0:T(8,128)(2,1)S(1)}, u32[]{:S(2)}, u32[]{:S(2)}) collective-permute-start(bf16[80,1280]{1,0:T(8,128)(2,1)S(1)} %copy-done.17), channel_id=1, source_target_pairs={{0,2},{1,3},{2,0},{3,1},{4,6},{5,7},{6,4},{7,5},{8,10},{9,11},{10,... | collective-permute-start | bytes 614408 | tf_op jit(solution)/shard_map/ppermute | solution.py:376
  31.3 9.0 %collective-permute-start.9 = (bf16[80,1280]{1,0:T(8,128)(2,1)S(1)}, bf16[80,1280]{1,0:T(8,128)(2,1)}, u32[]{:S(2)}, u32[]{:S(2)}) collective-permute-start(bf16[80,1280]{1,0:T(8,128)(2,1)S(1)} %collective-permute-done.6.rest_6_), channel_id=1, source_target_pairs={{0,12},{4,8},{8,4},{12,0},{16,28},{20,24},{24,20},{28,16},{1,13},{... | collective-permute-start | bytes 614408 | tf_op jit(solution)/shard_map/ppermute | solution.py:379
  31.5 9.5 %collective-permute-start.8 = (bf16[80,1280]{1,0:T(8,128)(2,1)S(1)}, bf16[80,1280]{1,0:T(8,128)(2,1)}, u32[]{:S(2)}, u32[]{:S(2)}) collective-permute-start(bf16[80,1280]{1,0:T(8,128)(2,1)S(1)} %collective-permute-done.6.rest_6_), channel_id=1, source_target_pairs={{0,8},{4,12},{8,0},{12,4},{16,24},{20,28},{24,16},{28,20},{1,9},{5... | collective-permute-start | bytes 614408 | tf_op jit(solution)/shard_map/ppermute | solution.py:379
  32.0 11.3 %collective-permute-start.7 = (bf16[80,1280]{1,0:T(8,128)(2,1)S(1)}, bf16[80,1280]{1,0:T(8,128)(2,1)}, u32[]{:S(2)}, u32[]{:S(2)}) collective-permute-start(bf16[80,1280]{1,0:T(8,128)(2,1)S(1)} %collective-permute-done.6.rest_6_), channel_id=1, source_target_pairs={{0,4},{4,0},{8,12},{12,8},{16,20},{20,16},{24,28},{28,24},{1,5},{5... | collective-permute-start | bytes 614408 | tf_op jit(solution)/shard_map/ppermute | solution.py:379
  34.8 8.6 %collective-permute-start.5 = (bf16[32,3200]{1,0:T(8,128)(2,1)}, bf16[32,3200]{1,0:T(8,128)(2,1)}, u32[]{:S(2)}, u32[]{:S(2)}) collective-permute-start(bf16[32,3200]{1,0:T(8,128)(2,1)} %fusion), channel_id=1, source_target_pairs={{0,2},{1,3},{2,0},{3,1},{4,6},{5,7},{6,4},{7,5},{8,10},{9,11},{10,... | collective-permute-start | bytes 614408 | tf_op jit(solution)/shard_map/ppermute | solution.py:376
  37.0 11.8 %collective-permute-start.18 = (bf16[80,2304]{1,0:T(8,128)(2,1)}, bf16[80,2304]{1,0:T(8,128)(2,1)}, u32[]{:S(2)}, u32[]{:S(2)}) collective-permute-start(bf16[80,2304]{1,0:T(8,128)(2,1)} %copy-done.15), channel_id=1, source_target_pairs={{0,2},{1,3},{2,0},{3,1},{4,6},{5,7},{6,4},{7,5},{8,10},{9,11},{10,... | collective-permute-start | bytes 1105928 | tf_op jit(solution)/shard_map/ppermute | solution.py:376
  37.6 16.9 %copy-start.5 = (bf16[2,320,640]{2,1,0:T(8,128)(2,1)S(1)}, bf16[2,320,640]{2,1,0:T(8,128)(2,1)}, u32[]{:S(2)}) copy-start(bf16[2,320,640]{2,1,0:T(8,128)(2,1)} %rest_3_.1) | copy-start | bytes 2457604
  40.3 12.6 %collective-permute-start.11 = (bf16[2,160,1280]{2,1,0:T(8,128)(2,1)S(1)}, bf16[2,160,1280]{2,1,0:T(8,128)(2,1)S(1)}, u32[]{:S(2)}, u32[]{:S(2)}) collective-permute-start(bf16[2,160,1280]{2,1,0:T(8,128)(2,1)S(1)} %copy-done.3), channel_id=1, source_target_pairs={{0,1},{1,0},{2,3},{3,2},{4,5},{5,4},{6,7},{7,6},{8,9},{9,8},{10,11... | collective-permute-start | bytes 2457608 | tf_op jit(solution)/shard_map/ppermute | solution.py:373
  41.1 13.4 %collective-permute-start.12 = (bf16[2,320,640]{2,1,0:T(8,128)(2,1)}, bf16[2,320,640]{2,1,0:T(8,128)(2,1)S(1)}, u32[]{:S(2)}, u32[]{:S(2)}) collective-permute-start(bf16[2,320,640]{2,1,0:T(8,128)(2,1)} %rest_3_.1), channel_id=1, source_target_pairs={{0,1},{1,0},{2,3},{3,2},{4,5},{5,4},{6,7},{7,6},{8,9},{9,8},{10,11... | collective-permute-start | bytes 2457608 | tf_op jit(solution)/shard_map/ppermute | solution.py:373
  43.3 25.7 %collective-permute-start.17 = (bf16[2,160,3200]{2,1,0:T(8,128)(2,1)S(1)}, bf16[2,160,3200]{2,1,0:T(8,128)(2,1)S(1)}, u32[]{:S(2)}, u32[]{:S(2)}) collective-permute-start(bf16[2,160,3200]{2,1,0:T(8,128)(2,1)S(1)} %copy-done.1), channel_id=1, source_target_pairs={{0,1},{1,0},{2,3},{3,2},{4,5},{5,4},{6,7},{7,6},{8,9},{9,8},{10,11... | collective-permute-start | bytes 6144008 | tf_op jit(solution)/shard_map/ppermute | solution.py:373
  43.3 5.5 %collective-permute-start.13 = (bf16[80,1280]{1,0:T(8,128)(2,1)S(1)}, bf16[80,1280]{1,0:T(8,128)(2,1)S(1)}, u32[]{:S(2)}, u32[]{:S(2)}) collective-permute-start(bf16[80,1280]{1,0:T(8,128)(2,1)S(1)} %collective-permute-done.6.rest_6_), channel_id=1, source_target_pairs={{0,1},{1,0},{2,3},{3,2},{4,5},{5,4},{6,7},{7,6},{8,9},{9,8},{10,11... | collective-permute-start | bytes 614408 | tf_op jit(solution)/shard_map/ppermute | solution.py:373
  48.8 1.7 %collective-permute-start.14 = (bf16[80,1280]{1,0:T(8,128)(2,1)}, bf16[80,1280]{1,0:T(8,128)(2,1)S(1)}, u32[]{:S(2)}, u32[]{:S(2)}) collective-permute-start(bf16[80,1280]{1,0:T(8,128)(2,1)} %collective-permute-done.7.rest_7_), channel_id=1, source_target_pairs={{0,1},{1,0},{2,3},{3,2},{4,5},{5,4},{6,7},{7,6},{8,9},{9,8},{10,11... | collective-permute-start | bytes 614408 | tf_op jit(solution)/shard_map/ppermute | solution.py:373
  48.8 2.0 %collective-permute-start.15 = (bf16[80,1280]{1,0:T(8,128)(2,1)}, bf16[80,1280]{1,0:T(8,128)(2,1)S(1)}, u32[]{:S(2)}, u32[]{:S(2)}) collective-permute-start(bf16[80,1280]{1,0:T(8,128)(2,1)} %collective-permute-done.8.rest_8_), channel_id=1, source_target_pairs={{0,1},{1,0},{2,3},{3,2},{4,5},{5,4},{6,7},{7,6},{8,9},{9,8},{10,11... | collective-permute-start | bytes 614408 | tf_op jit(solution)/shard_map/ppermute | solution.py:373
  50.4 1.7 %collective-permute-start.16 = (bf16[80,1280]{1,0:T(8,128)(2,1)}, bf16[80,1280]{1,0:T(8,128)(2,1)S(1)}, u32[]{:S(2)}, u32[]{:S(2)}) collective-permute-start(bf16[80,1280]{1,0:T(8,128)(2,1)} %collective-permute-done.9.rest_9_), channel_id=1, source_target_pairs={{0,1},{1,0},{2,3},{3,2},{4,5},{5,4},{6,7},{7,6},{8,9},{9,8},{10,11... | collective-permute-start | bytes 614408 | tf_op jit(solution)/shard_map/ppermute | solution.py:373
  50.7 1.7 %collective-permute-start.10 = (bf16[32,3200]{1,0:T(8,128)(2,1)S(1)}, bf16[32,3200]{1,0:T(8,128)(2,1)S(1)}, u32[]{:S(2)}, u32[]{:S(2)}) collective-permute-start(bf16[32,3200]{1,0:T(8,128)(2,1)S(1)} %add_convert_fusion.rest_0_), channel_id=1, source_target_pairs={{0,1},{1,0},{2,3},{3,2},{4,5},{5,4},{6,7},{7,6},{8,9},{9,8},{10,11... | collective-permute-start | bytes 614408 | tf_op jit(solution)/shard_map/ppermute | solution.py:373
  52.1 13.6 %collective-permute-start.20 = (bf16[80,2304]{1,0:T(8,128)(2,1)}, bf16[80,2304]{1,0:T(8,128)(2,1)S(1)}, u32[]{:S(2)}, u32[]{:S(2)}) collective-permute-start(bf16[80,2304]{1,0:T(8,128)(2,1)} %collective-permute-done.18.rest_4_), channel_id=1, source_target_pairs={{0,8},{4,12},{8,0},{12,4},{16,24},{20,28},{24,16},{28,20},{1,9},{5... | collective-permute-start | bytes 1105928 | tf_op jit(solution)/shard_map/ppermute | solution.py:379
  52.4 13.8 %collective-permute-start.19 = (bf16[80,2304]{1,0:T(8,128)(2,1)}, bf16[80,2304]{1,0:T(8,128)(2,1)S(1)}, u32[]{:S(2)}, u32[]{:S(2)}) collective-permute-start(bf16[80,2304]{1,0:T(8,128)(2,1)} %collective-permute-done.18.rest_4_), channel_id=1, source_target_pairs={{0,4},{4,0},{8,12},{12,8},{16,20},{20,16},{24,28},{28,24},{1,5},{5... | collective-permute-start | bytes 1105928 | tf_op jit(solution)/shard_map/ppermute | solution.py:379
  53.0 13.4 %collective-permute-start.21 = (bf16[80,2304]{1,0:T(8,128)(2,1)}, bf16[80,2304]{1,0:T(8,128)(2,1)S(1)}, u32[]{:S(2)}, u32[]{:S(2)}) collective-permute-start(bf16[80,2304]{1,0:T(8,128)(2,1)} %copy-done.14), channel_id=1, source_target_pairs={{0,2},{1,3},{2,0},{3,1},{4,6},{5,7},{6,4},{7,5},{8,10},{9,11},{10,... | collective-permute-start | bytes 1105928 | tf_op jit(solution)/shard_map/ppermute | solution.py:376
  65.7 2.0 %collective-permute-start.22 = (bf16[80,2304]{1,0:T(8,128)(2,1)}, bf16[80,2304]{1,0:T(8,128)(2,1)S(1)}, u32[]{:S(2)}, u32[]{:S(2)}) collective-permute-start(bf16[80,2304]{1,0:T(8,128)(2,1)} %collective-permute-done.18.rest_4_), channel_id=1, source_target_pairs={{0,1},{1,0},{2,3},{3,2},{4,5},{5,4},{6,7},{7,6},{8,9},{9,8},{10,11... | collective-permute-start | bytes 1105928 | tf_op jit(solution)/shard_map/ppermute | solution.py:373
  65.7 2.2 %collective-permute-start.24 = (bf16[80,2304]{1,0:T(8,128)(2,1)S(1)}, bf16[80,2304]{1,0:T(8,128)(2,1)S(1)}, u32[]{:S(2)}, u32[]{:S(2)}) collective-permute-start(bf16[80,2304]{1,0:T(8,128)(2,1)S(1)} %collective-permute-done.20.rest_6_), channel_id=1, source_target_pairs={{0,1},{1,0},{2,3},{3,2},{4,5},{5,4},{6,7},{7,6},{8,9},{9,8},{10,11... | collective-permute-start | bytes 1105928 | tf_op jit(solution)/shard_map/ppermute | solution.py:373
  66.2 2.2 %collective-permute-start.23 = (bf16[80,2304]{1,0:T(8,128)(2,1)S(1)}, bf16[80,2304]{1,0:T(8,128)(2,1)S(1)}, u32[]{:S(2)}, u32[]{:S(2)}) collective-permute-start(bf16[80,2304]{1,0:T(8,128)(2,1)S(1)} %collective-permute-done.19.rest_5_), channel_id=1, source_target_pairs={{0,1},{1,0},{2,3},{3,2},{4,5},{5,4},{6,7},{7,6},{8,9},{9,8},{10,11... | collective-permute-start | bytes 1105928 | tf_op jit(solution)/shard_map/ppermute | solution.py:373
  66.3 2.7 %collective-permute-start.25 = (bf16[80,2304]{1,0:T(8,128)(2,1)S(1)}, bf16[80,2304]{1,0:T(8,128)(2,1)S(1)}, u32[]{:S(2)}, u32[]{:S(2)}) collective-permute-start(bf16[80,2304]{1,0:T(8,128)(2,1)S(1)} %collective-permute-done.21.rest_7_), channel_id=1, source_target_pairs={{0,1},{1,0},{2,3},{3,2},{4,5},{5,4},{6,7},{7,6},{8,9},{9,8},{10,11... | collective-permute-start | bytes 1105928 | tf_op jit(solution)/shard_map/ppermute | solution.py:373
  (15 other events, 37.8 us)

commit v5 on v4

--- a/solution.py
+++ b/solution.py
@@ -24,6 +24,7 @@
 SMEM = pl.BlockSpec(memory_space=pltpu.SMEM)
 ANY = pl.BlockSpec(memory_space=pl.ANY)
 HBM = pl.BlockSpec(memory_space=pltpu.HBM)
+FREE = pl.CostEstimate(flops=0, bytes_accessed=0, transcendentals=0)
 CUT_A = 18 * 128
 CUT_B = 17 * 128
 
@@ -172,16 +173,17 @@
     depth = wo.shape[0] - CODES
     if split:
         core = lax.rem(lax.axis_index("roll"), 2)
-        taps = ((w[0], core * SLOT, SLOT), (w[1], (1 - core) * SLOT, SLOT))
-        w = w[2:]
+        taps = [(t, core * SLOT, SLOT, 0) for t in w[:2]] + [(t, (1 - core) * SLOT, SLOT, 0) for t in w[2:4]]
+        taps = [(t, at, n, i % 2) for i, (t, at, n, _) in enumerate(taps)]
+        w = w[4:]
     else:
-        taps = ((w[0], 0, CODES),)
+        taps = [(w[0], 0, CODES, 0)]
         w = w[1:]
     first = [
         pltpu.make_async_copy(
-            t.at[:, k * H : (k + 1) * H], tw.at[pl.ds(pl.multiple_of(k * CODES + at, 16), n)], sem.at[0]
+            t.at[:, k * H : (k + 1) * H], tw.at[i, pl.ds(pl.multiple_of(k * CODES + at, 16), n)], sem.at[0]
         )
-        for t, at, n in taps
+        for t, at, n, i in taps
         for k in range(KERNEL)
     ]
     first.append(pltpu.make_async_copy(table, wo.at[depth:], sem.at[0]))
@@ -241,8 +243,11 @@
             wait(copies)
 
     def mix(b):
-        once(b, first)
-        state[b] = dot(hot5[cuts[b] : cuts[b + 1]], tw[...])
+        if b == 0:
+            wait(first)
+            if split:
+                tw[0] = (tw[0].astype(F32) + tw[1].astype(F32)).astype(BF)
+        state[b] = dot(hot5[cuts[b] : cuts[b + 1]], tw[0])
 
     def act(b):
         state[b] = gelu(norm(state[b], gain_out[0:1])).astype(BF)
@@ -271,56 +276,113 @@
     stagger((mix, act, update, enter, widen, leave))
 
 
+def conv_copies(src, col, width, wt, per_tap, row, n, sem):
+    copies = []
+    done = 0
+    while done < width:
+        tap, inner = divmod(col + done, H)
+        step = min(H - inner, width - done)
+        copies.append(
+            pltpu.make_async_copy(
+                src.at[:, done : done + step],
+                wt.at[pl.ds(pl.multiple_of(tap * per_tap + row, 16), n), inner : inner + step],
+                sem,
+            )
+        )
+        done += step
+    return copies
+
+
+HEAD = 256
+TAIL = H - HEAD
+
+
+def windows(ci, lo, hi, first, width):
+    first = pl.multiple_of(first, 128)
+    return jnp.concatenate(
+        [ci[lo + k * DIL1 : hi + k * DIL1, pl.ds(first, width)] for k in range(KERNEL)], axis=1
+    )
+
+
+def head_kernel(ci, w_conv, near_conv, out, wt, sem):
+    x, core, _, _ = place()
+    n = w_conv.shape[1]
+    short = HEAD - n
+    done = None
+    for xx in range(2):
+        for cc in range(2):
+            copies = []
+            for c, w in ((cc, w_conv), (1 - cc, near_conv)):
+                if c == xx:
+                    copies += conv_copies(w.at[1], 0, KERNEL * H, wt, HEAD, short * xx, n, sem)
+                else:
+                    part = w.at[1, (n - short) * xx : (n - short) * xx + short]
+                    copies += conv_copies(part, 0, KERNEL * H, wt, HEAD, n * (1 - xx), short, sem)
+            done = copies
+
+            @pl.when((x == xx) & (core == cc))
+            def _():
+                start(copies)
+
+    rows = out.shape[0]
+    half = 16 * ((rows + 31) // 32)
+    for b, (lo, hi) in enumerate(((0, half), (half, rows))):
+        lhs = windows(ci, lo, hi, x * TAIL, HEAD)
+        if b == 0:
+            wait(done)
+        out[lo:hi] = dot(lhs, wt[...])
+
+
 def last_kernel(split, ci, hid, gain_out, *rest):
     *w, out, wt, wo, sem = rest
-
-    def conv(src, col, width, row, n):
-        copies = []
-        done = 0
-        while done < width:
-            tap, inner = divmod(col + done, H)
-            step = min(H - inner, width - done)
-            copies.append(
-                pltpu.make_async_copy(
-                    src.at[:, done : done + step],
-                    wt.at[pl.ds(tap * H + row, n), inner : inner + step],
-                    sem.at[0],
-                )
-            )
-            done += step
-        return copies
-
     if not split:
-        conv_copies = conv(w[0], 0, KERNEL * H, 0, H)
-        out_copies = [pltpu.make_async_copy(w[1], wo, sem.at[1])]
-        start(conv_copies + out_copies)
+        conv_in = conv_copies(w[0], 0, KERNEL * H, wt, H, 0, H, sem.at[0])
+        out_in = [pltpu.make_async_copy(w[1], wo, sem.at[1])]
+        start(conv_in + out_in)
+        first, width = 0, H
     else:
-        w_conv, w_out, near_conv, near_out = w[:4]
-        parts, near_parts = w[4:8], w[8:12]
+        head, w_conv, w_out, near_conv, near_out = w[:5]
+        parts, near_parts = w[5:9], w[9:13]
         x, core, y, z = place()
         n = w_out.shape[1]
         half = n // 2
+        left = 2 * n - HEAD
         rest_cols = KERNEL * H - CUT_B
-        conv_copies, out_copies = [], []
-        for c, v, o in ((core, w_conv, w_out), (1 - core, near_conv, near_out)):
+        first, width = (1 - x) * HEAD, TAIL
+        out_in = []
+        for c, o in ((core, w_out), (1 - core, near_out)):
             row = pl.multiple_of((2 * x + c) * n, 16)
-            conv_copies += conv(v.at[1], 0, KERNEL * H, row, n)
-            out_copies.append(pltpu.make_async_copy(o.at[1], wo.at[pl.ds(row, n)], sem.at[1]))
+            out_in.append(pltpu.make_async_copy(o.at[1], wo.at[pl.ds(row, n)], sem.at[1]))
+        from_row = pl.multiple_of((n - left) * (1 - x), 16)
+        own_in, near_in = [
+            conv_copies(v.at[1, pl.ds(from_row, left)], 0, KERNEL * H, wt, TAIL, 2 * n * x, left, sem.at[0])
+            for v in (w_conv, near_conv)
+        ]
+
+        @pl.when(core + x == 1)
+        def _():
+            start(own_in)
+
+        @pl.when(core + x != 1)
+        def _():
+            start(near_in)
 
         def far(head, tail):
             cv, out = [], []
             for c, of in ((core, parts), (1 - core, near_parts)):
+                at = c * n + left * (1 - x)
                 for p, zz in zip(head, (z, 1 - z)):
+                    cv += conv_copies(of[p], 0, CUT_A, wt, TAIL, at + zz * half, half, sem.at[0])
+                for p, zz in zip(tail, (z, 1 - z)):
+                    skip = CUT_A - CUT_B
+                    cv += conv_copies(
+                        of[p].at[:, skip:rest_cols], CUT_A, rest_cols - skip, wt, TAIL, at + zz * half, half, sem.at[0]
+                    )
                     row = pl.multiple_of((2 * (1 - x) + c) * n + zz * half, 16)
-                    cv += conv(of[p], 0, CUT_A, row, half)
-                for p, zz in zip(tail, (z, 1 - z)):
-                    row = pl.multiple_of((2 * (1 - x) + c) * n + zz * half, 16)
-                    skip = CUT_A - CUT_B
-                    cv += conv(of[p].at[:, skip:rest_cols], CUT_A, rest_cols - skip, row, half)
                     out.append(pltpu.make_async_copy(of[p].at[:, rest_cols:], wo.at[pl.ds(row, half)], sem.at[1]))
             return cv, out
 
-        start(conv_copies + out_copies)
+        start(out_in)
         far0, far1 = far((0, 2), (1, 3)), far((1, 3), (0, 2))
 
         @pl.when(y == 0)
@@ -331,25 +393,27 @@
         def _():
             start(far1[0] + far1[1])
 
-        conv_copies += far0[0]
-        out_copies += far0[1]
+        conv_in = own_in + far0[0]
+        out_in += far0[1]
 
     rows = out.shape[0]
     cuts = [0, 16 * ((rows + 31) // 32), rows]
     state = [None, None]
 
     def mix(b):
-        lhs = jnp.concatenate([ci[cuts[b] + k * DIL1 : cuts[b + 1] + k * DIL1] for k in range(KERNEL)], axis=1)
+        lhs = windows(ci, cuts[b], cuts[b + 1], first, width)
         if b == 0:
-            wait(conv_copies)
+            wait(conv_in)
         state[b] = dot(lhs, wt[...])
+        if split:
+            state[b] += head[cuts[b] : cuts[b + 1]]
 
     def act(b):
         state[b] = gelu(norm(state[b], gain_out[1:2])).astype(BF)
 
     def update(b):
         if b == 0:
-            wait(out_copies)
+            wait(out_in)
         hidden = hid[cuts[b] : cuts[b + 1]].astype(F32)
         out[cuts[b] : cuts[b + 1]] = (hidden + dot(state[b], wo[...])).astype(BF)
 
@@ -399,7 +463,8 @@
             pltpu.VMEM((CODES, width), F32),
             pltpu.SemaphoreType.DMA((2,)),
         ],
-        compiler_params=params(48),
+        cost_estimate=FREE,
+        compiler_params=params(60),
     )(embed_table, break_vec, gain_in, w_in, conv_w, w_out)
 
     if split:
@@ -407,26 +472,14 @@
         near_in, near_conv, near_out = [core_swap(after(w, own)) for w in (w_in, conv_w, w_out)]
         far_a = x_swap(parts[0])
         other = x_swap(own.astype(BF))
-        codes = after(codes, own)
-        low = seq_at % 2 == 0
-        ends = codes[rows - REACH :], codes[:REACH]
-        even = seq_swap(jnp.where(low, *ends), 1)
-        pairs = [(i, i + 1) for i in range(1, seqs - 1, 2)]
-        pairs.append((seqs - 1, 0))
-        odd = lax.ppermute(jnp.where(low, *ends[::-1]), "seq", pairs + [(j, i) for i, j in pairs])
-        before, behind = jnp.where(low, odd, even), jnp.where(low, even, odd)
         far_b = x_swap(after(parts[1], own))
-        other = after(other, before, behind)
+        other = after(other, far_a)
     else:
         own = lax.psum(part, "roll")
         other = jnp.zeros((CODES, H), BF)
         pairs = [(i, i + 1) for i in range(seqs - 1)]
         before = lax.ppermute(codes[rows - REACH :], "seq", pairs)
         behind = lax.ppermute(codes[:REACH], "seq", [(j, i) for i, j in pairs])
-    count = rows + 2 * REACH
-    spare = jnp.zeros((-count % 128,), jnp.int32)
-    near = jnp.concatenate([before, codes, behind, spare])[None]
-
     wide = KERNEL * H
     shapes = [(SLOT, F32), (SLOT, BF)] if split else [(CODES, F32)]
     taps = pl.pallas_call(
@@ -439,15 +492,25 @@
             pltpu.VMEM((CODES, wide), F32),
             pltpu.SemaphoreType.DMA,
         ],
+        cost_estimate=FREE,
         compiler_params=params(12),
     )(own, other, gain_mid, conv_w)
     if split:
-        mine = taps[0] + core_swap(taps[1]).astype(F32)
-        sent = mine.astype(BF)
+        sent = (taps[0] + core_swap(taps[1]).astype(F32)).astype(BF)
+        received = x_swap(sent)
+        near_sent = core_swap(sent)
         relay = after(far_a, sent)
         parts_a = [far_a] + [seq_swap(relay, b) for b in (1, 2, 3)]
-        near = after(near, sent)
-        other = x_swap(sent)
+        codes = after(codes, sent)
+        ends = codes[rows - REACH :], codes[:REACH]
+        low = seq_at % 2 == 0
+        even = seq_swap(jnp.where(low, *ends), 1)
+        pairs = [(i, i + 1) for i in range(1, seqs - 1, 2)]
+        pairs.append((seqs - 1, 0))
+        odd = lax.ppermute(jnp.where(low, *ends[::-1]), "seq", pairs + [(j, i) for i, j in pairs])
+        before, behind = jnp.where(low, odd, even), jnp.where(low, even, odd)
+    spare = jnp.zeros((-(rows + 2 * REACH) % 128,), jnp.int32)
+    near = jnp.concatenate([before, codes, behind, spare])[None]
 
     hot5, hot1 = pl.pallas_call(
         hot_kernel,
@@ -457,16 +520,18 @@
         ),
         in_specs=[SMEM, VMEM],
         out_specs=(VMEM, VMEM),
+        cost_estimate=FREE,
         compiler_params=params(12),
     )(span, near)
 
     if split:
-        mine = (mine + after(other, hot1, *parts_a).astype(F32)).astype(BF)
-        theirs = core_swap(mine)
-        near_a = [core_swap(relay)] + [core_swap(after(p, mine)) for p in parts_a[1:]]
-        relay = after(far_b, mine)
-        parts_b = [far_b, seq_swap(relay, 1), seq_swap(relay, 2), x_swap(after(parts[2], mine))]
-        weights_a = [mine, theirs, w_out, w_in, near_out, near_in] + parts_a + near_a
+        received = after(received, hot1, *parts_a)
+        near_received = core_swap(received)
+        near_a = [core_swap(relay)] + [core_swap(after(p, received)) for p in parts_a[1:]]
+        relay = after(far_b, received)
+        parts_b = [far_b, seq_swap(relay, 1), seq_swap(relay, 2), x_swap(after(parts[2], received))]
+        near_b = [core_swap(relay)]
+        weights_a = [sent, received, near_sent, near_received, w_out, w_in, near_out, near_in] + parts_a + near_a
     else:
         taps = lax.psum(taps[0], "roll").astype(BF)
         gather = lambda w: lax.all_gather(w, "roll", axis=0, tiled=True)
@@ -481,27 +546,39 @@
         in_specs=[SMEM, VMEM, VMEM, ANY, VMEM, VMEM, VMEM] + [HBM if w is w_out or w is w_in else ANY for w in weights_a],
         out_specs=(VMEM, VMEM),
         scratch_shapes=[
-            pltpu.VMEM((KERNEL * CODES, H), BF),
+            pltpu.VMEM((2, KERNEL * CODES, H), BF),
             pltpu.VMEM((H + CODES, width), BF),
             pltpu.VMEM((width, H), BF),
             pltpu.SemaphoreType.DMA((3,)),
         ],
+        cost_estimate=FREE,
         compiler_params=params(30),
     )(span, hot5, hot1, table, gain_out, gain_in, gain_mid, *weights_a)
 
     if split:
-        near_b = [core_swap(after(p, ci)) for p in parts_b]
-        weights_b = [conv_w, w_out, near_conv, near_out] + parts_b + near_b
+        near_b += [core_swap(after(p, ci)) for p in parts_b[1:]]
+        head = pl.pallas_call(
+            head_kernel,
+            out_shape=jax.ShapeDtypeStruct((rows, H), F32),
+            in_specs=[VMEM, HBM, ANY],
+            out_specs=VMEM,
+            scratch_shapes=[pltpu.VMEM((KERNEL * HEAD, H), BF), pltpu.SemaphoreType.DMA],
+            cost_estimate=FREE,
+            compiler_params=params(16),
+        )(ci, conv_w, near_conv)
+        weights_b = [head, conv_w, w_out, near_conv, near_out] + parts_b + near_b
     out = pl.pallas_call(
         functools.partial(last_kernel, split),
         out_shape=jax.ShapeDtypeStruct((rows, width), BF),
-        in_specs=[VMEM] * 3 + [HBM if w is w_out or w is conv_w else ANY for w in weights_b],
+        in_specs=[VMEM] * 3
+        + [HBM if w is w_out or w is conv_w else VMEM if split and w is head else ANY for w in weights_b],
         out_specs=VMEM,
         scratch_shapes=[
-            pltpu.VMEM((KERNEL * H, H), BF),
+            pltpu.VMEM((KERNEL * (TAIL if split else H), H), BF),
             pltpu.VMEM((H, width), BF),
             pltpu.SemaphoreType.DMA((2,)),
         ],
+        cost_estimate=FREE,
         compiler_params=params(24),
     )(ci, hid, gain_out, *weights_b)
     return out[None]

time: 76.5 us -> 63.4 us (0.83)
  local copies, waits for them, and re-layouts: 9.36 us -> 2.18 us
  waiting for transfers between devices: 22.4 us -> 16.7 us
  Pallas kernels: 21 us -> 22.2 us
  other arithmetic: 2.05 us -> 1.15 us
    unnamed x42 -> x18, local copies, waits for them, and re-layouts: 9.28 us -> 2.09 us
    ppermute x5, waiting for transfers between devices: 10.9 us -> 5.08 us  [x_swap(): return lax.ppermute(x, 'roll', [(i, i ^ 2) for i in range(rolls)])]
    ppermute x1, waiting for transfers between devices: 1 us -> 3.77 us  [per_device(): lax.ppermute(jnp.where(low, *ends[::-1]), 'seq', pairs + [(j, i) for i, j...]
    ppermute x14 -> x15, waiting for transfers between devices: 5.72 us -> 3.09 us  [core_swap(): return lax.ppermute(x, 'roll', [(i, i ^ 1) for i in range(rolls)])]
    pallas_call x0 -> x1, Pallas kernels: none -> 2.41 us  [per_device(): pl.pallas_call(head_kernel, out_shape=jax.ShapeDtypeStruct((rows, H), F32...]
    ppermute x6, starting transfers between devices: 6.99 us -> 4.81 us  [seq_swap(): return lax.ppermute(x, 'seq', [(i, i ^ bits) for i in range(seqs)])]
    ppermute x5, starting transfers between devices: 6.57 us -> 8.43 us  [x_swap(): return lax.ppermute(x, 'roll', [(i, i ^ 2) for i in range(rolls)])]
    convert_element_type x2 -> x1, other arithmetic: 1.87 us -> 0.05 us  [per_device(): sent = (taps[0] + core_swap(taps[1]).astype(F32)).astype(BF)]
  transfers between devices with their start and end apart: 26 -> 27, of which waited for: 15 -> 10; matrix products, arithmetic and copies ran while one was open for 3% -> 2% of each run, Pallas kernels for 15% -> 20%
where the time goes in v5:
time: 63.4 us; the launch traced here: 63.2 us
  Pallas kernels  22.2 us (35%)
  starting transfers between devices  19.9 us (31%)
  waiting for transfers between devices  16.7 us (26%)
  local copies, waits for them, and re-layouts  2.18 us (3%)
  other arithmetic  1.15 us (2%)
  between operations  1.01 us (2%)
    pallas_call x1, Pallas kernels, per_device(): pl.pallas_call(functools.partial(rows_kernel, split), out_shape=(jax.Shap...  9.35 us
    ppermute x5, starting transfers between devices, x_swap(): return lax.ppermute(x, 'roll', [(i, i ^ 2) for i in range(rolls)])  8.43 us
    pallas_call x1, Pallas kernels, per_device(): pl.pallas_call(functools.partial(last_kernel, split), out_shape=jax.Shape...  5.18 us
    ppermute x5, waiting for transfers between devices, x_swap(): return lax.ppermute(x, 'roll', [(i, i ^ 2) for i in range(rolls)])  5.08 us
    ppermute x6, starting transfers between devices, seq_swap(): return lax.ppermute(x, 'seq', [(i, i ^ bits) for i in range(seqs)])  4.81 us
    ppermute x6, waiting for transfers between devices, seq_swap(): return lax.ppermute(x, 'seq', [(i, i ^ bits) for i in range(seqs)])  4.74 us
    ppermute x1, waiting for transfers between devices, per_device(): lax.ppermute(jnp.where(low, *ends[::-1]), 'seq', pairs + [(j, i) for i, j...  3.77 us
    ppermute x1, starting transfers between devices, per_device(): lax.ppermute(jnp.where(low, *ends[::-1]), 'seq', pairs + [(j, i) for i, j...  3.43 us
  transfers between devices with their start and end apart: 27, of which 10 were waited for; matrix products, arithmetic and copies ran while one was open for 2% of the time, Pallas kernels for 20%

profile of v5, /device:TPU:0, one launch (start us, length us, event | category | flops | bytes accessed | tf_op | source)
XLA Modules:
  0.0 63.2 jit_solution(13441394411557218152)
XLA Ops:
  0.0 3.1 %shard_map.109 = (bf16[64,1280]{1,0:T(8,128)(2,1)}, f32[64,640]{1,0:T(8,128)}, bf16[80,1280]{1,0:T(8,128)(2,1)}, bf16[80,2304]{1,0:T(8,128)(2,1)}, bf16[80,2304]{1,0:T(8,128)(2,1)}) custom-call(f32[30,1280]{1,0:T(8,128)} %embed.1, f32[1280]{0:T(1024)} %brk.1, f32[2,1280]{1,0:T(2,128)} %gain_in.1, bf16[2,320,640]{2,1,0:T(8,128)(2,1)} %rest_5_.1, ...), custom_call_target="tpu_custom_call" | custom-call | tf_op jit(solution)/shard_map/pallas_call | solution.py:453
  3.1 0.5 collective-permute-start
  3.7 2.6 %collective-permute-start.2 = (bf16[80,1280]{1,0:T(8,128)(2,1)}, bf16[80,1280]{1,0:T(8,128)(2,1)}, u32[]{:S(2)}, u32[]{:S(2)}) collective-permute-start(bf16[80,1280]{1,0:T(8,128)(2,1)} %get-tuple-element.33), channel_id=1, source_target_pairs={{0,2},{1,3},{2,0},{3,1},{4,6},{5,7},{6,4},{7,5},{8,10},{9,11},{10,... | collective-permute-start | bytes 614408 | tf_op jit(solution)/shard_map/ppermute | solution.py:440
  6.2 0.9 %fusion = (bf16[64,640]{1,0:T(8,128)(2,1)S(1)}, f32[64,640]{1,0:T(8,128)S(1)}) fusion(f32[64,640]{1,0:T(8,128)} %get-tuple-element.32, f32[64,640]{1,0:T(8,128)S(1)} %collective-permute-done), kind=kLoop, calls=%fused_computation.7 | loop fusion | flops 81920 | bytes 573440 | tf_op jit(solution)/shard_map/convert_element_type | solution.py:474
  7.2 1.6 %collective-permute-start.1 = (bf16[64,640]{1,0:T(8,128)(2,1)S(1)}, bf16[64,640]{1,0:T(8,128)(2,1)S(1)}, u32[]{:S(2)}, u32[]{:S(2)}) collective-permute-start(bf16[64,640]{1,0:T(8,128)(2,1)S(1)} %get-tuple-element.59), channel_id=1, source_target_pairs={{0,2},{1,3},{2,0},{3,1},{4,6},{5,7},{6,4},{7,5},{8,10},{9,11},{10,... | collective-permute-start | bytes 245768 | tf_op jit(solution)/shard_map/ppermute | solution.py:440
  8.8 3.7 %collective-permute-done.2.rest_8_ = bf16[80,1280]{1,0:T(8,128)(2,1)} collective-permute-done((bf16[80,1280]{1,0:T(8,128)(2,1)}, bf16[80,1280]{1,0:T(8,128)(2,1)}, u32[]{:S(2)}, u32[]{:S(2)}) %collective-permute-start.2) | collective-permute-done | bytes 204832 | tf_op jit(solution)/shard_map/ppermute | solution.py:440
  12.5 1.4 %collective-permute-done.1.other = bf16[64,640]{1,0:T(8,128)(2,1)S(1)} collective-permute-done((bf16[64,640]{1,0:T(8,128)(2,1)S(1)}, bf16[64,640]{1,0:T(8,128)(2,1)S(1)}, u32[]{:S(2)}, u32[]{:S(2)}) %collective-permute-start.1) | collective-permute-done | bytes 81952 | tf_op jit(solution)/shard_map/ppermute | solution.py:440
  13.9 1.2 %shard_map.110 = (f32[32,3200]{1,0:T(8,128)S(1)}, bf16[32,3200]{1,0:T(8,128)(2,1)S(1)}) custom-call(f32[64,640]{1,0:T(8,128)S(1)} %get-tuple-element.60.own, bf16[64,640]{1,0:T(8,128)(2,1)S(1)} %collective-permute-done.1.other, f32[2,640]{1,0:T(2,128)S(1)} %copy-done.5, bf16[2,160,3200]{2,1,0:T(8,128)(2,1)S(1)} %copy-done), custom_call_target="tpu_custom_call" | custom-call | tf_op jit(solution)/shard_map/pallas_call | solution.py:485
  15.2 1.8 %collective-permute-start.19 = (bf16[80,2304]{1,0:T(8,128)(2,1)}, bf16[80,2304]{1,0:T(8,128)(2,1)S(1)}, u32[]{:S(2)}, u32[]{:S(2)}) collective-permute-start(bf16[80,2304]{1,0:T(8,128)(2,1)} %get-tuple-element.52), channel_id=1, source_target_pairs={{0,2},{1,3},{2,0},{3,1},{4,6},{5,7},{6,4},{7,5},{8,10},{9,11},{10,... | collective-permute-start | bytes 1105928 | tf_op jit(solution)/shard_map/ppermute | solution.py:440
  17.3 2.6 %collective-permute-start.9 = (bf16[80,1280]{1,0:T(8,128)(2,1)}, bf16[80,1280]{1,0:T(8,128)(2,1)}, u32[]{:S(2)}, u32[]{:S(2)}) collective-permute-start(bf16[80,1280]{1,0:T(8,128)(2,1)} %collective-permute-done.2.rest_8_), channel_id=1, source_target_pairs={{0,12},{4,8},{8,4},{12,0},{16,28},{20,24},{24,20},{28,16},{1,13},{... | collective-permute-start | bytes 614408 | tf_op jit(solution)/shard_map/ppermute | solution.py:443
  19.9 0.5 collective-permute-start.5
  20.4 3.4 %collective-permute-start.4 = (s32[384]{0:T(512)S(1)}, s32[384]{0:T(512)S(1)}, u32[]{:S(2)}, u32[]{:S(2)}) collective-permute-start(s32[384]{0:T(512)S(1)} %get-tuple-element.64), channel_id=1, source_target_pairs={{4,8},{12,16},{20,24},{28,0},{8,4},{16,12},{24,20},{0,28},{5,9},{1... | collective-permute-start | bytes 4616 | tf_op jit(solution)/shard_map/ppermute | solution.py:510
  23.9 0.2 collective-permute-start.8
  24.1 3.8 %collective-permute-done.4 = s32[384]{0:T(512)S(1)} collective-permute-done((s32[384]{0:T(512)S(1)}, s32[384]{0:T(512)S(1)}, u32[]{:S(2)}, u32[]{:S(2)}) %collective-permute-start.4) | collective-permute-done | bytes 1568 | tf_op jit(solution)/shard_map/ppermute | solution.py:510
  27.9 1.0 %collective-permute-start.6 = (bf16[32,3200]{1,0:T(8,128)(2,1)S(1)}, bf16[32,3200]{1,0:T(8,128)(2,1)}, u32[]{:S(2)}, u32[]{:S(2)}) collective-permute-start(bf16[32,3200]{1,0:T(8,128)(2,1)S(1)} %add_convert_fusion.rest_0_), channel_id=1, source_target_pairs={{0,2},{1,3},{2,0},{3,1},{4,6},{5,7},{6,4},{7,5},{8,10},{9,11},{10,... | collective-permute-start | bytes 614408 | tf_op jit(solution)/shard_map/ppermute | solution.py:440
  29.6 1.1 %collective-permute-done.8.rest_10_ = bf16[80,1280]{1,0:T(8,128)(2,1)} collective-permute-done((bf16[80,1280]{1,0:T(8,128)(2,1)}, bf16[80,1280]{1,0:T(8,128)(2,1)}, u32[]{:S(2)}, u32[]{:S(2)}) %collective-permute-start.8) | collective-permute-done | bytes 204832 | tf_op jit(solution)/shard_map/ppermute | solution.py:443
  30.6 3.7 %collective-permute-done.7.rest_9_ = bf16[80,1280]{1,0:T(8,128)(2,1)} collective-permute-done((bf16[80,1280]{1,0:T(8,128)(2,1)}, bf16[80,1280]{1,0:T(8,128)(2,1)}, u32[]{:S(2)}, u32[]{:S(2)}) %collective-permute-start.7) | collective-permute-done | bytes 204832 | tf_op jit(solution)/shard_map/ppermute | solution.py:443
  34.3 0.5 collective-permute-start.10
  34.9 1.0 %shard_map.111 = (bf16[1008,320]{1,0:T(8,128)(2,1)S(1)}, bf16[1008,64]{1,0:T(8,128)(2,1)S(1)}) custom-call(s32[2]{0:T(128)S(1)} %pad_add_fusion.span, s32[1,1280]{1,0:T(1,128)S(1)} %broadcast_in_dim.6.near), custom_call_target="tpu_custom_call" | custom-call | tf_op jit(solution)/shard_map/pallas_call | solution.py:515
  35.9 0.4 collective-permute-done.14.rest_12_
  36.5 0.4 collective-permute-start.16
  36.8 1.1 %collective-permute-done.15.rest_13_ = bf16[80,1280]{1,0:T(8,128)(2,1)S(1)} collective-permute-done((bf16[80,1280]{1,0:T(8,128)(2,1)}, bf16[80,1280]{1,0:T(8,128)(2,1)S(1)}, u32[]{:S(2)}, u32[]{:S(2)}) %collective-permute-start.15) | collective-permute-done | bytes 204832 | tf_op jit(solution)/shard_map/ppermute | solution.py:437
  38.5 1.1 %collective-permute-done.17.rest_15_ = bf16[80,1280]{1,0:T(8,128)(2,1)S(1)} collective-permute-done((bf16[80,1280]{1,0:T(8,128)(2,1)}, bf16[80,1280]{1,0:T(8,128)(2,1)S(1)}, u32[]{:S(2)}, u32[]{:S(2)}) %collective-permute-start.17) | collective-permute-done | bytes 204832 | tf_op jit(solution)/shard_map/ppermute | solution.py:437
  40.0 1.4 %collective-permute-start.20 = (bf16[80,2304]{1,0:T(8,128)(2,1)S(1)}, bf16[80,2304]{1,0:T(8,128)(2,1)S(1)}, u32[]{:S(2)}, u32[]{:S(2)}) collective-permute-start(bf16[80,2304]{1,0:T(8,128)(2,1)S(1)} %collective-permute-done.19.rest_5_), channel_id=1, source_target_pairs={{0,4},{4,0},{8,12},{12,8},{16,20},{20,16},{24,28},{28,24},{1,5},{5... | collective-permute-start | bytes 1105928 | tf_op jit(solution)/shard_map/ppermute | solution.py:443
  41.3 1.5 %collective-permute-start.22 = (bf16[80,2304]{1,0:T(8,128)(2,1)}, bf16[80,2304]{1,0:T(8,128)(2,1)S(1)}, u32[]{:S(2)}, u32[]{:S(2)}) collective-permute-start(bf16[80,2304]{1,0:T(8,128)(2,1)} %get-tuple-element.55), channel_id=1, source_target_pairs={{0,2},{1,3},{2,0},{3,1},{4,6},{5,7},{6,4},{7,5},{8,10},{9,11},{10,... | collective-permute-start | bytes 1105928 | tf_op jit(solution)/shard_map/ppermute | solution.py:440
  42.8 1.1 %copy-done.2 = bf16[2,320,640]{2,1,0:T(8,128)(2,1)S(1)} copy-done((bf16[2,320,640]{2,1,0:T(8,128)(2,1)S(1)}, bf16[2,320,640]{2,1,0:T(8,128)(2,1)}, u32[]{:S(2)}) %copy-start.2) | copy-done | bytes 819224
  44.0 0.9 %copy-done.3 = bf16[64,1280]{1,0:T(8,128)(2,1)S(1)} copy-done((bf16[64,1280]{1,0:T(8,128)(2,1)S(1)}, bf16[64,1280]{1,0:T(8,128)(2,1)}, u32[]{:S(2)}) %copy-start.3) | copy-done | bytes 163864
  44.9 9.3 %shard_map.112 = (bf16[1008,640]{1,0:T(8,128)(2,1)S(1)}, bf16[496,1280]{1,0:T(8,128)(2,1)S(1)}) custom-call(s32[2]{0:T(128)S(1)} %pad_add_fusion.span, bf16[1008,320]{1,0:T(8,128)(2,1)S(1)} %get-tuple-element.38.hot5, bf16[1008,64]{1,0:T(8,128)(2,1)S(1)} %get-tuple-element.39.hot1, bf16[64,1280]{1,0:T(8,128)(2,1)S(1)} %copy-done.3, f32[2,640]{1,0:T(2,128)S(1)} %copy-done.6, ...), custom_call_target="tpu_custom_call" | custom-call | tf_op jit(solution)/shard_map/pallas_call | solution.py:540
  54.3 0.6 collective-permute-start.25
  54.9 0.4 collective-permute-start.26
  55.4 2.4 %shard_map.113.rest_0_ = f32[496,640]{1,0:T(8,128)S(1)} custom-call(bf16[1008,640]{1,0:T(8,128)(2,1)S(1)} %get-tuple-element.48.ci, bf16[2,160,3200]{2,1,0:T(8,128)(2,1)S(1)} %copy-done, bf16[2,160,3200]{2,1,0:T(8,128)(2,1)} %collective-permute-done.18.near_conv.rest_3_), custom_call_target="tpu_custom_call" | custom-call | tf_op jit(solution)/shard_map/pallas_call | solution.py:560
  57.8 5.2 %shard_map.114 = bf16[496,1280]{1,0:T(8,128)(2,1)} custom-call(bf16[1008,640]{1,0:T(8,128)(2,1)S(1)} %get-tuple-element.48.ci, bf16[496,1280]{1,0:T(8,128)(2,1)S(1)} %get-tuple-element.49.hid, f32[2,640]{1,0:T(2,128)S(1)} %copy-done.6, f32[496,640]{1,0:T(8,128)S(1)} %shard_map.113.rest_0_, bf16[2,160,3200]{2,1,0:T(8,128)(2,1)S(1)} %copy-done, ...), custom_call_target="tpu_custom_call" | custom-call | tf_op jit(solution)/shard_map/pallas_call | solution.py:570
  (55 shorter events, 1.7 us)
Async XLA Ops:
  0.0 13.9 %copy-start = (bf16[2,160,3200]{2,1,0:T(8,128)(2,1)S(1)}, bf16[2,160,3200]{2,1,0:T(8,128)(2,1)}, u32[]{:S(2)}) copy-start(bf16[2,160,3200]{2,1,0:T(8,128)(2,1)} %rest_1_.1) | copy-start | bytes 6144004
  0.0 13.9 %copy-start.5 = (f32[2,640]{1,0:T(2,128)S(1)}, f32[2,640]{1,0:T(2,128)}, u32[]{:S(2)}) copy-start(f32[2,640]{1,0:T(2,128)} %gain_mid.1) | copy-start | bytes 15364
  3.1 3.1 %collective-permute-start = (f32[64,640]{1,0:T(8,128)}, f32[64,640]{1,0:T(8,128)S(1)}, u32[]{:S(2)}, u32[]{:S(2)}) collective-permute-start(f32[64,640]{1,0:T(8,128)} %get-tuple-element.32), channel_id=1, source_target_pairs={{0,1},{1,0},{2,3},{3,2},{4,5},{5,4},{6,7},{7,6},{8,9},{9,8},{10,11... | collective-permute-start | bytes 491528 | tf_op jit(solution)/shard_map/ppermute | solution.py:437
  3.7 8.8 %collective-permute-start.2 = (bf16[80,1280]{1,0:T(8,128)(2,1)}, bf16[80,1280]{1,0:T(8,128)(2,1)}, u32[]{:S(2)}, u32[]{:S(2)}) collective-permute-start(bf16[80,1280]{1,0:T(8,128)(2,1)} %get-tuple-element.33), channel_id=1, source_target_pairs={{0,2},{1,3},{2,0},{3,1},{4,6},{5,7},{6,4},{7,5},{8,10},{9,11},{10,... | collective-permute-start | bytes 614408 | tf_op jit(solution)/shard_map/ppermute | solution.py:440
  7.2 6.7 %collective-permute-start.1 = (bf16[64,640]{1,0:T(8,128)(2,1)S(1)}, bf16[64,640]{1,0:T(8,128)(2,1)S(1)}, u32[]{:S(2)}, u32[]{:S(2)}) collective-permute-start(bf16[64,640]{1,0:T(8,128)(2,1)S(1)} %get-tuple-element.59), channel_id=1, source_target_pairs={{0,2},{1,3},{2,0},{3,1},{4,6},{5,7},{6,4},{7,5},{8,10},{9,11},{10,... | collective-permute-start | bytes 245768 | tf_op jit(solution)/shard_map/ppermute | solution.py:440
  13.9 15.0 %copy-start.1 = (bf16[2,160,1280]{2,1,0:T(8,128)(2,1)S(1)}, bf16[2,160,1280]{2,1,0:T(8,128)(2,1)}, u32[]{:S(2)}) copy-start(bf16[2,160,1280]{2,1,0:T(8,128)(2,1)} %rest_2_.1) | copy-start | bytes 2457604
  13.9 28.9 %copy-start.4 = (f32[2,1280]{1,0:T(2,128)S(1)}, f32[2,1280]{1,0:T(2,128)}, u32[]{:S(2)}) copy-start(f32[2,1280]{1,0:T(2,128)} %gain_in.1) | copy-start | bytes 30724
  13.9 28.9 %copy-start.6 = (f32[2,640]{1,0:T(2,128)S(1)}, f32[2,640]{1,0:T(2,128)}, u32[]{:S(2)}) copy-start(f32[2,640]{1,0:T(2,128)} %gain_out.3) | copy-start | bytes 15364
  15.1 2.1 %collective-permute-start.3 = (bf16[32,3200]{1,0:T(8,128)(2,1)S(1)}, bf16[32,3200]{1,0:T(8,128)(2,1)S(1)}, u32[]{:S(2)}, u32[]{:S(2)}) collective-permute-start(bf16[32,3200]{1,0:T(8,128)(2,1)S(1)} %get-tuple-element.36), channel_id=1, source_target_pairs={{0,1},{1,0},{2,3},{3,2},{4,5},{5,4},{6,7},{7,6},{8,9},{9,8},{10,11... | collective-permute-start | bytes 614408 | tf_op jit(solution)/shard_map/ppermute | solution.py:437
  15.2 12.7 %collective-permute-start.19 = (bf16[80,2304]{1,0:T(8,128)(2,1)}, bf16[80,2304]{1,0:T(8,128)(2,1)S(1)}, u32[]{:S(2)}, u32[]{:S(2)}) collective-permute-start(bf16[80,2304]{1,0:T(8,128)(2,1)} %get-tuple-element.52), channel_id=1, source_target_pairs={{0,2},{1,3},{2,0},{3,1},{4,6},{5,7},{6,4},{7,5},{8,10},{9,11},{10,... | collective-permute-start | bytes 1105928 | tf_op jit(solution)/shard_map/ppermute | solution.py:440
  17.0 38.3 %collective-permute-start.18 = (bf16[2,160,3200]{2,1,0:T(8,128)(2,1)S(1)}, bf16[2,160,3200]{2,1,0:T(8,128)(2,1)}, u32[]{:S(2)}, u32[]{:S(2)}) collective-permute-start(bf16[2,160,3200]{2,1,0:T(8,128)(2,1)S(1)} %copy-done), channel_id=1, source_target_pairs={{0,1},{1,0},{2,3},{3,2},{4,5},{5,4},{6,7},{7,6},{8,9},{9,8},{10,11... | collective-permute-start | bytes 6144008 | tf_op jit(solution)/shard_map/ppermute | solution.py:437
  17.3 11.6 %collective-permute-start.9 = (bf16[80,1280]{1,0:T(8,128)(2,1)}, bf16[80,1280]{1,0:T(8,128)(2,1)}, u32[]{:S(2)}, u32[]{:S(2)}) collective-permute-start(bf16[80,1280]{1,0:T(8,128)(2,1)} %collective-permute-done.2.rest_8_), channel_id=1, source_target_pairs={{0,12},{4,8},{8,4},{12,0},{16,28},{20,24},{24,20},{28,16},{1,13},{... | collective-permute-start | bytes 614408 | tf_op jit(solution)/shard_map/ppermute | solution.py:443
  19.9 3.9 %collective-permute-start.5 = (s32[384]{0:T(512)S(1)}, s32[384]{0:T(512)S(1)}, u32[]{:S(2)}, u32[]{:S(2)}) collective-permute-start(s32[384]{0:T(512)S(1)} %get-tuple-element.63), channel_id=1, source_target_pairs={{0,4},{4,0},{8,12},{12,8},{16,20},{20,16},{24,28},{28,24},{1,5},{5... | collective-permute-start | bytes 4616 | tf_op jit(solution)/shard_map/ppermute | solution.py:443
  20.4 7.4 %collective-permute-start.4 = (s32[384]{0:T(512)S(1)}, s32[384]{0:T(512)S(1)}, u32[]{:S(2)}, u32[]{:S(2)}) collective-permute-start(s32[384]{0:T(512)S(1)} %get-tuple-element.64), channel_id=1, source_target_pairs={{4,8},{12,16},{20,24},{28,0},{8,4},{16,12},{24,20},{0,28},{5,9},{1... | collective-permute-start | bytes 4616 | tf_op jit(solution)/shard_map/ppermute | solution.py:510
  23.9 6.8 %collective-permute-start.8 = (bf16[80,1280]{1,0:T(8,128)(2,1)}, bf16[80,1280]{1,0:T(8,128)(2,1)}, u32[]{:S(2)}, u32[]{:S(2)}) collective-permute-start(bf16[80,1280]{1,0:T(8,128)(2,1)} %collective-permute-done.2.rest_8_), channel_id=1, source_target_pairs={{0,8},{4,12},{8,0},{12,4},{16,24},{20,28},{24,16},{28,20},{1,9},{5... | collective-permute-start | bytes 614408 | tf_op jit(solution)/shard_map/ppermute | solution.py:443
  27.9 6.4 %collective-permute-start.7 = (bf16[80,1280]{1,0:T(8,128)(2,1)}, bf16[80,1280]{1,0:T(8,128)(2,1)}, u32[]{:S(2)}, u32[]{:S(2)}) collective-permute-start(bf16[80,1280]{1,0:T(8,128)(2,1)} %collective-permute-done.2.rest_8_), channel_id=1, source_target_pairs={{0,4},{4,0},{8,12},{12,8},{16,20},{20,16},{24,28},{28,24},{1,5},{5... | collective-permute-start | bytes 614408 | tf_op jit(solution)/shard_map/ppermute | solution.py:443
  27.9 6.4 %collective-permute-start.6 = (bf16[32,3200]{1,0:T(8,128)(2,1)S(1)}, bf16[32,3200]{1,0:T(8,128)(2,1)}, u32[]{:S(2)}, u32[]{:S(2)}) collective-permute-start(bf16[32,3200]{1,0:T(8,128)(2,1)S(1)} %add_convert_fusion.rest_0_), channel_id=1, source_target_pairs={{0,2},{1,3},{2,0},{3,1},{4,6},{5,7},{6,4},{7,5},{8,10},{9,11},{10,... | collective-permute-start | bytes 614408 | tf_op jit(solution)/shard_map/ppermute | solution.py:440
  28.9 12.5 %collective-permute-start.12 = (bf16[2,160,1280]{2,1,0:T(8,128)(2,1)S(1)}, bf16[2,160,1280]{2,1,0:T(8,128)(2,1)}, u32[]{:S(2)}, u32[]{:S(2)}) collective-permute-start(bf16[2,160,1280]{2,1,0:T(8,128)(2,1)S(1)} %copy-done.1), channel_id=1, source_target_pairs={{0,1},{1,0},{2,3},{3,2},{4,5},{5,4},{6,7},{7,6},{8,9},{9,8},{10,11... | collective-permute-start | bytes 2457608 | tf_op jit(solution)/shard_map/ppermute | solution.py:437
  30.6 12.2 %collective-permute-start.13 = (bf16[2,320,640]{2,1,0:T(8,128)(2,1)}, bf16[2,320,640]{2,1,0:T(8,128)(2,1)}, u32[]{:S(2)}, u32[]{:S(2)}) collective-permute-start(bf16[2,320,640]{2,1,0:T(8,128)(2,1)} %rest_5_.1), channel_id=1, source_target_pairs={{0,1},{1,0},{2,3},{3,2},{4,5},{5,4},{6,7},{7,6},{8,9},{9,8},{10,11... | collective-permute-start | bytes 2457608 | tf_op jit(solution)/shard_map/ppermute | solution.py:437
  34.3 2.0 %collective-permute-start.14 = (bf16[80,1280]{1,0:T(8,128)(2,1)}, bf16[80,1280]{1,0:T(8,128)(2,1)}, u32[]{:S(2)}, u32[]{:S(2)}) collective-permute-start(bf16[80,1280]{1,0:T(8,128)(2,1)} %collective-permute-done.2.rest_8_), channel_id=1, source_target_pairs={{0,1},{1,0},{2,3},{3,2},{4,5},{5,4},{6,7},{7,6},{8,9},{9,8},{10,11... | collective-permute-start | bytes 614408 | tf_op jit(solution)/shard_map/ppermute | solution.py:437
  34.3 2.1 %collective-permute-start.10 = (bf16[32,3200]{1,0:T(8,128)(2,1)S(1)}, bf16[32,3200]{1,0:T(8,128)(2,1)}, u32[]{:S(2)}, u32[]{:S(2)}) collective-permute-start(bf16[32,3200]{1,0:T(8,128)(2,1)S(1)} %add_convert_fusion.rest_0_), channel_id=1, source_target_pairs={{0,1},{1,0},{2,3},{3,2},{4,5},{5,4},{6,7},{7,6},{8,9},{9,8},{10,11... | collective-permute-start | bytes 614408 | tf_op jit(solution)/shard_map/ppermute | solution.py:437
  36.3 1.7 %collective-permute-start.15 = (bf16[80,1280]{1,0:T(8,128)(2,1)}, bf16[80,1280]{1,0:T(8,128)(2,1)S(1)}, u32[]{:S(2)}, u32[]{:S(2)}) collective-permute-start(bf16[80,1280]{1,0:T(8,128)(2,1)} %collective-permute-done.7.rest_9_), channel_id=1, source_target_pairs={{0,1},{1,0},{2,3},{3,2},{4,5},{5,4},{6,7},{7,6},{8,9},{9,8},{10,11... | collective-permute-start | bytes 614408 | tf_op jit(solution)/shard_map/ppermute | solution.py:437
  36.5 1.8 %collective-permute-start.16 = (bf16[80,1280]{1,0:T(8,128)(2,1)}, bf16[80,1280]{1,0:T(8,128)(2,1)S(1)}, u32[]{:S(2)}, u32[]{:S(2)}) collective-permute-start(bf16[80,1280]{1,0:T(8,128)(2,1)} %collective-permute-done.8.rest_10_), channel_id=1, source_target_pairs={{0,1},{1,0},{2,3},{3,2},{4,5},{5,4},{6,7},{7,6},{8,9},{9,8},{10,11... | collective-permute-start | bytes 614408 | tf_op jit(solution)/shard_map/ppermute | solution.py:437
  38.0 1.7 %collective-permute-start.17 = (bf16[80,1280]{1,0:T(8,128)(2,1)}, bf16[80,1280]{1,0:T(8,128)(2,1)S(1)}, u32[]{:S(2)}, u32[]{:S(2)}) collective-permute-start(bf16[80,1280]{1,0:T(8,128)(2,1)} %collective-permute-done.9.rest_11_), channel_id=1, source_target_pairs={{0,1},{1,0},{2,3},{3,2},{4,5},{5,4},{6,7},{7,6},{8,9},{9,8},{10,11... | collective-permute-start | bytes 614408 | tf_op jit(solution)/shard_map/ppermute | solution.py:437
  38.3 1.7 %collective-permute-start.11 = (bf16[32,3200]{1,0:T(8,128)(2,1)}, bf16[32,3200]{1,0:T(8,128)(2,1)S(1)}, u32[]{:S(2)}, u32[]{:S(2)}) collective-permute-start(bf16[32,3200]{1,0:T(8,128)(2,1)} %collective-permute-done.6.rest_1_), channel_id=1, source_target_pairs={{0,1},{1,0},{2,3},{3,2},{4,5},{5,4},{6,7},{7,6},{8,9},{9,8},{10,11... | collective-permute-start | bytes 614408 | tf_op jit(solution)/shard_map/ppermute | solution.py:437
  39.7 14.6 %collective-permute-start.21 = (bf16[80,2304]{1,0:T(8,128)(2,1)S(1)}, bf16[80,2304]{1,0:T(8,128)(2,1)S(1)}, u32[]{:S(2)}, u32[]{:S(2)}) collective-permute-start(bf16[80,2304]{1,0:T(8,128)(2,1)S(1)} %collective-permute-done.19.rest_5_), channel_id=1, source_target_pairs={{0,8},{4,12},{8,0},{12,4},{16,24},{20,28},{24,16},{28,20},{1,9},{5... | collective-permute-start | bytes 1105928 | tf_op jit(solution)/shard_map/ppermute | solution.py:443
  40.0 14.9 %collective-permute-start.20 = (bf16[80,2304]{1,0:T(8,128)(2,1)S(1)}, bf16[80,2304]{1,0:T(8,128)(2,1)S(1)}, u32[]{:S(2)}, u32[]{:S(2)}) collective-permute-start(bf16[80,2304]{1,0:T(8,128)(2,1)S(1)} %collective-permute-done.19.rest_5_), channel_id=1, source_target_pairs={{0,4},{4,0},{8,12},{12,8},{16,20},{20,16},{24,28},{28,24},{1,5},{5... | collective-permute-start | bytes 1105928 | tf_op jit(solution)/shard_map/ppermute | solution.py:443
  41.3 13.6 %collective-permute-start.22 = (bf16[80,2304]{1,0:T(8,128)(2,1)}, bf16[80,2304]{1,0:T(8,128)(2,1)S(1)}, u32[]{:S(2)}, u32[]{:S(2)}) collective-permute-start(bf16[80,2304]{1,0:T(8,128)(2,1)} %get-tuple-element.55), channel_id=1, source_target_pairs={{0,2},{1,3},{2,0},{3,1},{4,6},{5,7},{6,4},{7,5},{8,10},{9,11},{10,... | collective-permute-start | bytes 1105928 | tf_op jit(solution)/shard_map/ppermute | solution.py:440
  42.8 15.0 %collective-permute-start.23 = (bf16[80,2304]{1,0:T(8,128)(2,1)S(1)}, bf16[80,2304]{1,0:T(8,128)(2,1)S(1)}, u32[]{:S(2)}, u32[]{:S(2)}) collective-permute-start(bf16[80,2304]{1,0:T(8,128)(2,1)S(1)} %collective-permute-done.19.rest_5_), channel_id=1, source_target_pairs={{0,1},{1,0},{2,3},{3,2},{4,5},{5,4},{6,7},{7,6},{8,9},{9,8},{10,11... | collective-permute-start | bytes 1105928 | tf_op jit(solution)/shard_map/ppermute | solution.py:437
  54.3 3.5 %collective-permute-start.25 = (bf16[80,2304]{1,0:T(8,128)(2,1)S(1)}, bf16[80,2304]{1,0:T(8,128)(2,1)S(1)}, u32[]{:S(2)}, u32[]{:S(2)}) collective-permute-start(bf16[80,2304]{1,0:T(8,128)(2,1)S(1)} %collective-permute-done.21.rest_7_), channel_id=1, source_target_pairs={{0,1},{1,0},{2,3},{3,2},{4,5},{5,4},{6,7},{7,6},{8,9},{9,8},{10,11... | collective-permute-start | bytes 1105928 | tf_op jit(solution)/shard_map/ppermute | solution.py:437
  54.8 3.0 %collective-permute-start.24 = (bf16[80,2304]{1,0:T(8,128)(2,1)S(1)}, bf16[80,2304]{1,0:T(8,128)(2,1)S(1)}, u32[]{:S(2)}, u32[]{:S(2)}) collective-permute-start(bf16[80,2304]{1,0:T(8,128)(2,1)S(1)} %collective-permute-done.20.rest_6_), channel_id=1, source_target_pairs={{0,1},{1,0},{2,3},{3,2},{4,5},{5,4},{6,7},{7,6},{8,9},{9,8},{10,11... | collective-permute-start | bytes 1105928 | tf_op jit(solution)/shard_map/ppermute | solution.py:437
  54.9 2.9 %collective-permute-start.26 = (bf16[80,2304]{1,0:T(8,128)(2,1)S(1)}, bf16[80,2304]{1,0:T(8,128)(2,1)S(1)}, u32[]{:S(2)}, u32[]{:S(2)}) collective-permute-start(bf16[80,2304]{1,0:T(8,128)(2,1)S(1)} %collective-permute-done.22.rest_8_), channel_id=1, source_target_pairs={{0,1},{1,0},{2,3},{3,2},{4,5},{5,4},{6,7},{7,6},{8,9},{9,8},{10,11... | collective-permute-start | bytes 1105928 | tf_op jit(solution)/shard_map/ppermute | solution.py:437
  (4 other events, 18.0 us)

commit v6 on v5

--- a/solution.py
+++ b/solution.py
@@ -99,26 +99,39 @@
 
 
 def first_kernel(split, embed, brk, gain, w_in, conv_w, w_out, table, part, *rest):
-    *parts, emb, bv, g, w, full, sem = rest
+    count = 3 if split else 0
+    parts, rest = rest[:count], rest[count:]
+    emb, bv, g, w, full, sem, *held = rest
     copies = [
         pltpu.make_async_copy(s, d, sem.at[0])
         for s, d in ((embed, emb), (brk, bv), (gain, g), (w_in.at[0], w))
     ]
     start(copies)
+    leaving = []
     if split:
         _, _, y, z = place()
         kinds = []
         for kind in range(2):
             kinds.append(
-                part_copies(kind == 1, z, w_in, conv_w, w_out, parts[0], parts[1], sem.at[1])
-                + part_copies(kind == 0, 1 - z, w_in, conv_w, w_out, None, parts[2], sem.at[1])
+                part_copies(kind == 1, z, w_in, conv_w, w_out, held[0], held[1], sem.at[1])
+                + part_copies(kind == 0, 1 - z, w_in, conv_w, w_out, None, held[2], sem.at[1])
             )
 
             @pl.when(y == kind)
             def _():
                 start(kinds[kind])
 
+        leaving = [pltpu.make_async_copy(s, d, sem.at[2]) for s, d in zip(held, parts)]
+
     wait(copies)
+    if split:
+        for kind in range(2):
+
+            @pl.when(y == kind)
+            def _():
+                wait(kinds[kind])
+
+        start(leaving)
     full[...] = jnp.zeros_like(full)
     full[0:VOCAB] = emb[...]
     full[SLOT : SLOT + VOCAB] = emb[...] + bv[...][None, :]
@@ -128,12 +141,7 @@
     rows = w.shape[0]
     mine = dot(normed, pick(normed.shape[1], rows, lax.axis_index("roll") * rows)).astype(BF)
     part[...] = dot(mine, w[...])
-    if split:
-        for kind in range(2):
-
-            @pl.when(y == kind)
-            def _():
-                wait(kinds[kind])
+    wait(leaving)
 
 
 def table_kernel(split, own, other, gain, w_all, *rest):
@@ -154,7 +162,13 @@
         outs[0][...] = full[...]
 
 
-def hot_kernel(span, near, hot5, hot1):
+def hot_kernel(split, span, near, *rest):
+    copies = []
+    if split:
+        *w, hot5, hot1, near_out, near_in, near_conv, sem = rest
+        copies = chip_copies(*w, near_out, near_in, near_conv, sem)
+    else:
+        hot5, hot1 = rest
     codes = near[...]
     count = codes.shape[1]
     rows = hot5.shape[0]
@@ -166,9 +180,10 @@
         hot5[:, k * CODES : (k + 1) * CODES] = taps[k * DIL0 : k * DIL0 + rows]
     center = jnp.where(lanes == codes, 1.0, 0.0).T.astype(BF)
     hot1[...] = center[HALF * DIL0 : HALF * DIL0 + rows]
-
-
-def rows_kernel(split, span, hot5, hot1, table, gain_out, gain_in, gain_mid, *rest):
+    wait(copies)
+
+
+def rows_kernel(split, span, hot5, hot1, gain_out, gain_in, gain_mid, *rest):
     *w, ci, hid, tw, wo, wi, sem = rest
     depth = wo.shape[0] - CODES
     if split:
@@ -178,7 +193,7 @@
         w = w[4:]
     else:
         taps = [(w[0], 0, CODES, 0)]
-        w = w[1:]
+        table, *w = w[1:]
     first = [
         pltpu.make_async_copy(
             t.at[:, k * H : (k + 1) * H], tw.at[i, pl.ds(pl.multiple_of(k * CODES + at, 16), n)], sem.at[0]
@@ -186,24 +201,27 @@
         for t, at, n, i in taps
         for k in range(KERNEL)
     ]
-    first.append(pltpu.make_async_copy(table, wo.at[depth:], sem.at[0]))
     start(first)
     if not split:
+        first.append(pltpu.make_async_copy(table, wo.at[depth:], sem.at[0]))
+        first[-1].start()
         out_copies = [pltpu.make_async_copy(w[0], wo.at[0:depth], sem.at[1])]
         in_copies = [pltpu.make_async_copy(w[1], wi, sem.at[2])]
         start(out_copies + in_copies)
     else:
-        w_out, w_in, near_out, near_in = w[:4]
-        parts, near_parts = w[4:8], w[8:12]
+        chip_out, chip_in = w[:2]
+        parts, near_parts = w[2:6], w[6:10]
         x, core, y, z = place()
-        n = w_out.shape[1]
-        m = w_in.shape[1]
+        n = depth // 4
+        m = 2 * n
         half = n // 2
-        out_copies, in_copies = [], []
-        for c, o, i in ((core, w_out, w_in), (1 - core, near_out, near_in)):
-            at = 2 * x + c
-            out_copies.append(pltpu.make_async_copy(o.at[0], wo.at[pl.ds(pl.multiple_of(at * n, 16), n)], sem.at[1]))
-            in_copies.append(pltpu.make_async_copy(i.at[1], wi.at[pl.ds(pl.multiple_of(at * m, 16), m)], sem.at[2]))
+        row = pl.multiple_of(x * 2 * n, 16)
+        out_copies = [
+            pltpu.make_async_copy(chip_out.at[0 : 2 * n], wo.at[pl.ds(row, 2 * n)], sem.at[1]),
+            pltpu.make_async_copy(chip_out.at[2 * n :], wo.at[depth:], sem.at[1]),
+        ]
+        row = pl.multiple_of(x * 2 * m, 16)
+        in_copies = [pltpu.make_async_copy(chip_in, wi.at[pl.ds(row, 2 * m)], sem.at[2])]
 
         def far(outs, ins):
             out, into = [], []
@@ -304,33 +322,38 @@
     )
 
 
-def head_kernel(ci, w_conv, near_conv, out, wt, sem):
+def chip_copies(table, w_out, w_in, w_conv, near_out, near_in, near_conv, chip_out, chip_in, chip_conv, sem):
     x, core, _, _ = place()
-    n = w_conv.shape[1]
+    n = w_out.shape[1]
+    m = w_in.shape[1]
     short = HEAD - n
     done = None
     for xx in range(2):
         for cc in range(2):
-            copies = []
-            for c, w in ((cc, w_conv), (1 - cc, near_conv)):
+            copies = [pltpu.make_async_copy(table, chip_out.at[2 * n :], sem)]
+            for c, o, i, w in ((cc, w_out, w_in, w_conv), (1 - cc, near_out, near_in, near_conv)):
+                copies.append(pltpu.make_async_copy(o.at[0], chip_out.at[c * n : (c + 1) * n], sem))
+                copies.append(pltpu.make_async_copy(i.at[1], chip_in.at[c * m : (c + 1) * m], sem))
                 if c == xx:
-                    copies += conv_copies(w.at[1], 0, KERNEL * H, wt, HEAD, short * xx, n, sem)
+                    copies += conv_copies(w.at[1], 0, KERNEL * H, chip_conv, HEAD, short * xx, n, sem)
                 else:
                     part = w.at[1, (n - short) * xx : (n - short) * xx + short]
-                    copies += conv_copies(part, 0, KERNEL * H, wt, HEAD, n * (1 - xx), short, sem)
+                    copies += conv_copies(part, 0, KERNEL * H, chip_conv, HEAD, n * (1 - xx), short, sem)
             done = copies
 
             @pl.when((x == xx) & (core == cc))
             def _():
                 start(copies)
 
+    return done
+
+
+def head_kernel(ci, w_conv, out):
+    x, _, _, _ = place()
     rows = out.shape[0]
     half = 16 * ((rows + 31) // 32)
-    for b, (lo, hi) in enumerate(((0, half), (half, rows))):
-        lhs = windows(ci, lo, hi, x * TAIL, HEAD)
-        if b == 0:
-            wait(done)
-        out[lo:hi] = dot(lhs, wt[...])
+    for lo, hi in ((0, half), (half, rows)):
+        out[lo:hi] = dot(windows(ci, lo, hi, x * TAIL, HEAD), w_conv[...])
 
 
 def last_kernel(split, ci, hid, gain_out, *rest):
@@ -454,26 +477,27 @@
         functools.partial(first_kernel, split),
         out_shape=[jax.ShapeDtypeStruct(n, t) for n, t in shapes],
         in_specs=[HBM] * 6,
-        out_specs=[VMEM] * len(shapes),
+        out_specs=[VMEM] * 2 + [HBM] * (len(shapes) - 2),
         scratch_shapes=[
             pltpu.VMEM(embed_table.shape, F32),
             pltpu.VMEM((width,), F32),
             pltpu.VMEM(gain_in.shape, F32),
             pltpu.VMEM(w_in.shape[1:], BF),
             pltpu.VMEM((CODES, width), F32),
-            pltpu.SemaphoreType.DMA((2,)),
-        ],
+            pltpu.SemaphoreType.DMA((3,)),
+        ]
+        + [pltpu.VMEM(n, t) for n, t in shapes[2:]],
         cost_estimate=FREE,
         compiler_params=params(60),
     )(embed_table, break_vec, gain_in, w_in, conv_w, w_out)
 
     if split:
         own = part + core_swap(part)
-        near_in, near_conv, near_out = [core_swap(after(w, own)) for w in (w_in, conv_w, w_out)]
-        far_a = x_swap(parts[0])
-        other = x_swap(own.astype(BF))
-        far_b = x_swap(after(parts[1], own))
-        other = after(other, far_a)
+        sent = own.astype(BF)
+        other = x_swap(sent)
+        pace = core_swap(sent[:16, :128])
+        far_a = x_swap(after(parts[0], pace))
+        near_out, near_in, near_conv = [core_swap(after(w, pace)) for w in (w_out, w_in, conv_w)]
     else:
         own = lax.psum(part, "roll")
         other = jnp.zeros((CODES, H), BF)
@@ -499,9 +523,11 @@
         sent = (taps[0] + core_swap(taps[1]).astype(F32)).astype(BF)
         received = x_swap(sent)
         near_sent = core_swap(sent)
-        relay = after(far_a, sent)
+        relay = after(far_a, near_sent)
         parts_a = [far_a] + [seq_swap(relay, b) for b in (1, 2, 3)]
-        codes = after(codes, sent)
+        far_b = x_swap(after(parts[1], near_sent))
+        near_received = core_swap(received)
+        codes = after(codes, received)
         ends = codes[rows - REACH :], codes[:REACH]
         low = seq_at % 2 == 0
         even = seq_swap(jnp.where(low, *ends), 1)
@@ -512,30 +538,32 @@
     spare = jnp.zeros((-(rows + 2 * REACH) % 128,), jnp.int32)
     near = jnp.concatenate([before, codes, behind, spare])[None]
 
-    hot5, hot1 = pl.pallas_call(
-        hot_kernel,
-        out_shape=(
-            jax.ShapeDtypeStruct((wide_rows, KERNEL * CODES), BF),
-            jax.ShapeDtypeStruct((wide_rows, CODES), BF),
-        ),
-        in_specs=[SMEM, VMEM],
-        out_specs=(VMEM, VMEM),
+    shapes = [(wide_rows, KERNEL * CODES), (wide_rows, CODES)]
+    operands, scratch = [], []
+    if split:
+        operands = [table, w_out, w_in, conv_w, near_out, near_in, near_conv]
+        shapes += [(4 * shard + CODES, width), (8 * shard, H), (KERNEL * HEAD, H)]
+        scratch = [pltpu.SemaphoreType.DMA]
+    hot5, hot1, *chip = pl.pallas_call(
+        functools.partial(hot_kernel, split),
+        out_shape=[jax.ShapeDtypeStruct(n, BF) for n in shapes],
+        in_specs=[SMEM, VMEM] + [ANY] * len(operands),
+        out_specs=[VMEM] * len(shapes),
+        scratch_shapes=scratch,
         cost_estimate=FREE,
-        compiler_params=params(12),
-    )(span, near)
-
-    if split:
-        received = after(received, hot1, *parts_a)
-        near_received = core_swap(received)
-        near_a = [core_swap(relay)] + [core_swap(after(p, received)) for p in parts_a[1:]]
-        relay = after(far_b, received)
-        parts_b = [far_b, seq_swap(relay, 1), seq_swap(relay, 2), x_swap(after(parts[2], received))]
+        compiler_params=params(16),
+    )(span, near, *operands)
+
+    if split:
+        near_a = [core_swap(relay)] + [core_swap(after(p, hot1)) for p in parts_a[1:]]
+        relay = after(far_b, hot1)
+        parts_b = [far_b, seq_swap(relay, 1), seq_swap(relay, 2), x_swap(after(parts[2], hot1))]
         near_b = [core_swap(relay)]
-        weights_a = [sent, received, near_sent, near_received, w_out, w_in, near_out, near_in] + parts_a + near_a
+        weights_a = [sent, received, near_sent, near_received] + chip[:2] + parts_a + near_a
     else:
         taps = lax.psum(taps[0], "roll").astype(BF)
         gather = lambda w: lax.all_gather(w, "roll", axis=0, tiled=True)
-        weights_a, weights_b = [taps, gather(w_out[0]), gather(w_in[1])], [gather(conv_w[1]), gather(w_out[1])]
+        weights_a, weights_b = [taps, table, gather(w_out[0]), gather(w_in[1])], [gather(conv_w[1]), gather(w_out[1])]
 
     ci, hid = pl.pallas_call(
         functools.partial(rows_kernel, split),
@@ -543,7 +571,7 @@
             jax.ShapeDtypeStruct((wide_rows, H), BF),
             jax.ShapeDtypeStruct((rows, width), BF),
         ),
-        in_specs=[SMEM, VMEM, VMEM, ANY, VMEM, VMEM, VMEM] + [HBM if w is w_out or w is w_in else ANY for w in weights_a],
+        in_specs=[SMEM] + [VMEM] * 5 + [ANY] * len(weights_a),
         out_specs=(VMEM, VMEM),
         scratch_shapes=[
             pltpu.VMEM((2, KERNEL * CODES, H), BF),
@@ -553,19 +581,18 @@
         ],
         cost_estimate=FREE,
         compiler_params=params(30),
-    )(span, hot5, hot1, table, gain_out, gain_in, gain_mid, *weights_a)
+    )(span, hot5, hot1, gain_out, gain_in, gain_mid, *weights_a)
 
     if split:
         near_b += [core_swap(after(p, ci)) for p in parts_b[1:]]
         head = pl.pallas_call(
             head_kernel,
             out_shape=jax.ShapeDtypeStruct((rows, H), F32),
-            in_specs=[VMEM, HBM, ANY],
+            in_specs=[VMEM] * 2,
             out_specs=VMEM,
-            scratch_shapes=[pltpu.VMEM((KERNEL * HEAD, H), BF), pltpu.SemaphoreType.DMA],
             cost_estimate=FREE,
             compiler_params=params(16),
-        )(ci, conv_w, near_conv)
+        )(ci, chip[2])
         weights_b = [head, conv_w, w_out, near_conv, near_out] + parts_b + near_b
     out = pl.pallas_call(
         functools.partial(last_kernel, split),

time: 63.4 us -> 76.4 us (1.21)
  waiting for transfers between devices: 16.7 us -> 21.8 us
  starting transfers between devices: 19.9 us -> 24.6 us
  local copies, waits for them, and re-layouts: 2.18 us -> 3.53 us
  other arithmetic: 1.15 us -> 2.07 us
    ppermute x5, waiting for transfers between devices: 5.08 us -> 9.13 us  [x_swap(): return lax.ppermute(x, 'roll', [(i, i ^ 2) for i in range(rolls)])]
    ppermute x1, waiting for transfers between devices: 3.77 us -> 1.49 us  [per_device(): lax.ppermute(jnp.where(low, *ends[::-1]), 'seq', pairs + [(j, i) for i, j...]
    ppermute x15 -> x16, waiting for transfers between devices: 3.09 us -> 5.18 us  [core_swap(): return lax.ppermute(x, 'roll', [(i, i ^ 1) for i in range(rolls)])]
    ppermute x6, starting transfers between devices: 4.81 us -> 6.73 us  [seq_swap(): return lax.ppermute(x, 'seq', [(i, i ^ bits) for i in range(seqs)])]
    pallas_call x1, Pallas kernels: 0.98 us -> 2.59 us  [per_device(): pl.pallas_call(functools.partial(hot_kernel, split), out_shape=[jax.Shape...]
    ppermute x1, starting transfers between devices: 3.43 us -> 4.81 us  [per_device(): lax.ppermute(jnp.where(low, *ends[::-1]), 'seq', pairs + [(j, i) for i, j...]
    unnamed x18 -> x28, local copies, waits for them, and re-layouts: 2.09 us -> 3.44 us
    pallas_call x1, Pallas kernels: 2.41 us -> 1.16 us  [per_device(): pl.pallas_call(head_kernel, out_shape=jax.ShapeDtypeStruct((rows, H), F32...]
  transfers between devices with their start and end apart: 27 -> 28, of which waited for: 10 -> 13; matrix products, arithmetic and copies ran while one was open for 2% -> 2% of each run, Pallas kernels for 20% -> 19%
where the time goes in v6:
time: 76.4 us; the launch traced here: 75.6 us
  starting transfers between devices  24.6 us (32%)
  Pallas kernels  22.6 us (30%)
  waiting for transfers between devices  21.8 us (29%)
  local copies, waits for them, and re-layouts  3.53 us (5%)
  other arithmetic  2.07 us (3%)
  between operations  1.01 us (1%)
    pallas_call x1, Pallas kernels, per_device(): pl.pallas_call(functools.partial(rows_kernel, split), out_shape=(jax.Shap...  9.38 us
    ppermute x5, waiting for transfers between devices, x_swap(): return lax.ppermute(x, 'roll', [(i, i ^ 2) for i in range(rolls)])  9.13 us
    ppermute x5, starting transfers between devices, x_swap(): return lax.ppermute(x, 'roll', [(i, i ^ 2) for i in range(rolls)])  8.93 us
    ppermute x6, starting transfers between devices, seq_swap(): return lax.ppermute(x, 'seq', [(i, i ^ bits) for i in range(seqs)])  6.73 us
    ppermute x6, waiting for transfers between devices, seq_swap(): return lax.ppermute(x, 'seq', [(i, i ^ bits) for i in range(seqs)])  5.98 us
    ppermute x16, waiting for transfers between devices, core_swap(): return lax.ppermute(x, 'roll', [(i, i ^ 1) for i in range(rolls)])  5.18 us
    pallas_call x1, Pallas kernels, per_device(): pl.pallas_call(functools.partial(last_kernel, split), out_shape=jax.Shape...  5.12 us
    ppermute x1, starting transfers between devices, per_device(): lax.ppermute(jnp.where(low, *ends[::-1]), 'seq', pairs + [(j, i) for i, j...  4.81 us
  transfers between devices with their start and end apart: 28, of which 13 were waited for; matrix products, arithmetic and copies ran while one was open for 2% of the time, Pallas kernels for 19%

profile of v6, /device:TPU:0, one launch (start us, length us, event | category | flops | bytes accessed | tf_op | source)
XLA Modules:
  0.0 75.6 jit_solution(16016586002666046868)
XLA Ops:
  0.0 3.2 %shard_map.109 = (bf16[64,1280]{1,0:T(8,128)(2,1)}, f32[64,640]{1,0:T(8,128)}, bf16[80,1280]{1,0:T(8,128)(2,1)}, bf16[80,2304]{1,0:T(8,128)(2,1)}, bf16[80,2304]{1,0:T(8,128)(2,1)}) custom-call(f32[30,1280]{1,0:T(8,128)} %embed.1, f32[1280]{0:T(1024)} %brk.1, f32[2,1280]{1,0:T(2,128)} %gain_in.1, bf16[2,320,640]{2,1,0:T(8,128)(2,1)} %rest_2_.2, ...), custom_call_target="tpu_custom_call" | custom-call | tf_op jit(solution)/shard_map/pallas_call | solution.py:476
  3.7 1.2 %collective-permute-done = f32[64,640]{1,0:T(8,128)S(1)} collective-permute-done((f32[64,640]{1,0:T(8,128)}, f32[64,640]{1,0:T(8,128)S(1)}, u32[]{:S(2)}, u32[]{:S(2)}) %collective-permute-start) | collective-permute-done | bytes 163872 | tf_op jit(solution)/shard_map/ppermute | solution.py:460
  5.0 0.9 %fusion = (bf16[64,640]{1,0:T(8,128)(2,1)S(1)}, f32[64,640]{1,0:T(8,128)S(1)}) fusion(f32[64,640]{1,0:T(8,128)} %get-tuple-element.34, f32[64,640]{1,0:T(8,128)S(1)} %collective-permute-done), kind=kLoop, calls=%fused_computation.7 | loop fusion | flops 81920 | bytes 573440 | tf_op jit(solution)/shard_map/convert_element_type | solution.py:496
  6.4 0.8 %collective-permute-done.6 = bf16[16,128]{1,0:T(8,128)(2,1)S(1)} collective-permute-done((bf16[16,128]{1,0:T(8,128)(2,1)S(1)}, bf16[16,128]{1,0:T(8,128)(2,1)S(1)}, u32[]{:S(2)}, u32[]{:S(2)}) %collective-permute-start.6) | collective-permute-done | bytes 4128 | tf_op jit(solution)/shard_map/ppermute | solution.py:460
  7.5 2.7 %collective-permute-start.1 = (bf16[64,640]{1,0:T(8,128)(2,1)S(1)}, bf16[64,640]{1,0:T(8,128)(2,1)S(1)}, u32[]{:S(2)}, u32[]{:S(2)}) collective-permute-start(bf16[64,640]{1,0:T(8,128)(2,1)S(1)} %get-tuple-element.63), channel_id=1, source_target_pairs={{0,2},{1,3},{2,0},{3,1},{4,6},{5,7},{6,4},{7,5},{8,10},{9,11},{10,... | collective-permute-start | bytes 245768 | tf_op jit(solution)/shard_map/ppermute | solution.py:463
  10.2 2.9 %collective-permute-done.1.other = bf16[64,640]{1,0:T(8,128)(2,1)S(1)} collective-permute-done((bf16[64,640]{1,0:T(8,128)(2,1)S(1)}, bf16[64,640]{1,0:T(8,128)(2,1)S(1)}, u32[]{:S(2)}, u32[]{:S(2)}) %collective-permute-start.1) | collective-permute-done | bytes 81952 | tf_op jit(solution)/shard_map/ppermute | solution.py:463
  13.1 1.2 %shard_map.110 = (f32[32,3200]{1,0:T(8,128)S(1)}, bf16[32,3200]{1,0:T(8,128)(2,1)S(1)}) custom-call(f32[64,640]{1,0:T(8,128)S(1)} %get-tuple-element.64.own, bf16[64,640]{1,0:T(8,128)(2,1)S(1)} %collective-permute-done.1.other, f32[2,640]{1,0:T(2,128)S(1)} %copy-done.9, bf16[2,160,3200]{2,1,0:T(8,128)(2,1)S(1)} %copy-done), custom_call_target="tpu_custom_call" | custom-call | tf_op jit(solution)/shard_map/pallas_call | solution.py:509
  15.0 1.0 %collective-permute-done.2 = bf16[32,3200]{1,0:T(8,128)(2,1)} collective-permute-done((bf16[32,3200]{1,0:T(8,128)(2,1)S(1)}, bf16[32,3200]{1,0:T(8,128)(2,1)}, u32[]{:S(2)}, u32[]{:S(2)}) %collective-permute-start.2) | collective-permute-done | bytes 204832 | tf_op jit(solution)/shard_map/ppermute | solution.py:460
  16.0 1.0 %add_convert_fusion.rest_0_ = bf16[32,3200]{1,0:T(8,128)(2,1)S(1)} fusion(f32[32,3200]{1,0:T(8,128)S(1)} %get-tuple-element.35, bf16[32,3200]{1,0:T(8,128)(2,1)} %collective-permute-done.2), kind=kLoop, calls=%fused_computation | loop fusion | flops 307200 | bytes 819200 | tf_op jit(solution)/shard_map/convert_element_type | solution.py:523
  17.2 1.8 %collective-permute-start.3 = (bf16[32,3200]{1,0:T(8,128)(2,1)S(1)}, bf16[32,3200]{1,0:T(8,128)(2,1)S(1)}, u32[]{:S(2)}, u32[]{:S(2)}) collective-permute-start(bf16[32,3200]{1,0:T(8,128)(2,1)S(1)} %add_convert_fusion.rest_0_), channel_id=1, source_target_pairs={{0,2},{1,3},{2,0},{3,1},{4,6},{5,7},{6,4},{7,5},{8,10},{9,11},{10,... | collective-permute-start | bytes 614408 | tf_op jit(solution)/shard_map/ppermute | solution.py:463
  18.9 0.7 copy-done.3
  19.6 1.3 %collective-permute-start.12 = (bf16[80,1280]{1,0:T(8,128)(2,1)}, bf16[80,1280]{1,0:T(8,128)(2,1)}, u32[]{:S(2)}, u32[]{:S(2)}) collective-permute-start(bf16[80,1280]{1,0:T(8,128)(2,1)} %get-tuple-element.47), channel_id=1, source_target_pairs={{0,2},{1,3},{2,0},{3,1},{4,6},{5,7},{6,4},{7,5},{8,10},{9,11},{10,... | collective-permute-start | bytes 614408 | tf_op jit(solution)/shard_map/ppermute | solution.py:463
  20.9 4.2 %collective-permute-done.3.rest_1_ = bf16[32,3200]{1,0:T(8,128)(2,1)S(1)} collective-permute-done((bf16[32,3200]{1,0:T(8,128)(2,1)S(1)}, bf16[32,3200]{1,0:T(8,128)(2,1)S(1)}, u32[]{:S(2)}, u32[]{:S(2)}) %collective-permute-start.3) | collective-permute-done | bytes 204832 | tf_op jit(solution)/shard_map/ppermute | solution.py:463
  25.1 0.7 copy-done.5
  25.7 1.7 %collective-permute-start.20 = (bf16[80,2304]{1,0:T(8,128)(2,1)}, bf16[80,2304]{1,0:T(8,128)(2,1)S(1)}, u32[]{:S(2)}, u32[]{:S(2)}) collective-permute-start(bf16[80,2304]{1,0:T(8,128)(2,1)} %get-tuple-element.56), channel_id=1, source_target_pairs={{0,2},{1,3},{2,0},{3,1},{4,6},{5,7},{6,4},{7,5},{8,10},{9,11},{10,... | collective-permute-start | bytes 1105928 | tf_op jit(solution)/shard_map/ppermute | solution.py:463
  27.6 2.0 %collective-permute-done.12.rest_6_ = bf16[80,1280]{1,0:T(8,128)(2,1)} collective-permute-done((bf16[80,1280]{1,0:T(8,128)(2,1)}, bf16[80,1280]{1,0:T(8,128)(2,1)}, u32[]{:S(2)}, u32[]{:S(2)}) %collective-permute-start.12) | collective-permute-done | bytes 204832 | tf_op jit(solution)/shard_map/ppermute | solution.py:463
  29.6 1.8 %collective-permute-start.5 = (s32[384]{0:T(512)S(1)}, s32[384]{0:T(512)S(1)}, u32[]{:S(2)}, u32[]{:S(2)}) collective-permute-start(s32[384]{0:T(512)S(1)} %get-tuple-element.67), channel_id=1, source_target_pairs={{0,4},{4,0},{8,12},{12,8},{16,20},{20,16},{24,28},{28,24},{1,5},{5... | collective-permute-start | bytes 4616 | tf_op jit(solution)/shard_map/ppermute | solution.py:466
  32.0 1.2 %collective-permute-done.5 = s32[384]{0:T(512)S(1)} collective-permute-done((s32[384]{0:T(512)S(1)}, s32[384]{0:T(512)S(1)}, u32[]{:S(2)}, u32[]{:S(2)}) %collective-permute-start.5) | collective-permute-done | bytes 1568 | tf_op jit(solution)/shard_map/ppermute | solution.py:466
  33.1 4.8 %collective-permute-start.4 = (s32[384]{0:T(512)S(1)}, s32[384]{0:T(512)S(1)}, u32[]{:S(2)}, u32[]{:S(2)}) collective-permute-start(s32[384]{0:T(512)S(1)} %get-tuple-element.68), channel_id=1, source_target_pairs={{4,8},{12,16},{20,24},{28,0},{8,4},{16,12},{24,20},{0,28},{5,9},{1... | collective-permute-start | bytes 4616 | tf_op jit(solution)/shard_map/ppermute | solution.py:536
  38.0 1.5 %collective-permute-done.4 = s32[384]{0:T(512)S(1)} collective-permute-done((s32[384]{0:T(512)S(1)}, s32[384]{0:T(512)S(1)}, u32[]{:S(2)}, u32[]{:S(2)}) %collective-permute-start.4) | collective-permute-done | bytes 1568 | tf_op jit(solution)/shard_map/ppermute | solution.py:536
  39.5 0.9 %collective-permute-start.15 = (bf16[80,1280]{1,0:T(8,128)(2,1)}, bf16[80,1280]{1,0:T(8,128)(2,1)}, u32[]{:S(2)}, u32[]{:S(2)}) collective-permute-start(bf16[80,1280]{1,0:T(8,128)(2,1)} %collective-permute-done.12.rest_6_), channel_id=1, source_target_pairs={{0,12},{4,8},{8,4},{12,0},{16,28},{20,24},{24,20},{28,16},{1,13},{... | collective-permute-start | bytes 614408 | tf_op jit(solution)/shard_map/ppermute | solution.py:466
  40.9 2.1 %collective-permute-start.13 = (bf16[80,1280]{1,0:T(8,128)(2,1)}, bf16[80,1280]{1,0:T(8,128)(2,1)}, u32[]{:S(2)}, u32[]{:S(2)}) collective-permute-start(bf16[80,1280]{1,0:T(8,128)(2,1)} %collective-permute-done.12.rest_6_), channel_id=1, source_target_pairs={{0,4},{4,0},{8,12},{12,8},{16,20},{20,16},{24,28},{28,24},{1,5},{5... | collective-permute-start | bytes 614408 | tf_op jit(solution)/shard_map/ppermute | solution.py:466
  43.1 1.1 %copy-done.2 = bf16[2,320,640]{2,1,0:T(8,128)(2,1)S(1)} copy-done((bf16[2,320,640]{2,1,0:T(8,128)(2,1)S(1)}, bf16[2,320,640]{2,1,0:T(8,128)(2,1)}, u32[]{:S(2)}) %copy-start.2) | copy-done | bytes 819224
  44.3 0.9 %copy-done.7 = bf16[64,1280]{1,0:T(8,128)(2,1)S(1)} copy-done((bf16[64,1280]{1,0:T(8,128)(2,1)S(1)}, bf16[64,1280]{1,0:T(8,128)(2,1)}, u32[]{:S(2)}) %copy-start.7) | copy-done | bytes 163864
  45.2 2.6 %shard_map.111 = (bf16[1008,320]{1,0:T(8,128)(2,1)S(1)}, bf16[1008,64]{1,0:T(8,128)(2,1)S(1)}, bf16[384,1280]{1,0:T(8,128)(2,1)S(1)}, bf16[640,640]{1,0:T(8,128)(2,1)S(1)}, bf16[1280,640]{1,0:T(8,128)(2,1)S(1)}) custom-call(s32[2]{0:T(128)S(1)} %pad_add_fusion.span, s32[1,1280]{1,0:T(1,128)S(1)} %broadcast_in_dim.6.near, bf16[64,1280]{1,0:T(8,128)(2,1)S(1)} %copy-done.7, ...), custom_call_target="tpu_custom_call" | custom-call | tf_op jit(solution)/shard_map/pallas_call | solution.py:547
  47.8 4.8 %collective-permute-done.13.rest_7_ = bf16[80,1280]{1,0:T(8,128)(2,1)} collective-permute-done((bf16[80,1280]{1,0:T(8,128)(2,1)}, bf16[80,1280]{1,0:T(8,128)(2,1)}, u32[]{:S(2)}, u32[]{:S(2)}) %collective-permute-start.13) | collective-permute-done | bytes 204832 | tf_op jit(solution)/shard_map/ppermute | solution.py:466
  53.1 1.5 %collective-permute-start.21 = (bf16[80,2304]{1,0:T(8,128)(2,1)S(1)}, bf16[80,2304]{1,0:T(8,128)(2,1)S(1)}, u32[]{:S(2)}, u32[]{:S(2)}) collective-permute-start(bf16[80,2304]{1,0:T(8,128)(2,1)S(1)} %collective-permute-done.20.rest_5_), channel_id=1, source_target_pairs={{0,4},{4,0},{8,12},{12,8},{16,20},{20,16},{24,28},{28,24},{1,5},{5... | collective-permute-start | bytes 1105928 | tf_op jit(solution)/shard_map/ppermute | solution.py:466
  54.6 1.5 %collective-permute-start.23 = (bf16[80,2304]{1,0:T(8,128)(2,1)S(1)}, bf16[80,2304]{1,0:T(8,128)(2,1)S(1)}, u32[]{:S(2)}, u32[]{:S(2)}) collective-permute-start(bf16[80,2304]{1,0:T(8,128)(2,1)S(1)} %copy-done.13), channel_id=1, source_target_pairs={{0,2},{1,3},{2,0},{3,1},{4,6},{5,7},{6,4},{7,5},{8,10},{9,11},{10,... | collective-permute-start | bytes 1105928 | tf_op jit(solution)/shard_map/ppermute | solution.py:463
  56.6 1.1 %collective-permute-done.18.rest_12_ = bf16[80,1280]{1,0:T(8,128)(2,1)S(1)} collective-permute-done((bf16[80,1280]{1,0:T(8,128)(2,1)}, bf16[80,1280]{1,0:T(8,128)(2,1)S(1)}, u32[]{:S(2)}, u32[]{:S(2)}) %collective-permute-start.18) | collective-permute-done | bytes 204832 | tf_op jit(solution)/shard_map/ppermute | solution.py:460
  58.1 9.4 %shard_map.112 = (bf16[1008,640]{1,0:T(8,128)(2,1)S(1)}, bf16[496,1280]{1,0:T(8,128)(2,1)S(1)}) custom-call(s32[2]{0:T(128)S(1)} %pad_add_fusion.span, bf16[1008,320]{1,0:T(8,128)(2,1)S(1)} %get-tuple-element.42.hot5, bf16[1008,64]{1,0:T(8,128)(2,1)S(1)} %get-tuple-element.43.hot1, f32[2,640]{1,0:T(2,128)S(1)} %copy-done.10, f32[2,1280]{1,0:T(2,128)S(1)} %copy-done.8, ...), custom_call_target="tpu_custom_call" | custom-call | tf_op jit(solution)/shard_map/pallas_call | solution.py:568
  68.3 1.2 %shard_map.113.rest_0_ = f32[496,640]{1,0:T(8,128)S(1)} custom-call(bf16[1008,640]{1,0:T(8,128)(2,1)S(1)} %get-tuple-element.52.ci, bf16[1280,640]{1,0:T(8,128)(2,1)S(1)} %get-tuple-element.54.w_conv), custom_call_target="tpu_custom_call" | custom-call | tf_op jit(solution)/shard_map/pallas_call | solution.py:588
  70.3 5.1 %shard_map.114 = bf16[496,1280]{1,0:T(8,128)(2,1)} custom-call(bf16[1008,640]{1,0:T(8,128)(2,1)S(1)} %get-tuple-element.52.ci, bf16[496,1280]{1,0:T(8,128)(2,1)S(1)} %get-tuple-element.53.hid, f32[2,640]{1,0:T(2,128)S(1)} %copy-done.10, f32[496,640]{1,0:T(8,128)S(1)} %shard_map.113.rest_0_, bf16[2,160,3200]{2,1,0:T(8,128)(2,1)S(1)} %copy-done, ...), custom_call_target="tpu_custom_call" | custom-call | tf_op jit(solution)/shard_map/pallas_call | solution.py:597
  (68 shorter events, 5.9 us)
Async XLA Ops:
  0.0 13.1 %copy-start.9 = (f32[2,640]{1,0:T(2,128)S(1)}, f32[2,640]{1,0:T(2,128)}, u32[]{:S(2)}) copy-start(f32[2,640]{1,0:T(2,128)} %gain_mid.1) | copy-start | bytes 15364
  3.2 1.8 %collective-permute-start = (f32[64,640]{1,0:T(8,128)}, f32[64,640]{1,0:T(8,128)S(1)}, u32[]{:S(2)}, u32[]{:S(2)}) collective-permute-start(f32[64,640]{1,0:T(8,128)} %get-tuple-element.34), channel_id=1, source_target_pairs={{0,1},{1,0},{2,3},{3,2},{4,5},{5,4},{6,7},{7,6},{8,9},{9,8},{10,11... | collective-permute-start | bytes 491528 | tf_op jit(solution)/shard_map/ppermute | solution.py:460
  5.9 1.3 %collective-permute-start.6 = (bf16[16,128]{1,0:T(8,128)(2,1)S(1)}, bf16[16,128]{1,0:T(8,128)(2,1)S(1)}, u32[]{:S(2)}, u32[]{:S(2)}) collective-permute-start(bf16[16,128]{1,0:T(8,128)(2,1)S(1)} %slice.12), channel_id=1, source_target_pairs={{0,1},{1,0},{2,3},{3,2},{4,5},{5,4},{6,7},{7,6},{8,9},{9,8},{10,11... | collective-permute-start | bytes 12296 | tf_op jit(solution)/shard_map/ppermute | solution.py:460
  7.2 33.7 %collective-permute-start.9 = (bf16[2,160,3200]{2,1,0:T(8,128)(2,1)S(1)}, bf16[2,160,3200]{2,1,0:T(8,128)(2,1)}, u32[]{:S(2)}, u32[]{:S(2)}) collective-permute-start(bf16[2,160,3200]{2,1,0:T(8,128)(2,1)S(1)} %copy-done), channel_id=1, source_target_pairs={{0,1},{1,0},{2,3},{3,2},{4,5},{5,4},{6,7},{7,6},{8,9},{9,8},{10,11... | collective-permute-start | bytes 6144008 | tf_op jit(solution)/shard_map/ppermute | solution.py:460
  7.5 5.6 %collective-permute-start.1 = (bf16[64,640]{1,0:T(8,128)(2,1)S(1)}, bf16[64,640]{1,0:T(8,128)(2,1)S(1)}, u32[]{:S(2)}, u32[]{:S(2)}) collective-permute-start(bf16[64,640]{1,0:T(8,128)(2,1)S(1)} %get-tuple-element.63), channel_id=1, source_target_pairs={{0,2},{1,3},{2,0},{3,1},{4,6},{5,7},{6,4},{7,5},{8,10},{9,11},{10,... | collective-permute-start | bytes 245768 | tf_op jit(solution)/shard_map/ppermute | solution.py:463
  14.3 1.7 %collective-permute-start.2 = (bf16[32,3200]{1,0:T(8,128)(2,1)S(1)}, bf16[32,3200]{1,0:T(8,128)(2,1)}, u32[]{:S(2)}, u32[]{:S(2)}) collective-permute-start(bf16[32,3200]{1,0:T(8,128)(2,1)S(1)} %get-tuple-element.36), channel_id=1, source_target_pairs={{0,1},{1,0},{2,3},{3,2},{4,5},{5,4},{6,7},{7,6},{8,9},{9,8},{10,11... | collective-permute-start | bytes 614408 | tf_op jit(solution)/shard_map/ppermute | solution.py:460
  14.4 25.1 %collective-permute-start.7 = (bf16[2,160,1280]{2,1,0:T(8,128)(2,1)S(1)}, bf16[2,160,1280]{2,1,0:T(8,128)(2,1)}, u32[]{:S(2)}, u32[]{:S(2)}) collective-permute-start(bf16[2,160,1280]{2,1,0:T(8,128)(2,1)S(1)} %copy-done.1), channel_id=1, source_target_pairs={{0,1},{1,0},{2,3},{3,2},{4,5},{5,4},{6,7},{7,6},{8,9},{9,8},{10,11... | collective-permute-start | bytes 2457608 | tf_op jit(solution)/shard_map/ppermute | solution.py:460
  14.9 25.5 %collective-permute-start.8 = (bf16[2,320,640]{2,1,0:T(8,128)(2,1)}, bf16[2,320,640]{2,1,0:T(8,128)(2,1)}, u32[]{:S(2)}, u32[]{:S(2)}) collective-permute-start(bf16[2,320,640]{2,1,0:T(8,128)(2,1)} %rest_2_.2), channel_id=1, source_target_pairs={{0,1},{1,0},{2,3},{3,2},{4,5},{5,4},{6,7},{7,6},{8,9},{9,8},{10,11... | collective-permute-start | bytes 2457608 | tf_op jit(solution)/shard_map/ppermute | solution.py:460
  17.0 2.0 %collective-permute-start.10 = (bf16[32,3200]{1,0:T(8,128)(2,1)S(1)}, bf16[32,3200]{1,0:T(8,128)(2,1)S(1)}, u32[]{:S(2)}, u32[]{:S(2)}) collective-permute-start(bf16[32,3200]{1,0:T(8,128)(2,1)S(1)} %add_convert_fusion.rest_0_), channel_id=1, source_target_pairs={{0,1},{1,0},{2,3},{3,2},{4,5},{5,4},{6,7},{7,6},{8,9},{9,8},{10,11... | collective-permute-start | bytes 614408 | tf_op jit(solution)/shard_map/ppermute | solution.py:460
  17.2 7.9 %collective-permute-start.3 = (bf16[32,3200]{1,0:T(8,128)(2,1)S(1)}, bf16[32,3200]{1,0:T(8,128)(2,1)S(1)}, u32[]{:S(2)}, u32[]{:S(2)}) collective-permute-start(bf16[32,3200]{1,0:T(8,128)(2,1)S(1)} %add_convert_fusion.rest_0_), channel_id=1, source_target_pairs={{0,2},{1,3},{2,0},{3,1},{4,6},{5,7},{6,4},{7,5},{8,10},{9,11},{10,... | collective-permute-start | bytes 614408 | tf_op jit(solution)/shard_map/ppermute | solution.py:463
  19.6 9.9 %collective-permute-start.12 = (bf16[80,1280]{1,0:T(8,128)(2,1)}, bf16[80,1280]{1,0:T(8,128)(2,1)}, u32[]{:S(2)}, u32[]{:S(2)}) collective-permute-start(bf16[80,1280]{1,0:T(8,128)(2,1)} %get-tuple-element.47), channel_id=1, source_target_pairs={{0,2},{1,3},{2,0},{3,1},{4,6},{5,7},{6,4},{7,5},{8,10},{9,11},{10,... | collective-permute-start | bytes 614408 | tf_op jit(solution)/shard_map/ppermute | solution.py:463
  25.7 26.9 %collective-permute-start.20 = (bf16[80,2304]{1,0:T(8,128)(2,1)}, bf16[80,2304]{1,0:T(8,128)(2,1)S(1)}, u32[]{:S(2)}, u32[]{:S(2)}) collective-permute-start(bf16[80,2304]{1,0:T(8,128)(2,1)} %get-tuple-element.56), channel_id=1, source_target_pairs={{0,2},{1,3},{2,0},{3,1},{4,6},{5,7},{6,4},{7,5},{8,10},{9,11},{10,... | collective-permute-start | bytes 1105928 | tf_op jit(solution)/shard_map/ppermute | solution.py:463
  29.6 3.6 %collective-permute-start.5 = (s32[384]{0:T(512)S(1)}, s32[384]{0:T(512)S(1)}, u32[]{:S(2)}, u32[]{:S(2)}) collective-permute-start(s32[384]{0:T(512)S(1)} %get-tuple-element.67), channel_id=1, source_target_pairs={{0,4},{4,0},{8,12},{12,8},{16,20},{20,16},{24,28},{28,24},{1,5},{5... | collective-permute-start | bytes 4616 | tf_op jit(solution)/shard_map/ppermute | solution.py:466
  33.1 6.4 %collective-permute-start.4 = (s32[384]{0:T(512)S(1)}, s32[384]{0:T(512)S(1)}, u32[]{:S(2)}, u32[]{:S(2)}) collective-permute-start(s32[384]{0:T(512)S(1)} %get-tuple-element.68), channel_id=1, source_target_pairs={{4,8},{12,16},{20,24},{28,0},{8,4},{16,12},{24,20},{0,28},{5,9},{1... | collective-permute-start | bytes 4616 | tf_op jit(solution)/shard_map/ppermute | solution.py:536
  39.5 13.6 %collective-permute-start.16 = (bf16[80,1280]{1,0:T(8,128)(2,1)}, bf16[80,1280]{1,0:T(8,128)(2,1)}, u32[]{:S(2)}, u32[]{:S(2)}) collective-permute-start(bf16[80,1280]{1,0:T(8,128)(2,1)} %collective-permute-done.12.rest_6_), channel_id=1, source_target_pairs={{0,1},{1,0},{2,3},{3,2},{4,5},{5,4},{6,7},{7,6},{8,9},{9,8},{10,11... | collective-permute-start | bytes 614408 | tf_op jit(solution)/shard_map/ppermute | solution.py:460
  39.5 13.6 %collective-permute-start.15 = (bf16[80,1280]{1,0:T(8,128)(2,1)}, bf16[80,1280]{1,0:T(8,128)(2,1)}, u32[]{:S(2)}, u32[]{:S(2)}) collective-permute-start(bf16[80,1280]{1,0:T(8,128)(2,1)} %collective-permute-done.12.rest_6_), channel_id=1, source_target_pairs={{0,12},{4,8},{8,4},{12,0},{16,28},{20,24},{24,20},{28,16},{1,13},{... | collective-permute-start | bytes 614408 | tf_op jit(solution)/shard_map/ppermute | solution.py:466
  40.4 14.2 %collective-permute-start.14 = (bf16[80,1280]{1,0:T(8,128)(2,1)}, bf16[80,1280]{1,0:T(8,128)(2,1)}, u32[]{:S(2)}, u32[]{:S(2)}) collective-permute-start(bf16[80,1280]{1,0:T(8,128)(2,1)} %collective-permute-done.12.rest_6_), channel_id=1, source_target_pairs={{0,8},{4,12},{8,0},{12,4},{16,24},{20,28},{24,16},{28,20},{1,9},{5... | collective-permute-start | bytes 614408 | tf_op jit(solution)/shard_map/ppermute | solution.py:466
  40.9 11.7 %collective-permute-start.13 = (bf16[80,1280]{1,0:T(8,128)(2,1)}, bf16[80,1280]{1,0:T(8,128)(2,1)}, u32[]{:S(2)}, u32[]{:S(2)}) collective-permute-start(bf16[80,1280]{1,0:T(8,128)(2,1)} %collective-permute-done.12.rest_6_), channel_id=1, source_target_pairs={{0,4},{4,0},{8,12},{12,8},{16,20},{20,16},{24,28},{28,24},{1,5},{5... | collective-permute-start | bytes 614408 | tf_op jit(solution)/shard_map/ppermute | solution.py:466
  45.2 12.9 %copy-start.4 = (bf16[32,3200]{1,0:T(8,128)(2,1)S(1)}, bf16[32,3200]{1,0:T(8,128)(2,1)}, u32[]{:S(2)}) copy-start(bf16[32,3200]{1,0:T(8,128)(2,1)} %copy-done.3) | copy-start | bytes 614404
  45.2 12.9 %copy-start.8 = (f32[2,1280]{1,0:T(2,128)S(1)}, f32[2,1280]{1,0:T(2,128)}, u32[]{:S(2)}) copy-start(f32[2,1280]{1,0:T(2,128)} %gain_in.1) | copy-start | bytes 30724
  45.2 12.9 %copy-start.10 = (f32[2,640]{1,0:T(2,128)S(1)}, f32[2,640]{1,0:T(2,128)}, u32[]{:S(2)}) copy-start(f32[2,640]{1,0:T(2,128)} %gain_out.3) | copy-start | bytes 15364
  52.6 3.5 %collective-permute-start.11 = (bf16[32,3200]{1,0:T(8,128)(2,1)S(1)}, bf16[32,3200]{1,0:T(8,128)(2,1)S(1)}, u32[]{:S(2)}, u32[]{:S(2)}) collective-permute-start(bf16[32,3200]{1,0:T(8,128)(2,1)S(1)} %copy-done.6), channel_id=1, source_target_pairs={{0,1},{1,0},{2,3},{3,2},{4,5},{5,4},{6,7},{7,6},{8,9},{9,8},{10,11... | collective-permute-start | bytes 614408 | tf_op jit(solution)/shard_map/ppermute | solution.py:460
  52.7 3.4 %collective-permute-start.17 = (bf16[80,1280]{1,0:T(8,128)(2,1)}, bf16[80,1280]{1,0:T(8,128)(2,1)S(1)}, u32[]{:S(2)}, u32[]{:S(2)}) collective-permute-start(bf16[80,1280]{1,0:T(8,128)(2,1)} %collective-permute-done.13.rest_7_), channel_id=1, source_target_pairs={{0,1},{1,0},{2,3},{3,2},{4,5},{5,4},{6,7},{7,6},{8,9},{9,8},{10,11... | collective-permute-start | bytes 614408 | tf_op jit(solution)/shard_map/ppermute | solution.py:460
  53.1 14.3 %collective-permute-start.22 = (bf16[80,2304]{1,0:T(8,128)(2,1)S(1)}, bf16[80,2304]{1,0:T(8,128)(2,1)S(1)}, u32[]{:S(2)}, u32[]{:S(2)}) collective-permute-start(bf16[80,2304]{1,0:T(8,128)(2,1)S(1)} %collective-permute-done.20.rest_5_), channel_id=1, source_target_pairs={{0,8},{4,12},{8,0},{12,4},{16,24},{20,28},{24,16},{28,20},{1,9},{5... | collective-permute-start | bytes 1105928 | tf_op jit(solution)/shard_map/ppermute | solution.py:466
  53.1 14.6 %collective-permute-start.21 = (bf16[80,2304]{1,0:T(8,128)(2,1)S(1)}, bf16[80,2304]{1,0:T(8,128)(2,1)S(1)}, u32[]{:S(2)}, u32[]{:S(2)}) collective-permute-start(bf16[80,2304]{1,0:T(8,128)(2,1)S(1)} %collective-permute-done.20.rest_5_), channel_id=1, source_target_pairs={{0,4},{4,0},{8,12},{12,8},{16,20},{20,16},{24,28},{28,24},{1,5},{5... | collective-permute-start | bytes 1105928 | tf_op jit(solution)/shard_map/ppermute | solution.py:466
  54.6 13.5 %collective-permute-start.23 = (bf16[80,2304]{1,0:T(8,128)(2,1)S(1)}, bf16[80,2304]{1,0:T(8,128)(2,1)S(1)}, u32[]{:S(2)}, u32[]{:S(2)}) collective-permute-start(bf16[80,2304]{1,0:T(8,128)(2,1)S(1)} %copy-done.13), channel_id=1, source_target_pairs={{0,2},{1,3},{2,0},{3,1},{4,6},{5,7},{6,4},{7,5},{8,10},{9,11},{10,... | collective-permute-start | bytes 1105928 | tf_op jit(solution)/shard_map/ppermute | solution.py:463
  56.1 1.7 %collective-permute-start.18 = (bf16[80,1280]{1,0:T(8,128)(2,1)}, bf16[80,1280]{1,0:T(8,128)(2,1)S(1)}, u32[]{:S(2)}, u32[]{:S(2)}) collective-permute-start(bf16[80,1280]{1,0:T(8,128)(2,1)} %collective-permute-done.14.rest_8_), channel_id=1, source_target_pairs={{0,1},{1,0},{2,3},{3,2},{4,5},{5,4},{6,7},{7,6},{8,9},{9,8},{10,11... | collective-permute-start | bytes 614408 | tf_op jit(solution)/shard_map/ppermute | solution.py:460
  56.1 1.9 %collective-permute-start.19 = (bf16[80,1280]{1,0:T(8,128)(2,1)}, bf16[80,1280]{1,0:T(8,128)(2,1)S(1)}, u32[]{:S(2)}, u32[]{:S(2)}) collective-permute-start(bf16[80,1280]{1,0:T(8,128)(2,1)} %collective-permute-done.15.rest_9_), channel_id=1, source_target_pairs={{0,1},{1,0},{2,3},{3,2},{4,5},{5,4},{6,7},{7,6},{8,9},{9,8},{10,11... | collective-permute-start | bytes 614408 | tf_op jit(solution)/shard_map/ppermute | solution.py:460
  57.8 11.7 %collective-permute-start.24 = (bf16[80,2304]{1,0:T(8,128)(2,1)S(1)}, bf16[80,2304]{1,0:T(8,128)(2,1)S(1)}, u32[]{:S(2)}, u32[]{:S(2)}) collective-permute-start(bf16[80,2304]{1,0:T(8,128)(2,1)S(1)} %collective-permute-done.20.rest_5_), channel_id=1, source_target_pairs={{0,1},{1,0},{2,3},{3,2},{4,5},{5,4},{6,7},{7,6},{8,9},{9,8},{10,11... | collective-permute-start | bytes 1105928 | tf_op jit(solution)/shard_map/ppermute | solution.py:460
  67.5 2.0 %collective-permute-start.26 = (bf16[80,2304]{1,0:T(8,128)(2,1)S(1)}, bf16[80,2304]{1,0:T(8,128)(2,1)S(1)}, u32[]{:S(2)}, u32[]{:S(2)}) collective-permute-start(bf16[80,2304]{1,0:T(8,128)(2,1)S(1)} %collective-permute-done.22.rest_7_), channel_id=1, source_target_pairs={{0,1},{1,0},{2,3},{3,2},{4,5},{5,4},{6,7},{7,6},{8,9},{9,8},{10,11... | collective-permute-start | bytes 1105928 | tf_op jit(solution)/shard_map/ppermute | solution.py:460
  67.8 2.0 %collective-permute-start.25 = (bf16[80,2304]{1,0:T(8,128)(2,1)S(1)}, bf16[80,2304]{1,0:T(8,128)(2,1)S(1)}, u32[]{:S(2)}, u32[]{:S(2)}) collective-permute-start(bf16[80,2304]{1,0:T(8,128)(2,1)S(1)} %collective-permute-done.21.rest_6_), channel_id=1, source_target_pairs={{0,1},{1,0},{2,3},{3,2},{4,5},{5,4},{6,7},{7,6},{8,9},{9,8},{10,11... | collective-permute-start | bytes 1105928 | tf_op jit(solution)/shard_map/ppermute | solution.py:460
  68.1 2.2 %collective-permute-start.27 = (bf16[80,2304]{1,0:T(8,128)(2,1)S(1)}, bf16[80,2304]{1,0:T(8,128)(2,1)S(1)}, u32[]{:S(2)}, u32[]{:S(2)}) collective-permute-start(bf16[80,2304]{1,0:T(8,128)(2,1)S(1)} %collective-permute-done.23.rest_8_), channel_id=1, source_target_pairs={{0,1},{1,0},{2,3},{3,2},{4,5},{5,4},{6,7},{7,6},{8,9},{9,8},{10,11... | collective-permute-start | bytes 1105928 | tf_op jit(solution)/shard_map/ppermute | solution.py:460
  (10 other events, 47.5 us)

commit v7 on v6

--- a/solution.py
+++ b/solution.py
@@ -25,6 +25,7 @@
 ANY = pl.BlockSpec(memory_space=pl.ANY)
 HBM = pl.BlockSpec(memory_space=pltpu.HBM)
 FREE = pl.CostEstimate(flops=0, bytes_accessed=0, transcendentals=0)
+LONG = pl.CostEstimate(flops=2 * 10**10, bytes_accessed=0, transcendentals=0)
 CUT_A = 18 * 128
 CUT_B = 17 * 128
 
@@ -162,13 +163,11 @@
         outs[0][...] = full[...]
 
 
-def hot_kernel(split, span, near, *rest):
-    copies = []
-    if split:
-        *w, hot5, hot1, near_out, near_in, near_conv, sem = rest
-        copies = chip_copies(*w, near_out, near_in, near_conv, sem)
-    else:
-        hot5, hot1 = rest
+def stage_kernel(*refs):
+    wait(chip_copies(*refs))
+
+
+def hot_kernel(span, near, hot5, hot1):
     codes = near[...]
     count = codes.shape[1]
     rows = hot5.shape[0]
@@ -180,7 +179,6 @@
         hot5[:, k * CODES : (k + 1) * CODES] = taps[k * DIL0 : k * DIL0 + rows]
     center = jnp.where(lanes == codes, 1.0, 0.0).T.astype(BF)
     hot1[...] = center[HALF * DIL0 : HALF * DIL0 + rows]
-    wait(copies)
 
 
 def rows_kernel(split, span, hot5, hot1, gain_out, gain_in, gain_mid, *rest):
@@ -492,12 +490,18 @@
     )(embed_table, break_vec, gain_in, w_in, conv_w, w_out)
 
     if split:
+        far_a = x_swap(parts[0])
         own = part + core_swap(part)
-        sent = own.astype(BF)
-        other = x_swap(sent)
-        pace = core_swap(sent[:16, :128])
-        far_a = x_swap(after(parts[0], pace))
-        near_out, near_in, near_conv = [core_swap(after(w, pace)) for w in (w_out, w_in, conv_w)]
+        other = x_swap(own.astype(BF))
+        near_out, near_in = core_swap(w_out), core_swap(w_in)
+        ends = codes[rows - REACH :], codes[:REACH]
+        low = seq_at % 2 == 0
+        even = seq_swap(jnp.where(low, *ends), 1)
+        pairs = [(i, i + 1) for i in range(1, seqs - 1, 2)]
+        pairs.append((seqs - 1, 0))
+        odd = lax.ppermute(jnp.where(low, *ends[::-1]), "seq", pairs + [(j, i) for i, j in pairs])
+        before, behind = jnp.where(low, odd, even), jnp.where(low, even, odd)
+        other = after(other, far_a, near_out, near_in, before, behind)
     else:
         own = lax.psum(part, "roll")
         other = jnp.zeros((CODES, H), BF)
@@ -520,46 +524,46 @@
         compiler_params=params(12),
     )(own, other, gain_mid, conv_w)
     if split:
+        near_conv = core_swap(after(conv_w, taps[1]))
+        relay = after(far_a, taps[1])
+        parts_a = [far_a] + [seq_swap(relay, b) for b in (1, 2, 3)]
         sent = (taps[0] + core_swap(taps[1]).astype(F32)).astype(BF)
         received = x_swap(sent)
-        near_sent = core_swap(sent)
-        relay = after(far_a, near_sent)
-        parts_a = [far_a] + [seq_swap(relay, b) for b in (1, 2, 3)]
-        far_b = x_swap(after(parts[1], near_sent))
-        near_received = core_swap(received)
-        codes = after(codes, received)
-        ends = codes[rows - REACH :], codes[:REACH]
-        low = seq_at % 2 == 0
-        even = seq_swap(jnp.where(low, *ends), 1)
-        pairs = [(i, i + 1) for i in range(1, seqs - 1, 2)]
-        pairs.append((seqs - 1, 0))
-        odd = lax.ppermute(jnp.where(low, *ends[::-1]), "seq", pairs + [(j, i) for i, j in pairs])
-        before, behind = jnp.where(low, odd, even), jnp.where(low, even, odd)
+        far_b = x_swap(after(parts[1], near_conv))
+        chip = pl.pallas_call(
+            stage_kernel,
+            out_shape=[
+                jax.ShapeDtypeStruct(n, BF)
+                for n in ((4 * shard + CODES, width), (8 * shard, H), (KERNEL * HEAD, H))
+            ],
+            in_specs=[ANY] * 7,
+            out_specs=[VMEM] * 3,
+            scratch_shapes=[pltpu.SemaphoreType.DMA],
+            cost_estimate=LONG,
+            compiler_params=params(16),
+        )(after(table, sent), w_out, w_in, conv_w, near_out, near_in, near_conv)
     spare = jnp.zeros((-(rows + 2 * REACH) % 128,), jnp.int32)
     near = jnp.concatenate([before, codes, behind, spare])[None]
-
-    shapes = [(wide_rows, KERNEL * CODES), (wide_rows, CODES)]
-    operands, scratch = [], []
-    if split:
-        operands = [table, w_out, w_in, conv_w, near_out, near_in, near_conv]
-        shapes += [(4 * shard + CODES, width), (8 * shard, H), (KERNEL * HEAD, H)]
-        scratch = [pltpu.SemaphoreType.DMA]
-    hot5, hot1, *chip = pl.pallas_call(
-        functools.partial(hot_kernel, split),
-        out_shape=[jax.ShapeDtypeStruct(n, BF) for n in shapes],
-        in_specs=[SMEM, VMEM] + [ANY] * len(operands),
-        out_specs=[VMEM] * len(shapes),
-        scratch_shapes=scratch,
+    if split:
+        near = after(near, chip[0])
+
+    hot5, hot1 = pl.pallas_call(
+        hot_kernel,
+        out_shape=[jax.ShapeDtypeStruct((wide_rows, n), BF) for n in (KERNEL * CODES, CODES)],
+        in_specs=[SMEM, VMEM],
+        out_specs=[VMEM] * 2,
         cost_estimate=FREE,
-        compiler_params=params(16),
-    )(span, near, *operands)
-
-    if split:
-        near_a = [core_swap(relay)] + [core_swap(after(p, hot1)) for p in parts_a[1:]]
-        relay = after(far_b, hot1)
-        parts_b = [far_b, seq_swap(relay, 1), seq_swap(relay, 2), x_swap(after(parts[2], hot1))]
-        near_b = [core_swap(relay)]
-        weights_a = [sent, received, near_sent, near_received] + chip[:2] + parts_a + near_a
+        compiler_params=params(12),
+    )(span, near)
+
+    if split:
+        received = after(received, hot1, *parts_a)
+        near_received = core_swap(received)
+        near_sent = core_swap(after(sent, received))
+        near_a = [core_swap(after(p, received)) for p in parts_a]
+        relay = after(far_b, received)
+        parts_b = [far_b, seq_swap(relay, 1), seq_swap(relay, 2), x_swap(after(parts[2], received))]
+        weights_a = [sent, received, near_sent, near_received] + list(chip[:2]) + parts_a + near_a
     else:
         taps = lax.psum(taps[0], "roll").astype(BF)
         gather = lambda w: lax.all_gather(w, "roll", axis=0, tiled=True)
@@ -579,18 +583,18 @@
             pltpu.VMEM((width, H), BF),
             pltpu.SemaphoreType.DMA((3,)),
         ],
-        cost_estimate=FREE,
+        cost_estimate=LONG,
         compiler_params=params(30),
     )(span, hot5, hot1, gain_out, gain_in, gain_mid, *weights_a)
 
     if split:
-        near_b += [core_swap(after(p, ci)) for p in parts_b[1:]]
+        near_b = [core_swap(after(p, ci)) for p in parts_b]
         head = pl.pallas_call(
             head_kernel,
             out_shape=jax.ShapeDtypeStruct((rows, H), F32),
             in_specs=[VMEM] * 2,
             out_specs=VMEM,
-            cost_estimate=FREE,
+            cost_estimate=LONG,
             compiler_params=params(16),
         )(ci, chip[2])
         weights_b = [head, conv_w, w_out, near_conv, near_out] + parts_b + near_b

time: 76.4 us -> 64.7 us (0.85)
  waiting for transfers between devices: 21.8 us -> 12 us
  starting transfers between devices: 24.6 us -> 20.5 us
  Pallas kernels: 22.6 us -> 24.5 us
    ppermute x6, waiting for transfers between devices: 5.98 us -> 0.02 us  [seq_swap(): return lax.ppermute(x, 'seq', [(i, i ^ bits) for i in range(seqs)])]
    ppermute x16 -> x15, waiting for transfers between devices: 5.18 us -> 1.51 us  [core_swap(): return lax.ppermute(x, 'roll', [(i, i ^ 1) for i in range(rolls)])]
    ppermute x5, starting transfers between devices: 8.93 us -> 5.74 us  [x_swap(): return lax.ppermute(x, 'roll', [(i, i ^ 2) for i in range(rolls)])]
    ppermute x1, waiting for transfers between devices: 1.49 us -> 0.01 us  [per_device(): lax.ppermute(jnp.where(low, *ends[::-1]), 'seq', pairs + [(j, i) for i, j...]
    ppermute x5, waiting for transfers between devices: 9.13 us -> 10.5 us  [x_swap(): return lax.ppermute(x, 'roll', [(i, i ^ 2) for i in range(rolls)])]
    ppermute x1, starting transfers between devices: 4.81 us -> 3.54 us  [per_device(): lax.ppermute(jnp.where(low, *ends[::-1]), 'seq', pairs + [(j, i) for i, j...]
    pallas_call x1, Pallas kernels: 9.38 us -> 10.2 us  [per_device(): pl.pallas_call(functools.partial(rows_kernel, split), out_shape=(jax.Shap...]
    unnamed x28 -> x26, local copies, waits for them, and re-layouts: 3.44 us -> 4.13 us
  transfers between devices with their start and end apart: 28 -> 27, of which waited for: 13 -> 6; matrix products, arithmetic and copies ran while one was open for 2% -> 3% of each run, Pallas kernels for 19% -> 27%
where the time goes in v7:
time: 64.7 us; the launch traced here: 64.3 us
  Pallas kernels  24.5 us (38%)
  starting transfers between devices  20.5 us (32%)
  waiting for transfers between devices  12 us (19%)
  local copies, waits for them, and re-layouts  4.21 us (7%)
  other arithmetic  2.09 us (3%)
  between operations  1.02 us (2%)
    ppermute x5, waiting for transfers between devices, x_swap(): return lax.ppermute(x, 'roll', [(i, i ^ 2) for i in range(rolls)])  10.5 us
    pallas_call x1, Pallas kernels, per_device(): pl.pallas_call(functools.partial(rows_kernel, split), out_shape=(jax.Shap...  10.2 us
    ppermute x6, starting transfers between devices, seq_swap(): return lax.ppermute(x, 'seq', [(i, i ^ bits) for i in range(seqs)])  7.24 us
    ppermute x5, starting transfers between devices, x_swap(): return lax.ppermute(x, 'roll', [(i, i ^ 2) for i in range(rolls)])  5.74 us
    pallas_call x1, Pallas kernels, per_device(): pl.pallas_call(functools.partial(last_kernel, split), out_shape=jax.Shape...  5.07 us
    unnamed x26, local copies, waits for them, and re-layouts  4.13 us
    ppermute x15, starting transfers between devices, core_swap(): return lax.ppermute(x, 'roll', [(i, i ^ 1) for i in range(rolls)])  3.99 us
    ppermute x1, starting transfers between devices, per_device(): lax.ppermute(jnp.where(low, *ends[::-1]), 'seq', pairs + [(j, i) for i, j...  3.54 us
  transfers between devices with their start and end apart: 27, of which 6 were waited for; matrix products, arithmetic and copies ran while one was open for 3% of the time, Pallas kernels for 27%

profile of v7, /device:TPU:0, one launch (start us, length us, event | category | flops | bytes accessed | tf_op | source)
XLA Modules:
  0.0 64.3 jit_solution(2828528711488947067)
XLA Ops:
  0.0 0.5 collective-permute-start.6
  0.6 3.1 %shard_map.109 = (bf16[64,1280]{1,0:T(8,128)(2,1)}, f32[64,640]{1,0:T(8,128)}, bf16[80,1280]{1,0:T(8,128)(2,1)}, bf16[80,2304]{1,0:T(8,128)(2,1)}, bf16[80,2304]{1,0:T(8,128)(2,1)}) custom-call(f32[30,1280]{1,0:T(8,128)} %embed.1, f32[1280]{0:T(1024)} %brk.1, f32[2,1280]{1,0:T(2,128)} %gain_in.1, bf16[2,320,640]{2,1,0:T(8,128)(2,1)} %refs_2_.1, ...), custom_call_target="tpu_custom_call" | custom-call | tf_op jit(solution)/shard_map/pallas_call | solution.py:474
  3.7 0.5 collective-permute-start.2
  4.4 2.6 %collective-permute-start.1 = (s32[384]{0:T(512)S(1)}, s32[384]{0:T(512)S(1)}, u32[]{:S(2)}, u32[]{:S(2)}) collective-permute-start(s32[384]{0:T(512)S(1)} %get-tuple-element.69), channel_id=1, source_target_pairs={{0,4},{4,0},{8,12},{12,8},{16,20},{20,16},{24,28},{28,24},{1,5},{5... | collective-permute-start | bytes 4616 | tf_op jit(solution)/shard_map/ppermute | solution.py:464
  7.0 3.5 %collective-permute-start = (s32[384]{0:T(512)S(1)}, s32[384]{0:T(512)S(1)}, u32[]{:S(2)}, u32[]{:S(2)}) collective-permute-start(s32[384]{0:T(512)S(1)} %get-tuple-element.70), channel_id=1, source_target_pairs={{4,8},{12,16},{20,24},{28,0},{8,4},{16,12},{24,20},{0,28},{5,9},{1... | collective-permute-start | bytes 4616 | tf_op jit(solution)/shard_map/ppermute | solution.py:502
  10.5 1.5 %collective-permute-start.4 = (bf16[80,1280]{1,0:T(8,128)(2,1)}, bf16[80,1280]{1,0:T(8,128)(2,1)S(1)}, u32[]{:S(2)}, u32[]{:S(2)}) collective-permute-start(bf16[80,1280]{1,0:T(8,128)(2,1)} %get-tuple-element.39), channel_id=1, source_target_pairs={{0,2},{1,3},{2,0},{3,1},{4,6},{5,7},{6,4},{7,5},{8,10},{9,11},{10,... | collective-permute-start | bytes 614408 | tf_op jit(solution)/shard_map/ppermute | solution.py:461
  12.0 1.0 %fusion.2 = (bf16[64,640]{1,0:T(8,128)(2,1)S(1)}, f32[64,640]{1,0:T(8,128)S(1)}) fusion(f32[64,640]{1,0:T(8,128)} %get-tuple-element.38, f32[64,640]{1,0:T(8,128)S(1)} %collective-permute-done.2), kind=kLoop, calls=%fused_computation.9 | loop fusion | flops 81920 | bytes 573440 | tf_op jit(solution)/shard_map/convert_element_type | solution.py:495
  13.0 0.6 collective-permute-start.3
  13.6 4.9 %collective-permute-done.4.rest_6_ = bf16[80,1280]{1,0:T(8,128)(2,1)S(1)} collective-permute-done((bf16[80,1280]{1,0:T(8,128)(2,1)}, bf16[80,1280]{1,0:T(8,128)(2,1)S(1)}, u32[]{:S(2)}, u32[]{:S(2)}) %collective-permute-start.4) | collective-permute-done | bytes 204832 | tf_op jit(solution)/shard_map/ppermute | solution.py:461
  18.5 0.9 %collective-permute-done.3.other = bf16[64,640]{1,0:T(8,128)(2,1)S(1)} collective-permute-done((bf16[64,640]{1,0:T(8,128)(2,1)S(1)}, bf16[64,640]{1,0:T(8,128)(2,1)S(1)}, u32[]{:S(2)}, u32[]{:S(2)}) %collective-permute-start.3) | collective-permute-done | bytes 81952 | tf_op jit(solution)/shard_map/ppermute | solution.py:461
  19.4 0.9 %copy-done.3 = bf16[2,160,1280]{2,1,0:T(8,128)(2,1)} copy-done((bf16[2,160,1280]{2,1,0:T(8,128)(2,1)}, bf16[2,160,1280]{2,1,0:T(8,128)(2,1)S(1)}, u32[]{:S(2)}) %copy-start.3) | copy-done | bytes 819224
  20.3 1.8 %shard_map.110 = (f32[32,3200]{1,0:T(8,128)S(1)}, bf16[32,3200]{1,0:T(8,128)(2,1)}) custom-call(f32[64,640]{1,0:T(8,128)S(1)} %get-tuple-element.72.own, bf16[64,640]{1,0:T(8,128)(2,1)S(1)} %collective-permute-done.3.other, f32[2,640]{1,0:T(2,128)S(1)} %copy-done.7, bf16[2,160,3200]{2,1,0:T(8,128)(2,1)S(1)} %copy-done), custom_call_target="tpu_custom_call" | custom-call | tf_op jit(solution)/shard_map/pallas_call | solution.py:513
  22.2 0.5 collective-permute-start.7
  23.5 0.6 collective-permute-start.12
  24.6 2.5 %collective-permute-start.10 = (bf16[80,1280]{1,0:T(8,128)(2,1)S(1)}, bf16[80,1280]{1,0:T(8,128)(2,1)S(1)}, u32[]{:S(2)}, u32[]{:S(2)}) collective-permute-start(bf16[80,1280]{1,0:T(8,128)(2,1)S(1)} %collective-permute-done.4.rest_6_), channel_id=1, source_target_pairs={{0,4},{4,0},{8,12},{12,8},{16,20},{20,16},{24,28},{28,24},{1,5},{5... | collective-permute-start | bytes 614408 | tf_op jit(solution)/shard_map/ppermute | solution.py:464
  27.1 1.0 %add_convert_fusion.rest_0_ = bf16[32,3200]{1,0:T(8,128)(2,1)S(1)} fusion(f32[32,3200]{1,0:T(8,128)S(1)} %get-tuple-element.41, bf16[32,3200]{1,0:T(8,128)(2,1)} %collective-permute-done.7), kind=kLoop, calls=%fused_computation | loop fusion | flops 307200 | bytes 819200 | tf_op jit(solution)/shard_map/convert_element_type | solution.py:530
  28.1 1.6 %collective-permute-start.9 = (bf16[32,3200]{1,0:T(8,128)(2,1)S(1)}, bf16[32,3200]{1,0:T(8,128)(2,1)S(1)}, u32[]{:S(2)}, u32[]{:S(2)}) collective-permute-start(bf16[32,3200]{1,0:T(8,128)(2,1)S(1)} %add_convert_fusion.rest_0_), channel_id=1, source_target_pairs={{0,2},{1,3},{2,0},{3,1},{4,6},{5,7},{6,4},{7,5},{8,10},{9,11},{10,... | collective-permute-start | bytes 614408 | tf_op jit(solution)/shard_map/ppermute | solution.py:461
  29.6 0.5 collective-permute-start.19
  30.2 1.1 %copy-done.2 = bf16[2,320,640]{2,1,0:T(8,128)(2,1)S(1)} copy-done((bf16[2,320,640]{2,1,0:T(8,128)(2,1)S(1)}, bf16[2,320,640]{2,1,0:T(8,128)(2,1)}, u32[]{:S(2)}) %copy-start.2) | copy-done | bytes 819224
  31.3 1.1 %copy-done.4 = bf16[2,160,1280]{2,1,0:T(8,128)(2,1)S(1)} copy-done((bf16[2,160,1280]{2,1,0:T(8,128)(2,1)S(1)}, bf16[2,160,1280]{2,1,0:T(8,128)(2,1)}, u32[]{:S(2)}) %copy-start.4) | copy-done | bytes 819224
  32.5 0.9 %copy-done.9 = bf16[64,1280]{1,0:T(8,128)(2,1)S(1)} copy-done((bf16[64,1280]{1,0:T(8,128)(2,1)S(1)}, bf16[64,1280]{1,0:T(8,128)(2,1)}, u32[]{:S(2)}) %copy-start.9) | copy-done | bytes 163864
  33.4 2.1 %shard_map.111 = (bf16[384,1280]{1,0:T(8,128)(2,1)S(1)}, bf16[640,640]{1,0:T(8,128)(2,1)S(1)}, bf16[1280,640]{1,0:T(8,128)(2,1)S(1)}) custom-call(bf16[64,1280]{1,0:T(8,128)(2,1)S(1)} %copy-done.9, bf16[2,160,1280]{2,1,0:T(8,128)(2,1)S(1)} %copy-done.1, bf16[2,320,640]{2,1,0:T(8,128)(2,1)S(1)} %copy-done.2, bf16[2,160,3200]{2,1,0:T(8,128)(2,1)S(1)} %copy-done, ...), custom_call_target="tpu_custom_call" | custom-call | flops 20000000000 | tf_op jit(solution)/shard_map/pallas_call | solution.py:533
  35.5 1.0 %shard_map.112 = (bf16[1008,320]{1,0:T(8,128)(2,1)S(1)}, bf16[1008,64]{1,0:T(8,128)(2,1)S(1)}) custom-call(s32[2]{0:T(128)S(1)} %pad_add_fusion.span, s32[1,1280]{1,0:T(1,128)S(1)} %broadcast_in_dim.6.near), custom_call_target="tpu_custom_call" | custom-call | tf_op jit(solution)/shard_map/pallas_call | solution.py:550
  36.6 0.5 collective-permute-start.15
  38.2 4.7 %collective-permute-done.19.rest_5_ = bf16[80,2304]{1,0:T(8,128)(2,1)S(1)} collective-permute-done((bf16[80,2304]{1,0:T(8,128)(2,1)}, bf16[80,2304]{1,0:T(8,128)(2,1)S(1)}, u32[]{:S(2)}, u32[]{:S(2)}) %collective-permute-start.19) | collective-permute-done | bytes 368672 | tf_op jit(solution)/shard_map/ppermute | solution.py:461
  42.9 1.6 %collective-permute-start.22 = (bf16[80,2304]{1,0:T(8,128)(2,1)S(1)}, bf16[80,2304]{1,0:T(8,128)(2,1)S(1)}, u32[]{:S(2)}, u32[]{:S(2)}) collective-permute-start(bf16[80,2304]{1,0:T(8,128)(2,1)S(1)} %copy-done.12), channel_id=1, source_target_pairs={{0,2},{1,3},{2,0},{3,1},{4,6},{5,7},{6,4},{7,5},{8,10},{9,11},{10,... | collective-permute-start | bytes 1105928 | tf_op jit(solution)/shard_map/ppermute | solution.py:461
  44.4 1.1 %collective-permute-start.20 = (bf16[80,2304]{1,0:T(8,128)(2,1)S(1)}, bf16[80,2304]{1,0:T(8,128)(2,1)S(1)}, u32[]{:S(2)}, u32[]{:S(2)}) collective-permute-start(bf16[80,2304]{1,0:T(8,128)(2,1)S(1)} %collective-permute-done.19.rest_5_), channel_id=1, source_target_pairs={{0,4},{4,0},{8,12},{12,8},{16,20},{20,16},{24,28},{28,24},{1,5},{5... | collective-permute-start | bytes 1105928 | tf_op jit(solution)/shard_map/ppermute | solution.py:464
  45.5 10.2 %shard_map.113 = (bf16[1008,640]{1,0:T(8,128)(2,1)S(1)}, bf16[496,1280]{1,0:T(8,128)(2,1)S(1)}) custom-call(s32[2]{0:T(128)S(1)} %pad_add_fusion.span, bf16[1008,320]{1,0:T(8,128)(2,1)S(1)} %get-tuple-element.47.hot5, bf16[1008,64]{1,0:T(8,128)(2,1)S(1)} %get-tuple-element.48.hot1, f32[2,640]{1,0:T(2,128)S(1)} %copy-done.8, f32[2,1280]{1,0:T(2,128)S(1)} %copy-done.6, ...), custom_call_target="tpu_custom_call" | custom-call | flops 20000000000 | tf_op jit(solution)/shard_map/pallas_call | solution.py:572
  56.9 1.2 %shard_map.114.rest_0_ = f32[496,640]{1,0:T(8,128)S(1)} custom-call(bf16[1008,640]{1,0:T(8,128)(2,1)S(1)} %get-tuple-element.57.ci, bf16[1280,640]{1,0:T(8,128)(2,1)S(1)} %get-tuple-element.59.w_conv), custom_call_target="tpu_custom_call" | custom-call | flops 20000000000 | tf_op jit(solution)/shard_map/pallas_call | solution.py:592
  58.1 0.5 collective-permute-done.25.rest_11_
  58.6 0.5 collective-permute-done.24.rest_10_
  59.1 5.1 %shard_map.115 = bf16[496,1280]{1,0:T(8,128)(2,1)} custom-call(bf16[1008,640]{1,0:T(8,128)(2,1)S(1)} %get-tuple-element.57.ci, bf16[496,1280]{1,0:T(8,128)(2,1)S(1)} %get-tuple-element.58.hid, f32[2,640]{1,0:T(2,128)S(1)} %copy-done.8, f32[496,640]{1,0:T(8,128)S(1)} %shard_map.114.rest_0_, bf16[2,160,3200]{2,1,0:T(8,128)(2,1)S(1)} %copy-done, ...), custom_call_target="tpu_custom_call" | custom-call | tf_op jit(solution)/shard_map/pallas_call | solution.py:601
  (64 shorter events, 3.2 us)
Async XLA Ops:
  0.0 20.3 %copy-start = (bf16[2,160,3200]{2,1,0:T(8,128)(2,1)S(1)}, bf16[2,160,3200]{2,1,0:T(8,128)(2,1)}, u32[]{:S(2)}) copy-start(bf16[2,160,3200]{2,1,0:T(8,128)(2,1)} %rest_1_.1) | copy-start | bytes 6144004
  0.0 20.3 %copy-start.7 = (f32[2,640]{1,0:T(2,128)S(1)}, f32[2,640]{1,0:T(2,128)}, u32[]{:S(2)}) copy-start(f32[2,640]{1,0:T(2,128)} %gain_mid.1) | copy-start | bytes 15364
  0.0 19.4 %collective-permute-start.6 = (bf16[2,320,640]{2,1,0:T(8,128)(2,1)}, bf16[2,320,640]{2,1,0:T(8,128)(2,1)}, u32[]{:S(2)}, u32[]{:S(2)}) collective-permute-start(bf16[2,320,640]{2,1,0:T(8,128)(2,1)} %refs_2_.1), channel_id=1, source_target_pairs={{0,1},{1,0},{2,3},{3,2},{4,5},{5,4},{6,7},{7,6},{8,9},{9,8},{10,11... | collective-permute-start | bytes 2457608 | tf_op jit(solution)/shard_map/ppermute | solution.py:458
  0.5 18.9 %collective-permute-start.5 = (bf16[2,160,1280]{2,1,0:T(8,128)(2,1)}, bf16[2,160,1280]{2,1,0:T(8,128)(2,1)S(1)}, u32[]{:S(2)}, u32[]{:S(2)}) collective-permute-start(bf16[2,160,1280]{2,1,0:T(8,128)(2,1)} %rest_2_.1), channel_id=1, source_target_pairs={{0,1},{1,0},{2,3},{3,2},{4,5},{5,4},{6,7},{7,6},{8,9},{9,8},{10,11... | collective-permute-start | bytes 2457608 | tf_op jit(solution)/shard_map/ppermute | solution.py:458
  3.7 6.8 %collective-permute-start.2 = (f32[64,640]{1,0:T(8,128)}, f32[64,640]{1,0:T(8,128)S(1)}, u32[]{:S(2)}, u32[]{:S(2)}) collective-permute-start(f32[64,640]{1,0:T(8,128)} %get-tuple-element.38), channel_id=1, source_target_pairs={{0,1},{1,0},{2,3},{3,2},{4,5},{5,4},{6,7},{7,6},{8,9},{9,8},{10,11... | collective-permute-start | bytes 491528 | tf_op jit(solution)/shard_map/ppermute | solution.py:458
  4.4 8.6 %collective-permute-start.1 = (s32[384]{0:T(512)S(1)}, s32[384]{0:T(512)S(1)}, u32[]{:S(2)}, u32[]{:S(2)}) collective-permute-start(s32[384]{0:T(512)S(1)} %get-tuple-element.69), channel_id=1, source_target_pairs={{0,4},{4,0},{8,12},{12,8},{16,20},{20,16},{24,28},{28,24},{1,5},{5... | collective-permute-start | bytes 4616 | tf_op jit(solution)/shard_map/ppermute | solution.py:464
  7.0 6.6 %collective-permute-start = (s32[384]{0:T(512)S(1)}, s32[384]{0:T(512)S(1)}, u32[]{:S(2)}, u32[]{:S(2)}) collective-permute-start(s32[384]{0:T(512)S(1)} %get-tuple-element.70), channel_id=1, source_target_pairs={{4,8},{12,16},{20,24},{28,0},{8,4},{16,12},{24,20},{0,28},{5,9},{1... | collective-permute-start | bytes 4616 | tf_op jit(solution)/shard_map/ppermute | solution.py:502
  10.5 8.0 %collective-permute-start.4 = (bf16[80,1280]{1,0:T(8,128)(2,1)}, bf16[80,1280]{1,0:T(8,128)(2,1)S(1)}, u32[]{:S(2)}, u32[]{:S(2)}) collective-permute-start(bf16[80,1280]{1,0:T(8,128)(2,1)} %get-tuple-element.39), channel_id=1, source_target_pairs={{0,2},{1,3},{2,0},{3,1},{4,6},{5,7},{6,4},{7,5},{8,10},{9,11},{10,... | collective-permute-start | bytes 614408 | tf_op jit(solution)/shard_map/ppermute | solution.py:461
  13.0 6.4 %collective-permute-start.3 = (bf16[64,640]{1,0:T(8,128)(2,1)S(1)}, bf16[64,640]{1,0:T(8,128)(2,1)S(1)}, u32[]{:S(2)}, u32[]{:S(2)}) collective-permute-start(bf16[64,640]{1,0:T(8,128)(2,1)S(1)} %get-tuple-element.71), channel_id=1, source_target_pairs={{0,2},{1,3},{2,0},{3,1},{4,6},{5,7},{6,4},{7,5},{8,10},{9,11},{10,... | collective-permute-start | bytes 245768 | tf_op jit(solution)/shard_map/ppermute | solution.py:461
  20.3 9.9 %copy-start.1 = (bf16[2,160,1280]{2,1,0:T(8,128)(2,1)S(1)}, bf16[2,160,1280]{2,1,0:T(8,128)(2,1)}, u32[]{:S(2)}) copy-start(bf16[2,160,1280]{2,1,0:T(8,128)(2,1)} %rest_2_.1) | copy-start | bytes 2457604
  22.2 7.5 %collective-permute-start.8 = (bf16[2,160,3200]{2,1,0:T(8,128)(2,1)S(1)}, bf16[2,160,3200]{2,1,0:T(8,128)(2,1)}, u32[]{:S(2)}, u32[]{:S(2)}) collective-permute-start(bf16[2,160,3200]{2,1,0:T(8,128)(2,1)S(1)} %copy-done), channel_id=1, source_target_pairs={{0,1},{1,0},{2,3},{3,2},{4,5},{5,4},{6,7},{7,6},{8,9},{9,8},{10,11... | collective-permute-start | bytes 6144008 | tf_op jit(solution)/shard_map/ppermute | solution.py:458
  22.2 4.9 %collective-permute-start.7 = (bf16[32,3200]{1,0:T(8,128)(2,1)}, bf16[32,3200]{1,0:T(8,128)(2,1)}, u32[]{:S(2)}, u32[]{:S(2)}) collective-permute-start(bf16[32,3200]{1,0:T(8,128)(2,1)} %get-tuple-element.42), channel_id=1, source_target_pairs={{0,1},{1,0},{2,3},{3,2},{4,5},{5,4},{6,7},{7,6},{8,9},{9,8},{10,11... | collective-permute-start | bytes 614408 | tf_op jit(solution)/shard_map/ppermute | solution.py:458
  23.5 13.0 %collective-permute-start.12 = (bf16[80,1280]{1,0:T(8,128)(2,1)S(1)}, bf16[80,1280]{1,0:T(8,128)(2,1)S(1)}, u32[]{:S(2)}, u32[]{:S(2)}) collective-permute-start(bf16[80,1280]{1,0:T(8,128)(2,1)S(1)} %collective-permute-done.4.rest_6_), channel_id=1, source_target_pairs={{0,12},{4,8},{8,4},{12,0},{16,28},{20,24},{24,20},{28,16},{1,13},{... | collective-permute-start | bytes 614408 | tf_op jit(solution)/shard_map/ppermute | solution.py:464
  24.1 12.4 %collective-permute-start.11 = (bf16[80,1280]{1,0:T(8,128)(2,1)S(1)}, bf16[80,1280]{1,0:T(8,128)(2,1)S(1)}, u32[]{:S(2)}, u32[]{:S(2)}) collective-permute-start(bf16[80,1280]{1,0:T(8,128)(2,1)S(1)} %collective-permute-done.4.rest_6_), channel_id=1, source_target_pairs={{0,8},{4,12},{8,0},{12,4},{16,24},{20,28},{24,16},{28,20},{1,9},{5... | collective-permute-start | bytes 614408 | tf_op jit(solution)/shard_map/ppermute | solution.py:464
  24.6 12.0 %collective-permute-start.10 = (bf16[80,1280]{1,0:T(8,128)(2,1)S(1)}, bf16[80,1280]{1,0:T(8,128)(2,1)S(1)}, u32[]{:S(2)}, u32[]{:S(2)}) collective-permute-start(bf16[80,1280]{1,0:T(8,128)(2,1)S(1)} %collective-permute-done.4.rest_6_), channel_id=1, source_target_pairs={{0,4},{4,0},{8,12},{12,8},{16,20},{20,16},{24,28},{28,24},{1,5},{5... | collective-permute-start | bytes 614408 | tf_op jit(solution)/shard_map/ppermute | solution.py:464
  28.1 8.5 %collective-permute-start.9 = (bf16[32,3200]{1,0:T(8,128)(2,1)S(1)}, bf16[32,3200]{1,0:T(8,128)(2,1)S(1)}, u32[]{:S(2)}, u32[]{:S(2)}) collective-permute-start(bf16[32,3200]{1,0:T(8,128)(2,1)S(1)} %add_convert_fusion.rest_0_), channel_id=1, source_target_pairs={{0,2},{1,3},{2,0},{3,1},{4,6},{5,7},{6,4},{7,5},{8,10},{9,11},{10,... | collective-permute-start | bytes 614408 | tf_op jit(solution)/shard_map/ppermute | solution.py:461
  29.6 13.2 %collective-permute-start.19 = (bf16[80,2304]{1,0:T(8,128)(2,1)}, bf16[80,2304]{1,0:T(8,128)(2,1)S(1)}, u32[]{:S(2)}, u32[]{:S(2)}) collective-permute-start(bf16[80,2304]{1,0:T(8,128)(2,1)} %get-tuple-element.61), channel_id=1, source_target_pairs={{0,2},{1,3},{2,0},{3,1},{4,6},{5,7},{6,4},{7,5},{8,10},{9,11},{10,... | collective-permute-start | bytes 1105928 | tf_op jit(solution)/shard_map/ppermute | solution.py:461
  33.4 12.2 %copy-start.6 = (f32[2,1280]{1,0:T(2,128)S(1)}, f32[2,1280]{1,0:T(2,128)}, u32[]{:S(2)}) copy-start(f32[2,1280]{1,0:T(2,128)} %gain_in.1) | copy-start | bytes 30724
  33.4 12.2 %copy-start.8 = (f32[2,640]{1,0:T(2,128)S(1)}, f32[2,640]{1,0:T(2,128)}, u32[]{:S(2)}) copy-start(f32[2,640]{1,0:T(2,128)} %gain_out.3) | copy-start | bytes 15364
  36.5 1.5 %collective-permute-start.13 = (bf16[32,3200]{1,0:T(8,128)(2,1)S(1)}, bf16[32,3200]{1,0:T(8,128)(2,1)S(1)}, u32[]{:S(2)}, u32[]{:S(2)}) collective-permute-start(bf16[32,3200]{1,0:T(8,128)(2,1)S(1)} %add_convert_fusion.rest_0_), channel_id=1, source_target_pairs={{0,1},{1,0},{2,3},{3,2},{4,5},{5,4},{6,7},{7,6},{8,9},{9,8},{10,11... | collective-permute-start | bytes 614408 | tf_op jit(solution)/shard_map/ppermute | solution.py:458
  36.6 6.2 %collective-permute-start.15 = (bf16[80,1280]{1,0:T(8,128)(2,1)S(1)}, bf16[80,1280]{1,0:T(8,128)(2,1)S(1)}, u32[]{:S(2)}, u32[]{:S(2)}) collective-permute-start(bf16[80,1280]{1,0:T(8,128)(2,1)S(1)} %collective-permute-done.4.rest_6_), channel_id=1, source_target_pairs={{0,1},{1,0},{2,3},{3,2},{4,5},{5,4},{6,7},{7,6},{8,9},{9,8},{10,11... | collective-permute-start | bytes 614408 | tf_op jit(solution)/shard_map/ppermute | solution.py:458
  37.1 7.3 %collective-permute-start.16 = (bf16[80,1280]{1,0:T(8,128)(2,1)S(1)}, bf16[80,1280]{1,0:T(8,128)(2,1)S(1)}, u32[]{:S(2)}, u32[]{:S(2)}) collective-permute-start(bf16[80,1280]{1,0:T(8,128)(2,1)S(1)} %collective-permute-done.10.rest_7_), channel_id=1, source_target_pairs={{0,1},{1,0},{2,3},{3,2},{4,5},{5,4},{6,7},{7,6},{8,9},{9,8},{10,11... | collective-permute-start | bytes 614408 | tf_op jit(solution)/shard_map/ppermute | solution.py:458
  37.2 7.2 %collective-permute-start.17 = (bf16[80,1280]{1,0:T(8,128)(2,1)S(1)}, bf16[80,1280]{1,0:T(8,128)(2,1)S(1)}, u32[]{:S(2)}, u32[]{:S(2)}) collective-permute-start(bf16[80,1280]{1,0:T(8,128)(2,1)S(1)} %collective-permute-done.11.rest_8_), channel_id=1, source_target_pairs={{0,1},{1,0},{2,3},{3,2},{4,5},{5,4},{6,7},{7,6},{8,9},{9,8},{10,11... | collective-permute-start | bytes 614408 | tf_op jit(solution)/shard_map/ppermute | solution.py:458
  38.1 7.5 %collective-permute-start.18 = (bf16[80,1280]{1,0:T(8,128)(2,1)S(1)}, bf16[80,1280]{1,0:T(8,128)(2,1)S(1)}, u32[]{:S(2)}, u32[]{:S(2)}) collective-permute-start(bf16[80,1280]{1,0:T(8,128)(2,1)S(1)} %collective-permute-done.12.rest_9_), channel_id=1, source_target_pairs={{0,1},{1,0},{2,3},{3,2},{4,5},{5,4},{6,7},{7,6},{8,9},{9,8},{10,11... | collective-permute-start | bytes 614408 | tf_op jit(solution)/shard_map/ppermute | solution.py:458
  42.9 2.7 %collective-permute-start.14 = (bf16[32,3200]{1,0:T(8,128)(2,1)S(1)}, bf16[32,3200]{1,0:T(8,128)(2,1)S(1)}, u32[]{:S(2)}, u32[]{:S(2)}) collective-permute-start(bf16[32,3200]{1,0:T(8,128)(2,1)S(1)} %collective-permute-done.9.rest_1_), channel_id=1, source_target_pairs={{0,1},{1,0},{2,3},{3,2},{4,5},{5,4},{6,7},{7,6},{8,9},{9,8},{10,11... | collective-permute-start | bytes 614408 | tf_op jit(solution)/shard_map/ppermute | solution.py:458
  42.9 13.0 %collective-permute-start.22 = (bf16[80,2304]{1,0:T(8,128)(2,1)S(1)}, bf16[80,2304]{1,0:T(8,128)(2,1)S(1)}, u32[]{:S(2)}, u32[]{:S(2)}) collective-permute-start(bf16[80,2304]{1,0:T(8,128)(2,1)S(1)} %copy-done.12), channel_id=1, source_target_pairs={{0,2},{1,3},{2,0},{3,1},{4,6},{5,7},{6,4},{7,5},{8,10},{9,11},{10,... | collective-permute-start | bytes 1105928 | tf_op jit(solution)/shard_map/ppermute | solution.py:461
  44.4 11.9 %collective-permute-start.21 = (bf16[80,2304]{1,0:T(8,128)(2,1)S(1)}, bf16[80,2304]{1,0:T(8,128)(2,1)S(1)}, u32[]{:S(2)}, u32[]{:S(2)}) collective-permute-start(bf16[80,2304]{1,0:T(8,128)(2,1)S(1)} %collective-permute-done.19.rest_5_), channel_id=1, source_target_pairs={{0,8},{4,12},{8,0},{12,4},{16,24},{20,28},{24,16},{28,20},{1,9},{5... | collective-permute-start | bytes 1105928 | tf_op jit(solution)/shard_map/ppermute | solution.py:464
  44.4 12.0 %collective-permute-start.20 = (bf16[80,2304]{1,0:T(8,128)(2,1)S(1)}, bf16[80,2304]{1,0:T(8,128)(2,1)S(1)}, u32[]{:S(2)}, u32[]{:S(2)}) collective-permute-start(bf16[80,2304]{1,0:T(8,128)(2,1)S(1)} %collective-permute-done.19.rest_5_), channel_id=1, source_target_pairs={{0,4},{4,0},{8,12},{12,8},{16,20},{20,16},{24,28},{28,24},{1,5},{5... | collective-permute-start | bytes 1105928 | tf_op jit(solution)/shard_map/ppermute | solution.py:464
  55.8 2.3 %collective-permute-start.23 = (bf16[80,2304]{1,0:T(8,128)(2,1)S(1)}, bf16[80,2304]{1,0:T(8,128)(2,1)S(1)}, u32[]{:S(2)}, u32[]{:S(2)}) collective-permute-start(bf16[80,2304]{1,0:T(8,128)(2,1)S(1)} %collective-permute-done.19.rest_5_), channel_id=1, source_target_pairs={{0,1},{1,0},{2,3},{3,2},{4,5},{5,4},{6,7},{7,6},{8,9},{9,8},{10,11... | collective-permute-start | bytes 1105928 | tf_op jit(solution)/shard_map/ppermute | solution.py:458
  55.9 2.2 %collective-permute-start.26 = (bf16[80,2304]{1,0:T(8,128)(2,1)S(1)}, bf16[80,2304]{1,0:T(8,128)(2,1)S(1)}, u32[]{:S(2)}, u32[]{:S(2)}) collective-permute-start(bf16[80,2304]{1,0:T(8,128)(2,1)S(1)} %collective-permute-done.22.rest_8_), channel_id=1, source_target_pairs={{0,1},{1,0},{2,3},{3,2},{4,5},{5,4},{6,7},{7,6},{8,9},{9,8},{10,11... | collective-permute-start | bytes 1105928 | tf_op jit(solution)/shard_map/ppermute | solution.py:458
  56.4 2.2 %collective-permute-start.25 = (bf16[80,2304]{1,0:T(8,128)(2,1)S(1)}, bf16[80,2304]{1,0:T(8,128)(2,1)S(1)}, u32[]{:S(2)}, u32[]{:S(2)}) collective-permute-start(bf16[80,2304]{1,0:T(8,128)(2,1)S(1)} %collective-permute-done.21.rest_7_), channel_id=1, source_target_pairs={{0,1},{1,0},{2,3},{3,2},{4,5},{5,4},{6,7},{7,6},{8,9},{9,8},{10,11... | collective-permute-start | bytes 1105928 | tf_op jit(solution)/shard_map/ppermute | solution.py:458
  56.4 2.7 %collective-permute-start.24 = (bf16[80,2304]{1,0:T(8,128)(2,1)S(1)}, bf16[80,2304]{1,0:T(8,128)(2,1)S(1)}, u32[]{:S(2)}, u32[]{:S(2)}) collective-permute-start(bf16[80,2304]{1,0:T(8,128)(2,1)S(1)} %collective-permute-done.20.rest_6_), channel_id=1, source_target_pairs={{0,1},{1,0},{2,3},{3,2},{4,5},{5,4},{6,7},{7,6},{8,9},{9,8},{10,11... | collective-permute-start | bytes 1105928 | tf_op jit(solution)/shard_map/ppermute | solution.py:458
  (8 other events, 24.3 us)

commit v8 on v7

--- a/solution.py
+++ b/solution.py
@@ -25,7 +25,6 @@
 ANY = pl.BlockSpec(memory_space=pl.ANY)
 HBM = pl.BlockSpec(memory_space=pltpu.HBM)
 FREE = pl.CostEstimate(flops=0, bytes_accessed=0, transcendentals=0)
-LONG = pl.CostEstimate(flops=2 * 10**10, bytes_accessed=0, transcendentals=0)
 CUT_A = 18 * 128
 CUT_B = 17 * 128
 
@@ -145,9 +144,11 @@
     wait(leaving)
 
 
-def table_kernel(split, own, other, gain, w_all, *rest):
-    *outs, w, full, sem = rest
-    copy = pltpu.make_async_copy(w_all.at[0], w, sem)
+def table_kernel(split, own, other, gain, w_all, table, *rest):
+    *outs, table_out, w, full, sem = rest
+    copies = [pltpu.make_async_copy(table, table_out, sem.at[1])]
+    start(copies)
+    copy = pltpu.make_async_copy(w_all.at[0], w, sem.at[0])
     copy.start()
     wide = own[...] + other[...].astype(F32)
     t = gelu(norm(wide, gain[0:1])).astype(BF)
@@ -161,10 +162,7 @@
         outs[1][...] = full[pl.ds(pl.multiple_of((1 - core) * SLOT, SLOT), SLOT)].astype(BF)
     else:
         outs[0][...] = full[...]
-
-
-def stage_kernel(*refs):
-    wait(chip_copies(*refs))
+    wait(copies)
 
 
 def hot_kernel(span, near, hot5, hot1):
@@ -207,19 +205,17 @@
         in_copies = [pltpu.make_async_copy(w[1], wi, sem.at[2])]
         start(out_copies + in_copies)
     else:
-        chip_out, chip_in = w[:2]
-        parts, near_parts = w[2:6], w[6:10]
+        w_out, w_in, near_out, near_in, table = w[:5]
+        parts, near_parts = w[5:9], w[9:13]
         x, core, y, z = place()
-        n = depth // 4
-        m = 2 * n
+        n = w_out.shape[1]
+        m = w_in.shape[1]
         half = n // 2
-        row = pl.multiple_of(x * 2 * n, 16)
-        out_copies = [
-            pltpu.make_async_copy(chip_out.at[0 : 2 * n], wo.at[pl.ds(row, 2 * n)], sem.at[1]),
-            pltpu.make_async_copy(chip_out.at[2 * n :], wo.at[depth:], sem.at[1]),
-        ]
-        row = pl.multiple_of(x * 2 * m, 16)
-        in_copies = [pltpu.make_async_copy(chip_in, wi.at[pl.ds(row, 2 * m)], sem.at[2])]
+        out_copies, in_copies = [pltpu.make_async_copy(table, wo.at[depth:], sem.at[1])], []
+        for c, o, i in ((core, w_out, w_in), (1 - core, near_out, near_in)):
+            at = 2 * x + c
+            out_copies.append(pltpu.make_async_copy(o.at[0], wo.at[pl.ds(pl.multiple_of(at * n, 16), n)], sem.at[1]))
+            in_copies.append(pltpu.make_async_copy(i.at[1], wi.at[pl.ds(pl.multiple_of(at * m, 16), m)], sem.at[2]))
 
         def far(outs, ins):
             out, into = [], []
@@ -320,38 +316,33 @@
     )
 
 
-def chip_copies(table, w_out, w_in, w_conv, near_out, near_in, near_conv, chip_out, chip_in, chip_conv, sem):
+def head_kernel(ci, w_conv, near_conv, out, wt, sem):
     x, core, _, _ = place()
-    n = w_out.shape[1]
-    m = w_in.shape[1]
+    n = w_conv.shape[1]
     short = HEAD - n
     done = None
     for xx in range(2):
         for cc in range(2):
-            copies = [pltpu.make_async_copy(table, chip_out.at[2 * n :], sem)]
-            for c, o, i, w in ((cc, w_out, w_in, w_conv), (1 - cc, near_out, near_in, near_conv)):
-                copies.append(pltpu.make_async_copy(o.at[0], chip_out.at[c * n : (c + 1) * n], sem))
-                copies.append(pltpu.make_async_copy(i.at[1], chip_in.at[c * m : (c + 1) * m], sem))
+            copies = []
+            for c, w in ((cc, w_conv), (1 - cc, near_conv)):
                 if c == xx:
-                    copies += conv_copies(w.at[1], 0, KERNEL * H, chip_conv, HEAD, short * xx, n, sem)
+                    copies += conv_copies(w.at[1], 0, KERNEL * H, wt, HEAD, short * xx, n, sem)
                 else:
                     part = w.at[1, (n - short) * xx : (n - short) * xx + short]
-                    copies += conv_copies(part, 0, KERNEL * H, chip_conv, HEAD, n * (1 - xx), short, sem)
+                    copies += conv_copies(part, 0, KERNEL * H, wt, HEAD, n * (1 - xx), short, sem)
             done = copies
 
             @pl.when((x == xx) & (core == cc))
             def _():
                 start(copies)
 
-    return done
-
-
-def head_kernel(ci, w_conv, out):
-    x, _, _, _ = place()
     rows = out.shape[0]
     half = 16 * ((rows + 31) // 32)
-    for lo, hi in ((0, half), (half, rows)):
-        out[lo:hi] = dot(windows(ci, lo, hi, x * TAIL, HEAD), w_conv[...])
+    for b, (lo, hi) in enumerate(((0, half), (half, rows))):
+        lhs = windows(ci, lo, hi, x * TAIL, HEAD)
+        if b == 0:
+            wait(done)
+        out[lo:hi] = dot(lhs, wt[...])
 
 
 def last_kernel(split, ci, hid, gain_out, *rest):
@@ -491,9 +482,9 @@
 
     if split:
         far_a = x_swap(parts[0])
-        own = part + core_swap(part)
+        near_out, near_in = core_swap(w_out), core_swap(w_in)
+        own = part + after(core_swap(part), near_out, near_in)
         other = x_swap(own.astype(BF))
-        near_out, near_in = core_swap(w_out), core_swap(w_in)
         ends = codes[rows - REACH :], codes[:REACH]
         low = seq_at % 2 == 0
         even = seq_swap(jnp.where(low, *ends), 1)
@@ -501,7 +492,7 @@
         pairs.append((seqs - 1, 0))
         odd = lax.ppermute(jnp.where(low, *ends[::-1]), "seq", pairs + [(j, i) for i, j in pairs])
         before, behind = jnp.where(low, odd, even), jnp.where(low, even, odd)
-        other = after(other, far_a, near_out, near_in, before, behind)
+        other = after(other, far_a)
     else:
         own = lax.psum(part, "roll")
         other = jnp.zeros((CODES, H), BF)
@@ -510,42 +501,30 @@
         behind = lax.ppermute(codes[:REACH], "seq", [(j, i) for i, j in pairs])
     wide = KERNEL * H
     shapes = [(SLOT, F32), (SLOT, BF)] if split else [(CODES, F32)]
-    taps = pl.pallas_call(
+    *taps, table = pl.pallas_call(
         functools.partial(table_kernel, split),
-        out_shape=[jax.ShapeDtypeStruct((n, wide), t) for n, t in shapes],
-        in_specs=[VMEM, VMEM, VMEM, HBM],
-        out_specs=[VMEM] * len(shapes),
+        out_shape=[jax.ShapeDtypeStruct((n, wide), t) for n, t in shapes]
+        + [jax.ShapeDtypeStruct(table.shape, BF)],
+        in_specs=[VMEM, VMEM, VMEM, HBM, HBM],
+        out_specs=[VMEM] * (len(shapes) + 1),
         scratch_shapes=[
             pltpu.VMEM(conv_w.shape[1:], BF),
             pltpu.VMEM((CODES, wide), F32),
-            pltpu.SemaphoreType.DMA,
+            pltpu.SemaphoreType.DMA((2,)),
         ],
         cost_estimate=FREE,
         compiler_params=params(12),
-    )(own, other, gain_mid, conv_w)
-    if split:
-        near_conv = core_swap(after(conv_w, taps[1]))
+    )(own, other, gain_mid, conv_w, table)
+    if split:
         relay = after(far_a, taps[1])
         parts_a = [far_a] + [seq_swap(relay, b) for b in (1, 2, 3)]
-        sent = (taps[0] + core_swap(taps[1]).astype(F32)).astype(BF)
+        sent = (taps[0] + after(core_swap(taps[1]), before, behind).astype(F32)).astype(BF)
         received = x_swap(sent)
-        far_b = x_swap(after(parts[1], near_conv))
-        chip = pl.pallas_call(
-            stage_kernel,
-            out_shape=[
-                jax.ShapeDtypeStruct(n, BF)
-                for n in ((4 * shard + CODES, width), (8 * shard, H), (KERNEL * HEAD, H))
-            ],
-            in_specs=[ANY] * 7,
-            out_specs=[VMEM] * 3,
-            scratch_shapes=[pltpu.SemaphoreType.DMA],
-            cost_estimate=LONG,
-            compiler_params=params(16),
-        )(after(table, sent), w_out, w_in, conv_w, near_out, near_in, near_conv)
+        far_b = x_swap(after(parts[1], taps[1]))
     spare = jnp.zeros((-(rows + 2 * REACH) % 128,), jnp.int32)
     near = jnp.concatenate([before, codes, behind, spare])[None]
     if split:
-        near = after(near, chip[0])
+        near = after(near, sent)
 
     hot5, hot1 = pl.pallas_call(
         hot_kernel,
@@ -557,13 +536,14 @@
     )(span, near)
 
     if split:
-        received = after(received, hot1, *parts_a)
+        received = after(received, hot1, far_b, *parts_a)
         near_received = core_swap(received)
         near_sent = core_swap(after(sent, received))
         near_a = [core_swap(after(p, received)) for p in parts_a]
         relay = after(far_b, received)
         parts_b = [far_b, seq_swap(relay, 1), seq_swap(relay, 2), x_swap(after(parts[2], received))]
-        weights_a = [sent, received, near_sent, near_received] + list(chip[:2]) + parts_a + near_a
+        weights_a = [sent, received, near_sent, near_received, w_out, w_in, near_out, near_in, table] + parts_a + near_a
+        near_conv = core_swap(after(conv_w, near_received))
     else:
         taps = lax.psum(taps[0], "roll").astype(BF)
         gather = lambda w: lax.all_gather(w, "roll", axis=0, tiled=True)
@@ -583,7 +563,7 @@
             pltpu.VMEM((width, H), BF),
             pltpu.SemaphoreType.DMA((3,)),
         ],
-        cost_estimate=LONG,
+        cost_estimate=FREE,
         compiler_params=params(30),
     )(span, hot5, hot1, gain_out, gain_in, gain_mid, *weights_a)
 
@@ -592,11 +572,12 @@
         head = pl.pallas_call(
             head_kernel,
             out_shape=jax.ShapeDtypeStruct((rows, H), F32),
-            in_specs=[VMEM] * 2,
+            in_specs=[VMEM, HBM, ANY],
             out_specs=VMEM,
-            cost_estimate=LONG,
+            scratch_shapes=[pltpu.VMEM((KERNEL * HEAD, H), BF), pltpu.SemaphoreType.DMA],
+            cost_estimate=FREE,
             compiler_params=params(16),
-        )(ci, chip[2])
+        )(ci, conv_w, near_conv)
         weights_b = [head, conv_w, w_out, near_conv, near_out] + parts_b + near_b
     out = pl.pallas_call(
         functools.partial(last_kernel, split),

time: 64.7 us -> 70.9 us (1.096)
  waiting for transfers between devices: 12 us -> 18.4 us
  Pallas kernels: 24.5 us -> 22.2 us
  starting transfers between devices: 20.5 us -> 22.1 us
  local copies, waits for them, and re-layouts: 4.21 us -> 5.77 us
  other arithmetic: 2.09 us -> 1.16 us
    ppermute x15, waiting for transfers between devices: 1.51 us -> 7.51 us  [core_swap(): return lax.ppermute(x, 'roll', [(i, i ^ 1) for i in range(rolls)])]
    ppermute x6, waiting for transfers between devices: 0.02 us -> 5.66 us  [seq_swap(): return lax.ppermute(x, 'seq', [(i, i ^ bits) for i in range(seqs)])]
    ppermute x5, waiting for transfers between devices: 10.5 us -> 5.27 us  [x_swap(): return lax.ppermute(x, 'roll', [(i, i ^ 2) for i in range(rolls)])]
    pallas_call x1 -> x0, Pallas kernels: 2.13 us -> none  [per_device(): pl.pallas_call(stage_kernel, out_shape=[jax.ShapeDtypeStruct(n, BF) for n...]
    ppermute x5, starting transfers between devices: 5.74 us -> 7.7 us  [x_swap(): return lax.ppermute(x, 'roll', [(i, i ^ 2) for i in range(rolls)])]
    unnamed x26, local copies, waits for them, and re-layouts: 4.13 us -> 5.69 us
    convert_element_type x1, other arithmetic: 0.97 us -> 0.04 us  [per_device(): (taps[0] + after(core_swap(taps[1]), before, behind).astype(F32)).astype(BF)]
  transfers between devices with their start and end apart: 27 -> 27, of which waited for: 6 -> 10; matrix products, arithmetic and copies ran while one was open for 3% -> 2% of each run, Pallas kernels for 27% -> 24%
where the time goes in v8:
time: 70.9 us; the launch traced here: 70.6 us
  Pallas kernels  22.2 us (31%)
  starting transfers between devices  22.1 us (31%)
  waiting for transfers between devices  18.4 us (26%)
  local copies, waits for them, and re-layouts  5.77 us (8%)
  other arithmetic  1.16 us (2%)
  between operations  0.99 us (1%)
    pallas_call x1, Pallas kernels, per_device(): pl.pallas_call(functools.partial(rows_kernel, split), out_shape=(jax.Shap...  10 us
    ppermute x5, starting transfers between devices, x_swap(): return lax.ppermute(x, 'roll', [(i, i ^ 2) for i in range(rolls)])  7.7 us
    ppermute x15, waiting for transfers between devices, core_swap(): return lax.ppermute(x, 'roll', [(i, i ^ 1) for i in range(rolls)])  7.51 us
    ppermute x6, starting transfers between devices, seq_swap(): return lax.ppermute(x, 'seq', [(i, i ^ bits) for i in range(seqs)])  7.48 us
    unnamed x26, local copies, waits for them, and re-layouts  5.69 us
    ppermute x6, waiting for transfers between devices, seq_swap(): return lax.ppermute(x, 'seq', [(i, i ^ bits) for i in range(seqs)])  5.66 us
    ppermute x5, waiting for transfers between devices, x_swap(): return lax.ppermute(x, 'roll', [(i, i ^ 2) for i in range(rolls)])  5.27 us
    pallas_call x1, Pallas kernels, per_device(): pl.pallas_call(functools.partial(last_kernel, split), out_shape=jax.Shape...  5.06 us
  transfers between devices with their start and end apart: 27, of which 10 were waited for; matrix products, arithmetic and copies ran while one was open for 2% of the time, Pallas kernels for 24%

profile of v8, /device:TPU:0, one launch (start us, length us, event | category | flops | bytes accessed | tf_op | source)
XLA Modules:
  0.0 70.6 jit_solution(7123327431624704378)
XLA Ops:
  0.6 3.1 %shard_map.109 = (bf16[64,1280]{1,0:T(8,128)(2,1)}, f32[64,640]{1,0:T(8,128)}, bf16[80,1280]{1,0:T(8,128)(2,1)}, bf16[80,2304]{1,0:T(8,128)(2,1)}, bf16[80,2304]{1,0:T(8,128)(2,1)}) custom-call(f32[30,1280]{1,0:T(8,128)} %embed.1, f32[1280]{0:T(1024)} %brk.1, f32[2,1280]{1,0:T(2,128)} %gain_in.1, bf16[2,320,640]{2,1,0:T(8,128)(2,1)} %rest_5_.1, ...), custom_call_target="tpu_custom_call" | custom-call | tf_op jit(solution)/shard_map/pallas_call | solution.py:465
  4.3 2.6 %collective-permute-start.6 = (bf16[80,1280]{1,0:T(8,128)(2,1)}, bf16[80,1280]{1,0:T(8,128)(2,1)}, u32[]{:S(2)}, u32[]{:S(2)}) collective-permute-start(bf16[80,1280]{1,0:T(8,128)(2,1)} %get-tuple-element.38), channel_id=1, source_target_pairs={{0,2},{1,3},{2,0},{3,1},{4,6},{5,7},{6,4},{7,5},{8,10},{9,11},{10,... | collective-permute-start | bytes 614408 | tf_op jit(solution)/shard_map/ppermute | solution.py:452
  6.9 0.9 %copy-done.3 = bf16[2,160,1280]{2,1,0:T(8,128)(2,1)} copy-done((bf16[2,160,1280]{2,1,0:T(8,128)(2,1)}, bf16[2,160,1280]{2,1,0:T(8,128)(2,1)S(1)}, u32[]{:S(2)}) %copy-start.3) | copy-done | bytes 819224
  7.8 0.9 %fusion.2 = (bf16[64,640]{1,0:T(8,128)(2,1)S(1)}, f32[64,640]{1,0:T(8,128)S(1)}) fusion(f32[64,640]{1,0:T(8,128)} %get-tuple-element.36, f32[64,640]{1,0:T(8,128)S(1)} %collective-permute-done.2), kind=kLoop, calls=%fused_computation.9 | loop fusion | flops 81920 | bytes 573440 | tf_op jit(solution)/shard_map/convert_element_type | solution.py:487
  8.7 1.6 %collective-permute-start.5 = (bf16[64,640]{1,0:T(8,128)(2,1)S(1)}, bf16[64,640]{1,0:T(8,128)(2,1)S(1)}, u32[]{:S(2)}, u32[]{:S(2)}) collective-permute-start(bf16[64,640]{1,0:T(8,128)(2,1)S(1)} %get-tuple-element.69), channel_id=1, source_target_pairs={{0,2},{1,3},{2,0},{3,1},{4,6},{5,7},{6,4},{7,5},{8,10},{9,11},{10,... | collective-permute-start | bytes 245768 | tf_op jit(solution)/shard_map/ppermute | solution.py:452
  10.4 1.6 %collective-permute-start.1 = (s32[384]{0:T(512)S(1)}, s32[384]{0:T(512)S(1)}, u32[]{:S(2)}, u32[]{:S(2)}) collective-permute-start(s32[384]{0:T(512)S(1)} %get-tuple-element.67), channel_id=1, source_target_pairs={{0,4},{4,0},{8,12},{12,8},{16,20},{20,16},{24,28},{28,24},{1,5},{5... | collective-permute-start | bytes 4616 | tf_op jit(solution)/shard_map/ppermute | solution.py:455
  12.0 3.5 %collective-permute-start = (s32[384]{0:T(512)S(1)}, s32[384]{0:T(512)S(1)}, u32[]{:S(2)}, u32[]{:S(2)}) collective-permute-start(s32[384]{0:T(512)S(1)} %get-tuple-element.68), channel_id=1, source_target_pairs={{4,8},{12,16},{20,24},{28,0},{8,4},{16,12},{24,20},{0,28},{5,9},{1... | collective-permute-start | bytes 4616 | tf_op jit(solution)/shard_map/ppermute | solution.py:493
  15.5 0.9 %copy-done.7 = bf16[64,1280]{1,0:T(8,128)(2,1)S(1)} copy-done((bf16[64,1280]{1,0:T(8,128)(2,1)S(1)}, bf16[64,1280]{1,0:T(8,128)(2,1)}, u32[]{:S(2)}) %copy-start.7) | copy-done | bytes 163864
  16.4 1.4 %shard_map.110 = (f32[32,3200]{1,0:T(8,128)S(1)}, bf16[32,3200]{1,0:T(8,128)(2,1)S(1)}, bf16[64,1280]{1,0:T(8,128)(2,1)S(1)}) custom-call(f32[64,640]{1,0:T(8,128)S(1)} %get-tuple-element.70.own, bf16[64,640]{1,0:T(8,128)(2,1)S(1)} %collective-permute-done.5.other, f32[2,640]{1,0:T(2,128)S(1)} %copy-done.9, bf16[2,160,3200]{2,1,0:T(8,128)(2,1)S(1)} %copy-done, ...), custom_call_target="tpu_custom_call" | custom-call | tf_op jit(solution)/shard_map/pallas_call | solution.py:504
  17.8 0.7 copy-done.5
  18.5 1.8 %collective-permute-start.12 = (bf16[80,1280]{1,0:T(8,128)(2,1)}, bf16[80,1280]{1,0:T(8,128)(2,1)}, u32[]{:S(2)}, u32[]{:S(2)}) collective-permute-start(bf16[80,1280]{1,0:T(8,128)(2,1)} %collective-permute-done.6.rest_9_), channel_id=1, source_target_pairs={{0,12},{4,8},{8,4},{12,0},{16,28},{20,24},{24,20},{28,16},{1,13},{... | collective-permute-start | bytes 614408 | tf_op jit(solution)/shard_map/ppermute | solution.py:455
  20.8 1.3 %collective-permute-start.10 = (bf16[80,1280]{1,0:T(8,128)(2,1)}, bf16[80,1280]{1,0:T(8,128)(2,1)}, u32[]{:S(2)}, u32[]{:S(2)}) collective-permute-start(bf16[80,1280]{1,0:T(8,128)(2,1)} %collective-permute-done.6.rest_9_), channel_id=1, source_target_pairs={{0,4},{4,0},{8,12},{12,8},{16,20},{20,16},{24,28},{28,24},{1,5},{5... | collective-permute-start | bytes 614408 | tf_op jit(solution)/shard_map/ppermute | solution.py:455
  22.1 0.7 %collective-permute-start.9 = (bf16[80,2304]{1,0:T(8,128)(2,1)}, bf16[80,2304]{1,0:T(8,128)(2,1)S(1)}, u32[]{:S(2)}, u32[]{:S(2)}) collective-permute-start(bf16[80,2304]{1,0:T(8,128)(2,1)} %get-tuple-element.48), channel_id=1, source_target_pairs={{0,2},{1,3},{2,0},{3,1},{4,6},{5,7},{6,4},{7,5},{8,10},{9,11},{10,... | collective-permute-start | bytes 1105928 | tf_op jit(solution)/shard_map/ppermute | solution.py:452
  22.8 1.4 %collective-permute-start.8 = (bf16[32,3200]{1,0:T(8,128)(2,1)S(1)}, bf16[32,3200]{1,0:T(8,128)(2,1)}, u32[]{:S(2)}, u32[]{:S(2)}) collective-permute-start(bf16[32,3200]{1,0:T(8,128)(2,1)S(1)} %add_convert_fusion.rest_0_), channel_id=1, source_target_pairs={{0,2},{1,3},{2,0},{3,1},{4,6},{5,7},{6,4},{7,5},{8,10},{9,11},{10,... | collective-permute-start | bytes 614408 | tf_op jit(solution)/shard_map/ppermute | solution.py:452
  25.0 1.0 %shard_map.111 = (bf16[1008,320]{1,0:T(8,128)(2,1)S(1)}, bf16[1008,64]{1,0:T(8,128)(2,1)S(1)}) custom-call(s32[2]{0:T(128)S(1)} %pad_add_fusion.span, s32[1,1280]{1,0:T(1,128)S(1)} %broadcast_in_dim.6.near), custom_call_target="tpu_custom_call" | custom-call | tf_op jit(solution)/shard_map/pallas_call | solution.py:529
  26.0 1.7 %collective-permute-done.12.rest_12_ = bf16[80,1280]{1,0:T(8,128)(2,1)} collective-permute-done((bf16[80,1280]{1,0:T(8,128)(2,1)}, bf16[80,1280]{1,0:T(8,128)(2,1)}, u32[]{:S(2)}, u32[]{:S(2)}) %collective-permute-start.12) | collective-permute-done | bytes 204832 | tf_op jit(solution)/shard_map/ppermute | solution.py:455
  27.7 3.3 %collective-permute-done.11.rest_11_ = bf16[80,1280]{1,0:T(8,128)(2,1)} collective-permute-done((bf16[80,1280]{1,0:T(8,128)(2,1)}, bf16[80,1280]{1,0:T(8,128)(2,1)}, u32[]{:S(2)}, u32[]{:S(2)}) %collective-permute-start.11) | collective-permute-done | bytes 204832 | tf_op jit(solution)/shard_map/ppermute | solution.py:455
  31.0 0.7 collective-permute-done.10.rest_10_
  31.7 2.1 %collective-permute-done.9.rest_5_ = bf16[80,2304]{1,0:T(8,128)(2,1)S(1)} collective-permute-done((bf16[80,2304]{1,0:T(8,128)(2,1)}, bf16[80,2304]{1,0:T(8,128)(2,1)S(1)}, u32[]{:S(2)}, u32[]{:S(2)}) %collective-permute-start.9) | collective-permute-done | bytes 368672 | tf_op jit(solution)/shard_map/ppermute | solution.py:452
  33.8 3.1 %collective-permute-done.8.rest_1_ = bf16[32,3200]{1,0:T(8,128)(2,1)} collective-permute-done((bf16[32,3200]{1,0:T(8,128)(2,1)S(1)}, bf16[32,3200]{1,0:T(8,128)(2,1)}, u32[]{:S(2)}, u32[]{:S(2)}) %collective-permute-start.8) | collective-permute-done | bytes 204832 | tf_op jit(solution)/shard_map/ppermute | solution.py:452
  36.9 1.7 %collective-permute-done.14.rest_3_ = bf16[32,3200]{1,0:T(8,128)(2,1)S(1)} collective-permute-done((bf16[32,3200]{1,0:T(8,128)(2,1)}, bf16[32,3200]{1,0:T(8,128)(2,1)S(1)}, u32[]{:S(2)}, u32[]{:S(2)}) %collective-permute-start.14) | collective-permute-done | bytes 204832 | tf_op jit(solution)/shard_map/ppermute | solution.py:449
  39.8 3.5 %collective-permute-done.13.rest_2_ = bf16[32,3200]{1,0:T(8,128)(2,1)S(1)} collective-permute-done((bf16[32,3200]{1,0:T(8,128)(2,1)S(1)}, bf16[32,3200]{1,0:T(8,128)(2,1)S(1)}, u32[]{:S(2)}, u32[]{:S(2)}) %collective-permute-start.13) | collective-permute-done | bytes 204832 | tf_op jit(solution)/shard_map/ppermute | solution.py:449
  43.3 0.8 %collective-permute-start.21 = (bf16[80,2304]{1,0:T(8,128)(2,1)S(1)}, bf16[80,2304]{1,0:T(8,128)(2,1)S(1)}, u32[]{:S(2)}, u32[]{:S(2)}) collective-permute-start(bf16[80,2304]{1,0:T(8,128)(2,1)S(1)} %collective-permute-done.9.rest_5_), channel_id=1, source_target_pairs={{0,8},{4,12},{8,0},{12,4},{16,24},{20,28},{24,16},{28,20},{1,9},{5... | collective-permute-start | bytes 1105928 | tf_op jit(solution)/shard_map/ppermute | solution.py:455
  44.1 1.5 %collective-permute-start.20 = (bf16[80,2304]{1,0:T(8,128)(2,1)S(1)}, bf16[80,2304]{1,0:T(8,128)(2,1)S(1)}, u32[]{:S(2)}, u32[]{:S(2)}) collective-permute-start(bf16[80,2304]{1,0:T(8,128)(2,1)S(1)} %collective-permute-done.9.rest_5_), channel_id=1, source_target_pairs={{0,4},{4,0},{8,12},{12,8},{16,20},{20,16},{24,28},{28,24},{1,5},{5... | collective-permute-start | bytes 1105928 | tf_op jit(solution)/shard_map/ppermute | solution.py:455
  45.6 1.5 %collective-permute-start.22 = (bf16[80,2304]{1,0:T(8,128)(2,1)}, bf16[80,2304]{1,0:T(8,128)(2,1)S(1)}, u32[]{:S(2)}, u32[]{:S(2)}) collective-permute-start(bf16[80,2304]{1,0:T(8,128)(2,1)} %get-tuple-element.62), channel_id=1, source_target_pairs={{0,2},{1,3},{2,0},{3,1},{4,6},{5,7},{6,4},{7,5},{8,10},{9,11},{10,... | collective-permute-start | bytes 1105928 | tf_op jit(solution)/shard_map/ppermute | solution.py:452
  47.1 1.7 %collective-permute-done.18.rest_16_ = bf16[80,1280]{1,0:T(8,128)(2,1)S(1)} collective-permute-done((bf16[80,1280]{1,0:T(8,128)(2,1)}, bf16[80,1280]{1,0:T(8,128)(2,1)S(1)}, u32[]{:S(2)}, u32[]{:S(2)}) %collective-permute-start.18) | collective-permute-done | bytes 204832 | tf_op jit(solution)/shard_map/ppermute | solution.py:449
  48.8 1.1 %copy-done.2 = bf16[2,320,640]{2,1,0:T(8,128)(2,1)S(1)} copy-done((bf16[2,320,640]{2,1,0:T(8,128)(2,1)S(1)}, bf16[2,320,640]{2,1,0:T(8,128)(2,1)}, u32[]{:S(2)}) %copy-start.2) | copy-done | bytes 819224
  49.9 1.1 %copy-done.4 = bf16[2,160,1280]{2,1,0:T(8,128)(2,1)S(1)} copy-done((bf16[2,160,1280]{2,1,0:T(8,128)(2,1)S(1)}, bf16[2,160,1280]{2,1,0:T(8,128)(2,1)}, u32[]{:S(2)}) %copy-start.4) | copy-done | bytes 819224
  51.1 0.9 %copy-done.6 = bf16[64,1280]{1,0:T(8,128)(2,1)S(1)} copy-done((bf16[64,1280]{1,0:T(8,128)(2,1)S(1)}, bf16[64,1280]{1,0:T(8,128)(2,1)}, u32[]{:S(2)}) %copy-start.6) | copy-done | bytes 163864
  52.0 10.0 %shard_map.112 = (bf16[1008,640]{1,0:T(8,128)(2,1)S(1)}, bf16[496,1280]{1,0:T(8,128)(2,1)S(1)}) custom-call(s32[2]{0:T(128)S(1)} %pad_add_fusion.span, bf16[1008,320]{1,0:T(8,128)(2,1)S(1)} %get-tuple-element.45.hot5, bf16[1008,64]{1,0:T(8,128)(2,1)S(1)} %get-tuple-element.46.hot1, f32[2,640]{1,0:T(2,128)S(1)} %copy-done.10, f32[2,1280]{1,0:T(2,128)S(1)} %copy-done.8, ...), custom_call_target="tpu_custom_call" | custom-call | tf_op jit(solution)/shard_map/pallas_call | solution.py:552
  63.2 1.6 %shard_map.113.rest_0_ = f32[496,640]{1,0:T(8,128)S(1)} custom-call(bf16[1008,640]{1,0:T(8,128)(2,1)S(1)} %get-tuple-element.57.ci, bf16[2,160,3200]{2,1,0:T(8,128)(2,1)S(1)} %copy-done, bf16[2,160,3200]{2,1,0:T(8,128)(2,1)S(1)} %collective-permute-done.19.near_conv.rest_3_), custom_call_target="tpu_custom_call" | custom-call | tf_op jit(solution)/shard_map/pallas_call | solution.py:572
  65.4 5.1 %shard_map.114 = bf16[496,1280]{1,0:T(8,128)(2,1)} custom-call(bf16[1008,640]{1,0:T(8,128)(2,1)S(1)} %get-tuple-element.57.ci, bf16[496,1280]{1,0:T(8,128)(2,1)S(1)} %get-tuple-element.58.hid, f32[2,640]{1,0:T(2,128)S(1)} %copy-done.10, f32[496,640]{1,0:T(8,128)S(1)} %shard_map.113.rest_0_, bf16[2,160,3200]{2,1,0:T(8,128)(2,1)S(1)} %copy-done, ...), custom_call_target="tpu_custom_call" | custom-call | tf_op jit(solution)/shard_map/pallas_call | solution.py:582
  (63 shorter events, 4.9 us)
Async XLA Ops:
  0.0 15.5 %copy-start = (bf16[2,160,3200]{2,1,0:T(8,128)(2,1)S(1)}, bf16[2,160,3200]{2,1,0:T(8,128)(2,1)}, u32[]{:S(2)}) copy-start(bf16[2,160,3200]{2,1,0:T(8,128)(2,1)} %rest_1_.1) | copy-start | bytes 6144004
  0.0 15.5 %copy-start.9 = (f32[2,640]{1,0:T(2,128)S(1)}, f32[2,640]{1,0:T(2,128)}, u32[]{:S(2)}) copy-start(f32[2,640]{1,0:T(2,128)} %gain_mid.1) | copy-start | bytes 15364
  0.0 6.9 %collective-permute-start.4 = (bf16[2,320,640]{2,1,0:T(8,128)(2,1)}, bf16[2,320,640]{2,1,0:T(8,128)(2,1)}, u32[]{:S(2)}, u32[]{:S(2)}) collective-permute-start(bf16[2,320,640]{2,1,0:T(8,128)(2,1)} %rest_5_.1), channel_id=1, source_target_pairs={{0,1},{1,0},{2,3},{3,2},{4,5},{5,4},{6,7},{7,6},{8,9},{9,8},{10,11... | collective-permute-start | bytes 2457608 | tf_op jit(solution)/shard_map/ppermute | solution.py:449
  0.5 6.3 %collective-permute-start.3 = (bf16[2,160,1280]{2,1,0:T(8,128)(2,1)}, bf16[2,160,1280]{2,1,0:T(8,128)(2,1)S(1)}, u32[]{:S(2)}, u32[]{:S(2)}) collective-permute-start(bf16[2,160,1280]{2,1,0:T(8,128)(2,1)} %rest_2_.1), channel_id=1, source_target_pairs={{0,1},{1,0},{2,3},{3,2},{4,5},{5,4},{6,7},{7,6},{8,9},{9,8},{10,11... | collective-permute-start | bytes 2457608 | tf_op jit(solution)/shard_map/ppermute | solution.py:449
  3.8 3.1 %collective-permute-start.2 = (f32[64,640]{1,0:T(8,128)}, f32[64,640]{1,0:T(8,128)S(1)}, u32[]{:S(2)}, u32[]{:S(2)}) collective-permute-start(f32[64,640]{1,0:T(8,128)} %get-tuple-element.36), channel_id=1, source_target_pairs={{0,1},{1,0},{2,3},{3,2},{4,5},{5,4},{6,7},{7,6},{8,9},{9,8},{10,11... | collective-permute-start | bytes 491528 | tf_op jit(solution)/shard_map/ppermute | solution.py:449
  4.3 11.2 %collective-permute-start.6 = (bf16[80,1280]{1,0:T(8,128)(2,1)}, bf16[80,1280]{1,0:T(8,128)(2,1)}, u32[]{:S(2)}, u32[]{:S(2)}) collective-permute-start(bf16[80,1280]{1,0:T(8,128)(2,1)} %get-tuple-element.38), channel_id=1, source_target_pairs={{0,2},{1,3},{2,0},{3,1},{4,6},{5,7},{6,4},{7,5},{8,10},{9,11},{10,... | collective-permute-start | bytes 614408 | tf_op jit(solution)/shard_map/ppermute | solution.py:452
  8.7 6.8 %collective-permute-start.5 = (bf16[64,640]{1,0:T(8,128)(2,1)S(1)}, bf16[64,640]{1,0:T(8,128)(2,1)S(1)}, u32[]{:S(2)}, u32[]{:S(2)}) collective-permute-start(bf16[64,640]{1,0:T(8,128)(2,1)S(1)} %get-tuple-element.69), channel_id=1, source_target_pairs={{0,2},{1,3},{2,0},{3,1},{4,6},{5,7},{6,4},{7,5},{8,10},{9,11},{10,... | collective-permute-start | bytes 245768 | tf_op jit(solution)/shard_map/ppermute | solution.py:452
  10.4 8.1 %collective-permute-start.1 = (s32[384]{0:T(512)S(1)}, s32[384]{0:T(512)S(1)}, u32[]{:S(2)}, u32[]{:S(2)}) collective-permute-start(s32[384]{0:T(512)S(1)} %get-tuple-element.67), channel_id=1, source_target_pairs={{0,4},{4,0},{8,12},{12,8},{16,20},{20,16},{24,28},{28,24},{1,5},{5... | collective-permute-start | bytes 4616 | tf_op jit(solution)/shard_map/ppermute | solution.py:455
  12.0 6.6 %collective-permute-start = (s32[384]{0:T(512)S(1)}, s32[384]{0:T(512)S(1)}, u32[]{:S(2)}, u32[]{:S(2)}) collective-permute-start(s32[384]{0:T(512)S(1)} %get-tuple-element.68), channel_id=1, source_target_pairs={{4,8},{12,16},{20,24},{28,0},{8,4},{16,12},{24,20},{0,28},{5,9},{1... | collective-permute-start | bytes 4616 | tf_op jit(solution)/shard_map/ppermute | solution.py:493
  16.4 32.4 %copy-start.1 = (bf16[2,160,1280]{2,1,0:T(8,128)(2,1)S(1)}, bf16[2,160,1280]{2,1,0:T(8,128)(2,1)}, u32[]{:S(2)}) copy-start(bf16[2,160,1280]{2,1,0:T(8,128)(2,1)} %rest_2_.1) | copy-start | bytes 2457604
  16.4 32.4 %copy-start.8 = (f32[2,1280]{1,0:T(2,128)S(1)}, f32[2,1280]{1,0:T(2,128)}, u32[]{:S(2)}) copy-start(f32[2,1280]{1,0:T(2,128)} %gain_in.1) | copy-start | bytes 30724
  16.4 32.4 %copy-start.10 = (f32[2,640]{1,0:T(2,128)S(1)}, f32[2,640]{1,0:T(2,128)}, u32[]{:S(2)}) copy-start(f32[2,640]{1,0:T(2,128)} %gain_out.3) | copy-start | bytes 15364
  18.5 4.3 %collective-permute-start.7 = (bf16[32,3200]{1,0:T(8,128)(2,1)S(1)}, bf16[32,3200]{1,0:T(8,128)(2,1)S(1)}, u32[]{:S(2)}, u32[]{:S(2)}) collective-permute-start(bf16[32,3200]{1,0:T(8,128)(2,1)S(1)} %get-tuple-element.42), channel_id=1, source_target_pairs={{0,1},{1,0},{2,3},{3,2},{4,5},{5,4},{6,7},{7,6},{8,9},{9,8},{10,11... | collective-permute-start | bytes 614408 | tf_op jit(solution)/shard_map/ppermute | solution.py:449
  18.5 9.2 %collective-permute-start.12 = (bf16[80,1280]{1,0:T(8,128)(2,1)}, bf16[80,1280]{1,0:T(8,128)(2,1)}, u32[]{:S(2)}, u32[]{:S(2)}) collective-permute-start(bf16[80,1280]{1,0:T(8,128)(2,1)} %collective-permute-done.6.rest_9_), channel_id=1, source_target_pairs={{0,12},{4,8},{8,4},{12,0},{16,28},{20,24},{24,20},{28,16},{1,13},{... | collective-permute-start | bytes 614408 | tf_op jit(solution)/shard_map/ppermute | solution.py:455
  20.4 10.7 %collective-permute-start.11 = (bf16[80,1280]{1,0:T(8,128)(2,1)}, bf16[80,1280]{1,0:T(8,128)(2,1)}, u32[]{:S(2)}, u32[]{:S(2)}) collective-permute-start(bf16[80,1280]{1,0:T(8,128)(2,1)} %collective-permute-done.6.rest_9_), channel_id=1, source_target_pairs={{0,8},{4,12},{8,0},{12,4},{16,24},{20,28},{24,16},{28,20},{1,9},{5... | collective-permute-start | bytes 614408 | tf_op jit(solution)/shard_map/ppermute | solution.py:455
  20.8 10.9 %collective-permute-start.10 = (bf16[80,1280]{1,0:T(8,128)(2,1)}, bf16[80,1280]{1,0:T(8,128)(2,1)}, u32[]{:S(2)}, u32[]{:S(2)}) collective-permute-start(bf16[80,1280]{1,0:T(8,128)(2,1)} %collective-permute-done.6.rest_9_), channel_id=1, source_target_pairs={{0,4},{4,0},{8,12},{12,8},{16,20},{20,16},{24,28},{28,24},{1,5},{5... | collective-permute-start | bytes 614408 | tf_op jit(solution)/shard_map/ppermute | solution.py:455
  22.1 11.7 %collective-permute-start.9 = (bf16[80,2304]{1,0:T(8,128)(2,1)}, bf16[80,2304]{1,0:T(8,128)(2,1)S(1)}, u32[]{:S(2)}, u32[]{:S(2)}) collective-permute-start(bf16[80,2304]{1,0:T(8,128)(2,1)} %get-tuple-element.48), channel_id=1, source_target_pairs={{0,2},{1,3},{2,0},{3,1},{4,6},{5,7},{6,4},{7,5},{8,10},{9,11},{10,... | collective-permute-start | bytes 1105928 | tf_op jit(solution)/shard_map/ppermute | solution.py:452
  22.8 14.1 %collective-permute-start.8 = (bf16[32,3200]{1,0:T(8,128)(2,1)S(1)}, bf16[32,3200]{1,0:T(8,128)(2,1)}, u32[]{:S(2)}, u32[]{:S(2)}) collective-permute-start(bf16[32,3200]{1,0:T(8,128)(2,1)S(1)} %add_convert_fusion.rest_0_), channel_id=1, source_target_pairs={{0,2},{1,3},{2,0},{3,1},{4,6},{5,7},{6,4},{7,5},{8,10},{9,11},{10,... | collective-permute-start | bytes 614408 | tf_op jit(solution)/shard_map/ppermute | solution.py:452
  36.9 1.7 %collective-permute-start.14 = (bf16[32,3200]{1,0:T(8,128)(2,1)}, bf16[32,3200]{1,0:T(8,128)(2,1)S(1)}, u32[]{:S(2)}, u32[]{:S(2)}) collective-permute-start(bf16[32,3200]{1,0:T(8,128)(2,1)} %collective-permute-done.8.rest_1_), channel_id=1, source_target_pairs={{0,1},{1,0},{2,3},{3,2},{4,5},{5,4},{6,7},{7,6},{8,9},{9,8},{10,11... | collective-permute-start | bytes 614408 | tf_op jit(solution)/shard_map/ppermute | solution.py:449
  38.6 24.6 %collective-permute-start.19 = (bf16[2,160,3200]{2,1,0:T(8,128)(2,1)S(1)}, bf16[2,160,3200]{2,1,0:T(8,128)(2,1)S(1)}, u32[]{:S(2)}, u32[]{:S(2)}) collective-permute-start(bf16[2,160,3200]{2,1,0:T(8,128)(2,1)S(1)} %copy-done), channel_id=1, source_target_pairs={{0,1},{1,0},{2,3},{3,2},{4,5},{5,4},{6,7},{7,6},{8,9},{9,8},{10,11... | collective-permute-start | bytes 6144008 | tf_op jit(solution)/shard_map/ppermute | solution.py:449
  38.7 4.5 %collective-permute-start.13 = (bf16[32,3200]{1,0:T(8,128)(2,1)S(1)}, bf16[32,3200]{1,0:T(8,128)(2,1)S(1)}, u32[]{:S(2)}, u32[]{:S(2)}) collective-permute-start(bf16[32,3200]{1,0:T(8,128)(2,1)S(1)} %add_convert_fusion.rest_0_), channel_id=1, source_target_pairs={{0,1},{1,0},{2,3},{3,2},{4,5},{5,4},{6,7},{7,6},{8,9},{9,8},{10,11... | collective-permute-start | bytes 614408 | tf_op jit(solution)/shard_map/ppermute | solution.py:449
  39.1 5.0 %collective-permute-start.15 = (bf16[80,1280]{1,0:T(8,128)(2,1)}, bf16[80,1280]{1,0:T(8,128)(2,1)S(1)}, u32[]{:S(2)}, u32[]{:S(2)}) collective-permute-start(bf16[80,1280]{1,0:T(8,128)(2,1)} %collective-permute-done.6.rest_9_), channel_id=1, source_target_pairs={{0,1},{1,0},{2,3},{3,2},{4,5},{5,4},{6,7},{7,6},{8,9},{9,8},{10,11... | collective-permute-start | bytes 614408 | tf_op jit(solution)/shard_map/ppermute | solution.py:449
  39.3 6.4 %collective-permute-start.16 = (bf16[80,1280]{1,0:T(8,128)(2,1)}, bf16[80,1280]{1,0:T(8,128)(2,1)S(1)}, u32[]{:S(2)}, u32[]{:S(2)}) collective-permute-start(bf16[80,1280]{1,0:T(8,128)(2,1)} %collective-permute-done.10.rest_10_), channel_id=1, source_target_pairs={{0,1},{1,0},{2,3},{3,2},{4,5},{5,4},{6,7},{7,6},{8,9},{9,8},{10,11... | collective-permute-start | bytes 614408 | tf_op jit(solution)/shard_map/ppermute | solution.py:449
  39.6 7.5 %collective-permute-start.17 = (bf16[80,1280]{1,0:T(8,128)(2,1)}, bf16[80,1280]{1,0:T(8,128)(2,1)S(1)}, u32[]{:S(2)}, u32[]{:S(2)}) collective-permute-start(bf16[80,1280]{1,0:T(8,128)(2,1)} %collective-permute-done.11.rest_11_), channel_id=1, source_target_pairs={{0,1},{1,0},{2,3},{3,2},{4,5},{5,4},{6,7},{7,6},{8,9},{9,8},{10,11... | collective-permute-start | bytes 614408 | tf_op jit(solution)/shard_map/ppermute | solution.py:449
  43.3 19.0 %collective-permute-start.21 = (bf16[80,2304]{1,0:T(8,128)(2,1)S(1)}, bf16[80,2304]{1,0:T(8,128)(2,1)S(1)}, u32[]{:S(2)}, u32[]{:S(2)}) collective-permute-start(bf16[80,2304]{1,0:T(8,128)(2,1)S(1)} %collective-permute-done.9.rest_5_), channel_id=1, source_target_pairs={{0,8},{4,12},{8,0},{12,4},{16,24},{20,28},{24,16},{28,20},{1,9},{5... | collective-permute-start | bytes 1105928 | tf_op jit(solution)/shard_map/ppermute | solution.py:455
  44.1 18.6 %collective-permute-start.20 = (bf16[80,2304]{1,0:T(8,128)(2,1)S(1)}, bf16[80,2304]{1,0:T(8,128)(2,1)S(1)}, u32[]{:S(2)}, u32[]{:S(2)}) collective-permute-start(bf16[80,2304]{1,0:T(8,128)(2,1)S(1)} %collective-permute-done.9.rest_5_), channel_id=1, source_target_pairs={{0,4},{4,0},{8,12},{12,8},{16,20},{20,16},{24,28},{28,24},{1,5},{5... | collective-permute-start | bytes 1105928 | tf_op jit(solution)/shard_map/ppermute | solution.py:455
  45.6 17.2 %collective-permute-start.22 = (bf16[80,2304]{1,0:T(8,128)(2,1)}, bf16[80,2304]{1,0:T(8,128)(2,1)S(1)}, u32[]{:S(2)}, u32[]{:S(2)}) collective-permute-start(bf16[80,2304]{1,0:T(8,128)(2,1)} %get-tuple-element.62), channel_id=1, source_target_pairs={{0,2},{1,3},{2,0},{3,1},{4,6},{5,7},{6,4},{7,5},{8,10},{9,11},{10,... | collective-permute-start | bytes 1105928 | tf_op jit(solution)/shard_map/ppermute | solution.py:452
  47.1 1.7 %collective-permute-start.18 = (bf16[80,1280]{1,0:T(8,128)(2,1)}, bf16[80,1280]{1,0:T(8,128)(2,1)S(1)}, u32[]{:S(2)}, u32[]{:S(2)}) collective-permute-start(bf16[80,1280]{1,0:T(8,128)(2,1)} %collective-permute-done.12.rest_12_), channel_id=1, source_target_pairs={{0,1},{1,0},{2,3},{3,2},{4,5},{5,4},{6,7},{7,6},{8,9},{9,8},{10,11... | collective-permute-start | bytes 614408 | tf_op jit(solution)/shard_map/ppermute | solution.py:449
  62.1 2.7 %collective-permute-start.23 = (bf16[80,2304]{1,0:T(8,128)(2,1)S(1)}, bf16[80,2304]{1,0:T(8,128)(2,1)S(1)}, u32[]{:S(2)}, u32[]{:S(2)}) collective-permute-start(bf16[80,2304]{1,0:T(8,128)(2,1)S(1)} %collective-permute-done.9.rest_5_), channel_id=1, source_target_pairs={{0,1},{1,0},{2,3},{3,2},{4,5},{5,4},{6,7},{7,6},{8,9},{9,8},{10,11... | collective-permute-start | bytes 1105928 | tf_op jit(solution)/shard_map/ppermute | solution.py:449
  62.3 2.5 %collective-permute-start.25 = (bf16[80,2304]{1,0:T(8,128)(2,1)S(1)}, bf16[80,2304]{1,0:T(8,128)(2,1)S(1)}, u32[]{:S(2)}, u32[]{:S(2)}) collective-permute-start(bf16[80,2304]{1,0:T(8,128)(2,1)S(1)} %collective-permute-done.21.rest_7_), channel_id=1, source_target_pairs={{0,1},{1,0},{2,3},{3,2},{4,5},{5,4},{6,7},{7,6},{8,9},{9,8},{10,11... | collective-permute-start | bytes 1105928 | tf_op jit(solution)/shard_map/ppermute | solution.py:449
  62.6 2.2 %collective-permute-start.24 = (bf16[80,2304]{1,0:T(8,128)(2,1)S(1)}, bf16[80,2304]{1,0:T(8,128)(2,1)S(1)}, u32[]{:S(2)}, u32[]{:S(2)}) collective-permute-start(bf16[80,2304]{1,0:T(8,128)(2,1)S(1)} %collective-permute-done.20.rest_6_), channel_id=1, source_target_pairs={{0,1},{1,0},{2,3},{3,2},{4,5},{5,4},{6,7},{7,6},{8,9},{9,8},{10,11... | collective-permute-start | bytes 1105928 | tf_op jit(solution)/shard_map/ppermute | solution.py:449
  62.8 2.6 %collective-permute-start.26 = (bf16[80,2304]{1,0:T(8,128)(2,1)S(1)}, bf16[80,2304]{1,0:T(8,128)(2,1)S(1)}, u32[]{:S(2)}, u32[]{:S(2)}) collective-permute-start(bf16[80,2304]{1,0:T(8,128)(2,1)S(1)} %collective-permute-done.22.rest_8_), channel_id=1, source_target_pairs={{0,1},{1,0},{2,3},{3,2},{4,5},{5,4},{6,7},{7,6},{8,9},{9,8},{10,11... | collective-permute-start | bytes 1105928 | tf_op jit(solution)/shard_map/ppermute | solution.py:449
  (8 other events, 19.4 us)

commit v9 on v8

--- a/solution.py
+++ b/solution.py
@@ -144,11 +144,9 @@
     wait(leaving)
 
 
-def table_kernel(split, own, other, gain, w_all, table, *rest):
-    *outs, table_out, w, full, sem = rest
-    copies = [pltpu.make_async_copy(table, table_out, sem.at[1])]
-    start(copies)
-    copy = pltpu.make_async_copy(w_all.at[0], w, sem.at[0])
+def table_kernel(split, own, other, gain, w_all, *rest):
+    *outs, w, full, sem = rest
+    copy = pltpu.make_async_copy(w_all.at[0], w, sem)
     copy.start()
     wide = own[...] + other[...].astype(F32)
     t = gelu(norm(wide, gain[0:1])).astype(BF)
@@ -162,6 +160,16 @@
         outs[1][...] = full[pl.ds(pl.multiple_of((1 - core) * SLOT, SLOT), SLOT)].astype(BF)
     else:
         outs[0][...] = full[...]
+
+
+def stage_kernel(table, w_out, w_in, near_out, near_in, chip_out, chip_in, sem):
+    _, core, _, _ = place()
+    n, m = w_out.shape[1], w_in.shape[1]
+    copies = [pltpu.make_async_copy(table, chip_out.at[2 * n :], sem)]
+    for c, o, i in ((core, w_out, w_in), (1 - core, near_out, near_in)):
+        copies.append(pltpu.make_async_copy(o.at[0], chip_out.at[pl.ds(pl.multiple_of(c * n, 16), n)], sem))
+        copies.append(pltpu.make_async_copy(i.at[1], chip_in.at[pl.ds(pl.multiple_of(c * m, 16), m)], sem))
+    start(copies)
     wait(copies)
 
 
@@ -205,17 +213,19 @@
         in_copies = [pltpu.make_async_copy(w[1], wi, sem.at[2])]
         start(out_copies + in_copies)
     else:
-        w_out, w_in, near_out, near_in, table = w[:5]
-        parts, near_parts = w[5:9], w[9:13]
+        chip_out, chip_in = w[:2]
+        parts, near_parts = w[2:6], w[6:10]
         x, core, y, z = place()
-        n = w_out.shape[1]
-        m = w_in.shape[1]
+        n = depth // 4
+        m = 2 * n
         half = n // 2
-        out_copies, in_copies = [pltpu.make_async_copy(table, wo.at[depth:], sem.at[1])], []
-        for c, o, i in ((core, w_out, w_in), (1 - core, near_out, near_in)):
-            at = 2 * x + c
-            out_copies.append(pltpu.make_async_copy(o.at[0], wo.at[pl.ds(pl.multiple_of(at * n, 16), n)], sem.at[1]))
-            in_copies.append(pltpu.make_async_copy(i.at[1], wi.at[pl.ds(pl.multiple_of(at * m, 16), m)], sem.at[2]))
+        row = pl.multiple_of(x * 2 * n, 16)
+        out_copies = [
+            pltpu.make_async_copy(chip_out.at[0 : 2 * n], wo.at[pl.ds(row, 2 * n)], sem.at[1]),
+            pltpu.make_async_copy(chip_out.at[2 * n :], wo.at[depth:], sem.at[1]),
+        ]
+        row = pl.multiple_of(x * 2 * m, 16)
+        in_copies = [pltpu.make_async_copy(chip_in, wi.at[pl.ds(row, 2 * m)], sem.at[2])]
 
         def far(outs, ins):
             out, into = [], []
@@ -482,8 +492,7 @@
 
     if split:
         far_a = x_swap(parts[0])
-        near_out, near_in = core_swap(w_out), core_swap(w_in)
-        own = part + after(core_swap(part), near_out, near_in)
+        own = part + core_swap(part)
         other = x_swap(own.astype(BF))
         ends = codes[rows - REACH :], codes[:REACH]
         low = seq_at % 2 == 0
@@ -492,6 +501,7 @@
         pairs.append((seqs - 1, 0))
         odd = lax.ppermute(jnp.where(low, *ends[::-1]), "seq", pairs + [(j, i) for i, j in pairs])
         before, behind = jnp.where(low, odd, even), jnp.where(low, even, odd)
+        far_b = x_swap(after(parts[1], other))
         other = after(other, far_a)
     else:
         own = lax.psum(part, "roll")
@@ -501,30 +511,39 @@
         behind = lax.ppermute(codes[:REACH], "seq", [(j, i) for i, j in pairs])
     wide = KERNEL * H
     shapes = [(SLOT, F32), (SLOT, BF)] if split else [(CODES, F32)]
-    *taps, table = pl.pallas_call(
+    taps = pl.pallas_call(
         functools.partial(table_kernel, split),
-        out_shape=[jax.ShapeDtypeStruct((n, wide), t) for n, t in shapes]
-        + [jax.ShapeDtypeStruct(table.shape, BF)],
-        in_specs=[VMEM, VMEM, VMEM, HBM, HBM],
-        out_specs=[VMEM] * (len(shapes) + 1),
+        out_shape=[jax.ShapeDtypeStruct((n, wide), t) for n, t in shapes],
+        in_specs=[VMEM, VMEM, VMEM, HBM],
+        out_specs=[VMEM] * len(shapes),
         scratch_shapes=[
             pltpu.VMEM(conv_w.shape[1:], BF),
             pltpu.VMEM((CODES, wide), F32),
-            pltpu.SemaphoreType.DMA((2,)),
+            pltpu.SemaphoreType.DMA,
         ],
         cost_estimate=FREE,
         compiler_params=params(12),
-    )(own, other, gain_mid, conv_w, table)
+    )(own, other, gain_mid, conv_w)
     if split:
         relay = after(far_a, taps[1])
         parts_a = [far_a] + [seq_swap(relay, b) for b in (1, 2, 3)]
-        sent = (taps[0] + after(core_swap(taps[1]), before, behind).astype(F32)).astype(BF)
+        sent = (taps[0] + after(core_swap(taps[1]), before, behind, far_b).astype(F32)).astype(BF)
         received = x_swap(sent)
-        far_b = x_swap(after(parts[1], taps[1]))
+        near_sent = core_swap(sent)
+        near_out, near_in = core_swap(after(w_out, sent)), core_swap(after(w_in, sent))
+        chip = pl.pallas_call(
+            stage_kernel,
+            out_shape=[jax.ShapeDtypeStruct(n, BF) for n in ((4 * shard + CODES, width), (8 * shard, H))],
+            in_specs=[ANY] * 5,
+            out_specs=[VMEM] * 2,
+            scratch_shapes=[pltpu.SemaphoreType.DMA],
+            cost_estimate=FREE,
+            compiler_params=params(16),
+        )(after(table, sent), w_out, w_in, near_out, near_in)
     spare = jnp.zeros((-(rows + 2 * REACH) % 128,), jnp.int32)
     near = jnp.concatenate([before, codes, behind, spare])[None]
     if split:
-        near = after(near, sent)
+        near = after(near, sent, chip[0])
 
     hot5, hot1 = pl.pallas_call(
         hot_kernel,
@@ -536,14 +555,13 @@
     )(span, near)
 
     if split:
-        received = after(received, hot1, far_b, *parts_a)
+        received = after(received, hot1, near_sent)
         near_received = core_swap(received)
-        near_sent = core_swap(after(sent, received))
-        near_a = [core_swap(after(p, received)) for p in parts_a]
+        near_a = [core_swap(after(p, hot1)) for p in parts_a]
         relay = after(far_b, received)
         parts_b = [far_b, seq_swap(relay, 1), seq_swap(relay, 2), x_swap(after(parts[2], received))]
-        weights_a = [sent, received, near_sent, near_received, w_out, w_in, near_out, near_in, table] + parts_a + near_a
-        near_conv = core_swap(after(conv_w, near_received))
+        weights_a = [sent, received, near_sent, near_received] + list(chip) + parts_a + near_a
+        near_conv = core_swap(after(conv_w, near_received, *near_a))
     else:
         taps = lax.psum(taps[0], "roll").astype(BF)
         gather = lambda w: lax.all_gather(w, "roll", axis=0, tiled=True)

time: 70.9 us -> 63.9 us (0.901)
  waiting for transfers between devices: 18.4 us -> 9.44 us
  starting transfers between devices: 22.1 us -> 23.2 us
    ppermute x6, waiting for transfers between devices: 5.66 us -> 0.02 us  [seq_swap(): return lax.ppermute(x, 'seq', [(i, i ^ bits) for i in range(seqs)])]
    ppermute x15, waiting for transfers between devices: 7.51 us -> 3.48 us  [core_swap(): return lax.ppermute(x, 'roll', [(i, i ^ 1) for i in range(rolls)])]
    ppermute x1, waiting for transfers between devices: 0.01 us -> 1.45 us  [per_device(): lax.ppermute(jnp.where(low, *ends[::-1]), 'seq', pairs + [(j, i) for i, j...]
    pallas_call x0 -> x1, Pallas kernels: none -> 1.05 us  [per_device(): pl.pallas_call(stage_kernel, out_shape=[jax.ShapeDtypeStruct(n, BF) for n...]
    ppermute x5, waiting for transfers between devices: 5.27 us -> 4.5 us  [x_swap(): return lax.ppermute(x, 'roll', [(i, i ^ 2) for i in range(rolls)])]
    unnamed x26 -> x32, local copies, waits for them, and re-layouts: 5.69 us -> 6.2 us
  transfers between devices with their start and end apart: 27 -> 27, of which waited for: 10 -> 11; matrix products, arithmetic and copies ran while one was open for 2% -> 0% of each run, Pallas kernels for 24% -> 22%
where the time goes in v9:
time: 63.9 us; the launch traced here: 63.6 us
  starting transfers between devices  23.2 us (36%)
  Pallas kernels  22.4 us (35%)
  waiting for transfers between devices  9.44 us (15%)
  local copies, waits for them, and re-layouts  6.28 us (10%)
  other arithmetic  1.16 us (2%)
  between operations  1.06 us (2%)
    pallas_call x1, Pallas kernels, per_device(): pl.pallas_call(functools.partial(rows_kernel, split), out_shape=(jax.Shap...  9.38 us
    ppermute x6, starting transfers between devices, seq_swap(): return lax.ppermute(x, 'seq', [(i, i ^ bits) for i in range(seqs)])  8.18 us
    ppermute x5, starting transfers between devices, x_swap(): return lax.ppermute(x, 'roll', [(i, i ^ 2) for i in range(rolls)])  7.74 us
    unnamed x32, local copies, waits for them, and re-layouts  6.2 us
    pallas_call x1, Pallas kernels, per_device(): pl.pallas_call(functools.partial(last_kernel, split), out_shape=jax.Shape...  5.06 us
    ppermute x5, waiting for transfers between devices, x_swap(): return lax.ppermute(x, 'roll', [(i, i ^ 2) for i in range(rolls)])  4.5 us
    ppermute x15, starting transfers between devices, core_swap(): return lax.ppermute(x, 'roll', [(i, i ^ 1) for i in range(rolls)])  3.78 us
    ppermute x1, starting transfers between devices, per_device(): lax.ppermute(jnp.where(low, *ends[::-1]), 'seq', pairs + [(j, i) for i, j...  3.54 us
  transfers between devices with their start and end apart: 27, of which 11 were waited for; matrix products, arithmetic and copies ran while one was open for 0% of the time, Pallas kernels for 22%

profile of v9, /device:TPU:0, one launch (start us, length us, event | category | flops | bytes accessed | tf_op | source)
XLA Modules:
  0.0 63.6 jit_solution(12613835202157521449)
XLA Ops:
  0.0 3.2 %shard_map.109 = (bf16[64,1280]{1,0:T(8,128)(2,1)}, f32[64,640]{1,0:T(8,128)}, bf16[80,1280]{1,0:T(8,128)(2,1)}, bf16[80,2304]{1,0:T(8,128)(2,1)}, bf16[80,2304]{1,0:T(8,128)(2,1)}) custom-call(f32[30,1280]{1,0:T(8,128)} %embed.1, f32[1280]{0:T(1024)} %brk.1, f32[2,1280]{1,0:T(2,128)} %gain_in.1, bf16[2,320,640]{2,1,0:T(8,128)(2,1)} %w_in.3, ...), custom_call_target="tpu_custom_call" | custom-call | tf_op jit(solution)/shard_map/pallas_call | solution.py:475
  3.2 0.5 collective-permute-start.2
  3.7 1.2 %collective-permute-done.2 = f32[64,640]{1,0:T(8,128)S(1)} collective-permute-done((f32[64,640]{1,0:T(8,128)}, f32[64,640]{1,0:T(8,128)S(1)}, u32[]{:S(2)}, u32[]{:S(2)}) %collective-permute-start.2) | collective-permute-done | bytes 163872 | tf_op jit(solution)/shard_map/ppermute | solution.py:459
  5.0 0.9 %fusion.2 = (bf16[64,640]{1,0:T(8,128)(2,1)S(1)}, f32[64,640]{1,0:T(8,128)S(1)}) fusion(f32[64,640]{1,0:T(8,128)} %get-tuple-element.38, f32[64,640]{1,0:T(8,128)S(1)} %collective-permute-done.2), kind=kLoop, calls=%fused_computation.9 | loop fusion | flops 81920 | bytes 573440 | tf_op jit(solution)/shard_map/convert_element_type | solution.py:496
  5.9 2.9 %collective-permute-start.3 = (bf16[64,640]{1,0:T(8,128)(2,1)S(1)}, bf16[64,640]{1,0:T(8,128)(2,1)S(1)}, u32[]{:S(2)}, u32[]{:S(2)}) collective-permute-start(bf16[64,640]{1,0:T(8,128)(2,1)S(1)} %get-tuple-element.73), channel_id=1, source_target_pairs={{0,2},{1,3},{2,0},{3,1},{4,6},{5,7},{6,4},{7,5},{8,10},{9,11},{10,... | collective-permute-start | bytes 245768 | tf_op jit(solution)/shard_map/ppermute | solution.py:462
  8.9 2.7 %collective-permute-done.3.other = bf16[64,640]{1,0:T(8,128)(2,1)S(1)} collective-permute-done((bf16[64,640]{1,0:T(8,128)(2,1)S(1)}, bf16[64,640]{1,0:T(8,128)(2,1)S(1)}, u32[]{:S(2)}, u32[]{:S(2)}) %collective-permute-start.3) | collective-permute-done | bytes 81952 | tf_op jit(solution)/shard_map/ppermute | solution.py:462
  11.7 2.5 %collective-permute-start.6 = (bf16[80,2304]{1,0:T(8,128)(2,1)}, bf16[80,2304]{1,0:T(8,128)(2,1)S(1)}, u32[]{:S(2)}, u32[]{:S(2)}) collective-permute-start(bf16[80,2304]{1,0:T(8,128)(2,1)} %get-tuple-element.44), channel_id=1, source_target_pairs={{0,2},{1,3},{2,0},{3,1},{4,6},{5,7},{6,4},{7,5},{8,10},{9,11},{10,... | collective-permute-start | bytes 1105928 | tf_op jit(solution)/shard_map/ppermute | solution.py:462
  14.3 1.6 %collective-permute-start.1 = (s32[384]{0:T(512)S(1)}, s32[384]{0:T(512)S(1)}, u32[]{:S(2)}, u32[]{:S(2)}) collective-permute-start(s32[384]{0:T(512)S(1)} %get-tuple-element.71), channel_id=1, source_target_pairs={{0,4},{4,0},{8,12},{12,8},{16,20},{20,16},{24,28},{28,24},{1,5},{5... | collective-permute-start | bytes 4616 | tf_op jit(solution)/shard_map/ppermute | solution.py:465
  15.8 3.5 %collective-permute-start = (s32[384]{0:T(512)S(1)}, s32[384]{0:T(512)S(1)}, u32[]{:S(2)}, u32[]{:S(2)}) collective-permute-start(s32[384]{0:T(512)S(1)} %get-tuple-element.72), channel_id=1, source_target_pairs={{4,8},{12,16},{20,24},{28,0},{8,4},{16,12},{24,20},{0,28},{5,9},{1... | collective-permute-start | bytes 4616 | tf_op jit(solution)/shard_map/ppermute | solution.py:502
  19.4 1.2 %shard_map.110 = (f32[32,3200]{1,0:T(8,128)S(1)}, bf16[32,3200]{1,0:T(8,128)(2,1)S(1)}) custom-call(f32[64,640]{1,0:T(8,128)S(1)} %get-tuple-element.74.own, bf16[64,640]{1,0:T(8,128)(2,1)S(1)} %collective-permute-done.3.other, f32[2,640]{1,0:T(2,128)S(1)} %copy-done.11, bf16[2,160,3200]{2,1,0:T(8,128)(2,1)S(1)} %copy-done), custom_call_target="tpu_custom_call" | custom-call | tf_op jit(solution)/shard_map/pallas_call | solution.py:514
  20.7 1.4 %collective-permute-done = s32[384]{0:T(512)S(1)} collective-permute-done((s32[384]{0:T(512)S(1)}, s32[384]{0:T(512)S(1)}, u32[]{:S(2)}, u32[]{:S(2)}) %collective-permute-start) | collective-permute-done | bytes 1568 | tf_op jit(solution)/shard_map/ppermute | solution.py:502
  22.1 1.8 %collective-permute-done.6.rest_5_ = bf16[80,2304]{1,0:T(8,128)(2,1)S(1)} collective-permute-done((bf16[80,2304]{1,0:T(8,128)(2,1)}, bf16[80,2304]{1,0:T(8,128)(2,1)S(1)}, u32[]{:S(2)}, u32[]{:S(2)}) %collective-permute-start.6) | collective-permute-done | bytes 368672 | tf_op jit(solution)/shard_map/ppermute | solution.py:462
  24.0 0.5 collective-permute-start.8
  24.5 2.8 %collective-permute-start.14 = (bf16[80,1280]{1,0:T(8,128)(2,1)}, bf16[80,1280]{1,0:T(8,128)(2,1)}, u32[]{:S(2)}, u32[]{:S(2)}) collective-permute-start(bf16[80,1280]{1,0:T(8,128)(2,1)} %collective-permute-done.4.rest_6_), channel_id=1, source_target_pairs={{0,12},{4,8},{8,4},{12,0},{16,28},{20,24},{24,20},{28,16},{1,13},{... | collective-permute-start | bytes 614408 | tf_op jit(solution)/shard_map/ppermute | solution.py:465
  27.3 0.4 collective-permute-start.13
  28.0 0.9 %copy-done.4 = bf16[2,160,1280]{2,1,0:T(8,128)(2,1)} copy-done((bf16[2,160,1280]{2,1,0:T(8,128)(2,1)}, bf16[2,160,1280]{2,1,0:T(8,128)(2,1)S(1)}, u32[]{:S(2)}) %copy-start.4) | copy-done | bytes 819224
  28.9 0.9 %copy-done.7 = bf16[2,320,640]{2,1,0:T(8,128)(2,1)} copy-done((bf16[2,320,640]{2,1,0:T(8,128)(2,1)}, bf16[2,320,640]{2,1,0:T(8,128)(2,1)S(1)}, u32[]{:S(2)}) %copy-start.7) | copy-done | bytes 819224
  29.8 1.7 %collective-permute-start.9 = (bf16[32,3200]{1,0:T(8,128)(2,1)S(1)}, bf16[32,3200]{1,0:T(8,128)(2,1)}, u32[]{:S(2)}, u32[]{:S(2)}) collective-permute-start(bf16[32,3200]{1,0:T(8,128)(2,1)S(1)} %add_convert_fusion.rest_0_), channel_id=1, source_target_pairs={{0,2},{1,3},{2,0},{3,1},{4,6},{5,7},{6,4},{7,5},{8,10},{9,11},{10,... | collective-permute-start | bytes 614408 | tf_op jit(solution)/shard_map/ppermute | solution.py:462
  32.4 1.1 %copy-done.3 = bf16[2,320,640]{2,1,0:T(8,128)(2,1)S(1)} copy-done((bf16[2,320,640]{2,1,0:T(8,128)(2,1)S(1)}, bf16[2,320,640]{2,1,0:T(8,128)(2,1)}, u32[]{:S(2)}) %copy-start.3) | copy-done | bytes 819224
  33.5 1.1 %copy-done.5 = bf16[2,160,1280]{2,1,0:T(8,128)(2,1)S(1)} copy-done((bf16[2,160,1280]{2,1,0:T(8,128)(2,1)S(1)}, bf16[2,160,1280]{2,1,0:T(8,128)(2,1)}, u32[]{:S(2)}) %copy-start.5) | copy-done | bytes 819224
  34.7 1.1 %copy-done.8 = bf16[2,320,640]{2,1,0:T(8,128)(2,1)S(1)} copy-done((bf16[2,320,640]{2,1,0:T(8,128)(2,1)S(1)}, bf16[2,320,640]{2,1,0:T(8,128)(2,1)}, u32[]{:S(2)}) %copy-start.8) | copy-done | bytes 819224
  35.8 0.9 %copy-done.9 = bf16[64,1280]{1,0:T(8,128)(2,1)S(1)} copy-done((bf16[64,1280]{1,0:T(8,128)(2,1)S(1)}, bf16[64,1280]{1,0:T(8,128)(2,1)}, u32[]{:S(2)}) %copy-start.9) | copy-done | bytes 163864
  36.7 1.0 %shard_map.111 = (bf16[384,1280]{1,0:T(8,128)(2,1)S(1)}, bf16[640,640]{1,0:T(8,128)(2,1)S(1)}) custom-call(bf16[64,1280]{1,0:T(8,128)(2,1)S(1)} %copy-done.9, bf16[2,160,1280]{2,1,0:T(8,128)(2,1)S(1)} %copy-done.1, bf16[2,320,640]{2,1,0:T(8,128)(2,1)S(1)} %copy-done.3, bf16[2,160,1280]{2,1,0:T(8,128)(2,1)S(1)} %copy-done.5, bf16[2,320,640]{2,1,0:T(8,128)(2,1)S(1)} %copy-done.8), custom_call_target="tpu_custom_call" | custom-call | tf_op jit(solution)/shard_map/pallas_call | solution.py:534
  37.8 1.0 %shard_map.112 = (bf16[1008,320]{1,0:T(8,128)(2,1)S(1)}, bf16[1008,64]{1,0:T(8,128)(2,1)S(1)}) custom-call(s32[2]{0:T(128)S(1)} %pad_add_fusion.span, s32[1,1280]{1,0:T(1,128)S(1)} %broadcast_in_dim.6.near), custom_call_target="tpu_custom_call" | custom-call | tf_op jit(solution)/shard_map/pallas_call | solution.py:548
  42.0 1.6 %collective-permute-start.21 = (bf16[80,2304]{1,0:T(8,128)(2,1)S(1)}, bf16[80,2304]{1,0:T(8,128)(2,1)S(1)}, u32[]{:S(2)}, u32[]{:S(2)}) collective-permute-start(bf16[80,2304]{1,0:T(8,128)(2,1)S(1)} %collective-permute-done.6.rest_5_), channel_id=1, source_target_pairs={{0,8},{4,12},{8,0},{12,4},{16,24},{20,28},{24,16},{28,20},{1,9},{5... | collective-permute-start | bytes 1105928 | tf_op jit(solution)/shard_map/ppermute | solution.py:465
  43.5 1.5 %collective-permute-start.20 = (bf16[80,2304]{1,0:T(8,128)(2,1)S(1)}, bf16[80,2304]{1,0:T(8,128)(2,1)S(1)}, u32[]{:S(2)}, u32[]{:S(2)}) collective-permute-start(bf16[80,2304]{1,0:T(8,128)(2,1)S(1)} %collective-permute-done.6.rest_5_), channel_id=1, source_target_pairs={{0,4},{4,0},{8,12},{12,8},{16,20},{20,16},{24,28},{28,24},{1,5},{5... | collective-permute-start | bytes 1105928 | tf_op jit(solution)/shard_map/ppermute | solution.py:465
  45.1 0.5 collective-permute-start.22
  45.6 9.4 %shard_map.113 = (bf16[1008,640]{1,0:T(8,128)(2,1)S(1)}, bf16[496,1280]{1,0:T(8,128)(2,1)S(1)}) custom-call(s32[2]{0:T(128)S(1)} %pad_add_fusion.span, bf16[1008,320]{1,0:T(8,128)(2,1)S(1)} %get-tuple-element.52.hot5, bf16[1008,64]{1,0:T(8,128)(2,1)S(1)} %get-tuple-element.53.hot1, f32[2,640]{1,0:T(2,128)S(1)} %copy-done.12, f32[2,1280]{1,0:T(2,128)S(1)} %copy-done.10, ...), custom_call_target="tpu_custom_call" | custom-call | tf_op jit(solution)/shard_map/pallas_call | solution.py:570
  55.1 0.5 collective-permute-start.25
  56.1 1.6 %shard_map.114.rest_0_ = f32[496,640]{1,0:T(8,128)S(1)} custom-call(bf16[1008,640]{1,0:T(8,128)(2,1)S(1)} %get-tuple-element.61.ci, bf16[2,160,3200]{2,1,0:T(8,128)(2,1)S(1)} %copy-done, bf16[2,160,3200]{2,1,0:T(8,128)(2,1)S(1)} %collective-permute-done.19.near_conv.rest_3_), custom_call_target="tpu_custom_call" | custom-call | tf_op jit(solution)/shard_map/pallas_call | solution.py:590
  57.8 0.5 collective-permute-done.26.rest_12_
  58.4 5.1 %shard_map.115 = bf16[496,1280]{1,0:T(8,128)(2,1)} custom-call(bf16[1008,640]{1,0:T(8,128)(2,1)S(1)} %get-tuple-element.61.ci, bf16[496,1280]{1,0:T(8,128)(2,1)S(1)} %get-tuple-element.62.hid, f32[2,640]{1,0:T(2,128)S(1)} %copy-done.12, f32[496,640]{1,0:T(8,128)S(1)} %shard_map.114.rest_0_, bf16[2,160,3200]{2,1,0:T(8,128)(2,1)S(1)} %copy-done, ...), custom_call_target="tpu_custom_call" | custom-call | tf_op jit(solution)/shard_map/pallas_call | solution.py:600
  (70 shorter events, 4.7 us)
Async XLA Ops:
  0.0 19.4 %copy-start = (bf16[2,160,3200]{2,1,0:T(8,128)(2,1)S(1)}, bf16[2,160,3200]{2,1,0:T(8,128)(2,1)}, u32[]{:S(2)}) copy-start(bf16[2,160,3200]{2,1,0:T(8,128)(2,1)} %rest_1_.1) | copy-start | bytes 6144004
  0.0 14.1 %copy-start.14 = (s32[1,496]{1,0:T(1,128)S(1)}, s32[1,496]{1,0:T(1,128)}, u32[]{:S(2)}) copy-start(s32[1,496]{1,0:T(1,128)} %param.12) | copy-start | bytes 5956
  0.0 14.1 %copy-start.13 = (s32[1,496]{1,0:T(1,128)S(1)}, s32[1,496]{1,0:T(1,128)}, u32[]{:S(2)}) copy-start(s32[1,496]{1,0:T(1,128)} %param.11) | copy-start | bytes 5956
  0.0 19.4 %copy-start.11 = (f32[2,640]{1,0:T(2,128)S(1)}, f32[2,640]{1,0:T(2,128)}, u32[]{:S(2)}) copy-start(f32[2,640]{1,0:T(2,128)} %gain_mid.1) | copy-start | bytes 15364
  3.2 1.8 %collective-permute-start.2 = (f32[64,640]{1,0:T(8,128)}, f32[64,640]{1,0:T(8,128)S(1)}, u32[]{:S(2)}, u32[]{:S(2)}) collective-permute-start(f32[64,640]{1,0:T(8,128)} %get-tuple-element.38), channel_id=1, source_target_pairs={{0,1},{1,0},{2,3},{3,2},{4,5},{5,4},{6,7},{7,6},{8,9},{9,8},{10,11... | collective-permute-start | bytes 491528 | tf_op jit(solution)/shard_map/ppermute | solution.py:459
  5.9 5.7 %collective-permute-start.3 = (bf16[64,640]{1,0:T(8,128)(2,1)S(1)}, bf16[64,640]{1,0:T(8,128)(2,1)S(1)}, u32[]{:S(2)}, u32[]{:S(2)}) collective-permute-start(bf16[64,640]{1,0:T(8,128)(2,1)S(1)} %get-tuple-element.73), channel_id=1, source_target_pairs={{0,2},{1,3},{2,0},{3,1},{4,6},{5,7},{6,4},{7,5},{8,10},{9,11},{10,... | collective-permute-start | bytes 245768 | tf_op jit(solution)/shard_map/ppermute | solution.py:462
  8.8 10.5 %collective-permute-start.4 = (bf16[80,1280]{1,0:T(8,128)(2,1)}, bf16[80,1280]{1,0:T(8,128)(2,1)}, u32[]{:S(2)}, u32[]{:S(2)}) collective-permute-start(bf16[80,1280]{1,0:T(8,128)(2,1)} %get-tuple-element.39), channel_id=1, source_target_pairs={{0,2},{1,3},{2,0},{3,1},{4,6},{5,7},{6,4},{7,5},{8,10},{9,11},{10,... | collective-permute-start | bytes 614408 | tf_op jit(solution)/shard_map/ppermute | solution.py:462
  11.7 12.2 %collective-permute-start.6 = (bf16[80,2304]{1,0:T(8,128)(2,1)}, bf16[80,2304]{1,0:T(8,128)(2,1)S(1)}, u32[]{:S(2)}, u32[]{:S(2)}) collective-permute-start(bf16[80,2304]{1,0:T(8,128)(2,1)} %get-tuple-element.44), channel_id=1, source_target_pairs={{0,2},{1,3},{2,0},{3,1},{4,6},{5,7},{6,4},{7,5},{8,10},{9,11},{10,... | collective-permute-start | bytes 1105928 | tf_op jit(solution)/shard_map/ppermute | solution.py:462
  14.3 6.4 %collective-permute-start.1 = (s32[384]{0:T(512)S(1)}, s32[384]{0:T(512)S(1)}, u32[]{:S(2)}, u32[]{:S(2)}) collective-permute-start(s32[384]{0:T(512)S(1)} %get-tuple-element.71), channel_id=1, source_target_pairs={{0,4},{4,0},{8,12},{12,8},{16,20},{20,16},{24,28},{28,24},{1,5},{5... | collective-permute-start | bytes 4616 | tf_op jit(solution)/shard_map/ppermute | solution.py:465
  15.8 6.3 %collective-permute-start = (s32[384]{0:T(512)S(1)}, s32[384]{0:T(512)S(1)}, u32[]{:S(2)}, u32[]{:S(2)}) collective-permute-start(s32[384]{0:T(512)S(1)} %get-tuple-element.72), channel_id=1, source_target_pairs={{4,8},{12,16},{20,24},{28,0},{8,4},{16,12},{24,20},{0,28},{5,9},{1... | collective-permute-start | bytes 4616 | tf_op jit(solution)/shard_map/ppermute | solution.py:502
  20.6 1.5 %collective-permute-start.5 = (bf16[32,3200]{1,0:T(8,128)(2,1)S(1)}, bf16[32,3200]{1,0:T(8,128)(2,1)S(1)}, u32[]{:S(2)}, u32[]{:S(2)}) collective-permute-start(bf16[32,3200]{1,0:T(8,128)(2,1)S(1)} %get-tuple-element.42), channel_id=1, source_target_pairs={{0,1},{1,0},{2,3},{3,2},{4,5},{5,4},{6,7},{7,6},{8,9},{9,8},{10,11... | collective-permute-start | bytes 614408 | tf_op jit(solution)/shard_map/ppermute | solution.py:459
  23.9 4.1 %collective-permute-start.7 = (bf16[2,160,1280]{2,1,0:T(8,128)(2,1)S(1)}, bf16[2,160,1280]{2,1,0:T(8,128)(2,1)S(1)}, u32[]{:S(2)}, u32[]{:S(2)}) collective-permute-start(bf16[2,160,1280]{2,1,0:T(8,128)(2,1)S(1)} %copy-done.1), channel_id=1, source_target_pairs={{0,1},{1,0},{2,3},{3,2},{4,5},{5,4},{6,7},{7,6},{8,9},{9,8},{10,11... | collective-permute-start | bytes 2457608 | tf_op jit(solution)/shard_map/ppermute | solution.py:459
  24.0 4.9 %collective-permute-start.8 = (bf16[2,320,640]{2,1,0:T(8,128)(2,1)S(1)}, bf16[2,320,640]{2,1,0:T(8,128)(2,1)S(1)}, u32[]{:S(2)}, u32[]{:S(2)}) collective-permute-start(bf16[2,320,640]{2,1,0:T(8,128)(2,1)S(1)} %copy-done.2), channel_id=1, source_target_pairs={{0,1},{1,0},{2,3},{3,2},{4,5},{5,4},{6,7},{7,6},{8,9},{9,8},{10,11... | collective-permute-start | bytes 2457608 | tf_op jit(solution)/shard_map/ppermute | solution.py:459
  24.5 14.3 %collective-permute-start.14 = (bf16[80,1280]{1,0:T(8,128)(2,1)}, bf16[80,1280]{1,0:T(8,128)(2,1)}, u32[]{:S(2)}, u32[]{:S(2)}) collective-permute-start(bf16[80,1280]{1,0:T(8,128)(2,1)} %collective-permute-done.4.rest_6_), channel_id=1, source_target_pairs={{0,12},{4,8},{8,4},{12,0},{16,28},{20,24},{24,20},{28,16},{1,13},{... | collective-permute-start | bytes 614408 | tf_op jit(solution)/shard_map/ppermute | solution.py:465
  27.3 11.5 %collective-permute-start.13 = (bf16[80,1280]{1,0:T(8,128)(2,1)}, bf16[80,1280]{1,0:T(8,128)(2,1)}, u32[]{:S(2)}, u32[]{:S(2)}) collective-permute-start(bf16[80,1280]{1,0:T(8,128)(2,1)} %collective-permute-done.4.rest_6_), channel_id=1, source_target_pairs={{0,8},{4,12},{8,0},{12,4},{16,24},{20,28},{24,16},{28,20},{1,9},{5... | collective-permute-start | bytes 614408 | tf_op jit(solution)/shard_map/ppermute | solution.py:465
  27.8 11.1 %collective-permute-start.12 = (bf16[80,1280]{1,0:T(8,128)(2,1)}, bf16[80,1280]{1,0:T(8,128)(2,1)}, u32[]{:S(2)}, u32[]{:S(2)}) collective-permute-start(bf16[80,1280]{1,0:T(8,128)(2,1)} %collective-permute-done.4.rest_6_), channel_id=1, source_target_pairs={{0,4},{4,0},{8,12},{12,8},{16,20},{20,16},{24,28},{28,24},{1,5},{5... | collective-permute-start | bytes 614408 | tf_op jit(solution)/shard_map/ppermute | solution.py:465
  28.9 9.9 %collective-permute-start.10 = (bf16[32,3200]{1,0:T(8,128)(2,1)S(1)}, bf16[32,3200]{1,0:T(8,128)(2,1)}, u32[]{:S(2)}, u32[]{:S(2)}) collective-permute-start(bf16[32,3200]{1,0:T(8,128)(2,1)S(1)} %add_convert_fusion.rest_0_), channel_id=1, source_target_pairs={{0,1},{1,0},{2,3},{3,2},{4,5},{5,4},{6,7},{7,6},{8,9},{9,8},{10,11... | collective-permute-start | bytes 614408 | tf_op jit(solution)/shard_map/ppermute | solution.py:459
  29.8 9.0 %collective-permute-start.9 = (bf16[32,3200]{1,0:T(8,128)(2,1)S(1)}, bf16[32,3200]{1,0:T(8,128)(2,1)}, u32[]{:S(2)}, u32[]{:S(2)}) collective-permute-start(bf16[32,3200]{1,0:T(8,128)(2,1)S(1)} %add_convert_fusion.rest_0_), channel_id=1, source_target_pairs={{0,2},{1,3},{2,0},{3,1},{4,6},{5,7},{6,4},{7,5},{8,10},{9,11},{10,... | collective-permute-start | bytes 614408 | tf_op jit(solution)/shard_map/ppermute | solution.py:462
  36.7 8.9 %copy-start.12 = (f32[2,640]{1,0:T(2,128)S(1)}, f32[2,640]{1,0:T(2,128)}, u32[]{:S(2)}) copy-start(f32[2,640]{1,0:T(2,128)} %gain_out.3) | copy-start | bytes 15364
  38.8 1.7 %collective-permute-start.11 = (bf16[32,3200]{1,0:T(8,128)(2,1)}, bf16[32,3200]{1,0:T(8,128)(2,1)S(1)}, u32[]{:S(2)}, u32[]{:S(2)}) collective-permute-start(bf16[32,3200]{1,0:T(8,128)(2,1)} %collective-permute-done.9.rest_1_), channel_id=1, source_target_pairs={{0,1},{1,0},{2,3},{3,2},{4,5},{5,4},{6,7},{7,6},{8,9},{9,8},{10,11... | collective-permute-start | bytes 614408 | tf_op jit(solution)/shard_map/ppermute | solution.py:459
  39.1 1.7 %collective-permute-start.15 = (bf16[80,1280]{1,0:T(8,128)(2,1)}, bf16[80,1280]{1,0:T(8,128)(2,1)S(1)}, u32[]{:S(2)}, u32[]{:S(2)}) collective-permute-start(bf16[80,1280]{1,0:T(8,128)(2,1)} %collective-permute-done.4.rest_6_), channel_id=1, source_target_pairs={{0,1},{1,0},{2,3},{3,2},{4,5},{5,4},{6,7},{7,6},{8,9},{9,8},{10,11... | collective-permute-start | bytes 614408 | tf_op jit(solution)/shard_map/ppermute | solution.py:459
  39.4 1.7 %collective-permute-start.16 = (bf16[80,1280]{1,0:T(8,128)(2,1)}, bf16[80,1280]{1,0:T(8,128)(2,1)S(1)}, u32[]{:S(2)}, u32[]{:S(2)}) collective-permute-start(bf16[80,1280]{1,0:T(8,128)(2,1)} %collective-permute-done.12.rest_7_), channel_id=1, source_target_pairs={{0,1},{1,0},{2,3},{3,2},{4,5},{5,4},{6,7},{7,6},{8,9},{9,8},{10,11... | collective-permute-start | bytes 614408 | tf_op jit(solution)/shard_map/ppermute | solution.py:459
  39.6 1.8 %collective-permute-start.17 = (bf16[80,1280]{1,0:T(8,128)(2,1)}, bf16[80,1280]{1,0:T(8,128)(2,1)S(1)}, u32[]{:S(2)}, u32[]{:S(2)}) collective-permute-start(bf16[80,1280]{1,0:T(8,128)(2,1)} %collective-permute-done.13.rest_8_), channel_id=1, source_target_pairs={{0,1},{1,0},{2,3},{3,2},{4,5},{5,4},{6,7},{7,6},{8,9},{9,8},{10,11... | collective-permute-start | bytes 614408 | tf_op jit(solution)/shard_map/ppermute | solution.py:459
  39.9 1.8 %collective-permute-start.18 = (bf16[80,1280]{1,0:T(8,128)(2,1)}, bf16[80,1280]{1,0:T(8,128)(2,1)S(1)}, u32[]{:S(2)}, u32[]{:S(2)}) collective-permute-start(bf16[80,1280]{1,0:T(8,128)(2,1)} %collective-permute-done.14.rest_9_), channel_id=1, source_target_pairs={{0,1},{1,0},{2,3},{3,2},{4,5},{5,4},{6,7},{7,6},{8,9},{9,8},{10,11... | collective-permute-start | bytes 614408 | tf_op jit(solution)/shard_map/ppermute | solution.py:459
  41.7 14.4 %collective-permute-start.19 = (bf16[2,160,3200]{2,1,0:T(8,128)(2,1)S(1)}, bf16[2,160,3200]{2,1,0:T(8,128)(2,1)S(1)}, u32[]{:S(2)}, u32[]{:S(2)}) collective-permute-start(bf16[2,160,3200]{2,1,0:T(8,128)(2,1)S(1)} %copy-done), channel_id=1, source_target_pairs={{0,1},{1,0},{2,3},{3,2},{4,5},{5,4},{6,7},{7,6},{8,9},{9,8},{10,11... | collective-permute-start | bytes 6144008 | tf_op jit(solution)/shard_map/ppermute | solution.py:459
  42.0 13.1 %collective-permute-start.21 = (bf16[80,2304]{1,0:T(8,128)(2,1)S(1)}, bf16[80,2304]{1,0:T(8,128)(2,1)S(1)}, u32[]{:S(2)}, u32[]{:S(2)}) collective-permute-start(bf16[80,2304]{1,0:T(8,128)(2,1)S(1)} %collective-permute-done.6.rest_5_), channel_id=1, source_target_pairs={{0,8},{4,12},{8,0},{12,4},{16,24},{20,28},{24,16},{28,20},{1,9},{5... | collective-permute-start | bytes 1105928 | tf_op jit(solution)/shard_map/ppermute | solution.py:465
  43.5 12.1 %collective-permute-start.20 = (bf16[80,2304]{1,0:T(8,128)(2,1)S(1)}, bf16[80,2304]{1,0:T(8,128)(2,1)S(1)}, u32[]{:S(2)}, u32[]{:S(2)}) collective-permute-start(bf16[80,2304]{1,0:T(8,128)(2,1)S(1)} %collective-permute-done.6.rest_5_), channel_id=1, source_target_pairs={{0,4},{4,0},{8,12},{12,8},{16,20},{20,16},{24,28},{28,24},{1,5},{5... | collective-permute-start | bytes 1105928 | tf_op jit(solution)/shard_map/ppermute | solution.py:465
  45.1 10.6 %collective-permute-start.22 = (bf16[80,2304]{1,0:T(8,128)(2,1)S(1)}, bf16[80,2304]{1,0:T(8,128)(2,1)S(1)}, u32[]{:S(2)}, u32[]{:S(2)}) collective-permute-start(bf16[80,2304]{1,0:T(8,128)(2,1)S(1)} %copy-done.15), channel_id=1, source_target_pairs={{0,2},{1,3},{2,0},{3,1},{4,6},{5,7},{6,4},{7,5},{8,10},{9,11},{10,... | collective-permute-start | bytes 1105928 | tf_op jit(solution)/shard_map/ppermute | solution.py:462
  55.0 2.7 %collective-permute-start.23 = (bf16[80,2304]{1,0:T(8,128)(2,1)S(1)}, bf16[80,2304]{1,0:T(8,128)(2,1)S(1)}, u32[]{:S(2)}, u32[]{:S(2)}) collective-permute-start(bf16[80,2304]{1,0:T(8,128)(2,1)S(1)} %collective-permute-done.6.rest_5_), channel_id=1, source_target_pairs={{0,1},{1,0},{2,3},{3,2},{4,5},{5,4},{6,7},{7,6},{8,9},{9,8},{10,11... | collective-permute-start | bytes 1105928 | tf_op jit(solution)/shard_map/ppermute | solution.py:459
  55.1 2.6 %collective-permute-start.25 = (bf16[80,2304]{1,0:T(8,128)(2,1)S(1)}, bf16[80,2304]{1,0:T(8,128)(2,1)S(1)}, u32[]{:S(2)}, u32[]{:S(2)}) collective-permute-start(bf16[80,2304]{1,0:T(8,128)(2,1)S(1)} %collective-permute-done.21.rest_7_), channel_id=1, source_target_pairs={{0,1},{1,0},{2,3},{3,2},{4,5},{5,4},{6,7},{7,6},{8,9},{9,8},{10,11... | collective-permute-start | bytes 1105928 | tf_op jit(solution)/shard_map/ppermute | solution.py:459
  55.6 2.2 %collective-permute-start.24 = (bf16[80,2304]{1,0:T(8,128)(2,1)S(1)}, bf16[80,2304]{1,0:T(8,128)(2,1)S(1)}, u32[]{:S(2)}, u32[]{:S(2)}) collective-permute-start(bf16[80,2304]{1,0:T(8,128)(2,1)S(1)} %collective-permute-done.20.rest_6_), channel_id=1, source_target_pairs={{0,1},{1,0},{2,3},{3,2},{4,5},{5,4},{6,7},{7,6},{8,9},{9,8},{10,11... | collective-permute-start | bytes 1105928 | tf_op jit(solution)/shard_map/ppermute | solution.py:459
  55.7 2.7 %collective-permute-start.26 = (bf16[80,2304]{1,0:T(8,128)(2,1)S(1)}, bf16[80,2304]{1,0:T(8,128)(2,1)S(1)}, u32[]{:S(2)}, u32[]{:S(2)}) collective-permute-start(bf16[80,2304]{1,0:T(8,128)(2,1)S(1)} %collective-permute-done.22.rest_8_), channel_id=1, source_target_pairs={{0,1},{1,0},{2,3},{3,2},{4,5},{5,4},{6,7},{7,6},{8,9},{9,8},{10,11... | collective-permute-start | bytes 1105928 | tf_op jit(solution)/shard_map/ppermute | solution.py:459
  (11 other events, 35.9 us)

commit v10 on v9

--- a/solution.py
+++ b/solution.py
@@ -162,18 +162,24 @@
         outs[0][...] = full[...]
 
 
-def stage_kernel(table, w_out, w_in, near_out, near_in, chip_out, chip_in, sem):
+def chip_copies(table, w_out, w_in, near_out, near_in, chip_out, chip_in, sem):
     _, core, _, _ = place()
     n, m = w_out.shape[1], w_in.shape[1]
     copies = [pltpu.make_async_copy(table, chip_out.at[2 * n :], sem)]
     for c, o, i in ((core, w_out, w_in), (1 - core, near_out, near_in)):
         copies.append(pltpu.make_async_copy(o.at[0], chip_out.at[pl.ds(pl.multiple_of(c * n, 16), n)], sem))
         copies.append(pltpu.make_async_copy(i.at[1], chip_in.at[pl.ds(pl.multiple_of(c * m, 16), m)], sem))
+    return copies
+
+
+def hot_kernel(split, span, near, *rest):
+    copies = []
+    if split:
+        *w, hot5, hot1, chip_out, chip_in, sem = rest
+        copies = chip_copies(*w, chip_out, chip_in, sem)
+    else:
+        hot5, hot1 = rest
     start(copies)
-    wait(copies)
-
-
-def hot_kernel(span, near, hot5, hot1):
     codes = near[...]
     count = codes.shape[1]
     rows = hot5.shape[0]
@@ -185,6 +191,7 @@
         hot5[:, k * CODES : (k + 1) * CODES] = taps[k * DIL0 : k * DIL0 + rows]
     center = jnp.where(lanes == codes, 1.0, 0.0).T.astype(BF)
     hot1[...] = center[HALF * DIL0 : HALF * DIL0 + rows]
+    wait(copies)
 
 
 def rows_kernel(split, span, hot5, hot1, gain_out, gain_in, gain_mid, *rest):
@@ -491,18 +498,21 @@
     )(embed_table, break_vec, gain_in, w_in, conv_w, w_out)
 
     if split:
-        far_a = x_swap(parts[0])
-        own = part + core_swap(part)
+        near_out, near_in = core_swap(w_out), core_swap(w_in)
+        low = roll_at % 2 == 0
+        ends = codes[rows - REACH :], codes[:REACH]
+        theirs = core_swap(jnp.where(low, *ends[::-1]))
+        own = part + after(core_swap(part), theirs)
         other = x_swap(own.astype(BF))
-        ends = codes[rows - REACH :], codes[:REACH]
-        low = seq_at % 2 == 0
-        even = seq_swap(jnp.where(low, *ends), 1)
-        pairs = [(i, i + 1) for i in range(1, seqs - 1, 2)]
-        pairs.append((seqs - 1, 0))
-        odd = lax.ppermute(jnp.where(low, *ends[::-1]), "seq", pairs + [(j, i) for i, j in pairs])
-        before, behind = jnp.where(low, odd, even), jnp.where(low, even, odd)
+        far_a = x_swap(after(parts[0], own))
+        pack = jnp.stack([jnp.where(low, *ends), theirs])
+        places = [(s, r) for s in range(seqs) for r in range(rolls)]
+        moves = [(s * rolls + r, (s + (1, -1)[r % 2]) % seqs * rolls + r) for s, r in places]
+        moved = lax.ppermute(after(pack, own), ("seq", "roll"), moves)
+        other = after(other, moved, near_out, near_in)
         far_b = x_swap(after(parts[1], other))
-        other = after(other, far_a)
+        came = core_swap(moved[1])
+        before, behind = jnp.where(low, moved[0], came), jnp.where(low, came, moved[0])
     else:
         own = lax.psum(part, "roll")
         other = jnp.zeros((CODES, H), BF)
@@ -527,40 +537,37 @@
     if split:
         relay = after(far_a, taps[1])
         parts_a = [far_a] + [seq_swap(relay, b) for b in (1, 2, 3)]
-        sent = (taps[0] + after(core_swap(taps[1]), before, behind, far_b).astype(F32)).astype(BF)
+        sent = (taps[0] + core_swap(taps[1]).astype(F32)).astype(BF)
         received = x_swap(sent)
-        near_sent = core_swap(sent)
-        near_out, near_in = core_swap(after(w_out, sent)), core_swap(after(w_in, sent))
-        chip = pl.pallas_call(
-            stage_kernel,
-            out_shape=[jax.ShapeDtypeStruct(n, BF) for n in ((4 * shard + CODES, width), (8 * shard, H))],
-            in_specs=[ANY] * 5,
-            out_specs=[VMEM] * 2,
-            scratch_shapes=[pltpu.SemaphoreType.DMA],
-            cost_estimate=FREE,
-            compiler_params=params(16),
-        )(after(table, sent), w_out, w_in, near_out, near_in)
     spare = jnp.zeros((-(rows + 2 * REACH) % 128,), jnp.int32)
     near = jnp.concatenate([before, codes, behind, spare])[None]
     if split:
-        near = after(near, sent, chip[0])
-
-    hot5, hot1 = pl.pallas_call(
-        hot_kernel,
-        out_shape=[jax.ShapeDtypeStruct((wide_rows, n), BF) for n in (KERNEL * CODES, CODES)],
-        in_specs=[SMEM, VMEM],
-        out_specs=[VMEM] * 2,
+        near = after(near, sent)
+
+    shapes = [(wide_rows, KERNEL * CODES), (wide_rows, CODES)]
+    operands, scratch = [], []
+    if split:
+        operands = [table, w_out, w_in, near_out, near_in]
+        shapes += [(4 * shard + CODES, width), (8 * shard, H)]
+        scratch = [pltpu.SemaphoreType.DMA]
+    hot5, hot1, *chip = pl.pallas_call(
+        functools.partial(hot_kernel, split),
+        out_shape=[jax.ShapeDtypeStruct(n, BF) for n in shapes],
+        in_specs=[SMEM, VMEM] + [ANY] * len(operands),
+        out_specs=[VMEM] * len(shapes),
+        scratch_shapes=scratch,
         cost_estimate=FREE,
-        compiler_params=params(12),
-    )(span, near)
-
-    if split:
-        received = after(received, hot1, near_sent)
+        compiler_params=params(16),
+    )(span, near, *operands)
+
+    if split:
+        near_sent = core_swap(after(sent, hot1))
+        received = after(received, hot1)
         near_received = core_swap(received)
-        near_a = [core_swap(after(p, hot1)) for p in parts_a]
-        relay = after(far_b, received)
+        near_a = [core_swap(after(p, hot1, far_b)) for p in parts_a]
+        relay = after(far_b, received, near_sent)
         parts_b = [far_b, seq_swap(relay, 1), seq_swap(relay, 2), x_swap(after(parts[2], received))]
-        weights_a = [sent, received, near_sent, near_received] + list(chip) + parts_a + near_a
+        weights_a = [sent, received, near_sent, near_received] + chip + parts_a + near_a
         near_conv = core_swap(after(conv_w, near_received, *near_a))
     else:
         taps = lax.psum(taps[0], "roll").astype(BF)

time: 63.9 us -> 63.1 us (0.987)
  waiting for transfers between devices: 9.44 us -> 19.3 us
  starting transfers between devices: 23.2 us -> 16.4 us
  local copies, waits for them, and re-layouts: 6.28 us -> 2.2 us
    unnamed x32 -> x20, local copies, waits for them, and re-layouts: 6.2 us -> 2.09 us
    ppermute x5, waiting for transfers between devices: 4.5 us -> 8.56 us  [x_swap(): return lax.ppermute(x, 'roll', [(i, i ^ 2) for i in range(rolls)])]
    ppermute x6 -> x5, starting transfers between devices: 8.18 us -> 4.33 us  [seq_swap(): return lax.ppermute(x, 'seq', [(i, i ^ bits) for i in range(seqs)])]
    ppermute x15 -> x17, waiting for transfers between devices: 3.48 us -> 7.25 us  [core_swap(): return lax.ppermute(x, 'roll', [(i, i ^ 1) for i in range(rolls)])]
    ppermute x1, waiting for transfers between devices: 1.45 us -> 3.5 us  [per_device(): moved = lax.ppermute(after(pack, own), ('seq', 'roll'), moves)]
    ppermute x1, starting transfers between devices: 3.54 us -> 1.53 us  [per_device(): moved = lax.ppermute(after(pack, own), ('seq', 'roll'), moves)]
    ppermute x5, starting transfers between devices: 7.74 us -> 6.08 us  [x_swap(): return lax.ppermute(x, 'roll', [(i, i ^ 2) for i in range(rolls)])]
    ppermute x15 -> x17, starting transfers between devices: 3.78 us -> 4.44 us  [core_swap(): return lax.ppermute(x, 'roll', [(i, i ^ 1) for i in range(rolls)])]
  transfers between devices with their start and end apart: 27 -> 28, of which waited for: 11 -> 9; matrix products, arithmetic and copies ran while one was open for 0% -> 2% of each run, Pallas kernels for 22% -> 28%
where the time goes in v10:
time: 63.1 us; the launch traced here: 62.9 us
  Pallas kernels  22.8 us (36%)
  waiting for transfers between devices  19.3 us (31%)
  starting transfers between devices  16.4 us (26%)
  local copies, waits for them, and re-layouts  2.2 us (3%)
  other arithmetic  1.18 us (2%)
  between operations  1.01 us (2%)
    pallas_call x1, Pallas kernels, per_device(): pl.pallas_call(functools.partial(rows_kernel, split), out_shape=(jax.Shap...  9.43 us
    ppermute x5, waiting for transfers between devices, x_swap(): return lax.ppermute(x, 'roll', [(i, i ^ 2) for i in range(rolls)])  8.56 us
    ppermute x17, waiting for transfers between devices, core_swap(): return lax.ppermute(x, 'roll', [(i, i ^ 1) for i in range(rolls)])  7.25 us
    ppermute x5, starting transfers between devices, x_swap(): return lax.ppermute(x, 'roll', [(i, i ^ 2) for i in range(rolls)])  6.08 us
    pallas_call x1, Pallas kernels, per_device(): pl.pallas_call(functools.partial(last_kernel, split), out_shape=jax.Shape...  4.85 us
    ppermute x17, starting transfers between devices, core_swap(): return lax.ppermute(x, 'roll', [(i, i ^ 1) for i in range(rolls)])  4.44 us
    ppermute x5, starting transfers between devices, seq_swap(): return lax.ppermute(x, 'seq', [(i, i ^ bits) for i in range(seqs)])  4.33 us
    ppermute x1, waiting for transfers between devices, per_device(): moved = lax.ppermute(after(pack, own), ('seq', 'roll'), moves)  3.5 us
  transfers between devices with their start and end apart: 28, of which 9 were waited for; matrix products, arithmetic and copies ran while one was open for 2% of the time, Pallas kernels for 28%

profile of v10, /device:TPU:0, one launch (start us, length us, event | category | flops | bytes accessed | tf_op | source)
XLA Modules:
  0.0 62.9 jit_solution(8225334940569947989)
XLA Ops:
  0.0 0.5 collective-permute-start.6
  0.6 3.2 %shard_map.109 = (bf16[64,1280]{1,0:T(8,128)(2,1)}, f32[64,640]{1,0:T(8,128)}, bf16[80,1280]{1,0:T(8,128)(2,1)}, bf16[80,2304]{1,0:T(8,128)(2,1)}, bf16[80,2304]{1,0:T(8,128)(2,1)}) custom-call(f32[30,1280]{1,0:T(8,128)} %embed.1, f32[1280]{0:T(1024)} %brk.1, f32[2,1280]{1,0:T(2,128)} %gain_in.1, bf16[2,320,640]{2,1,0:T(8,128)(2,1)} %rest_2_.2, ...), custom_call_target="tpu_custom_call" | custom-call | tf_op jit(solution)/shard_map/pallas_call | solution.py:482
  3.8 0.5 collective-permute-start.1
  4.5 1.1 %collective-permute-done = s32[384]{0:T(512)S(1)} collective-permute-done((s32[384]{0:T(512)S(1)}, s32[384]{0:T(512)S(1)}, u32[]{:S(2)}, u32[]{:S(2)}) %collective-permute-start) | collective-permute-done | bytes 1568 | tf_op jit(solution)/shard_map/ppermute | solution.py:466
  5.6 0.9 %fusion.1 = (bf16[64,640]{1,0:T(8,128)(2,1)S(1)}, f32[64,640]{1,0:T(8,128)S(1)}) fusion(f32[64,640]{1,0:T(8,128)} %get-tuple-element.38, f32[64,640]{1,0:T(8,128)S(1)} %collective-permute-done.1), kind=kLoop, calls=%fused_computation.11 | loop fusion | flops 81920 | bytes 573440 | tf_op jit(solution)/shard_map/convert_element_type | solution.py:506
  6.6 2.9 %collective-permute-start.4 = (bf16[64,640]{1,0:T(8,128)(2,1)S(1)}, bf16[64,640]{1,0:T(8,128)(2,1)S(1)}, u32[]{:S(2)}, u32[]{:S(2)}) collective-permute-start(bf16[64,640]{1,0:T(8,128)(2,1)S(1)} %get-tuple-element.73), channel_id=1, source_target_pairs={{0,2},{1,3},{2,0},{3,1},{4,6},{5,7},{6,4},{7,5},{8,10},{9,11},{10,... | collective-permute-start | bytes 245768 | tf_op jit(solution)/shard_map/ppermute | solution.py:469
  9.4 1.5 %collective-permute-start.2 = (s32[2,384]{1,0:T(2,128)S(1)}, s32[2,384]{1,0:T(2,128)S(1)}, u32[]{:S(2)}, u32[]{:S(2)}) collective-permute-start(s32[2,384]{1,0:T(2,128)S(1)} %pad_add_fusion), channel_id=1, source_target_pairs={{0,4},{1,29},{2,6},{3,31},{4,8},{5,1},{6,10},{7,3},{8,12},{9,5},{1... | collective-permute-start | bytes 9224 | tf_op jit(solution)/shard_map/ppermute | solution.py:511
  11.6 0.6 collective-permute-start.11
  12.2 3.5 %collective-permute-done.2 = s32[2,384]{1,0:T(2,128)S(1)} collective-permute-done((s32[2,384]{1,0:T(2,128)S(1)}, s32[2,384]{1,0:T(2,128)S(1)}, u32[]{:S(2)}, u32[]{:S(2)}) %collective-permute-start.2) | collective-permute-done | bytes 3104 | tf_op jit(solution)/shard_map/ppermute | solution.py:511
  15.8 1.2 %shard_map.110 = (f32[32,3200]{1,0:T(8,128)S(1)}, bf16[32,3200]{1,0:T(8,128)(2,1)S(1)}) custom-call(f32[64,640]{1,0:T(8,128)S(1)} %get-tuple-element.74.own, bf16[64,640]{1,0:T(8,128)(2,1)S(1)} %collective-permute-done.4.other, f32[2,640]{1,0:T(2,128)S(1)} %copy-done.5, bf16[2,160,3200]{2,1,0:T(8,128)(2,1)S(1)} %copy-done), custom_call_target="tpu_custom_call" | custom-call | tf_op jit(solution)/shard_map/pallas_call | solution.py:524
  17.1 0.6 collective-permute-start.3
  17.7 0.5 collective-permute-done.11.rest_6_
  18.2 2.1 %collective-permute-start.14 = (bf16[80,1280]{1,0:T(8,128)(2,1)}, bf16[80,1280]{1,0:T(8,128)(2,1)}, u32[]{:S(2)}, u32[]{:S(2)}) collective-permute-start(bf16[80,1280]{1,0:T(8,128)(2,1)} %collective-permute-done.11.rest_6_), channel_id=1, source_target_pairs={{0,12},{4,8},{8,4},{12,0},{16,28},{20,24},{24,20},{28,16},{1,13},{... | collective-permute-start | bytes 614408 | tf_op jit(solution)/shard_map/ppermute | solution.py:472
  20.3 0.4 collective-permute-start.13
  20.7 0.9 %collective-permute-start.12 = (bf16[80,1280]{1,0:T(8,128)(2,1)}, bf16[80,1280]{1,0:T(8,128)(2,1)}, u32[]{:S(2)}, u32[]{:S(2)}) collective-permute-start(bf16[80,1280]{1,0:T(8,128)(2,1)} %collective-permute-done.11.rest_6_), channel_id=1, source_target_pairs={{0,4},{4,0},{8,12},{12,8},{16,20},{20,16},{24,28},{28,24},{1,5},{5... | collective-permute-start | bytes 614408 | tf_op jit(solution)/shard_map/ppermute | solution.py:472
  21.7 0.5 collective-permute-start.15
  22.3 1.6 %collective-permute-start.8 = (bf16[32,3200]{1,0:T(8,128)(2,1)S(1)}, bf16[32,3200]{1,0:T(8,128)(2,1)}, u32[]{:S(2)}, u32[]{:S(2)}) collective-permute-start(bf16[32,3200]{1,0:T(8,128)(2,1)S(1)} %add_convert_fusion.rest_0_), channel_id=1, source_target_pairs={{0,2},{1,3},{2,0},{3,1},{4,6},{5,7},{6,4},{7,5},{8,10},{9,11},{10,... | collective-permute-start | bytes 614408 | tf_op jit(solution)/shard_map/ppermute | solution.py:469
  23.9 1.1 %copy-done.2 = bf16[2,320,640]{2,1,0:T(8,128)(2,1)S(1)} copy-done((bf16[2,320,640]{2,1,0:T(8,128)(2,1)S(1)}, bf16[2,320,640]{2,1,0:T(8,128)(2,1)}, u32[]{:S(2)}) %copy-start.2) | copy-done | bytes 819224
  25.1 0.9 %copy-done.3 = bf16[64,1280]{1,0:T(8,128)(2,1)S(1)} copy-done((bf16[64,1280]{1,0:T(8,128)(2,1)S(1)}, bf16[64,1280]{1,0:T(8,128)(2,1)}, u32[]{:S(2)}) %copy-start.3) | copy-done | bytes 163864
  26.0 2.5 %shard_map.111 = (bf16[1008,320]{1,0:T(8,128)(2,1)S(1)}, bf16[1008,64]{1,0:T(8,128)(2,1)S(1)}, bf16[384,1280]{1,0:T(8,128)(2,1)S(1)}, bf16[640,640]{1,0:T(8,128)(2,1)S(1)}) custom-call(s32[2]{0:T(128)S(1)} %pad_add_fusion.1.span, s32[1,1280]{1,0:T(1,128)S(1)} %broadcast_in_dim.6.near, bf16[64,1280]{1,0:T(8,128)(2,1)S(1)} %copy-done.3, ...), custom_call_target="tpu_custom_call" | custom-call | tf_op jit(solution)/shard_map/pallas_call | solution.py:553
  28.6 4.8 %collective-permute-done.15.rest_5_ = bf16[80,2304]{1,0:T(8,128)(2,1)S(1)} collective-permute-done((bf16[80,2304]{1,0:T(8,128)(2,1)}, bf16[80,2304]{1,0:T(8,128)(2,1)S(1)}, u32[]{:S(2)}, u32[]{:S(2)}) %collective-permute-start.15) | collective-permute-done | bytes 368672 | tf_op jit(solution)/shard_map/ppermute | solution.py:469
  33.4 0.5 collective-permute-start.17
  34.4 3.3 %collective-permute-done.8.rest_1_ = bf16[32,3200]{1,0:T(8,128)(2,1)} collective-permute-done((bf16[32,3200]{1,0:T(8,128)(2,1)S(1)}, bf16[32,3200]{1,0:T(8,128)(2,1)}, u32[]{:S(2)}, u32[]{:S(2)}) %collective-permute-start.8) | collective-permute-done | bytes 204832 | tf_op jit(solution)/shard_map/ppermute | solution.py:469
  37.7 1.6 %collective-permute-done.10.rest_3_ = bf16[32,3200]{1,0:T(8,128)(2,1)S(1)} collective-permute-done((bf16[32,3200]{1,0:T(8,128)(2,1)}, bf16[32,3200]{1,0:T(8,128)(2,1)S(1)}, u32[]{:S(2)}, u32[]{:S(2)}) %collective-permute-start.10) | collective-permute-done | bytes 204832 | tf_op jit(solution)/shard_map/ppermute | solution.py:466
  39.8 3.9 %collective-permute-done.9.rest_2_ = bf16[32,3200]{1,0:T(8,128)(2,1)S(1)} collective-permute-done((bf16[32,3200]{1,0:T(8,128)(2,1)S(1)}, bf16[32,3200]{1,0:T(8,128)(2,1)S(1)}, u32[]{:S(2)}, u32[]{:S(2)}) %collective-permute-start.9) | collective-permute-done | bytes 204832 | tf_op jit(solution)/shard_map/ppermute | solution.py:466
  44.0 0.6 collective-permute-start.21
  44.5 0.5 collective-permute-start.23
  45.1 9.4 %shard_map.112 = (bf16[1008,640]{1,0:T(8,128)(2,1)S(1)}, bf16[496,1280]{1,0:T(8,128)(2,1)S(1)}) custom-call(s32[2]{0:T(128)S(1)} %pad_add_fusion.1.span, bf16[1008,320]{1,0:T(8,128)(2,1)S(1)} %get-tuple-element.46.hot5, bf16[1008,64]{1,0:T(8,128)(2,1)S(1)} %get-tuple-element.47.hot1, f32[2,640]{1,0:T(2,128)S(1)} %copy-done.6, f32[2,1280]{1,0:T(2,128)S(1)} %copy-done.4, ...), custom_call_target="tpu_custom_call" | custom-call | tf_op jit(solution)/shard_map/pallas_call | solution.py:577
  54.6 0.5 collective-permute-start.26
  55.6 1.6 %shard_map.113.rest_0_ = f32[496,640]{1,0:T(8,128)S(1)} custom-call(bf16[1008,640]{1,0:T(8,128)(2,1)S(1)} %get-tuple-element.61.ci, bf16[2,160,3200]{2,1,0:T(8,128)(2,1)S(1)} %copy-done, bf16[2,160,3200]{2,1,0:T(8,128)(2,1)S(1)} %collective-permute-done.20.near_conv.rest_3_), custom_call_target="tpu_custom_call" | custom-call | tf_op jit(solution)/shard_map/pallas_call | solution.py:597
  57.3 0.5 collective-permute-done.27.rest_12_
  57.8 4.8 %shard_map.114 = bf16[496,1280]{1,0:T(8,128)(2,1)} custom-call(bf16[1008,640]{1,0:T(8,128)(2,1)S(1)} %get-tuple-element.61.ci, bf16[496,1280]{1,0:T(8,128)(2,1)S(1)} %get-tuple-element.62.hid, f32[2,640]{1,0:T(2,128)S(1)} %copy-done.6, f32[496,640]{1,0:T(8,128)S(1)} %shard_map.113.rest_0_, bf16[2,160,3200]{2,1,0:T(8,128)(2,1)S(1)} %copy-done, ...), custom_call_target="tpu_custom_call" | custom-call | tf_op jit(solution)/shard_map/pallas_call | solution.py:607
  (62 shorter events, 2.7 us)
Async XLA Ops:
  0.0 15.7 %copy-start.5 = (f32[2,640]{1,0:T(2,128)S(1)}, f32[2,640]{1,0:T(2,128)}, u32[]{:S(2)}) copy-start(f32[2,640]{1,0:T(2,128)} %gain_mid.1) | copy-start | bytes 15364
  0.0 15.7 %collective-permute-start.6 = (bf16[2,320,640]{2,1,0:T(8,128)(2,1)}, bf16[2,320,640]{2,1,0:T(8,128)(2,1)}, u32[]{:S(2)}, u32[]{:S(2)}) collective-permute-start(bf16[2,320,640]{2,1,0:T(8,128)(2,1)} %rest_2_.2), channel_id=1, source_target_pairs={{0,1},{1,0},{2,3},{3,2},{4,5},{5,4},{6,7},{7,6},{8,9},{9,8},{10,11... | collective-permute-start | bytes 2457608 | tf_op jit(solution)/shard_map/ppermute | solution.py:466
  0.5 15.2 %collective-permute-start.5 = (bf16[2,160,1280]{2,1,0:T(8,128)(2,1)}, bf16[2,160,1280]{2,1,0:T(8,128)(2,1)}, u32[]{:S(2)}, u32[]{:S(2)}) collective-permute-start(bf16[2,160,1280]{2,1,0:T(8,128)(2,1)} %rest_2_.3), channel_id=1, source_target_pairs={{0,1},{1,0},{2,3},{3,2},{4,5},{5,4},{6,7},{7,6},{8,9},{9,8},{10,11... | collective-permute-start | bytes 2457608 | tf_op jit(solution)/shard_map/ppermute | solution.py:466
  3.8 1.8 %collective-permute-start.1 = (f32[64,640]{1,0:T(8,128)}, f32[64,640]{1,0:T(8,128)S(1)}, u32[]{:S(2)}, u32[]{:S(2)}) collective-permute-start(f32[64,640]{1,0:T(8,128)} %get-tuple-element.38), channel_id=1, source_target_pairs={{0,1},{1,0},{2,3},{3,2},{4,5},{5,4},{6,7},{7,6},{8,9},{9,8},{10,11... | collective-permute-start | bytes 491528 | tf_op jit(solution)/shard_map/ppermute | solution.py:466
  4.4 1.2 %collective-permute-start = (s32[384]{0:T(512)S(1)}, s32[384]{0:T(512)S(1)}, u32[]{:S(2)}, u32[]{:S(2)}) collective-permute-start(s32[384]{0:T(512)S(1)} %get-tuple-element.78), channel_id=1, source_target_pairs={{0,1},{1,0},{2,3},{3,2},{4,5},{5,4},{6,7},{7,6},{8,9},{9,8},{10,11... | collective-permute-start | bytes 4616 | tf_op jit(solution)/shard_map/ppermute | solution.py:466
  6.6 9.2 %collective-permute-start.4 = (bf16[64,640]{1,0:T(8,128)(2,1)S(1)}, bf16[64,640]{1,0:T(8,128)(2,1)S(1)}, u32[]{:S(2)}, u32[]{:S(2)}) collective-permute-start(bf16[64,640]{1,0:T(8,128)(2,1)S(1)} %get-tuple-element.73), channel_id=1, source_target_pairs={{0,2},{1,3},{2,0},{3,1},{4,6},{5,7},{6,4},{7,5},{8,10},{9,11},{10,... | collective-permute-start | bytes 245768 | tf_op jit(solution)/shard_map/ppermute | solution.py:469
  9.4 6.3 %collective-permute-start.2 = (s32[2,384]{1,0:T(2,128)S(1)}, s32[2,384]{1,0:T(2,128)S(1)}, u32[]{:S(2)}, u32[]{:S(2)}) collective-permute-start(s32[2,384]{1,0:T(2,128)S(1)} %pad_add_fusion), channel_id=1, source_target_pairs={{0,4},{1,29},{2,6},{3,31},{4,8},{5,1},{6,10},{7,3},{8,12},{9,5},{1... | collective-permute-start | bytes 9224 | tf_op jit(solution)/shard_map/ppermute | solution.py:511
  11.6 6.6 %collective-permute-start.11 = (bf16[80,1280]{1,0:T(8,128)(2,1)}, bf16[80,1280]{1,0:T(8,128)(2,1)}, u32[]{:S(2)}, u32[]{:S(2)}) collective-permute-start(bf16[80,1280]{1,0:T(8,128)(2,1)} %get-tuple-element.53), channel_id=1, source_target_pairs={{0,2},{1,3},{2,0},{3,1},{4,6},{5,7},{6,4},{7,5},{8,10},{9,11},{10,... | collective-permute-start | bytes 614408 | tf_op jit(solution)/shard_map/ppermute | solution.py:469
  16.9 4.7 %collective-permute-start.7 = (bf16[32,3200]{1,0:T(8,128)(2,1)S(1)}, bf16[32,3200]{1,0:T(8,128)(2,1)S(1)}, u32[]{:S(2)}, u32[]{:S(2)}) collective-permute-start(bf16[32,3200]{1,0:T(8,128)(2,1)S(1)} %get-tuple-element.43), channel_id=1, source_target_pairs={{0,1},{1,0},{2,3},{3,2},{4,5},{5,4},{6,7},{7,6},{8,9},{9,8},{10,11... | collective-permute-start | bytes 614408 | tf_op jit(solution)/shard_map/ppermute | solution.py:466
  17.1 5.1 %collective-permute-start.3 = (s32[384]{0:T(512)S(1)}, s32[384]{0:T(512)S(1)}, u32[]{:S(2)}, u32[]{:S(2)}) collective-permute-start(s32[384]{0:T(512)S(1)} %get-tuple-element.71), channel_id=1, source_target_pairs={{0,1},{1,0},{2,3},{3,2},{4,5},{5,4},{6,7},{7,6},{8,9},{9,8},{10,11... | collective-permute-start | bytes 4616 | tf_op jit(solution)/shard_map/ppermute | solution.py:466
  18.2 10.4 %collective-permute-start.14 = (bf16[80,1280]{1,0:T(8,128)(2,1)}, bf16[80,1280]{1,0:T(8,128)(2,1)}, u32[]{:S(2)}, u32[]{:S(2)}) collective-permute-start(bf16[80,1280]{1,0:T(8,128)(2,1)} %collective-permute-done.11.rest_6_), channel_id=1, source_target_pairs={{0,12},{4,8},{8,4},{12,0},{16,28},{20,24},{24,20},{28,16},{1,13},{... | collective-permute-start | bytes 614408 | tf_op jit(solution)/shard_map/ppermute | solution.py:472
  20.3 13.1 %collective-permute-start.13 = (bf16[80,1280]{1,0:T(8,128)(2,1)}, bf16[80,1280]{1,0:T(8,128)(2,1)}, u32[]{:S(2)}, u32[]{:S(2)}) collective-permute-start(bf16[80,1280]{1,0:T(8,128)(2,1)} %collective-permute-done.11.rest_6_), channel_id=1, source_target_pairs={{0,8},{4,12},{8,0},{12,4},{16,24},{20,28},{24,16},{28,20},{1,9},{5... | collective-permute-start | bytes 614408 | tf_op jit(solution)/shard_map/ppermute | solution.py:472
  20.7 12.6 %collective-permute-start.12 = (bf16[80,1280]{1,0:T(8,128)(2,1)}, bf16[80,1280]{1,0:T(8,128)(2,1)}, u32[]{:S(2)}, u32[]{:S(2)}) collective-permute-start(bf16[80,1280]{1,0:T(8,128)(2,1)} %collective-permute-done.11.rest_6_), channel_id=1, source_target_pairs={{0,4},{4,0},{8,12},{12,8},{16,20},{20,16},{24,28},{28,24},{1,5},{5... | collective-permute-start | bytes 614408 | tf_op jit(solution)/shard_map/ppermute | solution.py:472
  21.7 11.7 %collective-permute-start.15 = (bf16[80,2304]{1,0:T(8,128)(2,1)}, bf16[80,2304]{1,0:T(8,128)(2,1)S(1)}, u32[]{:S(2)}, u32[]{:S(2)}) collective-permute-start(bf16[80,2304]{1,0:T(8,128)(2,1)} %get-tuple-element.56), channel_id=1, source_target_pairs={{0,2},{1,3},{2,0},{3,1},{4,6},{5,7},{6,4},{7,5},{8,10},{9,11},{10,... | collective-permute-start | bytes 1105928 | tf_op jit(solution)/shard_map/ppermute | solution.py:469
  22.3 15.4 %collective-permute-start.8 = (bf16[32,3200]{1,0:T(8,128)(2,1)S(1)}, bf16[32,3200]{1,0:T(8,128)(2,1)}, u32[]{:S(2)}, u32[]{:S(2)}) collective-permute-start(bf16[32,3200]{1,0:T(8,128)(2,1)S(1)} %add_convert_fusion.rest_0_), channel_id=1, source_target_pairs={{0,2},{1,3},{2,0},{3,1},{4,6},{5,7},{6,4},{7,5},{8,10},{9,11},{10,... | collective-permute-start | bytes 614408 | tf_op jit(solution)/shard_map/ppermute | solution.py:469
  26.0 18.5 %copy-start.9 = (bf16[80,2304]{1,0:T(8,128)(2,1)S(1)}, bf16[80,2304]{1,0:T(8,128)(2,1)}, u32[]{:S(2)}) copy-start(bf16[80,2304]{1,0:T(8,128)(2,1)} %get-tuple-element.66) | copy-start | bytes 1105924
  26.0 19.1 %copy-start.4 = (f32[2,1280]{1,0:T(2,128)S(1)}, f32[2,1280]{1,0:T(2,128)}, u32[]{:S(2)}) copy-start(f32[2,1280]{1,0:T(2,128)} %gain_in.1) | copy-start | bytes 30724
  26.0 19.1 %copy-start.6 = (f32[2,640]{1,0:T(2,128)S(1)}, f32[2,640]{1,0:T(2,128)}, u32[]{:S(2)}) copy-start(f32[2,640]{1,0:T(2,128)} %gain_out.3) | copy-start | bytes 15364
  33.4 4.3 %collective-permute-start.16 = (bf16[80,1280]{1,0:T(8,128)(2,1)}, bf16[80,1280]{1,0:T(8,128)(2,1)S(1)}, u32[]{:S(2)}, u32[]{:S(2)}) collective-permute-start(bf16[80,1280]{1,0:T(8,128)(2,1)} %collective-permute-done.11.rest_6_), channel_id=1, source_target_pairs={{0,1},{1,0},{2,3},{3,2},{4,5},{5,4},{6,7},{7,6},{8,9},{9,8},{10,11... | collective-permute-start | bytes 614408 | tf_op jit(solution)/shard_map/ppermute | solution.py:466
  33.4 4.3 %collective-permute-start.17 = (bf16[80,1280]{1,0:T(8,128)(2,1)}, bf16[80,1280]{1,0:T(8,128)(2,1)S(1)}, u32[]{:S(2)}, u32[]{:S(2)}) collective-permute-start(bf16[80,1280]{1,0:T(8,128)(2,1)} %collective-permute-done.12.rest_7_), channel_id=1, source_target_pairs={{0,1},{1,0},{2,3},{3,2},{4,5},{5,4},{6,7},{7,6},{8,9},{9,8},{10,11... | collective-permute-start | bytes 614408 | tf_op jit(solution)/shard_map/ppermute | solution.py:466
  33.9 3.8 %collective-permute-start.18 = (bf16[80,1280]{1,0:T(8,128)(2,1)}, bf16[80,1280]{1,0:T(8,128)(2,1)S(1)}, u32[]{:S(2)}, u32[]{:S(2)}) collective-permute-start(bf16[80,1280]{1,0:T(8,128)(2,1)} %collective-permute-done.13.rest_8_), channel_id=1, source_target_pairs={{0,1},{1,0},{2,3},{3,2},{4,5},{5,4},{6,7},{7,6},{8,9},{9,8},{10,11... | collective-permute-start | bytes 614408 | tf_op jit(solution)/shard_map/ppermute | solution.py:466
  33.9 3.7 %collective-permute-start.19 = (bf16[80,1280]{1,0:T(8,128)(2,1)}, bf16[80,1280]{1,0:T(8,128)(2,1)S(1)}, u32[]{:S(2)}, u32[]{:S(2)}) collective-permute-start(bf16[80,1280]{1,0:T(8,128)(2,1)} %collective-permute-done.14.rest_9_), channel_id=1, source_target_pairs={{0,1},{1,0},{2,3},{3,2},{4,5},{5,4},{6,7},{7,6},{8,9},{9,8},{10,11... | collective-permute-start | bytes 614408 | tf_op jit(solution)/shard_map/ppermute | solution.py:466
  37.6 1.7 %collective-permute-start.10 = (bf16[32,3200]{1,0:T(8,128)(2,1)}, bf16[32,3200]{1,0:T(8,128)(2,1)S(1)}, u32[]{:S(2)}, u32[]{:S(2)}) collective-permute-start(bf16[32,3200]{1,0:T(8,128)(2,1)} %collective-permute-done.8.rest_1_), channel_id=1, source_target_pairs={{0,1},{1,0},{2,3},{3,2},{4,5},{5,4},{6,7},{7,6},{8,9},{9,8},{10,11... | collective-permute-start | bytes 614408 | tf_op jit(solution)/shard_map/ppermute | solution.py:466
  39.3 16.3 %collective-permute-start.20 = (bf16[2,160,3200]{2,1,0:T(8,128)(2,1)S(1)}, bf16[2,160,3200]{2,1,0:T(8,128)(2,1)S(1)}, u32[]{:S(2)}, u32[]{:S(2)}) collective-permute-start(bf16[2,160,3200]{2,1,0:T(8,128)(2,1)S(1)} %copy-done), channel_id=1, source_target_pairs={{0,1},{1,0},{2,3},{3,2},{4,5},{5,4},{6,7},{7,6},{8,9},{9,8},{10,11... | collective-permute-start | bytes 6144008 | tf_op jit(solution)/shard_map/ppermute | solution.py:466
  39.4 4.2 %collective-permute-start.9 = (bf16[32,3200]{1,0:T(8,128)(2,1)S(1)}, bf16[32,3200]{1,0:T(8,128)(2,1)S(1)}, u32[]{:S(2)}, u32[]{:S(2)}) collective-permute-start(bf16[32,3200]{1,0:T(8,128)(2,1)S(1)} %add_convert_fusion.rest_0_), channel_id=1, source_target_pairs={{0,1},{1,0},{2,3},{3,2},{4,5},{5,4},{6,7},{7,6},{8,9},{9,8},{10,11... | collective-permute-start | bytes 614408 | tf_op jit(solution)/shard_map/ppermute | solution.py:466
  43.7 10.9 %collective-permute-start.22 = (bf16[80,2304]{1,0:T(8,128)(2,1)S(1)}, bf16[80,2304]{1,0:T(8,128)(2,1)S(1)}, u32[]{:S(2)}, u32[]{:S(2)}) collective-permute-start(bf16[80,2304]{1,0:T(8,128)(2,1)S(1)} %collective-permute-done.15.rest_5_), channel_id=1, source_target_pairs={{0,8},{4,12},{8,0},{12,4},{16,24},{20,28},{24,16},{28,20},{1,9},{5... | collective-permute-start | bytes 1105928 | tf_op jit(solution)/shard_map/ppermute | solution.py:472
  44.0 11.1 %collective-permute-start.21 = (bf16[80,2304]{1,0:T(8,128)(2,1)S(1)}, bf16[80,2304]{1,0:T(8,128)(2,1)S(1)}, u32[]{:S(2)}, u32[]{:S(2)}) collective-permute-start(bf16[80,2304]{1,0:T(8,128)(2,1)S(1)} %collective-permute-done.15.rest_5_), channel_id=1, source_target_pairs={{0,4},{4,0},{8,12},{12,8},{16,20},{20,16},{24,28},{28,24},{1,5},{5... | collective-permute-start | bytes 1105928 | tf_op jit(solution)/shard_map/ppermute | solution.py:472
  44.5 10.7 %collective-permute-start.23 = (bf16[80,2304]{1,0:T(8,128)(2,1)S(1)}, bf16[80,2304]{1,0:T(8,128)(2,1)S(1)}, u32[]{:S(2)}, u32[]{:S(2)}) collective-permute-start(bf16[80,2304]{1,0:T(8,128)(2,1)S(1)} %copy-done.9), channel_id=1, source_target_pairs={{0,2},{1,3},{2,0},{3,1},{4,6},{5,7},{6,4},{7,5},{8,10},{9,11},{10,... | collective-permute-start | bytes 1105928 | tf_op jit(solution)/shard_map/ppermute | solution.py:469
  54.5 2.7 %collective-permute-start.24 = (bf16[80,2304]{1,0:T(8,128)(2,1)S(1)}, bf16[80,2304]{1,0:T(8,128)(2,1)S(1)}, u32[]{:S(2)}, u32[]{:S(2)}) collective-permute-start(bf16[80,2304]{1,0:T(8,128)(2,1)S(1)} %collective-permute-done.15.rest_5_), channel_id=1, source_target_pairs={{0,1},{1,0},{2,3},{3,2},{4,5},{5,4},{6,7},{7,6},{8,9},{9,8},{10,11... | collective-permute-start | bytes 1105928 | tf_op jit(solution)/shard_map/ppermute | solution.py:466
  54.6 2.6 %collective-permute-start.26 = (bf16[80,2304]{1,0:T(8,128)(2,1)S(1)}, bf16[80,2304]{1,0:T(8,128)(2,1)S(1)}, u32[]{:S(2)}, u32[]{:S(2)}) collective-permute-start(bf16[80,2304]{1,0:T(8,128)(2,1)S(1)} %collective-permute-done.22.rest_7_), channel_id=1, source_target_pairs={{0,1},{1,0},{2,3},{3,2},{4,5},{5,4},{6,7},{7,6},{8,9},{9,8},{10,11... | collective-permute-start | bytes 1105928 | tf_op jit(solution)/shard_map/ppermute | solution.py:466
  55.1 2.2 %collective-permute-start.25 = (bf16[80,2304]{1,0:T(8,128)(2,1)S(1)}, bf16[80,2304]{1,0:T(8,128)(2,1)S(1)}, u32[]{:S(2)}, u32[]{:S(2)}) collective-permute-start(bf16[80,2304]{1,0:T(8,128)(2,1)S(1)} %collective-permute-done.21.rest_6_), channel_id=1, source_target_pairs={{0,1},{1,0},{2,3},{3,2},{4,5},{5,4},{6,7},{7,6},{8,9},{9,8},{10,11... | collective-permute-start | bytes 1105928 | tf_op jit(solution)/shard_map/ppermute | solution.py:466
  55.2 2.7 %collective-permute-start.27 = (bf16[80,2304]{1,0:T(8,128)(2,1)S(1)}, bf16[80,2304]{1,0:T(8,128)(2,1)S(1)}, u32[]{:S(2)}, u32[]{:S(2)}) collective-permute-start(bf16[80,2304]{1,0:T(8,128)(2,1)S(1)} %collective-permute-done.23.rest_8_), channel_id=1, source_target_pairs={{0,1},{1,0},{2,3},{3,2},{4,5},{5,4},{6,7},{7,6},{8,9},{9,8},{10,11... | collective-permute-start | bytes 1105928 | tf_op jit(solution)/shard_map/ppermute | solution.py:466
  (6 other events, 38.2 us)

commit v11 on v10

--- a/solution.py
+++ b/solution.py
@@ -505,12 +505,12 @@
         own = part + after(core_swap(part), theirs)
         other = x_swap(own.astype(BF))
         far_a = x_swap(after(parts[0], own))
+        far_b = x_swap(after(parts[1], own))
         pack = jnp.stack([jnp.where(low, *ends), theirs])
         places = [(s, r) for s in range(seqs) for r in range(rolls)]
         moves = [(s * rolls + r, (s + (1, -1)[r % 2]) % seqs * rolls + r) for s, r in places]
         moved = lax.ppermute(after(pack, own), ("seq", "roll"), moves)
         other = after(other, moved, near_out, near_in)
-        far_b = x_swap(after(parts[1], other))
         came = core_swap(moved[1])
         before, behind = jnp.where(low, moved[0], came), jnp.where(low, came, moved[0])
     else:
@@ -565,10 +565,10 @@
         received = after(received, hot1)
         near_received = core_swap(received)
         near_a = [core_swap(after(p, hot1, far_b)) for p in parts_a]
-        relay = after(far_b, received, near_sent)
+        relay = after(far_b, received)
         parts_b = [far_b, seq_swap(relay, 1), seq_swap(relay, 2), x_swap(after(parts[2], received))]
         weights_a = [sent, received, near_sent, near_received] + chip + parts_a + near_a
-        near_conv = core_swap(after(conv_w, near_received, *near_a))
+        near_conv = core_swap(after(conv_w, near_received, near_sent, *near_a))
     else:
         taps = lax.psum(taps[0], "roll").astype(BF)
         gather = lambda w: lax.all_gather(w, "roll", axis=0, tiled=True)

time: 63.1 us -> 58.5 us (0.927)
  waiting for transfers between devices: 19.3 us -> 10.4 us
  starting transfers between devices: 16.4 us -> 19.3 us
  Pallas kernels: 22.8 us -> 24.3 us
  local copies, waits for them, and re-layouts: 2.2 us -> 1.06 us
  other arithmetic: 1.18 us -> 2.1 us
    ppermute x5, waiting for transfers between devices: 8.56 us -> 3.07 us  [x_swap(): return lax.ppermute(x, 'roll', [(i, i ^ 2) for i in range(rolls)])]
    ppermute x17, waiting for transfers between devices: 7.25 us -> 3.26 us  [core_swap(): return lax.ppermute(x, 'roll', [(i, i ^ 1) for i in range(rolls)])]
    ppermute x5, waiting for transfers between devices: 0.01 us -> 1.69 us  [seq_swap(): return lax.ppermute(x, 'seq', [(i, i ^ bits) for i in range(seqs)])]
    ppermute x1, starting transfers between devices: 1.53 us -> 2.84 us  [per_device(): moved = lax.ppermute(after(pack, own), ('seq', 'roll'), moves)]
    unnamed x20, local copies, waits for them, and re-layouts: 2.09 us -> 0.95 us
    ppermute x1, waiting for transfers between devices: 3.5 us -> 2.4 us  [per_device(): moved = lax.ppermute(after(pack, own), ('seq', 'roll'), moves)]
    convert_element_type x1, other arithmetic: 0.05 us -> 0.97 us  [per_device(): sent = (taps[0] + core_swap(taps[1]).astype(F32)).astype(BF)]
    ppermute x17, starting transfers between devices: 4.44 us -> 5.22 us  [core_swap(): return lax.ppermute(x, 'roll', [(i, i ^ 1) for i in range(rolls)])]
  transfers between devices with their start and end apart: 28 -> 28, of which waited for: 9 -> 10; matrix products, arithmetic and copies ran while one was open for 2% -> 4% of each run, Pallas kernels for 28% -> 32%
where the time goes in v11:
time: 58.5 us; the launch traced here: 58.3 us
  Pallas kernels  24.3 us (42%)
  starting transfers between devices  19.3 us (33%)
  waiting for transfers between devices  10.4 us (18%)
  other arithmetic  2.1 us (4%)
  local copies, waits for them, and re-layouts  1.06 us (2%)
  between operations  1 us (2%)
    pallas_call x1, Pallas kernels, per_device(): pl.pallas_call(functools.partial(rows_kernel, split), out_shape=(jax.Shap...  9.74 us
    ppermute x5, starting transfers between devices, x_swap(): return lax.ppermute(x, 'roll', [(i, i ^ 2) for i in range(rolls)])  6.77 us
    pallas_call x1, Pallas kernels, per_device(): pl.pallas_call(functools.partial(last_kernel, split), out_shape=jax.Shape...  5.45 us
    ppermute x17, starting transfers between devices, core_swap(): return lax.ppermute(x, 'roll', [(i, i ^ 1) for i in range(rolls)])  5.22 us
    ppermute x5, starting transfers between devices, seq_swap(): return lax.ppermute(x, 'seq', [(i, i ^ bits) for i in range(seqs)])  4.51 us
    ppermute x17, waiting for transfers between devices, core_swap(): return lax.ppermute(x, 'roll', [(i, i ^ 1) for i in range(rolls)])  3.26 us
    pallas_call x1, Pallas kernels, per_device(): pl.pallas_call(functools.partial(first_kernel, split), out_shape=[jax.Sha...  3.21 us
    ppermute x5, waiting for transfers between devices, x_swap(): return lax.ppermute(x, 'roll', [(i, i ^ 2) for i in range(rolls)])  3.07 us
  transfers between devices with their start and end apart: 28, of which 10 were waited for; matrix products, arithmetic and copies ran while one was open for 4% of the time, Pallas kernels for 32%

profile of v11, /device:TPU:0, one launch (start us, length us, event | category | flops | bytes accessed | tf_op | source)
XLA Modules:
  0.0 58.3 jit_solution(11835200174794914385)
XLA Ops:
  0.0 0.5 collective-permute-start.6
  0.6 3.2 %shard_map.109 = (bf16[64,1280]{1,0:T(8,128)(2,1)}, f32[64,640]{1,0:T(8,128)}, bf16[80,1280]{1,0:T(8,128)(2,1)}, bf16[80,2304]{1,0:T(8,128)(2,1)}, bf16[80,2304]{1,0:T(8,128)(2,1)}) custom-call(f32[30,1280]{1,0:T(8,128)} %embed.1, f32[1280]{0:T(1024)} %brk.1, f32[2,1280]{1,0:T(2,128)} %gain_in.1, bf16[2,320,640]{2,1,0:T(8,128)(2,1)} %rest_2_.2, ...), custom_call_target="tpu_custom_call" | custom-call | tf_op jit(solution)/shard_map/pallas_call | solution.py:482
  3.8 0.5 collective-permute-start.1
  4.6 1.1 %collective-permute-done = s32[384]{0:T(512)S(1)} collective-permute-done((s32[384]{0:T(512)S(1)}, s32[384]{0:T(512)S(1)}, u32[]{:S(2)}, u32[]{:S(2)}) %collective-permute-start) | collective-permute-done | bytes 1568 | tf_op jit(solution)/shard_map/ppermute | solution.py:466
  5.7 1.0 %fusion.1 = (bf16[64,640]{1,0:T(8,128)(2,1)S(1)}, f32[64,640]{1,0:T(8,128)S(1)}) fusion(f32[64,640]{1,0:T(8,128)} %get-tuple-element.38, f32[64,640]{1,0:T(8,128)S(1)} %collective-permute-done.1), kind=kLoop, calls=%fused_computation.11 | loop fusion | flops 81920 | bytes 573440 | tf_op jit(solution)/shard_map/convert_element_type | solution.py:506
  6.6 2.8 %collective-permute-start.2 = (s32[2,384]{1,0:T(2,128)S(1)}, s32[2,384]{1,0:T(2,128)S(1)}, u32[]{:S(2)}, u32[]{:S(2)}) collective-permute-start(s32[2,384]{1,0:T(2,128)S(1)} %pad_add_fusion), channel_id=1, source_target_pairs={{0,4},{1,29},{2,6},{3,31},{4,8},{5,1},{6,10},{7,3},{8,12},{9,5},{1... | collective-permute-start | bytes 9224 | tf_op jit(solution)/shard_map/ppermute | solution.py:512
  10.1 1.6 %collective-permute-start.4 = (bf16[64,640]{1,0:T(8,128)(2,1)S(1)}, bf16[64,640]{1,0:T(8,128)(2,1)S(1)}, u32[]{:S(2)}, u32[]{:S(2)}) collective-permute-start(bf16[64,640]{1,0:T(8,128)(2,1)S(1)} %get-tuple-element.73), channel_id=1, source_target_pairs={{0,2},{1,3},{2,0},{3,1},{4,6},{5,7},{6,4},{7,5},{8,10},{9,11},{10,... | collective-permute-start | bytes 245768 | tf_op jit(solution)/shard_map/ppermute | solution.py:469
  11.7 2.4 %collective-permute-done.2 = s32[2,384]{1,0:T(2,128)S(1)} collective-permute-done((s32[2,384]{1,0:T(2,128)S(1)}, s32[2,384]{1,0:T(2,128)S(1)}, u32[]{:S(2)}, u32[]{:S(2)}) %collective-permute-start.2) | collective-permute-done | bytes 3104 | tf_op jit(solution)/shard_map/ppermute | solution.py:512
  14.1 0.4 collective-permute-start.3
  14.6 1.4 %collective-permute-start.11 = (bf16[80,1280]{1,0:T(8,128)(2,1)}, bf16[80,1280]{1,0:T(8,128)(2,1)}, u32[]{:S(2)}, u32[]{:S(2)}) collective-permute-start(bf16[80,1280]{1,0:T(8,128)(2,1)} %get-tuple-element.53), channel_id=1, source_target_pairs={{0,2},{1,3},{2,0},{3,1},{4,6},{5,7},{6,4},{7,5},{8,10},{9,11},{10,... | collective-permute-start | bytes 614408 | tf_op jit(solution)/shard_map/ppermute | solution.py:469
  15.9 0.7 %collective-permute-start.15 = (bf16[80,2304]{1,0:T(8,128)(2,1)}, bf16[80,2304]{1,0:T(8,128)(2,1)}, u32[]{:S(2)}, u32[]{:S(2)}) collective-permute-start(bf16[80,2304]{1,0:T(8,128)(2,1)} %get-tuple-element.56), channel_id=1, source_target_pairs={{0,2},{1,3},{2,0},{3,1},{4,6},{5,7},{6,4},{7,5},{8,10},{9,11},{10,... | collective-permute-start | bytes 1105928 | tf_op jit(solution)/shard_map/ppermute | solution.py:469
  16.6 1.8 %shard_map.110 = (f32[32,3200]{1,0:T(8,128)S(1)}, bf16[32,3200]{1,0:T(8,128)(2,1)}) custom-call(f32[64,640]{1,0:T(8,128)S(1)} %get-tuple-element.74.own, bf16[64,640]{1,0:T(8,128)(2,1)S(1)} %collective-permute-done.4.other, f32[2,640]{1,0:T(2,128)S(1)} %copy-done.5, bf16[2,160,3200]{2,1,0:T(8,128)(2,1)S(1)} %copy-done), custom_call_target="tpu_custom_call" | custom-call | tf_op jit(solution)/shard_map/pallas_call | solution.py:524
  18.5 1.2 %collective-permute-start.7 = (bf16[32,3200]{1,0:T(8,128)(2,1)}, bf16[32,3200]{1,0:T(8,128)(2,1)}, u32[]{:S(2)}, u32[]{:S(2)}) collective-permute-start(bf16[32,3200]{1,0:T(8,128)(2,1)} %get-tuple-element.43), channel_id=1, source_target_pairs={{0,1},{1,0},{2,3},{3,2},{4,5},{5,4},{6,7},{7,6},{8,9},{9,8},{10,11... | collective-permute-start | bytes 614408 | tf_op jit(solution)/shard_map/ppermute | solution.py:466
  19.7 3.1 %collective-permute-done.11.rest_6_ = bf16[80,1280]{1,0:T(8,128)(2,1)} collective-permute-done((bf16[80,1280]{1,0:T(8,128)(2,1)}, bf16[80,1280]{1,0:T(8,128)(2,1)}, u32[]{:S(2)}, u32[]{:S(2)}) %collective-permute-start.11) | collective-permute-done | bytes 204832 | tf_op jit(solution)/shard_map/ppermute | solution.py:469
  23.0 3.2 %collective-permute-start.12 = (bf16[80,1280]{1,0:T(8,128)(2,1)}, bf16[80,1280]{1,0:T(8,128)(2,1)S(1)}, u32[]{:S(2)}, u32[]{:S(2)}) collective-permute-start(bf16[80,1280]{1,0:T(8,128)(2,1)} %collective-permute-done.11.rest_6_), channel_id=1, source_target_pairs={{0,4},{4,0},{8,12},{12,8},{16,20},{20,16},{24,28},{28,24},{1,5},{5... | collective-permute-start | bytes 614408 | tf_op jit(solution)/shard_map/ppermute | solution.py:472
  26.3 1.0 %add_convert_fusion.rest_0_ = bf16[32,3200]{1,0:T(8,128)(2,1)S(1)} fusion(f32[32,3200]{1,0:T(8,128)S(1)} %get-tuple-element.42, bf16[32,3200]{1,0:T(8,128)(2,1)} %collective-permute-done.7), kind=kLoop, calls=%fused_computation | loop fusion | flops 307200 | bytes 819200 | tf_op jit(solution)/shard_map/convert_element_type | solution.py:540
  27.2 1.4 %collective-permute-start.8 = (bf16[32,3200]{1,0:T(8,128)(2,1)S(1)}, bf16[32,3200]{1,0:T(8,128)(2,1)S(1)}, u32[]{:S(2)}, u32[]{:S(2)}) collective-permute-start(bf16[32,3200]{1,0:T(8,128)(2,1)S(1)} %add_convert_fusion.rest_0_), channel_id=1, source_target_pairs={{0,2},{1,3},{2,0},{3,1},{4,6},{5,7},{6,4},{7,5},{8,10},{9,11},{10,... | collective-permute-start | bytes 614408 | tf_op jit(solution)/shard_map/ppermute | solution.py:469
  28.6 0.9 %copy-done.3 = bf16[64,1280]{1,0:T(8,128)(2,1)S(1)} copy-done((bf16[64,1280]{1,0:T(8,128)(2,1)S(1)}, bf16[64,1280]{1,0:T(8,128)(2,1)}, u32[]{:S(2)}) %copy-start.3) | copy-done | bytes 163864
  29.6 2.5 %shard_map.111 = (bf16[1008,320]{1,0:T(8,128)(2,1)S(1)}, bf16[1008,64]{1,0:T(8,128)(2,1)S(1)}, bf16[384,1280]{1,0:T(8,128)(2,1)S(1)}, bf16[640,640]{1,0:T(8,128)(2,1)S(1)}) custom-call(s32[2]{0:T(128)S(1)} %pad_add_fusion.1.span, s32[1,1280]{1,0:T(1,128)S(1)} %broadcast_in_dim.6.near, bf16[64,1280]{1,0:T(8,128)(2,1)S(1)} %copy-done.3, ...), custom_call_target="tpu_custom_call" | custom-call | tf_op jit(solution)/shard_map/pallas_call | solution.py:553
  32.2 1.7 %collective-permute-done.12.rest_7_ = bf16[80,1280]{1,0:T(8,128)(2,1)S(1)} collective-permute-done((bf16[80,1280]{1,0:T(8,128)(2,1)}, bf16[80,1280]{1,0:T(8,128)(2,1)S(1)}, u32[]{:S(2)}, u32[]{:S(2)}) %collective-permute-start.12) | collective-permute-done | bytes 204832 | tf_op jit(solution)/shard_map/ppermute | solution.py:472
  33.9 0.5 collective-permute-start.17
  34.4 0.5 collective-permute-start.19
  35.0 0.8 %collective-permute-done.16.rest_10_ = bf16[80,1280]{1,0:T(8,128)(2,1)S(1)} collective-permute-done((bf16[80,1280]{1,0:T(8,128)(2,1)}, bf16[80,1280]{1,0:T(8,128)(2,1)S(1)}, u32[]{:S(2)}, u32[]{:S(2)}) %collective-permute-start.16) | collective-permute-done | bytes 204832 | tf_op jit(solution)/shard_map/ppermute | solution.py:466
  35.9 0.3 collective-permute-done.19.rest_13_
  37.0 0.8 %collective-permute-start.21 = (bf16[80,2304]{1,0:T(8,128)(2,1)}, bf16[80,2304]{1,0:T(8,128)(2,1)S(1)}, u32[]{:S(2)}, u32[]{:S(2)}) collective-permute-start(bf16[80,2304]{1,0:T(8,128)(2,1)} %collective-permute-done.15.rest_5_), channel_id=1, source_target_pairs={{0,4},{4,0},{8,12},{12,8},{16,20},{20,16},{24,28},{28,24},{1,5},{5... | collective-permute-start | bytes 1105928 | tf_op jit(solution)/shard_map/ppermute | solution.py:472
  37.8 1.8 %collective-permute-start.23 = (bf16[80,2304]{1,0:T(8,128)(2,1)S(1)}, bf16[80,2304]{1,0:T(8,128)(2,1)S(1)}, u32[]{:S(2)}, u32[]{:S(2)}) collective-permute-start(bf16[80,2304]{1,0:T(8,128)(2,1)S(1)} %copy-done.9), channel_id=1, source_target_pairs={{0,2},{1,3},{2,0},{3,1},{4,6},{5,7},{6,4},{7,5},{8,10},{9,11},{10,... | collective-permute-start | bytes 1105928 | tf_op jit(solution)/shard_map/ppermute | solution.py:469
  39.6 9.7 %shard_map.112 = (bf16[1008,640]{1,0:T(8,128)(2,1)S(1)}, bf16[496,1280]{1,0:T(8,128)(2,1)S(1)}) custom-call(s32[2]{0:T(128)S(1)} %pad_add_fusion.1.span, bf16[1008,320]{1,0:T(8,128)(2,1)S(1)} %get-tuple-element.46.hot5, bf16[1008,64]{1,0:T(8,128)(2,1)S(1)} %get-tuple-element.47.hot1, f32[2,640]{1,0:T(2,128)S(1)} %copy-done.6, f32[2,1280]{1,0:T(2,128)S(1)} %copy-done.4, ...), custom_call_target="tpu_custom_call" | custom-call | tf_op jit(solution)/shard_map/pallas_call | solution.py:577
  49.4 0.5 collective-permute-start.26
  50.0 0.4 collective-permute-start.27
  50.4 1.6 %shard_map.113.rest_0_ = f32[496,640]{1,0:T(8,128)S(1)} custom-call(bf16[1008,640]{1,0:T(8,128)(2,1)S(1)} %get-tuple-element.61.ci, bf16[2,160,3200]{2,1,0:T(8,128)(2,1)S(1)} %copy-done, bf16[2,160,3200]{2,1,0:T(8,128)(2,1)S(1)} %collective-permute-done.20.near_conv.rest_3_), custom_call_target="tpu_custom_call" | custom-call | tf_op jit(solution)/shard_map/pallas_call | solution.py:597
  52.1 0.5 collective-permute-done.27.rest_12_
  52.6 5.4 %shard_map.114 = bf16[496,1280]{1,0:T(8,128)(2,1)} custom-call(bf16[1008,640]{1,0:T(8,128)(2,1)S(1)} %get-tuple-element.61.ci, bf16[496,1280]{1,0:T(8,128)(2,1)S(1)} %get-tuple-element.62.hid, f32[2,640]{1,0:T(2,128)S(1)} %copy-done.6, f32[496,640]{1,0:T(8,128)S(1)} %shard_map.113.rest_0_, bf16[2,160,3200]{2,1,0:T(8,128)(2,1)S(1)} %copy-done, ...), custom_call_target="tpu_custom_call" | custom-call | tf_op jit(solution)/shard_map/pallas_call | solution.py:607
  (62 shorter events, 2.1 us)
Async XLA Ops:
  0.0 16.6 %copy-start.5 = (f32[2,640]{1,0:T(2,128)S(1)}, f32[2,640]{1,0:T(2,128)}, u32[]{:S(2)}) copy-start(f32[2,640]{1,0:T(2,128)} %gain_mid.1) | copy-start | bytes 15364
  0.0 16.6 %collective-permute-start.6 = (bf16[2,320,640]{2,1,0:T(8,128)(2,1)}, bf16[2,320,640]{2,1,0:T(8,128)(2,1)}, u32[]{:S(2)}, u32[]{:S(2)}) collective-permute-start(bf16[2,320,640]{2,1,0:T(8,128)(2,1)} %rest_2_.2), channel_id=1, source_target_pairs={{0,1},{1,0},{2,3},{3,2},{4,5},{5,4},{6,7},{7,6},{8,9},{9,8},{10,11... | collective-permute-start | bytes 2457608 | tf_op jit(solution)/shard_map/ppermute | solution.py:466
  0.5 16.1 %collective-permute-start.5 = (bf16[2,160,1280]{2,1,0:T(8,128)(2,1)}, bf16[2,160,1280]{2,1,0:T(8,128)(2,1)}, u32[]{:S(2)}, u32[]{:S(2)}) collective-permute-start(bf16[2,160,1280]{2,1,0:T(8,128)(2,1)} %rest_2_.3), channel_id=1, source_target_pairs={{0,1},{1,0},{2,3},{3,2},{4,5},{5,4},{6,7},{7,6},{8,9},{9,8},{10,11... | collective-permute-start | bytes 2457608 | tf_op jit(solution)/shard_map/ppermute | solution.py:466
  0.6 16.0 %copy-start = (bf16[2,160,3200]{2,1,0:T(8,128)(2,1)S(1)}, bf16[2,160,3200]{2,1,0:T(8,128)(2,1)}, u32[]{:S(2)}) copy-start(bf16[2,160,3200]{2,1,0:T(8,128)(2,1)} %rest_1_.3) | copy-start | bytes 6144004
  3.8 1.8 %collective-permute-start.1 = (f32[64,640]{1,0:T(8,128)}, f32[64,640]{1,0:T(8,128)S(1)}, u32[]{:S(2)}, u32[]{:S(2)}) collective-permute-start(f32[64,640]{1,0:T(8,128)} %get-tuple-element.38), channel_id=1, source_target_pairs={{0,1},{1,0},{2,3},{3,2},{4,5},{5,4},{6,7},{7,6},{8,9},{9,8},{10,11... | collective-permute-start | bytes 491528 | tf_op jit(solution)/shard_map/ppermute | solution.py:466
  4.4 1.2 %collective-permute-start = (s32[384]{0:T(512)S(1)}, s32[384]{0:T(512)S(1)}, u32[]{:S(2)}, u32[]{:S(2)}) collective-permute-start(s32[384]{0:T(512)S(1)} %get-tuple-element.78), channel_id=1, source_target_pairs={{0,1},{1,0},{2,3},{3,2},{4,5},{5,4},{6,7},{7,6},{8,9},{9,8},{10,11... | collective-permute-start | bytes 4616 | tf_op jit(solution)/shard_map/ppermute | solution.py:466
  6.6 7.5 %collective-permute-start.2 = (s32[2,384]{1,0:T(2,128)S(1)}, s32[2,384]{1,0:T(2,128)S(1)}, u32[]{:S(2)}, u32[]{:S(2)}) collective-permute-start(s32[2,384]{1,0:T(2,128)S(1)} %pad_add_fusion), channel_id=1, source_target_pairs={{0,4},{1,29},{2,6},{3,31},{4,8},{5,1},{6,10},{7,3},{8,12},{9,5},{1... | collective-permute-start | bytes 9224 | tf_op jit(solution)/shard_map/ppermute | solution.py:512
  10.1 5.8 %collective-permute-start.4 = (bf16[64,640]{1,0:T(8,128)(2,1)S(1)}, bf16[64,640]{1,0:T(8,128)(2,1)S(1)}, u32[]{:S(2)}, u32[]{:S(2)}) collective-permute-start(bf16[64,640]{1,0:T(8,128)(2,1)S(1)} %get-tuple-element.73), channel_id=1, source_target_pairs={{0,2},{1,3},{2,0},{3,1},{4,6},{5,7},{6,4},{7,5},{8,10},{9,11},{10,... | collective-permute-start | bytes 245768 | tf_op jit(solution)/shard_map/ppermute | solution.py:469
  14.1 5.5 %collective-permute-start.3 = (s32[384]{0:T(512)S(1)}, s32[384]{0:T(512)S(1)}, u32[]{:S(2)}, u32[]{:S(2)}) collective-permute-start(s32[384]{0:T(512)S(1)} %get-tuple-element.71), channel_id=1, source_target_pairs={{0,1},{1,0},{2,3},{3,2},{4,5},{5,4},{6,7},{7,6},{8,9},{9,8},{10,11... | collective-permute-start | bytes 4616 | tf_op jit(solution)/shard_map/ppermute | solution.py:466
  14.6 14.1 %copy-start.1 = (bf16[2,160,1280]{2,1,0:T(8,128)(2,1)S(1)}, bf16[2,160,1280]{2,1,0:T(8,128)(2,1)}, u32[]{:S(2)}) copy-start(bf16[2,160,1280]{2,1,0:T(8,128)(2,1)} %rest_2_.3) | copy-start | bytes 2457604
  14.6 8.2 %collective-permute-start.11 = (bf16[80,1280]{1,0:T(8,128)(2,1)}, bf16[80,1280]{1,0:T(8,128)(2,1)}, u32[]{:S(2)}, u32[]{:S(2)}) collective-permute-start(bf16[80,1280]{1,0:T(8,128)(2,1)} %get-tuple-element.53), channel_id=1, source_target_pairs={{0,2},{1,3},{2,0},{3,1},{4,6},{5,7},{6,4},{7,5},{8,10},{9,11},{10,... | collective-permute-start | bytes 614408 | tf_op jit(solution)/shard_map/ppermute | solution.py:469
  15.9 16.2 %collective-permute-start.15 = (bf16[80,2304]{1,0:T(8,128)(2,1)}, bf16[80,2304]{1,0:T(8,128)(2,1)}, u32[]{:S(2)}, u32[]{:S(2)}) collective-permute-start(bf16[80,2304]{1,0:T(8,128)(2,1)} %get-tuple-element.56), channel_id=1, source_target_pairs={{0,2},{1,3},{2,0},{3,1},{4,6},{5,7},{6,4},{7,5},{8,10},{9,11},{10,... | collective-permute-start | bytes 1105928 | tf_op jit(solution)/shard_map/ppermute | solution.py:469
  18.5 7.8 %collective-permute-start.7 = (bf16[32,3200]{1,0:T(8,128)(2,1)}, bf16[32,3200]{1,0:T(8,128)(2,1)}, u32[]{:S(2)}, u32[]{:S(2)}) collective-permute-start(bf16[32,3200]{1,0:T(8,128)(2,1)} %get-tuple-element.43), channel_id=1, source_target_pairs={{0,1},{1,0},{2,3},{3,2},{4,5},{5,4},{6,7},{7,6},{8,9},{9,8},{10,11... | collective-permute-start | bytes 614408 | tf_op jit(solution)/shard_map/ppermute | solution.py:466
  22.8 9.4 %collective-permute-start.14 = (bf16[80,1280]{1,0:T(8,128)(2,1)}, bf16[80,1280]{1,0:T(8,128)(2,1)S(1)}, u32[]{:S(2)}, u32[]{:S(2)}) collective-permute-start(bf16[80,1280]{1,0:T(8,128)(2,1)} %collective-permute-done.11.rest_6_), channel_id=1, source_target_pairs={{0,12},{4,8},{8,4},{12,0},{16,28},{20,24},{24,20},{28,16},{1,13},{... | collective-permute-start | bytes 614408 | tf_op jit(solution)/shard_map/ppermute | solution.py:472
  22.8 9.4 %collective-permute-start.13 = (bf16[80,1280]{1,0:T(8,128)(2,1)}, bf16[80,1280]{1,0:T(8,128)(2,1)S(1)}, u32[]{:S(2)}, u32[]{:S(2)}) collective-permute-start(bf16[80,1280]{1,0:T(8,128)(2,1)} %collective-permute-done.11.rest_6_), channel_id=1, source_target_pairs={{0,8},{4,12},{8,0},{12,4},{16,24},{20,28},{24,16},{28,20},{1,9},{5... | collective-permute-start | bytes 614408 | tf_op jit(solution)/shard_map/ppermute | solution.py:472
  23.0 10.9 %collective-permute-start.12 = (bf16[80,1280]{1,0:T(8,128)(2,1)}, bf16[80,1280]{1,0:T(8,128)(2,1)S(1)}, u32[]{:S(2)}, u32[]{:S(2)}) collective-permute-start(bf16[80,1280]{1,0:T(8,128)(2,1)} %collective-permute-done.11.rest_6_), channel_id=1, source_target_pairs={{0,4},{4,0},{8,12},{12,8},{16,20},{20,16},{24,28},{28,24},{1,5},{5... | collective-permute-start | bytes 614408 | tf_op jit(solution)/shard_map/ppermute | solution.py:472
  27.2 7.2 %collective-permute-start.8 = (bf16[32,3200]{1,0:T(8,128)(2,1)S(1)}, bf16[32,3200]{1,0:T(8,128)(2,1)S(1)}, u32[]{:S(2)}, u32[]{:S(2)}) collective-permute-start(bf16[32,3200]{1,0:T(8,128)(2,1)S(1)} %add_convert_fusion.rest_0_), channel_id=1, source_target_pairs={{0,2},{1,3},{2,0},{3,1},{4,6},{5,7},{6,4},{7,5},{8,10},{9,11},{10,... | collective-permute-start | bytes 614408 | tf_op jit(solution)/shard_map/ppermute | solution.py:469
  29.6 10.0 %copy-start.6 = (f32[2,640]{1,0:T(2,128)S(1)}, f32[2,640]{1,0:T(2,128)}, u32[]{:S(2)}) copy-start(f32[2,640]{1,0:T(2,128)} %gain_out.3) | copy-start | bytes 15364
  32.1 2.8 %collective-permute-start.9 = (bf16[32,3200]{1,0:T(8,128)(2,1)S(1)}, bf16[32,3200]{1,0:T(8,128)(2,1)S(1)}, u32[]{:S(2)}, u32[]{:S(2)}) collective-permute-start(bf16[32,3200]{1,0:T(8,128)(2,1)S(1)} %add_convert_fusion.rest_0_), channel_id=1, source_target_pairs={{0,1},{1,0},{2,3},{3,2},{4,5},{5,4},{6,7},{7,6},{8,9},{9,8},{10,11... | collective-permute-start | bytes 614408 | tf_op jit(solution)/shard_map/ppermute | solution.py:466
  33.9 1.9 %collective-permute-start.16 = (bf16[80,1280]{1,0:T(8,128)(2,1)}, bf16[80,1280]{1,0:T(8,128)(2,1)S(1)}, u32[]{:S(2)}, u32[]{:S(2)}) collective-permute-start(bf16[80,1280]{1,0:T(8,128)(2,1)} %collective-permute-done.11.rest_6_), channel_id=1, source_target_pairs={{0,1},{1,0},{2,3},{3,2},{4,5},{5,4},{6,7},{7,6},{8,9},{9,8},{10,11... | collective-permute-start | bytes 614408 | tf_op jit(solution)/shard_map/ppermute | solution.py:466
  33.9 1.9 %collective-permute-start.17 = (bf16[80,1280]{1,0:T(8,128)(2,1)S(1)}, bf16[80,1280]{1,0:T(8,128)(2,1)S(1)}, u32[]{:S(2)}, u32[]{:S(2)}) collective-permute-start(bf16[80,1280]{1,0:T(8,128)(2,1)S(1)} %collective-permute-done.12.rest_7_), channel_id=1, source_target_pairs={{0,1},{1,0},{2,3},{3,2},{4,5},{5,4},{6,7},{7,6},{8,9},{9,8},{10,11... | collective-permute-start | bytes 614408 | tf_op jit(solution)/shard_map/ppermute | solution.py:466
  34.4 1.5 %collective-permute-start.18 = (bf16[80,1280]{1,0:T(8,128)(2,1)S(1)}, bf16[80,1280]{1,0:T(8,128)(2,1)S(1)}, u32[]{:S(2)}, u32[]{:S(2)}) collective-permute-start(bf16[80,1280]{1,0:T(8,128)(2,1)S(1)} %collective-permute-done.13.rest_8_), channel_id=1, source_target_pairs={{0,1},{1,0},{2,3},{3,2},{4,5},{5,4},{6,7},{7,6},{8,9},{9,8},{10,11... | collective-permute-start | bytes 614408 | tf_op jit(solution)/shard_map/ppermute | solution.py:466
  34.4 1.8 %collective-permute-start.19 = (bf16[80,1280]{1,0:T(8,128)(2,1)S(1)}, bf16[80,1280]{1,0:T(8,128)(2,1)S(1)}, u32[]{:S(2)}, u32[]{:S(2)}) collective-permute-start(bf16[80,1280]{1,0:T(8,128)(2,1)S(1)} %collective-permute-done.14.rest_9_), channel_id=1, source_target_pairs={{0,1},{1,0},{2,3},{3,2},{4,5},{5,4},{6,7},{7,6},{8,9},{9,8},{10,11... | collective-permute-start | bytes 614408 | tf_op jit(solution)/shard_map/ppermute | solution.py:466
  34.9 1.6 %collective-permute-start.10 = (bf16[32,3200]{1,0:T(8,128)(2,1)S(1)}, bf16[32,3200]{1,0:T(8,128)(2,1)S(1)}, u32[]{:S(2)}, u32[]{:S(2)}) collective-permute-start(bf16[32,3200]{1,0:T(8,128)(2,1)S(1)} %collective-permute-done.8.rest_1_), channel_id=1, source_target_pairs={{0,1},{1,0},{2,3},{3,2},{4,5},{5,4},{6,7},{7,6},{8,9},{9,8},{10,11... | collective-permute-start | bytes 614408 | tf_op jit(solution)/shard_map/ppermute | solution.py:466
  36.5 13.9 %collective-permute-start.20 = (bf16[2,160,3200]{2,1,0:T(8,128)(2,1)S(1)}, bf16[2,160,3200]{2,1,0:T(8,128)(2,1)S(1)}, u32[]{:S(2)}, u32[]{:S(2)}) collective-permute-start(bf16[2,160,3200]{2,1,0:T(8,128)(2,1)S(1)} %copy-done), channel_id=1, source_target_pairs={{0,1},{1,0},{2,3},{3,2},{4,5},{5,4},{6,7},{7,6},{8,9},{9,8},{10,11... | collective-permute-start | bytes 6144008 | tf_op jit(solution)/shard_map/ppermute | solution.py:466
  36.7 12.7 %collective-permute-start.22 = (bf16[80,2304]{1,0:T(8,128)(2,1)}, bf16[80,2304]{1,0:T(8,128)(2,1)S(1)}, u32[]{:S(2)}, u32[]{:S(2)}) collective-permute-start(bf16[80,2304]{1,0:T(8,128)(2,1)} %collective-permute-done.15.rest_5_), channel_id=1, source_target_pairs={{0,8},{4,12},{8,0},{12,4},{16,24},{20,28},{24,16},{28,20},{1,9},{5... | collective-permute-start | bytes 1105928 | tf_op jit(solution)/shard_map/ppermute | solution.py:472
  37.0 12.9 %collective-permute-start.21 = (bf16[80,2304]{1,0:T(8,128)(2,1)}, bf16[80,2304]{1,0:T(8,128)(2,1)S(1)}, u32[]{:S(2)}, u32[]{:S(2)}) collective-permute-start(bf16[80,2304]{1,0:T(8,128)(2,1)} %collective-permute-done.15.rest_5_), channel_id=1, source_target_pairs={{0,4},{4,0},{8,12},{12,8},{16,20},{20,16},{24,28},{28,24},{1,5},{5... | collective-permute-start | bytes 1105928 | tf_op jit(solution)/shard_map/ppermute | solution.py:472
  37.8 12.2 %collective-permute-start.23 = (bf16[80,2304]{1,0:T(8,128)(2,1)S(1)}, bf16[80,2304]{1,0:T(8,128)(2,1)S(1)}, u32[]{:S(2)}, u32[]{:S(2)}) collective-permute-start(bf16[80,2304]{1,0:T(8,128)(2,1)S(1)} %copy-done.9), channel_id=1, source_target_pairs={{0,2},{1,3},{2,0},{3,1},{4,6},{5,7},{6,4},{7,5},{8,10},{9,11},{10,... | collective-permute-start | bytes 1105928 | tf_op jit(solution)/shard_map/ppermute | solution.py:469
  49.3 2.7 %collective-permute-start.24 = (bf16[80,2304]{1,0:T(8,128)(2,1)}, bf16[80,2304]{1,0:T(8,128)(2,1)S(1)}, u32[]{:S(2)}, u32[]{:S(2)}) collective-permute-start(bf16[80,2304]{1,0:T(8,128)(2,1)} %collective-permute-done.15.rest_5_), channel_id=1, source_target_pairs={{0,1},{1,0},{2,3},{3,2},{4,5},{5,4},{6,7},{7,6},{8,9},{9,8},{10,11... | collective-permute-start | bytes 1105928 | tf_op jit(solution)/shard_map/ppermute | solution.py:466
  49.4 2.6 %collective-permute-start.26 = (bf16[80,2304]{1,0:T(8,128)(2,1)S(1)}, bf16[80,2304]{1,0:T(8,128)(2,1)S(1)}, u32[]{:S(2)}, u32[]{:S(2)}) collective-permute-start(bf16[80,2304]{1,0:T(8,128)(2,1)S(1)} %collective-permute-done.22.rest_7_), channel_id=1, source_target_pairs={{0,1},{1,0},{2,3},{3,2},{4,5},{5,4},{6,7},{7,6},{8,9},{9,8},{10,11... | collective-permute-start | bytes 1105928 | tf_op jit(solution)/shard_map/ppermute | solution.py:466
  49.9 2.2 %collective-permute-start.25 = (bf16[80,2304]{1,0:T(8,128)(2,1)S(1)}, bf16[80,2304]{1,0:T(8,128)(2,1)S(1)}, u32[]{:S(2)}, u32[]{:S(2)}) collective-permute-start(bf16[80,2304]{1,0:T(8,128)(2,1)S(1)} %collective-permute-done.21.rest_6_), channel_id=1, source_target_pairs={{0,1},{1,0},{2,3},{3,2},{4,5},{5,4},{6,7},{7,6},{8,9},{9,8},{10,11... | collective-permute-start | bytes 1105928 | tf_op jit(solution)/shard_map/ppermute | solution.py:466
  50.0 2.7 %collective-permute-start.27 = (bf16[80,2304]{1,0:T(8,128)(2,1)S(1)}, bf16[80,2304]{1,0:T(8,128)(2,1)S(1)}, u32[]{:S(2)}, u32[]{:S(2)}) collective-permute-start(bf16[80,2304]{1,0:T(8,128)(2,1)S(1)} %collective-permute-done.23.rest_8_), channel_id=1, source_target_pairs={{0,1},{1,0},{2,3},{3,2},{4,5},{5,4},{6,7},{7,6},{8,9},{9,8},{10,11... | collective-permute-start | bytes 1105928 | tf_op jit(solution)/shard_map/ppermute | solution.py:466
  (6 other events, 36.7 us)

commit v12 on v11

--- a/solution.py
+++ b/solution.py
@@ -124,20 +124,20 @@
         leaving = [pltpu.make_async_copy(s, d, sem.at[2]) for s, d in zip(held, parts)]
 
     wait(copies)
-    if split:
-        for kind in range(2):
-
-            @pl.when(y == kind)
-            def _():
-                wait(kinds[kind])
-
-        start(leaving)
     full[...] = jnp.zeros_like(full)
     full[0:VOCAB] = emb[...]
     full[SLOT : SLOT + VOCAB] = emb[...] + bv[...][None, :]
     hidden = full[...].astype(BF)
     table[...] = hidden
     normed = gelu(norm(hidden.astype(F32), g[0:1])).astype(BF)
+    if split:
+        for kind in range(2):
+
+            @pl.when(y == kind)
+            def _():
+                wait(kinds[kind])
+
+        start(leaving)
     rows = w.shape[0]
     mine = dot(normed, pick(normed.shape[1], rows, lax.axis_index("roll") * rows)).astype(BF)
     part[...] = dot(mine, w[...])
@@ -498,19 +498,19 @@
     )(embed_table, break_vec, gain_in, w_in, conv_w, w_out)
 
     if split:
+        far_a = x_swap(parts[0])
         near_out, near_in = core_swap(w_out), core_swap(w_in)
         low = roll_at % 2 == 0
         ends = codes[rows - REACH :], codes[:REACH]
         theirs = core_swap(jnp.where(low, *ends[::-1]))
         own = part + after(core_swap(part), theirs)
         other = x_swap(own.astype(BF))
-        far_a = x_swap(after(parts[0], own))
         far_b = x_swap(after(parts[1], own))
         pack = jnp.stack([jnp.where(low, *ends), theirs])
         places = [(s, r) for s in range(seqs) for r in range(rolls)]
         moves = [(s * rolls + r, (s + (1, -1)[r % 2]) % seqs * rolls + r) for s, r in places]
         moved = lax.ppermute(after(pack, own), ("seq", "roll"), moves)
-        other = after(other, moved, near_out, near_in)
+        other = after(other, near_out, near_in)
         came = core_swap(moved[1])
         before, behind = jnp.where(low, moved[0], came), jnp.where(low, came, moved[0])
     else:
@@ -537,7 +537,7 @@
     if split:
         relay = after(far_a, taps[1])
         parts_a = [far_a] + [seq_swap(relay, b) for b in (1, 2, 3)]
-        sent = (taps[0] + core_swap(taps[1]).astype(F32)).astype(BF)
+        sent = (taps[0] + after(core_swap(taps[1]), before, behind).astype(F32)).astype(BF)
         received = x_swap(sent)
     spare = jnp.zeros((-(rows + 2 * REACH) % 128,), jnp.int32)
     near = jnp.concatenate([before, codes, behind, spare])[None]

time: 58.5 us -> 59.4 us (1.015)
  waiting for transfers between devices: 10.4 us -> 11.5 us
    ppermute x5, waiting for transfers between devices: 1.69 us -> 3.89 us  [seq_swap(): return lax.ppermute(x, 'seq', [(i, i ^ bits) for i in range(seqs)])]
    ppermute x5, starting transfers between devices: 6.77 us -> 4.71 us  [x_swap(): return lax.ppermute(x, 'roll', [(i, i ^ 2) for i in range(rolls)])]
    ppermute x5, starting transfers between devices: 4.51 us -> 5.55 us  [seq_swap(): return lax.ppermute(x, 'seq', [(i, i ^ bits) for i in range(seqs)])]
    ppermute x17, starting transfers between devices: 5.22 us -> 6.02 us  [core_swap(): return lax.ppermute(x, 'roll', [(i, i ^ 1) for i in range(rolls)])]
  transfers between devices with their start and end apart: 28 -> 28, of which waited for: 10 -> 12; matrix products, arithmetic and copies ran while one was open for 4% -> 4% of each run, Pallas kernels for 32% -> 32%
where the time goes in v12:
time: 59.4 us; the launch traced here: 59.1 us
  Pallas kernels  24.4 us (41%)
  starting transfers between devices  19.1 us (32%)
  waiting for transfers between devices  11.5 us (19%)
  other arithmetic  2.1 us (4%)
  local copies, waits for them, and re-layouts  1.06 us (2%)
  between operations  0.99 us (2%)
    pallas_call x1, Pallas kernels, per_device(): pl.pallas_call(functools.partial(rows_kernel, split), out_shape=(jax.Shap...  9.74 us
    ppermute x17, starting transfers between devices, core_swap(): return lax.ppermute(x, 'roll', [(i, i ^ 1) for i in range(rolls)])  6.02 us
    ppermute x5, starting transfers between devices, seq_swap(): return lax.ppermute(x, 'seq', [(i, i ^ bits) for i in range(seqs)])  5.55 us
    pallas_call x1, Pallas kernels, per_device(): pl.pallas_call(functools.partial(last_kernel, split), out_shape=jax.Shape...  5.44 us
    ppermute x5, starting transfers between devices, x_swap(): return lax.ppermute(x, 'roll', [(i, i ^ 2) for i in range(rolls)])  4.71 us
    ppermute x5, waiting for transfers between devices, seq_swap(): return lax.ppermute(x, 'seq', [(i, i ^ bits) for i in range(seqs)])  3.89 us
    ppermute x17, waiting for transfers between devices, core_swap(): return lax.ppermute(x, 'roll', [(i, i ^ 1) for i in range(rolls)])  3.26 us
    pallas_call x1, Pallas kernels, per_device(): pl.pallas_call(functools.partial(first_kernel, split), out_shape=[jax.Sha...  3.25 us
  transfers between devices with their start and end apart: 28, of which 12 were waited for; matrix products, arithmetic and copies ran while one was open for 4% of the time, Pallas kernels for 32%

profile of v12, /device:TPU:0, one launch (start us, length us, event | category | flops | bytes accessed | tf_op | source)
XLA Modules:
  0.0 59.1 jit_solution(3025139072703249536)
XLA Ops:
  0.0 0.5 collective-permute-start.6
  0.6 3.3 %shard_map.109 = (bf16[64,1280]{1,0:T(8,128)(2,1)}, f32[64,640]{1,0:T(8,128)}, bf16[80,1280]{1,0:T(8,128)(2,1)}, bf16[80,2304]{1,0:T(8,128)(2,1)}, bf16[80,2304]{1,0:T(8,128)(2,1)}) custom-call(f32[30,1280]{1,0:T(8,128)} %embed.1, f32[1280]{0:T(1024)} %brk.1, f32[2,1280]{1,0:T(2,128)} %gain_in.1, bf16[2,320,640]{2,1,0:T(8,128)(2,1)} %rest_2_.2, ...), custom_call_target="tpu_custom_call" | custom-call | tf_op jit(solution)/shard_map/pallas_call | solution.py:482
  3.9 0.5 collective-permute-start.1
  4.6 1.1 %collective-permute-done = s32[384]{0:T(512)S(1)} collective-permute-done((s32[384]{0:T(512)S(1)}, s32[384]{0:T(512)S(1)}, u32[]{:S(2)}, u32[]{:S(2)}) %collective-permute-start) | collective-permute-done | bytes 1568 | tf_op jit(solution)/shard_map/ppermute | solution.py:466
  5.7 1.0 %fusion.1 = (bf16[64,640]{1,0:T(8,128)(2,1)S(1)}, f32[64,640]{1,0:T(8,128)S(1)}) fusion(f32[64,640]{1,0:T(8,128)} %get-tuple-element.38, f32[64,640]{1,0:T(8,128)S(1)} %collective-permute-done.1), kind=kLoop, calls=%fused_computation.11 | loop fusion | flops 81920 | bytes 573440 | tf_op jit(solution)/shard_map/convert_element_type | solution.py:507
  6.7 2.8 %collective-permute-start.2 = (s32[2,384]{1,0:T(2,128)S(1)}, s32[2,384]{1,0:T(2,128)S(1)}, u32[]{:S(2)}, u32[]{:S(2)}) collective-permute-start(s32[2,384]{1,0:T(2,128)S(1)} %pad_add_fusion), channel_id=1, source_target_pairs={{0,4},{1,29},{2,6},{3,31},{4,8},{5,1},{6,10},{7,3},{8,12},{9,5},{1... | collective-permute-start | bytes 9224 | tf_op jit(solution)/shard_map/ppermute | solution.py:512
  9.5 1.5 %collective-permute-start.11 = (bf16[80,1280]{1,0:T(8,128)(2,1)}, bf16[80,1280]{1,0:T(8,128)(2,1)}, u32[]{:S(2)}, u32[]{:S(2)}) collective-permute-start(bf16[80,1280]{1,0:T(8,128)(2,1)} %get-tuple-element.53), channel_id=1, source_target_pairs={{0,2},{1,3},{2,0},{3,1},{4,6},{5,7},{6,4},{7,5},{8,10},{9,11},{10,... | collective-permute-start | bytes 614408 | tf_op jit(solution)/shard_map/ppermute | solution.py:469
  11.6 0.6 %collective-permute-start.4 = (bf16[64,640]{1,0:T(8,128)(2,1)S(1)}, bf16[64,640]{1,0:T(8,128)(2,1)S(1)}, u32[]{:S(2)}, u32[]{:S(2)}) collective-permute-start(bf16[64,640]{1,0:T(8,128)(2,1)S(1)} %get-tuple-element.73), channel_id=1, source_target_pairs={{0,2},{1,3},{2,0},{3,1},{4,6},{5,7},{6,4},{7,5},{8,10},{9,11},{10,... | collective-permute-start | bytes 245768 | tf_op jit(solution)/shard_map/ppermute | solution.py:469
  12.2 1.9 %collective-permute-done.2 = s32[2,384]{1,0:T(2,128)S(1)} collective-permute-done((s32[2,384]{1,0:T(2,128)S(1)}, s32[2,384]{1,0:T(2,128)S(1)}, u32[]{:S(2)}, u32[]{:S(2)}) %collective-permute-start.2) | collective-permute-done | bytes 3104 | tf_op jit(solution)/shard_map/ppermute | solution.py:512
  14.1 0.6 %collective-permute-start.3 = (s32[384]{0:T(512)S(1)}, s32[384]{0:T(512)S(1)}, u32[]{:S(2)}, u32[]{:S(2)}) collective-permute-start(s32[384]{0:T(512)S(1)} %get-tuple-element.71), channel_id=1, source_target_pairs={{0,1},{1,0},{2,3},{3,2},{4,5},{5,4},{6,7},{7,6},{8,9},{9,8},{10,11... | collective-permute-start | bytes 4616 | tf_op jit(solution)/shard_map/ppermute | solution.py:466
  14.8 2.5 %collective-permute-done.4.other = bf16[64,640]{1,0:T(8,128)(2,1)S(1)} collective-permute-done((bf16[64,640]{1,0:T(8,128)(2,1)S(1)}, bf16[64,640]{1,0:T(8,128)(2,1)S(1)}, u32[]{:S(2)}, u32[]{:S(2)}) %collective-permute-start.4) | collective-permute-done | bytes 81952 | tf_op jit(solution)/shard_map/ppermute | solution.py:469
  17.3 1.5 %collective-permute-start.15 = (bf16[80,2304]{1,0:T(8,128)(2,1)}, bf16[80,2304]{1,0:T(8,128)(2,1)}, u32[]{:S(2)}, u32[]{:S(2)}) collective-permute-start(bf16[80,2304]{1,0:T(8,128)(2,1)} %get-tuple-element.56), channel_id=1, source_target_pairs={{0,2},{1,3},{2,0},{3,1},{4,6},{5,7},{6,4},{7,5},{8,10},{9,11},{10,... | collective-permute-start | bytes 1105928 | tf_op jit(solution)/shard_map/ppermute | solution.py:469
  18.8 1.8 %shard_map.110 = (f32[32,3200]{1,0:T(8,128)S(1)}, bf16[32,3200]{1,0:T(8,128)(2,1)}) custom-call(f32[64,640]{1,0:T(8,128)S(1)} %get-tuple-element.74.own, bf16[64,640]{1,0:T(8,128)(2,1)S(1)} %collective-permute-done.4.other, f32[2,640]{1,0:T(2,128)S(1)} %copy-done.5, bf16[2,160,3200]{2,1,0:T(8,128)(2,1)S(1)} %copy-done), custom_call_target="tpu_custom_call" | custom-call | tf_op jit(solution)/shard_map/pallas_call | solution.py:524
  20.7 1.7 %collective-permute-start.7 = (bf16[32,3200]{1,0:T(8,128)(2,1)}, bf16[32,3200]{1,0:T(8,128)(2,1)}, u32[]{:S(2)}, u32[]{:S(2)}) collective-permute-start(bf16[32,3200]{1,0:T(8,128)(2,1)} %get-tuple-element.43), channel_id=1, source_target_pairs={{0,1},{1,0},{2,3},{3,2},{4,5},{5,4},{6,7},{7,6},{8,9},{9,8},{10,11... | collective-permute-start | bytes 614408 | tf_op jit(solution)/shard_map/ppermute | solution.py:466
  22.5 1.1 %collective-permute-start.14 = (bf16[80,1280]{1,0:T(8,128)(2,1)}, bf16[80,1280]{1,0:T(8,128)(2,1)S(1)}, u32[]{:S(2)}, u32[]{:S(2)}) collective-permute-start(bf16[80,1280]{1,0:T(8,128)(2,1)} %collective-permute-done.11.rest_6_), channel_id=1, source_target_pairs={{0,12},{4,8},{8,4},{12,0},{16,28},{20,24},{24,20},{28,16},{1,13},{... | collective-permute-start | bytes 614408 | tf_op jit(solution)/shard_map/ppermute | solution.py:472
  24.0 2.0 %collective-permute-start.12 = (bf16[80,1280]{1,0:T(8,128)(2,1)}, bf16[80,1280]{1,0:T(8,128)(2,1)S(1)}, u32[]{:S(2)}, u32[]{:S(2)}) collective-permute-start(bf16[80,1280]{1,0:T(8,128)(2,1)} %collective-permute-done.11.rest_6_), channel_id=1, source_target_pairs={{0,4},{4,0},{8,12},{12,8},{16,20},{20,16},{24,28},{28,24},{1,5},{5... | collective-permute-start | bytes 614408 | tf_op jit(solution)/shard_map/ppermute | solution.py:472
  26.1 1.0 %add_convert_fusion.rest_0_ = bf16[32,3200]{1,0:T(8,128)(2,1)S(1)} fusion(f32[32,3200]{1,0:T(8,128)S(1)} %get-tuple-element.42, bf16[32,3200]{1,0:T(8,128)(2,1)} %collective-permute-done.7), kind=kLoop, calls=%fused_computation | loop fusion | flops 307200 | bytes 819200 | tf_op jit(solution)/shard_map/convert_element_type | solution.py:540
  27.0 0.6 %collective-permute-start.8 = (bf16[32,3200]{1,0:T(8,128)(2,1)S(1)}, bf16[32,3200]{1,0:T(8,128)(2,1)S(1)}, u32[]{:S(2)}, u32[]{:S(2)}) collective-permute-start(bf16[32,3200]{1,0:T(8,128)(2,1)S(1)} %add_convert_fusion.rest_0_), channel_id=1, source_target_pairs={{0,2},{1,3},{2,0},{3,1},{4,6},{5,7},{6,4},{7,5},{8,10},{9,11},{10,... | collective-permute-start | bytes 614408 | tf_op jit(solution)/shard_map/ppermute | solution.py:469
  27.6 0.9 %copy-done.3 = bf16[64,1280]{1,0:T(8,128)(2,1)S(1)} copy-done((bf16[64,1280]{1,0:T(8,128)(2,1)S(1)}, bf16[64,1280]{1,0:T(8,128)(2,1)}, u32[]{:S(2)}) %copy-start.3) | copy-done | bytes 163864
  28.6 2.5 %shard_map.111 = (bf16[1008,320]{1,0:T(8,128)(2,1)S(1)}, bf16[1008,64]{1,0:T(8,128)(2,1)S(1)}, bf16[384,1280]{1,0:T(8,128)(2,1)S(1)}, bf16[640,640]{1,0:T(8,128)(2,1)S(1)}) custom-call(s32[2]{0:T(128)S(1)} %pad_add_fusion.1.span, s32[1,1280]{1,0:T(1,128)S(1)} %broadcast_in_dim.6.near, bf16[64,1280]{1,0:T(8,128)(2,1)S(1)} %copy-done.3, ...), custom_call_target="tpu_custom_call" | custom-call | tf_op jit(solution)/shard_map/pallas_call | solution.py:553
  31.7 2.4 %collective-permute-done.13.rest_8_ = bf16[80,1280]{1,0:T(8,128)(2,1)S(1)} collective-permute-done((bf16[80,1280]{1,0:T(8,128)(2,1)}, bf16[80,1280]{1,0:T(8,128)(2,1)S(1)}, u32[]{:S(2)}, u32[]{:S(2)}) %collective-permute-start.13) | collective-permute-done | bytes 204832 | tf_op jit(solution)/shard_map/ppermute | solution.py:472
  34.1 1.0 %collective-permute-done.12.rest_7_ = bf16[80,1280]{1,0:T(8,128)(2,1)S(1)} collective-permute-done((bf16[80,1280]{1,0:T(8,128)(2,1)}, bf16[80,1280]{1,0:T(8,128)(2,1)S(1)}, u32[]{:S(2)}, u32[]{:S(2)}) %collective-permute-start.12) | collective-permute-done | bytes 204832 | tf_op jit(solution)/shard_map/ppermute | solution.py:472
  35.1 0.5 collective-permute-start.17
  35.6 0.5 collective-permute-start.19
  36.2 0.7 %collective-permute-done.16.rest_10_ = bf16[80,1280]{1,0:T(8,128)(2,1)S(1)} collective-permute-done((bf16[80,1280]{1,0:T(8,128)(2,1)}, bf16[80,1280]{1,0:T(8,128)(2,1)S(1)}, u32[]{:S(2)}, u32[]{:S(2)}) %collective-permute-start.16) | collective-permute-done | bytes 204832 | tf_op jit(solution)/shard_map/ppermute | solution.py:466
  37.9 1.4 %collective-permute-start.22 = (bf16[80,2304]{1,0:T(8,128)(2,1)}, bf16[80,2304]{1,0:T(8,128)(2,1)S(1)}, u32[]{:S(2)}, u32[]{:S(2)}) collective-permute-start(bf16[80,2304]{1,0:T(8,128)(2,1)} %collective-permute-done.15.rest_5_), channel_id=1, source_target_pairs={{0,8},{4,12},{8,0},{12,4},{16,24},{20,28},{24,16},{28,20},{1,9},{5... | collective-permute-start | bytes 1105928 | tf_op jit(solution)/shard_map/ppermute | solution.py:472
  39.3 0.6 %collective-permute-start.21 = (bf16[80,2304]{1,0:T(8,128)(2,1)}, bf16[80,2304]{1,0:T(8,128)(2,1)S(1)}, u32[]{:S(2)}, u32[]{:S(2)}) collective-permute-start(bf16[80,2304]{1,0:T(8,128)(2,1)} %collective-permute-done.15.rest_5_), channel_id=1, source_target_pairs={{0,4},{4,0},{8,12},{12,8},{16,20},{20,16},{24,28},{28,24},{1,5},{5... | collective-permute-start | bytes 1105928 | tf_op jit(solution)/shard_map/ppermute | solution.py:472
  39.9 0.5 collective-permute-start.23
  40.5 9.7 %shard_map.112 = (bf16[1008,640]{1,0:T(8,128)(2,1)S(1)}, bf16[496,1280]{1,0:T(8,128)(2,1)S(1)}) custom-call(s32[2]{0:T(128)S(1)} %pad_add_fusion.1.span, bf16[1008,320]{1,0:T(8,128)(2,1)S(1)} %get-tuple-element.47.hot5, bf16[1008,64]{1,0:T(8,128)(2,1)S(1)} %get-tuple-element.48.hot1, f32[2,640]{1,0:T(2,128)S(1)} %copy-done.6, f32[2,1280]{1,0:T(2,128)S(1)} %copy-done.4, ...), custom_call_target="tpu_custom_call" | custom-call | tf_op jit(solution)/shard_map/pallas_call | solution.py:577
  51.3 1.6 %shard_map.113.rest_0_ = f32[496,640]{1,0:T(8,128)S(1)} custom-call(bf16[1008,640]{1,0:T(8,128)(2,1)S(1)} %get-tuple-element.61.ci, bf16[2,160,3200]{2,1,0:T(8,128)(2,1)S(1)} %copy-done, bf16[2,160,3200]{2,1,0:T(8,128)(2,1)S(1)} %collective-permute-done.20.near_conv.rest_3_), custom_call_target="tpu_custom_call" | custom-call | tf_op jit(solution)/shard_map/pallas_call | solution.py:597
  53.0 0.5 collective-permute-done.27.rest_12_
  53.5 5.4 %shard_map.114 = bf16[496,1280]{1,0:T(8,128)(2,1)} custom-call(bf16[1008,640]{1,0:T(8,128)(2,1)S(1)} %get-tuple-element.61.ci, bf16[496,1280]{1,0:T(8,128)(2,1)S(1)} %get-tuple-element.62.hid, f32[2,640]{1,0:T(2,128)S(1)} %copy-done.6, f32[496,640]{1,0:T(8,128)S(1)} %shard_map.113.rest_0_, bf16[2,160,3200]{2,1,0:T(8,128)(2,1)S(1)} %copy-done, ...), custom_call_target="tpu_custom_call" | custom-call | tf_op jit(solution)/shard_map/pallas_call | solution.py:607
  (62 shorter events, 3.9 us)
Async XLA Ops:
  0.0 18.8 %copy-start.5 = (f32[2,640]{1,0:T(2,128)S(1)}, f32[2,640]{1,0:T(2,128)}, u32[]{:S(2)}) copy-start(f32[2,640]{1,0:T(2,128)} %gain_mid.1) | copy-start | bytes 15364
  0.0 18.8 %collective-permute-start.6 = (bf16[2,320,640]{2,1,0:T(8,128)(2,1)}, bf16[2,320,640]{2,1,0:T(8,128)(2,1)}, u32[]{:S(2)}, u32[]{:S(2)}) collective-permute-start(bf16[2,320,640]{2,1,0:T(8,128)(2,1)} %rest_2_.2), channel_id=1, source_target_pairs={{0,1},{1,0},{2,3},{3,2},{4,5},{5,4},{6,7},{7,6},{8,9},{9,8},{10,11... | collective-permute-start | bytes 2457608 | tf_op jit(solution)/shard_map/ppermute | solution.py:466
  0.5 18.3 %collective-permute-start.5 = (bf16[2,160,1280]{2,1,0:T(8,128)(2,1)}, bf16[2,160,1280]{2,1,0:T(8,128)(2,1)}, u32[]{:S(2)}, u32[]{:S(2)}) collective-permute-start(bf16[2,160,1280]{2,1,0:T(8,128)(2,1)} %rest_2_.3), channel_id=1, source_target_pairs={{0,1},{1,0},{2,3},{3,2},{4,5},{5,4},{6,7},{7,6},{8,9},{9,8},{10,11... | collective-permute-start | bytes 2457608 | tf_op jit(solution)/shard_map/ppermute | solution.py:466
  0.6 18.2 %copy-start = (bf16[2,160,3200]{2,1,0:T(8,128)(2,1)S(1)}, bf16[2,160,3200]{2,1,0:T(8,128)(2,1)}, u32[]{:S(2)}) copy-start(bf16[2,160,3200]{2,1,0:T(8,128)(2,1)} %rest_1_.3) | copy-start | bytes 6144004
  3.9 1.8 %collective-permute-start.1 = (f32[64,640]{1,0:T(8,128)}, f32[64,640]{1,0:T(8,128)S(1)}, u32[]{:S(2)}, u32[]{:S(2)}) collective-permute-start(f32[64,640]{1,0:T(8,128)} %get-tuple-element.38), channel_id=1, source_target_pairs={{0,1},{1,0},{2,3},{3,2},{4,5},{5,4},{6,7},{7,6},{8,9},{9,8},{10,11... | collective-permute-start | bytes 491528 | tf_op jit(solution)/shard_map/ppermute | solution.py:466
  4.5 1.2 %collective-permute-start = (s32[384]{0:T(512)S(1)}, s32[384]{0:T(512)S(1)}, u32[]{:S(2)}, u32[]{:S(2)}) collective-permute-start(s32[384]{0:T(512)S(1)} %get-tuple-element.78), channel_id=1, source_target_pairs={{0,1},{1,0},{2,3},{3,2},{4,5},{5,4},{6,7},{7,6},{8,9},{9,8},{10,11... | collective-permute-start | bytes 4616 | tf_op jit(solution)/shard_map/ppermute | solution.py:466
  6.7 7.5 %collective-permute-start.2 = (s32[2,384]{1,0:T(2,128)S(1)}, s32[2,384]{1,0:T(2,128)S(1)}, u32[]{:S(2)}, u32[]{:S(2)}) collective-permute-start(s32[2,384]{1,0:T(2,128)S(1)} %pad_add_fusion), channel_id=1, source_target_pairs={{0,4},{1,29},{2,6},{3,31},{4,8},{5,1},{6,10},{7,3},{8,12},{9,5},{1... | collective-permute-start | bytes 9224 | tf_op jit(solution)/shard_map/ppermute | solution.py:512
  9.5 13.0 %collective-permute-start.11 = (bf16[80,1280]{1,0:T(8,128)(2,1)}, bf16[80,1280]{1,0:T(8,128)(2,1)}, u32[]{:S(2)}, u32[]{:S(2)}) collective-permute-start(bf16[80,1280]{1,0:T(8,128)(2,1)} %get-tuple-element.53), channel_id=1, source_target_pairs={{0,2},{1,3},{2,0},{3,1},{4,6},{5,7},{6,4},{7,5},{8,10},{9,11},{10,... | collective-permute-start | bytes 614408 | tf_op jit(solution)/shard_map/ppermute | solution.py:469
  11.6 5.7 %collective-permute-start.4 = (bf16[64,640]{1,0:T(8,128)(2,1)S(1)}, bf16[64,640]{1,0:T(8,128)(2,1)S(1)}, u32[]{:S(2)}, u32[]{:S(2)}) collective-permute-start(bf16[64,640]{1,0:T(8,128)(2,1)S(1)} %get-tuple-element.73), channel_id=1, source_target_pairs={{0,2},{1,3},{2,0},{3,1},{4,6},{5,7},{6,4},{7,5},{8,10},{9,11},{10,... | collective-permute-start | bytes 245768 | tf_op jit(solution)/shard_map/ppermute | solution.py:469
  14.1 8.3 %collective-permute-start.3 = (s32[384]{0:T(512)S(1)}, s32[384]{0:T(512)S(1)}, u32[]{:S(2)}, u32[]{:S(2)}) collective-permute-start(s32[384]{0:T(512)S(1)} %get-tuple-element.71), channel_id=1, source_target_pairs={{0,1},{1,0},{2,3},{3,2},{4,5},{5,4},{6,7},{7,6},{8,9},{9,8},{10,11... | collective-permute-start | bytes 4616 | tf_op jit(solution)/shard_map/ppermute | solution.py:466
  14.8 12.8 %copy-start.1 = (bf16[2,160,1280]{2,1,0:T(8,128)(2,1)S(1)}, bf16[2,160,1280]{2,1,0:T(8,128)(2,1)}, u32[]{:S(2)}) copy-start(bf16[2,160,1280]{2,1,0:T(8,128)(2,1)} %rest_2_.3) | copy-start | bytes 2457604
  17.3 13.8 %collective-permute-start.15 = (bf16[80,2304]{1,0:T(8,128)(2,1)}, bf16[80,2304]{1,0:T(8,128)(2,1)}, u32[]{:S(2)}, u32[]{:S(2)}) collective-permute-start(bf16[80,2304]{1,0:T(8,128)(2,1)} %get-tuple-element.56), channel_id=1, source_target_pairs={{0,2},{1,3},{2,0},{3,1},{4,6},{5,7},{6,4},{7,5},{8,10},{9,11},{10,... | collective-permute-start | bytes 1105928 | tf_op jit(solution)/shard_map/ppermute | solution.py:469
  20.7 5.4 %collective-permute-start.7 = (bf16[32,3200]{1,0:T(8,128)(2,1)}, bf16[32,3200]{1,0:T(8,128)(2,1)}, u32[]{:S(2)}, u32[]{:S(2)}) collective-permute-start(bf16[32,3200]{1,0:T(8,128)(2,1)} %get-tuple-element.43), channel_id=1, source_target_pairs={{0,1},{1,0},{2,3},{3,2},{4,5},{5,4},{6,7},{7,6},{8,9},{9,8},{10,11... | collective-permute-start | bytes 614408 | tf_op jit(solution)/shard_map/ppermute | solution.py:466
  22.5 9.2 %collective-permute-start.14 = (bf16[80,1280]{1,0:T(8,128)(2,1)}, bf16[80,1280]{1,0:T(8,128)(2,1)S(1)}, u32[]{:S(2)}, u32[]{:S(2)}) collective-permute-start(bf16[80,1280]{1,0:T(8,128)(2,1)} %collective-permute-done.11.rest_6_), channel_id=1, source_target_pairs={{0,12},{4,8},{8,4},{12,0},{16,28},{20,24},{24,20},{28,16},{1,13},{... | collective-permute-start | bytes 614408 | tf_op jit(solution)/shard_map/ppermute | solution.py:472
  23.6 10.5 %collective-permute-start.13 = (bf16[80,1280]{1,0:T(8,128)(2,1)}, bf16[80,1280]{1,0:T(8,128)(2,1)S(1)}, u32[]{:S(2)}, u32[]{:S(2)}) collective-permute-start(bf16[80,1280]{1,0:T(8,128)(2,1)} %collective-permute-done.11.rest_6_), channel_id=1, source_target_pairs={{0,8},{4,12},{8,0},{12,4},{16,24},{20,28},{24,16},{28,20},{1,9},{5... | collective-permute-start | bytes 614408 | tf_op jit(solution)/shard_map/ppermute | solution.py:472
  24.0 11.1 %collective-permute-start.12 = (bf16[80,1280]{1,0:T(8,128)(2,1)}, bf16[80,1280]{1,0:T(8,128)(2,1)S(1)}, u32[]{:S(2)}, u32[]{:S(2)}) collective-permute-start(bf16[80,1280]{1,0:T(8,128)(2,1)} %collective-permute-done.11.rest_6_), channel_id=1, source_target_pairs={{0,4},{4,0},{8,12},{12,8},{16,20},{20,16},{24,28},{28,24},{1,5},{5... | collective-permute-start | bytes 614408 | tf_op jit(solution)/shard_map/ppermute | solution.py:472
  27.0 8.6 %collective-permute-start.8 = (bf16[32,3200]{1,0:T(8,128)(2,1)S(1)}, bf16[32,3200]{1,0:T(8,128)(2,1)S(1)}, u32[]{:S(2)}, u32[]{:S(2)}) collective-permute-start(bf16[32,3200]{1,0:T(8,128)(2,1)S(1)} %add_convert_fusion.rest_0_), channel_id=1, source_target_pairs={{0,2},{1,3},{2,0},{3,1},{4,6},{5,7},{6,4},{7,5},{8,10},{9,11},{10,... | collective-permute-start | bytes 614408 | tf_op jit(solution)/shard_map/ppermute | solution.py:469
  28.6 11.9 %copy-start.6 = (f32[2,640]{1,0:T(2,128)S(1)}, f32[2,640]{1,0:T(2,128)}, u32[]{:S(2)}) copy-start(f32[2,640]{1,0:T(2,128)} %gain_out.3) | copy-start | bytes 15364
  31.1 5.0 %collective-permute-start.9 = (bf16[32,3200]{1,0:T(8,128)(2,1)S(1)}, bf16[32,3200]{1,0:T(8,128)(2,1)S(1)}, u32[]{:S(2)}, u32[]{:S(2)}) collective-permute-start(bf16[32,3200]{1,0:T(8,128)(2,1)S(1)} %add_convert_fusion.rest_0_), channel_id=1, source_target_pairs={{0,1},{1,0},{2,3},{3,2},{4,5},{5,4},{6,7},{7,6},{8,9},{9,8},{10,11... | collective-permute-start | bytes 614408 | tf_op jit(solution)/shard_map/ppermute | solution.py:466
  35.1 1.8 %collective-permute-start.16 = (bf16[80,1280]{1,0:T(8,128)(2,1)}, bf16[80,1280]{1,0:T(8,128)(2,1)S(1)}, u32[]{:S(2)}, u32[]{:S(2)}) collective-permute-start(bf16[80,1280]{1,0:T(8,128)(2,1)} %collective-permute-done.11.rest_6_), channel_id=1, source_target_pairs={{0,1},{1,0},{2,3},{3,2},{4,5},{5,4},{6,7},{7,6},{8,9},{9,8},{10,11... | collective-permute-start | bytes 614408 | tf_op jit(solution)/shard_map/ppermute | solution.py:466
  35.1 1.8 %collective-permute-start.17 = (bf16[80,1280]{1,0:T(8,128)(2,1)S(1)}, bf16[80,1280]{1,0:T(8,128)(2,1)S(1)}, u32[]{:S(2)}, u32[]{:S(2)}) collective-permute-start(bf16[80,1280]{1,0:T(8,128)(2,1)S(1)} %collective-permute-done.12.rest_7_), channel_id=1, source_target_pairs={{0,1},{1,0},{2,3},{3,2},{4,5},{5,4},{6,7},{7,6},{8,9},{9,8},{10,11... | collective-permute-start | bytes 614408 | tf_op jit(solution)/shard_map/ppermute | solution.py:466
  35.6 1.5 %collective-permute-start.18 = (bf16[80,1280]{1,0:T(8,128)(2,1)S(1)}, bf16[80,1280]{1,0:T(8,128)(2,1)S(1)}, u32[]{:S(2)}, u32[]{:S(2)}) collective-permute-start(bf16[80,1280]{1,0:T(8,128)(2,1)S(1)} %collective-permute-done.13.rest_8_), channel_id=1, source_target_pairs={{0,1},{1,0},{2,3},{3,2},{4,5},{5,4},{6,7},{7,6},{8,9},{9,8},{10,11... | collective-permute-start | bytes 614408 | tf_op jit(solution)/shard_map/ppermute | solution.py:466
  35.6 1.8 %collective-permute-start.19 = (bf16[80,1280]{1,0:T(8,128)(2,1)S(1)}, bf16[80,1280]{1,0:T(8,128)(2,1)S(1)}, u32[]{:S(2)}, u32[]{:S(2)}) collective-permute-start(bf16[80,1280]{1,0:T(8,128)(2,1)S(1)} %collective-permute-done.14.rest_9_), channel_id=1, source_target_pairs={{0,1},{1,0},{2,3},{3,2},{4,5},{5,4},{6,7},{7,6},{8,9},{9,8},{10,11... | collective-permute-start | bytes 614408 | tf_op jit(solution)/shard_map/ppermute | solution.py:466
  36.1 1.6 %collective-permute-start.10 = (bf16[32,3200]{1,0:T(8,128)(2,1)S(1)}, bf16[32,3200]{1,0:T(8,128)(2,1)S(1)}, u32[]{:S(2)}, u32[]{:S(2)}) collective-permute-start(bf16[32,3200]{1,0:T(8,128)(2,1)S(1)} %collective-permute-done.8.rest_1_), channel_id=1, source_target_pairs={{0,1},{1,0},{2,3},{3,2},{4,5},{5,4},{6,7},{7,6},{8,9},{9,8},{10,11... | collective-permute-start | bytes 614408 | tf_op jit(solution)/shard_map/ppermute | solution.py:466
  37.7 13.6 %collective-permute-start.20 = (bf16[2,160,3200]{2,1,0:T(8,128)(2,1)S(1)}, bf16[2,160,3200]{2,1,0:T(8,128)(2,1)S(1)}, u32[]{:S(2)}, u32[]{:S(2)}) collective-permute-start(bf16[2,160,3200]{2,1,0:T(8,128)(2,1)S(1)} %copy-done), channel_id=1, source_target_pairs={{0,1},{1,0},{2,3},{3,2},{4,5},{5,4},{6,7},{7,6},{8,9},{9,8},{10,11... | collective-permute-start | bytes 6144008 | tf_op jit(solution)/shard_map/ppermute | solution.py:466
  37.9 12.4 %collective-permute-start.22 = (bf16[80,2304]{1,0:T(8,128)(2,1)}, bf16[80,2304]{1,0:T(8,128)(2,1)S(1)}, u32[]{:S(2)}, u32[]{:S(2)}) collective-permute-start(bf16[80,2304]{1,0:T(8,128)(2,1)} %collective-permute-done.15.rest_5_), channel_id=1, source_target_pairs={{0,8},{4,12},{8,0},{12,4},{16,24},{20,28},{24,16},{28,20},{1,9},{5... | collective-permute-start | bytes 1105928 | tf_op jit(solution)/shard_map/ppermute | solution.py:472
  39.3 11.5 %collective-permute-start.21 = (bf16[80,2304]{1,0:T(8,128)(2,1)}, bf16[80,2304]{1,0:T(8,128)(2,1)S(1)}, u32[]{:S(2)}, u32[]{:S(2)}) collective-permute-start(bf16[80,2304]{1,0:T(8,128)(2,1)} %collective-permute-done.15.rest_5_), channel_id=1, source_target_pairs={{0,4},{4,0},{8,12},{12,8},{16,20},{20,16},{24,28},{28,24},{1,5},{5... | collective-permute-start | bytes 1105928 | tf_op jit(solution)/shard_map/ppermute | solution.py:472
  39.9 11.0 %collective-permute-start.23 = (bf16[80,2304]{1,0:T(8,128)(2,1)S(1)}, bf16[80,2304]{1,0:T(8,128)(2,1)S(1)}, u32[]{:S(2)}, u32[]{:S(2)}) collective-permute-start(bf16[80,2304]{1,0:T(8,128)(2,1)S(1)} %copy-done.9), channel_id=1, source_target_pairs={{0,2},{1,3},{2,0},{3,1},{4,6},{5,7},{6,4},{7,5},{8,10},{9,11},{10,... | collective-permute-start | bytes 1105928 | tf_op jit(solution)/shard_map/ppermute | solution.py:469
  50.2 2.7 %collective-permute-start.24 = (bf16[80,2304]{1,0:T(8,128)(2,1)}, bf16[80,2304]{1,0:T(8,128)(2,1)S(1)}, u32[]{:S(2)}, u32[]{:S(2)}) collective-permute-start(bf16[80,2304]{1,0:T(8,128)(2,1)} %collective-permute-done.15.rest_5_), channel_id=1, source_target_pairs={{0,1},{1,0},{2,3},{3,2},{4,5},{5,4},{6,7},{7,6},{8,9},{9,8},{10,11... | collective-permute-start | bytes 1105928 | tf_op jit(solution)/shard_map/ppermute | solution.py:466
  50.3 2.6 %collective-permute-start.26 = (bf16[80,2304]{1,0:T(8,128)(2,1)S(1)}, bf16[80,2304]{1,0:T(8,128)(2,1)S(1)}, u32[]{:S(2)}, u32[]{:S(2)}) collective-permute-start(bf16[80,2304]{1,0:T(8,128)(2,1)S(1)} %collective-permute-done.22.rest_7_), channel_id=1, source_target_pairs={{0,1},{1,0},{2,3},{3,2},{4,5},{5,4},{6,7},{7,6},{8,9},{9,8},{10,11... | collective-permute-start | bytes 1105928 | tf_op jit(solution)/shard_map/ppermute | solution.py:466
  50.8 2.2 %collective-permute-start.25 = (bf16[80,2304]{1,0:T(8,128)(2,1)S(1)}, bf16[80,2304]{1,0:T(8,128)(2,1)S(1)}, u32[]{:S(2)}, u32[]{:S(2)}) collective-permute-start(bf16[80,2304]{1,0:T(8,128)(2,1)S(1)} %collective-permute-done.21.rest_6_), channel_id=1, source_target_pairs={{0,1},{1,0},{2,3},{3,2},{4,5},{5,4},{6,7},{7,6},{8,9},{9,8},{10,11... | collective-permute-start | bytes 1105928 | tf_op jit(solution)/shard_map/ppermute | solution.py:466
  50.9 2.7 %collective-permute-start.27 = (bf16[80,2304]{1,0:T(8,128)(2,1)S(1)}, bf16[80,2304]{1,0:T(8,128)(2,1)S(1)}, u32[]{:S(2)}, u32[]{:S(2)}) collective-permute-start(bf16[80,2304]{1,0:T(8,128)(2,1)S(1)} %collective-permute-done.23.rest_8_), channel_id=1, source_target_pairs={{0,1},{1,0},{2,3},{3,2},{4,5},{5,4},{6,7},{7,6},{8,9},{9,8},{10,11... | collective-permute-start | bytes 1105928 | tf_op jit(solution)/shard_map/ppermute | solution.py:466
  (6 other events, 38.1 us)

commit v13 on v12

--- a/solution.py
+++ b/solution.py
@@ -505,14 +505,12 @@
         theirs = core_swap(jnp.where(low, *ends[::-1]))
         own = part + after(core_swap(part), theirs)
         other = x_swap(own.astype(BF))
-        far_b = x_swap(after(parts[1], own))
+        far_b = x_swap(after(parts[1], other))
         pack = jnp.stack([jnp.where(low, *ends), theirs])
         places = [(s, r) for s in range(seqs) for r in range(rolls)]
         moves = [(s * rolls + r, (s + (1, -1)[r % 2]) % seqs * rolls + r) for s, r in places]
         moved = lax.ppermute(after(pack, own), ("seq", "roll"), moves)
-        other = after(other, near_out, near_in)
-        came = core_swap(moved[1])
-        before, behind = jnp.where(low, moved[0], came), jnp.where(low, came, moved[0])
+        other = after(other, near_out, near_in, far_a)
     else:
         own = lax.psum(part, "roll")
         other = jnp.zeros((CODES, H), BF)
@@ -537,8 +535,11 @@
     if split:
         relay = after(far_a, taps[1])
         parts_a = [far_a] + [seq_swap(relay, b) for b in (1, 2, 3)]
-        sent = (taps[0] + after(core_swap(taps[1]), before, behind).astype(F32)).astype(BF)
+        sent = (taps[0] + core_swap(taps[1]).astype(F32)).astype(BF)
         received = x_swap(sent)
+    if split:
+        came = core_swap(after(moved[1], sent))
+        before, behind = jnp.where(low, moved[0], came), jnp.where(low, came, moved[0])
     spare = jnp.zeros((-(rows + 2 * REACH) % 128,), jnp.int32)
     near = jnp.concatenate([before, codes, behind, spare])[None]
     if split:

time: 59.4 us -> 63.1 us (1.062)
  waiting for transfers between devices: 11.5 us -> 14.8 us
  local copies, waits for them, and re-layouts: 1.06 us -> 4.24 us
  starting transfers between devices: 19.1 us -> 16.4 us
    unnamed x20 -> x30, local copies, waits for them, and re-layouts: 0.95 us -> 4.13 us
    ppermute x5, waiting for transfers between devices: 2.48 us -> 5.32 us  [x_swap(): return lax.ppermute(x, 'roll', [(i, i ^ 2) for i in range(rolls)])]
    ppermute x17, starting transfers between devices: 6.02 us -> 3.82 us  [core_swap(): return lax.ppermute(x, 'roll', [(i, i ^ 1) for i in range(rolls)])]
    ppermute x1, waiting for transfers between devices: 1.87 us -> 3.96 us  [per_device(): moved = lax.ppermute(after(pack, own), ('seq', 'roll'), moves)]
    ppermute x5, starting transfers between devices: 4.71 us -> 6.41 us  [x_swap(): return lax.ppermute(x, 'roll', [(i, i ^ 2) for i in range(rolls)])]
    ppermute x5, starting transfers between devices: 5.55 us -> 4.33 us  [seq_swap(): return lax.ppermute(x, 'seq', [(i, i ^ bits) for i in range(seqs)])]
    ppermute x1, starting transfers between devices: 2.84 us -> 1.82 us  [per_device(): moved = lax.ppermute(after(pack, own), ('seq', 'roll'), moves)]
    ppermute x17, waiting for transfers between devices: 3.26 us -> 2.4 us  [core_swap(): return lax.ppermute(x, 'roll', [(i, i ^ 1) for i in range(rolls)])]
  transfers between devices with their start and end apart: 28 -> 28, of which waited for: 12 -> 12; matrix products, arithmetic and copies ran while one was open for 4% -> 4% of each run, Pallas kernels for 32% -> 28%
where the time goes in v13:
time: 63.1 us; the launch traced here: 62.8 us
  Pallas kernels  24.3 us (39%)
  starting transfers between devices  16.4 us (26%)
  waiting for transfers between devices  14.8 us (23%)
  local copies, waits for them, and re-layouts  4.24 us (7%)
  other arithmetic  2.11 us (3%)
  between operations  1.02 us (2%)
    pallas_call x1, Pallas kernels, per_device(): pl.pallas_call(functools.partial(rows_kernel, split), out_shape=(jax.Shap...  10.1 us
    ppermute x5, starting transfers between devices, x_swap(): return lax.ppermute(x, 'roll', [(i, i ^ 2) for i in range(rolls)])  6.41 us
    pallas_call x1, Pallas kernels, per_device(): pl.pallas_call(functools.partial(last_kernel, split), out_shape=jax.Shape...  5.56 us
    ppermute x5, waiting for transfers between devices, x_swap(): return lax.ppermute(x, 'roll', [(i, i ^ 2) for i in range(rolls)])  5.32 us
    ppermute x5, starting transfers between devices, seq_swap(): return lax.ppermute(x, 'seq', [(i, i ^ bits) for i in range(seqs)])  4.33 us
    unnamed x30, local copies, waits for them, and re-layouts  4.13 us
    ppermute x1, waiting for transfers between devices, per_device(): moved = lax.ppermute(after(pack, own), ('seq', 'roll'), moves)  3.96 us
    ppermute x17, starting transfers between devices, core_swap(): return lax.ppermute(x, 'roll', [(i, i ^ 1) for i in range(rolls)])  3.82 us
  transfers between devices with their start and end apart: 28, of which 12 were waited for; matrix products, arithmetic and copies ran while one was open for 4% of the time, Pallas kernels for 28%

profile of v13, /device:TPU:0, one launch (start us, length us, event | category | flops | bytes accessed | tf_op | source)
XLA Modules:
  0.0 62.8 jit_solution(8207315669300239863)
XLA Ops:
  0.0 0.5 collective-permute-start.5
  0.6 3.2 %shard_map.109 = (bf16[64,1280]{1,0:T(8,128)(2,1)}, f32[64,640]{1,0:T(8,128)}, bf16[80,1280]{1,0:T(8,128)(2,1)}, bf16[80,2304]{1,0:T(8,128)(2,1)}, bf16[80,2304]{1,0:T(8,128)(2,1)}) custom-call(f32[30,1280]{1,0:T(8,128)} %embed.1, f32[1280]{0:T(1024)} %brk.1, f32[2,1280]{1,0:T(2,128)} %gain_in.1, bf16[2,320,640]{2,1,0:T(8,128)(2,1)} %rest_2_.2, ...), custom_call_target="tpu_custom_call" | custom-call | tf_op jit(solution)/shard_map/pallas_call | solution.py:482
  3.8 0.5 collective-permute-start.1
  4.5 2.9 %collective-permute-start.6 = (bf16[80,1280]{1,0:T(8,128)(2,1)}, bf16[80,1280]{1,0:T(8,128)(2,1)S(1)}, u32[]{:S(2)}, u32[]{:S(2)}) collective-permute-start(bf16[80,1280]{1,0:T(8,128)(2,1)} %get-tuple-element.41), channel_id=1, source_target_pairs={{0,2},{1,3},{2,0},{3,1},{4,6},{5,7},{6,4},{7,5},{8,10},{9,11},{10,... | collective-permute-start | bytes 614408 | tf_op jit(solution)/shard_map/ppermute | solution.py:469
  7.4 0.9 %fusion.1 = (bf16[64,640]{1,0:T(8,128)(2,1)S(1)}, f32[64,640]{1,0:T(8,128)S(1)}) fusion(f32[64,640]{1,0:T(8,128)} %get-tuple-element.38, f32[64,640]{1,0:T(8,128)S(1)} %collective-permute-done.1), kind=kLoop, calls=%fused_computation.11 | loop fusion | flops 81920 | bytes 573440 | tf_op jit(solution)/shard_map/convert_element_type | solution.py:507
  8.4 1.0 %collective-permute-start.3 = (bf16[64,640]{1,0:T(8,128)(2,1)S(1)}, bf16[64,640]{1,0:T(8,128)(2,1)S(1)}, u32[]{:S(2)}, u32[]{:S(2)}) collective-permute-start(bf16[64,640]{1,0:T(8,128)(2,1)S(1)} %get-tuple-element.73), channel_id=1, source_target_pairs={{0,2},{1,3},{2,0},{3,1},{4,6},{5,7},{6,4},{7,5},{8,10},{9,11},{10,... | collective-permute-start | bytes 245768 | tf_op jit(solution)/shard_map/ppermute | solution.py:469
  9.4 4.1 %collective-permute-done.6.rest_6_ = bf16[80,1280]{1,0:T(8,128)(2,1)S(1)} collective-permute-done((bf16[80,1280]{1,0:T(8,128)(2,1)}, bf16[80,1280]{1,0:T(8,128)(2,1)S(1)}, u32[]{:S(2)}, u32[]{:S(2)}) %collective-permute-start.6) | collective-permute-done | bytes 204832 | tf_op jit(solution)/shard_map/ppermute | solution.py:469
  13.5 1.2 %collective-permute-done.3.other = bf16[64,640]{1,0:T(8,128)(2,1)S(1)} collective-permute-done((bf16[64,640]{1,0:T(8,128)(2,1)S(1)}, bf16[64,640]{1,0:T(8,128)(2,1)S(1)}, u32[]{:S(2)}, u32[]{:S(2)}) %collective-permute-start.3) | collective-permute-done | bytes 81952 | tf_op jit(solution)/shard_map/ppermute | solution.py:469
  14.7 0.9 %copy-done.3 = bf16[2,160,1280]{2,1,0:T(8,128)(2,1)} copy-done((bf16[2,160,1280]{2,1,0:T(8,128)(2,1)}, bf16[2,160,1280]{2,1,0:T(8,128)(2,1)S(1)}, u32[]{:S(2)}) %copy-start.3) | copy-done | bytes 819224
  15.6 1.2 %shard_map.110 = (f32[32,3200]{1,0:T(8,128)S(1)}, bf16[32,3200]{1,0:T(8,128)(2,1)S(1)}) custom-call(f32[64,640]{1,0:T(8,128)S(1)} %get-tuple-element.74.own, bf16[64,640]{1,0:T(8,128)(2,1)S(1)} %collective-permute-done.3.other, f32[2,640]{1,0:T(2,128)S(1)} %copy-done.10, bf16[2,160,3200]{2,1,0:T(8,128)(2,1)S(1)} %copy-done), custom_call_target="tpu_custom_call" | custom-call | tf_op jit(solution)/shard_map/pallas_call | solution.py:522
  16.9 1.8 %collective-permute-start.2 = (s32[2,384]{1,0:T(2,128)S(1)}, s32[2,384]{1,0:T(2,128)S(1)}, u32[]{:S(2)}, u32[]{:S(2)}) collective-permute-start(s32[2,384]{1,0:T(2,128)S(1)} %pad_add_fusion), channel_id=1, source_target_pairs={{0,4},{1,29},{2,6},{3,31},{4,8},{5,1},{6,10},{7,3},{8,12},{9,5},{1... | collective-permute-start | bytes 9224 | tf_op jit(solution)/shard_map/ppermute | solution.py:512
  19.4 4.0 %collective-permute-done.2 = s32[2,384]{1,0:T(2,128)S(1)} collective-permute-done((s32[2,384]{1,0:T(2,128)S(1)}, s32[2,384]{1,0:T(2,128)S(1)}, u32[]{:S(2)}, u32[]{:S(2)}) %collective-permute-start.2) | collective-permute-done | bytes 3104 | tf_op jit(solution)/shard_map/ppermute | solution.py:512
  23.4 1.7 %collective-permute-start.15 = (bf16[80,2304]{1,0:T(8,128)(2,1)}, bf16[80,2304]{1,0:T(8,128)(2,1)}, u32[]{:S(2)}, u32[]{:S(2)}) collective-permute-start(bf16[80,2304]{1,0:T(8,128)(2,1)} %get-tuple-element.56), channel_id=1, source_target_pairs={{0,2},{1,3},{2,0},{3,1},{4,6},{5,7},{6,4},{7,5},{8,10},{9,11},{10,... | collective-permute-start | bytes 1105928 | tf_op jit(solution)/shard_map/ppermute | solution.py:469
  25.1 1.0 %add_convert_fusion.rest_0_ = bf16[32,3200]{1,0:T(8,128)(2,1)S(1)} fusion(f32[32,3200]{1,0:T(8,128)S(1)} %get-tuple-element.43, bf16[32,3200]{1,0:T(8,128)(2,1)} %collective-permute-done.7), kind=kLoop, calls=%fused_computation | loop fusion | flops 307200 | bytes 819200 | tf_op jit(solution)/shard_map/convert_element_type | solution.py:538
  26.5 3.2 %collective-permute-start.12 = (bf16[80,1280]{1,0:T(8,128)(2,1)}, bf16[80,1280]{1,0:T(8,128)(2,1)}, u32[]{:S(2)}, u32[]{:S(2)}) collective-permute-start(bf16[80,1280]{1,0:T(8,128)(2,1)} %copy-done.6), channel_id=1, source_target_pairs={{0,4},{4,0},{8,12},{12,8},{16,20},{20,16},{24,28},{28,24},{1,5},{5... | collective-permute-start | bytes 614408 | tf_op jit(solution)/shard_map/ppermute | solution.py:472
  29.7 0.4 collective-permute-start.9
  30.2 1.1 %copy-done.2 = bf16[2,320,640]{2,1,0:T(8,128)(2,1)S(1)} copy-done((bf16[2,320,640]{2,1,0:T(8,128)(2,1)S(1)}, bf16[2,320,640]{2,1,0:T(8,128)(2,1)}, u32[]{:S(2)}) %copy-start.2) | copy-done | bytes 819224
  31.3 1.1 %copy-done.4 = bf16[2,160,1280]{2,1,0:T(8,128)(2,1)S(1)} copy-done((bf16[2,160,1280]{2,1,0:T(8,128)(2,1)S(1)}, bf16[2,160,1280]{2,1,0:T(8,128)(2,1)}, u32[]{:S(2)}) %copy-start.4) | copy-done | bytes 819224
  32.5 0.9 %copy-done.8 = bf16[64,1280]{1,0:T(8,128)(2,1)S(1)} copy-done((bf16[64,1280]{1,0:T(8,128)(2,1)S(1)}, bf16[64,1280]{1,0:T(8,128)(2,1)}, u32[]{:S(2)}) %copy-start.8) | copy-done | bytes 163864
  33.4 2.7 %shard_map.111 = (bf16[1008,320]{1,0:T(8,128)(2,1)S(1)}, bf16[1008,64]{1,0:T(8,128)(2,1)S(1)}, bf16[384,1280]{1,0:T(8,128)(2,1)S(1)}, bf16[640,640]{1,0:T(8,128)(2,1)S(1)}) custom-call(s32[2]{0:T(128)S(1)} %pad_add_fusion.1.span, s32[1,1280]{1,0:T(1,128)S(1)} %broadcast_in_dim.6.near, bf16[64,1280]{1,0:T(8,128)(2,1)S(1)} %copy-done.8, ...), custom_call_target="tpu_custom_call" | custom-call | tf_op jit(solution)/shard_map/pallas_call | solution.py:554
  36.5 2.7 %collective-permute-done.12.rest_7_ = bf16[80,1280]{1,0:T(8,128)(2,1)} collective-permute-done((bf16[80,1280]{1,0:T(8,128)(2,1)}, bf16[80,1280]{1,0:T(8,128)(2,1)}, u32[]{:S(2)}, u32[]{:S(2)}) %collective-permute-start.12) | collective-permute-done | bytes 204832 | tf_op jit(solution)/shard_map/ppermute | solution.py:472
  39.3 0.5 collective-permute-start.17
  39.9 0.5 collective-permute-start.19
  40.8 0.5 collective-permute-done.17.rest_11_
  41.6 0.5 collective-permute-done.11.rest_3_
  42.4 0.8 %collective-permute-start.21 = (bf16[80,2304]{1,0:T(8,128)(2,1)}, bf16[80,2304]{1,0:T(8,128)(2,1)S(1)}, u32[]{:S(2)}, u32[]{:S(2)}) collective-permute-start(bf16[80,2304]{1,0:T(8,128)(2,1)} %collective-permute-done.15.rest_5_), channel_id=1, source_target_pairs={{0,4},{4,0},{8,12},{12,8},{16,20},{20,16},{24,28},{28,24},{1,5},{5... | collective-permute-start | bytes 1105928 | tf_op jit(solution)/shard_map/ppermute | solution.py:472
  43.6 10.1 %shard_map.112 = (bf16[1008,640]{1,0:T(8,128)(2,1)S(1)}, bf16[496,1280]{1,0:T(8,128)(2,1)S(1)}) custom-call(s32[2]{0:T(128)S(1)} %pad_add_fusion.1.span, bf16[1008,320]{1,0:T(8,128)(2,1)S(1)} %get-tuple-element.48.hot5, bf16[1008,64]{1,0:T(8,128)(2,1)S(1)} %get-tuple-element.49.hot1, f32[2,640]{1,0:T(2,128)S(1)} %copy-done.11, f32[2,1280]{1,0:T(2,128)S(1)} %copy-done.9, ...), custom_call_target="tpu_custom_call" | custom-call | tf_op jit(solution)/shard_map/pallas_call | solution.py:578
  53.8 0.5 collective-permute-start.26
  54.4 0.4 collective-permute-start.27
  54.8 1.6 %shard_map.113.rest_0_ = f32[496,640]{1,0:T(8,128)S(1)} custom-call(bf16[1008,640]{1,0:T(8,128)(2,1)S(1)} %get-tuple-element.61.ci, bf16[2,160,3200]{2,1,0:T(8,128)(2,1)S(1)} %copy-done, bf16[2,160,3200]{2,1,0:T(8,128)(2,1)S(1)} %collective-permute-done.20.near_conv.rest_3_), custom_call_target="tpu_custom_call" | custom-call | tf_op jit(solution)/shard_map/pallas_call | solution.py:598
  56.5 0.5 collective-permute-done.27.rest_12_
  57.0 5.6 %shard_map.114 = bf16[496,1280]{1,0:T(8,128)(2,1)} custom-call(bf16[1008,640]{1,0:T(8,128)(2,1)S(1)} %get-tuple-element.61.ci, bf16[496,1280]{1,0:T(8,128)(2,1)S(1)} %get-tuple-element.62.hid, f32[2,640]{1,0:T(2,128)S(1)} %copy-done.11, f32[496,640]{1,0:T(8,128)S(1)} %shard_map.113.rest_0_, bf16[2,160,3200]{2,1,0:T(8,128)(2,1)S(1)} %copy-done, ...), custom_call_target="tpu_custom_call" | custom-call | tf_op jit(solution)/shard_map/pallas_call | solution.py:608
  (72 shorter events, 3.1 us)
Async XLA Ops:
  0.0 15.6 %copy-start = (bf16[2,160,3200]{2,1,0:T(8,128)(2,1)S(1)}, bf16[2,160,3200]{2,1,0:T(8,128)(2,1)}, u32[]{:S(2)}) copy-start(bf16[2,160,3200]{2,1,0:T(8,128)(2,1)} %rest_1_.3) | copy-start | bytes 6144004
  0.0 15.6 %copy-start.10 = (f32[2,640]{1,0:T(2,128)S(1)}, f32[2,640]{1,0:T(2,128)}, u32[]{:S(2)}) copy-start(f32[2,640]{1,0:T(2,128)} %gain_mid.1) | copy-start | bytes 15364
  0.0 14.7 %collective-permute-start.5 = (bf16[2,320,640]{2,1,0:T(8,128)(2,1)}, bf16[2,320,640]{2,1,0:T(8,128)(2,1)}, u32[]{:S(2)}, u32[]{:S(2)}) collective-permute-start(bf16[2,320,640]{2,1,0:T(8,128)(2,1)} %rest_2_.2), channel_id=1, source_target_pairs={{0,1},{1,0},{2,3},{3,2},{4,5},{5,4},{6,7},{7,6},{8,9},{9,8},{10,11... | collective-permute-start | bytes 2457608 | tf_op jit(solution)/shard_map/ppermute | solution.py:466
  0.5 14.2 %collective-permute-start.4 = (bf16[2,160,1280]{2,1,0:T(8,128)(2,1)}, bf16[2,160,1280]{2,1,0:T(8,128)(2,1)S(1)}, u32[]{:S(2)}, u32[]{:S(2)}) collective-permute-start(bf16[2,160,1280]{2,1,0:T(8,128)(2,1)} %rest_2_.3), channel_id=1, source_target_pairs={{0,1},{1,0},{2,3},{3,2},{4,5},{5,4},{6,7},{7,6},{8,9},{9,8},{10,11... | collective-permute-start | bytes 2457608 | tf_op jit(solution)/shard_map/ppermute | solution.py:466
  3.8 3.7 %collective-permute-start.1 = (f32[64,640]{1,0:T(8,128)}, f32[64,640]{1,0:T(8,128)S(1)}, u32[]{:S(2)}, u32[]{:S(2)}) collective-permute-start(f32[64,640]{1,0:T(8,128)} %get-tuple-element.38), channel_id=1, source_target_pairs={{0,1},{1,0},{2,3},{3,2},{4,5},{5,4},{6,7},{7,6},{8,9},{9,8},{10,11... | collective-permute-start | bytes 491528 | tf_op jit(solution)/shard_map/ppermute | solution.py:466
  4.4 3.0 %collective-permute-start = (s32[384]{0:T(512)S(1)}, s32[384]{0:T(512)S(1)}, u32[]{:S(2)}, u32[]{:S(2)}) collective-permute-start(s32[384]{0:T(512)S(1)} %get-tuple-element.78), channel_id=1, source_target_pairs={{0,1},{1,0},{2,3},{3,2},{4,5},{5,4},{6,7},{7,6},{8,9},{9,8},{10,11... | collective-permute-start | bytes 4616 | tf_op jit(solution)/shard_map/ppermute | solution.py:466
  4.5 9.0 %collective-permute-start.6 = (bf16[80,1280]{1,0:T(8,128)(2,1)}, bf16[80,1280]{1,0:T(8,128)(2,1)S(1)}, u32[]{:S(2)}, u32[]{:S(2)}) collective-permute-start(bf16[80,1280]{1,0:T(8,128)(2,1)} %get-tuple-element.41), channel_id=1, source_target_pairs={{0,2},{1,3},{2,0},{3,1},{4,6},{5,7},{6,4},{7,5},{8,10},{9,11},{10,... | collective-permute-start | bytes 614408 | tf_op jit(solution)/shard_map/ppermute | solution.py:469
  8.4 6.3 %collective-permute-start.3 = (bf16[64,640]{1,0:T(8,128)(2,1)S(1)}, bf16[64,640]{1,0:T(8,128)(2,1)S(1)}, u32[]{:S(2)}, u32[]{:S(2)}) collective-permute-start(bf16[64,640]{1,0:T(8,128)(2,1)S(1)} %get-tuple-element.73), channel_id=1, source_target_pairs={{0,2},{1,3},{2,0},{3,1},{4,6},{5,7},{6,4},{7,5},{8,10},{9,11},{10,... | collective-permute-start | bytes 245768 | tf_op jit(solution)/shard_map/ppermute | solution.py:469
  15.6 14.5 %copy-start.1 = (bf16[2,160,1280]{2,1,0:T(8,128)(2,1)S(1)}, bf16[2,160,1280]{2,1,0:T(8,128)(2,1)}, u32[]{:S(2)}) copy-start(bf16[2,160,1280]{2,1,0:T(8,128)(2,1)} %rest_2_.3) | copy-start | bytes 2457604
  16.8 8.3 %collective-permute-start.7 = (bf16[32,3200]{1,0:T(8,128)(2,1)S(1)}, bf16[32,3200]{1,0:T(8,128)(2,1)}, u32[]{:S(2)}, u32[]{:S(2)}) collective-permute-start(bf16[32,3200]{1,0:T(8,128)(2,1)S(1)} %get-tuple-element.44), channel_id=1, source_target_pairs={{0,1},{1,0},{2,3},{3,2},{4,5},{5,4},{6,7},{7,6},{8,9},{9,8},{10,11... | collective-permute-start | bytes 614408 | tf_op jit(solution)/shard_map/ppermute | solution.py:466
  16.9 6.4 %collective-permute-start.2 = (s32[2,384]{1,0:T(2,128)S(1)}, s32[2,384]{1,0:T(2,128)S(1)}, u32[]{:S(2)}, u32[]{:S(2)}) collective-permute-start(s32[2,384]{1,0:T(2,128)S(1)} %pad_add_fusion), channel_id=1, source_target_pairs={{0,4},{1,29},{2,6},{3,31},{4,8},{5,1},{6,10},{7,3},{8,12},{9,5},{1... | collective-permute-start | bytes 9224 | tf_op jit(solution)/shard_map/ppermute | solution.py:512
  23.4 12.8 %collective-permute-start.15 = (bf16[80,2304]{1,0:T(8,128)(2,1)}, bf16[80,2304]{1,0:T(8,128)(2,1)}, u32[]{:S(2)}, u32[]{:S(2)}) collective-permute-start(bf16[80,2304]{1,0:T(8,128)(2,1)} %get-tuple-element.56), channel_id=1, source_target_pairs={{0,2},{1,3},{2,0},{3,1},{4,6},{5,7},{6,4},{7,5},{8,10},{9,11},{10,... | collective-permute-start | bytes 1105928 | tf_op jit(solution)/shard_map/ppermute | solution.py:469
  26.1 3.7 %collective-permute-start.8 = (s32[384]{0:T(512)S(1)}, s32[384]{0:T(512)S(1)}, u32[]{:S(2)}, u32[]{:S(2)}) collective-permute-start(s32[384]{0:T(512)S(1)} %get-tuple-element.45), channel_id=1, source_target_pairs={{0,1},{1,0},{2,3},{3,2},{4,5},{5,4},{6,7},{7,6},{8,9},{9,8},{10,11... | collective-permute-start | bytes 4616 | tf_op jit(solution)/shard_map/ppermute | solution.py:466
  26.2 10.0 %collective-permute-start.14 = (bf16[80,1280]{1,0:T(8,128)(2,1)}, bf16[80,1280]{1,0:T(8,128)(2,1)S(1)}, u32[]{:S(2)}, u32[]{:S(2)}) collective-permute-start(bf16[80,1280]{1,0:T(8,128)(2,1)} %copy-done.6), channel_id=1, source_target_pairs={{0,12},{4,8},{8,4},{12,0},{16,28},{20,24},{24,20},{28,16},{1,13},{... | collective-permute-start | bytes 614408 | tf_op jit(solution)/shard_map/ppermute | solution.py:472
  26.2 10.3 %collective-permute-start.13 = (bf16[80,1280]{1,0:T(8,128)(2,1)}, bf16[80,1280]{1,0:T(8,128)(2,1)S(1)}, u32[]{:S(2)}, u32[]{:S(2)}) collective-permute-start(bf16[80,1280]{1,0:T(8,128)(2,1)} %copy-done.6), channel_id=1, source_target_pairs={{0,8},{4,12},{8,0},{12,4},{16,24},{20,28},{24,16},{28,20},{1,9},{5... | collective-permute-start | bytes 614408 | tf_op jit(solution)/shard_map/ppermute | solution.py:472
  26.5 12.8 %collective-permute-start.12 = (bf16[80,1280]{1,0:T(8,128)(2,1)}, bf16[80,1280]{1,0:T(8,128)(2,1)}, u32[]{:S(2)}, u32[]{:S(2)}) collective-permute-start(bf16[80,1280]{1,0:T(8,128)(2,1)} %copy-done.6), channel_id=1, source_target_pairs={{0,4},{4,0},{8,12},{12,8},{16,20},{20,16},{24,28},{28,24},{1,5},{5... | collective-permute-start | bytes 614408 | tf_op jit(solution)/shard_map/ppermute | solution.py:472
  29.7 10.1 %collective-permute-start.9 = (bf16[32,3200]{1,0:T(8,128)(2,1)S(1)}, bf16[32,3200]{1,0:T(8,128)(2,1)}, u32[]{:S(2)}, u32[]{:S(2)}) collective-permute-start(bf16[32,3200]{1,0:T(8,128)(2,1)S(1)} %add_convert_fusion.rest_0_), channel_id=1, source_target_pairs={{0,2},{1,3},{2,0},{3,1},{4,6},{5,7},{6,4},{7,5},{8,10},{9,11},{10,... | collective-permute-start | bytes 614408 | tf_op jit(solution)/shard_map/ppermute | solution.py:469
  33.4 10.2 %copy-start.11 = (f32[2,640]{1,0:T(2,128)S(1)}, f32[2,640]{1,0:T(2,128)}, u32[]{:S(2)}) copy-start(f32[2,640]{1,0:T(2,128)} %gain_out.3) | copy-start | bytes 15364
  36.1 4.2 %collective-permute-start.10 = (bf16[32,3200]{1,0:T(8,128)(2,1)S(1)}, bf16[32,3200]{1,0:T(8,128)(2,1)S(1)}, u32[]{:S(2)}, u32[]{:S(2)}) collective-permute-start(bf16[32,3200]{1,0:T(8,128)(2,1)S(1)} %add_convert_fusion.rest_0_), channel_id=1, source_target_pairs={{0,1},{1,0},{2,3},{3,2},{4,5},{5,4},{6,7},{7,6},{8,9},{9,8},{10,11... | collective-permute-start | bytes 614408 | tf_op jit(solution)/shard_map/ppermute | solution.py:466
  39.3 1.5 %collective-permute-start.16 = (bf16[80,1280]{1,0:T(8,128)(2,1)S(1)}, bf16[80,1280]{1,0:T(8,128)(2,1)S(1)}, u32[]{:S(2)}, u32[]{:S(2)}) collective-permute-start(bf16[80,1280]{1,0:T(8,128)(2,1)S(1)} %copy-done.7), channel_id=1, source_target_pairs={{0,1},{1,0},{2,3},{3,2},{4,5},{5,4},{6,7},{7,6},{8,9},{9,8},{10,11... | collective-permute-start | bytes 614408 | tf_op jit(solution)/shard_map/ppermute | solution.py:466
  39.3 1.9 %collective-permute-start.17 = (bf16[80,1280]{1,0:T(8,128)(2,1)}, bf16[80,1280]{1,0:T(8,128)(2,1)S(1)}, u32[]{:S(2)}, u32[]{:S(2)}) collective-permute-start(bf16[80,1280]{1,0:T(8,128)(2,1)} %collective-permute-done.12.rest_7_), channel_id=1, source_target_pairs={{0,1},{1,0},{2,3},{3,2},{4,5},{5,4},{6,7},{7,6},{8,9},{9,8},{10,11... | collective-permute-start | bytes 614408 | tf_op jit(solution)/shard_map/ppermute | solution.py:466
  39.8 1.5 %collective-permute-start.18 = (bf16[80,1280]{1,0:T(8,128)(2,1)S(1)}, bf16[80,1280]{1,0:T(8,128)(2,1)S(1)}, u32[]{:S(2)}, u32[]{:S(2)}) collective-permute-start(bf16[80,1280]{1,0:T(8,128)(2,1)S(1)} %collective-permute-done.13.rest_8_), channel_id=1, source_target_pairs={{0,1},{1,0},{2,3},{3,2},{4,5},{5,4},{6,7},{7,6},{8,9},{9,8},{10,11... | collective-permute-start | bytes 614408 | tf_op jit(solution)/shard_map/ppermute | solution.py:466
  39.9 1.8 %collective-permute-start.19 = (bf16[80,1280]{1,0:T(8,128)(2,1)S(1)}, bf16[80,1280]{1,0:T(8,128)(2,1)S(1)}, u32[]{:S(2)}, u32[]{:S(2)}) collective-permute-start(bf16[80,1280]{1,0:T(8,128)(2,1)S(1)} %collective-permute-done.14.rest_9_), channel_id=1, source_target_pairs={{0,1},{1,0},{2,3},{3,2},{4,5},{5,4},{6,7},{7,6},{8,9},{9,8},{10,11... | collective-permute-start | bytes 614408 | tf_op jit(solution)/shard_map/ppermute | solution.py:466
  40.3 1.8 %collective-permute-start.11 = (bf16[32,3200]{1,0:T(8,128)(2,1)}, bf16[32,3200]{1,0:T(8,128)(2,1)S(1)}, u32[]{:S(2)}, u32[]{:S(2)}) collective-permute-start(bf16[32,3200]{1,0:T(8,128)(2,1)} %collective-permute-done.9.rest_1_), channel_id=1, source_target_pairs={{0,1},{1,0},{2,3},{3,2},{4,5},{5,4},{6,7},{7,6},{8,9},{9,8},{10,11... | collective-permute-start | bytes 614408 | tf_op jit(solution)/shard_map/ppermute | solution.py:466
  42.1 12.7 %collective-permute-start.20 = (bf16[2,160,3200]{2,1,0:T(8,128)(2,1)S(1)}, bf16[2,160,3200]{2,1,0:T(8,128)(2,1)S(1)}, u32[]{:S(2)}, u32[]{:S(2)}) collective-permute-start(bf16[2,160,3200]{2,1,0:T(8,128)(2,1)S(1)} %copy-done), channel_id=1, source_target_pairs={{0,1},{1,0},{2,3},{3,2},{4,5},{5,4},{6,7},{7,6},{8,9},{9,8},{10,11... | collective-permute-start | bytes 6144008 | tf_op jit(solution)/shard_map/ppermute | solution.py:466
  42.4 11.4 %collective-permute-start.22 = (bf16[80,2304]{1,0:T(8,128)(2,1)}, bf16[80,2304]{1,0:T(8,128)(2,1)S(1)}, u32[]{:S(2)}, u32[]{:S(2)}) collective-permute-start(bf16[80,2304]{1,0:T(8,128)(2,1)} %collective-permute-done.15.rest_5_), channel_id=1, source_target_pairs={{0,8},{4,12},{8,0},{12,4},{16,24},{20,28},{24,16},{28,20},{1,9},{5... | collective-permute-start | bytes 1105928 | tf_op jit(solution)/shard_map/ppermute | solution.py:472
  42.4 11.9 %collective-permute-start.21 = (bf16[80,2304]{1,0:T(8,128)(2,1)}, bf16[80,2304]{1,0:T(8,128)(2,1)S(1)}, u32[]{:S(2)}, u32[]{:S(2)}) collective-permute-start(bf16[80,2304]{1,0:T(8,128)(2,1)} %collective-permute-done.15.rest_5_), channel_id=1, source_target_pairs={{0,4},{4,0},{8,12},{12,8},{16,20},{20,16},{24,28},{28,24},{1,5},{5... | collective-permute-start | bytes 1105928 | tf_op jit(solution)/shard_map/ppermute | solution.py:472
  43.2 11.2 %collective-permute-start.23 = (bf16[80,2304]{1,0:T(8,128)(2,1)S(1)}, bf16[80,2304]{1,0:T(8,128)(2,1)S(1)}, u32[]{:S(2)}, u32[]{:S(2)}) collective-permute-start(bf16[80,2304]{1,0:T(8,128)(2,1)S(1)} %copy-done.14), channel_id=1, source_target_pairs={{0,2},{1,3},{2,0},{3,1},{4,6},{5,7},{6,4},{7,5},{8,10},{9,11},{10,... | collective-permute-start | bytes 1105928 | tf_op jit(solution)/shard_map/ppermute | solution.py:469
  53.7 2.7 %collective-permute-start.24 = (bf16[80,2304]{1,0:T(8,128)(2,1)}, bf16[80,2304]{1,0:T(8,128)(2,1)S(1)}, u32[]{:S(2)}, u32[]{:S(2)}) collective-permute-start(bf16[80,2304]{1,0:T(8,128)(2,1)} %collective-permute-done.15.rest_5_), channel_id=1, source_target_pairs={{0,1},{1,0},{2,3},{3,2},{4,5},{5,4},{6,7},{7,6},{8,9},{9,8},{10,11... | collective-permute-start | bytes 1105928 | tf_op jit(solution)/shard_map/ppermute | solution.py:466
  53.8 2.6 %collective-permute-start.26 = (bf16[80,2304]{1,0:T(8,128)(2,1)S(1)}, bf16[80,2304]{1,0:T(8,128)(2,1)S(1)}, u32[]{:S(2)}, u32[]{:S(2)}) collective-permute-start(bf16[80,2304]{1,0:T(8,128)(2,1)S(1)} %collective-permute-done.22.rest_7_), channel_id=1, source_target_pairs={{0,1},{1,0},{2,3},{3,2},{4,5},{5,4},{6,7},{7,6},{8,9},{9,8},{10,11... | collective-permute-start | bytes 1105928 | tf_op jit(solution)/shard_map/ppermute | solution.py:466
  54.3 2.2 %collective-permute-start.25 = (bf16[80,2304]{1,0:T(8,128)(2,1)S(1)}, bf16[80,2304]{1,0:T(8,128)(2,1)S(1)}, u32[]{:S(2)}, u32[]{:S(2)}) collective-permute-start(bf16[80,2304]{1,0:T(8,128)(2,1)S(1)} %collective-permute-done.21.rest_6_), channel_id=1, source_target_pairs={{0,1},{1,0},{2,3},{3,2},{4,5},{5,4},{6,7},{7,6},{8,9},{9,8},{10,11... | collective-permute-start | bytes 1105928 | tf_op jit(solution)/shard_map/ppermute | solution.py:466
  54.4 2.7 %collective-permute-start.27 = (bf16[80,2304]{1,0:T(8,128)(2,1)S(1)}, bf16[80,2304]{1,0:T(8,128)(2,1)S(1)}, u32[]{:S(2)}, u32[]{:S(2)}) collective-permute-start(bf16[80,2304]{1,0:T(8,128)(2,1)S(1)} %collective-permute-done.23.rest_8_), channel_id=1, source_target_pairs={{0,1},{1,0},{2,3},{3,2},{4,5},{5,4},{6,7},{7,6},{8,9},{9,8},{10,11... | collective-permute-start | bytes 1105928 | tf_op jit(solution)/shard_map/ppermute | solution.py:466
  (11 other events, 43.2 us)

commit v14 on v13

--- a/solution.py
+++ b/solution.py
@@ -533,13 +533,12 @@
         compiler_params=params(12),
     )(own, other, gain_mid, conv_w)
     if split:
+        came = core_swap(after(moved[1], taps[1]))
+        before, behind = jnp.where(low, moved[0], came), jnp.where(low, came, moved[0])
         relay = after(far_a, taps[1])
         parts_a = [far_a] + [seq_swap(relay, b) for b in (1, 2, 3)]
-        sent = (taps[0] + core_swap(taps[1]).astype(F32)).astype(BF)
+        sent = (taps[0] + after(core_swap(taps[1]), before, behind).astype(F32)).astype(BF)
         received = x_swap(sent)
-    if split:
-        came = core_swap(after(moved[1], sent))
-        before, behind = jnp.where(low, moved[0], came), jnp.where(low, came, moved[0])
     spare = jnp.zeros((-(rows + 2 * REACH) % 128,), jnp.int32)
     near = jnp.concatenate([before, codes, behind, spare])[None]
     if split:

time: 63.1 us -> 57.9 us (0.918)
  waiting for transfers between devices: 14.8 us -> 9.86 us
  starting transfers between devices: 16.4 us -> 19.6 us
  local copies, waits for them, and re-layouts: 4.24 us -> 1.06 us
    ppermute x5, waiting for transfers between devices: 5.32 us -> 1.26 us  [x_swap(): return lax.ppermute(x, 'roll', [(i, i ^ 2) for i in range(rolls)])]
    unnamed x30 -> x20, local copies, waits for them, and re-layouts: 4.13 us -> 0.95 us
    ppermute x5, starting transfers between devices: 4.33 us -> 5.67 us  [seq_swap(): return lax.ppermute(x, 'seq', [(i, i ^ bits) for i in range(seqs)])]
    ppermute x5, waiting for transfers between devices: 3.08 us -> 1.75 us  [seq_swap(): return lax.ppermute(x, 'seq', [(i, i ^ bits) for i in range(seqs)])]
    ppermute x17, waiting for transfers between devices: 2.4 us -> 3.72 us  [core_swap(): return lax.ppermute(x, 'roll', [(i, i ^ 1) for i in range(rolls)])]
    ppermute x17, starting transfers between devices: 3.82 us -> 5.02 us  [core_swap(): return lax.ppermute(x, 'roll', [(i, i ^ 1) for i in range(rolls)])]
    ppermute x5, starting transfers between devices: 6.41 us -> 7.32 us  [x_swap(): return lax.ppermute(x, 'roll', [(i, i ^ 2) for i in range(rolls)])]
    ppermute x1, waiting for transfers between devices: 3.96 us -> 3.13 us  [per_device(): moved = lax.ppermute(after(pack, own), ('seq', 'roll'), moves)]
  transfers between devices with their start and end apart: 28 -> 28, of which waited for: 12 -> 10; matrix products, arithmetic and copies ran while one was open for 4% -> 4% of each run, Pallas kernels for 28% -> 29%
where the time goes in v14:
time: 57.9 us; the launch traced here: 57.7 us
  Pallas kernels  24.1 us (42%)
  starting transfers between devices  19.6 us (34%)
  waiting for transfers between devices  9.86 us (17%)
  other arithmetic  2.1 us (4%)
  local copies, waits for them, and re-layouts  1.06 us (2%)
  between operations  1 us (2%)
    pallas_call x1, Pallas kernels, per_device(): pl.pallas_call(functools.partial(rows_kernel, split), out_shape=(jax.Shap...  9.4 us
    ppermute x5, starting transfers between devices, x_swap(): return lax.ppermute(x, 'roll', [(i, i ^ 2) for i in range(rolls)])  7.32 us
    ppermute x5, starting transfers between devices, seq_swap(): return lax.ppermute(x, 'seq', [(i, i ^ bits) for i in range(seqs)])  5.67 us
    pallas_call x1, Pallas kernels, per_device(): pl.pallas_call(functools.partial(last_kernel, split), out_shape=jax.Shape...  5.44 us
    ppermute x17, starting transfers between devices, core_swap(): return lax.ppermute(x, 'roll', [(i, i ^ 1) for i in range(rolls)])  5.02 us
    ppermute x17, waiting for transfers between devices, core_swap(): return lax.ppermute(x, 'roll', [(i, i ^ 1) for i in range(rolls)])  3.72 us
    pallas_call x1, Pallas kernels, per_device(): pl.pallas_call(functools.partial(first_kernel, split), out_shape=[jax.Sha...  3.26 us
    ppermute x1, waiting for transfers between devices, per_device(): moved = lax.ppermute(after(pack, own), ('seq', 'roll'), moves)  3.13 us
  transfers between devices with their start and end apart: 28, of which 10 were waited for; matrix products, arithmetic and copies ran while one was open for 4% of the time, Pallas kernels for 29%

profile of v14, /device:TPU:0, one launch (start us, length us, event | category | flops | bytes accessed | tf_op | source)
XLA Modules:
  0.0 57.7 jit_solution(7594716565350964249)
XLA Ops:
  0.0 0.5 collective-permute-start.5
  0.6 3.3 %shard_map.109 = (bf16[64,1280]{1,0:T(8,128)(2,1)}, f32[64,640]{1,0:T(8,128)}, bf16[80,1280]{1,0:T(8,128)(2,1)}, bf16[80,2304]{1,0:T(8,128)(2,1)}, bf16[80,2304]{1,0:T(8,128)(2,1)}) custom-call(f32[30,1280]{1,0:T(8,128)} %embed.1, f32[1280]{0:T(1024)} %brk.1, f32[2,1280]{1,0:T(2,128)} %gain_in.1, bf16[2,320,640]{2,1,0:T(8,128)(2,1)} %rest_2_.2, ...), custom_call_target="tpu_custom_call" | custom-call | tf_op jit(solution)/shard_map/pallas_call | solution.py:482
  3.9 0.5 collective-permute-start.1
  4.6 2.9 %collective-permute-start.6 = (bf16[80,1280]{1,0:T(8,128)(2,1)}, bf16[80,1280]{1,0:T(8,128)(2,1)}, u32[]{:S(2)}, u32[]{:S(2)}) collective-permute-start(bf16[80,1280]{1,0:T(8,128)(2,1)} %get-tuple-element.42), channel_id=1, source_target_pairs={{0,2},{1,3},{2,0},{3,1},{4,6},{5,7},{6,4},{7,5},{8,10},{9,11},{10,... | collective-permute-start | bytes 614408 | tf_op jit(solution)/shard_map/ppermute | solution.py:469
  7.5 0.9 %fusion.1 = (bf16[64,640]{1,0:T(8,128)(2,1)S(1)}, f32[64,640]{1,0:T(8,128)S(1)}) fusion(f32[64,640]{1,0:T(8,128)} %get-tuple-element.39, f32[64,640]{1,0:T(8,128)S(1)} %collective-permute-done.1), kind=kLoop, calls=%fused_computation.11 | loop fusion | flops 81920 | bytes 573440 | tf_op jit(solution)/shard_map/convert_element_type | solution.py:507
  8.5 1.6 %collective-permute-start.2 = (s32[2,384]{1,0:T(2,128)S(1)}, s32[2,384]{1,0:T(2,128)S(1)}, u32[]{:S(2)}, u32[]{:S(2)}) collective-permute-start(s32[2,384]{1,0:T(2,128)S(1)} %pad_add_fusion), channel_id=1, source_target_pairs={{0,4},{1,29},{2,6},{3,31},{4,8},{5,1},{6,10},{7,3},{8,12},{9,5},{1... | collective-permute-start | bytes 9224 | tf_op jit(solution)/shard_map/ppermute | solution.py:512
  10.7 1.0 %collective-permute-start.3 = (bf16[64,640]{1,0:T(8,128)(2,1)S(1)}, bf16[64,640]{1,0:T(8,128)(2,1)S(1)}, u32[]{:S(2)}, u32[]{:S(2)}) collective-permute-start(bf16[64,640]{1,0:T(8,128)(2,1)S(1)} %get-tuple-element.75), channel_id=1, source_target_pairs={{0,2},{1,3},{2,0},{3,1},{4,6},{5,7},{6,4},{7,5},{8,10},{9,11},{10,... | collective-permute-start | bytes 245768 | tf_op jit(solution)/shard_map/ppermute | solution.py:469
  11.7 3.1 %collective-permute-done.2 = s32[2,384]{1,0:T(2,128)S(1)} collective-permute-done((s32[2,384]{1,0:T(2,128)S(1)}, s32[2,384]{1,0:T(2,128)S(1)}, u32[]{:S(2)}, u32[]{:S(2)}) %collective-permute-start.2) | collective-permute-done | bytes 3104 | tf_op jit(solution)/shard_map/ppermute | solution.py:512
  15.2 1.9 %shard_map.110 = (f32[32,3200]{1,0:T(8,128)S(1)}, bf16[32,3200]{1,0:T(8,128)(2,1)}) custom-call(f32[64,640]{1,0:T(8,128)S(1)} %get-tuple-element.76.own, bf16[64,640]{1,0:T(8,128)(2,1)S(1)} %collective-permute-done.3.other, f32[2,640]{1,0:T(2,128)S(1)} %copy-done.5, bf16[2,160,3200]{2,1,0:T(8,128)(2,1)S(1)} %copy-done), custom_call_target="tpu_custom_call" | custom-call | tf_op jit(solution)/shard_map/pallas_call | solution.py:522
  17.1 1.5 %collective-permute-start.7 = (s32[384]{0:T(512)S(1)}, s32[384]{0:T(512)S(1)}, u32[]{:S(2)}, u32[]{:S(2)}) collective-permute-start(s32[384]{0:T(512)S(1)} %get-tuple-element.45), channel_id=1, source_target_pairs={{0,1},{1,0},{2,3},{3,2},{4,5},{5,4},{6,7},{7,6},{8,9},{9,8},{10,11... | collective-permute-start | bytes 4616 | tf_op jit(solution)/shard_map/ppermute | solution.py:466
  18.7 1.4 %collective-permute-start.15 = (bf16[80,2304]{1,0:T(8,128)(2,1)}, bf16[80,2304]{1,0:T(8,128)(2,1)}, u32[]{:S(2)}, u32[]{:S(2)}) collective-permute-start(bf16[80,2304]{1,0:T(8,128)(2,1)} %get-tuple-element.58), channel_id=1, source_target_pairs={{0,2},{1,3},{2,0},{3,1},{4,6},{5,7},{6,4},{7,5},{8,10},{9,11},{10,... | collective-permute-start | bytes 1105928 | tf_op jit(solution)/shard_map/ppermute | solution.py:469
  20.0 1.1 %collective-permute-start.14 = (bf16[80,1280]{1,0:T(8,128)(2,1)}, bf16[80,1280]{1,0:T(8,128)(2,1)}, u32[]{:S(2)}, u32[]{:S(2)}) collective-permute-start(bf16[80,1280]{1,0:T(8,128)(2,1)} %collective-permute-done.6.rest_6_), channel_id=1, source_target_pairs={{0,12},{4,8},{8,4},{12,0},{16,28},{20,24},{24,20},{28,16},{1,13},{... | collective-permute-start | bytes 614408 | tf_op jit(solution)/shard_map/ppermute | solution.py:472
  21.6 1.9 %collective-permute-start.12 = (bf16[80,1280]{1,0:T(8,128)(2,1)}, bf16[80,1280]{1,0:T(8,128)(2,1)}, u32[]{:S(2)}, u32[]{:S(2)}) collective-permute-start(bf16[80,1280]{1,0:T(8,128)(2,1)} %collective-permute-done.6.rest_6_), channel_id=1, source_target_pairs={{0,4},{4,0},{8,12},{12,8},{16,20},{20,16},{24,28},{28,24},{1,5},{5... | collective-permute-start | bytes 614408 | tf_op jit(solution)/shard_map/ppermute | solution.py:472
  23.6 1.7 %collective-permute-done.8 = bf16[32,3200]{1,0:T(8,128)(2,1)} collective-permute-done((bf16[32,3200]{1,0:T(8,128)(2,1)}, bf16[32,3200]{1,0:T(8,128)(2,1)}, u32[]{:S(2)}, u32[]{:S(2)}) %collective-permute-start.8) | collective-permute-done | bytes 204832 | tf_op jit(solution)/shard_map/ppermute | solution.py:466
  25.3 1.0 %add_convert_fusion.rest_0_ = bf16[32,3200]{1,0:T(8,128)(2,1)S(1)} fusion(f32[32,3200]{1,0:T(8,128)S(1)} %get-tuple-element.46, bf16[32,3200]{1,0:T(8,128)(2,1)} %collective-permute-done.8), kind=kLoop, calls=%fused_computation | loop fusion | flops 307200 | bytes 819200 | tf_op jit(solution)/shard_map/convert_element_type | solution.py:540
  26.3 0.7 %collective-permute-start.9 = (bf16[32,3200]{1,0:T(8,128)(2,1)S(1)}, bf16[32,3200]{1,0:T(8,128)(2,1)S(1)}, u32[]{:S(2)}, u32[]{:S(2)}) collective-permute-start(bf16[32,3200]{1,0:T(8,128)(2,1)S(1)} %add_convert_fusion.rest_0_), channel_id=1, source_target_pairs={{0,2},{1,3},{2,0},{3,1},{4,6},{5,7},{6,4},{7,5},{8,10},{9,11},{10,... | collective-permute-start | bytes 614408 | tf_op jit(solution)/shard_map/ppermute | solution.py:469
  27.0 0.9 %copy-done.3 = bf16[64,1280]{1,0:T(8,128)(2,1)S(1)} copy-done((bf16[64,1280]{1,0:T(8,128)(2,1)S(1)}, bf16[64,1280]{1,0:T(8,128)(2,1)}, u32[]{:S(2)}) %copy-start.3) | copy-done | bytes 163864
  27.9 2.5 %shard_map.111 = (bf16[1008,320]{1,0:T(8,128)(2,1)S(1)}, bf16[1008,64]{1,0:T(8,128)(2,1)S(1)}, bf16[384,1280]{1,0:T(8,128)(2,1)S(1)}, bf16[640,640]{1,0:T(8,128)(2,1)S(1)}) custom-call(s32[2]{0:T(128)S(1)} %pad_add_fusion.1.span, s32[1,1280]{1,0:T(1,128)S(1)} %broadcast_in_dim.6.near, bf16[64,1280]{1,0:T(8,128)(2,1)S(1)} %copy-done.3, ...), custom_call_target="tpu_custom_call" | custom-call | tf_op jit(solution)/shard_map/pallas_call | solution.py:553
  30.6 0.9 %collective-permute-done.13.rest_8_ = bf16[80,1280]{1,0:T(8,128)(2,1)} collective-permute-done((bf16[80,1280]{1,0:T(8,128)(2,1)}, bf16[80,1280]{1,0:T(8,128)(2,1)}, u32[]{:S(2)}, u32[]{:S(2)}) %collective-permute-start.13) | collective-permute-done | bytes 204832 | tf_op jit(solution)/shard_map/ppermute | solution.py:472
  31.5 0.9 %collective-permute-done.12.rest_7_ = bf16[80,1280]{1,0:T(8,128)(2,1)} collective-permute-done((bf16[80,1280]{1,0:T(8,128)(2,1)}, bf16[80,1280]{1,0:T(8,128)(2,1)}, u32[]{:S(2)}, u32[]{:S(2)}) %collective-permute-start.12) | collective-permute-done | bytes 204832 | tf_op jit(solution)/shard_map/ppermute | solution.py:472
  32.4 0.5 collective-permute-start.17
  32.9 0.9 %collective-permute-done.9.rest_1_ = bf16[32,3200]{1,0:T(8,128)(2,1)S(1)} collective-permute-done((bf16[32,3200]{1,0:T(8,128)(2,1)S(1)}, bf16[32,3200]{1,0:T(8,128)(2,1)S(1)}, u32[]{:S(2)}, u32[]{:S(2)}) %collective-permute-start.9) | collective-permute-done | bytes 204832 | tf_op jit(solution)/shard_map/ppermute | solution.py:469
  33.8 0.5 collective-permute-start.11
  34.6 1.1 %collective-permute-done.19.rest_13_ = bf16[80,1280]{1,0:T(8,128)(2,1)S(1)} collective-permute-done((bf16[80,1280]{1,0:T(8,128)(2,1)}, bf16[80,1280]{1,0:T(8,128)(2,1)S(1)}, u32[]{:S(2)}, u32[]{:S(2)}) %collective-permute-start.19) | collective-permute-done | bytes 204832 | tf_op jit(solution)/shard_map/ppermute | solution.py:466
  35.8 0.7 %collective-permute-start.22 = (bf16[80,2304]{1,0:T(8,128)(2,1)}, bf16[80,2304]{1,0:T(8,128)(2,1)S(1)}, u32[]{:S(2)}, u32[]{:S(2)}) collective-permute-start(bf16[80,2304]{1,0:T(8,128)(2,1)} %collective-permute-done.15.rest_5_), channel_id=1, source_target_pairs={{0,8},{4,12},{8,0},{12,4},{16,24},{20,28},{24,16},{28,20},{1,9},{5... | collective-permute-start | bytes 1105928 | tf_op jit(solution)/shard_map/ppermute | solution.py:472
  36.5 1.5 %collective-permute-start.21 = (bf16[80,2304]{1,0:T(8,128)(2,1)}, bf16[80,2304]{1,0:T(8,128)(2,1)S(1)}, u32[]{:S(2)}, u32[]{:S(2)}) collective-permute-start(bf16[80,2304]{1,0:T(8,128)(2,1)} %collective-permute-done.15.rest_5_), channel_id=1, source_target_pairs={{0,4},{4,0},{8,12},{12,8},{16,20},{20,16},{24,28},{28,24},{1,5},{5... | collective-permute-start | bytes 1105928 | tf_op jit(solution)/shard_map/ppermute | solution.py:472
  38.0 1.3 %collective-permute-start.23 = (bf16[80,2304]{1,0:T(8,128)(2,1)S(1)}, bf16[80,2304]{1,0:T(8,128)(2,1)S(1)}, u32[]{:S(2)}, u32[]{:S(2)}) collective-permute-start(bf16[80,2304]{1,0:T(8,128)(2,1)S(1)} %copy-done.9), channel_id=1, source_target_pairs={{0,2},{1,3},{2,0},{3,1},{4,6},{5,7},{6,4},{7,5},{8,10},{9,11},{10,... | collective-permute-start | bytes 1105928 | tf_op jit(solution)/shard_map/ppermute | solution.py:469
  39.3 9.4 %shard_map.112 = (bf16[1008,640]{1,0:T(8,128)(2,1)S(1)}, bf16[496,1280]{1,0:T(8,128)(2,1)S(1)}) custom-call(s32[2]{0:T(128)S(1)} %pad_add_fusion.1.span, bf16[1008,320]{1,0:T(8,128)(2,1)S(1)} %get-tuple-element.50.hot5, bf16[1008,64]{1,0:T(8,128)(2,1)S(1)} %get-tuple-element.51.hot1, f32[2,640]{1,0:T(2,128)S(1)} %copy-done.6, f32[2,1280]{1,0:T(2,128)S(1)} %copy-done.4, ...), custom_call_target="tpu_custom_call" | custom-call | tf_op jit(solution)/shard_map/pallas_call | solution.py:577
  48.8 0.5 collective-permute-start.26
  49.8 1.6 %shard_map.113.rest_0_ = f32[496,640]{1,0:T(8,128)S(1)} custom-call(bf16[1008,640]{1,0:T(8,128)(2,1)S(1)} %get-tuple-element.63.ci, bf16[2,160,3200]{2,1,0:T(8,128)(2,1)S(1)} %copy-done, bf16[2,160,3200]{2,1,0:T(8,128)(2,1)S(1)} %collective-permute-done.20.near_conv.rest_3_), custom_call_target="tpu_custom_call" | custom-call | tf_op jit(solution)/shard_map/pallas_call | solution.py:597
  51.5 0.5 collective-permute-done.27.rest_12_
  52.1 5.4 %shard_map.114 = bf16[496,1280]{1,0:T(8,128)(2,1)} custom-call(bf16[1008,640]{1,0:T(8,128)(2,1)S(1)} %get-tuple-element.63.ci, bf16[496,1280]{1,0:T(8,128)(2,1)S(1)} %get-tuple-element.64.hid, f32[2,640]{1,0:T(2,128)S(1)} %copy-done.6, f32[496,640]{1,0:T(8,128)S(1)} %shard_map.113.rest_0_, bf16[2,160,3200]{2,1,0:T(8,128)(2,1)S(1)} %copy-done, ...), custom_call_target="tpu_custom_call" | custom-call | tf_op jit(solution)/shard_map/pallas_call | solution.py:607
  (62 shorter events, 2.6 us)
Async XLA Ops:
  0.0 15.2 %copy-start.5 = (f32[2,640]{1,0:T(2,128)S(1)}, f32[2,640]{1,0:T(2,128)}, u32[]{:S(2)}) copy-start(f32[2,640]{1,0:T(2,128)} %gain_mid.1) | copy-start | bytes 15364
  0.0 15.2 %collective-permute-start.5 = (bf16[2,320,640]{2,1,0:T(8,128)(2,1)}, bf16[2,320,640]{2,1,0:T(8,128)(2,1)}, u32[]{:S(2)}, u32[]{:S(2)}) collective-permute-start(bf16[2,320,640]{2,1,0:T(8,128)(2,1)} %rest_2_.2), channel_id=1, source_target_pairs={{0,1},{1,0},{2,3},{3,2},{4,5},{5,4},{6,7},{7,6},{8,9},{9,8},{10,11... | collective-permute-start | bytes 2457608 | tf_op jit(solution)/shard_map/ppermute | solution.py:466
  0.5 14.7 %collective-permute-start.4 = (bf16[2,160,1280]{2,1,0:T(8,128)(2,1)}, bf16[2,160,1280]{2,1,0:T(8,128)(2,1)}, u32[]{:S(2)}, u32[]{:S(2)}) collective-permute-start(bf16[2,160,1280]{2,1,0:T(8,128)(2,1)} %rest_2_.3), channel_id=1, source_target_pairs={{0,1},{1,0},{2,3},{3,2},{4,5},{5,4},{6,7},{7,6},{8,9},{9,8},{10,11... | collective-permute-start | bytes 2457608 | tf_op jit(solution)/shard_map/ppermute | solution.py:466
  0.6 14.6 %copy-start = (bf16[2,160,3200]{2,1,0:T(8,128)(2,1)S(1)}, bf16[2,160,3200]{2,1,0:T(8,128)(2,1)}, u32[]{:S(2)}) copy-start(bf16[2,160,3200]{2,1,0:T(8,128)(2,1)} %rest_1_.3) | copy-start | bytes 6144004
  3.9 3.7 %collective-permute-start.1 = (f32[64,640]{1,0:T(8,128)}, f32[64,640]{1,0:T(8,128)S(1)}, u32[]{:S(2)}, u32[]{:S(2)}) collective-permute-start(f32[64,640]{1,0:T(8,128)} %get-tuple-element.39), channel_id=1, source_target_pairs={{0,1},{1,0},{2,3},{3,2},{4,5},{5,4},{6,7},{7,6},{8,9},{9,8},{10,11... | collective-permute-start | bytes 491528 | tf_op jit(solution)/shard_map/ppermute | solution.py:466
  4.5 3.0 %collective-permute-start = (s32[384]{0:T(512)S(1)}, s32[384]{0:T(512)S(1)}, u32[]{:S(2)}, u32[]{:S(2)}) collective-permute-start(s32[384]{0:T(512)S(1)} %get-tuple-element.80), channel_id=1, source_target_pairs={{0,1},{1,0},{2,3},{3,2},{4,5},{5,4},{6,7},{7,6},{8,9},{9,8},{10,11... | collective-permute-start | bytes 4616 | tf_op jit(solution)/shard_map/ppermute | solution.py:466
  4.6 10.3 %collective-permute-start.6 = (bf16[80,1280]{1,0:T(8,128)(2,1)}, bf16[80,1280]{1,0:T(8,128)(2,1)}, u32[]{:S(2)}, u32[]{:S(2)}) collective-permute-start(bf16[80,1280]{1,0:T(8,128)(2,1)} %get-tuple-element.42), channel_id=1, source_target_pairs={{0,2},{1,3},{2,0},{3,1},{4,6},{5,7},{6,4},{7,5},{8,10},{9,11},{10,... | collective-permute-start | bytes 614408 | tf_op jit(solution)/shard_map/ppermute | solution.py:469
  8.5 6.3 %collective-permute-start.2 = (s32[2,384]{1,0:T(2,128)S(1)}, s32[2,384]{1,0:T(2,128)S(1)}, u32[]{:S(2)}, u32[]{:S(2)}) collective-permute-start(s32[2,384]{1,0:T(2,128)S(1)} %pad_add_fusion), channel_id=1, source_target_pairs={{0,4},{1,29},{2,6},{3,31},{4,8},{5,1},{6,10},{7,3},{8,12},{9,5},{1... | collective-permute-start | bytes 9224 | tf_op jit(solution)/shard_map/ppermute | solution.py:512
  10.7 4.5 %collective-permute-start.3 = (bf16[64,640]{1,0:T(8,128)(2,1)S(1)}, bf16[64,640]{1,0:T(8,128)(2,1)S(1)}, u32[]{:S(2)}, u32[]{:S(2)}) collective-permute-start(bf16[64,640]{1,0:T(8,128)(2,1)S(1)} %get-tuple-element.75), channel_id=1, source_target_pairs={{0,2},{1,3},{2,0},{3,1},{4,6},{5,7},{6,4},{7,5},{8,10},{9,11},{10,... | collective-permute-start | bytes 245768 | tf_op jit(solution)/shard_map/ppermute | solution.py:469
  14.9 12.2 %copy-start.1 = (bf16[2,160,1280]{2,1,0:T(8,128)(2,1)S(1)}, bf16[2,160,1280]{2,1,0:T(8,128)(2,1)}, u32[]{:S(2)}) copy-start(bf16[2,160,1280]{2,1,0:T(8,128)(2,1)} %rest_2_.3) | copy-start | bytes 2457604
  17.1 6.4 %collective-permute-start.7 = (s32[384]{0:T(512)S(1)}, s32[384]{0:T(512)S(1)}, u32[]{:S(2)}, u32[]{:S(2)}) collective-permute-start(s32[384]{0:T(512)S(1)} %get-tuple-element.45), channel_id=1, source_target_pairs={{0,1},{1,0},{2,3},{3,2},{4,5},{5,4},{6,7},{7,6},{8,9},{9,8},{10,11... | collective-permute-start | bytes 4616 | tf_op jit(solution)/shard_map/ppermute | solution.py:466
  18.7 11.8 %collective-permute-start.15 = (bf16[80,2304]{1,0:T(8,128)(2,1)}, bf16[80,2304]{1,0:T(8,128)(2,1)}, u32[]{:S(2)}, u32[]{:S(2)}) collective-permute-start(bf16[80,2304]{1,0:T(8,128)(2,1)} %get-tuple-element.58), channel_id=1, source_target_pairs={{0,2},{1,3},{2,0},{3,1},{4,6},{5,7},{6,4},{7,5},{8,10},{9,11},{10,... | collective-permute-start | bytes 1105928 | tf_op jit(solution)/shard_map/ppermute | solution.py:469
  20.0 10.6 %collective-permute-start.14 = (bf16[80,1280]{1,0:T(8,128)(2,1)}, bf16[80,1280]{1,0:T(8,128)(2,1)}, u32[]{:S(2)}, u32[]{:S(2)}) collective-permute-start(bf16[80,1280]{1,0:T(8,128)(2,1)} %collective-permute-done.6.rest_6_), channel_id=1, source_target_pairs={{0,12},{4,8},{8,4},{12,0},{16,28},{20,24},{24,20},{28,16},{1,13},{... | collective-permute-start | bytes 614408 | tf_op jit(solution)/shard_map/ppermute | solution.py:472
  21.1 10.4 %collective-permute-start.13 = (bf16[80,1280]{1,0:T(8,128)(2,1)}, bf16[80,1280]{1,0:T(8,128)(2,1)}, u32[]{:S(2)}, u32[]{:S(2)}) collective-permute-start(bf16[80,1280]{1,0:T(8,128)(2,1)} %collective-permute-done.6.rest_6_), channel_id=1, source_target_pairs={{0,8},{4,12},{8,0},{12,4},{16,24},{20,28},{24,16},{28,20},{1,9},{5... | collective-permute-start | bytes 614408 | tf_op jit(solution)/shard_map/ppermute | solution.py:472
  21.6 10.8 %collective-permute-start.12 = (bf16[80,1280]{1,0:T(8,128)(2,1)}, bf16[80,1280]{1,0:T(8,128)(2,1)}, u32[]{:S(2)}, u32[]{:S(2)}) collective-permute-start(bf16[80,1280]{1,0:T(8,128)(2,1)} %collective-permute-done.6.rest_6_), channel_id=1, source_target_pairs={{0,4},{4,0},{8,12},{12,8},{16,20},{20,16},{24,28},{28,24},{1,5},{5... | collective-permute-start | bytes 614408 | tf_op jit(solution)/shard_map/ppermute | solution.py:472
  23.5 1.8 %collective-permute-start.8 = (bf16[32,3200]{1,0:T(8,128)(2,1)}, bf16[32,3200]{1,0:T(8,128)(2,1)}, u32[]{:S(2)}, u32[]{:S(2)}) collective-permute-start(bf16[32,3200]{1,0:T(8,128)(2,1)} %get-tuple-element.44), channel_id=1, source_target_pairs={{0,1},{1,0},{2,3},{3,2},{4,5},{5,4},{6,7},{7,6},{8,9},{9,8},{10,11... | collective-permute-start | bytes 614408 | tf_op jit(solution)/shard_map/ppermute | solution.py:466
  26.3 7.5 %collective-permute-start.9 = (bf16[32,3200]{1,0:T(8,128)(2,1)S(1)}, bf16[32,3200]{1,0:T(8,128)(2,1)S(1)}, u32[]{:S(2)}, u32[]{:S(2)}) collective-permute-start(bf16[32,3200]{1,0:T(8,128)(2,1)S(1)} %add_convert_fusion.rest_0_), channel_id=1, source_target_pairs={{0,2},{1,3},{2,0},{3,1},{4,6},{5,7},{6,4},{7,5},{8,10},{9,11},{10,... | collective-permute-start | bytes 614408 | tf_op jit(solution)/shard_map/ppermute | solution.py:469
  27.9 11.4 %copy-start.6 = (f32[2,640]{1,0:T(2,128)S(1)}, f32[2,640]{1,0:T(2,128)}, u32[]{:S(2)}) copy-start(f32[2,640]{1,0:T(2,128)} %gain_out.3) | copy-start | bytes 15364
  30.5 3.3 %collective-permute-start.10 = (bf16[32,3200]{1,0:T(8,128)(2,1)S(1)}, bf16[32,3200]{1,0:T(8,128)(2,1)S(1)}, u32[]{:S(2)}, u32[]{:S(2)}) collective-permute-start(bf16[32,3200]{1,0:T(8,128)(2,1)S(1)} %add_convert_fusion.rest_0_), channel_id=1, source_target_pairs={{0,1},{1,0},{2,3},{3,2},{4,5},{5,4},{6,7},{7,6},{8,9},{9,8},{10,11... | collective-permute-start | bytes 614408 | tf_op jit(solution)/shard_map/ppermute | solution.py:466
  32.3 2.0 %collective-permute-start.16 = (bf16[80,1280]{1,0:T(8,128)(2,1)}, bf16[80,1280]{1,0:T(8,128)(2,1)S(1)}, u32[]{:S(2)}, u32[]{:S(2)}) collective-permute-start(bf16[80,1280]{1,0:T(8,128)(2,1)} %collective-permute-done.6.rest_6_), channel_id=1, source_target_pairs={{0,1},{1,0},{2,3},{3,2},{4,5},{5,4},{6,7},{7,6},{8,9},{9,8},{10,11... | collective-permute-start | bytes 614408 | tf_op jit(solution)/shard_map/ppermute | solution.py:466
  32.4 1.9 %collective-permute-start.17 = (bf16[80,1280]{1,0:T(8,128)(2,1)}, bf16[80,1280]{1,0:T(8,128)(2,1)S(1)}, u32[]{:S(2)}, u32[]{:S(2)}) collective-permute-start(bf16[80,1280]{1,0:T(8,128)(2,1)} %collective-permute-done.12.rest_7_), channel_id=1, source_target_pairs={{0,1},{1,0},{2,3},{3,2},{4,5},{5,4},{6,7},{7,6},{8,9},{9,8},{10,11... | collective-permute-start | bytes 614408 | tf_op jit(solution)/shard_map/ppermute | solution.py:466
  32.9 1.7 %collective-permute-start.18 = (bf16[80,1280]{1,0:T(8,128)(2,1)}, bf16[80,1280]{1,0:T(8,128)(2,1)S(1)}, u32[]{:S(2)}, u32[]{:S(2)}) collective-permute-start(bf16[80,1280]{1,0:T(8,128)(2,1)} %collective-permute-done.13.rest_8_), channel_id=1, source_target_pairs={{0,1},{1,0},{2,3},{3,2},{4,5},{5,4},{6,7},{7,6},{8,9},{9,8},{10,11... | collective-permute-start | bytes 614408 | tf_op jit(solution)/shard_map/ppermute | solution.py:466
  33.8 1.9 %collective-permute-start.19 = (bf16[80,1280]{1,0:T(8,128)(2,1)}, bf16[80,1280]{1,0:T(8,128)(2,1)S(1)}, u32[]{:S(2)}, u32[]{:S(2)}) collective-permute-start(bf16[80,1280]{1,0:T(8,128)(2,1)} %collective-permute-done.14.rest_9_), channel_id=1, source_target_pairs={{0,1},{1,0},{2,3},{3,2},{4,5},{5,4},{6,7},{7,6},{8,9},{9,8},{10,11... | collective-permute-start | bytes 614408 | tf_op jit(solution)/shard_map/ppermute | solution.py:466
  33.8 1.9 %collective-permute-start.11 = (bf16[32,3200]{1,0:T(8,128)(2,1)S(1)}, bf16[32,3200]{1,0:T(8,128)(2,1)S(1)}, u32[]{:S(2)}, u32[]{:S(2)}) collective-permute-start(bf16[32,3200]{1,0:T(8,128)(2,1)S(1)} %collective-permute-done.9.rest_1_), channel_id=1, source_target_pairs={{0,1},{1,0},{2,3},{3,2},{4,5},{5,4},{6,7},{7,6},{8,9},{9,8},{10,11... | collective-permute-start | bytes 614408 | tf_op jit(solution)/shard_map/ppermute | solution.py:466
  35.7 14.2 %collective-permute-start.20 = (bf16[2,160,3200]{2,1,0:T(8,128)(2,1)S(1)}, bf16[2,160,3200]{2,1,0:T(8,128)(2,1)S(1)}, u32[]{:S(2)}, u32[]{:S(2)}) collective-permute-start(bf16[2,160,3200]{2,1,0:T(8,128)(2,1)S(1)} %copy-done), channel_id=1, source_target_pairs={{0,1},{1,0},{2,3},{3,2},{4,5},{5,4},{6,7},{7,6},{8,9},{9,8},{10,11... | collective-permute-start | bytes 6144008 | tf_op jit(solution)/shard_map/ppermute | solution.py:466
  35.8 13.0 %collective-permute-start.22 = (bf16[80,2304]{1,0:T(8,128)(2,1)}, bf16[80,2304]{1,0:T(8,128)(2,1)S(1)}, u32[]{:S(2)}, u32[]{:S(2)}) collective-permute-start(bf16[80,2304]{1,0:T(8,128)(2,1)} %collective-permute-done.15.rest_5_), channel_id=1, source_target_pairs={{0,8},{4,12},{8,0},{12,4},{16,24},{20,28},{24,16},{28,20},{1,9},{5... | collective-permute-start | bytes 1105928 | tf_op jit(solution)/shard_map/ppermute | solution.py:472
  36.5 12.8 %collective-permute-start.21 = (bf16[80,2304]{1,0:T(8,128)(2,1)}, bf16[80,2304]{1,0:T(8,128)(2,1)S(1)}, u32[]{:S(2)}, u32[]{:S(2)}) collective-permute-start(bf16[80,2304]{1,0:T(8,128)(2,1)} %collective-permute-done.15.rest_5_), channel_id=1, source_target_pairs={{0,4},{4,0},{8,12},{12,8},{16,20},{20,16},{24,28},{28,24},{1,5},{5... | collective-permute-start | bytes 1105928 | tf_op jit(solution)/shard_map/ppermute | solution.py:472
  38.0 11.4 %collective-permute-start.23 = (bf16[80,2304]{1,0:T(8,128)(2,1)S(1)}, bf16[80,2304]{1,0:T(8,128)(2,1)S(1)}, u32[]{:S(2)}, u32[]{:S(2)}) collective-permute-start(bf16[80,2304]{1,0:T(8,128)(2,1)S(1)} %copy-done.9), channel_id=1, source_target_pairs={{0,2},{1,3},{2,0},{3,1},{4,6},{5,7},{6,4},{7,5},{8,10},{9,11},{10,... | collective-permute-start | bytes 1105928 | tf_op jit(solution)/shard_map/ppermute | solution.py:469
  48.7 2.7 %collective-permute-start.24 = (bf16[80,2304]{1,0:T(8,128)(2,1)}, bf16[80,2304]{1,0:T(8,128)(2,1)S(1)}, u32[]{:S(2)}, u32[]{:S(2)}) collective-permute-start(bf16[80,2304]{1,0:T(8,128)(2,1)} %collective-permute-done.15.rest_5_), channel_id=1, source_target_pairs={{0,1},{1,0},{2,3},{3,2},{4,5},{5,4},{6,7},{7,6},{8,9},{9,8},{10,11... | collective-permute-start | bytes 1105928 | tf_op jit(solution)/shard_map/ppermute | solution.py:466
  48.8 2.6 %collective-permute-start.26 = (bf16[80,2304]{1,0:T(8,128)(2,1)S(1)}, bf16[80,2304]{1,0:T(8,128)(2,1)S(1)}, u32[]{:S(2)}, u32[]{:S(2)}) collective-permute-start(bf16[80,2304]{1,0:T(8,128)(2,1)S(1)} %collective-permute-done.22.rest_7_), channel_id=1, source_target_pairs={{0,1},{1,0},{2,3},{3,2},{4,5},{5,4},{6,7},{7,6},{8,9},{9,8},{10,11... | collective-permute-start | bytes 1105928 | tf_op jit(solution)/shard_map/ppermute | solution.py:466
  49.3 2.2 %collective-permute-start.25 = (bf16[80,2304]{1,0:T(8,128)(2,1)S(1)}, bf16[80,2304]{1,0:T(8,128)(2,1)S(1)}, u32[]{:S(2)}, u32[]{:S(2)}) collective-permute-start(bf16[80,2304]{1,0:T(8,128)(2,1)S(1)} %collective-permute-done.21.rest_6_), channel_id=1, source_target_pairs={{0,1},{1,0},{2,3},{3,2},{4,5},{5,4},{6,7},{7,6},{8,9},{9,8},{10,11... | collective-permute-start | bytes 1105928 | tf_op jit(solution)/shard_map/ppermute | solution.py:466
  49.4 2.7 %collective-permute-start.27 = (bf16[80,2304]{1,0:T(8,128)(2,1)S(1)}, bf16[80,2304]{1,0:T(8,128)(2,1)S(1)}, u32[]{:S(2)}, u32[]{:S(2)}) collective-permute-start(bf16[80,2304]{1,0:T(8,128)(2,1)S(1)} %collective-permute-done.23.rest_8_), channel_id=1, source_target_pairs={{0,1},{1,0},{2,3},{3,2},{4,5},{5,4},{6,7},{7,6},{8,9},{9,8},{10,11... | collective-permute-start | bytes 1105928 | tf_op jit(solution)/shard_map/ppermute | solution.py:466
  (6 other events, 34.5 us)

commit v15 on v13

--- a/solution.py
+++ b/solution.py
@@ -98,31 +98,44 @@
     return [pltpu.make_async_copy(s, d, sem) for s, d in pairs]
 
 
-def first_kernel(split, embed, brk, gain, w_in, conv_w, w_out, table, part, *rest):
-    count = 3 if split else 0
-    parts, rest = rest[:count], rest[count:]
-    emb, bv, g, w, full, sem, *held = rest
-    copies = [
-        pltpu.make_async_copy(s, d, sem.at[0])
-        for s, d in ((embed, emb), (brk, bv), (gain, g), (w_in.at[0], w))
+def parts_kernel(w_in, conv_w, w_out, *rest):
+    parts, held, sem = rest[:3], rest[3:6], rest[6]
+    _, _, y, z = place()
+    for kind in range(2):
+        copies = part_copies(kind == 1, z, w_in, conv_w, w_out, held[0], held[1], sem.at[0])
+        copies += part_copies(kind == 0, 1 - z, w_in, conv_w, w_out, None, held[2], sem.at[0])
+
+        @pl.when(y == kind)
+        def _():
+            start(copies)
+            wait(copies)
+
+    leaving = [pltpu.make_async_copy(s, d, sem.at[1]) for s, d in zip(held, parts)]
+    start(leaving)
+    wait(leaving)
+
+
+def two_shares(split, w_all, w, sem):
+    if not split:
+        return [pltpu.make_async_copy(w_all[0].at[0], w, sem)]
+    _, core, _, _ = place()
+    n = w_all[0].shape[1]
+    return [
+        pltpu.make_async_copy(v.at[0], w.at[pl.ds(pl.multiple_of(c * n, 16), n)], sem)
+        for v, c in zip(w_all, (core, 1 - core))
     ]
-    start(copies)
-    leaving = []
-    if split:
-        _, _, y, z = place()
-        kinds = []
-        for kind in range(2):
-            kinds.append(
-                part_copies(kind == 1, z, w_in, conv_w, w_out, held[0], held[1], sem.at[1])
-                + part_copies(kind == 0, 1 - z, w_in, conv_w, w_out, None, held[2], sem.at[1])
-            )
-
-            @pl.when(y == kind)
-            def _():
-                start(kinds[kind])
-
-        leaving = [pltpu.make_async_copy(s, d, sem.at[2]) for s, d in zip(held, parts)]
-
+
+
+def chosen(split, x, rows):
+    at = place()[0] if split else lax.axis_index("roll")
+    return dot(x, pick(x.shape[1], rows, at * rows)).astype(BF)
+
+
+def embed_kernel(split, embed, brk, gain, *rest):
+    *w_all, table, part, sent, emb, bv, g, w, full, sem = rest
+    copies = [pltpu.make_async_copy(s, d, sem.at[0]) for s, d in ((embed, emb), (brk, bv), (gain, g))]
+    shares = two_shares(split, w_all, w, sem.at[1])
+    start(copies + shares)
     wait(copies)
     full[...] = jnp.zeros_like(full)
     full[0:VOCAB] = emb[...]
@@ -130,36 +143,27 @@
     hidden = full[...].astype(BF)
     table[...] = hidden
     normed = gelu(norm(hidden.astype(F32), g[0:1])).astype(BF)
-    if split:
-        for kind in range(2):
-
-            @pl.when(y == kind)
-            def _():
-                wait(kinds[kind])
-
-        start(leaving)
-    rows = w.shape[0]
-    mine = dot(normed, pick(normed.shape[1], rows, lax.axis_index("roll") * rows)).astype(BF)
-    part[...] = dot(mine, w[...])
-    wait(leaving)
-
-
-def table_kernel(split, own, other, gain, w_all, *rest):
-    *outs, w, full, sem = rest
-    copy = pltpu.make_async_copy(w_all.at[0], w, sem)
-    copy.start()
+    mine = chosen(split, normed, w.shape[0])
+    wait(shares)
+    total = dot(mine, w[...])
+    part[...] = total
+    sent[...] = total.astype(BF)
+
+
+def table_kernel(split, own, other, gain, *rest):
+    *w_all, out, w, rows, sem = rest
+    shares = two_shares(split, w_all, w, sem)
+    start(shares)
     wide = own[...] + other[...].astype(F32)
     t = gelu(norm(wide, gain[0:1])).astype(BF)
-    rows = w.shape[0]
-    mine = dot(t, pick(t.shape[1], rows, lax.axis_index("roll") * rows)).astype(BF)
-    copy.wait()
-    full[...] = dot(mine, w[...])
-    if split:
-        core = lax.rem(lax.axis_index("roll"), 2)
-        outs[0][...] = full[pl.ds(pl.multiple_of(core * SLOT, SLOT), SLOT)]
-        outs[1][...] = full[pl.ds(pl.multiple_of((1 - core) * SLOT, SLOT), SLOT)].astype(BF)
-    else:
-        outs[0][...] = full[...]
+    rows[...] = chosen(split, t, w.shape[0]).astype(F32)
+    if split:
+        _, core, _, _ = place()
+        mine = rows[pl.ds(pl.multiple_of(core * SLOT, SLOT), SLOT)]
+    else:
+        mine = rows[...]
+    wait(shares)
+    out[...] = dot(mine.astype(BF), w[...]).astype(out.dtype)
 
 
 def chip_copies(table, w_out, w_in, near_out, near_in, chip_out, chip_in, sem):
@@ -476,41 +480,52 @@
     codes = tokens[0] + SLOT * breaks[0]
 
     shard = w_out.shape[1] // 2
-    shapes = [((CODES, width), BF), ((CODES, H), F32)]
-    if split:
-        shapes += [((shard, width), BF), ((shard, CUT_A), BF), ((shard, CUT_A), BF)]
-    table, part, *parts = pl.pallas_call(
-        functools.partial(first_kernel, split),
-        out_shape=[jax.ShapeDtypeStruct(n, t) for n, t in shapes],
-        in_specs=[HBM] * 6,
-        out_specs=[VMEM] * 2 + [HBM] * (len(shapes) - 2),
+    ins, convs, shares = [w_in], [conv_w], 1
+    if split:
+        near_in, near_conv, near_out = core_swap(w_in), core_swap(conv_w), core_swap(w_out)
+        ins, convs, shares = [w_in, near_in], [conv_w, near_conv], 2
+        shapes = [(shard, width), (shard, CUT_A), (shard, CUT_A)]
+        parts = pl.pallas_call(
+            parts_kernel,
+            out_shape=[jax.ShapeDtypeStruct(n, BF) for n in shapes],
+            in_specs=[HBM] * 3,
+            out_specs=[HBM] * 3,
+            scratch_shapes=[pltpu.VMEM(n, BF) for n in shapes] + [pltpu.SemaphoreType.DMA((2,))],
+            cost_estimate=FREE,
+            compiler_params=params(60),
+        )(w_in, conv_w, w_out)
+        far_a = x_swap(parts[0])
+    table, part, sent = pl.pallas_call(
+        functools.partial(embed_kernel, split),
+        out_shape=[
+            jax.ShapeDtypeStruct((CODES, width), BF),
+            jax.ShapeDtypeStruct((CODES, H), F32),
+            jax.ShapeDtypeStruct((CODES, H), BF),
+        ],
+        in_specs=[HBM] * (3 + shares),
+        out_specs=[VMEM] * 3,
         scratch_shapes=[
             pltpu.VMEM(embed_table.shape, F32),
             pltpu.VMEM((width,), F32),
             pltpu.VMEM(gain_in.shape, F32),
-            pltpu.VMEM(w_in.shape[1:], BF),
+            pltpu.VMEM((shares * w_in.shape[1], H), BF),
             pltpu.VMEM((CODES, width), F32),
-            pltpu.SemaphoreType.DMA((3,)),
-        ]
-        + [pltpu.VMEM(n, t) for n, t in shapes[2:]],
+            pltpu.SemaphoreType.DMA((2,)),
+        ],
         cost_estimate=FREE,
         compiler_params=params(60),
-    )(embed_table, break_vec, gain_in, w_in, conv_w, w_out)
-
-    if split:
-        far_a = x_swap(parts[0])
-        near_out, near_in = core_swap(w_out), core_swap(w_in)
+    )(embed_table, break_vec, gain_in, *ins)
+
+    if split:
+        own, other = part, x_swap(sent)
+        far_b = x_swap(after(parts[1], other))
         low = roll_at % 2 == 0
         ends = codes[rows - REACH :], codes[:REACH]
-        theirs = core_swap(jnp.where(low, *ends[::-1]))
-        own = part + after(core_swap(part), theirs)
-        other = x_swap(own.astype(BF))
-        far_b = x_swap(after(parts[1], other))
-        pack = jnp.stack([jnp.where(low, *ends), theirs])
+        pack = jnp.stack([jnp.where(low, *ends), core_swap(after(jnp.where(low, *ends[::-1]), parts[0]))])
         places = [(s, r) for s in range(seqs) for r in range(rolls)]
         moves = [(s * rolls + r, (s + (1, -1)[r % 2]) % seqs * rolls + r) for s, r in places]
-        moved = lax.ppermute(after(pack, own), ("seq", "roll"), moves)
-        other = after(other, near_out, near_in, far_a)
+        moved = lax.ppermute(after(pack, table), ("seq", "roll"), moves)
+        other = after(other, moved, near_out, far_a)
     else:
         own = lax.psum(part, "roll")
         other = jnp.zeros((CODES, H), BF)
@@ -518,26 +533,24 @@
         before = lax.ppermute(codes[rows - REACH :], "seq", pairs)
         behind = lax.ppermute(codes[:REACH], "seq", [(j, i) for i, j in pairs])
     wide = KERNEL * H
-    shapes = [(SLOT, F32), (SLOT, BF)] if split else [(CODES, F32)]
     taps = pl.pallas_call(
         functools.partial(table_kernel, split),
-        out_shape=[jax.ShapeDtypeStruct((n, wide), t) for n, t in shapes],
-        in_specs=[VMEM, VMEM, VMEM, HBM],
-        out_specs=[VMEM] * len(shapes),
+        out_shape=jax.ShapeDtypeStruct((SLOT, wide) if split else (CODES, wide), BF if split else F32),
+        in_specs=[VMEM] * 3 + [HBM] * shares,
+        out_specs=VMEM,
         scratch_shapes=[
-            pltpu.VMEM(conv_w.shape[1:], BF),
-            pltpu.VMEM((CODES, wide), F32),
+            pltpu.VMEM((shares * conv_w.shape[1], wide), BF),
+            pltpu.VMEM((CODES, shares * conv_w.shape[1]), F32),
             pltpu.SemaphoreType.DMA,
         ],
         cost_estimate=FREE,
-        compiler_params=params(12),
-    )(own, other, gain_mid, conv_w)
-    if split:
-        relay = after(far_a, taps[1])
+        compiler_params=params(16),
+    )(own, other, gain_mid, *convs)
+    if split:
+        sent = taps
+        received = x_swap(sent)
+        relay = after(far_a, sent)
         parts_a = [far_a] + [seq_swap(relay, b) for b in (1, 2, 3)]
-        sent = (taps[0] + core_swap(taps[1]).astype(F32)).astype(BF)
-        received = x_swap(sent)
-    if split:
         came = core_swap(after(moved[1], sent))
         before, behind = jnp.where(low, moved[0], came), jnp.where(low, came, moved[0])
     spare = jnp.zeros((-(rows + 2 * REACH) % 128,), jnp.int32)
@@ -569,9 +582,8 @@
         relay = after(far_b, received)
         parts_b = [far_b, seq_swap(relay, 1), seq_swap(relay, 2), x_swap(after(parts[2], received))]
         weights_a = [sent, received, near_sent, near_received] + chip + parts_a + near_a
-        near_conv = core_swap(after(conv_w, near_received, near_sent, *near_a))
-    else:
-        taps = lax.psum(taps[0], "roll").astype(BF)
+    else:
+        taps = lax.psum(taps, "roll").astype(BF)
         gather = lambda w: lax.all_gather(w, "roll", axis=0, tiled=True)
         weights_a, weights_b = [taps, table, gather(w_out[0]), gather(w_in[1])], [gather(conv_w[1]), gather(w_out[1])]
 

time: 63.1 us -> 59.5 us (0.943)
  waiting for transfers between devices: 14.8 us -> 7.37 us
  Pallas kernels: 24.3 us -> 26.9 us
  starting transfers between devices: 16.4 us -> 18.4 us
  other arithmetic: 2.11 us -> 0.19 us
  local copies, waits for them, and re-layouts: 4.24 us -> 5.14 us
    ppermute x5, waiting for transfers between devices: 5.32 us -> 0.79 us  [x_swap(): return lax.ppermute(x, 'roll', [(i, i ^ 2) for i in range(rolls)])]
    pallas_call x2 -> x3, Pallas kernels: 4.31 us -> 7.2 us  [the longest x1 2.69 us: per_device(): pl.pallas_call(functools.partial(embed_kernel, split), out_shape=[jax.Sha...]
    ppermute x1, waiting for transfers between devices: 3.96 us -> 1.6 us  [per_device(): moved = lax.ppermute(after(pack, table), ('seq', 'roll'), moves)]
    ppermute x5, starting transfers between devices: 6.41 us -> 8.51 us  [x_swap(): return lax.ppermute(x, 'roll', [(i, i ^ 2) for i in range(rolls)])]
    convert_element_type x2 -> x0, other arithmetic: 1.93 us -> none  [the longest x1 0.98 us: per_device(): sent = (taps[0] + core_swap(taps[1]).astype(F32)).astype(BF)]
    unnamed x30 -> x28, local copies, waits for them, and re-layouts: 4.13 us -> 5.03 us
    pallas_call x1, Pallas kernels: 1.57 us -> 2.41 us  [per_device(): pl.pallas_call(head_kernel, out_shape=jax.ShapeDtypeStruct((rows, H), F32...]
    pallas_call x1, Pallas kernels: 10.1 us -> 9.41 us  [per_device(): pl.pallas_call(functools.partial(rows_kernel, split), out_shape=(jax.Shap...]
  transfers between devices with their start and end apart: 28 -> 26, of which waited for: 12 -> 7; matrix products, arithmetic and copies ran while one was open for 4% -> 0% of each run, Pallas kernels for 28% -> 37%
where the time goes in v15:
time: 59.5 us; the launch traced here: 59 us
  Pallas kernels  26.9 us (45%)
  starting transfers between devices  18.4 us (31%)
  waiting for transfers between devices  7.37 us (12%)
  local copies, waits for them, and re-layouts  5.14 us (9%)
  between operations  1.07 us (2%)
    pallas_call x1, Pallas kernels, per_device(): pl.pallas_call(functools.partial(rows_kernel, split), out_shape=(jax.Shap...  9.41 us
    ppermute x5, starting transfers between devices, x_swap(): return lax.ppermute(x, 'roll', [(i, i ^ 2) for i in range(rolls)])  8.51 us
    pallas_call x1, Pallas kernels, per_device(): pl.pallas_call(functools.partial(last_kernel, split), out_shape=jax.Shape...  5.15 us
    unnamed x28, local copies, waits for them, and re-layouts  5.03 us
    ppermute x5, starting transfers between devices, seq_swap(): return lax.ppermute(x, 'seq', [(i, i ^ bits) for i in range(seqs)])  4.98 us
    ppermute x15, starting transfers between devices, core_swap(): return lax.ppermute(x, 'roll', [(i, i ^ 1) for i in range(rolls)])  3.37 us
    ppermute x5, waiting for transfers between devices, seq_swap(): return lax.ppermute(x, 'seq', [(i, i ^ bits) for i in range(seqs)])  3.1 us
    pallas_call x1, Pallas kernels, per_device(): pl.pallas_call(functools.partial(hot_kernel, split), out_shape=[jax.Shape...  2.71 us
  transfers between devices with their start and end apart: 26, of which 7 were waited for; matrix products, arithmetic and copies ran while one was open for 0% of the time, Pallas kernels for 37%

profile of v15, /device:TPU:0, one launch (start us, length us, event | category | flops | bytes accessed | tf_op | source)
XLA Modules:
  0.0 59.0 jit_solution(13694257684466491685)
XLA Ops:
  0.0 0.5 collective-permute-start.6
  0.5 0.5 collective-permute-start.4
  1.0 2.3 %shard_map.109 = (bf16[80,1280]{1,0:T(8,128)(2,1)}, bf16[80,2304]{1,0:T(8,128)(2,1)}, bf16[80,2304]{1,0:T(8,128)(2,1)}) custom-call(bf16[2,320,640]{2,1,0:T(8,128)(2,1)} %rest_2_.2, bf16[2,160,3200]{2,1,0:T(8,128)(2,1)} %rest_1_.3, bf16[2,160,1280]{2,1,0:T(8,128)(2,1)} %rest_2_.3), custom_call_target="tpu_custom_call" | custom-call | tf_op jit(solution)/shard_map/pallas_call | solution.py:488
  3.5 2.9 %collective-permute-start.5 = (bf16[80,1280]{1,0:T(8,128)(2,1)}, bf16[80,1280]{1,0:T(8,128)(2,1)}, u32[]{:S(2)}, u32[]{:S(2)}) collective-permute-start(bf16[80,1280]{1,0:T(8,128)(2,1)} %get-tuple-element.36), channel_id=1, source_target_pairs={{0,2},{1,3},{2,0},{3,1},{4,6},{5,7},{6,4},{7,5},{8,10},{9,11},{10,... | collective-permute-start | bytes 614408 | tf_op jit(solution)/shard_map/ppermute | solution.py:473
  6.5 0.3 collective-permute-done.1.rest_1_.rest_4_
  6.9 2.7 %shard_map.110 = (bf16[64,1280]{1,0:T(8,128)(2,1)}, f32[64,640]{1,0:T(8,128)}, bf16[64,640]{1,0:T(8,128)(2,1)}) custom-call(f32[30,1280]{1,0:T(8,128)} %embed.1, f32[1280]{0:T(1024)} %brk.1, f32[2,1280]{1,0:T(2,128)} %gain_in.1, bf16[2,320,640]{2,1,0:T(8,128)(2,1)} %rest_2_.2, bf16[2,320,640]{2,1,0:T(8,128)(2,1)} %collective-permute-done.1.rest_1_.rest_4_), custom_call_target="tpu_custom_call" | custom-call | tf_op jit(solution)/shard_map/pallas_call | solution.py:498
  9.6 2.9 %collective-permute-start.3 = (bf16[64,640]{1,0:T(8,128)(2,1)}, bf16[64,640]{1,0:T(8,128)(2,1)S(1)}, u32[]{:S(2)}, u32[]{:S(2)}) collective-permute-start(bf16[64,640]{1,0:T(8,128)(2,1)} %get-tuple-element.41), channel_id=1, source_target_pairs={{0,2},{1,3},{2,0},{3,1},{4,6},{5,7},{6,4},{7,5},{8,10},{9,11},{10,... | collective-permute-start | bytes 245768 | tf_op jit(solution)/shard_map/ppermute | solution.py:473
  12.5 1.5 %collective-permute-start.2 = (s32[2,384]{1,0:T(2,128)S(1)}, s32[2,384]{1,0:T(2,128)S(1)}, u32[]{:S(2)}, u32[]{:S(2)}) collective-permute-start(s32[2,384]{1,0:T(2,128)S(1)} %pad_add_fusion), channel_id=1, source_target_pairs={{0,4},{1,29},{2,6},{3,31},{4,8},{5,1},{6,10},{7,3},{8,12},{9,5},{1... | collective-permute-start | bytes 9224 | tf_op jit(solution)/shard_map/ppermute | solution.py:527
  14.7 0.8 %collective-permute-done.3.other = bf16[64,640]{1,0:T(8,128)(2,1)S(1)} collective-permute-done((bf16[64,640]{1,0:T(8,128)(2,1)}, bf16[64,640]{1,0:T(8,128)(2,1)S(1)}, u32[]{:S(2)}, u32[]{:S(2)}) %collective-permute-start.3) | collective-permute-done | bytes 81952 | tf_op jit(solution)/shard_map/ppermute | solution.py:473
  15.4 1.7 %collective-permute-start.14 = (bf16[80,2304]{1,0:T(8,128)(2,1)}, bf16[80,2304]{1,0:T(8,128)(2,1)S(1)}, u32[]{:S(2)}, u32[]{:S(2)}) collective-permute-start(bf16[80,2304]{1,0:T(8,128)(2,1)} %get-tuple-element.53), channel_id=1, source_target_pairs={{0,2},{1,3},{2,0},{3,1},{4,6},{5,7},{6,4},{7,5},{8,10},{9,11},{10,... | collective-permute-start | bytes 1105928 | tf_op jit(solution)/shard_map/ppermute | solution.py:473
  17.2 1.6 %collective-permute-done.2 = s32[2,384]{1,0:T(2,128)S(1)} collective-permute-done((s32[2,384]{1,0:T(2,128)S(1)}, s32[2,384]{1,0:T(2,128)S(1)}, u32[]{:S(2)}, u32[]{:S(2)}) %collective-permute-start.2) | collective-permute-done | bytes 3104 | tf_op jit(solution)/shard_map/ppermute | solution.py:527
  18.8 0.9 %copy-done.3 = bf16[2,160,1280]{2,1,0:T(8,128)(2,1)} copy-done((bf16[2,160,1280]{2,1,0:T(8,128)(2,1)}, bf16[2,160,1280]{2,1,0:T(8,128)(2,1)S(1)}, u32[]{:S(2)}) %copy-start.3) | copy-done | bytes 819224
  19.7 0.9 %copy-done.6 = f32[64,640]{1,0:T(8,128)S(1)} copy-done((f32[64,640]{1,0:T(8,128)S(1)}, f32[64,640]{1,0:T(8,128)}, u32[]{:S(2)}) %copy-start.6) | copy-done | bytes 163864
  20.7 2.2 %shard_map.111.rest_0_ = bf16[32,3200]{1,0:T(8,128)(2,1)S(1)} custom-call(f32[64,640]{1,0:T(8,128)S(1)} %copy-done.6, bf16[64,640]{1,0:T(8,128)(2,1)S(1)} %collective-permute-done.3.other, f32[2,640]{1,0:T(2,128)S(1)} %copy-done.9, bf16[2,160,3200]{2,1,0:T(8,128)(2,1)S(1)} %copy-done, bf16[2,160,3200]{2,1,0:T(8,128)(2,1)} %collective-permute-done.6.rest_1_.near_conv.rest_3_), custom_call_target="tpu_custom_call" | custom-call | tf_op jit(solution)/shard_map/pallas_call | solution.py:536
  23.0 0.9 %collective-permute-start.13 = (bf16[80,1280]{1,0:T(8,128)(2,1)}, bf16[80,1280]{1,0:T(8,128)(2,1)}, u32[]{:S(2)}, u32[]{:S(2)}) collective-permute-start(bf16[80,1280]{1,0:T(8,128)(2,1)} %collective-permute-done.5.rest_6_), channel_id=1, source_target_pairs={{0,12},{4,8},{8,4},{12,0},{16,28},{20,24},{24,20},{28,16},{1,13},{... | collective-permute-start | bytes 614408 | tf_op jit(solution)/shard_map/ppermute | solution.py:476
  24.0 0.4 collective-permute-start.12
  24.4 2.1 %collective-permute-start.11 = (bf16[80,1280]{1,0:T(8,128)(2,1)}, bf16[80,1280]{1,0:T(8,128)(2,1)}, u32[]{:S(2)}, u32[]{:S(2)}) collective-permute-start(bf16[80,1280]{1,0:T(8,128)(2,1)} %collective-permute-done.5.rest_6_), channel_id=1, source_target_pairs={{0,4},{4,0},{8,12},{12,8},{16,20},{20,16},{24,28},{28,24},{1,5},{5... | collective-permute-start | bytes 614408 | tf_op jit(solution)/shard_map/ppermute | solution.py:476
  26.5 0.4 collective-permute-start.8
  27.0 1.1 %copy-done.2 = bf16[2,320,640]{2,1,0:T(8,128)(2,1)S(1)} copy-done((bf16[2,320,640]{2,1,0:T(8,128)(2,1)S(1)}, bf16[2,320,640]{2,1,0:T(8,128)(2,1)}, u32[]{:S(2)}) %copy-start.2) | copy-done | bytes 819224
  28.2 1.1 %copy-done.4 = bf16[2,160,1280]{2,1,0:T(8,128)(2,1)S(1)} copy-done((bf16[2,160,1280]{2,1,0:T(8,128)(2,1)S(1)}, bf16[2,160,1280]{2,1,0:T(8,128)(2,1)}, u32[]{:S(2)}) %copy-start.4) | copy-done | bytes 819224
  29.3 0.9 %copy-done.7 = bf16[64,1280]{1,0:T(8,128)(2,1)S(1)} copy-done((bf16[64,1280]{1,0:T(8,128)(2,1)S(1)}, bf16[64,1280]{1,0:T(8,128)(2,1)}, u32[]{:S(2)}) %copy-start.7) | copy-done | bytes 163864
  30.2 2.7 %shard_map.112 = (bf16[1008,320]{1,0:T(8,128)(2,1)S(1)}, bf16[1008,64]{1,0:T(8,128)(2,1)S(1)}, bf16[384,1280]{1,0:T(8,128)(2,1)S(1)}, bf16[640,640]{1,0:T(8,128)(2,1)S(1)}) custom-call(s32[2]{0:T(128)S(1)} %pad_add_fusion.1.span, s32[1,1280]{1,0:T(1,128)S(1)} %broadcast_in_dim.6.near, bf16[64,1280]{1,0:T(8,128)(2,1)S(1)} %copy-done.7, ...), custom_call_target="tpu_custom_call" | custom-call | tf_op jit(solution)/shard_map/pallas_call | solution.py:567
  33.0 3.1 %collective-permute-done.11.rest_7_ = bf16[80,1280]{1,0:T(8,128)(2,1)} collective-permute-done((bf16[80,1280]{1,0:T(8,128)(2,1)}, bf16[80,1280]{1,0:T(8,128)(2,1)}, u32[]{:S(2)}, u32[]{:S(2)}) %collective-permute-start.11) | collective-permute-done | bytes 204832 | tf_op jit(solution)/shard_map/ppermute | solution.py:476
  36.2 0.5 collective-permute-start.10
  36.7 1.5 %collective-permute-start.19 = (bf16[80,2304]{1,0:T(8,128)(2,1)S(1)}, bf16[80,2304]{1,0:T(8,128)(2,1)S(1)}, u32[]{:S(2)}, u32[]{:S(2)}) collective-permute-start(bf16[80,2304]{1,0:T(8,128)(2,1)S(1)} %collective-permute-done.14.rest_5_), channel_id=1, source_target_pairs={{0,4},{4,0},{8,12},{12,8},{16,20},{20,16},{24,28},{28,24},{1,5},{5... | collective-permute-start | bytes 1105928 | tf_op jit(solution)/shard_map/ppermute | solution.py:476
  38.2 0.5 collective-permute-start.21
  38.8 0.5 collective-permute-start.18
  39.3 1.1 %collective-permute-done.17.rest_12_ = bf16[80,1280]{1,0:T(8,128)(2,1)S(1)} collective-permute-done((bf16[80,1280]{1,0:T(8,128)(2,1)}, bf16[80,1280]{1,0:T(8,128)(2,1)S(1)}, u32[]{:S(2)}, u32[]{:S(2)}) %collective-permute-start.17) | collective-permute-done | bytes 204832 | tf_op jit(solution)/shard_map/ppermute | solution.py:470
  40.4 0.3 collective-permute-done.18.rest_13_
  40.7 9.4 %shard_map.113 = (bf16[1008,640]{1,0:T(8,128)(2,1)S(1)}, bf16[496,1280]{1,0:T(8,128)(2,1)S(1)}) custom-call(s32[2]{0:T(128)S(1)} %pad_add_fusion.1.span, bf16[1008,320]{1,0:T(8,128)(2,1)S(1)} %get-tuple-element.45.hot5, bf16[1008,64]{1,0:T(8,128)(2,1)S(1)} %get-tuple-element.46.hot1, f32[2,640]{1,0:T(2,128)S(1)} %copy-done.10, f32[2,1280]{1,0:T(2,128)S(1)} %copy-done.8, ...), custom_call_target="tpu_custom_call" | custom-call | tf_op jit(solution)/shard_map/pallas_call | solution.py:590
  51.2 2.4 %shard_map.114.rest_0_ = f32[496,640]{1,0:T(8,128)S(1)} custom-call(bf16[1008,640]{1,0:T(8,128)(2,1)S(1)} %get-tuple-element.58.ci, bf16[2,160,3200]{2,1,0:T(8,128)(2,1)S(1)} %copy-done, bf16[2,160,3200]{2,1,0:T(8,128)(2,1)} %collective-permute-done.6.rest_1_.near_conv.rest_3_), custom_call_target="tpu_custom_call" | custom-call | tf_op jit(solution)/shard_map/pallas_call | solution.py:610
  53.7 5.1 %shard_map.115 = bf16[496,1280]{1,0:T(8,128)(2,1)} custom-call(bf16[1008,640]{1,0:T(8,128)(2,1)S(1)} %get-tuple-element.58.ci, bf16[496,1280]{1,0:T(8,128)(2,1)S(1)} %get-tuple-element.59.hid, f32[2,640]{1,0:T(2,128)S(1)} %copy-done.10, f32[496,640]{1,0:T(8,128)S(1)} %shard_map.114.rest_0_, bf16[2,160,3200]{2,1,0:T(8,128)(2,1)S(1)} %copy-done, ...), custom_call_target="tpu_custom_call" | custom-call | tf_op jit(solution)/shard_map/pallas_call | solution.py:620
  (65 shorter events, 2.0 us)
Async XLA Ops:
  0.0 19.7 %collective-permute-start.6 = (bf16[2,160,3200]{2,1,0:T(8,128)(2,1)}, bf16[2,160,3200]{2,1,0:T(8,128)(2,1)}, u32[]{:S(2)}, u32[]{:S(2)}) collective-permute-start(bf16[2,160,3200]{2,1,0:T(8,128)(2,1)} %rest_1_.3), channel_id=1, source_target_pairs={{0,1},{1,0},{2,3},{3,2},{4,5},{5,4},{6,7},{7,6},{8,9},{9,8},{10,11... | collective-permute-start | bytes 6144008 | tf_op jit(solution)/shard_map/ppermute | solution.py:470
  0.5 6.4 %collective-permute-start.1 = (bf16[2,320,640]{2,1,0:T(8,128)(2,1)}, bf16[2,320,640]{2,1,0:T(8,128)(2,1)}, u32[]{:S(2)}, u32[]{:S(2)}) collective-permute-start(bf16[2,320,640]{2,1,0:T(8,128)(2,1)} %rest_2_.2), channel_id=1, source_target_pairs={{0,1},{1,0},{2,3},{3,2},{4,5},{5,4},{6,7},{7,6},{8,9},{9,8},{10,11... | collective-permute-start | bytes 2457608 | tf_op jit(solution)/shard_map/ppermute | solution.py:470
  0.5 18.3 %collective-permute-start.4 = (bf16[2,160,1280]{2,1,0:T(8,128)(2,1)}, bf16[2,160,1280]{2,1,0:T(8,128)(2,1)S(1)}, u32[]{:S(2)}, u32[]{:S(2)}) collective-permute-start(bf16[2,160,1280]{2,1,0:T(8,128)(2,1)} %rest_2_.3), channel_id=1, source_target_pairs={{0,1},{1,0},{2,3},{3,2},{4,5},{5,4},{6,7},{7,6},{8,9},{9,8},{10,11... | collective-permute-start | bytes 2457608 | tf_op jit(solution)/shard_map/ppermute | solution.py:470
  1.0 18.8 %copy-start = (bf16[2,160,3200]{2,1,0:T(8,128)(2,1)S(1)}, bf16[2,160,3200]{2,1,0:T(8,128)(2,1)}, u32[]{:S(2)}) copy-start(bf16[2,160,3200]{2,1,0:T(8,128)(2,1)} %rest_1_.3) | copy-start | bytes 6144004
  3.3 16.5 %copy-start.9 = (f32[2,640]{1,0:T(2,128)S(1)}, f32[2,640]{1,0:T(2,128)}, u32[]{:S(2)}) copy-start(f32[2,640]{1,0:T(2,128)} %gain_mid.1) | copy-start | bytes 15364
  3.4 3.1 %collective-permute-start = (s32[384]{0:T(512)S(1)}, s32[384]{0:T(512)S(1)}, u32[]{:S(2)}, u32[]{:S(2)}) collective-permute-start(s32[384]{0:T(512)S(1)} %get-tuple-element.37), channel_id=1, source_target_pairs={{0,1},{1,0},{2,3},{3,2},{4,5},{5,4},{6,7},{7,6},{8,9},{9,8},{10,11... | collective-permute-start | bytes 4616 | tf_op jit(solution)/shard_map/ppermute | solution.py:470
  3.5 15.3 %collective-permute-start.5 = (bf16[80,1280]{1,0:T(8,128)(2,1)}, bf16[80,1280]{1,0:T(8,128)(2,1)}, u32[]{:S(2)}, u32[]{:S(2)}) collective-permute-start(bf16[80,1280]{1,0:T(8,128)(2,1)} %get-tuple-element.36), channel_id=1, source_target_pairs={{0,2},{1,3},{2,0},{3,1},{4,6},{5,7},{6,4},{7,5},{8,10},{9,11},{10,... | collective-permute-start | bytes 614408 | tf_op jit(solution)/shard_map/ppermute | solution.py:473
  9.6 5.9 %collective-permute-start.3 = (bf16[64,640]{1,0:T(8,128)(2,1)}, bf16[64,640]{1,0:T(8,128)(2,1)S(1)}, u32[]{:S(2)}, u32[]{:S(2)}) collective-permute-start(bf16[64,640]{1,0:T(8,128)(2,1)} %get-tuple-element.41), channel_id=1, source_target_pairs={{0,2},{1,3},{2,0},{3,1},{4,6},{5,7},{6,4},{7,5},{8,10},{9,11},{10,... | collective-permute-start | bytes 245768 | tf_op jit(solution)/shard_map/ppermute | solution.py:473
  12.5 6.3 %collective-permute-start.2 = (s32[2,384]{1,0:T(2,128)S(1)}, s32[2,384]{1,0:T(2,128)S(1)}, u32[]{:S(2)}, u32[]{:S(2)}) collective-permute-start(s32[2,384]{1,0:T(2,128)S(1)} %pad_add_fusion), channel_id=1, source_target_pairs={{0,4},{1,29},{2,6},{3,31},{4,8},{5,1},{6,10},{7,3},{8,12},{9,5},{1... | collective-permute-start | bytes 9224 | tf_op jit(solution)/shard_map/ppermute | solution.py:527
  15.4 17.5 %collective-permute-start.14 = (bf16[80,2304]{1,0:T(8,128)(2,1)}, bf16[80,2304]{1,0:T(8,128)(2,1)S(1)}, u32[]{:S(2)}, u32[]{:S(2)}) collective-permute-start(bf16[80,2304]{1,0:T(8,128)(2,1)} %get-tuple-element.53), channel_id=1, source_target_pairs={{0,2},{1,3},{2,0},{3,1},{4,6},{5,7},{6,4},{7,5},{8,10},{9,11},{10,... | collective-permute-start | bytes 1105928 | tf_op jit(solution)/shard_map/ppermute | solution.py:473
  20.7 6.4 %copy-start.1 = (bf16[2,160,1280]{2,1,0:T(8,128)(2,1)S(1)}, bf16[2,160,1280]{2,1,0:T(8,128)(2,1)}, u32[]{:S(2)}) copy-start(bf16[2,160,1280]{2,1,0:T(8,128)(2,1)} %rest_2_.3) | copy-start | bytes 2457604
  22.9 3.7 %collective-permute-start.7 = (s32[384]{0:T(512)S(1)}, s32[384]{0:T(512)S(1)}, u32[]{:S(2)}, u32[]{:S(2)}) collective-permute-start(s32[384]{0:T(512)S(1)} %get-tuple-element.43), channel_id=1, source_target_pairs={{0,1},{1,0},{2,3},{3,2},{4,5},{5,4},{6,7},{7,6},{8,9},{9,8},{10,11... | collective-permute-start | bytes 4616 | tf_op jit(solution)/shard_map/ppermute | solution.py:470
  23.0 13.6 %collective-permute-start.13 = (bf16[80,1280]{1,0:T(8,128)(2,1)}, bf16[80,1280]{1,0:T(8,128)(2,1)}, u32[]{:S(2)}, u32[]{:S(2)}) collective-permute-start(bf16[80,1280]{1,0:T(8,128)(2,1)} %collective-permute-done.5.rest_6_), channel_id=1, source_target_pairs={{0,12},{4,8},{8,4},{12,0},{16,28},{20,24},{24,20},{28,16},{1,13},{... | collective-permute-start | bytes 614408 | tf_op jit(solution)/shard_map/ppermute | solution.py:476
  24.0 12.7 %collective-permute-start.12 = (bf16[80,1280]{1,0:T(8,128)(2,1)}, bf16[80,1280]{1,0:T(8,128)(2,1)}, u32[]{:S(2)}, u32[]{:S(2)}) collective-permute-start(bf16[80,1280]{1,0:T(8,128)(2,1)} %collective-permute-done.5.rest_6_), channel_id=1, source_target_pairs={{0,8},{4,12},{8,0},{12,4},{16,24},{20,28},{24,16},{28,20},{1,9},{5... | collective-permute-start | bytes 614408 | tf_op jit(solution)/shard_map/ppermute | solution.py:476
  24.4 11.7 %collective-permute-start.11 = (bf16[80,1280]{1,0:T(8,128)(2,1)}, bf16[80,1280]{1,0:T(8,128)(2,1)}, u32[]{:S(2)}, u32[]{:S(2)}) collective-permute-start(bf16[80,1280]{1,0:T(8,128)(2,1)} %collective-permute-done.5.rest_6_), channel_id=1, source_target_pairs={{0,4},{4,0},{8,12},{12,8},{16,20},{20,16},{24,28},{28,24},{1,5},{5... | collective-permute-start | bytes 614408 | tf_op jit(solution)/shard_map/ppermute | solution.py:476
  26.5 9.6 %collective-permute-start.8 = (bf16[32,3200]{1,0:T(8,128)(2,1)S(1)}, bf16[32,3200]{1,0:T(8,128)(2,1)}, u32[]{:S(2)}, u32[]{:S(2)}) collective-permute-start(bf16[32,3200]{1,0:T(8,128)(2,1)S(1)} %shard_map.111.rest_0_), channel_id=1, source_target_pairs={{0,2},{1,3},{2,0},{3,1},{4,6},{5,7},{6,4},{7,5},{8,10},{9,11},{10,... | collective-permute-start | bytes 614408 | tf_op jit(solution)/shard_map/ppermute | solution.py:473
  30.2 8.0 %copy-start.13 = (bf16[80,2304]{1,0:T(8,128)(2,1)S(1)}, bf16[80,2304]{1,0:T(8,128)(2,1)}, u32[]{:S(2)}) copy-start(bf16[80,2304]{1,0:T(8,128)(2,1)} %get-tuple-element.62) | copy-start | bytes 1105924
  30.2 10.5 %copy-start.8 = (f32[2,1280]{1,0:T(2,128)S(1)}, f32[2,1280]{1,0:T(2,128)}, u32[]{:S(2)}) copy-start(f32[2,1280]{1,0:T(2,128)} %gain_in.1) | copy-start | bytes 30724
  30.2 10.5 %copy-start.10 = (f32[2,640]{1,0:T(2,128)S(1)}, f32[2,640]{1,0:T(2,128)}, u32[]{:S(2)}) copy-start(f32[2,640]{1,0:T(2,128)} %gain_out.3) | copy-start | bytes 15364
  33.0 3.8 %collective-permute-start.9 = (bf16[32,3200]{1,0:T(8,128)(2,1)S(1)}, bf16[32,3200]{1,0:T(8,128)(2,1)S(1)}, u32[]{:S(2)}, u32[]{:S(2)}) collective-permute-start(bf16[32,3200]{1,0:T(8,128)(2,1)S(1)} %shard_map.111.rest_0_), channel_id=1, source_target_pairs={{0,1},{1,0},{2,3},{3,2},{4,5},{5,4},{6,7},{7,6},{8,9},{9,8},{10,11... | collective-permute-start | bytes 614408 | tf_op jit(solution)/shard_map/ppermute | solution.py:470
  36.1 2.1 %collective-permute-start.15 = (bf16[80,1280]{1,0:T(8,128)(2,1)}, bf16[80,1280]{1,0:T(8,128)(2,1)S(1)}, u32[]{:S(2)}, u32[]{:S(2)}) collective-permute-start(bf16[80,1280]{1,0:T(8,128)(2,1)} %collective-permute-done.5.rest_6_), channel_id=1, source_target_pairs={{0,1},{1,0},{2,3},{3,2},{4,5},{5,4},{6,7},{7,6},{8,9},{9,8},{10,11... | collective-permute-start | bytes 614408 | tf_op jit(solution)/shard_map/ppermute | solution.py:470
  36.2 2.6 %collective-permute-start.10 = (bf16[32,3200]{1,0:T(8,128)(2,1)}, bf16[32,3200]{1,0:T(8,128)(2,1)S(1)}, u32[]{:S(2)}, u32[]{:S(2)}) collective-permute-start(bf16[32,3200]{1,0:T(8,128)(2,1)} %collective-permute-done.8.rest_1_), channel_id=1, source_target_pairs={{0,1},{1,0},{2,3},{3,2},{4,5},{5,4},{6,7},{7,6},{8,9},{9,8},{10,11... | collective-permute-start | bytes 614408 | tf_op jit(solution)/shard_map/ppermute | solution.py:470
  36.6 2.1 %collective-permute-start.16 = (bf16[80,1280]{1,0:T(8,128)(2,1)}, bf16[80,1280]{1,0:T(8,128)(2,1)S(1)}, u32[]{:S(2)}, u32[]{:S(2)}) collective-permute-start(bf16[80,1280]{1,0:T(8,128)(2,1)} %collective-permute-done.11.rest_7_), channel_id=1, source_target_pairs={{0,1},{1,0},{2,3},{3,2},{4,5},{5,4},{6,7},{7,6},{8,9},{9,8},{10,11... | collective-permute-start | bytes 614408 | tf_op jit(solution)/shard_map/ppermute | solution.py:470
  36.7 13.7 %collective-permute-start.20 = (bf16[80,2304]{1,0:T(8,128)(2,1)S(1)}, bf16[80,2304]{1,0:T(8,128)(2,1)S(1)}, u32[]{:S(2)}, u32[]{:S(2)}) collective-permute-start(bf16[80,2304]{1,0:T(8,128)(2,1)S(1)} %collective-permute-done.14.rest_5_), channel_id=1, source_target_pairs={{0,8},{4,12},{8,0},{12,4},{16,24},{20,28},{24,16},{28,20},{1,9},{5... | collective-permute-start | bytes 1105928 | tf_op jit(solution)/shard_map/ppermute | solution.py:476
  36.7 14.0 %collective-permute-start.19 = (bf16[80,2304]{1,0:T(8,128)(2,1)S(1)}, bf16[80,2304]{1,0:T(8,128)(2,1)S(1)}, u32[]{:S(2)}, u32[]{:S(2)}) collective-permute-start(bf16[80,2304]{1,0:T(8,128)(2,1)S(1)} %collective-permute-done.14.rest_5_), channel_id=1, source_target_pairs={{0,4},{4,0},{8,12},{12,8},{16,20},{20,16},{24,28},{28,24},{1,5},{5... | collective-permute-start | bytes 1105928 | tf_op jit(solution)/shard_map/ppermute | solution.py:476
  38.2 12.7 %collective-permute-start.21 = (bf16[80,2304]{1,0:T(8,128)(2,1)S(1)}, bf16[80,2304]{1,0:T(8,128)(2,1)S(1)}, u32[]{:S(2)}, u32[]{:S(2)}) collective-permute-start(bf16[80,2304]{1,0:T(8,128)(2,1)S(1)} %copy-done.13), channel_id=1, source_target_pairs={{0,2},{1,3},{2,0},{3,1},{4,6},{5,7},{6,4},{7,5},{8,10},{9,11},{10,... | collective-permute-start | bytes 1105928 | tf_op jit(solution)/shard_map/ppermute | solution.py:473
  38.8 1.7 %collective-permute-start.17 = (bf16[80,1280]{1,0:T(8,128)(2,1)}, bf16[80,1280]{1,0:T(8,128)(2,1)S(1)}, u32[]{:S(2)}, u32[]{:S(2)}) collective-permute-start(bf16[80,1280]{1,0:T(8,128)(2,1)} %collective-permute-done.12.rest_8_), channel_id=1, source_target_pairs={{0,1},{1,0},{2,3},{3,2},{4,5},{5,4},{6,7},{7,6},{8,9},{9,8},{10,11... | collective-permute-start | bytes 614408 | tf_op jit(solution)/shard_map/ppermute | solution.py:470
  38.8 1.9 %collective-permute-start.18 = (bf16[80,1280]{1,0:T(8,128)(2,1)}, bf16[80,1280]{1,0:T(8,128)(2,1)S(1)}, u32[]{:S(2)}, u32[]{:S(2)}) collective-permute-start(bf16[80,1280]{1,0:T(8,128)(2,1)} %collective-permute-done.13.rest_9_), channel_id=1, source_target_pairs={{0,1},{1,0},{2,3},{3,2},{4,5},{5,4},{6,7},{7,6},{8,9},{9,8},{10,11... | collective-permute-start | bytes 614408 | tf_op jit(solution)/shard_map/ppermute | solution.py:470
  50.1 3.5 %collective-permute-start.22 = (bf16[80,2304]{1,0:T(8,128)(2,1)S(1)}, bf16[80,2304]{1,0:T(8,128)(2,1)S(1)}, u32[]{:S(2)}, u32[]{:S(2)}) collective-permute-start(bf16[80,2304]{1,0:T(8,128)(2,1)S(1)} %collective-permute-done.14.rest_5_), channel_id=1, source_target_pairs={{0,1},{1,0},{2,3},{3,2},{4,5},{5,4},{6,7},{7,6},{8,9},{9,8},{10,11... | collective-permute-start | bytes 1105928 | tf_op jit(solution)/shard_map/ppermute | solution.py:470
  50.4 3.2 %collective-permute-start.24 = (bf16[80,2304]{1,0:T(8,128)(2,1)S(1)}, bf16[80,2304]{1,0:T(8,128)(2,1)S(1)}, u32[]{:S(2)}, u32[]{:S(2)}) collective-permute-start(bf16[80,2304]{1,0:T(8,128)(2,1)S(1)} %collective-permute-done.20.rest_7_), channel_id=1, source_target_pairs={{0,1},{1,0},{2,3},{3,2},{4,5},{5,4},{6,7},{7,6},{8,9},{9,8},{10,11... | collective-permute-start | bytes 1105928 | tf_op jit(solution)/shard_map/ppermute | solution.py:470
  50.7 3.0 %collective-permute-start.23 = (bf16[80,2304]{1,0:T(8,128)(2,1)S(1)}, bf16[80,2304]{1,0:T(8,128)(2,1)S(1)}, u32[]{:S(2)}, u32[]{:S(2)}) collective-permute-start(bf16[80,2304]{1,0:T(8,128)(2,1)S(1)} %collective-permute-done.19.rest_6_), channel_id=1, source_target_pairs={{0,1},{1,0},{2,3},{3,2},{4,5},{5,4},{6,7},{7,6},{8,9},{9,8},{10,11... | collective-permute-start | bytes 1105928 | tf_op jit(solution)/shard_map/ppermute | solution.py:470
  51.0 2.7 %collective-permute-start.25 = (bf16[80,2304]{1,0:T(8,128)(2,1)S(1)}, bf16[80,2304]{1,0:T(8,128)(2,1)S(1)}, u32[]{:S(2)}, u32[]{:S(2)}) collective-permute-start(bf16[80,2304]{1,0:T(8,128)(2,1)S(1)} %collective-permute-done.21.rest_8_), channel_id=1, source_target_pairs={{0,1},{1,0},{2,3},{3,2},{4,5},{5,4},{6,7},{7,6},{8,9},{9,8},{10,11... | collective-permute-start | bytes 1105928 | tf_op jit(solution)/shard_map/ppermute | solution.py:470
  (8 other events, 13.2 us)

commit v16 on v15

--- a/solution.py
+++ b/solution.py
@@ -524,8 +524,8 @@
         pack = jnp.stack([jnp.where(low, *ends), core_swap(after(jnp.where(low, *ends[::-1]), parts[0]))])
         places = [(s, r) for s in range(seqs) for r in range(rolls)]
         moves = [(s * rolls + r, (s + (1, -1)[r % 2]) % seqs * rolls + r) for s, r in places]
-        moved = lax.ppermute(after(pack, table), ("seq", "roll"), moves)
-        other = after(other, moved, near_out, far_a)
+        moved = lax.ppermute(after(pack, table, near_out), ("seq", "roll"), moves)
+        other = after(other, far_a)
     else:
         own = lax.psum(part, "roll")
         other = jnp.zeros((CODES, H), BF)

time: 59.5 us -> 58.9 us (0.990)
  starting transfers between devices: 18.4 us -> 17.4 us
    ppermute x1, waiting for transfers between devices: 1.6 us -> 2.5 us  [per_device(): moved = lax.ppermute(after(pack, table, near_out), ('seq', 'roll'), moves)]
    ppermute x5, waiting for transfers between devices: 0.79 us -> 0.01 us  [x_swap(): return lax.ppermute(x, 'roll', [(i, i ^ 2) for i in range(rolls)])]
    ppermute x5, starting transfers between devices: 4.98 us -> 4.33 us  [seq_swap(): return lax.ppermute(x, 'seq', [(i, i ^ bits) for i in range(seqs)])]
  transfers between devices with their start and end apart: 26 -> 26, of which waited for: 7 -> 7; matrix products, arithmetic and copies ran while one was open for 0% -> 1% of each run, Pallas kernels for 37% -> 37%
where the time goes in v16:
time: 58.9 us; the launch traced here: 58.5 us
  Pallas kernels  26.9 us (46%)
  starting transfers between devices  17.4 us (30%)
  waiting for transfers between devices  7.74 us (13%)
  local copies, waits for them, and re-layouts  5.14 us (9%)
  between operations  1.09 us (2%)
    pallas_call x1, Pallas kernels, per_device(): pl.pallas_call(functools.partial(rows_kernel, split), out_shape=(jax.Shap...  9.41 us
    ppermute x5, starting transfers between devices, x_swap(): return lax.ppermute(x, 'roll', [(i, i ^ 2) for i in range(rolls)])  8.22 us
    pallas_call x1, Pallas kernels, per_device(): pl.pallas_call(functools.partial(last_kernel, split), out_shape=jax.Shape...  5.15 us
    unnamed x28, local copies, waits for them, and re-layouts  5.03 us
    ppermute x5, starting transfers between devices, seq_swap(): return lax.ppermute(x, 'seq', [(i, i ^ bits) for i in range(seqs)])  4.33 us
    ppermute x15, starting transfers between devices, core_swap(): return lax.ppermute(x, 'roll', [(i, i ^ 1) for i in range(rolls)])  3.31 us
    ppermute x5, waiting for transfers between devices, seq_swap(): return lax.ppermute(x, 'seq', [(i, i ^ bits) for i in range(seqs)])  3.1 us
    pallas_call x1, Pallas kernels, per_device(): pl.pallas_call(functools.partial(embed_kernel, split), out_shape=[jax.Sha...  2.72 us
  transfers between devices with their start and end apart: 26, of which 7 were waited for; matrix products, arithmetic and copies ran while one was open for 1% of the time, Pallas kernels for 37%

profile of v16, /device:TPU:0, one launch (start us, length us, event | category | flops | bytes accessed | tf_op | source)
XLA Modules:
  0.0 58.5 jit_solution(11557593633126019796)
XLA Ops:
  0.0 0.5 collective-permute-start.6
  0.5 0.5 collective-permute-start.2
  1.0 2.3 %shard_map.109 = (bf16[80,1280]{1,0:T(8,128)(2,1)}, bf16[80,2304]{1,0:T(8,128)(2,1)}, bf16[80,2304]{1,0:T(8,128)(2,1)}) custom-call(bf16[2,320,640]{2,1,0:T(8,128)(2,1)} %rest_2_.2, bf16[2,160,3200]{2,1,0:T(8,128)(2,1)} %rest_1_.3, bf16[2,160,1280]{2,1,0:T(8,128)(2,1)} %rest_2_.3), custom_call_target="tpu_custom_call" | custom-call | tf_op jit(solution)/shard_map/pallas_call | solution.py:488
  3.5 2.9 %collective-permute-start.5 = (bf16[80,1280]{1,0:T(8,128)(2,1)}, bf16[80,1280]{1,0:T(8,128)(2,1)}, u32[]{:S(2)}, u32[]{:S(2)}) collective-permute-start(bf16[80,1280]{1,0:T(8,128)(2,1)} %get-tuple-element.36), channel_id=1, source_target_pairs={{0,2},{1,3},{2,0},{3,1},{4,6},{5,7},{6,4},{7,5},{8,10},{9,11},{10,... | collective-permute-start | bytes 614408 | tf_op jit(solution)/shard_map/ppermute | solution.py:473
  6.5 0.3 collective-permute-done.1.rest_1_.rest_4_
  6.9 2.7 %shard_map.110 = (bf16[64,1280]{1,0:T(8,128)(2,1)}, f32[64,640]{1,0:T(8,128)}, bf16[64,640]{1,0:T(8,128)(2,1)}) custom-call(f32[30,1280]{1,0:T(8,128)} %embed.1, f32[1280]{0:T(1024)} %brk.1, f32[2,1280]{1,0:T(2,128)} %gain_in.1, bf16[2,320,640]{2,1,0:T(8,128)(2,1)} %rest_2_.2, bf16[2,320,640]{2,1,0:T(8,128)(2,1)} %collective-permute-done.1.rest_1_.rest_4_), custom_call_target="tpu_custom_call" | custom-call | tf_op jit(solution)/shard_map/pallas_call | solution.py:498
  9.6 2.9 %collective-permute-start.4 = (bf16[64,640]{1,0:T(8,128)(2,1)}, bf16[64,640]{1,0:T(8,128)(2,1)S(1)}, u32[]{:S(2)}, u32[]{:S(2)}) collective-permute-start(bf16[64,640]{1,0:T(8,128)(2,1)} %get-tuple-element.41), channel_id=1, source_target_pairs={{0,2},{1,3},{2,0},{3,1},{4,6},{5,7},{6,4},{7,5},{8,10},{9,11},{10,... | collective-permute-start | bytes 245768 | tf_op jit(solution)/shard_map/ppermute | solution.py:473
  12.5 0.9 %copy-done.3 = bf16[2,160,1280]{2,1,0:T(8,128)(2,1)} copy-done((bf16[2,160,1280]{2,1,0:T(8,128)(2,1)}, bf16[2,160,1280]{2,1,0:T(8,128)(2,1)S(1)}, u32[]{:S(2)}) %copy-start.3) | copy-done | bytes 819224
  13.4 1.5 %collective-permute-start.3 = (s32[2,384]{1,0:T(2,128)S(1)}, s32[2,384]{1,0:T(2,128)S(1)}, u32[]{:S(2)}, u32[]{:S(2)}) collective-permute-start(s32[2,384]{1,0:T(2,128)S(1)} %pad_add_fusion), channel_id=1, source_target_pairs={{0,4},{1,29},{2,6},{3,31},{4,8},{5,1},{6,10},{7,3},{8,12},{9,5},{1... | collective-permute-start | bytes 9224 | tf_op jit(solution)/shard_map/ppermute | solution.py:527
  15.6 1.6 %collective-permute-start.14 = (bf16[80,2304]{1,0:T(8,128)(2,1)}, bf16[80,2304]{1,0:T(8,128)(2,1)S(1)}, u32[]{:S(2)}, u32[]{:S(2)}) collective-permute-start(bf16[80,2304]{1,0:T(8,128)(2,1)} %get-tuple-element.53), channel_id=1, source_target_pairs={{0,2},{1,3},{2,0},{3,1},{4,6},{5,7},{6,4},{7,5},{8,10},{9,11},{10,... | collective-permute-start | bytes 1105928 | tf_op jit(solution)/shard_map/ppermute | solution.py:473
  17.2 2.5 %collective-permute-done.3 = s32[2,384]{1,0:T(2,128)S(1)} collective-permute-done((s32[2,384]{1,0:T(2,128)S(1)}, s32[2,384]{1,0:T(2,128)S(1)}, u32[]{:S(2)}, u32[]{:S(2)}) %collective-permute-start.3) | collective-permute-done | bytes 3104 | tf_op jit(solution)/shard_map/ppermute | solution.py:527
  19.8 0.9 %copy-done.6 = f32[64,640]{1,0:T(8,128)S(1)} copy-done((f32[64,640]{1,0:T(8,128)S(1)}, f32[64,640]{1,0:T(8,128)}, u32[]{:S(2)}) %copy-start.6) | copy-done | bytes 163864
  20.7 2.2 %shard_map.111.rest_0_ = bf16[32,3200]{1,0:T(8,128)(2,1)S(1)} custom-call(f32[64,640]{1,0:T(8,128)S(1)} %copy-done.6, bf16[64,640]{1,0:T(8,128)(2,1)S(1)} %collective-permute-done.4.other, f32[2,640]{1,0:T(2,128)S(1)} %copy-done.9, bf16[2,160,3200]{2,1,0:T(8,128)(2,1)S(1)} %copy-done, bf16[2,160,3200]{2,1,0:T(8,128)(2,1)} %collective-permute-done.6.rest_1_.near_conv.rest_3_), custom_call_target="tpu_custom_call" | custom-call | tf_op jit(solution)/shard_map/pallas_call | solution.py:536
  23.1 0.4 collective-permute-start.12
  23.6 3.0 %collective-permute-start.11 = (bf16[80,1280]{1,0:T(8,128)(2,1)}, bf16[80,1280]{1,0:T(8,128)(2,1)}, u32[]{:S(2)}, u32[]{:S(2)}) collective-permute-start(bf16[80,1280]{1,0:T(8,128)(2,1)} %collective-permute-done.5.rest_6_), channel_id=1, source_target_pairs={{0,4},{4,0},{8,12},{12,8},{16,20},{20,16},{24,28},{28,24},{1,5},{5... | collective-permute-start | bytes 614408 | tf_op jit(solution)/shard_map/ppermute | solution.py:476
  26.6 0.4 collective-permute-start.8
  27.1 1.1 %copy-done.2 = bf16[2,320,640]{2,1,0:T(8,128)(2,1)S(1)} copy-done((bf16[2,320,640]{2,1,0:T(8,128)(2,1)S(1)}, bf16[2,320,640]{2,1,0:T(8,128)(2,1)}, u32[]{:S(2)}) %copy-start.2) | copy-done | bytes 819224
  28.2 1.1 %copy-done.4 = bf16[2,160,1280]{2,1,0:T(8,128)(2,1)S(1)} copy-done((bf16[2,160,1280]{2,1,0:T(8,128)(2,1)S(1)}, bf16[2,160,1280]{2,1,0:T(8,128)(2,1)}, u32[]{:S(2)}) %copy-start.4) | copy-done | bytes 819224
  29.3 0.9 %copy-done.7 = bf16[64,1280]{1,0:T(8,128)(2,1)S(1)} copy-done((bf16[64,1280]{1,0:T(8,128)(2,1)S(1)}, bf16[64,1280]{1,0:T(8,128)(2,1)}, u32[]{:S(2)}) %copy-start.7) | copy-done | bytes 163864
  30.3 2.7 %shard_map.112 = (bf16[1008,320]{1,0:T(8,128)(2,1)S(1)}, bf16[1008,64]{1,0:T(8,128)(2,1)S(1)}, bf16[384,1280]{1,0:T(8,128)(2,1)S(1)}, bf16[640,640]{1,0:T(8,128)(2,1)S(1)}) custom-call(s32[2]{0:T(128)S(1)} %pad_add_fusion.1.span, s32[1,1280]{1,0:T(1,128)S(1)} %broadcast_in_dim.6.near, bf16[64,1280]{1,0:T(8,128)(2,1)S(1)} %copy-done.7, ...), custom_call_target="tpu_custom_call" | custom-call | tf_op jit(solution)/shard_map/pallas_call | solution.py:567
  33.1 3.1 %collective-permute-done.11.rest_7_ = bf16[80,1280]{1,0:T(8,128)(2,1)} collective-permute-done((bf16[80,1280]{1,0:T(8,128)(2,1)}, bf16[80,1280]{1,0:T(8,128)(2,1)}, u32[]{:S(2)}, u32[]{:S(2)}) %collective-permute-start.11) | collective-permute-done | bytes 204832 | tf_op jit(solution)/shard_map/ppermute | solution.py:476
  36.2 0.5 collective-permute-start.10
  36.8 0.8 %collective-permute-start.19 = (bf16[80,2304]{1,0:T(8,128)(2,1)S(1)}, bf16[80,2304]{1,0:T(8,128)(2,1)S(1)}, u32[]{:S(2)}, u32[]{:S(2)}) collective-permute-start(bf16[80,2304]{1,0:T(8,128)(2,1)S(1)} %collective-permute-done.14.rest_5_), channel_id=1, source_target_pairs={{0,4},{4,0},{8,12},{12,8},{16,20},{20,16},{24,28},{28,24},{1,5},{5... | collective-permute-start | bytes 1105928 | tf_op jit(solution)/shard_map/ppermute | solution.py:476
  37.8 0.4 collective-permute-start.21
  38.4 0.3 collective-permute-start.18
  38.7 1.1 %collective-permute-done.17.rest_12_ = bf16[80,1280]{1,0:T(8,128)(2,1)S(1)} collective-permute-done((bf16[80,1280]{1,0:T(8,128)(2,1)}, bf16[80,1280]{1,0:T(8,128)(2,1)S(1)}, u32[]{:S(2)}, u32[]{:S(2)}) %collective-permute-start.17) | collective-permute-done | bytes 204832 | tf_op jit(solution)/shard_map/ppermute | solution.py:470
  39.9 0.3 collective-permute-done.18.rest_13_
  40.2 9.4 %shard_map.113 = (bf16[1008,640]{1,0:T(8,128)(2,1)S(1)}, bf16[496,1280]{1,0:T(8,128)(2,1)S(1)}) custom-call(s32[2]{0:T(128)S(1)} %pad_add_fusion.1.span, bf16[1008,320]{1,0:T(8,128)(2,1)S(1)} %get-tuple-element.45.hot5, bf16[1008,64]{1,0:T(8,128)(2,1)S(1)} %get-tuple-element.46.hot1, f32[2,640]{1,0:T(2,128)S(1)} %copy-done.10, f32[2,1280]{1,0:T(2,128)S(1)} %copy-done.8, ...), custom_call_target="tpu_custom_call" | custom-call | tf_op jit(solution)/shard_map/pallas_call | solution.py:590
  49.9 0.3 collective-permute-start.24
  50.4 0.3 collective-permute-start.25
  50.7 2.4 %shard_map.114.rest_0_ = f32[496,640]{1,0:T(8,128)S(1)} custom-call(bf16[1008,640]{1,0:T(8,128)(2,1)S(1)} %get-tuple-element.58.ci, bf16[2,160,3200]{2,1,0:T(8,128)(2,1)S(1)} %copy-done, bf16[2,160,3200]{2,1,0:T(8,128)(2,1)} %collective-permute-done.6.rest_1_.near_conv.rest_3_), custom_call_target="tpu_custom_call" | custom-call | tf_op jit(solution)/shard_map/pallas_call | solution.py:610
  53.2 5.1 %shard_map.115 = bf16[496,1280]{1,0:T(8,128)(2,1)} custom-call(bf16[1008,640]{1,0:T(8,128)(2,1)S(1)} %get-tuple-element.58.ci, bf16[496,1280]{1,0:T(8,128)(2,1)S(1)} %get-tuple-element.59.hid, f32[2,640]{1,0:T(2,128)S(1)} %copy-done.10, f32[496,640]{1,0:T(8,128)S(1)} %shard_map.114.rest_0_, bf16[2,160,3200]{2,1,0:T(8,128)(2,1)S(1)} %copy-done, ...), custom_call_target="tpu_custom_call" | custom-call | tf_op jit(solution)/shard_map/pallas_call | solution.py:620
  (65 shorter events, 1.8 us)
Async XLA Ops:
  0.0 19.7 %collective-permute-start.6 = (bf16[2,160,3200]{2,1,0:T(8,128)(2,1)}, bf16[2,160,3200]{2,1,0:T(8,128)(2,1)}, u32[]{:S(2)}, u32[]{:S(2)}) collective-permute-start(bf16[2,160,3200]{2,1,0:T(8,128)(2,1)} %rest_1_.3), channel_id=1, source_target_pairs={{0,1},{1,0},{2,3},{3,2},{4,5},{5,4},{6,7},{7,6},{8,9},{9,8},{10,11... | collective-permute-start | bytes 6144008 | tf_op jit(solution)/shard_map/ppermute | solution.py:470
  0.5 6.4 %collective-permute-start.1 = (bf16[2,320,640]{2,1,0:T(8,128)(2,1)}, bf16[2,320,640]{2,1,0:T(8,128)(2,1)}, u32[]{:S(2)}, u32[]{:S(2)}) collective-permute-start(bf16[2,320,640]{2,1,0:T(8,128)(2,1)} %rest_2_.2), channel_id=1, source_target_pairs={{0,1},{1,0},{2,3},{3,2},{4,5},{5,4},{6,7},{7,6},{8,9},{9,8},{10,11... | collective-permute-start | bytes 2457608 | tf_op jit(solution)/shard_map/ppermute | solution.py:470
  0.5 12.0 %collective-permute-start.2 = (bf16[2,160,1280]{2,1,0:T(8,128)(2,1)}, bf16[2,160,1280]{2,1,0:T(8,128)(2,1)S(1)}, u32[]{:S(2)}, u32[]{:S(2)}) collective-permute-start(bf16[2,160,1280]{2,1,0:T(8,128)(2,1)} %rest_2_.3), channel_id=1, source_target_pairs={{0,1},{1,0},{2,3},{3,2},{4,5},{5,4},{6,7},{7,6},{8,9},{9,8},{10,11... | collective-permute-start | bytes 2457608 | tf_op jit(solution)/shard_map/ppermute | solution.py:470
  1.0 18.8 %copy-start = (bf16[2,160,3200]{2,1,0:T(8,128)(2,1)S(1)}, bf16[2,160,3200]{2,1,0:T(8,128)(2,1)}, u32[]{:S(2)}) copy-start(bf16[2,160,3200]{2,1,0:T(8,128)(2,1)} %rest_1_.3) | copy-start | bytes 6144004
  3.3 16.5 %copy-start.9 = (f32[2,640]{1,0:T(2,128)S(1)}, f32[2,640]{1,0:T(2,128)}, u32[]{:S(2)}) copy-start(f32[2,640]{1,0:T(2,128)} %gain_mid.1) | copy-start | bytes 15364
  3.4 3.1 %collective-permute-start = (s32[384]{0:T(512)S(1)}, s32[384]{0:T(512)S(1)}, u32[]{:S(2)}, u32[]{:S(2)}) collective-permute-start(s32[384]{0:T(512)S(1)} %get-tuple-element.37), channel_id=1, source_target_pairs={{0,1},{1,0},{2,3},{3,2},{4,5},{5,4},{6,7},{7,6},{8,9},{9,8},{10,11... | collective-permute-start | bytes 4616 | tf_op jit(solution)/shard_map/ppermute | solution.py:470
  3.5 16.2 %collective-permute-start.5 = (bf16[80,1280]{1,0:T(8,128)(2,1)}, bf16[80,1280]{1,0:T(8,128)(2,1)}, u32[]{:S(2)}, u32[]{:S(2)}) collective-permute-start(bf16[80,1280]{1,0:T(8,128)(2,1)} %get-tuple-element.36), channel_id=1, source_target_pairs={{0,2},{1,3},{2,0},{3,1},{4,6},{5,7},{6,4},{7,5},{8,10},{9,11},{10,... | collective-permute-start | bytes 614408 | tf_op jit(solution)/shard_map/ppermute | solution.py:473
  9.6 6.0 %collective-permute-start.4 = (bf16[64,640]{1,0:T(8,128)(2,1)}, bf16[64,640]{1,0:T(8,128)(2,1)S(1)}, u32[]{:S(2)}, u32[]{:S(2)}) collective-permute-start(bf16[64,640]{1,0:T(8,128)(2,1)} %get-tuple-element.41), channel_id=1, source_target_pairs={{0,2},{1,3},{2,0},{3,1},{4,6},{5,7},{6,4},{7,5},{8,10},{9,11},{10,... | collective-permute-start | bytes 245768 | tf_op jit(solution)/shard_map/ppermute | solution.py:473
  13.4 6.3 %collective-permute-start.3 = (s32[2,384]{1,0:T(2,128)S(1)}, s32[2,384]{1,0:T(2,128)S(1)}, u32[]{:S(2)}, u32[]{:S(2)}) collective-permute-start(s32[2,384]{1,0:T(2,128)S(1)} %pad_add_fusion), channel_id=1, source_target_pairs={{0,4},{1,29},{2,6},{3,31},{4,8},{5,1},{6,10},{7,3},{8,12},{9,5},{1... | collective-permute-start | bytes 9224 | tf_op jit(solution)/shard_map/ppermute | solution.py:527
  15.6 17.4 %collective-permute-start.14 = (bf16[80,2304]{1,0:T(8,128)(2,1)}, bf16[80,2304]{1,0:T(8,128)(2,1)S(1)}, u32[]{:S(2)}, u32[]{:S(2)}) collective-permute-start(bf16[80,2304]{1,0:T(8,128)(2,1)} %get-tuple-element.53), channel_id=1, source_target_pairs={{0,2},{1,3},{2,0},{3,1},{4,6},{5,7},{6,4},{7,5},{8,10},{9,11},{10,... | collective-permute-start | bytes 1105928 | tf_op jit(solution)/shard_map/ppermute | solution.py:473
  20.7 6.4 %copy-start.1 = (bf16[2,160,1280]{2,1,0:T(8,128)(2,1)S(1)}, bf16[2,160,1280]{2,1,0:T(8,128)(2,1)}, u32[]{:S(2)}) copy-start(bf16[2,160,1280]{2,1,0:T(8,128)(2,1)} %rest_2_.3) | copy-start | bytes 2457604
  22.9 3.7 %collective-permute-start.7 = (s32[384]{0:T(512)S(1)}, s32[384]{0:T(512)S(1)}, u32[]{:S(2)}, u32[]{:S(2)}) collective-permute-start(s32[384]{0:T(512)S(1)} %get-tuple-element.43), channel_id=1, source_target_pairs={{0,1},{1,0},{2,3},{3,2},{4,5},{5,4},{6,7},{7,6},{8,9},{9,8},{10,11... | collective-permute-start | bytes 4616 | tf_op jit(solution)/shard_map/ppermute | solution.py:470
  23.1 13.6 %collective-permute-start.13 = (bf16[80,1280]{1,0:T(8,128)(2,1)}, bf16[80,1280]{1,0:T(8,128)(2,1)}, u32[]{:S(2)}, u32[]{:S(2)}) collective-permute-start(bf16[80,1280]{1,0:T(8,128)(2,1)} %collective-permute-done.5.rest_6_), channel_id=1, source_target_pairs={{0,12},{4,8},{8,4},{12,0},{16,28},{20,24},{24,20},{28,16},{1,13},{... | collective-permute-start | bytes 614408 | tf_op jit(solution)/shard_map/ppermute | solution.py:476
  23.1 13.6 %collective-permute-start.12 = (bf16[80,1280]{1,0:T(8,128)(2,1)}, bf16[80,1280]{1,0:T(8,128)(2,1)}, u32[]{:S(2)}, u32[]{:S(2)}) collective-permute-start(bf16[80,1280]{1,0:T(8,128)(2,1)} %collective-permute-done.5.rest_6_), channel_id=1, source_target_pairs={{0,8},{4,12},{8,0},{12,4},{16,24},{20,28},{24,16},{28,20},{1,9},{5... | collective-permute-start | bytes 614408 | tf_op jit(solution)/shard_map/ppermute | solution.py:476
  23.6 12.6 %collective-permute-start.11 = (bf16[80,1280]{1,0:T(8,128)(2,1)}, bf16[80,1280]{1,0:T(8,128)(2,1)}, u32[]{:S(2)}, u32[]{:S(2)}) collective-permute-start(bf16[80,1280]{1,0:T(8,128)(2,1)} %collective-permute-done.5.rest_6_), channel_id=1, source_target_pairs={{0,4},{4,0},{8,12},{12,8},{16,20},{20,16},{24,28},{28,24},{1,5},{5... | collective-permute-start | bytes 614408 | tf_op jit(solution)/shard_map/ppermute | solution.py:476
  26.6 9.6 %collective-permute-start.8 = (bf16[32,3200]{1,0:T(8,128)(2,1)S(1)}, bf16[32,3200]{1,0:T(8,128)(2,1)}, u32[]{:S(2)}, u32[]{:S(2)}) collective-permute-start(bf16[32,3200]{1,0:T(8,128)(2,1)S(1)} %shard_map.111.rest_0_), channel_id=1, source_target_pairs={{0,2},{1,3},{2,0},{3,1},{4,6},{5,7},{6,4},{7,5},{8,10},{9,11},{10,... | collective-permute-start | bytes 614408 | tf_op jit(solution)/shard_map/ppermute | solution.py:473
  30.3 7.6 %copy-start.13 = (bf16[80,2304]{1,0:T(8,128)(2,1)S(1)}, bf16[80,2304]{1,0:T(8,128)(2,1)}, u32[]{:S(2)}) copy-start(bf16[80,2304]{1,0:T(8,128)(2,1)} %get-tuple-element.62) | copy-start | bytes 1105924
  30.3 9.9 %copy-start.8 = (f32[2,1280]{1,0:T(2,128)S(1)}, f32[2,1280]{1,0:T(2,128)}, u32[]{:S(2)}) copy-start(f32[2,1280]{1,0:T(2,128)} %gain_in.1) | copy-start | bytes 30724
  30.3 9.9 %copy-start.10 = (f32[2,640]{1,0:T(2,128)S(1)}, f32[2,640]{1,0:T(2,128)}, u32[]{:S(2)}) copy-start(f32[2,640]{1,0:T(2,128)} %gain_out.3) | copy-start | bytes 15364
  33.0 3.8 %collective-permute-start.9 = (bf16[32,3200]{1,0:T(8,128)(2,1)S(1)}, bf16[32,3200]{1,0:T(8,128)(2,1)S(1)}, u32[]{:S(2)}, u32[]{:S(2)}) collective-permute-start(bf16[32,3200]{1,0:T(8,128)(2,1)S(1)} %shard_map.111.rest_0_), channel_id=1, source_target_pairs={{0,1},{1,0},{2,3},{3,2},{4,5},{5,4},{6,7},{7,6},{8,9},{9,8},{10,11... | collective-permute-start | bytes 614408 | tf_op jit(solution)/shard_map/ppermute | solution.py:470
  36.2 1.7 %collective-permute-start.15 = (bf16[80,1280]{1,0:T(8,128)(2,1)}, bf16[80,1280]{1,0:T(8,128)(2,1)S(1)}, u32[]{:S(2)}, u32[]{:S(2)}) collective-permute-start(bf16[80,1280]{1,0:T(8,128)(2,1)} %collective-permute-done.5.rest_6_), channel_id=1, source_target_pairs={{0,1},{1,0},{2,3},{3,2},{4,5},{5,4},{6,7},{7,6},{8,9},{9,8},{10,11... | collective-permute-start | bytes 614408 | tf_op jit(solution)/shard_map/ppermute | solution.py:470
  36.2 2.0 %collective-permute-start.10 = (bf16[32,3200]{1,0:T(8,128)(2,1)}, bf16[32,3200]{1,0:T(8,128)(2,1)S(1)}, u32[]{:S(2)}, u32[]{:S(2)}) collective-permute-start(bf16[32,3200]{1,0:T(8,128)(2,1)} %collective-permute-done.8.rest_1_), channel_id=1, source_target_pairs={{0,1},{1,0},{2,3},{3,2},{4,5},{5,4},{6,7},{7,6},{8,9},{9,8},{10,11... | collective-permute-start | bytes 614408 | tf_op jit(solution)/shard_map/ppermute | solution.py:470
  36.7 1.7 %collective-permute-start.16 = (bf16[80,1280]{1,0:T(8,128)(2,1)}, bf16[80,1280]{1,0:T(8,128)(2,1)S(1)}, u32[]{:S(2)}, u32[]{:S(2)}) collective-permute-start(bf16[80,1280]{1,0:T(8,128)(2,1)} %collective-permute-done.11.rest_7_), channel_id=1, source_target_pairs={{0,1},{1,0},{2,3},{3,2},{4,5},{5,4},{6,7},{7,6},{8,9},{9,8},{10,11... | collective-permute-start | bytes 614408 | tf_op jit(solution)/shard_map/ppermute | solution.py:470
  36.8 13.1 %collective-permute-start.20 = (bf16[80,2304]{1,0:T(8,128)(2,1)S(1)}, bf16[80,2304]{1,0:T(8,128)(2,1)S(1)}, u32[]{:S(2)}, u32[]{:S(2)}) collective-permute-start(bf16[80,2304]{1,0:T(8,128)(2,1)S(1)} %collective-permute-done.14.rest_5_), channel_id=1, source_target_pairs={{0,8},{4,12},{8,0},{12,4},{16,24},{20,28},{24,16},{28,20},{1,9},{5... | collective-permute-start | bytes 1105928 | tf_op jit(solution)/shard_map/ppermute | solution.py:476
  36.8 13.4 %collective-permute-start.19 = (bf16[80,2304]{1,0:T(8,128)(2,1)S(1)}, bf16[80,2304]{1,0:T(8,128)(2,1)S(1)}, u32[]{:S(2)}, u32[]{:S(2)}) collective-permute-start(bf16[80,2304]{1,0:T(8,128)(2,1)S(1)} %collective-permute-done.14.rest_5_), channel_id=1, source_target_pairs={{0,4},{4,0},{8,12},{12,8},{16,20},{20,16},{24,28},{28,24},{1,5},{5... | collective-permute-start | bytes 1105928 | tf_op jit(solution)/shard_map/ppermute | solution.py:476
  37.8 12.6 %collective-permute-start.21 = (bf16[80,2304]{1,0:T(8,128)(2,1)S(1)}, bf16[80,2304]{1,0:T(8,128)(2,1)S(1)}, u32[]{:S(2)}, u32[]{:S(2)}) collective-permute-start(bf16[80,2304]{1,0:T(8,128)(2,1)S(1)} %copy-done.13), channel_id=1, source_target_pairs={{0,2},{1,3},{2,0},{3,1},{4,6},{5,7},{6,4},{7,5},{8,10},{9,11},{10,... | collective-permute-start | bytes 1105928 | tf_op jit(solution)/shard_map/ppermute | solution.py:473
  38.2 1.7 %collective-permute-start.17 = (bf16[80,1280]{1,0:T(8,128)(2,1)}, bf16[80,1280]{1,0:T(8,128)(2,1)S(1)}, u32[]{:S(2)}, u32[]{:S(2)}) collective-permute-start(bf16[80,1280]{1,0:T(8,128)(2,1)} %collective-permute-done.12.rest_8_), channel_id=1, source_target_pairs={{0,1},{1,0},{2,3},{3,2},{4,5},{5,4},{6,7},{7,6},{8,9},{9,8},{10,11... | collective-permute-start | bytes 614408 | tf_op jit(solution)/shard_map/ppermute | solution.py:470
  38.4 1.8 %collective-permute-start.18 = (bf16[80,1280]{1,0:T(8,128)(2,1)}, bf16[80,1280]{1,0:T(8,128)(2,1)S(1)}, u32[]{:S(2)}, u32[]{:S(2)}) collective-permute-start(bf16[80,1280]{1,0:T(8,128)(2,1)} %collective-permute-done.13.rest_9_), channel_id=1, source_target_pairs={{0,1},{1,0},{2,3},{3,2},{4,5},{5,4},{6,7},{7,6},{8,9},{9,8},{10,11... | collective-permute-start | bytes 614408 | tf_op jit(solution)/shard_map/ppermute | solution.py:470
  49.6 3.5 %collective-permute-start.22 = (bf16[80,2304]{1,0:T(8,128)(2,1)S(1)}, bf16[80,2304]{1,0:T(8,128)(2,1)S(1)}, u32[]{:S(2)}, u32[]{:S(2)}) collective-permute-start(bf16[80,2304]{1,0:T(8,128)(2,1)S(1)} %collective-permute-done.14.rest_5_), channel_id=1, source_target_pairs={{0,1},{1,0},{2,3},{3,2},{4,5},{5,4},{6,7},{7,6},{8,9},{9,8},{10,11... | collective-permute-start | bytes 1105928 | tf_op jit(solution)/shard_map/ppermute | solution.py:470
  49.9 3.2 %collective-permute-start.24 = (bf16[80,2304]{1,0:T(8,128)(2,1)S(1)}, bf16[80,2304]{1,0:T(8,128)(2,1)S(1)}, u32[]{:S(2)}, u32[]{:S(2)}) collective-permute-start(bf16[80,2304]{1,0:T(8,128)(2,1)S(1)} %collective-permute-done.20.rest_7_), channel_id=1, source_target_pairs={{0,1},{1,0},{2,3},{3,2},{4,5},{5,4},{6,7},{7,6},{8,9},{9,8},{10,11... | collective-permute-start | bytes 1105928 | tf_op jit(solution)/shard_map/ppermute | solution.py:470
  50.2 3.0 %collective-permute-start.23 = (bf16[80,2304]{1,0:T(8,128)(2,1)S(1)}, bf16[80,2304]{1,0:T(8,128)(2,1)S(1)}, u32[]{:S(2)}, u32[]{:S(2)}) collective-permute-start(bf16[80,2304]{1,0:T(8,128)(2,1)S(1)} %collective-permute-done.19.rest_6_), channel_id=1, source_target_pairs={{0,1},{1,0},{2,3},{3,2},{4,5},{5,4},{6,7},{7,6},{8,9},{9,8},{10,11... | collective-permute-start | bytes 1105928 | tf_op jit(solution)/shard_map/ppermute | solution.py:470
  50.4 2.7 %collective-permute-start.25 = (bf16[80,2304]{1,0:T(8,128)(2,1)S(1)}, bf16[80,2304]{1,0:T(8,128)(2,1)S(1)}, u32[]{:S(2)}, u32[]{:S(2)}) collective-permute-start(bf16[80,2304]{1,0:T(8,128)(2,1)S(1)} %collective-permute-done.21.rest_8_), channel_id=1, source_target_pairs={{0,1},{1,0},{2,3},{3,2},{4,5},{5,4},{6,7},{7,6},{8,9},{9,8},{10,11... | collective-permute-start | bytes 1105928 | tf_op jit(solution)/shard_map/ppermute | solution.py:470
  (8 other events, 13.3 us)

commit v17 on v14

--- a/solution.py
+++ b/solution.py
@@ -146,6 +146,8 @@
 
 def table_kernel(split, own, other, gain, w_all, *rest):
     *outs, w, full, sem = rest
+    if split:
+        outs[2][...] = gain[0:1, 0:128]
     copy = pltpu.make_async_copy(w_all.at[0], w, sem)
     copy.start()
     wide = own[...] + other[...].astype(F32)
@@ -518,10 +520,10 @@
         before = lax.ppermute(codes[rows - REACH :], "seq", pairs)
         behind = lax.ppermute(codes[:REACH], "seq", [(j, i) for i, j in pairs])
     wide = KERNEL * H
-    shapes = [(SLOT, F32), (SLOT, BF)] if split else [(CODES, F32)]
+    shapes = [((SLOT, wide), F32), ((SLOT, wide), BF), ((1, 128), F32)] if split else [((CODES, wide), F32)]
     taps = pl.pallas_call(
         functools.partial(table_kernel, split),
-        out_shape=[jax.ShapeDtypeStruct((n, wide), t) for n, t in shapes],
+        out_shape=[jax.ShapeDtypeStruct(n, t) for n, t in shapes],
         in_specs=[VMEM, VMEM, VMEM, HBM],
         out_specs=[VMEM] * len(shapes),
         scratch_shapes=[
@@ -533,9 +535,9 @@
         compiler_params=params(12),
     )(own, other, gain_mid, conv_w)
     if split:
-        came = core_swap(after(moved[1], taps[1]))
+        came = core_swap(after(moved[1], taps[2]))
         before, behind = jnp.where(low, moved[0], came), jnp.where(low, came, moved[0])
-        relay = after(far_a, taps[1])
+        relay = after(far_a, taps[2])
         parts_a = [far_a] + [seq_swap(relay, b) for b in (1, 2, 3)]
         sent = (taps[0] + after(core_swap(taps[1]), before, behind).astype(F32)).astype(BF)
         received = x_swap(sent)

time: 57.9 us -> 57.9 us (level)
  no operation moved by 1% of the time
where the time goes in v17:
time: 57.9 us; the launch traced here: 57.7 us
  Pallas kernels  24.1 us (42%)
  starting transfers between devices  19.6 us (34%)
  waiting for transfers between devices  9.86 us (17%)
  other arithmetic  2.1 us (4%)
  local copies, waits for them, and re-layouts  1.06 us (2%)
  between operations  1 us (2%)
    pallas_call x1, Pallas kernels, per_device(): pl.pallas_call(functools.partial(rows_kernel, split), out_shape=(jax.Shap...  9.42 us
    ppermute x5, starting transfers between devices, x_swap(): return lax.ppermute(x, 'roll', [(i, i ^ 2) for i in range(rolls)])  7.32 us
    ppermute x5, starting transfers between devices, seq_swap(): return lax.ppermute(x, 'seq', [(i, i ^ bits) for i in range(seqs)])  5.66 us
    pallas_call x1, Pallas kernels, per_device(): pl.pallas_call(functools.partial(last_kernel, split), out_shape=jax.Shape...  5.46 us
    ppermute x17, starting transfers between devices, core_swap(): return lax.ppermute(x, 'roll', [(i, i ^ 1) for i in range(rolls)])  5.02 us
    ppermute x17, waiting for transfers between devices, core_swap(): return lax.ppermute(x, 'roll', [(i, i ^ 1) for i in range(rolls)])  3.72 us
    pallas_call x1, Pallas kernels, per_device(): pl.pallas_call(functools.partial(first_kernel, split), out_shape=[jax.Sha...  3.24 us
    ppermute x1, waiting for transfers between devices, per_device(): moved = lax.ppermute(after(pack, own), ('seq', 'roll'), moves)  3.13 us
  transfers between devices with their start and end apart: 28, of which 10 were waited for; matrix products, arithmetic and copies ran while one was open for 4% of the time, Pallas kernels for 29%

profile of v17, /device:TPU:0, one launch (start us, length us, event | category | flops | bytes accessed | tf_op | source)
XLA Modules:
  0.0 57.7 jit_solution(17817587707721085180)
XLA Ops:
  0.0 0.5 collective-permute-start.5
  0.6 3.2 %shard_map.109 = (bf16[64,1280]{1,0:T(8,128)(2,1)}, f32[64,640]{1,0:T(8,128)}, bf16[80,1280]{1,0:T(8,128)(2,1)}, bf16[80,2304]{1,0:T(8,128)(2,1)}, bf16[80,2304]{1,0:T(8,128)(2,1)}) custom-call(f32[30,1280]{1,0:T(8,128)} %embed.1, f32[1280]{0:T(1024)} %brk.1, f32[2,1280]{1,0:T(2,128)} %gain_in.1, bf16[2,320,640]{2,1,0:T(8,128)(2,1)} %rest_2_.2, ...), custom_call_target="tpu_custom_call" | custom-call | tf_op jit(solution)/shard_map/pallas_call | solution.py:484
  3.9 0.5 collective-permute-start.1
  4.6 2.9 %collective-permute-start.6 = (bf16[80,1280]{1,0:T(8,128)(2,1)}, bf16[80,1280]{1,0:T(8,128)(2,1)}, u32[]{:S(2)}, u32[]{:S(2)}) collective-permute-start(bf16[80,1280]{1,0:T(8,128)(2,1)} %get-tuple-element.43), channel_id=1, source_target_pairs={{0,2},{1,3},{2,0},{3,1},{4,6},{5,7},{6,4},{7,5},{8,10},{9,11},{10,... | collective-permute-start | bytes 614408 | tf_op jit(solution)/shard_map/ppermute | solution.py:471
  7.5 1.0 %fusion.1 = (bf16[64,640]{1,0:T(8,128)(2,1)S(1)}, f32[64,640]{1,0:T(8,128)S(1)}) fusion(f32[64,640]{1,0:T(8,128)} %get-tuple-element.40, f32[64,640]{1,0:T(8,128)S(1)} %collective-permute-done.1), kind=kLoop, calls=%fused_computation.11 | loop fusion | flops 81920 | bytes 573440 | tf_op jit(solution)/shard_map/convert_element_type | solution.py:509
  8.5 1.6 %collective-permute-start.2 = (s32[2,384]{1,0:T(2,128)S(1)}, s32[2,384]{1,0:T(2,128)S(1)}, u32[]{:S(2)}, u32[]{:S(2)}) collective-permute-start(s32[2,384]{1,0:T(2,128)S(1)} %pad_add_fusion), channel_id=1, source_target_pairs={{0,4},{1,29},{2,6},{3,31},{4,8},{5,1},{6,10},{7,3},{8,12},{9,5},{1... | collective-permute-start | bytes 9224 | tf_op jit(solution)/shard_map/ppermute | solution.py:514
  10.7 1.0 %collective-permute-start.3 = (bf16[64,640]{1,0:T(8,128)(2,1)S(1)}, bf16[64,640]{1,0:T(8,128)(2,1)S(1)}, u32[]{:S(2)}, u32[]{:S(2)}) collective-permute-start(bf16[64,640]{1,0:T(8,128)(2,1)S(1)} %get-tuple-element.77), channel_id=1, source_target_pairs={{0,2},{1,3},{2,0},{3,1},{4,6},{5,7},{6,4},{7,5},{8,10},{9,11},{10,... | collective-permute-start | bytes 245768 | tf_op jit(solution)/shard_map/ppermute | solution.py:471
  11.7 3.1 %collective-permute-done.2 = s32[2,384]{1,0:T(2,128)S(1)} collective-permute-done((s32[2,384]{1,0:T(2,128)S(1)}, s32[2,384]{1,0:T(2,128)S(1)}, u32[]{:S(2)}, u32[]{:S(2)}) %collective-permute-start.2) | collective-permute-done | bytes 3104 | tf_op jit(solution)/shard_map/ppermute | solution.py:514
  15.2 1.8 %shard_map.110 = (f32[32,3200]{1,0:T(8,128)S(1)}, bf16[32,3200]{1,0:T(8,128)(2,1)}, f32[1,128]{1,0:T(1,128)}) custom-call(f32[64,640]{1,0:T(8,128)S(1)} %get-tuple-element.78.own, bf16[64,640]{1,0:T(8,128)(2,1)S(1)} %collective-permute-done.3.other, f32[2,640]{1,0:T(2,128)S(1)} %copy-done.5, bf16[2,160,3200]{2,1,0:T(8,128)(2,1)S(1)} %copy-done), custom_call_target="tpu_custom_call" | custom-call | tf_op jit(solution)/shard_map/pallas_call | solution.py:524
  17.1 1.5 %collective-permute-start.7 = (s32[384]{0:T(512)S(1)}, s32[384]{0:T(512)S(1)}, u32[]{:S(2)}, u32[]{:S(2)}) collective-permute-start(s32[384]{0:T(512)S(1)} %get-tuple-element.46), channel_id=1, source_target_pairs={{0,1},{1,0},{2,3},{3,2},{4,5},{5,4},{6,7},{7,6},{8,9},{9,8},{10,11... | collective-permute-start | bytes 4616 | tf_op jit(solution)/shard_map/ppermute | solution.py:468
  18.6 1.4 %collective-permute-start.15 = (bf16[80,2304]{1,0:T(8,128)(2,1)}, bf16[80,2304]{1,0:T(8,128)(2,1)}, u32[]{:S(2)}, u32[]{:S(2)}) collective-permute-start(bf16[80,2304]{1,0:T(8,128)(2,1)} %get-tuple-element.60), channel_id=1, source_target_pairs={{0,2},{1,3},{2,0},{3,1},{4,6},{5,7},{6,4},{7,5},{8,10},{9,11},{10,... | collective-permute-start | bytes 1105928 | tf_op jit(solution)/shard_map/ppermute | solution.py:471
  20.0 1.1 %collective-permute-start.14 = (bf16[80,1280]{1,0:T(8,128)(2,1)}, bf16[80,1280]{1,0:T(8,128)(2,1)}, u32[]{:S(2)}, u32[]{:S(2)}) collective-permute-start(bf16[80,1280]{1,0:T(8,128)(2,1)} %collective-permute-done.6.rest_6_), channel_id=1, source_target_pairs={{0,12},{4,8},{8,4},{12,0},{16,28},{20,24},{24,20},{28,16},{1,13},{... | collective-permute-start | bytes 614408 | tf_op jit(solution)/shard_map/ppermute | solution.py:474
  21.5 1.9 %collective-permute-start.12 = (bf16[80,1280]{1,0:T(8,128)(2,1)}, bf16[80,1280]{1,0:T(8,128)(2,1)}, u32[]{:S(2)}, u32[]{:S(2)}) collective-permute-start(bf16[80,1280]{1,0:T(8,128)(2,1)} %collective-permute-done.6.rest_6_), channel_id=1, source_target_pairs={{0,4},{4,0},{8,12},{12,8},{16,20},{20,16},{24,28},{28,24},{1,5},{5... | collective-permute-start | bytes 614408 | tf_op jit(solution)/shard_map/ppermute | solution.py:474
  23.6 1.7 %collective-permute-done.8 = bf16[32,3200]{1,0:T(8,128)(2,1)} collective-permute-done((bf16[32,3200]{1,0:T(8,128)(2,1)}, bf16[32,3200]{1,0:T(8,128)(2,1)}, u32[]{:S(2)}, u32[]{:S(2)}) %collective-permute-start.8) | collective-permute-done | bytes 204832 | tf_op jit(solution)/shard_map/ppermute | solution.py:468
  25.3 1.0 %add_convert_fusion.rest_0_ = bf16[32,3200]{1,0:T(8,128)(2,1)S(1)} fusion(f32[32,3200]{1,0:T(8,128)S(1)} %get-tuple-element.47, bf16[32,3200]{1,0:T(8,128)(2,1)} %collective-permute-done.8), kind=kLoop, calls=%fused_computation | loop fusion | flops 307200 | bytes 819200 | tf_op jit(solution)/shard_map/convert_element_type | solution.py:542
  26.3 0.7 %collective-permute-start.9 = (bf16[32,3200]{1,0:T(8,128)(2,1)S(1)}, bf16[32,3200]{1,0:T(8,128)(2,1)S(1)}, u32[]{:S(2)}, u32[]{:S(2)}) collective-permute-start(bf16[32,3200]{1,0:T(8,128)(2,1)S(1)} %add_convert_fusion.rest_0_), channel_id=1, source_target_pairs={{0,2},{1,3},{2,0},{3,1},{4,6},{5,7},{6,4},{7,5},{8,10},{9,11},{10,... | collective-permute-start | bytes 614408 | tf_op jit(solution)/shard_map/ppermute | solution.py:471
  27.0 0.9 %copy-done.3 = bf16[64,1280]{1,0:T(8,128)(2,1)S(1)} copy-done((bf16[64,1280]{1,0:T(8,128)(2,1)S(1)}, bf16[64,1280]{1,0:T(8,128)(2,1)}, u32[]{:S(2)}) %copy-start.3) | copy-done | bytes 163864
  27.9 2.5 %shard_map.111 = (bf16[1008,320]{1,0:T(8,128)(2,1)S(1)}, bf16[1008,64]{1,0:T(8,128)(2,1)S(1)}, bf16[384,1280]{1,0:T(8,128)(2,1)S(1)}, bf16[640,640]{1,0:T(8,128)(2,1)S(1)}) custom-call(s32[2]{0:T(128)S(1)} %pad_add_fusion.1.span, s32[1,1280]{1,0:T(1,128)S(1)} %broadcast_in_dim.6.near, bf16[64,1280]{1,0:T(8,128)(2,1)S(1)} %copy-done.3, ...), custom_call_target="tpu_custom_call" | custom-call | tf_op jit(solution)/shard_map/pallas_call | solution.py:555
  30.6 0.9 %collective-permute-done.13.rest_8_ = bf16[80,1280]{1,0:T(8,128)(2,1)} collective-permute-done((bf16[80,1280]{1,0:T(8,128)(2,1)}, bf16[80,1280]{1,0:T(8,128)(2,1)}, u32[]{:S(2)}, u32[]{:S(2)}) %collective-permute-start.13) | collective-permute-done | bytes 204832 | tf_op jit(solution)/shard_map/ppermute | solution.py:474
  31.5 0.9 %collective-permute-done.12.rest_7_ = bf16[80,1280]{1,0:T(8,128)(2,1)} collective-permute-done((bf16[80,1280]{1,0:T(8,128)(2,1)}, bf16[80,1280]{1,0:T(8,128)(2,1)}, u32[]{:S(2)}, u32[]{:S(2)}) %collective-permute-start.12) | collective-permute-done | bytes 204832 | tf_op jit(solution)/shard_map/ppermute | solution.py:474
  32.3 0.5 collective-permute-start.17
  32.9 0.9 %collective-permute-done.9.rest_1_ = bf16[32,3200]{1,0:T(8,128)(2,1)S(1)} collective-permute-done((bf16[32,3200]{1,0:T(8,128)(2,1)S(1)}, bf16[32,3200]{1,0:T(8,128)(2,1)S(1)}, u32[]{:S(2)}, u32[]{:S(2)}) %collective-permute-start.9) | collective-permute-done | bytes 204832 | tf_op jit(solution)/shard_map/ppermute | solution.py:471
  33.8 0.5 collective-permute-start.11
  34.6 1.1 %collective-permute-done.19.rest_13_ = bf16[80,1280]{1,0:T(8,128)(2,1)S(1)} collective-permute-done((bf16[80,1280]{1,0:T(8,128)(2,1)}, bf16[80,1280]{1,0:T(8,128)(2,1)S(1)}, u32[]{:S(2)}, u32[]{:S(2)}) %collective-permute-start.19) | collective-permute-done | bytes 204832 | tf_op jit(solution)/shard_map/ppermute | solution.py:468
  35.8 0.7 %collective-permute-start.22 = (bf16[80,2304]{1,0:T(8,128)(2,1)}, bf16[80,2304]{1,0:T(8,128)(2,1)S(1)}, u32[]{:S(2)}, u32[]{:S(2)}) collective-permute-start(bf16[80,2304]{1,0:T(8,128)(2,1)} %collective-permute-done.15.rest_5_), channel_id=1, source_target_pairs={{0,8},{4,12},{8,0},{12,4},{16,24},{20,28},{24,16},{28,20},{1,9},{5... | collective-permute-start | bytes 1105928 | tf_op jit(solution)/shard_map/ppermute | solution.py:474
  36.4 1.5 %collective-permute-start.21 = (bf16[80,2304]{1,0:T(8,128)(2,1)}, bf16[80,2304]{1,0:T(8,128)(2,1)S(1)}, u32[]{:S(2)}, u32[]{:S(2)}) collective-permute-start(bf16[80,2304]{1,0:T(8,128)(2,1)} %collective-permute-done.15.rest_5_), channel_id=1, source_target_pairs={{0,4},{4,0},{8,12},{12,8},{16,20},{20,16},{24,28},{28,24},{1,5},{5... | collective-permute-start | bytes 1105928 | tf_op jit(solution)/shard_map/ppermute | solution.py:474
  38.0 1.3 %collective-permute-start.23 = (bf16[80,2304]{1,0:T(8,128)(2,1)S(1)}, bf16[80,2304]{1,0:T(8,128)(2,1)S(1)}, u32[]{:S(2)}, u32[]{:S(2)}) collective-permute-start(bf16[80,2304]{1,0:T(8,128)(2,1)S(1)} %copy-done.9), channel_id=1, source_target_pairs={{0,2},{1,3},{2,0},{3,1},{4,6},{5,7},{6,4},{7,5},{8,10},{9,11},{10,... | collective-permute-start | bytes 1105928 | tf_op jit(solution)/shard_map/ppermute | solution.py:471
  39.3 9.4 %shard_map.112 = (bf16[1008,640]{1,0:T(8,128)(2,1)S(1)}, bf16[496,1280]{1,0:T(8,128)(2,1)S(1)}) custom-call(s32[2]{0:T(128)S(1)} %pad_add_fusion.1.span, bf16[1008,320]{1,0:T(8,128)(2,1)S(1)} %get-tuple-element.52.hot5, bf16[1008,64]{1,0:T(8,128)(2,1)S(1)} %get-tuple-element.53.hot1, f32[2,640]{1,0:T(2,128)S(1)} %copy-done.6, f32[2,1280]{1,0:T(2,128)S(1)} %copy-done.4, ...), custom_call_target="tpu_custom_call" | custom-call | tf_op jit(solution)/shard_map/pallas_call | solution.py:579
  48.8 0.5 collective-permute-start.26
  49.8 1.6 %shard_map.113.rest_0_ = f32[496,640]{1,0:T(8,128)S(1)} custom-call(bf16[1008,640]{1,0:T(8,128)(2,1)S(1)} %get-tuple-element.65.ci, bf16[2,160,3200]{2,1,0:T(8,128)(2,1)S(1)} %copy-done, bf16[2,160,3200]{2,1,0:T(8,128)(2,1)S(1)} %collective-permute-done.20.near_conv.rest_3_), custom_call_target="tpu_custom_call" | custom-call | tf_op jit(solution)/shard_map/pallas_call | solution.py:599
  51.5 0.5 collective-permute-done.27.rest_12_
  52.0 5.5 %shard_map.114 = bf16[496,1280]{1,0:T(8,128)(2,1)} custom-call(bf16[1008,640]{1,0:T(8,128)(2,1)S(1)} %get-tuple-element.65.ci, bf16[496,1280]{1,0:T(8,128)(2,1)S(1)} %get-tuple-element.66.hid, f32[2,640]{1,0:T(2,128)S(1)} %copy-done.6, f32[496,640]{1,0:T(8,128)S(1)} %shard_map.113.rest_0_, bf16[2,160,3200]{2,1,0:T(8,128)(2,1)S(1)} %copy-done, ...), custom_call_target="tpu_custom_call" | custom-call | tf_op jit(solution)/shard_map/pallas_call | solution.py:609
  (62 shorter events, 2.6 us)
Async XLA Ops:
  0.0 15.2 %copy-start.5 = (f32[2,640]{1,0:T(2,128)S(1)}, f32[2,640]{1,0:T(2,128)}, u32[]{:S(2)}) copy-start(f32[2,640]{1,0:T(2,128)} %gain_mid.1) | copy-start | bytes 15364
  0.0 15.2 %collective-permute-start.5 = (bf16[2,320,640]{2,1,0:T(8,128)(2,1)}, bf16[2,320,640]{2,1,0:T(8,128)(2,1)}, u32[]{:S(2)}, u32[]{:S(2)}) collective-permute-start(bf16[2,320,640]{2,1,0:T(8,128)(2,1)} %rest_2_.2), channel_id=1, source_target_pairs={{0,1},{1,0},{2,3},{3,2},{4,5},{5,4},{6,7},{7,6},{8,9},{9,8},{10,11... | collective-permute-start | bytes 2457608 | tf_op jit(solution)/shard_map/ppermute | solution.py:468
  0.5 14.7 %collective-permute-start.4 = (bf16[2,160,1280]{2,1,0:T(8,128)(2,1)}, bf16[2,160,1280]{2,1,0:T(8,128)(2,1)}, u32[]{:S(2)}, u32[]{:S(2)}) collective-permute-start(bf16[2,160,1280]{2,1,0:T(8,128)(2,1)} %rest_2_.3), channel_id=1, source_target_pairs={{0,1},{1,0},{2,3},{3,2},{4,5},{5,4},{6,7},{7,6},{8,9},{9,8},{10,11... | collective-permute-start | bytes 2457608 | tf_op jit(solution)/shard_map/ppermute | solution.py:468
  0.6 14.6 %copy-start = (bf16[2,160,3200]{2,1,0:T(8,128)(2,1)S(1)}, bf16[2,160,3200]{2,1,0:T(8,128)(2,1)}, u32[]{:S(2)}) copy-start(bf16[2,160,3200]{2,1,0:T(8,128)(2,1)} %rest_1_.3) | copy-start | bytes 6144004
  3.9 3.7 %collective-permute-start.1 = (f32[64,640]{1,0:T(8,128)}, f32[64,640]{1,0:T(8,128)S(1)}, u32[]{:S(2)}, u32[]{:S(2)}) collective-permute-start(f32[64,640]{1,0:T(8,128)} %get-tuple-element.40), channel_id=1, source_target_pairs={{0,1},{1,0},{2,3},{3,2},{4,5},{5,4},{6,7},{7,6},{8,9},{9,8},{10,11... | collective-permute-start | bytes 491528 | tf_op jit(solution)/shard_map/ppermute | solution.py:468
  4.5 3.0 %collective-permute-start = (s32[384]{0:T(512)S(1)}, s32[384]{0:T(512)S(1)}, u32[]{:S(2)}, u32[]{:S(2)}) collective-permute-start(s32[384]{0:T(512)S(1)} %get-tuple-element.82), channel_id=1, source_target_pairs={{0,1},{1,0},{2,3},{3,2},{4,5},{5,4},{6,7},{7,6},{8,9},{9,8},{10,11... | collective-permute-start | bytes 4616 | tf_op jit(solution)/shard_map/ppermute | solution.py:468
  4.6 10.3 %collective-permute-start.6 = (bf16[80,1280]{1,0:T(8,128)(2,1)}, bf16[80,1280]{1,0:T(8,128)(2,1)}, u32[]{:S(2)}, u32[]{:S(2)}) collective-permute-start(bf16[80,1280]{1,0:T(8,128)(2,1)} %get-tuple-element.43), channel_id=1, source_target_pairs={{0,2},{1,3},{2,0},{3,1},{4,6},{5,7},{6,4},{7,5},{8,10},{9,11},{10,... | collective-permute-start | bytes 614408 | tf_op jit(solution)/shard_map/ppermute | solution.py:471
  8.5 6.3 %collective-permute-start.2 = (s32[2,384]{1,0:T(2,128)S(1)}, s32[2,384]{1,0:T(2,128)S(1)}, u32[]{:S(2)}, u32[]{:S(2)}) collective-permute-start(s32[2,384]{1,0:T(2,128)S(1)} %pad_add_fusion), channel_id=1, source_target_pairs={{0,4},{1,29},{2,6},{3,31},{4,8},{5,1},{6,10},{7,3},{8,12},{9,5},{1... | collective-permute-start | bytes 9224 | tf_op jit(solution)/shard_map/ppermute | solution.py:514
  10.7 4.5 %collective-permute-start.3 = (bf16[64,640]{1,0:T(8,128)(2,1)S(1)}, bf16[64,640]{1,0:T(8,128)(2,1)S(1)}, u32[]{:S(2)}, u32[]{:S(2)}) collective-permute-start(bf16[64,640]{1,0:T(8,128)(2,1)S(1)} %get-tuple-element.77), channel_id=1, source_target_pairs={{0,2},{1,3},{2,0},{3,1},{4,6},{5,7},{6,4},{7,5},{8,10},{9,11},{10,... | collective-permute-start | bytes 245768 | tf_op jit(solution)/shard_map/ppermute | solution.py:471
  14.8 12.2 %copy-start.1 = (bf16[2,160,1280]{2,1,0:T(8,128)(2,1)S(1)}, bf16[2,160,1280]{2,1,0:T(8,128)(2,1)}, u32[]{:S(2)}) copy-start(bf16[2,160,1280]{2,1,0:T(8,128)(2,1)} %rest_2_.3) | copy-start | bytes 2457604
  17.1 6.4 %collective-permute-start.7 = (s32[384]{0:T(512)S(1)}, s32[384]{0:T(512)S(1)}, u32[]{:S(2)}, u32[]{:S(2)}) collective-permute-start(s32[384]{0:T(512)S(1)} %get-tuple-element.46), channel_id=1, source_target_pairs={{0,1},{1,0},{2,3},{3,2},{4,5},{5,4},{6,7},{7,6},{8,9},{9,8},{10,11... | collective-permute-start | bytes 4616 | tf_op jit(solution)/shard_map/ppermute | solution.py:468
  18.6 11.8 %collective-permute-start.15 = (bf16[80,2304]{1,0:T(8,128)(2,1)}, bf16[80,2304]{1,0:T(8,128)(2,1)}, u32[]{:S(2)}, u32[]{:S(2)}) collective-permute-start(bf16[80,2304]{1,0:T(8,128)(2,1)} %get-tuple-element.60), channel_id=1, source_target_pairs={{0,2},{1,3},{2,0},{3,1},{4,6},{5,7},{6,4},{7,5},{8,10},{9,11},{10,... | collective-permute-start | bytes 1105928 | tf_op jit(solution)/shard_map/ppermute | solution.py:471
  20.0 10.6 %collective-permute-start.14 = (bf16[80,1280]{1,0:T(8,128)(2,1)}, bf16[80,1280]{1,0:T(8,128)(2,1)}, u32[]{:S(2)}, u32[]{:S(2)}) collective-permute-start(bf16[80,1280]{1,0:T(8,128)(2,1)} %collective-permute-done.6.rest_6_), channel_id=1, source_target_pairs={{0,12},{4,8},{8,4},{12,0},{16,28},{20,24},{24,20},{28,16},{1,13},{... | collective-permute-start | bytes 614408 | tf_op jit(solution)/shard_map/ppermute | solution.py:474
  21.1 10.4 %collective-permute-start.13 = (bf16[80,1280]{1,0:T(8,128)(2,1)}, bf16[80,1280]{1,0:T(8,128)(2,1)}, u32[]{:S(2)}, u32[]{:S(2)}) collective-permute-start(bf16[80,1280]{1,0:T(8,128)(2,1)} %collective-permute-done.6.rest_6_), channel_id=1, source_target_pairs={{0,8},{4,12},{8,0},{12,4},{16,24},{20,28},{24,16},{28,20},{1,9},{5... | collective-permute-start | bytes 614408 | tf_op jit(solution)/shard_map/ppermute | solution.py:474
  21.5 10.8 %collective-permute-start.12 = (bf16[80,1280]{1,0:T(8,128)(2,1)}, bf16[80,1280]{1,0:T(8,128)(2,1)}, u32[]{:S(2)}, u32[]{:S(2)}) collective-permute-start(bf16[80,1280]{1,0:T(8,128)(2,1)} %collective-permute-done.6.rest_6_), channel_id=1, source_target_pairs={{0,4},{4,0},{8,12},{12,8},{16,20},{20,16},{24,28},{28,24},{1,5},{5... | collective-permute-start | bytes 614408 | tf_op jit(solution)/shard_map/ppermute | solution.py:474
  23.5 1.8 %collective-permute-start.8 = (bf16[32,3200]{1,0:T(8,128)(2,1)}, bf16[32,3200]{1,0:T(8,128)(2,1)}, u32[]{:S(2)}, u32[]{:S(2)}) collective-permute-start(bf16[32,3200]{1,0:T(8,128)(2,1)} %get-tuple-element.48), channel_id=1, source_target_pairs={{0,1},{1,0},{2,3},{3,2},{4,5},{5,4},{6,7},{7,6},{8,9},{9,8},{10,11... | collective-permute-start | bytes 614408 | tf_op jit(solution)/shard_map/ppermute | solution.py:468
  26.3 7.5 %collective-permute-start.9 = (bf16[32,3200]{1,0:T(8,128)(2,1)S(1)}, bf16[32,3200]{1,0:T(8,128)(2,1)S(1)}, u32[]{:S(2)}, u32[]{:S(2)}) collective-permute-start(bf16[32,3200]{1,0:T(8,128)(2,1)S(1)} %add_convert_fusion.rest_0_), channel_id=1, source_target_pairs={{0,2},{1,3},{2,0},{3,1},{4,6},{5,7},{6,4},{7,5},{8,10},{9,11},{10,... | collective-permute-start | bytes 614408 | tf_op jit(solution)/shard_map/ppermute | solution.py:471
  27.9 11.4 %copy-start.6 = (f32[2,640]{1,0:T(2,128)S(1)}, f32[2,640]{1,0:T(2,128)}, u32[]{:S(2)}) copy-start(f32[2,640]{1,0:T(2,128)} %gain_out.3) | copy-start | bytes 15364
  30.5 3.3 %collective-permute-start.10 = (bf16[32,3200]{1,0:T(8,128)(2,1)S(1)}, bf16[32,3200]{1,0:T(8,128)(2,1)S(1)}, u32[]{:S(2)}, u32[]{:S(2)}) collective-permute-start(bf16[32,3200]{1,0:T(8,128)(2,1)S(1)} %add_convert_fusion.rest_0_), channel_id=1, source_target_pairs={{0,1},{1,0},{2,3},{3,2},{4,5},{5,4},{6,7},{7,6},{8,9},{9,8},{10,11... | collective-permute-start | bytes 614408 | tf_op jit(solution)/shard_map/ppermute | solution.py:468
  32.3 2.0 %collective-permute-start.16 = (bf16[80,1280]{1,0:T(8,128)(2,1)}, bf16[80,1280]{1,0:T(8,128)(2,1)S(1)}, u32[]{:S(2)}, u32[]{:S(2)}) collective-permute-start(bf16[80,1280]{1,0:T(8,128)(2,1)} %collective-permute-done.6.rest_6_), channel_id=1, source_target_pairs={{0,1},{1,0},{2,3},{3,2},{4,5},{5,4},{6,7},{7,6},{8,9},{9,8},{10,11... | collective-permute-start | bytes 614408 | tf_op jit(solution)/shard_map/ppermute | solution.py:468
  32.3 1.9 %collective-permute-start.17 = (bf16[80,1280]{1,0:T(8,128)(2,1)}, bf16[80,1280]{1,0:T(8,128)(2,1)S(1)}, u32[]{:S(2)}, u32[]{:S(2)}) collective-permute-start(bf16[80,1280]{1,0:T(8,128)(2,1)} %collective-permute-done.12.rest_7_), channel_id=1, source_target_pairs={{0,1},{1,0},{2,3},{3,2},{4,5},{5,4},{6,7},{7,6},{8,9},{9,8},{10,11... | collective-permute-start | bytes 614408 | tf_op jit(solution)/shard_map/ppermute | solution.py:468
  32.8 1.7 %collective-permute-start.18 = (bf16[80,1280]{1,0:T(8,128)(2,1)}, bf16[80,1280]{1,0:T(8,128)(2,1)S(1)}, u32[]{:S(2)}, u32[]{:S(2)}) collective-permute-start(bf16[80,1280]{1,0:T(8,128)(2,1)} %collective-permute-done.13.rest_8_), channel_id=1, source_target_pairs={{0,1},{1,0},{2,3},{3,2},{4,5},{5,4},{6,7},{7,6},{8,9},{9,8},{10,11... | collective-permute-start | bytes 614408 | tf_op jit(solution)/shard_map/ppermute | solution.py:468
  33.8 1.9 %collective-permute-start.19 = (bf16[80,1280]{1,0:T(8,128)(2,1)}, bf16[80,1280]{1,0:T(8,128)(2,1)S(1)}, u32[]{:S(2)}, u32[]{:S(2)}) collective-permute-start(bf16[80,1280]{1,0:T(8,128)(2,1)} %collective-permute-done.14.rest_9_), channel_id=1, source_target_pairs={{0,1},{1,0},{2,3},{3,2},{4,5},{5,4},{6,7},{7,6},{8,9},{9,8},{10,11... | collective-permute-start | bytes 614408 | tf_op jit(solution)/shard_map/ppermute | solution.py:468
  33.8 1.9 %collective-permute-start.11 = (bf16[32,3200]{1,0:T(8,128)(2,1)S(1)}, bf16[32,3200]{1,0:T(8,128)(2,1)S(1)}, u32[]{:S(2)}, u32[]{:S(2)}) collective-permute-start(bf16[32,3200]{1,0:T(8,128)(2,1)S(1)} %collective-permute-done.9.rest_1_), channel_id=1, source_target_pairs={{0,1},{1,0},{2,3},{3,2},{4,5},{5,4},{6,7},{7,6},{8,9},{9,8},{10,11... | collective-permute-start | bytes 614408 | tf_op jit(solution)/shard_map/ppermute | solution.py:468
  35.6 14.2 %collective-permute-start.20 = (bf16[2,160,3200]{2,1,0:T(8,128)(2,1)S(1)}, bf16[2,160,3200]{2,1,0:T(8,128)(2,1)S(1)}, u32[]{:S(2)}, u32[]{:S(2)}) collective-permute-start(bf16[2,160,3200]{2,1,0:T(8,128)(2,1)S(1)} %copy-done), channel_id=1, source_target_pairs={{0,1},{1,0},{2,3},{3,2},{4,5},{5,4},{6,7},{7,6},{8,9},{9,8},{10,11... | collective-permute-start | bytes 6144008 | tf_op jit(solution)/shard_map/ppermute | solution.py:468
  35.8 13.0 %collective-permute-start.22 = (bf16[80,2304]{1,0:T(8,128)(2,1)}, bf16[80,2304]{1,0:T(8,128)(2,1)S(1)}, u32[]{:S(2)}, u32[]{:S(2)}) collective-permute-start(bf16[80,2304]{1,0:T(8,128)(2,1)} %collective-permute-done.15.rest_5_), channel_id=1, source_target_pairs={{0,8},{4,12},{8,0},{12,4},{16,24},{20,28},{24,16},{28,20},{1,9},{5... | collective-permute-start | bytes 1105928 | tf_op jit(solution)/shard_map/ppermute | solution.py:474
  36.4 12.9 %collective-permute-start.21 = (bf16[80,2304]{1,0:T(8,128)(2,1)}, bf16[80,2304]{1,0:T(8,128)(2,1)S(1)}, u32[]{:S(2)}, u32[]{:S(2)}) collective-permute-start(bf16[80,2304]{1,0:T(8,128)(2,1)} %collective-permute-done.15.rest_5_), channel_id=1, source_target_pairs={{0,4},{4,0},{8,12},{12,8},{16,20},{20,16},{24,28},{28,24},{1,5},{5... | collective-permute-start | bytes 1105928 | tf_op jit(solution)/shard_map/ppermute | solution.py:474
  38.0 11.4 %collective-permute-start.23 = (bf16[80,2304]{1,0:T(8,128)(2,1)S(1)}, bf16[80,2304]{1,0:T(8,128)(2,1)S(1)}, u32[]{:S(2)}, u32[]{:S(2)}) collective-permute-start(bf16[80,2304]{1,0:T(8,128)(2,1)S(1)} %copy-done.9), channel_id=1, source_target_pairs={{0,2},{1,3},{2,0},{3,1},{4,6},{5,7},{6,4},{7,5},{8,10},{9,11},{10,... | collective-permute-start | bytes 1105928 | tf_op jit(solution)/shard_map/ppermute | solution.py:471
  48.7 2.7 %collective-permute-start.24 = (bf16[80,2304]{1,0:T(8,128)(2,1)}, bf16[80,2304]{1,0:T(8,128)(2,1)S(1)}, u32[]{:S(2)}, u32[]{:S(2)}) collective-permute-start(bf16[80,2304]{1,0:T(8,128)(2,1)} %collective-permute-done.15.rest_5_), channel_id=1, source_target_pairs={{0,1},{1,0},{2,3},{3,2},{4,5},{5,4},{6,7},{7,6},{8,9},{9,8},{10,11... | collective-permute-start | bytes 1105928 | tf_op jit(solution)/shard_map/ppermute | solution.py:468
  48.8 2.6 %collective-permute-start.26 = (bf16[80,2304]{1,0:T(8,128)(2,1)S(1)}, bf16[80,2304]{1,0:T(8,128)(2,1)S(1)}, u32[]{:S(2)}, u32[]{:S(2)}) collective-permute-start(bf16[80,2304]{1,0:T(8,128)(2,1)S(1)} %collective-permute-done.22.rest_7_), channel_id=1, source_target_pairs={{0,1},{1,0},{2,3},{3,2},{4,5},{5,4},{6,7},{7,6},{8,9},{9,8},{10,11... | collective-permute-start | bytes 1105928 | tf_op jit(solution)/shard_map/ppermute | solution.py:468
  49.3 2.2 %collective-permute-start.25 = (bf16[80,2304]{1,0:T(8,128)(2,1)S(1)}, bf16[80,2304]{1,0:T(8,128)(2,1)S(1)}, u32[]{:S(2)}, u32[]{:S(2)}) collective-permute-start(bf16[80,2304]{1,0:T(8,128)(2,1)S(1)} %collective-permute-done.21.rest_6_), channel_id=1, source_target_pairs={{0,1},{1,0},{2,3},{3,2},{4,5},{5,4},{6,7},{7,6},{8,9},{9,8},{10,11... | collective-permute-start | bytes 1105928 | tf_op jit(solution)/shard_map/ppermute | solution.py:468
  49.4 2.7 %collective-permute-start.27 = (bf16[80,2304]{1,0:T(8,128)(2,1)S(1)}, bf16[80,2304]{1,0:T(8,128)(2,1)S(1)}, u32[]{:S(2)}, u32[]{:S(2)}) collective-permute-start(bf16[80,2304]{1,0:T(8,128)(2,1)S(1)} %collective-permute-done.23.rest_8_), channel_id=1, source_target_pairs={{0,1},{1,0},{2,3},{3,2},{4,5},{5,4},{6,7},{7,6},{8,9},{9,8},{10,11... | collective-permute-start | bytes 1105928 | tf_op jit(solution)/shard_map/ppermute | solution.py:468
  (6 other events, 34.4 us)

commit v18 on v17

--- a/solution.py
+++ b/solution.py
@@ -539,7 +539,7 @@
         before, behind = jnp.where(low, moved[0], came), jnp.where(low, came, moved[0])
         relay = after(far_a, taps[2])
         parts_a = [far_a] + [seq_swap(relay, b) for b in (1, 2, 3)]
-        sent = (taps[0] + after(core_swap(taps[1]), before, behind).astype(F32)).astype(BF)
+        sent = (taps[0] + core_swap(taps[1]).astype(F32)).astype(BF)
         received = x_swap(sent)
     spare = jnp.zeros((-(rows + 2 * REACH) % 128,), jnp.int32)
     near = jnp.concatenate([before, codes, behind, spare])[None]

time: 57.9 us -> 57.9 us (level)
  no operation moved by 1% of the time
where the time goes in v18:
time: 57.9 us; the launch traced here: 57.7 us
  Pallas kernels  24.1 us (42%)
  starting transfers between devices  19.6 us (34%)
  waiting for transfers between devices  9.86 us (17%)
  other arithmetic  2.1 us (4%)
  local copies, waits for them, and re-layouts  1.06 us (2%)
  between operations  1 us (2%)
    pallas_call x1, Pallas kernels, per_device(): pl.pallas_call(functools.partial(rows_kernel, split), out_shape=(jax.Shap...  9.42 us
    ppermute x5, starting transfers between devices, x_swap(): return lax.ppermute(x, 'roll', [(i, i ^ 2) for i in range(rolls)])  7.32 us
    ppermute x5, starting transfers between devices, seq_swap(): return lax.ppermute(x, 'seq', [(i, i ^ bits) for i in range(seqs)])  5.66 us
    pallas_call x1, Pallas kernels, per_device(): pl.pallas_call(functools.partial(last_kernel, split), out_shape=jax.Shape...  5.46 us
    ppermute x17, starting transfers between devices, core_swap(): return lax.ppermute(x, 'roll', [(i, i ^ 1) for i in range(rolls)])  5.02 us
    ppermute x17, waiting for transfers between devices, core_swap(): return lax.ppermute(x, 'roll', [(i, i ^ 1) for i in range(rolls)])  3.72 us
    pallas_call x1, Pallas kernels, per_device(): pl.pallas_call(functools.partial(first_kernel, split), out_shape=[jax.Sha...  3.24 us
    ppermute x1, waiting for transfers between devices, per_device(): moved = lax.ppermute(after(pack, own), ('seq', 'roll'), moves)  3.13 us
  transfers between devices with their start and end apart: 28, of which 10 were waited for; matrix products, arithmetic and copies ran while one was open for 4% of the time, Pallas kernels for 29%

profile of v18, /device:TPU:0, one launch (start us, length us, event | category | flops | bytes accessed | tf_op | source)
XLA Modules:
  0.0 57.7 jit_solution(17817587707721085180)
XLA Ops:
  0.0 0.5 collective-permute-start.5
  0.6 3.2 %shard_map.109 = (bf16[64,1280]{1,0:T(8,128)(2,1)}, f32[64,640]{1,0:T(8,128)}, bf16[80,1280]{1,0:T(8,128)(2,1)}, bf16[80,2304]{1,0:T(8,128)(2,1)}, bf16[80,2304]{1,0:T(8,128)(2,1)}) custom-call(f32[30,1280]{1,0:T(8,128)} %embed.1, f32[1280]{0:T(1024)} %brk.1, f32[2,1280]{1,0:T(2,128)} %gain_in.1, bf16[2,320,640]{2,1,0:T(8,128)(2,1)} %rest_2_.2, ...), custom_call_target="tpu_custom_call" | custom-call | tf_op jit(solution)/shard_map/pallas_call | solution.py:484
  3.9 0.5 collective-permute-start.1
  4.6 2.9 %collective-permute-start.6 = (bf16[80,1280]{1,0:T(8,128)(2,1)}, bf16[80,1280]{1,0:T(8,128)(2,1)}, u32[]{:S(2)}, u32[]{:S(2)}) collective-permute-start(bf16[80,1280]{1,0:T(8,128)(2,1)} %get-tuple-element.42), channel_id=1, source_target_pairs={{0,2},{1,3},{2,0},{3,1},{4,6},{5,7},{6,4},{7,5},{8,10},{9,11},{10,... | collective-permute-start | bytes 614408 | tf_op jit(solution)/shard_map/ppermute | solution.py:471
  7.5 1.0 %fusion.1 = (bf16[64,640]{1,0:T(8,128)(2,1)S(1)}, f32[64,640]{1,0:T(8,128)S(1)}) fusion(f32[64,640]{1,0:T(8,128)} %get-tuple-element.39, f32[64,640]{1,0:T(8,128)S(1)} %collective-permute-done.1), kind=kLoop, calls=%fused_computation.11 | loop fusion | flops 81920 | bytes 573440 | tf_op jit(solution)/shard_map/convert_element_type | solution.py:509
  8.5 1.6 %collective-permute-start.2 = (s32[2,384]{1,0:T(2,128)S(1)}, s32[2,384]{1,0:T(2,128)S(1)}, u32[]{:S(2)}, u32[]{:S(2)}) collective-permute-start(s32[2,384]{1,0:T(2,128)S(1)} %pad_add_fusion), channel_id=1, source_target_pairs={{0,4},{1,29},{2,6},{3,31},{4,8},{5,1},{6,10},{7,3},{8,12},{9,5},{1... | collective-permute-start | bytes 9224 | tf_op jit(solution)/shard_map/ppermute | solution.py:514
  10.7 1.0 %collective-permute-start.3 = (bf16[64,640]{1,0:T(8,128)(2,1)S(1)}, bf16[64,640]{1,0:T(8,128)(2,1)S(1)}, u32[]{:S(2)}, u32[]{:S(2)}) collective-permute-start(bf16[64,640]{1,0:T(8,128)(2,1)S(1)} %get-tuple-element.75), channel_id=1, source_target_pairs={{0,2},{1,3},{2,0},{3,1},{4,6},{5,7},{6,4},{7,5},{8,10},{9,11},{10,... | collective-permute-start | bytes 245768 | tf_op jit(solution)/shard_map/ppermute | solution.py:471
  11.7 3.1 %collective-permute-done.2 = s32[2,384]{1,0:T(2,128)S(1)} collective-permute-done((s32[2,384]{1,0:T(2,128)S(1)}, s32[2,384]{1,0:T(2,128)S(1)}, u32[]{:S(2)}, u32[]{:S(2)}) %collective-permute-start.2) | collective-permute-done | bytes 3104 | tf_op jit(solution)/shard_map/ppermute | solution.py:514
  15.2 1.8 %shard_map.110 = (f32[32,3200]{1,0:T(8,128)S(1)}, bf16[32,3200]{1,0:T(8,128)(2,1)}, f32[1,128]{1,0:T(1,128)}) custom-call(f32[64,640]{1,0:T(8,128)S(1)} %get-tuple-element.76.own, bf16[64,640]{1,0:T(8,128)(2,1)S(1)} %collective-permute-done.3.other, f32[2,640]{1,0:T(2,128)S(1)} %copy-done.5, bf16[2,160,3200]{2,1,0:T(8,128)(2,1)S(1)} %copy-done), custom_call_target="tpu_custom_call" | custom-call | tf_op jit(solution)/shard_map/pallas_call | solution.py:524
  17.1 1.5 %collective-permute-start.7 = (s32[384]{0:T(512)S(1)}, s32[384]{0:T(512)S(1)}, u32[]{:S(2)}, u32[]{:S(2)}) collective-permute-start(s32[384]{0:T(512)S(1)} %get-tuple-element.45), channel_id=1, source_target_pairs={{0,1},{1,0},{2,3},{3,2},{4,5},{5,4},{6,7},{7,6},{8,9},{9,8},{10,11... | collective-permute-start | bytes 4616 | tf_op jit(solution)/shard_map/ppermute | solution.py:468
  18.6 1.4 %collective-permute-start.15 = (bf16[80,2304]{1,0:T(8,128)(2,1)}, bf16[80,2304]{1,0:T(8,128)(2,1)}, u32[]{:S(2)}, u32[]{:S(2)}) collective-permute-start(bf16[80,2304]{1,0:T(8,128)(2,1)} %get-tuple-element.58), channel_id=1, source_target_pairs={{0,2},{1,3},{2,0},{3,1},{4,6},{5,7},{6,4},{7,5},{8,10},{9,11},{10,... | collective-permute-start | bytes 1105928 | tf_op jit(solution)/shard_map/ppermute | solution.py:471
  20.0 1.1 %collective-permute-start.14 = (bf16[80,1280]{1,0:T(8,128)(2,1)}, bf16[80,1280]{1,0:T(8,128)(2,1)}, u32[]{:S(2)}, u32[]{:S(2)}) collective-permute-start(bf16[80,1280]{1,0:T(8,128)(2,1)} %collective-permute-done.6.rest_6_), channel_id=1, source_target_pairs={{0,12},{4,8},{8,4},{12,0},{16,28},{20,24},{24,20},{28,16},{1,13},{... | collective-permute-start | bytes 614408 | tf_op jit(solution)/shard_map/ppermute | solution.py:474
  21.5 1.9 %collective-permute-start.12 = (bf16[80,1280]{1,0:T(8,128)(2,1)}, bf16[80,1280]{1,0:T(8,128)(2,1)}, u32[]{:S(2)}, u32[]{:S(2)}) collective-permute-start(bf16[80,1280]{1,0:T(8,128)(2,1)} %collective-permute-done.6.rest_6_), channel_id=1, source_target_pairs={{0,4},{4,0},{8,12},{12,8},{16,20},{20,16},{24,28},{28,24},{1,5},{5... | collective-permute-start | bytes 614408 | tf_op jit(solution)/shard_map/ppermute | solution.py:474
  23.6 1.7 %collective-permute-done.8 = bf16[32,3200]{1,0:T(8,128)(2,1)} collective-permute-done((bf16[32,3200]{1,0:T(8,128)(2,1)}, bf16[32,3200]{1,0:T(8,128)(2,1)}, u32[]{:S(2)}, u32[]{:S(2)}) %collective-permute-start.8) | collective-permute-done | bytes 204832 | tf_op jit(solution)/shard_map/ppermute | solution.py:468
  25.3 1.0 %add_convert_fusion.rest_0_ = bf16[32,3200]{1,0:T(8,128)(2,1)S(1)} fusion(f32[32,3200]{1,0:T(8,128)S(1)} %get-tuple-element.46, bf16[32,3200]{1,0:T(8,128)(2,1)} %collective-permute-done.8), kind=kLoop, calls=%fused_computation | loop fusion | flops 307200 | bytes 819200 | tf_op jit(solution)/shard_map/convert_element_type | solution.py:542
  26.3 0.7 %collective-permute-start.9 = (bf16[32,3200]{1,0:T(8,128)(2,1)S(1)}, bf16[32,3200]{1,0:T(8,128)(2,1)S(1)}, u32[]{:S(2)}, u32[]{:S(2)}) collective-permute-start(bf16[32,3200]{1,0:T(8,128)(2,1)S(1)} %add_convert_fusion.rest_0_), channel_id=1, source_target_pairs={{0,2},{1,3},{2,0},{3,1},{4,6},{5,7},{6,4},{7,5},{8,10},{9,11},{10,... | collective-permute-start | bytes 614408 | tf_op jit(solution)/shard_map/ppermute | solution.py:471
  27.0 0.9 %copy-done.3 = bf16[64,1280]{1,0:T(8,128)(2,1)S(1)} copy-done((bf16[64,1280]{1,0:T(8,128)(2,1)S(1)}, bf16[64,1280]{1,0:T(8,128)(2,1)}, u32[]{:S(2)}) %copy-start.3) | copy-done | bytes 163864
  27.9 2.5 %shard_map.111 = (bf16[1008,320]{1,0:T(8,128)(2,1)S(1)}, bf16[1008,64]{1,0:T(8,128)(2,1)S(1)}, bf16[384,1280]{1,0:T(8,128)(2,1)S(1)}, bf16[640,640]{1,0:T(8,128)(2,1)S(1)}) custom-call(s32[2]{0:T(128)S(1)} %pad_add_fusion.1.span, s32[1,1280]{1,0:T(1,128)S(1)} %broadcast_in_dim.6.near, bf16[64,1280]{1,0:T(8,128)(2,1)S(1)} %copy-done.3, ...), custom_call_target="tpu_custom_call" | custom-call | tf_op jit(solution)/shard_map/pallas_call | solution.py:555
  30.6 0.9 %collective-permute-done.13.rest_8_ = bf16[80,1280]{1,0:T(8,128)(2,1)} collective-permute-done((bf16[80,1280]{1,0:T(8,128)(2,1)}, bf16[80,1280]{1,0:T(8,128)(2,1)}, u32[]{:S(2)}, u32[]{:S(2)}) %collective-permute-start.13) | collective-permute-done | bytes 204832 | tf_op jit(solution)/shard_map/ppermute | solution.py:474
  31.5 0.9 %collective-permute-done.12.rest_7_ = bf16[80,1280]{1,0:T(8,128)(2,1)} collective-permute-done((bf16[80,1280]{1,0:T(8,128)(2,1)}, bf16[80,1280]{1,0:T(8,128)(2,1)}, u32[]{:S(2)}, u32[]{:S(2)}) %collective-permute-start.12) | collective-permute-done | bytes 204832 | tf_op jit(solution)/shard_map/ppermute | solution.py:474
  32.3 0.5 collective-permute-start.17
  32.9 0.9 %collective-permute-done.9.rest_1_ = bf16[32,3200]{1,0:T(8,128)(2,1)S(1)} collective-permute-done((bf16[32,3200]{1,0:T(8,128)(2,1)S(1)}, bf16[32,3200]{1,0:T(8,128)(2,1)S(1)}, u32[]{:S(2)}, u32[]{:S(2)}) %collective-permute-start.9) | collective-permute-done | bytes 204832 | tf_op jit(solution)/shard_map/ppermute | solution.py:471
  33.8 0.5 collective-permute-start.11
  34.6 1.1 %collective-permute-done.19.rest_13_ = bf16[80,1280]{1,0:T(8,128)(2,1)S(1)} collective-permute-done((bf16[80,1280]{1,0:T(8,128)(2,1)}, bf16[80,1280]{1,0:T(8,128)(2,1)S(1)}, u32[]{:S(2)}, u32[]{:S(2)}) %collective-permute-start.19) | collective-permute-done | bytes 204832 | tf_op jit(solution)/shard_map/ppermute | solution.py:468
  35.8 0.7 %collective-permute-start.22 = (bf16[80,2304]{1,0:T(8,128)(2,1)}, bf16[80,2304]{1,0:T(8,128)(2,1)S(1)}, u32[]{:S(2)}, u32[]{:S(2)}) collective-permute-start(bf16[80,2304]{1,0:T(8,128)(2,1)} %collective-permute-done.15.rest_5_), channel_id=1, source_target_pairs={{0,8},{4,12},{8,0},{12,4},{16,24},{20,28},{24,16},{28,20},{1,9},{5... | collective-permute-start | bytes 1105928 | tf_op jit(solution)/shard_map/ppermute | solution.py:474
  36.4 1.5 %collective-permute-start.21 = (bf16[80,2304]{1,0:T(8,128)(2,1)}, bf16[80,2304]{1,0:T(8,128)(2,1)S(1)}, u32[]{:S(2)}, u32[]{:S(2)}) collective-permute-start(bf16[80,2304]{1,0:T(8,128)(2,1)} %collective-permute-done.15.rest_5_), channel_id=1, source_target_pairs={{0,4},{4,0},{8,12},{12,8},{16,20},{20,16},{24,28},{28,24},{1,5},{5... | collective-permute-start | bytes 1105928 | tf_op jit(solution)/shard_map/ppermute | solution.py:474
  38.0 1.3 %collective-permute-start.23 = (bf16[80,2304]{1,0:T(8,128)(2,1)S(1)}, bf16[80,2304]{1,0:T(8,128)(2,1)S(1)}, u32[]{:S(2)}, u32[]{:S(2)}) collective-permute-start(bf16[80,2304]{1,0:T(8,128)(2,1)S(1)} %copy-done.9), channel_id=1, source_target_pairs={{0,2},{1,3},{2,0},{3,1},{4,6},{5,7},{6,4},{7,5},{8,10},{9,11},{10,... | collective-permute-start | bytes 1105928 | tf_op jit(solution)/shard_map/ppermute | solution.py:471
  39.3 9.4 %shard_map.112 = (bf16[1008,640]{1,0:T(8,128)(2,1)S(1)}, bf16[496,1280]{1,0:T(8,128)(2,1)S(1)}) custom-call(s32[2]{0:T(128)S(1)} %pad_add_fusion.1.span, bf16[1008,320]{1,0:T(8,128)(2,1)S(1)} %get-tuple-element.50.hot5, bf16[1008,64]{1,0:T(8,128)(2,1)S(1)} %get-tuple-element.51.hot1, f32[2,640]{1,0:T(2,128)S(1)} %copy-done.6, f32[2,1280]{1,0:T(2,128)S(1)} %copy-done.4, ...), custom_call_target="tpu_custom_call" | custom-call | tf_op jit(solution)/shard_map/pallas_call | solution.py:579
  48.8 0.5 collective-permute-start.26
  49.8 1.6 %shard_map.113.rest_0_ = f32[496,640]{1,0:T(8,128)S(1)} custom-call(bf16[1008,640]{1,0:T(8,128)(2,1)S(1)} %get-tuple-element.63.ci, bf16[2,160,3200]{2,1,0:T(8,128)(2,1)S(1)} %copy-done, bf16[2,160,3200]{2,1,0:T(8,128)(2,1)S(1)} %collective-permute-done.20.near_conv.rest_3_), custom_call_target="tpu_custom_call" | custom-call | tf_op jit(solution)/shard_map/pallas_call | solution.py:599
  51.5 0.5 collective-permute-done.27.rest_12_
  52.0 5.5 %shard_map.114 = bf16[496,1280]{1,0:T(8,128)(2,1)} custom-call(bf16[1008,640]{1,0:T(8,128)(2,1)S(1)} %get-tuple-element.63.ci, bf16[496,1280]{1,0:T(8,128)(2,1)S(1)} %get-tuple-element.64.hid, f32[2,640]{1,0:T(2,128)S(1)} %copy-done.6, f32[496,640]{1,0:T(8,128)S(1)} %shard_map.113.rest_0_, bf16[2,160,3200]{2,1,0:T(8,128)(2,1)S(1)} %copy-done, ...), custom_call_target="tpu_custom_call" | custom-call | tf_op jit(solution)/shard_map/pallas_call | solution.py:609
  (62 shorter events, 2.6 us)
Async XLA Ops:
  0.0 15.2 %copy-start.5 = (f32[2,640]{1,0:T(2,128)S(1)}, f32[2,640]{1,0:T(2,128)}, u32[]{:S(2)}) copy-start(f32[2,640]{1,0:T(2,128)} %gain_mid.1) | copy-start | bytes 15364
  0.0 15.2 %collective-permute-start.5 = (bf16[2,320,640]{2,1,0:T(8,128)(2,1)}, bf16[2,320,640]{2,1,0:T(8,128)(2,1)}, u32[]{:S(2)}, u32[]{:S(2)}) collective-permute-start(bf16[2,320,640]{2,1,0:T(8,128)(2,1)} %rest_2_.2), channel_id=1, source_target_pairs={{0,1},{1,0},{2,3},{3,2},{4,5},{5,4},{6,7},{7,6},{8,9},{9,8},{10,11... | collective-permute-start | bytes 2457608 | tf_op jit(solution)/shard_map/ppermute | solution.py:468
  0.5 14.7 %collective-permute-start.4 = (bf16[2,160,1280]{2,1,0:T(8,128)(2,1)}, bf16[2,160,1280]{2,1,0:T(8,128)(2,1)}, u32[]{:S(2)}, u32[]{:S(2)}) collective-permute-start(bf16[2,160,1280]{2,1,0:T(8,128)(2,1)} %rest_2_.3), channel_id=1, source_target_pairs={{0,1},{1,0},{2,3},{3,2},{4,5},{5,4},{6,7},{7,6},{8,9},{9,8},{10,11... | collective-permute-start | bytes 2457608 | tf_op jit(solution)/shard_map/ppermute | solution.py:468
  0.6 14.6 %copy-start = (bf16[2,160,3200]{2,1,0:T(8,128)(2,1)S(1)}, bf16[2,160,3200]{2,1,0:T(8,128)(2,1)}, u32[]{:S(2)}) copy-start(bf16[2,160,3200]{2,1,0:T(8,128)(2,1)} %rest_1_.3) | copy-start | bytes 6144004
  3.9 3.7 %collective-permute-start.1 = (f32[64,640]{1,0:T(8,128)}, f32[64,640]{1,0:T(8,128)S(1)}, u32[]{:S(2)}, u32[]{:S(2)}) collective-permute-start(f32[64,640]{1,0:T(8,128)} %get-tuple-element.39), channel_id=1, source_target_pairs={{0,1},{1,0},{2,3},{3,2},{4,5},{5,4},{6,7},{7,6},{8,9},{9,8},{10,11... | collective-permute-start | bytes 491528 | tf_op jit(solution)/shard_map/ppermute | solution.py:468
  4.5 3.0 %collective-permute-start = (s32[384]{0:T(512)S(1)}, s32[384]{0:T(512)S(1)}, u32[]{:S(2)}, u32[]{:S(2)}) collective-permute-start(s32[384]{0:T(512)S(1)} %get-tuple-element.80), channel_id=1, source_target_pairs={{0,1},{1,0},{2,3},{3,2},{4,5},{5,4},{6,7},{7,6},{8,9},{9,8},{10,11... | collective-permute-start | bytes 4616 | tf_op jit(solution)/shard_map/ppermute | solution.py:468
  4.6 10.3 %collective-permute-start.6 = (bf16[80,1280]{1,0:T(8,128)(2,1)}, bf16[80,1280]{1,0:T(8,128)(2,1)}, u32[]{:S(2)}, u32[]{:S(2)}) collective-permute-start(bf16[80,1280]{1,0:T(8,128)(2,1)} %get-tuple-element.42), channel_id=1, source_target_pairs={{0,2},{1,3},{2,0},{3,1},{4,6},{5,7},{6,4},{7,5},{8,10},{9,11},{10,... | collective-permute-start | bytes 614408 | tf_op jit(solution)/shard_map/ppermute | solution.py:471
  8.5 6.3 %collective-permute-start.2 = (s32[2,384]{1,0:T(2,128)S(1)}, s32[2,384]{1,0:T(2,128)S(1)}, u32[]{:S(2)}, u32[]{:S(2)}) collective-permute-start(s32[2,384]{1,0:T(2,128)S(1)} %pad_add_fusion), channel_id=1, source_target_pairs={{0,4},{1,29},{2,6},{3,31},{4,8},{5,1},{6,10},{7,3},{8,12},{9,5},{1... | collective-permute-start | bytes 9224 | tf_op jit(solution)/shard_map/ppermute | solution.py:514
  10.7 4.5 %collective-permute-start.3 = (bf16[64,640]{1,0:T(8,128)(2,1)S(1)}, bf16[64,640]{1,0:T(8,128)(2,1)S(1)}, u32[]{:S(2)}, u32[]{:S(2)}) collective-permute-start(bf16[64,640]{1,0:T(8,128)(2,1)S(1)} %get-tuple-element.75), channel_id=1, source_target_pairs={{0,2},{1,3},{2,0},{3,1},{4,6},{5,7},{6,4},{7,5},{8,10},{9,11},{10,... | collective-permute-start | bytes 245768 | tf_op jit(solution)/shard_map/ppermute | solution.py:471
  14.8 12.2 %copy-start.1 = (bf16[2,160,1280]{2,1,0:T(8,128)(2,1)S(1)}, bf16[2,160,1280]{2,1,0:T(8,128)(2,1)}, u32[]{:S(2)}) copy-start(bf16[2,160,1280]{2,1,0:T(8,128)(2,1)} %rest_2_.3) | copy-start | bytes 2457604
  17.1 6.4 %collective-permute-start.7 = (s32[384]{0:T(512)S(1)}, s32[384]{0:T(512)S(1)}, u32[]{:S(2)}, u32[]{:S(2)}) collective-permute-start(s32[384]{0:T(512)S(1)} %get-tuple-element.45), channel_id=1, source_target_pairs={{0,1},{1,0},{2,3},{3,2},{4,5},{5,4},{6,7},{7,6},{8,9},{9,8},{10,11... | collective-permute-start | bytes 4616 | tf_op jit(solution)/shard_map/ppermute | solution.py:468
  18.6 11.8 %collective-permute-start.15 = (bf16[80,2304]{1,0:T(8,128)(2,1)}, bf16[80,2304]{1,0:T(8,128)(2,1)}, u32[]{:S(2)}, u32[]{:S(2)}) collective-permute-start(bf16[80,2304]{1,0:T(8,128)(2,1)} %get-tuple-element.58), channel_id=1, source_target_pairs={{0,2},{1,3},{2,0},{3,1},{4,6},{5,7},{6,4},{7,5},{8,10},{9,11},{10,... | collective-permute-start | bytes 1105928 | tf_op jit(solution)/shard_map/ppermute | solution.py:471
  20.0 10.6 %collective-permute-start.14 = (bf16[80,1280]{1,0:T(8,128)(2,1)}, bf16[80,1280]{1,0:T(8,128)(2,1)}, u32[]{:S(2)}, u32[]{:S(2)}) collective-permute-start(bf16[80,1280]{1,0:T(8,128)(2,1)} %collective-permute-done.6.rest_6_), channel_id=1, source_target_pairs={{0,12},{4,8},{8,4},{12,0},{16,28},{20,24},{24,20},{28,16},{1,13},{... | collective-permute-start | bytes 614408 | tf_op jit(solution)/shard_map/ppermute | solution.py:474
  21.1 10.4 %collective-permute-start.13 = (bf16[80,1280]{1,0:T(8,128)(2,1)}, bf16[80,1280]{1,0:T(8,128)(2,1)}, u32[]{:S(2)}, u32[]{:S(2)}) collective-permute-start(bf16[80,1280]{1,0:T(8,128)(2,1)} %collective-permute-done.6.rest_6_), channel_id=1, source_target_pairs={{0,8},{4,12},{8,0},{12,4},{16,24},{20,28},{24,16},{28,20},{1,9},{5... | collective-permute-start | bytes 614408 | tf_op jit(solution)/shard_map/ppermute | solution.py:474
  21.5 10.8 %collective-permute-start.12 = (bf16[80,1280]{1,0:T(8,128)(2,1)}, bf16[80,1280]{1,0:T(8,128)(2,1)}, u32[]{:S(2)}, u32[]{:S(2)}) collective-permute-start(bf16[80,1280]{1,0:T(8,128)(2,1)} %collective-permute-done.6.rest_6_), channel_id=1, source_target_pairs={{0,4},{4,0},{8,12},{12,8},{16,20},{20,16},{24,28},{28,24},{1,5},{5... | collective-permute-start | bytes 614408 | tf_op jit(solution)/shard_map/ppermute | solution.py:474
  23.5 1.8 %collective-permute-start.8 = (bf16[32,3200]{1,0:T(8,128)(2,1)}, bf16[32,3200]{1,0:T(8,128)(2,1)}, u32[]{:S(2)}, u32[]{:S(2)}) collective-permute-start(bf16[32,3200]{1,0:T(8,128)(2,1)} %get-tuple-element.47), channel_id=1, source_target_pairs={{0,1},{1,0},{2,3},{3,2},{4,5},{5,4},{6,7},{7,6},{8,9},{9,8},{10,11... | collective-permute-start | bytes 614408 | tf_op jit(solution)/shard_map/ppermute | solution.py:468
  26.3 7.5 %collective-permute-start.9 = (bf16[32,3200]{1,0:T(8,128)(2,1)S(1)}, bf16[32,3200]{1,0:T(8,128)(2,1)S(1)}, u32[]{:S(2)}, u32[]{:S(2)}) collective-permute-start(bf16[32,3200]{1,0:T(8,128)(2,1)S(1)} %add_convert_fusion.rest_0_), channel_id=1, source_target_pairs={{0,2},{1,3},{2,0},{3,1},{4,6},{5,7},{6,4},{7,5},{8,10},{9,11},{10,... | collective-permute-start | bytes 614408 | tf_op jit(solution)/shard_map/ppermute | solution.py:471
  27.9 11.4 %copy-start.6 = (f32[2,640]{1,0:T(2,128)S(1)}, f32[2,640]{1,0:T(2,128)}, u32[]{:S(2)}) copy-start(f32[2,640]{1,0:T(2,128)} %gain_out.3) | copy-start | bytes 15364
  30.5 3.3 %collective-permute-start.10 = (bf16[32,3200]{1,0:T(8,128)(2,1)S(1)}, bf16[32,3200]{1,0:T(8,128)(2,1)S(1)}, u32[]{:S(2)}, u32[]{:S(2)}) collective-permute-start(bf16[32,3200]{1,0:T(8,128)(2,1)S(1)} %add_convert_fusion.rest_0_), channel_id=1, source_target_pairs={{0,1},{1,0},{2,3},{3,2},{4,5},{5,4},{6,7},{7,6},{8,9},{9,8},{10,11... | collective-permute-start | bytes 614408 | tf_op jit(solution)/shard_map/ppermute | solution.py:468
  32.3 2.0 %collective-permute-start.16 = (bf16[80,1280]{1,0:T(8,128)(2,1)}, bf16[80,1280]{1,0:T(8,128)(2,1)S(1)}, u32[]{:S(2)}, u32[]{:S(2)}) collective-permute-start(bf16[80,1280]{1,0:T(8,128)(2,1)} %collective-permute-done.6.rest_6_), channel_id=1, source_target_pairs={{0,1},{1,0},{2,3},{3,2},{4,5},{5,4},{6,7},{7,6},{8,9},{9,8},{10,11... | collective-permute-start | bytes 614408 | tf_op jit(solution)/shard_map/ppermute | solution.py:468
  32.3 1.9 %collective-permute-start.17 = (bf16[80,1280]{1,0:T(8,128)(2,1)}, bf16[80,1280]{1,0:T(8,128)(2,1)S(1)}, u32[]{:S(2)}, u32[]{:S(2)}) collective-permute-start(bf16[80,1280]{1,0:T(8,128)(2,1)} %collective-permute-done.12.rest_7_), channel_id=1, source_target_pairs={{0,1},{1,0},{2,3},{3,2},{4,5},{5,4},{6,7},{7,6},{8,9},{9,8},{10,11... | collective-permute-start | bytes 614408 | tf_op jit(solution)/shard_map/ppermute | solution.py:468
  32.8 1.7 %collective-permute-start.18 = (bf16[80,1280]{1,0:T(8,128)(2,1)}, bf16[80,1280]{1,0:T(8,128)(2,1)S(1)}, u32[]{:S(2)}, u32[]{:S(2)}) collective-permute-start(bf16[80,1280]{1,0:T(8,128)(2,1)} %collective-permute-done.13.rest_8_), channel_id=1, source_target_pairs={{0,1},{1,0},{2,3},{3,2},{4,5},{5,4},{6,7},{7,6},{8,9},{9,8},{10,11... | collective-permute-start | bytes 614408 | tf_op jit(solution)/shard_map/ppermute | solution.py:468
  33.8 1.9 %collective-permute-start.19 = (bf16[80,1280]{1,0:T(8,128)(2,1)}, bf16[80,1280]{1,0:T(8,128)(2,1)S(1)}, u32[]{:S(2)}, u32[]{:S(2)}) collective-permute-start(bf16[80,1280]{1,0:T(8,128)(2,1)} %collective-permute-done.14.rest_9_), channel_id=1, source_target_pairs={{0,1},{1,0},{2,3},{3,2},{4,5},{5,4},{6,7},{7,6},{8,9},{9,8},{10,11... | collective-permute-start | bytes 614408 | tf_op jit(solution)/shard_map/ppermute | solution.py:468
  33.8 1.9 %collective-permute-start.11 = (bf16[32,3200]{1,0:T(8,128)(2,1)S(1)}, bf16[32,3200]{1,0:T(8,128)(2,1)S(1)}, u32[]{:S(2)}, u32[]{:S(2)}) collective-permute-start(bf16[32,3200]{1,0:T(8,128)(2,1)S(1)} %collective-permute-done.9.rest_1_), channel_id=1, source_target_pairs={{0,1},{1,0},{2,3},{3,2},{4,5},{5,4},{6,7},{7,6},{8,9},{9,8},{10,11... | collective-permute-start | bytes 614408 | tf_op jit(solution)/shard_map/ppermute | solution.py:468
  35.6 14.2 %collective-permute-start.20 = (bf16[2,160,3200]{2,1,0:T(8,128)(2,1)S(1)}, bf16[2,160,3200]{2,1,0:T(8,128)(2,1)S(1)}, u32[]{:S(2)}, u32[]{:S(2)}) collective-permute-start(bf16[2,160,3200]{2,1,0:T(8,128)(2,1)S(1)} %copy-done), channel_id=1, source_target_pairs={{0,1},{1,0},{2,3},{3,2},{4,5},{5,4},{6,7},{7,6},{8,9},{9,8},{10,11... | collective-permute-start | bytes 6144008 | tf_op jit(solution)/shard_map/ppermute | solution.py:468
  35.8 13.0 %collective-permute-start.22 = (bf16[80,2304]{1,0:T(8,128)(2,1)}, bf16[80,2304]{1,0:T(8,128)(2,1)S(1)}, u32[]{:S(2)}, u32[]{:S(2)}) collective-permute-start(bf16[80,2304]{1,0:T(8,128)(2,1)} %collective-permute-done.15.rest_5_), channel_id=1, source_target_pairs={{0,8},{4,12},{8,0},{12,4},{16,24},{20,28},{24,16},{28,20},{1,9},{5... | collective-permute-start | bytes 1105928 | tf_op jit(solution)/shard_map/ppermute | solution.py:474
  36.4 12.9 %collective-permute-start.21 = (bf16[80,2304]{1,0:T(8,128)(2,1)}, bf16[80,2304]{1,0:T(8,128)(2,1)S(1)}, u32[]{:S(2)}, u32[]{:S(2)}) collective-permute-start(bf16[80,2304]{1,0:T(8,128)(2,1)} %collective-permute-done.15.rest_5_), channel_id=1, source_target_pairs={{0,4},{4,0},{8,12},{12,8},{16,20},{20,16},{24,28},{28,24},{1,5},{5... | collective-permute-start | bytes 1105928 | tf_op jit(solution)/shard_map/ppermute | solution.py:474
  38.0 11.4 %collective-permute-start.23 = (bf16[80,2304]{1,0:T(8,128)(2,1)S(1)}, bf16[80,2304]{1,0:T(8,128)(2,1)S(1)}, u32[]{:S(2)}, u32[]{:S(2)}) collective-permute-start(bf16[80,2304]{1,0:T(8,128)(2,1)S(1)} %copy-done.9), channel_id=1, source_target_pairs={{0,2},{1,3},{2,0},{3,1},{4,6},{5,7},{6,4},{7,5},{8,10},{9,11},{10,... | collective-permute-start | bytes 1105928 | tf_op jit(solution)/shard_map/ppermute | solution.py:471
  48.7 2.7 %collective-permute-start.24 = (bf16[80,2304]{1,0:T(8,128)(2,1)}, bf16[80,2304]{1,0:T(8,128)(2,1)S(1)}, u32[]{:S(2)}, u32[]{:S(2)}) collective-permute-start(bf16[80,2304]{1,0:T(8,128)(2,1)} %collective-permute-done.15.rest_5_), channel_id=1, source_target_pairs={{0,1},{1,0},{2,3},{3,2},{4,5},{5,4},{6,7},{7,6},{8,9},{9,8},{10,11... | collective-permute-start | bytes 1105928 | tf_op jit(solution)/shard_map/ppermute | solution.py:468
  48.8 2.6 %collective-permute-start.26 = (bf16[80,2304]{1,0:T(8,128)(2,1)S(1)}, bf16[80,2304]{1,0:T(8,128)(2,1)S(1)}, u32[]{:S(2)}, u32[]{:S(2)}) collective-permute-start(bf16[80,2304]{1,0:T(8,128)(2,1)S(1)} %collective-permute-done.22.rest_7_), channel_id=1, source_target_pairs={{0,1},{1,0},{2,3},{3,2},{4,5},{5,4},{6,7},{7,6},{8,9},{9,8},{10,11... | collective-permute-start | bytes 1105928 | tf_op jit(solution)/shard_map/ppermute | solution.py:468
  49.3 2.2 %collective-permute-start.25 = (bf16[80,2304]{1,0:T(8,128)(2,1)S(1)}, bf16[80,2304]{1,0:T(8,128)(2,1)S(1)}, u32[]{:S(2)}, u32[]{:S(2)}) collective-permute-start(bf16[80,2304]{1,0:T(8,128)(2,1)S(1)} %collective-permute-done.21.rest_6_), channel_id=1, source_target_pairs={{0,1},{1,0},{2,3},{3,2},{4,5},{5,4},{6,7},{7,6},{8,9},{9,8},{10,11... | collective-permute-start | bytes 1105928 | tf_op jit(solution)/shard_map/ppermute | solution.py:468
  49.4 2.7 %collective-permute-start.27 = (bf16[80,2304]{1,0:T(8,128)(2,1)S(1)}, bf16[80,2304]{1,0:T(8,128)(2,1)S(1)}, u32[]{:S(2)}, u32[]{:S(2)}) collective-permute-start(bf16[80,2304]{1,0:T(8,128)(2,1)S(1)} %collective-permute-done.23.rest_8_), channel_id=1, source_target_pairs={{0,1},{1,0},{2,3},{3,2},{4,5},{5,4},{6,7},{7,6},{8,9},{9,8},{10,11... | collective-permute-start | bytes 1105928 | tf_op jit(solution)/shard_map/ppermute | solution.py:468
  (6 other events, 34.4 us)
